TPU v7x, 32 devices: a whole 2x2x4 slice. The times are simulated.
32 devices in a mesh: section: 2 (over core), expert: 16 (over z, y, x).
Axes of the slice: x: 2, y: 2, z: 4, core: 2. Of those that a mesh axis runs over, the one named last changes fastest.
Arguments:
- layer_in: bfloat16 [2, 2048, 5120], P('section', 'expert'), may hold values from -50 to 50
- memory: bfloat16 [2, 128, 2, 5120], P('section', 'expert'), may hold values from -80 to 80
- cotangent: bfloat16 [2, 2048, 5120], P('section', 'expert'), may hold values from -6 to 6
- norm_gain: float32 [2, 5120], P('section'), may hold values from 0.5 to 1.5
- attn_gain: float32 [2, 5120], P('section'), may hold values from 0.5 to 1.5
- expert_in: bfloat16 [2, 5120, 10240], P('section', None, 'expert'), may hold values from -0.078125 to 0.078125
- expert_out: bfloat16 [2, 10240, 5120], P('section', 'expert'), may hold values from -0.0625 to 0.0625
- slot_index: int32 [2, 2048], P('section', 'expert'), may hold values from -1 to 7, as said below
- gate_prob: float32 [2, 2048], P('section', 'expert'), may hold values from 0.2 to 1
Outputs:
- layer_out: bfloat16 [2, 2048, 5120], P('section', 'expert')
- arriving: bfloat16 [2, 2048, 5120], P('section', 'expert')
- grad_memory: float32 [2, 128, 2, 5120], P('section', 'expert')
Inputs may be any that keep to these rules, and one draw needn't show every extreme that they name: `slot_index`: within each aligned block of 128 tokens of a layer the slots used are 0 to that block's count minus 1, each once; counts lie between 8 // 3 (at least 1) and 8, and every layer has a block with all 8 slots used.
All inputs are finite; a program needn't handle non-finite values.
Results may differ from a plain program's by a relative error of at most 0.0049.
The roundings to bfloat16 on the way count: a program that leaves them out, or rounds other values in their place, can miss the bound.
Values may be sent and summed in bfloat16 or wider, within the bound.
No kernel may reach another device: no remote copies, remote signals or barrier semaphores. Data moves between devices by JAX's collectives and lax.ppermute only.
A program may use at most 128 MiB of HBM per device.

v0:
```python
import jax
import jax.numpy as jnp
from jax import lax
from jax.sharding import PartitionSpec as P

HD = 128
CAP = 8


def passed_along(block, axis, distance):
    devices = range(lax.axis_size(axis))
    route = [(i - distance, i) for i in devices if i - distance in devices]
    return lax.ppermute(block, axis, route)


def rms_scale(values, scale_row):
    return values * lax.rsqrt(jnp.mean(values * values, axis=-1, keepdims=True) + 1e-06) * scale_row


def attend_parts(per_head_queries, per_head_keys, per_head_values, incoming_head_gradient):
    scaling_factor = HD ** (-0.5)
    attention_scores = (
        jnp.einsum(
            "ksu,lsu->skl", per_head_queries, per_head_keys, preferred_element_type=jnp.float32
        )
        * scaling_factor
    )
    highest = jnp.max(attention_scores, axis=-1, keepdims=True)
    weights = jnp.exp(attention_scores - highest)
    weights = weights / jnp.sum(weights, axis=-1, keepdims=True)
    rounded_down = weights.astype(jnp.bfloat16)
    expert_mixture = jnp.einsum(
        "cif,fcv->icv", rounded_down, per_head_values, preferred_element_type=jnp.float32
    )
    probability_gradient = jnp.einsum(
        "ksu,lsu->skl", incoming_head_gradient, per_head_values, preferred_element_type=jnp.float32
    )
    dscore = (
        weights
        * (probability_gradient - jnp.sum(probability_gradient * weights, axis=-1, keepdims=True))
        * scaling_factor
    )
    upper_limit = dscore.astype(jnp.bfloat16)
    lower_limit = (dscore - upper_limit.astype(jnp.float32)).astype(jnp.bfloat16)
    return (
        expert_mixture.reshape(expert_mixture.shape[0], -1),
        rounded_down,
        upper_limit,
        lower_limit,
    )


def local(
    layer_in, memory, cotangent, norm_gain, attn_gain, expert_in, expert_out, slot_index, gate_prob
):
    sections = lax.axis_size("section")
    decoder = lax.axis_index("section") >= sections // 2
    sources = lax.all_gather(memory[0], "expert", axis=0, tiled=True)
    source_rows = sources.shape[0]
    per_head_keys = sources[:, 0].reshape(source_rows, -1, HD)
    per_head_values = sources[:, 1].reshape(source_rows, -1, HD)
    current = layer_in[0].astype(jnp.float32)
    queries = rms_scale(current, attn_gain[0]).astype(jnp.bfloat16)
    query_rows = queries.shape[0]
    per_head_queries = queries.reshape(query_rows, -1, HD)
    incoming_head_gradient = cotangent[0].reshape(query_rows, -1, HD)
    expert_mixture, rounded_down, upper_limit, lower_limit = attend_parts(
        per_head_queries, per_head_keys, per_head_values, incoming_head_gradient
    )
    decoder_mask = decoder.astype(jnp.float32)
    expert_mixture = expert_mixture * decoder_mask
    residual = (current + expert_mixture).astype(jnp.bfloat16)
    normed = rms_scale(residual.astype(jnp.float32), norm_gain[0]).astype(jnp.bfloat16)
    onehot = (slot_index[0][None, :] == jnp.arange(CAP, dtype=jnp.int32)[:, None]).astype(
        jnp.bfloat16
    )
    capacity = jnp.dot(onehot, normed, preferred_element_type=jnp.float32).astype(jnp.bfloat16)
    gathered = lax.all_gather(capacity, "expert", axis=0, tiled=True)
    hidden = jax.nn.gelu(
        jnp.dot(gathered, expert_in[0], preferred_element_type=jnp.float32)
    ).astype(jnp.bfloat16)
    returned = lax.psum_scatter(
        jnp.dot(hidden, expert_out[0], preferred_element_type=jnp.float32).astype(jnp.bfloat16),
        "expert",
        scatter_dimension=0,
        tiled=True,
    ).astype(jnp.float32)
    combined = jnp.dot(onehot.astype(jnp.float32).T, returned, precision=lax.Precision.HIGHEST)
    output = (residual.astype(jnp.float32) + gate_prob[0][:, None] * combined).astype(jnp.bfloat16)
    arriving = passed_along(output, "section", 1)
    value_gradient_rows = jnp.einsum(
        "yfg,fyb->gyb", rounded_down, incoming_head_gradient, preferred_element_type=jnp.float32
    )
    key_gradient_rows = jnp.einsum(
        "yfg,fyb->gyb", upper_limit, per_head_queries, preferred_element_type=jnp.float32
    )
    key_gradient_rows = key_gradient_rows + jnp.einsum(
        "yfg,fyb->gyb", lower_limit, per_head_queries, preferred_element_type=jnp.float32
    )
    stacked = jnp.stack(
        [key_gradient_rows.reshape(source_rows, -1), value_gradient_rows.reshape(source_rows, -1)],
        axis=1,
    )
    total_grad = lax.psum_scatter(stacked * decoder_mask, "expert", scatter_dimension=0, tiled=True)
    return (output[None], arriving[None], total_grad[None])


def solution(mesh):
    placed = (
        P("section", "expert", None),
        P("section", "expert", None, None),
        P("section", "expert", None),
        P("section", None),
        P("section", None),
        P("section", None, "expert"),
        P("section", "expert", None),
        P("section", "expert"),
        P("section", "expert"),
    )
    return jax.shard_map(
        local,
        mesh=mesh,
        in_specs=placed,
        out_specs=(
            P("section", "expert", None),
            P("section", "expert", None),
            P("section", "expert", None, None),
        ),
        check_vma=False,
    )
```

profile of v0, /device:TPU:1, one launch (start us, length us, event | category | flops | bytes accessed | tf_op | source)
XLA Modules:
  0.0 446.4 jit_solution(18176795829044050495)
XLA Ops:
  7.2 0.0 copy-start
  7.2 0.0 all-gather.6.cloned.1.call-start
  7.2 0.7 all-gather.6.cloned.1.call-update
  7.9 0.0 all-gather.4.cloned.1.call-start
  8.0 0.0 copy-start.6
  8.0 2.8 copy.61
  10.8 0.0 copy-done
  10.8 0.3 fusion.14
  11.2 0.0 copy-done.6
  11.2 3.0 multiply_convert_fusion
  14.2 61.9 %all-gather.6.cloned.1.call-done = bf16[1,128,2,5120]{3,2,0,1:T(2,128)(2,1)} async-done(((bf16[1,8,2,5120]{3,2,0,1:T(2,128)(2,1)}), bf16[1,128,2,5120]{3,2,0,1:T(2,128)(2,1)}) %all-gather.6.cloned.1.call-update) | async-done | bytes 2621456 | tf_op jit(solution)/shard_map/all_gather | solution.py:58
  76.1 7.4 %copy.41 = bf16[1,128,2,5120]{1,3,2,0:T(8,128)(2,1)} copy(bf16[1,128,2,5120]{3,2,0,1:T(2,128)(2,1)} %all-gather.6.cloned.1.call-done) | data formatting | bytes 5242880 | tf_op jit(solution)/shard_map/all_gather | solution.py:58
  83.6 2.9 fusion.72
  86.5 4.3 fusion.73
  90.8 3.8 convolution_multiply_fusion.1
  94.6 3.2 copy.45
  97.8 0.0 copy-start.7
  97.8 0.0 copy-start.9
  97.8 2.2 fusion.11
  100.0 0.0 copy-start.3
  100.1 1.1 copy-done.3
  101.1 0.0 copy-done.7
  101.1 0.0 copy-done.9
  101.1 1.1 convolution_convert_fusion
  102.2 0.0 all-gather.4.cloned.1.call-update
  102.3 0.0 reduce-scatter.2.cloned.1.call-start
  102.3 55.0 %all-gather.4.cloned.1.call-done = bf16[128,5120]{1,0:T(8,128)(2,1)} async-done(((bf16[8,5120]{1,0:T(8,128)(2,1)}), bf16[128,5120]{1,0:T(8,128)(2,1)}) %all-gather.4.cloned.1.call-update) | async-done | bytes 1310736 | tf_op jit(solution)/shard_map/all_gather | solution.py:78
  157.3 8.5 %fusion.8 = bf16[128,5120]{1,0:T(8,128)(2,1)} fusion(bf16[1,640,5120]{2,1,0:T(8,128)(2,1)} %param.15, bf16[128,5120]{1,0:T(8,128)(2,1)} %all-gather.4.cloned.1.call-done, bf16[1,5120,640]{2,1,0:T(8,128)(2,1)} %param.14), kind=kOutput, calls=%fused_computation.9 | convolution fusion | flops 1679114240 | bytes 15728640 | tf_op jit(solution)/shard_map/dot_general | solution.py:83
  165.8 0.0 reduce-scatter.2.cloned.1.call-update
  165.8 0.0 all-reduce.3.cloned.1.call-start
  165.9 1.8 copy.62
  167.6 0.0 copy-start.1
  167.6 2.1 fusion.74
  169.8 0.0 copy-done.1
  169.8 0.0 copy-start.2
  169.8 7.2 %fusion.27 = f32[40,128,128]{2,1,0:T(8,128)} fusion(bf16[128,40,128]{0,2,1:T(8,128)(2,1)} %multiply_convert_fusion, f32[40,128,128]{1,2,0:T(8,128)} %fusion.74, f32[40,128,128]{1,2,0:T(8,128)} %get-tuple-element.8, f32[40,128]{1,0:T(8,128)S(1)} %get-tuple-element.7), kind=kOutput, calls=%fused_computation.36 | convolution fusion | flops 172364928 | bytes 9195520 | tf_op jit(solution)/shard_map/yfg,fyb->gyb/dot_general | solution.py:94
  176.9 0.0 copy-done.2
  176.9 7.5 %convolution_add_fusion = f32[40,128,128]{2,1,0:T(8,128)} fusion(f32[40,128,128]{2,1,0:T(8,128)} %fusion.27, bf16[128,40,128]{0,2,1:T(8,128)(2,1)S(1)} %copy-done.2, f32[40,128,128]{1,2,0:T(8,128)} %fusion.74, f32[40,128,128]{1,2,0:T(8,128)} %get-tuple-element.8, f32[40,128]{1,0:T(8,128)S(1)} %get-tuple-element.7), kind=kOutput, calls=%fused_computation.30 | convolution fusion | flops 174986368 | bytes 11816960 | tf_op jit(solution)/shard_map/yfg,fyb->gyb/dot_general | solution.py:97
  184.5 5.0 %copy.52 = f32[128,1,5120]{2,1,0:T(1,128)S(1)} copy(f32[128,1,5120]{0,2,1:T(8,128)} %bitcast.65) | data formatting | bytes 5242880 | tf_op jit(solution)/shard_map/stack;reshape | solution.py:100
  189.5 4.7 %fusion.37 = f32[40,128,128]{1,2,0:T(8,128)} fusion(bf16[128,40,128]{0,2,1:T(8,128)(2,1)} %bitcast.63, f32[40,128,128]{1,2,0:T(8,128)} %get-tuple-element.8, f32[40,128]{1,0:T(8,128)S(1)} %get-tuple-element.7), kind=kOutput, calls=%fused_computation.38 | convolution fusion | flops 169082880 | bytes 6574080 | tf_op jit(solution)/shard_map/yfg,fyb->gyb/dot_general | solution.py:91
  194.1 6.6 %copy.53 = f32[128,1,5120]{2,1,0:T(1,128)} copy(f32[128,1,5120]{0,2,1:T(8,128)} %bitcast.66) | data formatting | bytes 5242880 | tf_op jit(solution)/shard_map/stack;reshape | solution.py:100
  200.7 7.8 %maximum_multiply_fusion = f32[128,2,5120]{2,1,0:T(2,128)} fusion(f32[128,1,5120]{2,1,0:T(1,128)} %copy.53, f32[128,1,5120]{2,1,0:T(1,128)S(1)} %copy.52, f32[]{:T(128)S(6)} %convert_element_type.62), kind=kLoop, calls=%fused_computation.11 | loop fusion | flops 2621440 | bytes 10485764 | tf_op jit(solution)/shard_map/mul | solution.py:104
  208.4 0.0 copy-start.4
  208.4 0.0 copy-start.8
  208.4 0.0 all-reduce.3.cloned.1.call-update
  208.5 0.0 copy-start.10
  208.5 25.7 %reduce-scatter.2.cloned.1.call-done = bf16[8,5120]{1,0:T(8,128)(2,1)} async-done(((bf16[128,5120]{1,0:T(8,128)(2,1)}), bf16[8,5120]{1,0:T(8,128)(2,1)}) %reduce-scatter.2.cloned.1.call-update) | async-done | bytes 81936 | tf_op jit(solution)/shard_map/reduce_scatter | solution.py:82
  234.2 0.0 copy-done.4
  234.2 0.0 copy-done.8
  234.2 1.4 fusion.7
  235.6 0.0 copy-start.5
  235.6 1.3 collective-permute-start
  236.9 0.0 copy-done.10
  236.9 0.6 dynamic-slice
  238.2 199.0 %all-reduce.3.cloned.1.call-done = f32[128,2,5120]{2,1,0:T(2,128)} async-done(((f32[128,2,5120]{2,1,0:T(2,128)}), f32[128,2,5120]{2,1,0:T(2,128)}) %all-reduce.3.cloned.1.call-update) | async-done | bytes 5242896
  437.1 1.7 dynamic-slice_bitcast_fusion
  438.8 0.0 collective-permute-done
  438.8 1.1 copy.65
  439.9 0.0 copy-done.5
  (2 shorter events, 0.0 us)
Async XLA Ops:
  7.2 3.7 copy-start
  7.2 68.9 %all-gather.6.cloned.1.call-start = ((), (), s32[]{:S(2)}) async-start(), calls=%async_computation.3 | async-start | bytes 2785280 | tf_op jit(solution)/shard_map/all_gather | solution.py:58
  7.9 149.4 %all-gather.4.cloned.1.call-start = ((), (), s32[]{:S(2)}) async-start(), calls=%async_computation.1 | async-start | bytes 1392640 | tf_op jit(solution)/shard_map/all_gather | solution.py:78
  8.0 3.2 copy-start.6
  97.8 3.3 copy-start.7
  97.8 3.3 copy-start.9
  100.0 1.1 copy-start.3
  102.3 131.9 %reduce-scatter.2.cloned.1.call-start = ((), (), s32[]{:S(2)}) async-start(), calls=%async_computation.2 | async-start | bytes 1392640 | tf_op jit(solution)/shard_map/reduce_scatter | solution.py:82
  165.8 271.3 %all-reduce.3.cloned.1.call-start = ((), (), s32[]{:S(2)}) async-start(), calls=%async_computation.4 | async-start | bytes 10485760
  167.6 2.1 copy-start.1
  169.8 7.2 %copy-start.2 = (bf16[128,40,128]{0,2,1:T(8,128)(2,1)S(1)}, bf16[128,40,128]{0,2,1:T(8,128)(2,1)}, u32[]{:S(2)}) copy-start(bf16[128,40,128]{0,2,1:T(8,128)(2,1)} %multiply_convert_fusion) | copy-start | bytes 3932164
  208.4 25.7 %copy-start.4 = (bf16[128,5120]{1,0:T(8,128)(2,1)S(1)}, bf16[128,5120]{1,0:T(8,128)(2,1)}, u32[]{:S(2)}) copy-start(bf16[128,5120]{1,0:T(8,128)(2,1)} %copy-done.3) | copy-start | bytes 3932164
  208.4 25.7 %copy-start.8 = (f32[1,128]{1,0:T(1,128)S(1)}, f32[1,128]{1,0:T(1,128)}, u32[]{:S(2)}) copy-start(f32[1,128]{1,0:T(1,128)} %param.17) | copy-start | bytes 1540
  208.5 28.5 %copy-start.10 = (u32[32]{0:T(128)S(1)}, u32[32]{0:T(128)}, u32[]{:S(2)}) copy-start(u32[32]{0:T(128)} %constant.39) | copy-start | bytes 388
  235.6 204.3 %copy-start.5 = (bf16[128,5120]{1,0:T(8,128)(2,1)}, bf16[128,5120]{1,0:T(8,128)(2,1)S(1)}, u32[]{:S(2)}) copy-start(bf16[128,5120]{1,0:T(8,128)(2,1)S(1)} %fusion.7) | copy-start | bytes 3932164
  235.6 203.2 %collective-permute-start = (bf16[128,5120]{1,0:T(8,128)(2,1)S(1)}, bf16[128,5120]{1,0:T(8,128)(2,1)S(1)}, u32[]{:S(2)}, u32[]{:S(2)}) collective-permute-start(bf16[128,5120]{1,0:T(8,128)(2,1)S(1)} %fusion.7), channel_id=1, source_target_pairs={{0,16},{1,17},{2,18},{3,19},{4,20},{5,21},{6,22},{7,23},{8,24},{9,... | collective-permute-start | bytes 3932168 | tf_op jit(solution)/shard_map/ppermute | solution.py:13
Sparse Core Ops, SparseCore 0:
  10.7 65.3 all-gather.5
  102.4 54.8 all-gather.3
  165.9 68.1 reduce-scatter.1
  239.7 197.3 all-reduce.2
where the time goes:
time: 448 us; the launch traced here: 446 us
  waiting for transfers between devices  342 us (76%)
  matrix products  40.6 us (9%)
  local copies, waits for them, and re-layouts  34.2 us (8%)
  between operations  14.5 us (3%)
  other arithmetic  13.4 us (3%)
    unnamed x5, waiting for transfers between devices  200 us
    all_gather x1, waiting for transfers between devices, local(): sources = lax.all_gather(memory[0], 'expert', axis=0, tiled=True)  61.9 us
    all_gather x1, waiting for transfers between devices, local(): gathered = lax.all_gather(capacity, 'expert', axis=0, tiled=True)  55 us
    reduce_scatter x1, waiting for transfers between devices, local(): lax.psum_scatter(jnp.dot(hidden, expert_out[0], preferred_element_type=jn...  25.7 us
    another operation x2, local copies, waits for them, and re-layouts, local(): jnp.stack([key_gradient_rows.reshape(source_rows, -1), value_gradient_row...  11.5 us
  transfers between devices with their start and end apart: 5, of which 4 were waited for; matrix products, arithmetic and copies ran while one was open for 12% of the time, Pallas kernels for 0%

commit v1 on v0

v1 whole, which is shorter than its diff:
```python
import functools

import jax
import jax.numpy as jnp
from jax import lax
from jax.experimental import pallas as pl
from jax.experimental.pallas import tpu as pltpu
from jax.sharding import PartitionSpec as P

HD = 128
CAP = 8


def passed_along(block, axis, distance):
    devices = range(lax.axis_size(axis))
    route = [(i - distance, i) for i in devices if i - distance in devices]
    return lax.ppermute(block, axis, route)


def swapped(block):
    sections = lax.axis_size("section")
    return lax.ppermute(block, "section", [(i, (i + sections // 2) % sections) for i in range(sections)])


def partner(position, distance, size):
    return position ^ distance if size & (size - 1) == 0 else (position + distance) % size


class Grid:
    def __init__(self, size):
        a = 4 if size % 4 == 0 else 1
        c = 2 if (size // a) % 2 == 0 else 1
        self.sizes = (a, size // a // c, c)
        self.size = size

    def shift(self, block, by, back=False):
        sizes = self.sizes
        route = []
        for index in range(self.size):
            at = (index // (sizes[1] * sizes[2]), index // sizes[2] % sizes[1], index % sizes[2])
            to = [partner(p, d, n) for p, d, n in zip(at, by, sizes)]
            route.append((index, (to[0] * sizes[1] + to[1]) * sizes[2] + to[2]))
        if back:
            route = [(target, source) for source, target in route]
        return lax.ppermute(block, "expert", route)

    def offsets(self):
        _, nb, nc = self.sizes
        return [(b, c) for b in range(nb) for c in range(nc)]

    def heights(self, rows):
        na = self.sizes[0]
        half = rows * (na - na // 2)
        listed = []
        for b, c in self.offsets():
            listed += [half, na * rows - half] if b and c else [na * rows]
        return listed

    def types(self):
        listed = []
        for b, c in self.offsets():
            listed += [jnp.bfloat16] * 2 if b and c else [jnp.float32]
        return listed

    def gather(self, block):
        na, nb, nc = self.sizes
        rows = block.shape[0]
        own = [block] + [self.shift(block, (s, 0, 0)) for s in range(1, na)]
        own = jnp.concatenate(own, axis=0)
        half = rows * (na - na // 2)
        pieces = {(0, 0): [own]}
        for b in range(1, nb):
            pieces[b, 0] = [self.shift(own, (0, b, 0))]
        for c in range(1, nc):
            pieces[0, c] = [self.shift(own, (0, 0, c))]
        for b in range(1, nb):
            for c in range(1, nc):
                first = self.shift(pieces[b, 0][0][:half], (0, 0, c))
                second = self.shift(pieces[0, c][0][half:], (0, b, 0))
                pieces[b, c] = [first, second]
        return sum((pieces[k] for k in self.offsets()), [])

    def scatter(self, pieces, rows, after=(None, None, None)):
        na, nb, nc = self.sizes
        half = rows * (na - na // 2)
        held, at = {}, 0
        for k in self.offsets():
            count = 2 if k[0] and k[1] else 1
            held[k] = pieces[at : at + count]
            at += count
        arrived = []
        for b in range(1, nb):
            more = [self.shift(held[b, c][0], (0, 0, c), back=True) for c in range(1, nc)]
            arrived.append((held[b, 0][0], more, 0, (0, b, 0)))
        for c in range(1, nc):
            more = [self.shift(held[b, c][1], (0, b, 0), back=True) for b in range(1, nb)]
            arrived.append((held[0, c][0], more, half, (0, 0, c)))
        arrived = [
            self.shift(add_half(piece, more, start, after[0]), by, back=True)
            for piece, more, start, by in arrived
        ]
        blocks = add_blocks(held[0, 0][0], arrived, rows, after[1])
        more = [self.shift(blocks[s], (s, 0, 0), back=True) for s in range(1, na)]
        return add_last(blocks[0], more, after[2])


def compiler_params():
    return pltpu.CompilerParams(vmem_limit_bytes=24 * 2**20)


def in_vmem(count):
    return [pl.BlockSpec(memory_space=pltpu.VMEM)] * count


ANYWHERE = pl.BlockSpec(memory_space=pl.ANY)
LAST = (((1,), (1,)), ((), ()))
PLAIN = (((1,), (0,)), ((), ()))


def dot(left, right, dims=PLAIN):
    return lax.dot_general(left, right, dims, preferred_element_type=jnp.float32)


def local_kernel(kernel, name, outs, args, after=None, flops=0, scalars=0, **more):
    args = list(args)
    in_specs = [pl.BlockSpec(memory_space=pltpu.SMEM)] * scalars + in_vmem(len(args) - scalars)
    count = len(args)
    body = kernel
    if after is not None:
        args.append(after)
        in_specs.append(ANYWHERE)

        def body(*refs):
            kernel(*refs[:count], *refs[count + 1 :])

    moved = sum(x.size * x.dtype.itemsize for x in args[:count]) + sum(
        x.size * x.dtype.itemsize for x in outs
    )
    return pl.pallas_call(
        body,
        out_shape=tuple(outs),
        in_specs=in_specs,
        out_specs=tuple(in_vmem(len(outs))),
        compiler_params=compiler_params(),
        cost_estimate=pl.CostEstimate(flops=flops, bytes_accessed=moved, transcendentals=0),
        name=name,
        **more,
    )(*args)


def add_half(piece, more, start, after):
    rows = more[0].shape[0]

    def add(whole, terms):
        there = whole[start : start + rows]
        for term in terms:
            there = there + term.astype(jnp.float32)
        parts = [whole[:start], there, whole[start + rows :]]
        return jnp.concatenate([p for p in parts if p.shape[0]], axis=0).astype(jnp.bfloat16)

    if rows % 16:
        return add(piece, more)

    def kernel(piece_ref, *refs):
        refs[-1][...] = add(piece_ref[...], [r[...] for r in refs[:-1]])

    one = jax.ShapeDtypeStruct(piece.shape, jnp.bfloat16)
    return local_kernel(kernel, "add_half", [one], [piece, *more], after)[0]


def add_blocks(piece, more, rows, after):
    count = piece.shape[0] // rows
    types = [jnp.float32] + [jnp.bfloat16] * (count - 1)

    def add(whole, terms):
        for term in terms:
            whole = whole + term.astype(jnp.float32)
        return [whole[s * rows : (s + 1) * rows].astype(t) for s, t in enumerate(types)]

    if rows % 8:
        return add(piece, more)

    def kernel(*refs):
        terms = [r[...] for r in refs[: 1 + len(more)]]
        for ref, block in zip(refs[1 + len(more) :], add(terms[0], terms[1:])):
            ref[...] = block

    outs = [jax.ShapeDtypeStruct((rows, piece.shape[1]), t) for t in types]
    return local_kernel(kernel, "add_blocks", outs, [piece, *more], after)


def add_last(block, more, after):
    def kernel(block_ref, *refs):
        total = block_ref[...]
        for ref in refs[:-1]:
            total = total + ref[...].astype(jnp.float32)
        refs[-1][...] = total

    one = jax.ShapeDtypeStruct(block.shape, jnp.float32)
    return local_kernel(kernel, "add_last", [one], [block, *more], after)[0]


def head_loop(heads, some_heads):
    few = next(u for u in (5, 4, 2, 1) if heads % u == 0)

    def step(g, carry):
        numbers = [g * few + u for u in range(few)]
        some_heads(numbers, [pl.ds(pl.multiple_of(h * HD, HD), HD) for h in numbers])
        return carry

    lax.fori_loop(0, heads // few, step, 0)


def beside(columns, width):
    return [pl.ds(pl.multiple_of(width + c.start, HD), HD) for c in columns]


def stacked(refs, columns):
    return [jnp.concatenate([r[:, c] for r in refs], axis=0) for c in columns]


def make_queries(x, gain):
    tokens, width = x.shape
    half = width // 2

    def kernel(x_ref, gain_ref, *q_refs):
        x = x_ref[...].astype(jnp.float32)
        inverse = lax.rsqrt(jnp.mean(x * x, axis=-1, keepdims=True) + 1e-06)
        for at, ref in zip((0, half), q_refs):
            x = x_ref[:, at : at + half].astype(jnp.float32)
            ref[...] = (x * inverse * gain_ref[:, at : at + half]).astype(jnp.bfloat16)

    one = jax.ShapeDtypeStruct((tokens, half), jnp.bfloat16)
    return local_kernel(kernel, "queries", [one, one], [x, gain])


def attend(q, pieces):
    tokens, width = q.shape
    heads = width // HD
    rows = sum(p.shape[0] for p in pieces)
    count = len(pieces)

    def kernel(q_ref, *refs):
        kv_refs, (mixed_ref, p_ref) = refs[:count], refs[count:]

        def some_heads(numbers, columns):
            keys = stacked(kv_refs, columns)
            values = stacked(kv_refs, beside(columns, width))
            scores = [dot(k, q_ref[:, c], LAST) * HD**-0.5 for k, c in zip(keys, columns)]
            e = [jnp.exp(s - jnp.max(s, axis=0, keepdims=True)) for s in scores]
            w = [x * (1.0 / jnp.sum(x, axis=0, keepdims=True)) for x in e]
            mixed = [dot(x.astype(jnp.bfloat16).T, v) for x, v in zip(w, values)]
            for h, c, x, m in zip(numbers, columns, w, mixed):
                p_ref[h] = x
                mixed_ref[:, c] = m.astype(jnp.bfloat16)

        head_loop(heads, some_heads)

    outs = [
        jax.ShapeDtypeStruct((tokens, width), jnp.bfloat16),
        jax.ShapeDtypeStruct((heads, rows, tokens), jnp.float32),
    ]
    return local_kernel(kernel, "attend", outs, [q, *pieces], flops=4 * tokens * rows * width)


def gradient(q, cot, p, pieces, heights, types, after):
    tokens, width = q.shape
    heads, rows, _ = p.shape
    count = len(pieces)

    def kernel(q_ref, cot_ref, p_ref, *refs):
        kv_refs, out_refs = refs[:count], refs[count:]

        def some_heads(numbers, columns):
            values = stacked(kv_refs, beside(columns, width))
            q = [q_ref[:, c] for c in columns]
            cot = [cot_ref[:, c] for c in columns]
            w = [p_ref[h] for h in numbers]
            dp = [dot(v, c, LAST) for v, c in zip(values, cot)]
            ds = [
                x * (d - jnp.sum(d * x, axis=0, keepdims=True)) * HD**-0.5 for d, x in zip(dp, w)
            ]
            upper = [x.astype(jnp.bfloat16) for x in ds]
            lower = [(x - u.astype(jnp.float32)).astype(jnp.bfloat16) for x, u in zip(ds, upper)]
            dk = [
                dot(jnp.concatenate([u, v], axis=1), jnp.concatenate([x, x], axis=0))
                for u, v, x in zip(upper, lower, q)
            ]
            dv = [dot(x.astype(jnp.bfloat16), c) for x, c in zip(w, cot)]
            for there, grads in ((columns, dk), (beside(columns, width), dv)):
                for c, g in zip(there, grads):
                    at = 0
                    for ref in out_refs:
                        ref[:, c] = g[at : at + ref.shape[0]].astype(ref.dtype)
                        at += ref.shape[0]

        head_loop(heads, some_heads)

    outs = [jax.ShapeDtypeStruct((n, 2 * width), t) for n, t in zip(heights, types)]
    return local_kernel(
        kernel, "gradient", outs, [q, cot, p, *pieces], after, flops=10 * tokens * rows * width
    )


def settle(flag, x, first, second, norm_gain, slots):
    tokens, width = x.shape
    half = width // 2

    def kernel(flag, x_ref, first_ref, second_ref, norm_ref, slot_ref, res_ref, cap_ref):
        onehot = slot_ref[...] == lax.broadcasted_iota(jnp.int32, (CAP, tokens), 0)
        onehot = jnp.where(onehot, 1.0, 0.0).astype(jnp.bfloat16)
        attends = jnp.full((tokens, 1), flag[0], jnp.int32) == 1
        chosen = []
        for at, ref in ((0, first_ref), (half, second_ref)):
            mixed = jnp.where(attends, ref[...].astype(jnp.float32), 0.0)
            res = (x_ref[:, at : at + half].astype(jnp.float32) + mixed).astype(jnp.bfloat16)
            res_ref[:, at : at + half] = res
            chosen.append(dot(onehot, res))
        squares = sum(jnp.sum(c * c, axis=-1, keepdims=True) for c in chosen)
        inverse = lax.rsqrt(squares / width + 1e-06)
        for at, c in zip((0, half), chosen):
            rows = (c * inverse * norm_ref[:, at : at + half]).astype(jnp.bfloat16)
            cap_ref[:, at : at + half] = rows

    outs = [
        jax.ShapeDtypeStruct((tokens, width), jnp.bfloat16),
        jax.ShapeDtypeStruct((CAP, width), jnp.bfloat16),
    ]
    return local_kernel(
        kernel, "settle", outs, [flag, x, first, second, norm_gain, slots], scalars=1
    )


def expert(w1, w2, pieces, heights, types, after):
    width, units = w1.shape
    rows = sum(heights)
    count = len(pieces)
    steps = next(s for s in (4, 2, 1) if width % (s * 128) == 0)
    step = width // steps

    def kernel(w1_any, w2_any, _, *refs):
        in_refs, out_refs = refs[:count], refs[count : count + len(heights)]
        w1_ref, w2_ref, sems = refs[count + len(heights) :]
        parts = [slice(i * step, (i + 1) * step) for i in range(steps)]
        copies = [
            pltpu.make_async_copy(w1_any.at[c, :], w1_ref.at[c, :], sems.at[0, i])
            for i, c in enumerate(parts)
        ]
        later = [
            pltpu.make_async_copy(w2_any.at[:, c], w2_ref.at[:, c], sems.at[1, i])
            for i, c in enumerate(parts)
        ]
        for copy in copies + later:
            copy.start()
        hidden = jnp.zeros((rows, units), jnp.float32)
        for copy, c in zip(copies, parts):
            x = jnp.concatenate([r[:, c] for r in in_refs], axis=0)
            copy.wait()
            hidden = hidden + dot(x, w1_ref[c, :])
        hidden = jax.nn.gelu(hidden).astype(jnp.bfloat16)
        for copy, c in zip(later, parts):
            copy.wait()
            y = dot(hidden, w2_ref[:, c])
            at = 0
            for ref in out_refs:
                ref[:, c] = y[at : at + ref.shape[0]].astype(ref.dtype)
                at += ref.shape[0]

    return pl.pallas_call(
        kernel,
        out_shape=tuple(jax.ShapeDtypeStruct((n, width), t) for n, t in zip(heights, types)),
        in_specs=[ANYWHERE] * 3 + in_vmem(count),
        out_specs=tuple(in_vmem(len(heights))),
        scratch_shapes=[
            pltpu.VMEM((width, units), w1.dtype),
            pltpu.VMEM((units, width), w2.dtype),
            pltpu.SemaphoreType.DMA((2, steps)),
        ],
        compiler_params=pltpu.CompilerParams(vmem_limit_bytes=48 * 2**20),
        cost_estimate=pl.CostEstimate(
            flops=4 * rows * width * units, bytes_accessed=4 * width * units, transcendentals=0
        ),
        name="expert",
    )(w1, w2, after, *pieces)


def finish(own, before):
    one = jax.ShapeDtypeStruct(own[0].shape, jnp.bfloat16)
    tokens, width = one.shape
    step = next(s for s in (1280, 1024, 512, 256, 128) if width % s == 0)

    def kernel(*refs):
        for res_ref, back_ref, gate_ref, out_ref in (refs[0:3] + refs[6:7], refs[3:6] + refs[7:8]):
            gate = jnp.broadcast_to(gate_ref[0:1], (CAP, tokens)).T[:, 0:1]
            slots = lax.broadcasted_iota(jnp.int32, (CAP, tokens), 0).astype(jnp.float32)
            onehot = jnp.where(gate_ref[1:2] == slots, 1.0, 0.0).T
            onehot = jnp.concatenate([onehot] * 3, axis=1).astype(jnp.bfloat16)
            for at in range(0, width, step):
                columns = slice(at, at + step)
                back = back_ref[:, columns]
                high = back.astype(jnp.bfloat16).astype(jnp.float32)
                middle = (back - high).astype(jnp.bfloat16).astype(jnp.float32)
                parts = jnp.concatenate([high, middle, back - high - middle], axis=0)
                moved = dot(onehot, parts.astype(jnp.bfloat16))
                res = res_ref[:, columns].astype(jnp.float32)
                out_ref[:, columns] = (res + gate * moved).astype(jnp.bfloat16)

    return local_kernel(
        kernel, "finish", [one, one], [*own, *before], flops=100 * tokens * width
    )


def local(
    layer_in, memory, cotangent, norm_gain, attn_gain, expert_in, expert_out, slot_index, gate_prob
):
    sections = lax.axis_size("section")
    decoder = lax.axis_index("section") >= sections // 2
    flag = decoder.astype(jnp.int32).reshape(1)
    grid = Grid(lax.axis_size("expert"))
    own_rows, _, width = memory[0].shape
    half = width // 2
    heights, types = grid.heights(own_rows), grid.types()
    narrow = any(n % 16 for n in heights)

    def shared(first, second):
        return jnp.where(decoder, second, swapped(first))

    stash = shared(
        memory[0, :, :, :half].reshape(own_rows, width),
        memory[0, :, :, half:].reshape(own_rows, width),
    )
    pieces = grid.gather(stash)
    queries = shared(*make_queries(layer_in[0], attn_gain))
    upstream = shared(cotangent[0, :, :half], cotangent[0, :, half:])
    if narrow:
        pieces = [jnp.concatenate(pieces, axis=0)]
    mixed, weights = attend(queries, pieces)
    residual, capacity = settle(flag, layer_in[0], swapped(mixed), mixed, norm_gain, slot_index)
    gathered = grid.gather(capacity)
    gates = jnp.concatenate([gate_prob, slot_index.astype(jnp.float32)], axis=0)
    residual_before = passed_along(residual, "section", 1)
    gates_before = passed_along(gates, "section", 1)
    computed = expert(
        expert_in[0], expert_out[0], gathered, grid.heights(CAP), types, residual_before
    )
    returned = grid.scatter(computed, CAP)
    returned_before = passed_along(returned, "section", 1)
    output, arriving = finish(
        (residual, returned, gates), (residual_before, returned_before, gates_before)
    )
    if narrow:
        whole = [sum(heights)], [jnp.float32]
        (whole,) = gradient(queries, upstream, weights, pieces, *whole, capacity)
        parts, at = [], 0
        for n, t in zip(heights, types):
            parts.append(whole[at : at + n].astype(t))
            at += n
    else:
        parts = gradient(queries, upstream, weights, pieces, heights, types, capacity)
    total_grad = grid.scatter(parts, own_rows, (gathered[-1], computed[0], returned))
    first = swapped(total_grad).reshape(own_rows, 2, half)
    total_grad = jnp.concatenate([first, total_grad.reshape(own_rows, 2, half)], axis=2)
    total_grad = jnp.where(decoder, total_grad, 0.0)
    return (output[None], arriving[None], total_grad[None])


def solution(mesh):
    placed = (
        P("section", "expert", None),
        P("section", "expert", None, None),
        P("section", "expert", None),
        P("section", None),
        P("section", None),
        P("section", None, "expert"),
        P("section", "expert", None),
        P("section", "expert"),
        P("section", "expert"),
    )
    return jax.shard_map(
        local,
        mesh=mesh,
        in_specs=placed,
        out_specs=(
            P("section", "expert", None),
            P("section", "expert", None),
            P("section", "expert", None, None),
        ),
        check_vma=False,
    )
```

time: 448 us -> 119 us (0.27)
  waiting for transfers between devices: 342 us -> 41.7 us
  starting transfers between devices: 1.45 us -> 52.2 us
  matrix products: 40.6 us -> 0 us
  local copies, waits for them, and re-layouts: 34.2 us -> 5.79 us
  Pallas kernels: 0 us -> 16.1 us
  between operations: 14.5 us -> 0.91 us
  other arithmetic: 13.4 us -> 1.08 us
    unnamed x5 -> x0, waiting for transfers between devices: 200 us -> none
    all_gather x2 -> x0, waiting for transfers between devices: 117 us -> none  [the longest x1 61.9 us: local(): sources = lax.all_gather(memory[0], 'expert', axis=0, tiled=True)]
    ppermute x0 -> x33, starting transfers between devices: none -> 48.4 us  [the longest x28 37.4 us: shift(): return lax.ppermute(block, 'expert', route)]
    ppermute x0 -> x33, waiting for transfers between devices: none -> 40.9 us  [the longest x28 38.6 us: shift(): return lax.ppermute(block, 'expert', route)]
    dot_general x8 -> x0, matrix products: 36.3 us -> none  [the longest x1 8.48 us: local(): jnp.dot(hidden, expert_out[0], preferred_element_type=jnp.float32)]
    reduce_scatter x1 -> x0, waiting for transfers between devices: 25.7 us -> none  [local(): lax.psum_scatter(jnp.dot(hidden, expert_out[0], preferred_element_type=jn...]
    pallas_call x0 -> x14, Pallas kernels: none -> 16.1 us  [the longest x13 10.5 us: local_kernel(): pl.pallas_call(body, out_shape=tuple(outs), in_specs=in_specs, out_specs=...]
    another operation x3 -> x0, local copies, waits for them, and re-layouts: 13.3 us -> none  [the longest x2 11.5 us: local(): jnp.stack([key_gradient_rows.reshape(source_rows, -1), value_gradient_row...]
  transfers between devices with their start and end apart: 5 -> 36, of which waited for: 4 -> 16; matrix products, arithmetic and copies ran while one was open for 12% -> 2% of each run, Pallas kernels for 0% -> 9%
where the time goes in v1:
time: 119 us; the launch traced here: 118 us
  starting transfers between devices  52.2 us (44%)
  waiting for transfers between devices  41.7 us (35%)
  Pallas kernels  16.1 us (14%)
  local copies, waits for them, and re-layouts  5.79 us (5%)
    ppermute x28, waiting for transfers between devices, shift(): return lax.ppermute(block, 'expert', route)  38.6 us
    ppermute x28, starting transfers between devices, shift(): return lax.ppermute(block, 'expert', route)  37.4 us
    ppermute x5, starting transfers between devices, swapped(): lax.ppermute(block, 'section', [(i, (i + sections // 2) % sections) for i...  11 us
    pallas_call x13, Pallas kernels, local_kernel(): pl.pallas_call(body, out_shape=tuple(outs), in_specs=in_specs, out_specs=...  10.5 us
    pallas_call x1, Pallas kernels, expert(): pl.pallas_call(kernel, out_shape=tuple((jax.ShapeDtypeStruct((n, width),...  5.67 us
    unnamed x26, local copies, waits for them, and re-layouts  4.58 us
    ppermute x3, starting transfers between devices, passed_along(): return lax.ppermute(block, axis, route)  3.86 us
  transfers between devices with their start and end apart: 36, of which 16 were waited for; matrix products, arithmetic and copies ran while one was open for 2% of the time, Pallas kernels for 9%

profile of v1, /device:TPU:1, one launch (start us, length us, event | category | flops | bytes accessed | tf_op | source)
XLA Modules:
  0.0 117.9 jit_solution(8068534150324266505)
XLA Ops:
  0.6 1.0 slice_bitcast_fusion.1
  1.7 0.1 collective-permute-start.1
  1.8 1.2 %collective-permute-done.1 = bf16[8,5120]{1,0:T(8,128)(2,1)S(1)} collective-permute-done((bf16[8,5120]{1,0:T(8,128)(2,1)S(1)}, bf16[8,5120]{1,0:T(8,128)(2,1)S(1)}, u32[]{:S(2)}, u32[]{:S(2)}) %collective-permute-start.1) | collective-permute-done | bytes 81952 | tf_op jit(solution)/shard_map/ppermute | solution.py:22
  3.1 2.5 %collective-permute-start.2 = (bf16[8,5120]{1,0:T(8,128)(2,1)S(1)}, bf16[8,5120]{1,0:T(8,128)(2,1)S(1)}, u32[]{:S(2)}, u32[]{:S(2)}) collective-permute-start(bf16[8,5120]{1,0:T(8,128)(2,1)S(1)} %broadcast_select_fusion.1), channel_id=1, source_target_pairs={{0,4},{1,5},{2,6},{3,7},{4,0},{5,1},{6,2},{7,3},{8,12},{9,13},{10,... | collective-permute-start | bytes 245768 | tf_op jit(solution)/shard_map/ppermute | solution.py:45
  5.6 2.3 %collective-permute-start.3 = (bf16[8,5120]{1,0:T(8,128)(2,1)S(1)}, bf16[8,5120]{1,0:T(8,128)(2,1)S(1)}, u32[]{:S(2)}, u32[]{:S(2)}) collective-permute-start(bf16[8,5120]{1,0:T(8,128)(2,1)S(1)} %broadcast_select_fusion.1), channel_id=1, source_target_pairs={{0,8},{1,9},{2,10},{3,11},{4,12},{5,13},{6,14},{7,15},{8,0},{9,1},... | collective-permute-start | bytes 245768 | tf_op jit(solution)/shard_map/ppermute | solution.py:45
  7.9 1.3 %copy-done = bf16[1,128,5120]{2,1,0:T(8,128)(2,1)S(1)} copy-done((bf16[1,128,5120]{2,1,0:T(8,128)(2,1)S(1)}, bf16[1,128,5120]{2,1,0:T(8,128)(2,1)}, u32[]{:S(2)}) %copy-start) | copy-done | bytes 1310744
  9.2 0.7 copy-done.5
  9.9 0.9 queries.1
  10.8 1.0 collective-permute-start
  11.8 1.4 %collective-permute-done.4 = bf16[8,5120]{1,0:T(8,128)(2,1)S(1)} collective-permute-done((bf16[8,5120]{1,0:T(8,128)(2,1)S(1)}, bf16[8,5120]{1,0:T(8,128)(2,1)S(1)}, u32[]{:S(2)}, u32[]{:S(2)}) %collective-permute-start.4) | collective-permute-done | bytes 81952 | tf_op jit(solution)/shard_map/ppermute | solution.py:45
  13.2 1.3 %collective-permute-start.6 = (bf16[32,5120]{1,0:T(8,128)(2,1)S(1)}, bf16[32,5120]{1,0:T(8,128)(2,1)S(1)}, u32[]{:S(2)}, u32[]{:S(2)}) collective-permute-start(bf16[32,5120]{1,0:T(8,128)(2,1)S(1)} %pad_maximum_fusion.refs_0_.refs_3_), channel_id=1, source_target_pairs={{0,2},{1,3},{2,0},{3,1},{4,6},{5,7},{6,4},{7,5},{8,10},{9,11},{10,... | collective-permute-start | bytes 983048 | tf_op jit(solution)/shard_map/ppermute | solution.py:45
  14.5 1.2 %collective-permute-start.5 = (bf16[32,5120]{1,0:T(8,128)(2,1)S(1)}, bf16[32,5120]{1,0:T(8,128)(2,1)S(1)}, u32[]{:S(2)}, u32[]{:S(2)}) collective-permute-start(bf16[32,5120]{1,0:T(8,128)(2,1)S(1)} %pad_maximum_fusion.refs_0_.refs_3_), channel_id=1, source_target_pairs={{0,1},{1,0},{2,3},{3,2},{4,5},{5,4},{6,7},{7,6},{8,9},{9,8},{10,11... | collective-permute-start | bytes 983048 | tf_op jit(solution)/shard_map/ppermute | solution.py:45
  15.7 4.3 %collective-permute-done.6.refs_2_.refs_5_ = bf16[32,5120]{1,0:T(8,128)(2,1)S(1)} collective-permute-done((bf16[32,5120]{1,0:T(8,128)(2,1)S(1)}, bf16[32,5120]{1,0:T(8,128)(2,1)S(1)}, u32[]{:S(2)}, u32[]{:S(2)}) %collective-permute-start.6) | collective-permute-done | bytes 327712 | tf_op jit(solution)/shard_map/ppermute | solution.py:45
  20.0 1.3 %collective-permute-start.7 = (bf16[16,5120]{1,0:T(8,128)(2,1)S(1)}, bf16[16,5120]{1,0:T(8,128)(2,1)S(1)}, u32[]{:S(2)}, u32[]{:S(2)}) collective-permute-start(bf16[16,5120]{1,0:T(8,128)(2,1)S(1)} %slice.32), channel_id=1, source_target_pairs={{0,1},{1,0},{2,3},{3,2},{4,5},{5,4},{6,7},{7,6},{8,9},{9,8},{10,11... | collective-permute-start | bytes 491528 | tf_op jit(solution)/shard_map/ppermute | solution.py:45
  21.3 1.3 %collective-permute-start.8 = (bf16[16,5120]{1,0:T(8,128)(2,1)S(1)}, bf16[16,5120]{1,0:T(8,128)(2,1)S(1)}, u32[]{:S(2)}, u32[]{:S(2)}) collective-permute-start(bf16[16,5120]{1,0:T(8,128)(2,1)S(1)} %slice.33), channel_id=1, source_target_pairs={{0,2},{1,3},{2,0},{3,1},{4,6},{5,7},{6,4},{7,5},{8,10},{9,11},{10,... | collective-permute-start | bytes 491528 | tf_op jit(solution)/shard_map/ppermute | solution.py:45
  22.7 3.0 %collective-permute-done.7.refs_3_.refs_6_ = bf16[16,5120]{1,0:T(8,128)(2,1)S(1)} collective-permute-done((bf16[16,5120]{1,0:T(8,128)(2,1)S(1)}, bf16[16,5120]{1,0:T(8,128)(2,1)S(1)}, u32[]{:S(2)}, u32[]{:S(2)}) %collective-permute-start.7) | collective-permute-done | bytes 163872 | tf_op jit(solution)/shard_map/ppermute | solution.py:45
  25.7 2.8 %attend.1 = (bf16[128,2560]{1,0:T(8,128)(2,1)}, f32[20,128,128]{2,1,0:T(8,128)S(1)}) custom-call(bf16[128,2560]{1,0:T(8,128)(2,1)S(1)} %broadcast_select_fusion.q_ref.refs_0_, bf16[32,5120]{1,0:T(8,128)(2,1)S(1)} %pad_maximum_fusion.refs_0_.refs_3_, bf16[32,5120]{1,0:T(8,128)(2,1)S(1)} %collective-permute-done.5.refs_1_.refs_4_, ...), custom_call_target="tpu_custom_call" | custom-call | flops 167772160 | bytes 3932160 | tf_op jit(solution)/shard_map/attend/pallas_call | solution.py:139
  28.5 1.1 copy-done.2
  29.6 5.7 %collective-permute-start.9 = (bf16[128,2560]{1,0:T(8,128)(2,1)}, bf16[128,2560]{1,0:T(8,128)(2,1)}, u32[]{:S(2)}, u32[]{:S(2)}) collective-permute-start(bf16[128,2560]{1,0:T(8,128)(2,1)} %get-tuple-element.31.second_ref), channel_id=1, source_target_pairs={{0,16},{16,0},{1,17},{17,1},{2,18},{18,2},{3,19},{19,3},{4,20},{20... | collective-permute-start | bytes 1966088 | tf_op jit(solution)/shard_map/ppermute | solution.py:22
  35.3 0.9 slice_bitcast_fusion
  36.2 1.2 collective-permute-done.9.first_ref
  37.4 1.9 %settle.1 = (bf16[128,5120]{1,0:T(8,128)(2,1)S(1)}, bf16[8,5120]{1,0:T(8,128)(2,1)S(1)}) custom-call(s32[1]{0:T(128)} %bitcast.flag, bf16[128,5120]{1,0:T(8,128)(2,1)S(1)} %bitcast.21, bf16[128,2560]{1,0:T(8,128)(2,1)} %collective-permute-done.9.first_ref, bf16[128,2560]{1,0:T(8,128)(2,1)} %get-tuple-element.31.second_ref, f32[1,5120]{1,0:T(1,128)S(1)} %copy-done.4, ...), custom_call_target="tpu_custom_call" | custom-call | bytes 4035076 | tf_op jit(solution)/shard_map/settle/pallas_call | solution.py:139
  39.3 1.6 %collective-permute-start.11 = (bf16[8,5120]{1,0:T(8,128)(2,1)S(1)}, bf16[8,5120]{1,0:T(8,128)(2,1)S(1)}, u32[]{:S(2)}, u32[]{:S(2)}) collective-permute-start(bf16[8,5120]{1,0:T(8,128)(2,1)S(1)} %get-tuple-element.33.refs_8_), channel_id=1, source_target_pairs={{0,4},{1,5},{2,6},{3,7},{4,0},{5,1},{6,2},{7,3},{8,12},{9,13},{10,... | collective-permute-start | bytes 245768 | tf_op jit(solution)/shard_map/ppermute | solution.py:45
  40.9 1.0 collective-permute-start.12
  41.9 1.2 collective-permute-start.13
  43.1 1.3 %collective-permute-start.10 = (bf16[128,5120]{1,0:T(8,128)(2,1)S(1)}, bf16[128,5120]{1,0:T(8,128)(2,1)S(1)}, u32[]{:S(2)}, u32[]{:S(2)}) collective-permute-start(bf16[128,5120]{1,0:T(8,128)(2,1)S(1)} %get-tuple-element.32.refs_0_), channel_id=1, source_target_pairs={{0,16},{1,17},{2,18},{3,19},{4,20},{5,21},{6,22},{7,23},{8,24},{9,... | collective-permute-start | bytes 3932168 | tf_op jit(solution)/shard_map/ppermute | solution.py:17
  44.4 1.6 %collective-permute-done.12 = bf16[8,5120]{1,0:T(8,128)(2,1)S(1)} collective-permute-done((bf16[8,5120]{1,0:T(8,128)(2,1)S(1)}, bf16[8,5120]{1,0:T(8,128)(2,1)S(1)}, u32[]{:S(2)}, u32[]{:S(2)}) %collective-permute-start.12) | collective-permute-done | bytes 81952 | tf_op jit(solution)/shard_map/ppermute | solution.py:45
  46.0 2.5 %collective-permute-done.13 = bf16[8,5120]{1,0:T(8,128)(2,1)S(1)} collective-permute-done((bf16[8,5120]{1,0:T(8,128)(2,1)S(1)}, bf16[8,5120]{1,0:T(8,128)(2,1)S(1)}, u32[]{:S(2)}, u32[]{:S(2)}) %collective-permute-start.13) | collective-permute-done | bytes 81952 | tf_op jit(solution)/shard_map/ppermute | solution.py:45
  48.5 1.2 %collective-permute-start.14 = (bf16[32,5120]{1,0:T(8,128)(2,1)S(1)}, bf16[32,5120]{1,0:T(8,128)(2,1)S(1)}, u32[]{:S(2)}, u32[]{:S(2)}) collective-permute-start(bf16[32,5120]{1,0:T(8,128)(2,1)S(1)} %constant_dynamic-update-slice_fusion.refs_0_), channel_id=1, source_target_pairs={{0,1},{1,0},{2,3},{3,2},{4,5},{5,4},{6,7},{7,6},{8,9},{9,8},{10,11... | collective-permute-start | bytes 983048 | tf_op jit(solution)/shard_map/ppermute | solution.py:45
  49.7 1.0 collective-permute-start.15
  50.8 4.4 %collective-permute-done.14.refs_1_ = bf16[32,5120]{1,0:T(8,128)(2,1)S(1)} collective-permute-done((bf16[32,5120]{1,0:T(8,128)(2,1)S(1)}, bf16[32,5120]{1,0:T(8,128)(2,1)S(1)}, u32[]{:S(2)}, u32[]{:S(2)}) %collective-permute-start.14) | collective-permute-done | bytes 327712 | tf_op jit(solution)/shard_map/ppermute | solution.py:45
  55.2 3.0 %collective-permute-start.17 = (bf16[16,5120]{1,0:T(8,128)(2,1)S(1)}, bf16[16,5120]{1,0:T(8,128)(2,1)S(1)}, u32[]{:S(2)}, u32[]{:S(2)}) collective-permute-start(bf16[16,5120]{1,0:T(8,128)(2,1)S(1)} %slice.35), channel_id=1, source_target_pairs={{0,2},{1,3},{2,0},{3,1},{4,6},{5,7},{6,4},{7,5},{8,10},{9,11},{10,... | collective-permute-start | bytes 491528 | tf_op jit(solution)/shard_map/ppermute | solution.py:45
  58.2 0.3 collective-permute-start.16
  58.5 2.4 %collective-permute-done.17.refs_4_.refs_2_ = bf16[16,5120]{1,0:T(8,128)(2,1)S(1)} collective-permute-done((bf16[16,5120]{1,0:T(8,128)(2,1)S(1)}, bf16[16,5120]{1,0:T(8,128)(2,1)S(1)}, u32[]{:S(2)}, u32[]{:S(2)}) %collective-permute-start.17) | collective-permute-done | bytes 163872 | tf_op jit(solution)/shard_map/ppermute | solution.py:45
  60.9 1.8 %collective-permute-done.16.refs_3_ = bf16[16,5120]{1,0:T(8,128)(2,1)S(1)} collective-permute-done((bf16[16,5120]{1,0:T(8,128)(2,1)S(1)}, bf16[16,5120]{1,0:T(8,128)(2,1)S(1)}, u32[]{:S(2)}, u32[]{:S(2)}) %collective-permute-start.16) | collective-permute-done | bytes 163872 | tf_op jit(solution)/shard_map/ppermute | solution.py:45
  62.7 5.7 %expert.1 = (f32[32,5120]{1,0:T(8,128)S(1)}, f32[32,5120]{1,0:T(8,128)S(1)}, f32[32,5120]{1,0:T(8,128)S(1)}, bf16[16,5120]{1,0:T(8,128)(2,1)S(1)}, bf16[16,5120]{1,0:T(8,128)(2,1)S(1)}) custom-call(bf16[5120,640]{1,0:T(8,128)(2,1)} %bitcast.23, bf16[640,5120]{1,0:T(8,128)(2,1)} %bitcast.24, bf16[128,5120]{1,0:T(8,128)(2,1)S(1)} %collective-permute-done.10._.refs_3_, ...), custom_call_target="tpu_custom_call" | custom-call | flops 1677721600 | bytes 13107200 | tf_op jit(solution)/shard_map/expert/pallas_call | solution.py:369
  68.5 0.8 collective-permute-start.18
  69.3 0.4 copy-done.3
  69.7 1.9 %gradient.1 = (f32[32,5120]{1,0:T(8,128)S(1)}, f32[32,5120]{1,0:T(8,128)S(1)}, f32[32,5120]{1,0:T(8,128)S(1)}, bf16[16,5120]{1,0:T(8,128)(2,1)S(1)}, bf16[16,5120]{1,0:T(8,128)(2,1)S(1)}) custom-call(bf16[128,2560]{1,0:T(8,128)(2,1)S(1)} %broadcast_select_fusion.q_ref.refs_0_, bf16[128,2560]{1,0:T(8,128)(2,1)S(1)} %bitcast_select_fusion.refs_1_, ...), custom_call_target="tpu_custom_call" | custom-call | flops 419430400 | bytes 6225920 | tf_op jit(solution)/shard_map/gradient/pallas_call | solution.py:139
  71.6 0.4 collective-permute-start.30
  72.0 1.4 %collective-permute-start.28 = (bf16[16,5120]{1,0:T(8,128)(2,1)S(1)}, bf16[16,5120]{1,0:T(8,128)(2,1)S(1)}, u32[]{:S(2)}, u32[]{:S(2)}) collective-permute-start(bf16[16,5120]{1,0:T(8,128)(2,1)S(1)} %get-tuple-element.48), channel_id=1, source_target_pairs={{1,0},{0,1},{3,2},{2,3},{5,4},{4,5},{7,6},{6,7},{9,8},{8,9},{11,10... | collective-permute-start | bytes 491528 | tf_op jit(solution)/shard_map/ppermute | solution.py:45
  73.7 1.2 collective-permute-start.19
  74.9 2.2 %collective-permute-done.30.refs_1_ = bf16[16,5120]{1,0:T(8,128)(2,1)S(1)} collective-permute-done((bf16[16,5120]{1,0:T(8,128)(2,1)S(1)}, bf16[16,5120]{1,0:T(8,128)(2,1)S(1)}, u32[]{:S(2)}, u32[]{:S(2)}) %collective-permute-start.30) | collective-permute-done | bytes 163872 | tf_op jit(solution)/shard_map/ppermute | solution.py:45
  77.1 0.7 collective-permute-start.31
  77.8 1.5 %collective-permute-start.29 = (bf16[32,5120]{1,0:T(8,128)(2,1)S(1)}, bf16[32,5120]{1,0:T(8,128)(2,1)S(1)}, u32[]{:S(2)}, u32[]{:S(2)}) collective-permute-start(bf16[32,5120]{1,0:T(8,128)(2,1)S(1)} %add_half.6), channel_id=1, source_target_pairs={{2,0},{3,1},{0,2},{1,3},{6,4},{7,5},{4,6},{5,7},{10,8},{11,9},{8,1... | collective-permute-start | bytes 983048 | tf_op jit(solution)/shard_map/ppermute | solution.py:45
  79.3 3.2 %collective-permute-done.21.refs_2_ = bf16[32,5120]{1,0:T(8,128)(2,1)S(1)} collective-permute-done((bf16[32,5120]{1,0:T(8,128)(2,1)S(1)}, bf16[32,5120]{1,0:T(8,128)(2,1)S(1)}, u32[]{:S(2)}, u32[]{:S(2)}) %collective-permute-start.21) | collective-permute-done | bytes 327712 | tf_op jit(solution)/shard_map/ppermute | solution.py:45
  82.4 0.1 add_blocks.2
  82.5 3.7 %collective-permute-start.22 = (bf16[8,5120]{1,0:T(8,128)(2,1)S(1)}, bf16[8,5120]{1,0:T(8,128)(2,1)S(1)}, u32[]{:S(2)}, u32[]{:S(2)}) collective-permute-start(bf16[8,5120]{1,0:T(8,128)(2,1)S(1)} %get-tuple-element.40), channel_id=1, source_target_pairs={{4,0},{5,1},{6,2},{7,3},{0,4},{1,5},{2,6},{3,7},{12,8},{13,9},{14,... | collective-permute-start | bytes 245768 | tf_op jit(solution)/shard_map/ppermute | solution.py:45
  86.2 3.2 %collective-permute-done.31.refs_2_ = bf16[32,5120]{1,0:T(8,128)(2,1)S(1)} collective-permute-done((bf16[32,5120]{1,0:T(8,128)(2,1)S(1)}, bf16[32,5120]{1,0:T(8,128)(2,1)S(1)}, u32[]{:S(2)}, u32[]{:S(2)}) %collective-permute-start.31) | collective-permute-done | bytes 327712 | tf_op jit(solution)/shard_map/ppermute | solution.py:45
  89.6 3.7 %collective-permute-start.32 = (bf16[8,5120]{1,0:T(8,128)(2,1)S(1)}, bf16[8,5120]{1,0:T(8,128)(2,1)S(1)}, u32[]{:S(2)}, u32[]{:S(2)}) collective-permute-start(bf16[8,5120]{1,0:T(8,128)(2,1)S(1)} %get-tuple-element.52), channel_id=1, source_target_pairs={{4,0},{5,1},{6,2},{7,3},{0,4},{1,5},{2,6},{3,7},{12,8},{13,9},{14,... | collective-permute-start | bytes 245768 | tf_op jit(solution)/shard_map/ppermute | solution.py:45
  93.3 1.1 collective-permute-start.23
  94.4 1.1 collective-permute-start.24
  95.5 1.5 %collective-permute-start.33 = (bf16[8,5120]{1,0:T(8,128)(2,1)S(1)}, bf16[8,5120]{1,0:T(8,128)(2,1)S(1)}, u32[]{:S(2)}, u32[]{:S(2)}) collective-permute-start(bf16[8,5120]{1,0:T(8,128)(2,1)S(1)} %get-tuple-element.53), channel_id=1, source_target_pairs={{8,0},{9,1},{10,2},{11,3},{12,4},{13,5},{14,6},{15,7},{0,8},{1,9},... | collective-permute-start | bytes 245768 | tf_op jit(solution)/shard_map/ppermute | solution.py:45
  96.9 1.1 collective-permute-start.34
  98.0 2.1 %collective-permute-done.24.refs_2_ = bf16[8,5120]{1,0:T(8,128)(2,1)S(1)} collective-permute-done((bf16[8,5120]{1,0:T(8,128)(2,1)S(1)}, bf16[8,5120]{1,0:T(8,128)(2,1)S(1)}, u32[]{:S(2)}, u32[]{:S(2)}) %collective-permute-start.24) | collective-permute-done | bytes 81952 | tf_op jit(solution)/shard_map/ppermute | solution.py:45
  100.2 6.4 %collective-permute-done.33.refs_2_ = bf16[8,5120]{1,0:T(8,128)(2,1)S(1)} collective-permute-done((bf16[8,5120]{1,0:T(8,128)(2,1)S(1)}, bf16[8,5120]{1,0:T(8,128)(2,1)S(1)}, u32[]{:S(2)}, u32[]{:S(2)}) %collective-permute-start.33) | collective-permute-done | bytes 81952 | tf_op jit(solution)/shard_map/ppermute | solution.py:45
  106.7 4.1 %collective-permute-start.35 = (f32[8,5120]{1,0:T(8,128)S(1)}, f32[8,5120]{1,0:T(8,128)S(1)}, u32[]{:S(2)}, u32[]{:S(2)}) collective-permute-start(f32[8,5120]{1,0:T(8,128)S(1)} %add_last.3), channel_id=1, source_target_pairs={{0,16},{16,0},{1,17},{17,1},{2,18},{18,2},{3,19},{19,3},{4,20},{20... | collective-permute-start | bytes 491528 | tf_op jit(solution)/shard_map/ppermute | solution.py:22
  110.8 1.3 %collective-permute-start.26 = (f32[2,128]{1,0:T(2,128)S(1)}, f32[2,128]{1,0:T(2,128)S(1)}, u32[]{:S(2)}, u32[]{:S(2)}) collective-permute-start(f32[2,128]{1,0:T(2,128)S(1)} %pad_maximum_fusion.1.refs_2_), channel_id=1, source_target_pairs={{0,16},{1,17},{2,18},{3,19},{4,20},{5,21},{6,22},{7,23},{8,24},{9,... | collective-permute-start | bytes 3080 | tf_op jit(solution)/shard_map/ppermute | solution.py:17
  112.1 1.3 %collective-permute-start.25 = (f32[8,5120]{1,0:T(8,128)S(1)}, f32[8,5120]{1,0:T(8,128)S(1)}, u32[]{:S(2)}, u32[]{:S(2)}) collective-permute-start(f32[8,5120]{1,0:T(8,128)S(1)} %add_last.2.refs_1_.refs_4_), channel_id=1, source_target_pairs={{0,16},{1,17},{2,18},{3,19},{4,20},{5,21},{6,22},{7,23},{8,24},{9,... | collective-permute-start | bytes 491528 | tf_op jit(solution)/shard_map/ppermute | solution.py:17
  113.4 0.1 copy.13
  113.6 0.1 copy.12
  113.7 0.9 maximum_select_fusion
  114.6 0.8 collective-permute-done.25.refs_4_
  115.4 2.5 %finish.1 = (bf16[128,5120]{1,0:T(8,128)(2,1)}, bf16[128,5120]{1,0:T(8,128)(2,1)}) custom-call(bf16[128,5120]{1,0:T(8,128)(2,1)S(1)} %get-tuple-element.32.refs_0_, f32[8,5120]{1,0:T(8,128)S(1)} %add_last.2.refs_1_.refs_4_, f32[2,128]{1,0:T(2,128)S(1)} %pad_maximum_fusion.1.refs_2_, bf16[128,5120]{1,0:T(8,128)(2,1)S(1)} %collective-permute-done.10._.refs_3_, ...), custom_call_target="tpu_custom_call" | custom-call | flops 65536000 | bytes 5572608 | tf_op jit(solution)/shard_map/finish/pallas_call | solution.py:139
  (63 shorter events, 0.9 us)
Async XLA Ops:
  1.7 1.3 %collective-permute-start.1 = (bf16[8,5120]{1,0:T(8,128)(2,1)S(1)}, bf16[8,5120]{1,0:T(8,128)(2,1)S(1)}, u32[]{:S(2)}, u32[]{:S(2)}) collective-permute-start(bf16[8,5120]{1,0:T(8,128)(2,1)S(1)} %bitcast.27), channel_id=1, source_target_pairs={{0,16},{16,0},{1,17},{17,1},{2,18},{18,2},{3,19},{19,3},{4,20},{20... | collective-permute-start | bytes 245768 | tf_op jit(solution)/shard_map/ppermute | solution.py:22
  3.1 8.7 %collective-permute-start.2 = (bf16[8,5120]{1,0:T(8,128)(2,1)S(1)}, bf16[8,5120]{1,0:T(8,128)(2,1)S(1)}, u32[]{:S(2)}, u32[]{:S(2)}) collective-permute-start(bf16[8,5120]{1,0:T(8,128)(2,1)S(1)} %broadcast_select_fusion.1), channel_id=1, source_target_pairs={{0,4},{1,5},{2,6},{3,7},{4,0},{5,1},{6,2},{7,3},{8,12},{9,13},{10,... | collective-permute-start | bytes 245768 | tf_op jit(solution)/shard_map/ppermute | solution.py:45
  5.6 6.2 %collective-permute-start.3 = (bf16[8,5120]{1,0:T(8,128)(2,1)S(1)}, bf16[8,5120]{1,0:T(8,128)(2,1)S(1)}, u32[]{:S(2)}, u32[]{:S(2)}) collective-permute-start(bf16[8,5120]{1,0:T(8,128)(2,1)S(1)} %broadcast_select_fusion.1), channel_id=1, source_target_pairs={{0,8},{1,9},{2,10},{3,11},{4,12},{5,13},{6,14},{7,15},{8,0},{9,1},... | collective-permute-start | bytes 245768 | tf_op jit(solution)/shard_map/ppermute | solution.py:45
  7.9 5.3 %collective-permute-start.4 = (bf16[8,5120]{1,0:T(8,128)(2,1)S(1)}, bf16[8,5120]{1,0:T(8,128)(2,1)S(1)}, u32[]{:S(2)}, u32[]{:S(2)}) collective-permute-start(bf16[8,5120]{1,0:T(8,128)(2,1)S(1)} %broadcast_select_fusion.1), channel_id=1, source_target_pairs={{0,12},{1,13},{2,14},{3,15},{4,8},{5,9},{6,10},{7,11},{8,4},{9,5},... | collective-permute-start | bytes 245768 | tf_op jit(solution)/shard_map/ppermute | solution.py:45
  7.9 1.3 %copy-start = (bf16[1,128,5120]{2,1,0:T(8,128)(2,1)S(1)}, bf16[1,128,5120]{2,1,0:T(8,128)(2,1)}, u32[]{:S(2)}) copy-start(bf16[1,128,5120]{2,1,0:T(8,128)(2,1)} %param.9) | copy-start | bytes 3932164
  9.2 0.7 copy-start.5
  10.8 11.8 %collective-permute-start = (bf16[128,2560]{1,0:T(8,128)(2,1)S(1)}, bf16[128,2560]{1,0:T(8,128)(2,1)S(1)}, u32[]{:S(2)}, u32[]{:S(2)}) collective-permute-start(bf16[128,2560]{1,0:T(8,128)(2,1)S(1)} %get-tuple-element.30), channel_id=1, source_target_pairs={{0,16},{16,0},{1,17},{17,1},{2,18},{18,2},{3,19},{19,3},{4,20},{20... | collective-permute-start | bytes 1966088 | tf_op jit(solution)/shard_map/ppermute | solution.py:22
  13.2 6.8 %collective-permute-start.6 = (bf16[32,5120]{1,0:T(8,128)(2,1)S(1)}, bf16[32,5120]{1,0:T(8,128)(2,1)S(1)}, u32[]{:S(2)}, u32[]{:S(2)}) collective-permute-start(bf16[32,5120]{1,0:T(8,128)(2,1)S(1)} %pad_maximum_fusion.refs_0_.refs_3_), channel_id=1, source_target_pairs={{0,2},{1,3},{2,0},{3,1},{4,6},{5,7},{6,4},{7,5},{8,10},{9,11},{10,... | collective-permute-start | bytes 983048 | tf_op jit(solution)/shard_map/ppermute | solution.py:45
  14.5 6.8 %collective-permute-start.5 = (bf16[32,5120]{1,0:T(8,128)(2,1)S(1)}, bf16[32,5120]{1,0:T(8,128)(2,1)S(1)}, u32[]{:S(2)}, u32[]{:S(2)}) collective-permute-start(bf16[32,5120]{1,0:T(8,128)(2,1)S(1)} %pad_maximum_fusion.refs_0_.refs_3_), channel_id=1, source_target_pairs={{0,1},{1,0},{2,3},{3,2},{4,5},{5,4},{6,7},{7,6},{8,9},{9,8},{10,11... | collective-permute-start | bytes 983048 | tf_op jit(solution)/shard_map/ppermute | solution.py:45
  20.0 5.7 %collective-permute-start.7 = (bf16[16,5120]{1,0:T(8,128)(2,1)S(1)}, bf16[16,5120]{1,0:T(8,128)(2,1)S(1)}, u32[]{:S(2)}, u32[]{:S(2)}) collective-permute-start(bf16[16,5120]{1,0:T(8,128)(2,1)S(1)} %slice.32), channel_id=1, source_target_pairs={{0,1},{1,0},{2,3},{3,2},{4,5},{5,4},{6,7},{7,6},{8,9},{9,8},{10,11... | collective-permute-start | bytes 491528 | tf_op jit(solution)/shard_map/ppermute | solution.py:45
  21.3 4.4 %collective-permute-start.8 = (bf16[16,5120]{1,0:T(8,128)(2,1)S(1)}, bf16[16,5120]{1,0:T(8,128)(2,1)S(1)}, u32[]{:S(2)}, u32[]{:S(2)}) collective-permute-start(bf16[16,5120]{1,0:T(8,128)(2,1)S(1)} %slice.33), channel_id=1, source_target_pairs={{0,2},{1,3},{2,0},{3,1},{4,6},{5,7},{6,4},{7,5},{8,10},{9,11},{10,... | collective-permute-start | bytes 491528 | tf_op jit(solution)/shard_map/ppermute | solution.py:45
  22.6 12.7 %copy-start.7 = (bf16[1,128,5120]{2,1,0:T(8,128)(2,1)S(1)}, bf16[1,128,5120]{2,1,0:T(8,128)(2,1)}, u32[]{:S(2)}) copy-start(bf16[1,128,5120]{2,1,0:T(8,128)(2,1)} %param.11) | copy-start | bytes 3932164
  22.7 14.7 %copy-start.1 = (bf16[1,128,5120]{2,1,0:T(8,128)(2,1)S(1)}, bf16[1,128,5120]{2,1,0:T(8,128)(2,1)}, u32[]{:S(2)}) copy-start(bf16[1,128,5120]{2,1,0:T(8,128)(2,1)} %param.9) | copy-start | bytes 3932164
  22.7 14.7 %copy-start.4 = (f32[1,5120]{1,0:T(1,128)S(1)}, f32[1,5120]{1,0:T(1,128)}, u32[]{:S(2)}) copy-start(f32[1,5120]{1,0:T(1,128)} %norm_ref.1) | copy-start | bytes 61444
  22.7 14.7 %copy-start.6 = (s32[1,128]{1,0:T(1,128)S(1)}, s32[1,128]{1,0:T(1,128)}, u32[]{:S(2)}) copy-start(s32[1,128]{1,0:T(1,128)} %slot_ref.1) | copy-start | bytes 1540
  28.5 1.1 copy-start.2
  29.6 7.8 %collective-permute-start.9 = (bf16[128,2560]{1,0:T(8,128)(2,1)}, bf16[128,2560]{1,0:T(8,128)(2,1)}, u32[]{:S(2)}, u32[]{:S(2)}) collective-permute-start(bf16[128,2560]{1,0:T(8,128)(2,1)} %get-tuple-element.31.second_ref), channel_id=1, source_target_pairs={{0,16},{16,0},{1,17},{17,1},{2,18},{18,2},{3,19},{19,3},{4,20},{20... | collective-permute-start | bytes 1966088 | tf_op jit(solution)/shard_map/ppermute | solution.py:22
  36.2 33.0 %collective-permute-start.27 = (bf16[128,2560]{1,0:T(8,128)(2,1)}, bf16[128,2560]{1,0:T(8,128)(2,1)}, u32[]{:S(2)}, u32[]{:S(2)}) collective-permute-start(bf16[128,2560]{1,0:T(8,128)(2,1)} %slice_bitcast_fusion), channel_id=1, source_target_pairs={{0,16},{16,0},{1,17},{17,1},{2,18},{18,2},{3,19},{19,3},{4,20},{20... | collective-permute-start | bytes 1966088 | tf_op jit(solution)/shard_map/ppermute | solution.py:22
  39.3 5.0 %collective-permute-start.11 = (bf16[8,5120]{1,0:T(8,128)(2,1)S(1)}, bf16[8,5120]{1,0:T(8,128)(2,1)S(1)}, u32[]{:S(2)}, u32[]{:S(2)}) collective-permute-start(bf16[8,5120]{1,0:T(8,128)(2,1)S(1)} %get-tuple-element.33.refs_8_), channel_id=1, source_target_pairs={{0,4},{1,5},{2,6},{3,7},{4,0},{5,1},{6,2},{7,3},{8,12},{9,13},{10,... | collective-permute-start | bytes 245768 | tf_op jit(solution)/shard_map/ppermute | solution.py:45
  40.9 5.1 %collective-permute-start.12 = (bf16[8,5120]{1,0:T(8,128)(2,1)S(1)}, bf16[8,5120]{1,0:T(8,128)(2,1)S(1)}, u32[]{:S(2)}, u32[]{:S(2)}) collective-permute-start(bf16[8,5120]{1,0:T(8,128)(2,1)S(1)} %get-tuple-element.33.refs_8_), channel_id=1, source_target_pairs={{0,8},{1,9},{2,10},{3,11},{4,12},{5,13},{6,14},{7,15},{8,0},{9,1},... | collective-permute-start | bytes 245768 | tf_op jit(solution)/shard_map/ppermute | solution.py:45
  41.9 6.6 %collective-permute-start.13 = (bf16[8,5120]{1,0:T(8,128)(2,1)S(1)}, bf16[8,5120]{1,0:T(8,128)(2,1)S(1)}, u32[]{:S(2)}, u32[]{:S(2)}) collective-permute-start(bf16[8,5120]{1,0:T(8,128)(2,1)S(1)} %get-tuple-element.33.refs_8_), channel_id=1, source_target_pairs={{0,12},{1,13},{2,14},{3,15},{4,8},{5,9},{6,10},{7,11},{8,4},{9,5},... | collective-permute-start | bytes 245768 | tf_op jit(solution)/shard_map/ppermute | solution.py:45
  43.1 19.6 %collective-permute-start.10 = (bf16[128,5120]{1,0:T(8,128)(2,1)S(1)}, bf16[128,5120]{1,0:T(8,128)(2,1)S(1)}, u32[]{:S(2)}, u32[]{:S(2)}) collective-permute-start(bf16[128,5120]{1,0:T(8,128)(2,1)S(1)} %get-tuple-element.32.refs_0_), channel_id=1, source_target_pairs={{0,16},{1,17},{2,18},{3,19},{4,20},{5,21},{6,22},{7,23},{8,24},{9,... | collective-permute-start | bytes 3932168 | tf_op jit(solution)/shard_map/ppermute | solution.py:17
  48.5 6.7 %collective-permute-start.14 = (bf16[32,5120]{1,0:T(8,128)(2,1)S(1)}, bf16[32,5120]{1,0:T(8,128)(2,1)S(1)}, u32[]{:S(2)}, u32[]{:S(2)}) collective-permute-start(bf16[32,5120]{1,0:T(8,128)(2,1)S(1)} %constant_dynamic-update-slice_fusion.refs_0_), channel_id=1, source_target_pairs={{0,1},{1,0},{2,3},{3,2},{4,5},{5,4},{6,7},{7,6},{8,9},{9,8},{10,11... | collective-permute-start | bytes 983048 | tf_op jit(solution)/shard_map/ppermute | solution.py:45
  49.7 8.4 %collective-permute-start.15 = (bf16[32,5120]{1,0:T(8,128)(2,1)S(1)}, bf16[32,5120]{1,0:T(8,128)(2,1)S(1)}, u32[]{:S(2)}, u32[]{:S(2)}) collective-permute-start(bf16[32,5120]{1,0:T(8,128)(2,1)S(1)} %constant_dynamic-update-slice_fusion.refs_0_), channel_id=1, source_target_pairs={{0,2},{1,3},{2,0},{3,1},{4,6},{5,7},{6,4},{7,5},{8,10},{9,11},{10,... | collective-permute-start | bytes 983048 | tf_op jit(solution)/shard_map/ppermute | solution.py:45
  55.2 5.7 %collective-permute-start.17 = (bf16[16,5120]{1,0:T(8,128)(2,1)S(1)}, bf16[16,5120]{1,0:T(8,128)(2,1)S(1)}, u32[]{:S(2)}, u32[]{:S(2)}) collective-permute-start(bf16[16,5120]{1,0:T(8,128)(2,1)S(1)} %slice.35), channel_id=1, source_target_pairs={{0,2},{1,3},{2,0},{3,1},{4,6},{5,7},{6,4},{7,5},{8,10},{9,11},{10,... | collective-permute-start | bytes 491528 | tf_op jit(solution)/shard_map/ppermute | solution.py:45
  58.2 4.5 %collective-permute-start.16 = (bf16[16,5120]{1,0:T(8,128)(2,1)S(1)}, bf16[16,5120]{1,0:T(8,128)(2,1)S(1)}, u32[]{:S(2)}, u32[]{:S(2)}) collective-permute-start(bf16[16,5120]{1,0:T(8,128)(2,1)S(1)} %slice.34), channel_id=1, source_target_pairs={{0,1},{1,0},{2,3},{3,2},{4,5},{5,4},{6,7},{7,6},{8,9},{9,8},{10,11... | collective-permute-start | bytes 491528 | tf_op jit(solution)/shard_map/ppermute | solution.py:45
  62.7 6.6 %copy-start.8 = (bf16[1,128,5120]{2,1,0:T(8,128)(2,1)S(1)}, bf16[1,128,5120]{2,1,0:T(8,128)(2,1)}, u32[]{:S(2)}) copy-start(bf16[1,128,5120]{2,1,0:T(8,128)(2,1)} %param.11) | copy-start | bytes 3932164
  68.4 1.3 %copy-start.3 = (f32[20,128,128]{2,1,0:T(8,128)S(1)}, f32[20,128,128]{2,1,0:T(8,128)}, u32[]{:S(2)}) copy-start(f32[20,128,128]{2,1,0:T(8,128)} %copy-done.2) | copy-start | bytes 3932164
  68.4 5.1 %collective-permute-start.20 = (bf16[16,5120]{1,0:T(8,128)(2,1)S(1)}, bf16[16,5120]{1,0:T(8,128)(2,1)S(1)}, u32[]{:S(2)}, u32[]{:S(2)}) collective-permute-start(bf16[16,5120]{1,0:T(8,128)(2,1)S(1)} %get-tuple-element.38), channel_id=1, source_target_pairs={{2,0},{3,1},{0,2},{1,3},{6,4},{7,5},{4,6},{5,7},{10,8},{11,9},{8,1... | collective-permute-start | bytes 491528 | tf_op jit(solution)/shard_map/ppermute | solution.py:45
  68.5 5.2 %collective-permute-start.18 = (bf16[16,5120]{1,0:T(8,128)(2,1)S(1)}, bf16[16,5120]{1,0:T(8,128)(2,1)S(1)}, u32[]{:S(2)}, u32[]{:S(2)}) collective-permute-start(bf16[16,5120]{1,0:T(8,128)(2,1)S(1)} %get-tuple-element.36), channel_id=1, source_target_pairs={{1,0},{0,1},{3,2},{2,3},{5,4},{4,5},{7,6},{6,7},{9,8},{8,9},{11,10... | collective-permute-start | bytes 491528 | tf_op jit(solution)/shard_map/ppermute | solution.py:45
  71.6 5.4 %collective-permute-start.30 = (bf16[16,5120]{1,0:T(8,128)(2,1)S(1)}, bf16[16,5120]{1,0:T(8,128)(2,1)S(1)}, u32[]{:S(2)}, u32[]{:S(2)}) collective-permute-start(bf16[16,5120]{1,0:T(8,128)(2,1)S(1)} %get-tuple-element.50), channel_id=1, source_target_pairs={{2,0},{3,1},{0,2},{1,3},{6,4},{7,5},{4,6},{5,7},{10,8},{11,9},{8,1... | collective-permute-start | bytes 491528 | tf_op jit(solution)/shard_map/ppermute | solution.py:45
  72.0 5.7 %collective-permute-start.28 = (bf16[16,5120]{1,0:T(8,128)(2,1)S(1)}, bf16[16,5120]{1,0:T(8,128)(2,1)S(1)}, u32[]{:S(2)}, u32[]{:S(2)}) collective-permute-start(bf16[16,5120]{1,0:T(8,128)(2,1)S(1)} %get-tuple-element.48), channel_id=1, source_target_pairs={{1,0},{0,1},{3,2},{2,3},{5,4},{4,5},{7,6},{6,7},{9,8},{8,9},{11,10... | collective-permute-start | bytes 491528 | tf_op jit(solution)/shard_map/ppermute | solution.py:45
  73.6 8.9 %collective-permute-start.21 = (bf16[32,5120]{1,0:T(8,128)(2,1)S(1)}, bf16[32,5120]{1,0:T(8,128)(2,1)S(1)}, u32[]{:S(2)}, u32[]{:S(2)}) collective-permute-start(bf16[32,5120]{1,0:T(8,128)(2,1)S(1)} %add_half.5), channel_id=1, source_target_pairs={{1,0},{0,1},{3,2},{2,3},{5,4},{4,5},{7,6},{6,7},{9,8},{8,9},{11,10... | collective-permute-start | bytes 983048 | tf_op jit(solution)/shard_map/ppermute | solution.py:45
  73.7 8.7 %collective-permute-start.19 = (bf16[32,5120]{1,0:T(8,128)(2,1)S(1)}, bf16[32,5120]{1,0:T(8,128)(2,1)S(1)}, u32[]{:S(2)}, u32[]{:S(2)}) collective-permute-start(bf16[32,5120]{1,0:T(8,128)(2,1)S(1)} %add_half.4), channel_id=1, source_target_pairs={{2,0},{3,1},{0,2},{1,3},{6,4},{7,5},{4,6},{5,7},{10,8},{11,9},{8,1... | collective-permute-start | bytes 983048 | tf_op jit(solution)/shard_map/ppermute | solution.py:45
  77.1 12.4 %collective-permute-start.31 = (bf16[32,5120]{1,0:T(8,128)(2,1)S(1)}, bf16[32,5120]{1,0:T(8,128)(2,1)S(1)}, u32[]{:S(2)}, u32[]{:S(2)}) collective-permute-start(bf16[32,5120]{1,0:T(8,128)(2,1)S(1)} %add_half.7), channel_id=1, source_target_pairs={{1,0},{0,1},{3,2},{2,3},{5,4},{4,5},{7,6},{6,7},{9,8},{8,9},{11,10... | collective-permute-start | bytes 983048 | tf_op jit(solution)/shard_map/ppermute | solution.py:45
  77.8 11.7 %collective-permute-start.29 = (bf16[32,5120]{1,0:T(8,128)(2,1)S(1)}, bf16[32,5120]{1,0:T(8,128)(2,1)S(1)}, u32[]{:S(2)}, u32[]{:S(2)}) collective-permute-start(bf16[32,5120]{1,0:T(8,128)(2,1)S(1)} %add_half.6), channel_id=1, source_target_pairs={{2,0},{3,1},{0,2},{1,3},{6,4},{7,5},{4,6},{5,7},{10,8},{11,9},{8,1... | collective-permute-start | bytes 983048 | tf_op jit(solution)/shard_map/ppermute | solution.py:45
  82.5 14.4 %collective-permute-start.22 = (bf16[8,5120]{1,0:T(8,128)(2,1)S(1)}, bf16[8,5120]{1,0:T(8,128)(2,1)S(1)}, u32[]{:S(2)}, u32[]{:S(2)}) collective-permute-start(bf16[8,5120]{1,0:T(8,128)(2,1)S(1)} %get-tuple-element.40), channel_id=1, source_target_pairs={{4,0},{5,1},{6,2},{7,3},{0,4},{1,5},{2,6},{3,7},{12,8},{13,9},{14,... | collective-permute-start | bytes 245768 | tf_op jit(solution)/shard_map/ppermute | solution.py:45
  89.5 21.3 %copy-start.9 = (f32[1,128]{1,0:T(1,128)S(1)}, f32[1,128]{1,0:T(1,128)}, u32[]{:S(2)}) copy-start(f32[1,128]{1,0:T(1,128)} %param.17) | copy-start | bytes 1540
  89.6 10.6 %collective-permute-start.32 = (bf16[8,5120]{1,0:T(8,128)(2,1)S(1)}, bf16[8,5120]{1,0:T(8,128)(2,1)S(1)}, u32[]{:S(2)}, u32[]{:S(2)}) collective-permute-start(bf16[8,5120]{1,0:T(8,128)(2,1)S(1)} %get-tuple-element.52), channel_id=1, source_target_pairs={{4,0},{5,1},{6,2},{7,3},{0,4},{1,5},{2,6},{3,7},{12,8},{13,9},{14,... | collective-permute-start | bytes 245768 | tf_op jit(solution)/shard_map/ppermute | solution.py:45
  93.3 4.7 %collective-permute-start.23 = (bf16[8,5120]{1,0:T(8,128)(2,1)S(1)}, bf16[8,5120]{1,0:T(8,128)(2,1)S(1)}, u32[]{:S(2)}, u32[]{:S(2)}) collective-permute-start(bf16[8,5120]{1,0:T(8,128)(2,1)S(1)} %get-tuple-element.41), channel_id=1, source_target_pairs={{8,0},{9,1},{10,2},{11,3},{12,4},{13,5},{14,6},{15,7},{0,8},{1,9},... | collective-permute-start | bytes 245768 | tf_op jit(solution)/shard_map/ppermute | solution.py:45
  94.4 5.8 %collective-permute-start.24 = (bf16[8,5120]{1,0:T(8,128)(2,1)S(1)}, bf16[8,5120]{1,0:T(8,128)(2,1)S(1)}, u32[]{:S(2)}, u32[]{:S(2)}) collective-permute-start(bf16[8,5120]{1,0:T(8,128)(2,1)S(1)} %get-tuple-element.42), channel_id=1, source_target_pairs={{12,0},{13,1},{14,2},{15,3},{8,4},{9,5},{10,6},{11,7},{4,8},{5,9},... | collective-permute-start | bytes 245768 | tf_op jit(solution)/shard_map/ppermute | solution.py:45
  95.5 11.2 %collective-permute-start.33 = (bf16[8,5120]{1,0:T(8,128)(2,1)S(1)}, bf16[8,5120]{1,0:T(8,128)(2,1)S(1)}, u32[]{:S(2)}, u32[]{:S(2)}) collective-permute-start(bf16[8,5120]{1,0:T(8,128)(2,1)S(1)} %get-tuple-element.53), channel_id=1, source_target_pairs={{8,0},{9,1},{10,2},{11,3},{12,4},{13,5},{14,6},{15,7},{0,8},{1,9},... | collective-permute-start | bytes 245768 | tf_op jit(solution)/shard_map/ppermute | solution.py:45
  96.9 9.7 %collective-permute-start.34 = (bf16[8,5120]{1,0:T(8,128)(2,1)S(1)}, bf16[8,5120]{1,0:T(8,128)(2,1)S(1)}, u32[]{:S(2)}, u32[]{:S(2)}) collective-permute-start(bf16[8,5120]{1,0:T(8,128)(2,1)S(1)} %get-tuple-element.54), channel_id=1, source_target_pairs={{12,0},{13,1},{14,2},{15,3},{8,4},{9,5},{10,6},{11,7},{4,8},{5,9},... | collective-permute-start | bytes 245768 | tf_op jit(solution)/shard_map/ppermute | solution.py:45
  106.7 6.9 %collective-permute-start.35 = (f32[8,5120]{1,0:T(8,128)S(1)}, f32[8,5120]{1,0:T(8,128)S(1)}, u32[]{:S(2)}, u32[]{:S(2)}) collective-permute-start(f32[8,5120]{1,0:T(8,128)S(1)} %add_last.3), channel_id=1, source_target_pairs={{0,16},{16,0},{1,17},{17,1},{2,18},{18,2},{3,19},{19,3},{4,20},{20... | collective-permute-start | bytes 491528 | tf_op jit(solution)/shard_map/ppermute | solution.py:22
  110.8 3.8 %collective-permute-start.26 = (f32[2,128]{1,0:T(2,128)S(1)}, f32[2,128]{1,0:T(2,128)S(1)}, u32[]{:S(2)}, u32[]{:S(2)}) collective-permute-start(f32[2,128]{1,0:T(2,128)S(1)} %pad_maximum_fusion.1.refs_2_), channel_id=1, source_target_pairs={{0,16},{1,17},{2,18},{3,19},{4,20},{5,21},{6,22},{7,23},{8,24},{9,... | collective-permute-start | bytes 3080 | tf_op jit(solution)/shard_map/ppermute | solution.py:17
  112.1 3.3 %collective-permute-start.25 = (f32[8,5120]{1,0:T(8,128)S(1)}, f32[8,5120]{1,0:T(8,128)S(1)}, u32[]{:S(2)}, u32[]{:S(2)}) collective-permute-start(f32[8,5120]{1,0:T(8,128)S(1)} %add_last.2.refs_1_.refs_4_), channel_id=1, source_target_pairs={{0,16},{1,17},{2,18},{3,19},{4,20},{5,21},{6,22},{7,23},{8,24},{9,... | collective-permute-start | bytes 491528 | tf_op jit(solution)/shard_map/ppermute | solution.py:17

commit v2 on v1

v2 whole, which is shorter than its diff:
```python
import functools

import jax
import jax.numpy as jnp
from jax import lax
from jax.experimental import pallas as pl
from jax.experimental.pallas import tpu as pltpu
from jax.sharding import PartitionSpec as P

HD = 128
CAP = 8


def passed_along(block, axis, distance):
    devices = range(lax.axis_size(axis))
    route = [(i - distance, i) for i in devices if i - distance in devices]
    return lax.ppermute(block, axis, route)


def swapped(block):
    sections = lax.axis_size("section")
    return lax.ppermute(block, "section", [(i, (i + sections // 2) % sections) for i in range(sections)])


def to_decoder(block):
    apart = lax.axis_size("section") // 2
    return lax.ppermute(block, "section", [(i, i + apart) for i in range(apart)])


def partner(position, distance, size):
    return position ^ distance if size & (size - 1) == 0 else (position + distance) % size


class Grid:
    def __init__(self, size):
        side = 2 if size % 4 == 0 else 1
        self.sizes = (size // side**2, side, side)
        self.size = size

    def shift(self, block, by, back=False):
        sizes = self.sizes
        route = []
        for index in range(self.size):
            at = (index // (sizes[1] * sizes[2]), index // sizes[2] % sizes[1], index % sizes[2])
            to = [partner(p, d, n) for p, d, n in zip(at, by, sizes)]
            route.append((index, (to[0] * sizes[1] + to[1]) * sizes[2] + to[2]))
        if back:
            route = [(target, source) for source, target in route]
        return lax.ppermute(block, "expert", route)

    def offsets(self):
        _, nb, nc = self.sizes
        return [(b, c) for b in range(nb) for c in range(nc)]

    def heights(self, rows):
        na = self.sizes[0]
        half = rows * (na - na // 2)
        listed = []
        for b, c in self.offsets():
            listed += [half, na * rows - half] if b and c else [na * rows]
        return listed

    def types(self):
        listed = []
        for b, c in self.offsets():
            listed += [jnp.bfloat16] * 2 if b and c else [jnp.float32]
        return listed

    def line(self, block):
        return join([block] + [self.shift(block, (s, 0, 0)) for s in range(1, self.sizes[0])])

    def plane(self, blocks):
        return [blocks[0]] + [
            self.shift(block, (0, b, c)) for block, (b, c) in zip(blocks[1:], self.offsets()[1:])
        ]

    def gather(self, block, after):
        na, nb, nc = self.sizes
        own = self.line(block)
        half = block.shape[0] * (na - na // 2)
        pieces = {(0, 0): [own]}
        for b in range(1, nb):
            pieces[b, 0] = [self.shift(own, (0, b, 0))]
        for c in range(1, nc):
            pieces[0, c] = [self.shift(own, (0, 0, c))]
        for b in range(1, nb):
            for c in range(1, nc):
                first, second = halves_of(pieces[b, 0][0], pieces[0, c][0], half, after)
                first, second = self.shift(first, (0, 0, c)), self.shift(second, (0, b, 0))
                pieces[b, c] = [first, second]
        return sum((pieces[k] for k in self.offsets()), [])

    def scatter(self, pieces, rows, first=()):
        na, nb, nc = self.sizes
        half = rows * (na - na // 2)
        held, at = {}, 0
        for k in self.offsets():
            count = 2 if k[0] and k[1] else 1
            held[k] = pieces[at : at + count]
            at += count
        arrived = []
        for b in range(1, nb):
            more = [self.shift(held[b, c][0], (0, 0, c), back=True) for c in range(1, nc)]
            arrived.append((held[b, 0][0], more, 0, (0, b, 0)))
        for c in range(1, nc):
            more = [self.shift(held[b, c][1], (0, b, 0), back=True) for b in range(1, nb)]
            arrived.append((held[0, c][0], more, half, (0, 0, c)))
        arrived = [
            (add_half(piece, more, start, first), by) for piece, more, start, by in arrived
        ]
        halves = [piece for piece, _ in arrived]
        arrived = [self.shift(piece, by, back=True) for piece, by in arrived]
        after = yield halves
        blocks = add_blocks(held[0, 0][0], arrived, rows, after)
        yield self.last(blocks)

    def last(self, blocks):
        more = [self.shift(blocks[s], (s, 0, 0), back=True) for s in range(1, self.sizes[0])]
        return add_last(blocks[0], more)


def compiler_params():
    return pltpu.CompilerParams(vmem_limit_bytes=20 * 2**20)


def in_vmem(count):
    return [pl.BlockSpec(memory_space=pltpu.VMEM)] * count


ANYWHERE = pl.BlockSpec(memory_space=pl.ANY)
LAST = (((1,), (1,)), ((), ()))
PLAIN = (((1,), (0,)), ((), ()))


def dot(left, right, dims=PLAIN):
    return lax.dot_general(left, right, dims, preferred_element_type=jnp.float32)


def local_kernel(kernel, name, outs, args, after=(), flops=0, scalars=0, **more):
    args = list(args)
    in_specs = [pl.BlockSpec(memory_space=pltpu.SMEM)] * scalars + in_vmem(len(args) - scalars)
    count = len(args)
    body = kernel
    if after:
        args += after
        in_specs += [ANYWHERE] * len(after)

        def body(*refs):
            kernel(*refs[:count], *refs[count + len(after) :])

    moved = sum(x.size * x.dtype.itemsize for x in args[:count]) + sum(
        x.size * x.dtype.itemsize for x in outs
    )
    return pl.pallas_call(
        body,
        out_shape=tuple(outs),
        in_specs=in_specs,
        out_specs=tuple(in_vmem(len(outs))),
        compiler_params=compiler_params(),
        cost_estimate=pl.CostEstimate(flops=flops, bytes_accessed=moved, transcendentals=0),
        name=name,
        **more,
    )(*args)


def join(blocks):
    if blocks[0].shape[0] % 8:
        return jnp.concatenate(blocks, axis=0)

    def kernel(*refs):
        rows = jnp.concatenate([r[...].astype(jnp.float32) for r in refs[:-1]], axis=0)
        refs[-1][...] = rows.astype(jnp.bfloat16)

    one = jax.ShapeDtypeStruct((len(blocks) * blocks[0].shape[0], blocks[0].shape[1]), jnp.bfloat16)
    return local_kernel(kernel, "join", [one], blocks)[0]


def halves_of(first, second, half, after):
    if half % 16:
        return first[:half], second[half:]

    def kernel(first_ref, second_ref, upper_ref, lower_ref):
        upper_ref[...] = first_ref[:half]
        lower_ref[...] = second_ref[half:]

    width = first.shape[1]
    outs = [
        jax.ShapeDtypeStruct((half, width), first.dtype),
        jax.ShapeDtypeStruct((second.shape[0] - half, width), first.dtype),
    ]
    return local_kernel(kernel, "halves", outs, [first, second], after)


def add_half(piece, more, start, after):
    rows = more[0].shape[0]

    def add(whole, terms):
        there = whole[start : start + rows]
        for term in terms:
            there = there + term.astype(jnp.float32)
        parts = [whole[:start], there, whole[start + rows :]]
        return jnp.concatenate([p for p in parts if p.shape[0]], axis=0).astype(jnp.bfloat16)

    if rows % 16:
        return add(piece, more)

    def kernel(piece_ref, *refs):
        refs[-1][...] = add(piece_ref[...], [r[...] for r in refs[:-1]])

    one = jax.ShapeDtypeStruct(piece.shape, jnp.bfloat16)
    return local_kernel(kernel, "add_half", [one], [piece, *more], after)[0]


def add_blocks(piece, more, rows, after):
    count = piece.shape[0] // rows
    types = [jnp.float32] + [jnp.bfloat16] * (count - 1)

    def add(whole, terms):
        for term in terms:
            whole = whole + term.astype(jnp.float32)
        return [whole[s * rows : (s + 1) * rows].astype(t) for s, t in enumerate(types)]

    if rows % 8:
        return add(piece, more)

    def kernel(*refs):
        terms = [r[...] for r in refs[: 1 + len(more)]]
        for ref, block in zip(refs[1 + len(more) :], add(terms[0], terms[1:])):
            ref[...] = block

    outs = [jax.ShapeDtypeStruct((rows, piece.shape[1]), t) for t in types]
    return local_kernel(kernel, "add_blocks", outs, [piece, *more], after)


def add_last(block, more):
    def kernel(block_ref, *refs):
        total = block_ref[...]
        for ref in refs[:-1]:
            total = total + ref[...].astype(jnp.float32)
        refs[-1][...] = total

    one = jax.ShapeDtypeStruct(block.shape, jnp.float32)
    return local_kernel(kernel, "add_last", [one], [block, *more])[0]


class Place:
    def __init__(self, section, sections, index, shares):
        self.args = [section.reshape(1), index.reshape(1)]
        self.sections, self.shares = sections, shares

    def decodes(self, refs):
        return refs[0][0] >= self.sections // 2

    def columns(self, refs, k, width, start=0):
        share = jnp.bitwise_xor(lax.rem(refs[1][0], self.shares), k)
        return pl.ds(pl.multiple_of(start + share * width, HD), width)


def spread_stash(place, first, second):
    rows, width = first.shape
    part = width // 2 // place.shares

    def kernel(*refs):
        (first_ref, second_ref), out_refs = refs[2:4], refs[4:]
        for at in (0, 1):
            for k, ref in enumerate(out_refs):
                columns = place.columns(refs, k, part, at * (width // 2))
                one = first_ref[:, columns].astype(jnp.float32)
                two = second_ref[:, columns].astype(jnp.float32)
                mine = jnp.where(jnp.full((rows, 1), refs[0][0]) >= place.sections // 2, two, one)
                ref[:, at * part : (at + 1) * part] = mine.astype(jnp.bfloat16)

    outs = [jax.ShapeDtypeStruct((rows, 2 * part), jnp.bfloat16)] * place.shares
    return local_kernel(kernel, "spread_stash", outs, [*place.args, first, second], scalars=2)


def prepare(place, x, gain, cot, gate, slots, after):
    tokens, width = x.shape
    half = width // 2
    part = half // place.shares

    def kernel(*refs):
        x_ref, gain_ref, cot_ref, gate_ref, slot_ref = refs[2:7]
        copy_ref, q_refs, cot_refs, gates_ref = refs[7], refs[8:10], refs[10:12], refs[12]
        copy_ref[...] = x_ref[...]
        gates_ref[0:1] = gate_ref[...]
        gates_ref[1:2] = slot_ref[...].astype(jnp.float32)
        x = x_ref[...].astype(jnp.float32)
        inverse = lax.rsqrt(jnp.mean(x * x, axis=-1, keepdims=True) + 1e-06)
        for at, q_ref, part_ref in zip((0, half), q_refs, cot_refs):
            for k in range(place.shares):
                columns = place.columns(refs, k, part, at)
                x = x_ref[:, columns].astype(jnp.float32)
                q_ref[k] = (x * inverse * gain_ref[:, columns]).astype(jnp.bfloat16)
                part_ref[k] = cot_ref[:, columns]

    one = jax.ShapeDtypeStruct((place.shares, tokens, part), jnp.bfloat16)
    outs = [
        jax.ShapeDtypeStruct((tokens, width), x.dtype),
        *[one] * 4,
        jax.ShapeDtypeStruct((2, tokens), jnp.float32),
    ]
    args = [*place.args, x, gain, cot, gate, slots]
    return local_kernel(kernel, "prepare", outs, args, after, scalars=2)


def pick(place, first, second):
    def kernel(*refs):
        (first_ref, second_ref), out_refs = refs[2:4], refs[4:]

        @pl.when(place.decodes(refs))
        def _():
            for k, ref in enumerate(out_refs):
                ref[...] = second_ref[k]

        @pl.when(jnp.logical_not(place.decodes(refs)))
        def _():
            for k, ref in enumerate(out_refs):
                ref[...] = first_ref[k]

    outs = [jax.ShapeDtypeStruct(first.shape[1:], first.dtype)] * first.shape[0]
    return local_kernel(kernel, "pick", outs, [*place.args, first, second], scalars=2)


def pile(blocks):
    def kernel(*refs):
        for k, ref in enumerate(refs[:-1]):
            refs[-1][k] = ref[...]

    one = jax.ShapeDtypeStruct((len(blocks), *blocks[0].shape), blocks[0].dtype)
    return local_kernel(kernel, "pile", [one], blocks)[0]


def attend(stash, queries, after):
    tokens, width = queries[0].shape
    heads = width // HD
    rows = stash.shape[0]
    count = len(queries)

    def kernel(stash_ref, *refs):
        q_refs, mixed_refs, p_ref = refs[:count], refs[count : 2 * count], refs[2 * count]
        for h in range(heads):
            c = slice(h * HD, (h + 1) * HD)
            keys, values = stash_ref[:, c], stash_ref[:, width + h * HD : width + (h + 1) * HD]
            scores = [dot(keys, ref[:, c], LAST) * HD**-0.5 for ref in q_refs]
            e = [jnp.exp(s - jnp.max(s, axis=0, keepdims=True)) for s in scores]
            w = [x * (1.0 / jnp.sum(x, axis=0, keepdims=True)) for x in e]
            mixed = [dot(x.astype(jnp.bfloat16).T, values) for x in w]
            for k, (x, m) in enumerate(zip(w, mixed)):
                p_ref[h, k] = x
                mixed_refs[k][:, c] = m.astype(jnp.bfloat16)

    outs = [jax.ShapeDtypeStruct((tokens, width), jnp.bfloat16)] * count
    outs.append(jax.ShapeDtypeStruct((heads, count, rows, tokens), jnp.float32))
    *mixed, weights = local_kernel(
        kernel, "attend", outs, [stash, *queries], after, flops=4 * count * tokens * rows * width
    )
    return mixed, weights


def gradient(stash, queries, cots, p, blocks, after):
    tokens, width = queries[0].shape
    heads, count, rows, _ = p.shape
    height = rows // blocks

    def kernel(stash_ref, p_ref, *refs):
        q_refs, cot_refs, out_refs = refs[:count], refs[count : 2 * count], refs[2 * count :]
        for h in range(heads):
            c = slice(h * HD, (h + 1) * HD)
            there = slice(width + h * HD, width + (h + 1) * HD)
            values = stash_ref[:, there]
            q = [ref[:, c] for ref in q_refs]
            cot = [ref[:, c] for ref in cot_refs]
            w = [p_ref[h, k] for k in range(count)]
            dp = [dot(values, x, LAST) for x in cot]
            ds = [
                x * (d - jnp.sum(d * x, axis=0, keepdims=True)) * HD**-0.5 for d, x in zip(dp, w)
            ]
            upper = [x.astype(jnp.bfloat16) for x in ds]
            lower = [(x - u.astype(jnp.float32)).astype(jnp.bfloat16) for x, u in zip(ds, upper)]
            dk = sum(
                dot(jnp.concatenate([u, v], axis=1), jnp.concatenate([x, x], axis=0))
                for u, v, x in zip(upper, lower, q)
            )
            dv = sum(dot(x.astype(jnp.bfloat16), y) for x, y in zip(w, cot))
            for columns, grad in ((c, dk), (there, dv)):
                for s, ref in enumerate(out_refs):
                    ref[:, columns] = grad[s * height : (s + 1) * height].astype(ref.dtype)

    types = [jnp.float32] + [jnp.bfloat16] * (blocks - 1)
    outs = [jax.ShapeDtypeStruct((height, 2 * width), t) for t in types]
    return local_kernel(
        kernel, "gradient", outs, [stash, p, *queries, *cots], after,
        flops=10 * count * tokens * rows * width,
    )


def settle(place, x, first, second, norm_gain, gates):
    tokens, width = x.shape
    shares, _, part = first.shape

    def kernel(*refs):
        x_ref, first_ref, second_ref, norm_ref, gate_ref, res_ref, cap_ref, sel_ref = refs[2:]
        slots = lax.broadcasted_iota(jnp.int32, (CAP, tokens), 0).astype(jnp.float32)
        onehot = jnp.where(gate_ref[1:2] == slots, 1.0, 0.0).astype(jnp.bfloat16)
        attends = jnp.full((tokens, 1), refs[0][0]) >= place.sections // 2
        squares = jnp.zeros((CAP, 1), jnp.float32)
        for at, ref in ((0, first_ref), (width // 2, second_ref)):
            for k in range(shares):
                columns = place.columns(refs, k, part, at)
                mixed = jnp.where(attends, ref[k].astype(jnp.float32), 0.0)
                res = (x_ref[:, columns].astype(jnp.float32) + mixed).astype(jnp.bfloat16)
                res_ref[:, columns] = res
                chosen = dot(onehot, res)
                sel_ref[:, columns] = chosen
                squares = squares + jnp.sum(chosen * chosen, axis=-1, keepdims=True)
        inverse = lax.rsqrt(squares / width + 1e-06)
        cap_ref[...] = (sel_ref[...] * inverse * norm_ref[...]).astype(jnp.bfloat16)

    outs = [
        jax.ShapeDtypeStruct((tokens, width), jnp.bfloat16),
        jax.ShapeDtypeStruct((CAP, width), jnp.bfloat16),
    ]
    return local_kernel(
        kernel, "settle", outs, [*place.args, x, first, second, norm_gain, gates], scalars=2,
        scratch_shapes=[pltpu.VMEM((CAP, width), jnp.float32)],
    )


def add_line(blocks, rows, after):
    count = blocks[0].shape[0] // rows

    def add(terms):
        total = sum((t.astype(jnp.float32) for t in terms[1:]), terms[0])
        return [total[k * rows : (k + 1) * rows] for k in range(count)]

    if rows % 8:
        return add(blocks)

    def kernel(*refs):
        for ref, block in zip(refs[len(blocks) :], add([r[...] for r in refs[: len(blocks)]])):
            ref[...] = block

    outs = [jax.ShapeDtypeStruct((rows, blocks[0].shape[1]), jnp.float32)] * count
    return local_kernel(kernel, "add_line", outs, blocks, after)


def lay_out(place, first, second):
    shares, rows, part = first.shape
    part = part // 2
    half = shares * part

    def kernel(*refs):
        first_ref, second_ref, out_ref = refs[2:]
        decodes = jnp.full((rows, 1), refs[0][0]) >= place.sections // 2
        for at in (0, 1):
            for side, ref in ((0, first_ref), (half, second_ref)):
                for k in range(shares):
                    columns = place.columns(refs, k, part, at * 2 * half + side)
                    block = ref[k, :, at * part : (at + 1) * part]
                    out_ref[:, columns] = jnp.where(decodes, block, 0.0)

    one = jax.ShapeDtypeStruct((rows, 4 * half), jnp.float32)
    return local_kernel(kernel, "lay_out", [one], [*place.args, first, second], scalars=2)[0]


def expert(w1, w2, pieces, heights, types, after):
    width, units = w1.shape
    rows = sum(heights)
    count = len(pieces)
    steps = next(s for s in (4, 2, 1) if width % (s * 128) == 0)
    step = width // steps

    def kernel(w1_ref, w2_ref, *refs):
        in_refs, out_refs = refs[:count], refs[count:]
        parts = [slice(i * step, (i + 1) * step) for i in range(steps)]
        hidden = jnp.zeros((rows, units), jnp.float32)
        for c in parts:
            hidden = hidden + dot(jnp.concatenate([r[:, c] for r in in_refs], axis=0), w1_ref[c, :])
        hidden = jax.nn.gelu(hidden).astype(jnp.bfloat16)
        for c in parts:
            y = dot(hidden, w2_ref[:, c])
            at = 0
            for ref in out_refs:
                ref[:, c] = y[at : at + ref.shape[0]].astype(ref.dtype)
                at += ref.shape[0]

    outs = [jax.ShapeDtypeStruct((n, width), t) for n, t in zip(heights, types)]
    return local_kernel(
        kernel, "expert", outs, [w1, w2, *pieces], after, flops=4 * rows * width * units
    )


def finish(res, back, gates, after=()):
    one = jax.ShapeDtypeStruct(res.shape, jnp.bfloat16)
    tokens, width = res.shape
    step = next(s for s in (1280, 1024, 512, 256, 128) if width % s == 0)

    def kernel(res_ref, back_ref, gate_ref, out_ref):
        gate = jnp.broadcast_to(gate_ref[0:1], (CAP, tokens)).T[:, 0:1]
        slots = lax.broadcasted_iota(jnp.int32, (CAP, tokens), 0).astype(jnp.float32)
        onehot = jnp.where(gate_ref[1:2] == slots, 1.0, 0.0).T
        onehot = jnp.concatenate([onehot] * 3, axis=1).astype(jnp.bfloat16)
        for at in range(0, width, step):
            columns = slice(at, at + step)
            back = back_ref[:, columns]
            high = back.astype(jnp.bfloat16).astype(jnp.float32)
            middle = (back - high).astype(jnp.bfloat16).astype(jnp.float32)
            parts = jnp.concatenate([high, middle, back - high - middle], axis=0)
            moved = dot(onehot, parts.astype(jnp.bfloat16))
            here = res_ref[:, columns].astype(jnp.float32)
            out_ref[:, columns] = (here + gate * moved).astype(jnp.bfloat16)

    return local_kernel(
        kernel, "finish", [one], [res, back, gates], after, flops=50 * tokens * width
    )[0]


def local(
    layer_in, memory, cotangent, norm_gain, attn_gain, expert_in, expert_out, slot_index, gate_prob
):
    sections = lax.axis_size("section")
    section, index = lax.axis_index("section"), lax.axis_index("expert")
    grid = Grid(lax.axis_size("expert"))
    lines = grid.sizes[0]
    place = Place(section, sections, index, grid.size // lines)
    own_rows, _, width = memory[0].shape
    half = width // 2

    first = swapped(memory[0, :, :, :half].reshape(own_rows, width))
    second = memory[0, :, :, half:].reshape(own_rows, width)
    shares = join(grid.plane(spread_stash(place, first, second)))
    stash = grid.line(shares)
    current, q_first, q_second, cot_first, cot_second, gates = prepare(
        place, layer_in[0], attn_gain, cotangent[0], gate_prob, slot_index, [shares]
    )
    queries = grid.plane(pick(place, swapped(q_first), q_second))
    cots = pick(place, swapped(cot_first), cot_second)

    gates_before = passed_along(gates, "section", 1)
    early = [cots[0], gates_before]
    if sections == 2:
        residual_before = passed_along(current, "section", 1)
        early.append(residual_before)
    mixed, weights = attend(stash, queries, early)
    mixed = pile(grid.plane(mixed))
    residual, capacity = settle(place, current, to_decoder(mixed), mixed, norm_gain, gates)
    if sections != 2:
        residual_before = passed_along(residual, "section", 1)
    grads = gradient(stash, queries, grid.plane(cots), weights, lines, [capacity])
    gathered = grid.gather(capacity, [grads[0]])
    computed = expert(
        expert_in[0], expert_out[0], gathered, grid.heights(CAP), grid.types(), [residual_before]
    )
    results = grid.scatter(computed, CAP)
    sent = next(results)
    grads = [grads[0]] + [grid.shift(grads[s], (s, 0, 0), back=True) for s in range(1, lines)]
    grads = pile(grid.plane(add_line(grads, own_rows, sent)))
    returned = results.send([])
    returned_before = passed_along(returned, "section", 1)
    output = finish(residual, returned, gates)
    arriving = finish(residual_before, returned_before, gates_before)
    total_grad = lay_out(place, to_decoder(grads), grads).reshape(own_rows, 2, width)
    return (output[None], arriving[None], total_grad[None])


def solution(mesh):
    placed = (
        P("section", "expert", None),
        P("section", "expert", None, None),
        P("section", "expert", None),
        P("section", None),
        P("section", None),
        P("section", None, "expert"),
        P("section", "expert", None),
        P("section", "expert"),
        P("section", "expert"),
    )
    return jax.shard_map(
        local,
        mesh=mesh,
        in_specs=placed,
        out_specs=(
            P("section", "expert", None),
            P("section", "expert", None),
            P("section", "expert", None, None),
        ),
        check_vma=False,
    )
```

time: 119 us -> 131 us (1.10)
  waiting for transfers between devices: 41.7 us -> 67.3 us
  starting transfers between devices: 52.2 us -> 43.9 us
  Pallas kernels: 16.1 us -> 11.2 us
    ppermute x0 -> x2, waiting for transfers between devices: none -> 15.4 us  [to_decoder(): lax.ppermute(block, 'section', [(i, i + apart) for i in range(apart)])]
    ppermute x28 -> x35, waiting for transfers between devices: 38.6 us -> 48.5 us  [shift(): return lax.ppermute(block, 'expert', route)]
    ppermute x5 -> x3, starting transfers between devices: 11 us -> 2.41 us  [swapped(): lax.ppermute(block, 'section', [(i, (i + sections // 2) % sections) for i...]
    pallas_call x1 -> x0, Pallas kernels: 5.67 us -> none  [expert(): pl.pallas_call(kernel, out_shape=tuple((jax.ShapeDtypeStruct((n, width),...]
    ppermute x0 -> x2, starting transfers between devices: none -> 2.58 us  [to_decoder(): lax.ppermute(block, 'section', [(i, i + apart) for i in range(apart)])]
    ppermute x28 -> x35, starting transfers between devices: 37.4 us -> 34.9 us  [shift(): return lax.ppermute(block, 'expert', route)]
    unnamed x26 -> x22, local copies, waits for them, and re-layouts: 4.58 us -> 6.73 us
    ppermute x3, waiting for transfers between devices: 0.81 us -> 2.28 us  [passed_along(): return lax.ppermute(block, axis, route)]
  transfers between devices with their start and end apart: 36 -> 43, of which waited for: 16 -> 23; matrix products, arithmetic and copies ran while one was open for 2% -> 1% of each run, Pallas kernels for 9% -> 3%
where the time goes in v2:
time: 131 us; the launch traced here: 130 us
  waiting for transfers between devices  67.3 us (51%)
  starting transfers between devices  43.9 us (34%)
  Pallas kernels  11.2 us (9%)
  local copies, waits for them, and re-layouts  6.73 us (5%)
    ppermute x35, waiting for transfers between devices, shift(): return lax.ppermute(block, 'expert', route)  48.5 us
    ppermute x35, starting transfers between devices, shift(): return lax.ppermute(block, 'expert', route)  34.9 us
    ppermute x2, waiting for transfers between devices, to_decoder(): lax.ppermute(block, 'section', [(i, i + apart) for i in range(apart)])  15.4 us
    pallas_call x22, Pallas kernels, local_kernel(): pl.pallas_call(body, out_shape=tuple(outs), in_specs=in_specs, out_specs=...  11.2 us
    unnamed x22, local copies, waits for them, and re-layouts  6.73 us
    ppermute x3, starting transfers between devices, passed_along(): return lax.ppermute(block, axis, route)  4 us
  transfers between devices with their start and end apart: 43, of which 23 were waited for; matrix products, arithmetic and copies ran while one was open for 1% of the time, Pallas kernels for 3%

profile of v2, /device:TPU:1, one launch (start us, length us, event | category | flops | bytes accessed | tf_op | source)
XLA Modules:
  0.0 130.1 jit_solution(378513260769798900)
XLA Ops:
  0.6 1.0 slice_bitcast_fusion
  1.8 1.2 collective-permute-done.refs_2_
  3.1 2.4 %collective-permute-start.1 = (bf16[8,1280]{1,0:T(8,128)(2,1)S(1)}, bf16[8,1280]{1,0:T(8,128)(2,1)S(1)}, u32[]{:S(2)}, u32[]{:S(2)}) collective-permute-start(bf16[8,1280]{1,0:T(8,128)(2,1)S(1)} %get-tuple-element.48), channel_id=1, source_target_pairs={{0,1},{1,0},{2,3},{3,2},{4,5},{5,4},{6,7},{7,6},{8,9},{9,8},{10,11... | collective-permute-start | bytes 61448 | tf_op jit(solution)/shard_map/ppermute | solution.py:49
  5.5 1.2 collective-permute-start.2
  6.8 1.4 %collective-permute-done.2.refs_2_ = bf16[8,1280]{1,0:T(8,128)(2,1)S(1)} collective-permute-done((bf16[8,1280]{1,0:T(8,128)(2,1)S(1)}, bf16[8,1280]{1,0:T(8,128)(2,1)S(1)}, u32[]{:S(2)}, u32[]{:S(2)}) %collective-permute-start.2) | collective-permute-done | bytes 20512 | tf_op jit(solution)/shard_map/ppermute | solution.py:49
  8.1 2.1 %collective-permute-done.3.refs_3_ = bf16[8,1280]{1,0:T(8,128)(2,1)S(1)} collective-permute-done((bf16[8,1280]{1,0:T(8,128)(2,1)S(1)}, bf16[8,1280]{1,0:T(8,128)(2,1)S(1)}, u32[]{:S(2)}, u32[]{:S(2)}) %collective-permute-start.3) | collective-permute-done | bytes 20512 | tf_op jit(solution)/shard_map/ppermute | solution.py:49
  10.3 1.3 %copy-done.1 = bf16[1,128,5120]{2,1,0:T(8,128)(2,1)S(1)} copy-done((bf16[1,128,5120]{2,1,0:T(8,128)(2,1)S(1)}, bf16[1,128,5120]{2,1,0:T(8,128)(2,1)}, u32[]{:S(2)}) %copy-start.1) | copy-done | bytes 1310744
  11.6 1.3 %copy-done.2 = bf16[1,128,5120]{2,1,0:T(8,128)(2,1)S(1)} copy-done((bf16[1,128,5120]{2,1,0:T(8,128)(2,1)S(1)}, bf16[1,128,5120]{2,1,0:T(8,128)(2,1)}, u32[]{:S(2)}) %copy-start.2) | copy-done | bytes 1310744
  12.9 0.7 copy-done.3
  13.6 0.7 copy-done.5
  14.3 0.7 copy-done.6
  14.9 0.8 prepare.1
  15.8 1.4 %collective-permute-start.13 = (bf16[128,5120]{1,0:T(8,128)(2,1)S(1)}, bf16[128,5120]{1,0:T(8,128)(2,1)S(1)}, u32[]{:S(2)}, u32[]{:S(2)}) collective-permute-start(bf16[128,5120]{1,0:T(8,128)(2,1)S(1)} %get-tuple-element.51.refs_2_), channel_id=1, source_target_pairs={{0,16},{1,17},{2,18},{3,19},{4,20},{5,21},{6,22},{7,23},{8,24},{9,... | collective-permute-start | bytes 3932168 | tf_op jit(solution)/shard_map/ppermute | solution.py:17
  17.2 2.2 %collective-permute-start.7 = (bf16[4,128,640]{2,1,0:T(8,128)(2,1)S(1)}, bf16[4,128,640]{2,1,0:T(8,128)(2,1)S(1)}, u32[]{:S(2)}, u32[]{:S(2)}) collective-permute-start(bf16[4,128,640]{2,1,0:T(8,128)(2,1)S(1)} %get-tuple-element.52), channel_id=1, source_target_pairs={{0,16},{16,0},{1,17},{17,1},{2,18},{18,2},{3,19},{19,3},{4,20},{20... | collective-permute-start | bytes 1966088 | tf_op jit(solution)/shard_map/ppermute | solution.py:22
  19.5 3.3 %collective-permute-start.6 = (bf16[32,1280]{1,0:T(8,128)(2,1)S(1)}, bf16[32,1280]{1,0:T(8,128)(2,1)S(1)}, u32[]{:S(2)}, u32[]{:S(2)}) collective-permute-start(bf16[32,1280]{1,0:T(8,128)(2,1)S(1)} %join.3.refs_7_.refs_0_), channel_id=1, source_target_pairs={{0,12},{1,13},{2,14},{3,15},{4,8},{5,9},{6,10},{7,11},{8,4},{9,5},... | collective-permute-start | bytes 245768 | tf_op jit(solution)/shard_map/ppermute | solution.py:49
  22.8 1.2 collective-permute-start.4
  24.1 0.9 collective-permute-done.6.refs_3_
  25.2 4.2 %collective-permute-done.5.refs_2_ = bf16[32,1280]{1,0:T(8,128)(2,1)S(1)} collective-permute-done((bf16[32,1280]{1,0:T(8,128)(2,1)S(1)}, bf16[32,1280]{1,0:T(8,128)(2,1)S(1)}, u32[]{:S(2)}, u32[]{:S(2)}) %collective-permute-start.5) | collective-permute-done | bytes 81952 | tf_op jit(solution)/shard_map/ppermute | solution.py:49
  29.6 1.2 collective-permute-start.10
  30.9 1.3 collective-permute-start.12
  32.2 2.3 %collective-permute-done.12.refs_6_.gate_ref = f32[2,128]{1,0:T(2,128)S(1)} collective-permute-done((f32[2,128]{1,0:T(2,128)S(1)}, f32[2,128]{1,0:T(2,128)S(1)}, u32[]{:S(2)}, u32[]{:S(2)}) %collective-permute-start.12) | collective-permute-done | bytes 1056 | tf_op jit(solution)/shard_map/ppermute | solution.py:17
  34.5 3.3 %collective-permute-done.9.refs_3_.refs_4_ = bf16[128,640]{1,0:T(8,128)(2,1)S(1)} collective-permute-done((bf16[128,640]{1,0:T(8,128)(2,1)S(1)}, bf16[128,640]{1,0:T(8,128)(2,1)S(1)}, u32[]{:S(2)}, u32[]{:S(2)}) %collective-permute-start.9) | collective-permute-done | bytes 163872 | tf_op jit(solution)/shard_map/ppermute | solution.py:49
  37.9 1.8 %attend.1 = (bf16[128,640]{1,0:T(8,128)(2,1)S(1)}, bf16[128,640]{1,0:T(8,128)(2,1)S(1)}, bf16[128,640]{1,0:T(8,128)(2,1)S(1)}, bf16[128,640]{1,0:T(8,128)(2,1)S(1)}, f32[5,4,128,128]{3,2,1,0:T(8,128)S(1)}) custom-call(bf16[128,1280]{1,0:T(8,128)(2,1)S(1)} %join.4.refs_0_, bf16[128,640]{1,0:T(8,128)(2,1)S(1)} %get-tuple-element.54.refs_1_.refs_2_, ...), custom_call_target="tpu_custom_call" | custom-call | flops 167772160 | bytes 2949120 | tf_op jit(solution)/shard_map/attend/pallas_call | solution.py:154
  40.0 2.4 %collective-permute-start.16 = (bf16[128,640]{1,0:T(8,128)(2,1)S(1)}, bf16[128,640]{1,0:T(8,128)(2,1)S(1)}, u32[]{:S(2)}, u32[]{:S(2)}) collective-permute-start(bf16[128,640]{1,0:T(8,128)(2,1)S(1)} %get-tuple-element.65), channel_id=1, source_target_pairs={{0,3},{1,2},{2,1},{3,0},{4,7},{5,6},{6,5},{7,4},{8,11},{9,10},{10,... | collective-permute-start | bytes 491528 | tf_op jit(solution)/shard_map/ppermute | solution.py:49
  42.4 1.5 %collective-permute-done.14.refs_1_ = bf16[128,640]{1,0:T(8,128)(2,1)S(1)} collective-permute-done((bf16[128,640]{1,0:T(8,128)(2,1)S(1)}, bf16[128,640]{1,0:T(8,128)(2,1)S(1)}, u32[]{:S(2)}, u32[]{:S(2)}) %collective-permute-start.14) | collective-permute-done | bytes 163872 | tf_op jit(solution)/shard_map/ppermute | solution.py:49
  43.9 2.8 %collective-permute-done.15.refs_2_ = bf16[128,640]{1,0:T(8,128)(2,1)S(1)} collective-permute-done((bf16[128,640]{1,0:T(8,128)(2,1)S(1)}, bf16[128,640]{1,0:T(8,128)(2,1)S(1)}, u32[]{:S(2)}, u32[]{:S(2)}) %collective-permute-start.15) | collective-permute-done | bytes 163872 | tf_op jit(solution)/shard_map/ppermute | solution.py:49
  46.7 1.3 collective-permute-start.17
  48.0 5.0 %collective-permute-done.17.refs_3_ = bf16[4,128,640]{2,1,0:T(8,128)(2,1)S(1)} collective-permute-done((bf16[4,128,640]{2,1,0:T(8,128)(2,1)S(1)}, bf16[4,128,640]{2,1,0:T(8,128)(2,1)S(1)}, u32[]{:S(2)}, u32[]{:S(2)}) %collective-permute-start.17) | collective-permute-done | bytes 655392 | tf_op jit(solution)/shard_map/ppermute | solution.py:27
  53.0 0.7 settle.1
  53.7 2.3 %collective-permute-start.20 = (bf16[8,5120]{1,0:T(8,128)(2,1)S(1)}, bf16[8,5120]{1,0:T(8,128)(2,1)S(1)}, u32[]{:S(2)}, u32[]{:S(2)}) collective-permute-start(bf16[8,5120]{1,0:T(8,128)(2,1)S(1)} %get-tuple-element.67.refs_0_.refs_10_), channel_id=1, source_target_pairs={{0,12},{1,13},{2,14},{3,15},{4,8},{5,9},{6,10},{7,11},{8,4},{9,5},... | collective-permute-start | bytes 245768 | tf_op jit(solution)/shard_map/ppermute | solution.py:49
  56.0 1.3 %collective-permute-start.18 = (bf16[8,5120]{1,0:T(8,128)(2,1)S(1)}, bf16[8,5120]{1,0:T(8,128)(2,1)S(1)}, u32[]{:S(2)}, u32[]{:S(2)}) collective-permute-start(bf16[8,5120]{1,0:T(8,128)(2,1)S(1)} %get-tuple-element.67.refs_0_.refs_10_), channel_id=1, source_target_pairs={{0,4},{1,5},{2,6},{3,7},{4,0},{5,1},{6,2},{7,3},{8,12},{9,13},{10,... | collective-permute-start | bytes 245768 | tf_op jit(solution)/shard_map/ppermute | solution.py:49
  57.3 2.2 %collective-permute-done.20.refs_3_ = bf16[8,5120]{1,0:T(8,128)(2,1)S(1)} collective-permute-done((bf16[8,5120]{1,0:T(8,128)(2,1)S(1)}, bf16[8,5120]{1,0:T(8,128)(2,1)S(1)}, u32[]{:S(2)}, u32[]{:S(2)}) %collective-permute-start.20) | collective-permute-done | bytes 81952 | tf_op jit(solution)/shard_map/ppermute | solution.py:49
  59.5 4.0 %collective-permute-done.19.refs_2_ = bf16[8,5120]{1,0:T(8,128)(2,1)S(1)} collective-permute-done((bf16[8,5120]{1,0:T(8,128)(2,1)S(1)}, bf16[8,5120]{1,0:T(8,128)(2,1)S(1)}, u32[]{:S(2)}, u32[]{:S(2)}) %collective-permute-start.19) | collective-permute-done | bytes 81952 | tf_op jit(solution)/shard_map/ppermute | solution.py:49
  63.5 1.0 collective-permute-start.22
  64.5 1.1 collective-permute-start.21
  66.5 1.7 %collective-permute-start.25 = (bf16[128,640]{1,0:T(8,128)(2,1)S(1)}, bf16[128,640]{1,0:T(8,128)(2,1)S(1)}, u32[]{:S(2)}, u32[]{:S(2)}) collective-permute-start(bf16[128,640]{1,0:T(8,128)(2,1)S(1)} %get-tuple-element.71), channel_id=1, source_target_pairs={{0,3},{1,2},{2,1},{3,0},{4,7},{5,6},{6,5},{7,4},{8,11},{9,10},{10,... | collective-permute-start | bytes 491528 | tf_op jit(solution)/shard_map/ppermute | solution.py:49
  68.2 8.3 %collective-permute-done.23.refs_7_ = bf16[128,640]{1,0:T(8,128)(2,1)S(1)} collective-permute-done((bf16[128,640]{1,0:T(8,128)(2,1)S(1)}, bf16[128,640]{1,0:T(8,128)(2,1)S(1)}, u32[]{:S(2)}, u32[]{:S(2)}) %collective-permute-start.23) | collective-permute-done | bytes 163872 | tf_op jit(solution)/shard_map/ppermute | solution.py:49
  76.5 3.8 %collective-permute-done.25.refs_9_ = bf16[128,640]{1,0:T(8,128)(2,1)S(1)} collective-permute-done((bf16[128,640]{1,0:T(8,128)(2,1)S(1)}, bf16[128,640]{1,0:T(8,128)(2,1)S(1)}, u32[]{:S(2)}, u32[]{:S(2)}) %collective-permute-start.25) | collective-permute-done | bytes 163872 | tf_op jit(solution)/shard_map/ppermute | solution.py:49
  80.2 1.6 %gradient.1 = (f32[32,1280]{1,0:T(8,128)S(1)}, bf16[32,1280]{1,0:T(8,128)(2,1)S(1)}, bf16[32,1280]{1,0:T(8,128)(2,1)S(1)}, bf16[32,1280]{1,0:T(8,128)(2,1)S(1)}) custom-call(bf16[128,1280]{1,0:T(8,128)(2,1)S(1)} %join.4.refs_0_, f32[5,4,128,128]{3,2,1,0:T(8,128)S(1)} %get-tuple-element.68.refs_1_, bf16[128,640]{1,0:T(8,128)(2,1)S(1)} %get-tuple-element.54.refs_1_.refs_2_, ...), custom_call_target="tpu_custom_call" | custom-call | flops 419430400 | bytes 3358720 | tf_op jit(solution)/shard_map/gradient/pallas_call | solution.py:154
  81.9 1.3 collective-permute-start.26
  83.2 0.8 collective-permute-start.27
  83.9 2.2 %collective-permute-done.26.refs_5_ = bf16[16,5120]{1,0:T(8,128)(2,1)S(1)} collective-permute-done((bf16[16,5120]{1,0:T(8,128)(2,1)S(1)}, bf16[16,5120]{1,0:T(8,128)(2,1)S(1)}, u32[]{:S(2)}, u32[]{:S(2)}) %collective-permute-start.26) | collective-permute-done | bytes 163872 | tf_op jit(solution)/shard_map/ppermute | solution.py:49
  86.1 1.5 %collective-permute-done.27.refs_6_ = bf16[16,5120]{1,0:T(8,128)(2,1)S(1)} collective-permute-done((bf16[16,5120]{1,0:T(8,128)(2,1)S(1)}, bf16[16,5120]{1,0:T(8,128)(2,1)S(1)}, u32[]{:S(2)}, u32[]{:S(2)}) %collective-permute-start.27) | collective-permute-done | bytes 163872 | tf_op jit(solution)/shard_map/ppermute | solution.py:49
  87.6 2.4 %expert.1 = (f32[32,5120]{1,0:T(8,128)S(1)}, f32[32,5120]{1,0:T(8,128)S(1)}, f32[32,5120]{1,0:T(8,128)S(1)}, bf16[16,5120]{1,0:T(8,128)(2,1)S(1)}, bf16[16,5120]{1,0:T(8,128)(2,1)S(1)}) custom-call(bf16[5120,640]{1,0:T(8,128)(2,1)S(1)} %bitcast.19, bf16[640,5120]{1,0:T(8,128)(2,1)S(1)} %bitcast.20, bf16[32,5120]{1,0:T(8,128)(2,1)S(1)} %join.5.refs_2_, ...), custom_call_target="tpu_custom_call" | custom-call | flops 1677721600 | bytes 16711680 | tf_op jit(solution)/shard_map/expert/pallas_call | solution.py:154
  90.0 0.8 collective-permute-start.30
  91.2 3.0 %collective-permute-done.30.refs_0_ = bf16[16,5120]{1,0:T(8,128)(2,1)S(1)} collective-permute-done((bf16[16,5120]{1,0:T(8,128)(2,1)S(1)}, bf16[16,5120]{1,0:T(8,128)(2,1)S(1)}, u32[]{:S(2)}, u32[]{:S(2)}) %collective-permute-start.30) | collective-permute-done | bytes 163872 | tf_op jit(solution)/shard_map/ppermute | solution.py:49
  95.0 0.8 collective-permute-start.29
  95.8 2.5 %collective-permute-start.37 = (bf16[32,1280]{1,0:T(8,128)(2,1)S(1)}, bf16[32,1280]{1,0:T(8,128)(2,1)S(1)}, u32[]{:S(2)}, u32[]{:S(2)}) collective-permute-start(bf16[32,1280]{1,0:T(8,128)(2,1)S(1)} %get-tuple-element.85), channel_id=1, source_target_pairs={{8,0},{9,1},{10,2},{11,3},{12,4},{13,5},{14,6},{15,7},{0,8},{1,9},... | collective-permute-start | bytes 245768 | tf_op jit(solution)/shard_map/ppermute | solution.py:49
  98.3 1.1 collective-permute-start.38
  99.4 0.7 collective-permute-done.37.refs_2_
  100.1 3.3 %collective-permute-done.38.refs_3_ = bf16[32,1280]{1,0:T(8,128)(2,1)S(1)} collective-permute-done((bf16[32,1280]{1,0:T(8,128)(2,1)S(1)}, bf16[32,1280]{1,0:T(8,128)(2,1)S(1)}, u32[]{:S(2)}, u32[]{:S(2)}) %collective-permute-start.38) | collective-permute-done | bytes 81952 | tf_op jit(solution)/shard_map/ppermute | solution.py:49
  103.4 1.0 collective-permute-start.39
  104.6 1.4 %collective-permute-start.33 = (bf16[8,5120]{1,0:T(8,128)(2,1)S(1)}, bf16[8,5120]{1,0:T(8,128)(2,1)S(1)}, u32[]{:S(2)}, u32[]{:S(2)}) collective-permute-start(bf16[8,5120]{1,0:T(8,128)(2,1)S(1)} %get-tuple-element.82), channel_id=1, source_target_pairs={{8,0},{9,1},{10,2},{11,3},{12,4},{13,5},{14,6},{15,7},{0,8},{1,9},... | collective-permute-start | bytes 245768 | tf_op jit(solution)/shard_map/ppermute | solution.py:49
  105.9 2.2 %collective-permute-start.34 = (bf16[8,5120]{1,0:T(8,128)(2,1)S(1)}, bf16[8,5120]{1,0:T(8,128)(2,1)S(1)}, u32[]{:S(2)}, u32[]{:S(2)}) collective-permute-start(bf16[8,5120]{1,0:T(8,128)(2,1)S(1)} %get-tuple-element.83), channel_id=1, source_target_pairs={{12,0},{13,1},{14,2},{15,3},{8,4},{9,5},{10,6},{11,7},{4,8},{5,9},... | collective-permute-start | bytes 245768 | tf_op jit(solution)/shard_map/ppermute | solution.py:49
  108.1 0.7 collective-permute-start.40
  108.8 1.1 collective-permute-start.41
  109.9 1.4 %collective-permute-done.40.refs_2_ = f32[8,1280]{1,0:T(8,128)S(1)} collective-permute-done((f32[8,1280]{1,0:T(8,128)S(1)}, f32[8,1280]{1,0:T(8,128)S(1)}, u32[]{:S(2)}, u32[]{:S(2)}) %collective-permute-start.40) | collective-permute-done | bytes 40992 | tf_op jit(solution)/shard_map/ppermute | solution.py:49
  111.2 1.3 %collective-permute-done.41.refs_3_ = f32[8,1280]{1,0:T(8,128)S(1)} collective-permute-done((f32[8,1280]{1,0:T(8,128)S(1)}, f32[8,1280]{1,0:T(8,128)S(1)}, u32[]{:S(2)}, u32[]{:S(2)}) %collective-permute-start.41) | collective-permute-done | bytes 40992 | tf_op jit(solution)/shard_map/ppermute | solution.py:49
  112.6 1.3 collective-permute-start.42
  113.9 1.3 collective-permute-start.35
  115.2 10.4 %collective-permute-done.42.refs_2_ = f32[4,8,1280]{2,1,0:T(8,128)S(1)} collective-permute-done((f32[4,8,1280]{2,1,0:T(8,128)S(1)}, f32[4,8,1280]{2,1,0:T(8,128)S(1)}, u32[]{:S(2)}, u32[]{:S(2)}) %collective-permute-start.42) | collective-permute-done | bytes 163872 | tf_op jit(solution)/shard_map/ppermute | solution.py:27
  125.7 1.0 copy.12
  126.6 1.7 %finish.2 = bf16[128,5120]{1,0:T(8,128)(2,1)} custom-call(bf16[128,5120]{1,0:T(8,128)(2,1)S(1)} %get-tuple-element.66.res_ref, f32[8,5120]{1,0:T(8,128)S(1)} %add_last.1.back_ref, f32[2,128]{1,0:T(2,128)S(1)} %get-tuple-element.61.refs_6_.gate_ref), custom_call_target="tpu_custom_call" | custom-call | flops 32768000 | bytes 2786304 | tf_op jit(solution)/shard_map/finish/pallas_call | solution.py:154
  128.4 1.7 %finish.3 = bf16[128,5120]{1,0:T(8,128)(2,1)} custom-call(bf16[128,5120]{1,0:T(8,128)(2,1)S(1)} %collective-permute-done.13.refs_7_.res_ref, f32[8,5120]{1,0:T(8,128)S(1)} %collective-permute-done.35.back_ref, f32[2,128]{1,0:T(2,128)S(1)} %collective-permute-done.12.refs_6_.gate_ref), custom_call_target="tpu_custom_call" | custom-call | flops 32768000 | bytes 2786304 | tf_op jit(solution)/shard_map/finish/pallas_call | solution.py:154
  (67 shorter events, 3.9 us)
Async XLA Ops:
  1.7 1.3 %collective-permute-start = (bf16[8,5120]{1,0:T(8,128)(2,1)S(1)}, bf16[8,5120]{1,0:T(8,128)(2,1)S(1)}, u32[]{:S(2)}, u32[]{:S(2)}) collective-permute-start(bf16[8,5120]{1,0:T(8,128)(2,1)S(1)} %bitcast.27), channel_id=1, source_target_pairs={{0,16},{16,0},{1,17},{17,1},{2,18},{18,2},{3,19},{19,3},{4,20},{20... | collective-permute-start | bytes 245768 | tf_op jit(solution)/shard_map/ppermute | solution.py:22
  3.1 3.7 %collective-permute-start.1 = (bf16[8,1280]{1,0:T(8,128)(2,1)S(1)}, bf16[8,1280]{1,0:T(8,128)(2,1)S(1)}, u32[]{:S(2)}, u32[]{:S(2)}) collective-permute-start(bf16[8,1280]{1,0:T(8,128)(2,1)S(1)} %get-tuple-element.48), channel_id=1, source_target_pairs={{0,1},{1,0},{2,3},{3,2},{4,5},{5,4},{6,7},{7,6},{8,9},{9,8},{10,11... | collective-permute-start | bytes 61448 | tf_op jit(solution)/shard_map/ppermute | solution.py:49
  5.5 2.6 %collective-permute-start.2 = (bf16[8,1280]{1,0:T(8,128)(2,1)S(1)}, bf16[8,1280]{1,0:T(8,128)(2,1)S(1)}, u32[]{:S(2)}, u32[]{:S(2)}) collective-permute-start(bf16[8,1280]{1,0:T(8,128)(2,1)S(1)} %get-tuple-element.49), channel_id=1, source_target_pairs={{0,2},{1,3},{2,0},{3,1},{4,6},{5,7},{6,4},{7,5},{8,10},{9,11},{10,... | collective-permute-start | bytes 61448 | tf_op jit(solution)/shard_map/ppermute | solution.py:49
  6.7 3.5 %collective-permute-start.3 = (bf16[8,1280]{1,0:T(8,128)(2,1)S(1)}, bf16[8,1280]{1,0:T(8,128)(2,1)S(1)}, u32[]{:S(2)}, u32[]{:S(2)}) collective-permute-start(bf16[8,1280]{1,0:T(8,128)(2,1)S(1)} %get-tuple-element.50), channel_id=1, source_target_pairs={{0,3},{1,2},{2,1},{3,0},{4,7},{5,6},{6,5},{7,4},{8,11},{9,10},{10,... | collective-permute-start | bytes 61448 | tf_op jit(solution)/shard_map/ppermute | solution.py:49
  10.3 1.3 %copy-start.1 = (bf16[1,128,5120]{2,1,0:T(8,128)(2,1)S(1)}, bf16[1,128,5120]{2,1,0:T(8,128)(2,1)}, u32[]{:S(2)}) copy-start(bf16[1,128,5120]{2,1,0:T(8,128)(2,1)} %param.9) | copy-start | bytes 3932164
  11.6 1.3 %copy-start.2 = (bf16[1,128,5120]{2,1,0:T(8,128)(2,1)S(1)}, bf16[1,128,5120]{2,1,0:T(8,128)(2,1)}, u32[]{:S(2)}) copy-start(bf16[1,128,5120]{2,1,0:T(8,128)(2,1)} %param.11) | copy-start | bytes 3932164
  12.9 0.7 copy-start.3
  13.6 0.7 copy-start.5
  14.3 0.7 copy-start.6
  14.9 72.7 %slice-start = ((s8[6553600]{0:T(1024)(128)(4,1)}), s8[4194304]{0:T(1024)(128)(4,1)S(1)}, s32[]{:S(2)}) async-start(s8[6553600]{0:T(1024)(128)(4,1)} %bitcast.17), calls=%async_computation | async-start | bytes 8388608
  15.8 22.1 %collective-permute-start.13 = (bf16[128,5120]{1,0:T(8,128)(2,1)S(1)}, bf16[128,5120]{1,0:T(8,128)(2,1)S(1)}, u32[]{:S(2)}, u32[]{:S(2)}) collective-permute-start(bf16[128,5120]{1,0:T(8,128)(2,1)S(1)} %get-tuple-element.51.refs_2_), channel_id=1, source_target_pairs={{0,16},{1,17},{2,18},{3,19},{4,20},{5,21},{6,22},{7,23},{8,24},{9,... | collective-permute-start | bytes 3932168 | tf_op jit(solution)/shard_map/ppermute | solution.py:17
  17.2 5.6 %collective-permute-start.7 = (bf16[4,128,640]{2,1,0:T(8,128)(2,1)S(1)}, bf16[4,128,640]{2,1,0:T(8,128)(2,1)S(1)}, u32[]{:S(2)}, u32[]{:S(2)}) collective-permute-start(bf16[4,128,640]{2,1,0:T(8,128)(2,1)S(1)} %get-tuple-element.52), channel_id=1, source_target_pairs={{0,16},{16,0},{1,17},{17,1},{2,18},{18,2},{3,19},{19,3},{4,20},{20... | collective-permute-start | bytes 1966088 | tf_op jit(solution)/shard_map/ppermute | solution.py:22
  19.4 11.5 %collective-permute-start.11 = (bf16[4,128,640]{2,1,0:T(8,128)(2,1)S(1)}, bf16[4,128,640]{2,1,0:T(8,128)(2,1)S(1)}, u32[]{:S(2)}, u32[]{:S(2)}) collective-permute-start(bf16[4,128,640]{2,1,0:T(8,128)(2,1)S(1)} %get-tuple-element.58), channel_id=1, source_target_pairs={{0,16},{16,0},{1,17},{17,1},{2,18},{18,2},{3,19},{19,3},{4,20},{20... | collective-permute-start | bytes 1966088 | tf_op jit(solution)/shard_map/ppermute | solution.py:22
  19.5 5.5 %collective-permute-start.6 = (bf16[32,1280]{1,0:T(8,128)(2,1)S(1)}, bf16[32,1280]{1,0:T(8,128)(2,1)S(1)}, u32[]{:S(2)}, u32[]{:S(2)}) collective-permute-start(bf16[32,1280]{1,0:T(8,128)(2,1)S(1)} %join.3.refs_7_.refs_0_), channel_id=1, source_target_pairs={{0,12},{1,13},{2,14},{3,15},{4,8},{5,9},{6,10},{7,11},{8,4},{9,5},... | collective-permute-start | bytes 245768 | tf_op jit(solution)/shard_map/ppermute | solution.py:49
  22.8 6.6 %collective-permute-start.5 = (bf16[32,1280]{1,0:T(8,128)(2,1)S(1)}, bf16[32,1280]{1,0:T(8,128)(2,1)S(1)}, u32[]{:S(2)}, u32[]{:S(2)}) collective-permute-start(bf16[32,1280]{1,0:T(8,128)(2,1)S(1)} %join.3.refs_7_.refs_0_), channel_id=1, source_target_pairs={{0,8},{1,9},{2,10},{3,11},{4,12},{5,13},{6,14},{7,15},{8,0},{9,1},... | collective-permute-start | bytes 245768 | tf_op jit(solution)/shard_map/ppermute | solution.py:49
  22.8 6.8 %collective-permute-start.4 = (bf16[32,1280]{1,0:T(8,128)(2,1)S(1)}, bf16[32,1280]{1,0:T(8,128)(2,1)S(1)}, u32[]{:S(2)}, u32[]{:S(2)}) collective-permute-start(bf16[32,1280]{1,0:T(8,128)(2,1)S(1)} %join.3.refs_7_.refs_0_), channel_id=1, source_target_pairs={{0,4},{1,5},{2,6},{3,7},{4,0},{5,1},{6,2},{7,3},{8,12},{9,13},{10,... | collective-permute-start | bytes 245768 | tf_op jit(solution)/shard_map/ppermute | solution.py:49
  25.0 9.5 %collective-permute-start.8 = (bf16[128,640]{1,0:T(8,128)(2,1)S(1)}, bf16[128,640]{1,0:T(8,128)(2,1)S(1)}, u32[]{:S(2)}, u32[]{:S(2)}) collective-permute-start(bf16[128,640]{1,0:T(8,128)(2,1)S(1)} %get-tuple-element.55), channel_id=1, source_target_pairs={{0,1},{1,0},{2,3},{3,2},{4,5},{5,4},{6,7},{7,6},{8,9},{9,8},{10,11... | collective-permute-start | bytes 491528 | tf_op jit(solution)/shard_map/ppermute | solution.py:49
  29.4 8.4 %collective-permute-start.9 = (bf16[128,640]{1,0:T(8,128)(2,1)S(1)}, bf16[128,640]{1,0:T(8,128)(2,1)S(1)}, u32[]{:S(2)}, u32[]{:S(2)}) collective-permute-start(bf16[128,640]{1,0:T(8,128)(2,1)S(1)} %get-tuple-element.56), channel_id=1, source_target_pairs={{0,2},{1,3},{2,0},{3,1},{4,6},{5,7},{6,4},{7,5},{8,10},{9,11},{10,... | collective-permute-start | bytes 491528 | tf_op jit(solution)/shard_map/ppermute | solution.py:49
  29.6 8.2 %collective-permute-start.10 = (bf16[128,640]{1,0:T(8,128)(2,1)S(1)}, bf16[128,640]{1,0:T(8,128)(2,1)S(1)}, u32[]{:S(2)}, u32[]{:S(2)}) collective-permute-start(bf16[128,640]{1,0:T(8,128)(2,1)S(1)} %get-tuple-element.57), channel_id=1, source_target_pairs={{0,3},{1,2},{2,1},{3,0},{4,7},{5,6},{6,5},{7,4},{8,11},{9,10},{10,... | collective-permute-start | bytes 491528 | tf_op jit(solution)/shard_map/ppermute | solution.py:49
  30.9 3.7 %collective-permute-start.12 = (f32[2,128]{1,0:T(2,128)S(1)}, f32[2,128]{1,0:T(2,128)S(1)}, u32[]{:S(2)}, u32[]{:S(2)}) collective-permute-start(f32[2,128]{1,0:T(2,128)S(1)} %get-tuple-element.61.refs_6_.gate_ref), channel_id=1, source_target_pairs={{0,16},{1,17},{2,18},{3,19},{4,20},{5,21},{6,22},{7,23},{8,24},{9,... | collective-permute-start | bytes 3080 | tf_op jit(solution)/shard_map/ppermute | solution.py:17
  37.8 15.2 %copy-start.4 = (f32[1,5120]{1,0:T(1,128)S(1)}, f32[1,5120]{1,0:T(1,128)}, u32[]{:S(2)}) copy-start(f32[1,5120]{1,0:T(1,128)} %refs_5_.3) | copy-start | bytes 61444
  37.8 49.8 %copy-start = (bf16[1,640,5120]{2,1,0:T(8,128)(2,1)S(1)}, bf16[1,640,5120]{2,1,0:T(8,128)(2,1)}, u32[]{:S(2)}) copy-start(bf16[1,640,5120]{2,1,0:T(8,128)(2,1)} %param.15) | copy-start | bytes 19660804
  39.6 48.0 %slice-start.1 = ((s8[6553600]{0:T(1024)(128)(4,1)}), s8[2359296]{0:T(1024)(128)(4,1)S(1)}, s32[]{:S(2)}) async-start(s8[6553600]{0:T(1024)(128)(4,1)} %bitcast.17), calls=%async_computation.1 | async-start | bytes 4718592
  39.7 4.2 %collective-permute-start.14 = (bf16[128,640]{1,0:T(8,128)(2,1)S(1)}, bf16[128,640]{1,0:T(8,128)(2,1)S(1)}, u32[]{:S(2)}, u32[]{:S(2)}) collective-permute-start(bf16[128,640]{1,0:T(8,128)(2,1)S(1)} %get-tuple-element.63), channel_id=1, source_target_pairs={{0,1},{1,0},{2,3},{3,2},{4,5},{5,4},{6,7},{7,6},{8,9},{9,8},{10,11... | collective-permute-start | bytes 491528 | tf_op jit(solution)/shard_map/ppermute | solution.py:49
  40.0 6.7 %collective-permute-start.15 = (bf16[128,640]{1,0:T(8,128)(2,1)S(1)}, bf16[128,640]{1,0:T(8,128)(2,1)S(1)}, u32[]{:S(2)}, u32[]{:S(2)}) collective-permute-start(bf16[128,640]{1,0:T(8,128)(2,1)S(1)} %get-tuple-element.64), channel_id=1, source_target_pairs={{0,2},{1,3},{2,0},{3,1},{4,6},{5,7},{6,4},{7,5},{8,10},{9,11},{10,... | collective-permute-start | bytes 491528 | tf_op jit(solution)/shard_map/ppermute | solution.py:49
  40.0 6.7 %collective-permute-start.16 = (bf16[128,640]{1,0:T(8,128)(2,1)S(1)}, bf16[128,640]{1,0:T(8,128)(2,1)S(1)}, u32[]{:S(2)}, u32[]{:S(2)}) collective-permute-start(bf16[128,640]{1,0:T(8,128)(2,1)S(1)} %get-tuple-element.65), channel_id=1, source_target_pairs={{0,3},{1,2},{2,1},{3,0},{4,7},{5,6},{6,5},{7,4},{8,11},{9,10},{10,... | collective-permute-start | bytes 491528 | tf_op jit(solution)/shard_map/ppermute | solution.py:49
  46.7 6.3 %collective-permute-start.17 = (bf16[4,128,640]{2,1,0:T(8,128)(2,1)S(1)}, bf16[4,128,640]{2,1,0:T(8,128)(2,1)S(1)}, u32[]{:S(2)}, u32[]{:S(2)}) collective-permute-start(bf16[4,128,640]{2,1,0:T(8,128)(2,1)S(1)} %pile.2.refs_4_), channel_id=1, source_target_pairs={{0,16},{1,17},{2,18},{3,19},{4,20},{5,21},{6,22},{7,23},{8,24},{9,... | collective-permute-start | bytes 1966088 | tf_op jit(solution)/shard_map/ppermute | solution.py:27
  53.7 5.8 %collective-permute-start.20 = (bf16[8,5120]{1,0:T(8,128)(2,1)S(1)}, bf16[8,5120]{1,0:T(8,128)(2,1)S(1)}, u32[]{:S(2)}, u32[]{:S(2)}) collective-permute-start(bf16[8,5120]{1,0:T(8,128)(2,1)S(1)} %get-tuple-element.67.refs_0_.refs_10_), channel_id=1, source_target_pairs={{0,12},{1,13},{2,14},{3,15},{4,8},{5,9},{6,10},{7,11},{8,4},{9,5},... | collective-permute-start | bytes 245768 | tf_op jit(solution)/shard_map/ppermute | solution.py:49
  56.0 7.5 %collective-permute-start.19 = (bf16[8,5120]{1,0:T(8,128)(2,1)S(1)}, bf16[8,5120]{1,0:T(8,128)(2,1)S(1)}, u32[]{:S(2)}, u32[]{:S(2)}) collective-permute-start(bf16[8,5120]{1,0:T(8,128)(2,1)S(1)} %get-tuple-element.67.refs_0_.refs_10_), channel_id=1, source_target_pairs={{0,8},{1,9},{2,10},{3,11},{4,12},{5,13},{6,14},{7,15},{8,0},{9,1},... | collective-permute-start | bytes 245768 | tf_op jit(solution)/shard_map/ppermute | solution.py:49
  56.0 7.5 %collective-permute-start.18 = (bf16[8,5120]{1,0:T(8,128)(2,1)S(1)}, bf16[8,5120]{1,0:T(8,128)(2,1)S(1)}, u32[]{:S(2)}, u32[]{:S(2)}) collective-permute-start(bf16[8,5120]{1,0:T(8,128)(2,1)S(1)} %get-tuple-element.67.refs_0_.refs_10_), channel_id=1, source_target_pairs={{0,4},{1,5},{2,6},{3,7},{4,0},{5,1},{6,2},{7,3},{8,12},{9,13},{10,... | collective-permute-start | bytes 245768 | tf_op jit(solution)/shard_map/ppermute | solution.py:49
  63.5 18.3 %collective-permute-start.22 = (bf16[32,5120]{1,0:T(8,128)(2,1)S(1)}, bf16[32,5120]{1,0:T(8,128)(2,1)S(1)}, u32[]{:S(2)}, u32[]{:S(2)}) collective-permute-start(bf16[32,5120]{1,0:T(8,128)(2,1)S(1)} %join.5.refs_2_), channel_id=1, source_target_pairs={{0,2},{1,3},{2,0},{3,1},{4,6},{5,7},{6,4},{7,5},{8,10},{9,11},{10,... | collective-permute-start | bytes 983048 | tf_op jit(solution)/shard_map/ppermute | solution.py:49
  64.5 17.4 %collective-permute-start.21 = (bf16[32,5120]{1,0:T(8,128)(2,1)S(1)}, bf16[32,5120]{1,0:T(8,128)(2,1)S(1)}, u32[]{:S(2)}, u32[]{:S(2)}) collective-permute-start(bf16[32,5120]{1,0:T(8,128)(2,1)S(1)} %join.5.refs_2_), channel_id=1, source_target_pairs={{0,1},{1,0},{2,3},{3,2},{4,5},{5,4},{6,7},{7,6},{8,9},{9,8},{10,11... | collective-permute-start | bytes 983048 | tf_op jit(solution)/shard_map/ppermute | solution.py:49
  65.5 10.9 %collective-permute-start.23 = (bf16[128,640]{1,0:T(8,128)(2,1)S(1)}, bf16[128,640]{1,0:T(8,128)(2,1)S(1)}, u32[]{:S(2)}, u32[]{:S(2)}) collective-permute-start(bf16[128,640]{1,0:T(8,128)(2,1)S(1)} %get-tuple-element.69), channel_id=1, source_target_pairs={{0,1},{1,0},{2,3},{3,2},{4,5},{5,4},{6,7},{7,6},{8,9},{9,8},{10,11... | collective-permute-start | bytes 491528 | tf_op jit(solution)/shard_map/ppermute | solution.py:49
  65.9 10.5 %collective-permute-start.24 = (bf16[128,640]{1,0:T(8,128)(2,1)S(1)}, bf16[128,640]{1,0:T(8,128)(2,1)S(1)}, u32[]{:S(2)}, u32[]{:S(2)}) collective-permute-start(bf16[128,640]{1,0:T(8,128)(2,1)S(1)} %get-tuple-element.70), channel_id=1, source_target_pairs={{0,2},{1,3},{2,0},{3,1},{4,6},{5,7},{6,4},{7,5},{8,10},{9,11},{10,... | collective-permute-start | bytes 491528 | tf_op jit(solution)/shard_map/ppermute | solution.py:49
  66.5 13.8 %collective-permute-start.25 = (bf16[128,640]{1,0:T(8,128)(2,1)S(1)}, bf16[128,640]{1,0:T(8,128)(2,1)S(1)}, u32[]{:S(2)}, u32[]{:S(2)}) collective-permute-start(bf16[128,640]{1,0:T(8,128)(2,1)S(1)} %get-tuple-element.71), channel_id=1, source_target_pairs={{0,3},{1,2},{2,1},{3,0},{4,7},{5,6},{6,5},{7,4},{8,11},{9,10},{10,... | collective-permute-start | bytes 491528 | tf_op jit(solution)/shard_map/ppermute | solution.py:49
  81.9 4.2 %collective-permute-start.26 = (bf16[16,5120]{1,0:T(8,128)(2,1)S(1)}, bf16[16,5120]{1,0:T(8,128)(2,1)S(1)}, u32[]{:S(2)}, u32[]{:S(2)}) collective-permute-start(bf16[16,5120]{1,0:T(8,128)(2,1)S(1)} %get-tuple-element.73), channel_id=1, source_target_pairs={{0,1},{1,0},{2,3},{3,2},{4,5},{5,4},{6,7},{7,6},{8,9},{9,8},{10,11... | collective-permute-start | bytes 491528 | tf_op jit(solution)/shard_map/ppermute | solution.py:49
  83.2 4.5 %collective-permute-start.27 = (bf16[16,5120]{1,0:T(8,128)(2,1)S(1)}, bf16[16,5120]{1,0:T(8,128)(2,1)S(1)}, u32[]{:S(2)}, u32[]{:S(2)}) collective-permute-start(bf16[16,5120]{1,0:T(8,128)(2,1)S(1)} %get-tuple-element.74), channel_id=1, source_target_pairs={{0,2},{1,3},{2,0},{3,1},{4,6},{5,7},{6,4},{7,5},{8,10},{9,11},{10,... | collective-permute-start | bytes 491528 | tf_op jit(solution)/shard_map/ppermute | solution.py:49
  90.0 4.2 %collective-permute-start.30 = (bf16[16,5120]{1,0:T(8,128)(2,1)S(1)}, bf16[16,5120]{1,0:T(8,128)(2,1)S(1)}, u32[]{:S(2)}, u32[]{:S(2)}) collective-permute-start(bf16[16,5120]{1,0:T(8,128)(2,1)S(1)} %get-tuple-element.79), channel_id=1, source_target_pairs={{2,0},{3,1},{0,2},{1,3},{6,4},{7,5},{4,6},{5,7},{10,8},{11,9},{8,1... | collective-permute-start | bytes 491528 | tf_op jit(solution)/shard_map/ppermute | solution.py:49
  90.8 4.2 %collective-permute-start.28 = (bf16[16,5120]{1,0:T(8,128)(2,1)S(1)}, bf16[16,5120]{1,0:T(8,128)(2,1)S(1)}, u32[]{:S(2)}, u32[]{:S(2)}) collective-permute-start(bf16[16,5120]{1,0:T(8,128)(2,1)S(1)} %get-tuple-element.77), channel_id=1, source_target_pairs={{1,0},{0,1},{3,2},{2,3},{5,4},{4,5},{7,6},{6,7},{9,8},{8,9},{11,10... | collective-permute-start | bytes 491528 | tf_op jit(solution)/shard_map/ppermute | solution.py:49
  94.3 10.1 %collective-permute-start.31 = (bf16[32,5120]{1,0:T(8,128)(2,1)S(1)}, bf16[32,5120]{1,0:T(8,128)(2,1)S(1)}, u32[]{:S(2)}, u32[]{:S(2)}) collective-permute-start(bf16[32,5120]{1,0:T(8,128)(2,1)S(1)} %add_half.3.refs_5_), channel_id=1, source_target_pairs={{1,0},{0,1},{3,2},{2,3},{5,4},{4,5},{7,6},{6,7},{9,8},{8,9},{11,10... | collective-permute-start | bytes 983048 | tf_op jit(solution)/shard_map/ppermute | solution.py:49
  95.0 9.3 %collective-permute-start.29 = (bf16[32,5120]{1,0:T(8,128)(2,1)S(1)}, bf16[32,5120]{1,0:T(8,128)(2,1)S(1)}, u32[]{:S(2)}, u32[]{:S(2)}) collective-permute-start(bf16[32,5120]{1,0:T(8,128)(2,1)S(1)} %add_half.2.refs_4_), channel_id=1, source_target_pairs={{2,0},{3,1},{0,2},{1,3},{6,4},{7,5},{4,6},{5,7},{10,8},{11,9},{8,1... | collective-permute-start | bytes 983048 | tf_op jit(solution)/shard_map/ppermute | solution.py:49
  95.8 3.6 %collective-permute-start.36 = (bf16[32,1280]{1,0:T(8,128)(2,1)S(1)}, bf16[32,1280]{1,0:T(8,128)(2,1)S(1)}, u32[]{:S(2)}, u32[]{:S(2)}) collective-permute-start(bf16[32,1280]{1,0:T(8,128)(2,1)S(1)} %get-tuple-element.84), channel_id=1, source_target_pairs={{4,0},{5,1},{6,2},{7,3},{0,4},{1,5},{2,6},{3,7},{12,8},{13,9},{14,... | collective-permute-start | bytes 245768 | tf_op jit(solution)/shard_map/ppermute | solution.py:49
  95.8 4.3 %collective-permute-start.37 = (bf16[32,1280]{1,0:T(8,128)(2,1)S(1)}, bf16[32,1280]{1,0:T(8,128)(2,1)S(1)}, u32[]{:S(2)}, u32[]{:S(2)}) collective-permute-start(bf16[32,1280]{1,0:T(8,128)(2,1)S(1)} %get-tuple-element.85), channel_id=1, source_target_pairs={{8,0},{9,1},{10,2},{11,3},{12,4},{13,5},{14,6},{15,7},{0,8},{1,9},... | collective-permute-start | bytes 245768 | tf_op jit(solution)/shard_map/ppermute | solution.py:49
  98.3 5.1 %collective-permute-start.38 = (bf16[32,1280]{1,0:T(8,128)(2,1)S(1)}, bf16[32,1280]{1,0:T(8,128)(2,1)S(1)}, u32[]{:S(2)}, u32[]{:S(2)}) collective-permute-start(bf16[32,1280]{1,0:T(8,128)(2,1)S(1)} %get-tuple-element.86), channel_id=1, source_target_pairs={{12,0},{13,1},{14,2},{15,3},{8,4},{9,5},{10,6},{11,7},{4,8},{5,9},... | collective-permute-start | bytes 245768 | tf_op jit(solution)/shard_map/ppermute | solution.py:49
  103.4 5.4 %collective-permute-start.39 = (f32[8,1280]{1,0:T(8,128)S(1)}, f32[8,1280]{1,0:T(8,128)S(1)}, u32[]{:S(2)}, u32[]{:S(2)}) collective-permute-start(f32[8,1280]{1,0:T(8,128)S(1)} %get-tuple-element.88), channel_id=1, source_target_pairs={{0,1},{1,0},{2,3},{3,2},{4,5},{5,4},{6,7},{7,6},{8,9},{9,8},{10,11... | collective-permute-start | bytes 122888 | tf_op jit(solution)/shard_map/ppermute | solution.py:49
  104.5 9.4 %collective-permute-start.32 = (bf16[8,5120]{1,0:T(8,128)(2,1)S(1)}, bf16[8,5120]{1,0:T(8,128)(2,1)S(1)}, u32[]{:S(2)}, u32[]{:S(2)}) collective-permute-start(bf16[8,5120]{1,0:T(8,128)(2,1)S(1)} %get-tuple-element.81), channel_id=1, source_target_pairs={{4,0},{5,1},{6,2},{7,3},{0,4},{1,5},{2,6},{3,7},{12,8},{13,9},{14,... | collective-permute-start | bytes 245768 | tf_op jit(solution)/shard_map/ppermute | solution.py:49
  104.6 9.3 %collective-permute-start.33 = (bf16[8,5120]{1,0:T(8,128)(2,1)S(1)}, bf16[8,5120]{1,0:T(8,128)(2,1)S(1)}, u32[]{:S(2)}, u32[]{:S(2)}) collective-permute-start(bf16[8,5120]{1,0:T(8,128)(2,1)S(1)} %get-tuple-element.82), channel_id=1, source_target_pairs={{8,0},{9,1},{10,2},{11,3},{12,4},{13,5},{14,6},{15,7},{0,8},{1,9},... | collective-permute-start | bytes 245768 | tf_op jit(solution)/shard_map/ppermute | solution.py:49
  105.9 8.0 %collective-permute-start.34 = (bf16[8,5120]{1,0:T(8,128)(2,1)S(1)}, bf16[8,5120]{1,0:T(8,128)(2,1)S(1)}, u32[]{:S(2)}, u32[]{:S(2)}) collective-permute-start(bf16[8,5120]{1,0:T(8,128)(2,1)S(1)} %get-tuple-element.83), channel_id=1, source_target_pairs={{12,0},{13,1},{14,2},{15,3},{8,4},{9,5},{10,6},{11,7},{4,8},{5,9},... | collective-permute-start | bytes 245768 | tf_op jit(solution)/shard_map/ppermute | solution.py:49
  108.1 3.1 %collective-permute-start.40 = (f32[8,1280]{1,0:T(8,128)S(1)}, f32[8,1280]{1,0:T(8,128)S(1)}, u32[]{:S(2)}, u32[]{:S(2)}) collective-permute-start(f32[8,1280]{1,0:T(8,128)S(1)} %get-tuple-element.89), channel_id=1, source_target_pairs={{0,2},{1,3},{2,0},{3,1},{4,6},{5,7},{6,4},{7,5},{8,10},{9,11},{10,... | collective-permute-start | bytes 122888 | tf_op jit(solution)/shard_map/ppermute | solution.py:49
  108.8 3.8 %collective-permute-start.41 = (f32[8,1280]{1,0:T(8,128)S(1)}, f32[8,1280]{1,0:T(8,128)S(1)}, u32[]{:S(2)}, u32[]{:S(2)}) collective-permute-start(f32[8,1280]{1,0:T(8,128)S(1)} %get-tuple-element.90), channel_id=1, source_target_pairs={{0,3},{1,2},{2,1},{3,0},{4,7},{5,6},{6,5},{7,4},{8,11},{9,10},{10,... | collective-permute-start | bytes 122888 | tf_op jit(solution)/shard_map/ppermute | solution.py:49
  112.6 13.0 %collective-permute-start.42 = (f32[4,8,1280]{2,1,0:T(8,128)S(1)}, f32[4,8,1280]{2,1,0:T(8,128)S(1)}, u32[]{:S(2)}, u32[]{:S(2)}) collective-permute-start(f32[4,8,1280]{2,1,0:T(8,128)S(1)} %pile.3.refs_3_), channel_id=1, source_target_pairs={{0,16},{1,17},{2,18},{3,19},{4,20},{5,21},{6,22},{7,23},{8,24},{9,... | collective-permute-start | bytes 491528 | tf_op jit(solution)/shard_map/ppermute | solution.py:27
  113.9 14.4 %collective-permute-start.35 = (f32[8,5120]{1,0:T(8,128)S(1)}, f32[8,5120]{1,0:T(8,128)S(1)}, u32[]{:S(2)}, u32[]{:S(2)}) collective-permute-start(f32[8,5120]{1,0:T(8,128)S(1)} %add_last.1.back_ref), channel_id=1, source_target_pairs={{0,16},{1,17},{2,18},{3,19},{4,20},{5,21},{6,22},{7,23},{8,24},{9,... | collective-permute-start | bytes 491528 | tf_op jit(solution)/shard_map/ppermute | solution.py:17

commit v3 on v1

--- a/solution.py
+++ b/solution.py
@@ -20,6 +20,11 @@
 def swapped(block):
     sections = lax.axis_size("section")
     return lax.ppermute(block, "section", [(i, (i + sections // 2) % sections) for i in range(sections)])
+
+
+def to_decoder(block):
+    apart = lax.axis_size("section") // 2
+    return lax.ppermute(block, "section", [(i, i + apart) for i in range(apart)])
 
 
 def partner(position, distance, size):
@@ -65,8 +70,7 @@
     def gather(self, block):
         na, nb, nc = self.sizes
         rows = block.shape[0]
-        own = [block] + [self.shift(block, (s, 0, 0)) for s in range(1, na)]
-        own = jnp.concatenate(own, axis=0)
+        own = join([block] + [self.shift(block, (s, 0, 0)) for s in range(1, na)])
         half = rows * (na - na // 2)
         pieces = {(0, 0): [own]}
         for b in range(1, nb):
@@ -80,7 +84,7 @@
                 pieces[b, c] = [first, second]
         return sum((pieces[k] for k in self.offsets()), [])
 
-    def scatter(self, pieces, rows, after=(None, None, None)):
+    def scatter(self, pieces, rows, after=()):
         na, nb, nc = self.sizes
         half = rows * (na - na // 2)
         held, at = {}, 0
@@ -95,17 +99,17 @@
         for c in range(1, nc):
             more = [self.shift(held[b, c][1], (0, b, 0), back=True) for b in range(1, nb)]
             arrived.append((held[0, c][0], more, half, (0, 0, c)))
-        arrived = [
-            self.shift(add_half(piece, more, start, after[0]), by, back=True)
-            for piece, more, start, by in arrived
-        ]
-        blocks = add_blocks(held[0, 0][0], arrived, rows, after[1])
+        halves = [add_half(piece, more, start, after) for piece, more, start, _ in arrived]
+        arrived = [self.shift(piece, by, back=True) for piece, (*_, by) in zip(halves, arrived)]
+        after = yield halves
+        blocks = add_blocks(held[0, 0][0], arrived, rows, after)
         more = [self.shift(blocks[s], (s, 0, 0), back=True) for s in range(1, na)]
-        return add_last(blocks[0], more, after[2])
+        after = yield blocks
+        yield add_last(blocks[0], more, after)
 
 
 def compiler_params():
-    return pltpu.CompilerParams(vmem_limit_bytes=24 * 2**20)
+    return pltpu.CompilerParams(vmem_limit_bytes=20 * 2**20)
 
 
 def in_vmem(count):
@@ -121,17 +125,17 @@
     return lax.dot_general(left, right, dims, preferred_element_type=jnp.float32)
 
 
-def local_kernel(kernel, name, outs, args, after=None, flops=0, scalars=0, **more):
+def local_kernel(kernel, name, outs, args, after=(), flops=0, scalars=0, **more):
     args = list(args)
     in_specs = [pl.BlockSpec(memory_space=pltpu.SMEM)] * scalars + in_vmem(len(args) - scalars)
     count = len(args)
     body = kernel
-    if after is not None:
-        args.append(after)
-        in_specs.append(ANYWHERE)
+    if after:
+        args += after
+        in_specs += [ANYWHERE] * len(after)
 
         def body(*refs):
-            kernel(*refs[:count], *refs[count + 1 :])
+            kernel(*refs[:count], *refs[count + len(after) :])
 
     moved = sum(x.size * x.dtype.itemsize for x in args[:count]) + sum(
         x.size * x.dtype.itemsize for x in outs
@@ -148,6 +152,18 @@
     )(*args)
 
 
+def join(blocks):
+    if blocks[0].shape[0] % 8:
+        return jnp.concatenate(blocks, axis=0)
+
+    def kernel(*refs):
+        rows = jnp.concatenate([r[...].astype(jnp.float32) for r in refs[:-1]], axis=0)
+        refs[-1][...] = rows.astype(jnp.bfloat16)
+
+    one = jax.ShapeDtypeStruct((len(blocks) * blocks[0].shape[0], blocks[0].shape[1]), jnp.bfloat16)
+    return local_kernel(kernel, "join", [one], blocks)[0]
+
+
 def add_half(piece, more, start, after):
     rows = more[0].shape[0]
 
@@ -219,29 +235,85 @@
     return [jnp.concatenate([r[:, c] for r in refs], axis=0) for c in columns]
 
 
-def make_queries(x, gain):
+EXTRA = 16
+
+
+def extra_rows(gate, slots):
+    high = gate.astype(jnp.bfloat16).astype(jnp.float32)
+    middle = (gate - high).astype(jnp.bfloat16).astype(jnp.float32)
+    none = jnp.zeros((EXTRA - 4, gate.shape[1]), jnp.float32)
+    rows = [high, middle, gate - high - middle, slots, none]
+    return jnp.concatenate(rows, axis=0).astype(jnp.bfloat16)
+
+
+def make_queries(x, gain, gate, slots, after):
     tokens, width = x.shape
     half = width // 2
 
-    def kernel(x_ref, gain_ref, *q_refs):
+    quarter = half // 2
+
+    def kernel(x_ref, gain_ref, gate_ref, slot_ref, copy_ref, *refs):
+        *q_refs, gates_ref = refs
+        gate, slots = gate_ref[...], slot_ref[...].astype(jnp.float32)
+        copy_ref[:tokens] = x_ref[...]
+        copy_ref[tokens:] = jnp.zeros((EXTRA, width), jnp.bfloat16)
+        copy_ref[tokens:, :tokens] = extra_rows(gate, slots)
+        gates_ref[0:1] = gate
+        gates_ref[1:2] = slots
         x = x_ref[...].astype(jnp.float32)
         inverse = lax.rsqrt(jnp.mean(x * x, axis=-1, keepdims=True) + 1e-06)
-        for at, ref in zip((0, half), q_refs):
-            x = x_ref[:, at : at + half].astype(jnp.float32)
-            ref[...] = (x * inverse * gain_ref[:, at : at + half]).astype(jnp.bfloat16)
-
+        for at, ref in zip((0, quarter, half), q_refs):
+            columns = slice(at, at + ref.shape[1])
+            x = x_ref[:, columns].astype(jnp.float32)
+            ref[...] = (x * inverse * gain_ref[:, columns]).astype(jnp.bfloat16)
+
+    part = jax.ShapeDtypeStruct((tokens, quarter), jnp.bfloat16)
     one = jax.ShapeDtypeStruct((tokens, half), jnp.bfloat16)
-    return local_kernel(kernel, "queries", [one, one], [x, gain])
-
-
-def attend(q, pieces):
-    tokens, width = q.shape
+    same = jax.ShapeDtypeStruct((tokens + EXTRA, width), x.dtype)
+    pair = jax.ShapeDtypeStruct((2, tokens), jnp.float32)
+    return local_kernel(
+        kernel, "queries", [same, part, part, one, pair], [x, gain, gate, slots], after
+    )
+
+
+def cut(x, after):
+    tokens, width = x.shape
+    widths = [width // 4, width // 4, width // 2]
+
+    def kernel(x_ref, *refs):
+        at = 0
+        for ref in refs:
+            ref[...] = x_ref[:, at : at + ref.shape[1]]
+            at += ref.shape[1]
+
+    outs = [jax.ShapeDtypeStruct((tokens, n), x.dtype) for n in widths]
+    return local_kernel(kernel, "cut", outs, [x], after)
+
+
+def choose(section, sections, first_refs, second_ref, out_ref):
+    @pl.when(section[0] >= sections // 2)
+    def _():
+        out_ref[...] = second_ref[...]
+
+    @pl.when(section[0] < sections // 2)
+    def _():
+        at = 0
+        for ref in first_refs:
+            out_ref[:, at : at + ref.shape[1]] = ref[...]
+            at += ref.shape[1]
+
+
+def attend(section, sections, first, second, pieces, after):
+    tokens, width = second.shape
     heads = width // HD
     rows = sum(p.shape[0] for p in pieces)
     count = len(pieces)
 
-    def kernel(q_ref, *refs):
-        kv_refs, (mixed_ref, p_ref) = refs[:count], refs[count:]
+    def kernel(section, *refs):
+        *first_refs, second_ref = refs[: len(first) + 1]
+        refs = refs[len(first) + 1 :]
+        kv_refs, (mixed_ref, p_ref, q_ref) = refs[:count], refs[count:]
+        choose(section, sections, first_refs, second_ref, q_ref)
 
         def some_heads(numbers, columns):
             keys = stacked(kv_refs, columns)
@@ -259,17 +331,24 @@
     outs = [
         jax.ShapeDtypeStruct((tokens, width), jnp.bfloat16),
         jax.ShapeDtypeStruct((heads, rows, tokens), jnp.float32),
+        jax.ShapeDtypeStruct((tokens, width), jnp.bfloat16),
     ]
-    return local_kernel(kernel, "attend", outs, [q, *pieces], flops=4 * tokens * rows * width)
-
-
-def gradient(q, cot, p, pieces, heights, types, after):
+    args = [section.reshape(1), *first, second, *pieces]
+    return local_kernel(
+        kernel, "attend", outs, args, after, flops=4 * tokens * rows * width, scalars=1
+    )
+
+
+def gradient(section, sections, q, first, second, p, pieces, heights, types):
     tokens, width = q.shape
     heads, rows, _ = p.shape
     count = len(pieces)
 
-    def kernel(q_ref, cot_ref, p_ref, *refs):
-        kv_refs, out_refs = refs[:count], refs[count:]
+    def kernel(section, q_ref, *refs):
+        *first_refs, second_ref, p_ref = refs[: len(first) + 2]
+        refs = refs[len(first) + 2 :]
+        kv_refs, out_refs, cot_ref = refs[:count], refs[count:-1], refs[-1]
+        choose(section, sections, first_refs, second_ref, cot_ref)
 
         def some_heads(numbers, columns):
             values = stacked(kv_refs, beside(columns, width))
@@ -298,22 +377,28 @@
 
     outs = [jax.ShapeDtypeStruct((n, 2 * width), t) for n, t in zip(heights, types)]
     return local_kernel(
-        kernel, "gradient", outs, [q, cot, p, *pieces], after, flops=10 * tokens * rows * width
-    )
-
-
-def settle(flag, x, first, second, norm_gain, slots):
-    tokens, width = x.shape
+        kernel,
+        "gradient",
+        outs,
+        [section.reshape(1), q, *first, second, p, *pieces],
+        flops=10 * tokens * rows * width,
+        scalars=1,
+        scratch_shapes=[pltpu.VMEM((tokens, width), jnp.bfloat16)],
+    )
+
+
+def settle(section, sections, x, first, second, norm_gain, gates, after):
+    tokens, width = first.shape[0], x.shape[1]
     half = width // 2
 
-    def kernel(flag, x_ref, first_ref, second_ref, norm_ref, slot_ref, res_ref, cap_ref):
-        onehot = slot_ref[...] == lax.broadcasted_iota(jnp.int32, (CAP, tokens), 0)
-        onehot = jnp.where(onehot, 1.0, 0.0).astype(jnp.bfloat16)
-        attends = jnp.full((tokens, 1), flag[0], jnp.int32) == 1
+    def kernel(section, x_ref, first_ref, second_ref, norm_ref, gate_ref, res_ref, cap_ref):
+        slots = lax.broadcasted_iota(jnp.int32, (CAP, tokens), 0).astype(jnp.float32)
+        onehot = jnp.where(gate_ref[1:2] == slots, 1.0, 0.0).astype(jnp.bfloat16)
+        attends = jnp.full((tokens, 1), section[0], jnp.int32) >= sections // 2
         chosen = []
         for at, ref in ((0, first_ref), (half, second_ref)):
             mixed = jnp.where(attends, ref[...].astype(jnp.float32), 0.0)
-            res = (x_ref[:, at : at + half].astype(jnp.float32) + mixed).astype(jnp.bfloat16)
+            res = (x_ref[:tokens, at : at + half].astype(jnp.float32) + mixed).astype(jnp.bfloat16)
             res_ref[:, at : at + half] = res
             chosen.append(dot(onehot, res))
         squares = sum(jnp.sum(c * c, axis=-1, keepdims=True) for c in chosen)
@@ -327,7 +412,8 @@
         jax.ShapeDtypeStruct((CAP, width), jnp.bfloat16),
     ]
     return local_kernel(
-        kernel, "settle", outs, [flag, x, first, second, norm_gain, slots], scalars=1
+        kernel, "settle", outs, [section.reshape(1), x, first, second, norm_gain, gates], after,
+        scalars=1,
     )
 
 
@@ -338,127 +424,118 @@
     steps = next(s for s in (4, 2, 1) if width % (s * 128) == 0)
     step = width // steps
 
-    def kernel(w1_any, w2_any, _, *refs):
-        in_refs, out_refs = refs[:count], refs[count : count + len(heights)]
-        w1_ref, w2_ref, sems = refs[count + len(heights) :]
+    def kernel(w1_ref, w2_ref, *refs):
+        in_refs, out_refs = refs[:count], refs[count:]
         parts = [slice(i * step, (i + 1) * step) for i in range(steps)]
-        copies = [
-            pltpu.make_async_copy(w1_any.at[c, :], w1_ref.at[c, :], sems.at[0, i])
-            for i, c in enumerate(parts)
-        ]
-        later = [
-            pltpu.make_async_copy(w2_any.at[:, c], w2_ref.at[:, c], sems.at[1, i])
-            for i, c in enumerate(parts)
-        ]
-        for copy in copies + later:
-            copy.start()
         hidden = jnp.zeros((rows, units), jnp.float32)
-        for copy, c in zip(copies, parts):
-            x = jnp.concatenate([r[:, c] for r in in_refs], axis=0)
-            copy.wait()
-            hidden = hidden + dot(x, w1_ref[c, :])
+        for c in parts:
+            hidden = hidden + dot(jnp.concatenate([r[:, c] for r in in_refs], axis=0), w1_ref[c, :])
         hidden = jax.nn.gelu(hidden).astype(jnp.bfloat16)
-        for copy, c in zip(later, parts):
-            copy.wait()
+        for c in parts:
             y = dot(hidden, w2_ref[:, c])
             at = 0
             for ref in out_refs:
                 ref[:, c] = y[at : at + ref.shape[0]].astype(ref.dtype)
                 at += ref.shape[0]
 
-    return pl.pallas_call(
-        kernel,
-        out_shape=tuple(jax.ShapeDtypeStruct((n, width), t) for n, t in zip(heights, types)),
-        in_specs=[ANYWHERE] * 3 + in_vmem(count),
-        out_specs=tuple(in_vmem(len(heights))),
-        scratch_shapes=[
-            pltpu.VMEM((width, units), w1.dtype),
-            pltpu.VMEM((units, width), w2.dtype),
-            pltpu.SemaphoreType.DMA((2, steps)),
-        ],
-        compiler_params=pltpu.CompilerParams(vmem_limit_bytes=48 * 2**20),
-        cost_estimate=pl.CostEstimate(
-            flops=4 * rows * width * units, bytes_accessed=4 * width * units, transcendentals=0
-        ),
-        name="expert",
-    )(w1, w2, after, *pieces)
-
-
-def finish(own, before):
-    one = jax.ShapeDtypeStruct(own[0].shape, jnp.bfloat16)
-    tokens, width = one.shape
+    outs = [jax.ShapeDtypeStruct((n, width), t) for n, t in zip(heights, types)]
+    return local_kernel(
+        kernel, "expert", outs, [w1, w2, *pieces], after, flops=4 * rows * width * units
+    )
+
+
+def finish(res, back, gates=None):
+    tokens, width = res.shape[0] - (EXTRA if gates is None else 0), res.shape[1]
+    one = jax.ShapeDtypeStruct((tokens, width), jnp.bfloat16)
     step = next(s for s in (1280, 1024, 512, 256, 128) if width % s == 0)
 
-    def kernel(*refs):
-        for res_ref, back_ref, gate_ref, out_ref in (refs[0:3] + refs[6:7], refs[3:6] + refs[7:8]):
-            gate = jnp.broadcast_to(gate_ref[0:1], (CAP, tokens)).T[:, 0:1]
-            slots = lax.broadcasted_iota(jnp.int32, (CAP, tokens), 0).astype(jnp.float32)
-            onehot = jnp.where(gate_ref[1:2] == slots, 1.0, 0.0).T
-            onehot = jnp.concatenate([onehot] * 3, axis=1).astype(jnp.bfloat16)
-            for at in range(0, width, step):
-                columns = slice(at, at + step)
-                back = back_ref[:, columns]
-                high = back.astype(jnp.bfloat16).astype(jnp.float32)
-                middle = (back - high).astype(jnp.bfloat16).astype(jnp.float32)
-                parts = jnp.concatenate([high, middle, back - high - middle], axis=0)
-                moved = dot(onehot, parts.astype(jnp.bfloat16))
-                res = res_ref[:, columns].astype(jnp.float32)
-                out_ref[:, columns] = (res + gate * moved).astype(jnp.bfloat16)
-
-    return local_kernel(
-        kernel, "finish", [one, one], [*own, *before], flops=100 * tokens * width
-    )
+    def kernel(res_ref, back_ref, *refs):
+        out_ref = refs[-1]
+        if gates is None:
+            extra = res_ref[tokens:, :tokens].astype(jnp.float32)
+            gate, slot = extra[0:1] + extra[1:2] + extra[2:3], extra[3:4]
+        else:
+            gate, slot = refs[0][0:1], refs[0][1:2]
+        gate = jnp.broadcast_to(gate, (CAP, tokens)).T[:, 0:1]
+        slots = lax.broadcasted_iota(jnp.int32, (CAP, tokens), 0).astype(jnp.float32)
+        onehot = jnp.where(slot == slots, 1.0, 0.0).T
+        onehot = jnp.concatenate([onehot] * 3, axis=1).astype(jnp.bfloat16)
+        for at in range(0, width, step):
+            columns = slice(at, at + step)
+            back = back_ref[:, columns]
+            high = back.astype(jnp.bfloat16).astype(jnp.float32)
+            middle = (back - high).astype(jnp.bfloat16).astype(jnp.float32)
+            parts = jnp.concatenate([high, middle, back - high - middle], axis=0)
+            moved = dot(onehot, parts.astype(jnp.bfloat16))
+            here = res_ref[:tokens, columns].astype(jnp.float32)
+            out_ref[:, columns] = (here + gate * moved).astype(jnp.bfloat16)
+
+    args = [res, back] + ([] if gates is None else [gates])
+    return local_kernel(kernel, "finish", [one], args, flops=50 * tokens * width)[0]
 
 
 def local(
     layer_in, memory, cotangent, norm_gain, attn_gain, expert_in, expert_out, slot_index, gate_prob
 ):
     sections = lax.axis_size("section")
-    decoder = lax.axis_index("section") >= sections // 2
-    flag = decoder.astype(jnp.int32).reshape(1)
+    section = lax.axis_index("section")
+    decoder = section >= sections // 2
     grid = Grid(lax.axis_size("expert"))
     own_rows, _, width = memory[0].shape
     half = width // 2
-    heights, types = grid.heights(own_rows), grid.types()
+    heights = grid.heights(own_rows)
     narrow = any(n % 16 for n in heights)
 
-    def shared(first, second):
-        return jnp.where(decoder, second, swapped(first))
-
-    stash = shared(
-        memory[0, :, :, :half].reshape(own_rows, width),
-        memory[0, :, :, half:].reshape(own_rows, width),
-    )
-    pieces = grid.gather(stash)
-    queries = shared(*make_queries(layer_in[0], attn_gain))
-    upstream = shared(cotangent[0, :, :half], cotangent[0, :, half:])
+    first = swapped(memory[0, :, :, :half].reshape(own_rows, width))
+    second = memory[0, :, :, half:].reshape(own_rows, width)
+    pieces = grid.gather(jnp.where(decoder, second, first))
+    current, *first, second, gates = make_queries(
+        layer_in[0], attn_gain, gate_prob, slot_index, [pieces[0]]
+    )
+    first = [swapped(q) for q in first]
+    *upstream, cot_second = cut(cotangent[0], [gates])
+    upstream = [swapped(c) for c in upstream]
     if narrow:
         pieces = [jnp.concatenate(pieces, axis=0)]
-    mixed, weights = attend(queries, pieces)
-    residual, capacity = settle(flag, layer_in[0], swapped(mixed), mixed, norm_gain, slot_index)
-    gathered = grid.gather(capacity)
-    gates = jnp.concatenate([gate_prob, slot_index.astype(jnp.float32)], axis=0)
-    residual_before = passed_along(residual, "section", 1)
-    gates_before = passed_along(gates, "section", 1)
-    computed = expert(
-        expert_in[0], expert_out[0], gathered, grid.heights(CAP), types, residual_before
-    )
-    returned = grid.scatter(computed, CAP)
-    returned_before = passed_along(returned, "section", 1)
-    output, arriving = finish(
-        (residual, returned, gates), (residual_before, returned_before, gates_before)
-    )
+
+    mixed, weights, queries = attend(
+        section, sections, first, second, pieces, upstream
+    )
+    cots = (upstream, cot_second)
     if narrow:
         whole = [sum(heights)], [jnp.float32]
-        (whole,) = gradient(queries, upstream, weights, pieces, *whole, capacity)
+        (whole,) = gradient(section, sections, queries, *cots, weights, pieces, *whole)
         parts, at = [], 0
-        for n, t in zip(heights, types):
+        for n, t in zip(heights, grid.types()):
             parts.append(whole[at : at + n].astype(t))
             at += n
     else:
-        parts = gradient(queries, upstream, weights, pieces, heights, types, capacity)
-    total_grad = grid.scatter(parts, own_rows, (gathered[-1], computed[0], returned))
-    first = swapped(total_grad).reshape(own_rows, 2, half)
+        parts = gradient(section, sections, queries, *cots, weights, pieces, heights, grid.types())
+    residual, capacity = settle(
+        section, sections, current, to_decoder(mixed), mixed, norm_gain, gates, [parts[0]]
+    )
+    if sections == 2:
+        residual_before = passed_along(current, "section", 1)
+    else:
+        extra = extra_rows(gates[0:1], gates[1:2])
+        extra = jnp.pad(extra, ((0, 0), (0, width - extra.shape[1])))
+        residual_before = passed_along(jnp.concatenate([residual, extra], axis=0), "section", 1)
+    gathered = grid.gather(capacity)
+    grads = grid.scatter(parts, own_rows, [gathered[1]])
+    halves = next(grads)
+    computed = expert(
+        expert_in[0], expert_out[0], gathered, grid.heights(CAP), grid.types(),
+        [residual_before, *halves],
+    )
+    blocks = grads.send([computed[0]])
+    results = grid.scatter(computed, CAP, [blocks[0]])
+    total_grad = grads.send(next(results))
+    results.send([total_grad])
+    returned = results.send([])
+    returned_before = passed_along(returned, "section", 1)
+    output = finish(residual, returned, gates)
+    arriving = finish(residual_before, returned_before)
+    first = to_decoder(total_grad).reshape(own_rows, 2, half)
     total_grad = jnp.concatenate([first, total_grad.reshape(own_rows, 2, half)], axis=2)
     total_grad = jnp.where(decoder, total_grad, 0.0)
     return (output[None], arriving[None], total_grad[None])

time: 119 us -> 105 us (0.88)
  starting transfers between devices: 52.2 us -> 36.4 us
  waiting for transfers between devices: 41.7 us -> 51.1 us
  local copies, waits for them, and re-layouts: 5.79 us -> 1.51 us
  Pallas kernels: 16.1 us -> 11.9 us
    ppermute x28, starting transfers between devices: 37.4 us -> 26.6 us  [shift(): return lax.ppermute(block, 'expert', route)]
    ppermute x5, starting transfers between devices: 11 us -> 4.61 us  [swapped(): lax.ppermute(block, 'section', [(i, (i + sections // 2) % sections) for i...]
    pallas_call x1 -> x0, Pallas kernels: 5.67 us -> none  [expert(): pl.pallas_call(kernel, out_shape=tuple((jax.ShapeDtypeStruct((n, width),...]
    ppermute x28, waiting for transfers between devices: 38.6 us -> 42.4 us  [shift(): return lax.ppermute(block, 'expert', route)]
    ppermute x3 -> x2, waiting for transfers between devices: 0.81 us -> 4.29 us  [passed_along(): return lax.ppermute(block, axis, route)]
    unnamed x26 -> x21, local copies, waits for them, and re-layouts: 4.58 us -> 1.21 us
    ppermute x0 -> x2, waiting for transfers between devices: none -> 3.21 us  [to_decoder(): lax.ppermute(block, 'section', [(i, i + apart) for i in range(apart)])]
    ppermute x0 -> x2, starting transfers between devices: none -> 2.58 us  [to_decoder(): lax.ppermute(block, 'section', [(i, i + apart) for i in range(apart)])]
  transfers between devices with their start and end apart: 36 -> 37, of which waited for: 16 -> 20; matrix products, arithmetic and copies ran while one was open for 2% -> 1% of each run, Pallas kernels for 9% -> 10%
where the time goes in v3:
time: 105 us; the launch traced here: 103 us
  waiting for transfers between devices  51.1 us (49%)
  starting transfers between devices  36.4 us (35%)
  Pallas kernels  11.9 us (11%)
  local copies, waits for them, and re-layouts  1.51 us (1%)
    ppermute x28, waiting for transfers between devices, shift(): return lax.ppermute(block, 'expert', route)  42.4 us
    ppermute x28, starting transfers between devices, shift(): return lax.ppermute(block, 'expert', route)  26.6 us
    pallas_call x18, Pallas kernels, local_kernel(): pl.pallas_call(body, out_shape=tuple(outs), in_specs=in_specs, out_specs=...  11.9 us
    ppermute x5, starting transfers between devices, swapped(): lax.ppermute(block, 'section', [(i, (i + sections // 2) % sections) for i...  4.61 us
    ppermute x2, waiting for transfers between devices, passed_along(): return lax.ppermute(block, axis, route)  4.29 us
    ppermute x2, waiting for transfers between devices, to_decoder(): lax.ppermute(block, 'section', [(i, i + apart) for i in range(apart)])  3.21 us
    ppermute x2, starting transfers between devices, to_decoder(): lax.ppermute(block, 'section', [(i, i + apart) for i in range(apart)])  2.58 us
    ppermute x2, starting transfers between devices, passed_along(): return lax.ppermute(block, axis, route)  2.57 us
  transfers between devices with their start and end apart: 37, of which 20 were waited for; matrix products, arithmetic and copies ran while one was open for 1% of the time, Pallas kernels for 10%

profile of v3, /device:TPU:1, one launch (start us, length us, event | category | flops | bytes accessed | tf_op | source)
XLA Modules:
  0.0 102.8 jit_solution(9554869344931268134)
XLA Ops:
  0.7 1.1 %slice_bitcast_fusion = (bf16[1,8,2,2560]{3,2,1,0:T(2,128)(2,1)S(1)}, bf16[1,8,2,2560]{3,2,1,0:T(2,128)(2,1)S(1)}) fusion(bf16[1,8,2,5120]{3,2,1,0:T(2,128)(2,1)} %param.10), kind=kLoop, calls=%fused_computation.1 | loop fusion | bytes 327680
  1.8 0.1 collective-permute-start
  2.0 1.2 %collective-permute-done = bf16[8,5120]{1,0:T(8,128)(2,1)S(1)} collective-permute-done((bf16[8,5120]{1,0:T(8,128)(2,1)S(1)}, bf16[8,5120]{1,0:T(8,128)(2,1)S(1)}, u32[]{:S(2)}, u32[]{:S(2)}) %collective-permute-start) | collective-permute-done | bytes 81952 | tf_op jit(solution)/shard_map/ppermute | solution.py:22
  3.2 4.5 %collective-permute-start.3 = (bf16[8,5120]{1,0:T(8,128)(2,1)S(1)}, bf16[8,5120]{1,0:T(8,128)(2,1)S(1)}, u32[]{:S(2)}, u32[]{:S(2)}) collective-permute-start(bf16[8,5120]{1,0:T(8,128)(2,1)S(1)} %broadcast_select_fusion.refs_0_), channel_id=1, source_target_pairs={{0,12},{1,13},{2,14},{3,15},{4,8},{5,9},{6,10},{7,11},{8,4},{9,5},... | collective-permute-start | bytes 245768 | tf_op jit(solution)/shard_map/ppermute | solution.py:50
  7.7 0.4 collective-permute-start.1
  8.1 2.2 %collective-permute-done.3.refs_3_ = bf16[8,5120]{1,0:T(8,128)(2,1)S(1)} collective-permute-done((bf16[8,5120]{1,0:T(8,128)(2,1)S(1)}, bf16[8,5120]{1,0:T(8,128)(2,1)S(1)}, u32[]{:S(2)}, u32[]{:S(2)}) %collective-permute-start.3) | collective-permute-done | bytes 81952 | tf_op jit(solution)/shard_map/ppermute | solution.py:50
  10.3 4.1 %collective-permute-done.2.refs_2_ = bf16[8,5120]{1,0:T(8,128)(2,1)S(1)} collective-permute-done((bf16[8,5120]{1,0:T(8,128)(2,1)S(1)}, bf16[8,5120]{1,0:T(8,128)(2,1)S(1)}, u32[]{:S(2)}, u32[]{:S(2)}) %collective-permute-start.2) | collective-permute-done | bytes 81952 | tf_op jit(solution)/shard_map/ppermute | solution.py:50
  14.4 1.3 %collective-permute-start.7 = (bf16[32,5120]{1,0:T(8,128)(2,1)S(1)}, bf16[32,5120]{1,0:T(8,128)(2,1)S(1)}, u32[]{:S(2)}, u32[]{:S(2)}) collective-permute-start(bf16[32,5120]{1,0:T(8,128)(2,1)S(1)} %join.2.refs_4_), channel_id=1, source_target_pairs={{0,2},{1,3},{2,0},{3,1},{4,6},{5,7},{6,4},{7,5},{8,10},{9,11},{10,... | collective-permute-start | bytes 983048 | tf_op jit(solution)/shard_map/ppermute | solution.py:50
  15.7 1.2 %collective-permute-start.6 = (bf16[32,5120]{1,0:T(8,128)(2,1)S(1)}, bf16[32,5120]{1,0:T(8,128)(2,1)S(1)}, u32[]{:S(2)}, u32[]{:S(2)}) collective-permute-start(bf16[32,5120]{1,0:T(8,128)(2,1)S(1)} %join.2.refs_4_), channel_id=1, source_target_pairs={{0,1},{1,0},{2,3},{3,2},{4,5},{5,4},{6,7},{7,6},{8,9},{9,8},{10,11... | collective-permute-start | bytes 983048 | tf_op jit(solution)/shard_map/ppermute | solution.py:50
  16.9 0.9 queries.1
  17.8 1.8 %collective-permute-start.4 = (bf16[128,1280]{1,0:T(8,128)(2,1)S(1)}, bf16[128,1280]{1,0:T(8,128)(2,1)S(1)}, u32[]{:S(2)}, u32[]{:S(2)}) collective-permute-start(bf16[128,1280]{1,0:T(8,128)(2,1)S(1)} %get-tuple-element.35), channel_id=1, source_target_pairs={{0,16},{16,0},{1,17},{17,1},{2,18},{18,2},{3,19},{19,3},{4,20},{20... | collective-permute-start | bytes 983048 | tf_op jit(solution)/shard_map/ppermute | solution.py:22
  19.8 0.5 collective-permute-start.10
  20.3 2.2 %collective-permute-done.7.refs_6_ = bf16[32,5120]{1,0:T(8,128)(2,1)S(1)} collective-permute-done((bf16[32,5120]{1,0:T(8,128)(2,1)S(1)}, bf16[32,5120]{1,0:T(8,128)(2,1)S(1)}, u32[]{:S(2)}, u32[]{:S(2)}) %collective-permute-start.7) | collective-permute-done | bytes 327712 | tf_op jit(solution)/shard_map/ppermute | solution.py:50
  22.5 2.1 %collective-permute-start.11 = (bf16[128,1280]{1,0:T(8,128)(2,1)S(1)}, bf16[128,1280]{1,0:T(8,128)(2,1)S(1)}, u32[]{:S(2)}, u32[]{:S(2)}) collective-permute-start(bf16[128,1280]{1,0:T(8,128)(2,1)S(1)} %get-tuple-element.40), channel_id=1, source_target_pairs={{0,16},{16,0},{1,17},{17,1},{2,18},{18,2},{3,19},{19,3},{4,20},{20... | collective-permute-start | bytes 983048 | tf_op jit(solution)/shard_map/ppermute | solution.py:22
  24.6 1.3 %collective-permute-start.20 = (bf16[144,5120]{1,0:T(8,128)(2,1)S(1)}, bf16[144,5120]{1,0:T(8,128)(2,1)S(1)}, u32[]{:S(2)}, u32[]{:S(2)}) collective-permute-start(bf16[144,5120]{1,0:T(8,128)(2,1)S(1)} %get-tuple-element.34.refs_1_), channel_id=1, source_target_pairs={{0,16},{1,17},{2,18},{3,19},{4,20},{5,21},{6,22},{7,23},{8,24},{9,... | collective-permute-start | bytes 4423688 | tf_op jit(solution)/shard_map/ppermute | solution.py:17
  25.9 1.3 %collective-permute-start.8 = (bf16[16,5120]{1,0:T(8,128)(2,1)S(1)}, bf16[16,5120]{1,0:T(8,128)(2,1)S(1)}, u32[]{:S(2)}, u32[]{:S(2)}) collective-permute-start(bf16[16,5120]{1,0:T(8,128)(2,1)S(1)} %slice.24), channel_id=1, source_target_pairs={{0,1},{1,0},{2,3},{3,2},{4,5},{5,4},{6,7},{7,6},{8,9},{9,8},{10,11... | collective-permute-start | bytes 491528 | tf_op jit(solution)/shard_map/ppermute | solution.py:50
  27.2 1.2 %collective-permute-start.9 = (bf16[16,5120]{1,0:T(8,128)(2,1)S(1)}, bf16[16,5120]{1,0:T(8,128)(2,1)S(1)}, u32[]{:S(2)}, u32[]{:S(2)}) collective-permute-start(bf16[16,5120]{1,0:T(8,128)(2,1)S(1)} %slice.25), channel_id=1, source_target_pairs={{0,2},{1,3},{2,0},{3,1},{4,6},{5,7},{6,4},{7,5},{8,10},{9,11},{10,... | collective-permute-start | bytes 491528 | tf_op jit(solution)/shard_map/ppermute | solution.py:50
  28.5 1.7 %collective-permute-done.8.refs_7_ = bf16[16,5120]{1,0:T(8,128)(2,1)S(1)} collective-permute-done((bf16[16,5120]{1,0:T(8,128)(2,1)S(1)}, bf16[16,5120]{1,0:T(8,128)(2,1)S(1)}, u32[]{:S(2)}, u32[]{:S(2)}) %collective-permute-start.8) | collective-permute-done | bytes 163872 | tf_op jit(solution)/shard_map/ppermute | solution.py:50
  30.2 1.5 %collective-permute-done.9.refs_8_ = bf16[16,5120]{1,0:T(8,128)(2,1)S(1)} collective-permute-done((bf16[16,5120]{1,0:T(8,128)(2,1)S(1)}, bf16[16,5120]{1,0:T(8,128)(2,1)S(1)}, u32[]{:S(2)}, u32[]{:S(2)}) %collective-permute-start.9) | collective-permute-done | bytes 163872 | tf_op jit(solution)/shard_map/ppermute | solution.py:50
  31.7 2.0 %attend.1 = (bf16[128,2560]{1,0:T(8,128)(2,1)S(1)}, f32[20,128,128]{2,1,0:T(8,128)S(1)}, bf16[128,2560]{1,0:T(8,128)(2,1)S(1)}) custom-call(s32[1]{0:T(128)} %bitcast.refs_0_.section, bf16[128,1280]{1,0:T(8,128)(2,1)S(1)} %collective-permute-done.4.refs_1_, bf16[128,1280]{1,0:T(8,128)(2,1)S(1)} %collective-permute-done.5.refs_2_, ...), custom_call_target="tpu_custom_call" | custom-call | flops 167772160 | bytes 5242884 | tf_op jit(solution)/shard_map/attend/pallas_call | solution.py:143
  33.7 1.3 %collective-permute-start.12 = (bf16[128,2560]{1,0:T(8,128)(2,1)S(1)}, bf16[128,2560]{1,0:T(8,128)(2,1)S(1)}, u32[]{:S(2)}, u32[]{:S(2)}) collective-permute-start(bf16[128,2560]{1,0:T(8,128)(2,1)S(1)} %get-tuple-element.41.refs_3_), channel_id=1, source_target_pairs={{0,16},{1,17},{2,18},{3,19},{4,20},{5,21},{6,22},{7,23},{8,24},{9,... | collective-permute-start | bytes 1966088 | tf_op jit(solution)/shard_map/ppermute | solution.py:27
  35.0 2.0 %gradient.1 = (f32[32,5120]{1,0:T(8,128)S(1)}, f32[32,5120]{1,0:T(8,128)S(1)}, f32[32,5120]{1,0:T(8,128)S(1)}, bf16[16,5120]{1,0:T(8,128)(2,1)S(1)}, bf16[16,5120]{1,0:T(8,128)(2,1)S(1)}) custom-call(s32[1]{0:T(128)} %bitcast.refs_0_.section, bf16[128,2560]{1,0:T(8,128)(2,1)S(1)} %get-tuple-element.42.q_ref, ...), custom_call_target="tpu_custom_call" | custom-call | flops 419430400 | bytes 6881284 | tf_op jit(solution)/shard_map/gradient/pallas_call | solution.py:143
  37.0 2.0 %collective-permute-done.12.refs_2_ = bf16[128,2560]{1,0:T(8,128)(2,1)S(1)} collective-permute-done((bf16[128,2560]{1,0:T(8,128)(2,1)S(1)}, bf16[128,2560]{1,0:T(8,128)(2,1)S(1)}, u32[]{:S(2)}, u32[]{:S(2)}) %collective-permute-start.12) | collective-permute-done | bytes 655392 | tf_op jit(solution)/shard_map/ppermute | solution.py:27
  39.0 0.7 settle.1
  39.7 2.4 %collective-permute-start.15 = (bf16[8,5120]{1,0:T(8,128)(2,1)S(1)}, bf16[8,5120]{1,0:T(8,128)(2,1)S(1)}, u32[]{:S(2)}, u32[]{:S(2)}) collective-permute-start(bf16[8,5120]{1,0:T(8,128)(2,1)S(1)} %get-tuple-element.47.refs_0_), channel_id=1, source_target_pairs={{0,12},{1,13},{2,14},{3,15},{4,8},{5,9},{6,10},{7,11},{8,4},{9,5},... | collective-permute-start | bytes 245768 | tf_op jit(solution)/shard_map/ppermute | solution.py:50
  42.1 1.2 %collective-permute-start.13 = (bf16[8,5120]{1,0:T(8,128)(2,1)S(1)}, bf16[8,5120]{1,0:T(8,128)(2,1)S(1)}, u32[]{:S(2)}, u32[]{:S(2)}) collective-permute-start(bf16[8,5120]{1,0:T(8,128)(2,1)S(1)} %get-tuple-element.47.refs_0_), channel_id=1, source_target_pairs={{0,4},{1,5},{2,6},{3,7},{4,0},{5,1},{6,2},{7,3},{8,12},{9,13},{10,... | collective-permute-start | bytes 245768 | tf_op jit(solution)/shard_map/ppermute | solution.py:50
  43.3 1.7 %collective-permute-done.15.refs_3_ = bf16[8,5120]{1,0:T(8,128)(2,1)S(1)} collective-permute-done((bf16[8,5120]{1,0:T(8,128)(2,1)S(1)}, bf16[8,5120]{1,0:T(8,128)(2,1)S(1)}, u32[]{:S(2)}, u32[]{:S(2)}) %collective-permute-start.15) | collective-permute-done | bytes 81952 | tf_op jit(solution)/shard_map/ppermute | solution.py:50
  45.0 4.7 %collective-permute-done.14.refs_2_ = bf16[8,5120]{1,0:T(8,128)(2,1)S(1)} collective-permute-done((bf16[8,5120]{1,0:T(8,128)(2,1)S(1)}, bf16[8,5120]{1,0:T(8,128)(2,1)S(1)}, u32[]{:S(2)}, u32[]{:S(2)}) %collective-permute-start.14) | collective-permute-done | bytes 81952 | tf_op jit(solution)/shard_map/ppermute | solution.py:50
  49.8 1.2 %collective-permute-start.17 = (bf16[32,5120]{1,0:T(8,128)(2,1)S(1)}, bf16[32,5120]{1,0:T(8,128)(2,1)S(1)}, u32[]{:S(2)}, u32[]{:S(2)}) collective-permute-start(bf16[32,5120]{1,0:T(8,128)(2,1)S(1)} %join.3.refs_2_), channel_id=1, source_target_pairs={{0,2},{1,3},{2,0},{3,1},{4,6},{5,7},{6,4},{7,5},{8,10},{9,11},{10,... | collective-permute-start | bytes 983048 | tf_op jit(solution)/shard_map/ppermute | solution.py:50
  51.0 0.3 collective-permute-start.16
  51.2 1.2 %collective-permute-start.21 = (bf16[16,5120]{1,0:T(8,128)(2,1)S(1)}, bf16[16,5120]{1,0:T(8,128)(2,1)S(1)}, u32[]{:S(2)}, u32[]{:S(2)}) collective-permute-start(bf16[16,5120]{1,0:T(8,128)(2,1)S(1)} %get-tuple-element.49), channel_id=1, source_target_pairs={{1,0},{0,1},{3,2},{2,3},{5,4},{4,5},{7,6},{6,7},{9,8},{8,9},{11,10... | collective-permute-start | bytes 491528 | tf_op jit(solution)/shard_map/ppermute | solution.py:50
  52.4 0.3 collective-permute-start.22
  52.8 5.7 %collective-permute-done.17.refs_4_ = bf16[32,5120]{1,0:T(8,128)(2,1)S(1)} collective-permute-done((bf16[32,5120]{1,0:T(8,128)(2,1)S(1)}, bf16[32,5120]{1,0:T(8,128)(2,1)S(1)}, u32[]{:S(2)}, u32[]{:S(2)}) %collective-permute-start.17) | collective-permute-done | bytes 327712 | tf_op jit(solution)/shard_map/ppermute | solution.py:50
  58.5 0.3 collective-permute-start.18
  58.8 0.5 collective-permute-done.16.refs_2_.refs_3_
  59.3 0.7 collective-permute-start.19
  60.0 2.8 %collective-permute-done.21.refs_1_ = bf16[16,5120]{1,0:T(8,128)(2,1)S(1)} collective-permute-done((bf16[16,5120]{1,0:T(8,128)(2,1)S(1)}, bf16[16,5120]{1,0:T(8,128)(2,1)S(1)}, u32[]{:S(2)}, u32[]{:S(2)}) %collective-permute-start.21) | collective-permute-done | bytes 163872 | tf_op jit(solution)/shard_map/ppermute | solution.py:50
  62.9 0.4 collective-permute-start.24
  63.3 0.3 collective-permute-start.25
  63.7 2.7 %collective-permute-done.18.refs_5_ = bf16[16,5120]{1,0:T(8,128)(2,1)S(1)} collective-permute-done((bf16[16,5120]{1,0:T(8,128)(2,1)S(1)}, bf16[16,5120]{1,0:T(8,128)(2,1)S(1)}, u32[]{:S(2)}, u32[]{:S(2)}) %collective-permute-start.18) | collective-permute-done | bytes 163872 | tf_op jit(solution)/shard_map/ppermute | solution.py:50
  66.4 2.3 %expert.1 = (f32[32,5120]{1,0:T(8,128)S(1)}, f32[32,5120]{1,0:T(8,128)S(1)}, f32[32,5120]{1,0:T(8,128)S(1)}, bf16[16,5120]{1,0:T(8,128)(2,1)S(1)}, bf16[16,5120]{1,0:T(8,128)(2,1)S(1)}) custom-call(bf16[5120,640]{1,0:T(8,128)(2,1)S(1)} %bitcast.19, bf16[640,5120]{1,0:T(8,128)(2,1)S(1)} %bitcast.20, bf16[32,5120]{1,0:T(8,128)(2,1)S(1)} %join.3.refs_2_, ...), custom_call_target="tpu_custom_call" | custom-call | flops 1677721600 | bytes 16711680 | tf_op jit(solution)/shard_map/expert/pallas_call | solution.py:143
  68.7 0.4 collective-permute-start.27
  69.1 0.3 collective-permute-start.23
  69.4 3.2 %collective-permute-done.24.refs_1_ = bf16[32,5120]{1,0:T(8,128)(2,1)S(1)} collective-permute-done((bf16[32,5120]{1,0:T(8,128)(2,1)S(1)}, bf16[32,5120]{1,0:T(8,128)(2,1)S(1)}, u32[]{:S(2)}, u32[]{:S(2)}) %collective-permute-start.24) | collective-permute-done | bytes 327712 | tf_op jit(solution)/shard_map/ppermute | solution.py:50
  72.6 3.4 %collective-permute-done.27.refs_1_ = bf16[16,5120]{1,0:T(8,128)(2,1)S(1)} collective-permute-done((bf16[16,5120]{1,0:T(8,128)(2,1)S(1)}, bf16[16,5120]{1,0:T(8,128)(2,1)S(1)}, u32[]{:S(2)}, u32[]{:S(2)}) %collective-permute-start.27) | collective-permute-done | bytes 163872 | tf_op jit(solution)/shard_map/ppermute | solution.py:50
  76.1 0.3 collective-permute-start.28
  76.4 0.2 collective-permute-start.26
  76.6 2.6 %collective-permute-start.30 = (bf16[8,5120]{1,0:T(8,128)(2,1)S(1)}, bf16[8,5120]{1,0:T(8,128)(2,1)S(1)}, u32[]{:S(2)}, u32[]{:S(2)}) collective-permute-start(bf16[8,5120]{1,0:T(8,128)(2,1)S(1)} %get-tuple-element.59), channel_id=1, source_target_pairs={{8,0},{9,1},{10,2},{11,3},{12,4},{13,5},{14,6},{15,7},{0,8},{1,9},... | collective-permute-start | bytes 245768 | tf_op jit(solution)/shard_map/ppermute | solution.py:50
  79.2 1.0 collective-permute-start.31
  80.2 0.8 collective-permute-done.30.refs_2_
  81.0 3.8 %collective-permute-done.31.refs_3_ = bf16[8,5120]{1,0:T(8,128)(2,1)S(1)} collective-permute-done((bf16[8,5120]{1,0:T(8,128)(2,1)S(1)}, bf16[8,5120]{1,0:T(8,128)(2,1)S(1)}, u32[]{:S(2)}, u32[]{:S(2)}) %collective-permute-start.31) | collective-permute-done | bytes 81952 | tf_op jit(solution)/shard_map/ppermute | solution.py:50
  84.9 1.3 %collective-permute-start.36 = (f32[8,5120]{1,0:T(8,128)S(1)}, f32[8,5120]{1,0:T(8,128)S(1)}, u32[]{:S(2)}, u32[]{:S(2)}) collective-permute-start(f32[8,5120]{1,0:T(8,128)S(1)} %add_last.2.refs_3_), channel_id=1, source_target_pairs={{0,16},{1,17},{2,18},{3,19},{4,20},{5,21},{6,22},{7,23},{8,24},{9,... | collective-permute-start | bytes 491528 | tf_op jit(solution)/shard_map/ppermute | solution.py:27
  86.2 0.1 add_blocks.3
  86.4 0.8 collective-permute-start.33
  87.2 2.8 %collective-permute-start.34 = (bf16[8,5120]{1,0:T(8,128)(2,1)S(1)}, bf16[8,5120]{1,0:T(8,128)(2,1)S(1)}, u32[]{:S(2)}, u32[]{:S(2)}) collective-permute-start(bf16[8,5120]{1,0:T(8,128)(2,1)S(1)} %get-tuple-element.64), channel_id=1, source_target_pairs={{12,0},{13,1},{14,2},{15,3},{8,4},{9,5},{10,6},{11,7},{4,8},{5,9},... | collective-permute-start | bytes 245768 | tf_op jit(solution)/shard_map/ppermute | solution.py:50
  90.0 0.1 copy.13
  90.1 1.2 %collective-permute-done.36 = f32[8,5120]{1,0:T(8,128)S(1)} collective-permute-done((f32[8,5120]{1,0:T(8,128)S(1)}, f32[8,5120]{1,0:T(8,128)S(1)}, u32[]{:S(2)}, u32[]{:S(2)}) %collective-permute-start.36) | collective-permute-done | bytes 163872 | tf_op jit(solution)/shard_map/ppermute | solution.py:27
  91.3 0.1 copy.12
  91.4 1.3 %collective-permute-done.34.refs_2_ = bf16[8,5120]{1,0:T(8,128)(2,1)S(1)} collective-permute-done((bf16[8,5120]{1,0:T(8,128)(2,1)S(1)}, bf16[8,5120]{1,0:T(8,128)(2,1)S(1)}, u32[]{:S(2)}, u32[]{:S(2)}) %collective-permute-start.34) | collective-permute-done | bytes 81952 | tf_op jit(solution)/shard_map/ppermute | solution.py:50
  92.8 1.3 %collective-permute-start.35 = (f32[8,5120]{1,0:T(8,128)S(1)}, f32[8,5120]{1,0:T(8,128)S(1)}, u32[]{:S(2)}, u32[]{:S(2)}) collective-permute-start(f32[8,5120]{1,0:T(8,128)S(1)} %add_last.3.back_ref), channel_id=1, source_target_pairs={{0,16},{1,17},{2,18},{3,19},{4,20},{5,21},{6,22},{7,23},{8,24},{9,... | collective-permute-start | bytes 491528 | tf_op jit(solution)/shard_map/ppermute | solution.py:17
  94.1 0.9 maximum_select_fusion
  95.0 1.7 %finish.2 = bf16[128,5120]{1,0:T(8,128)(2,1)} custom-call(bf16[128,5120]{1,0:T(8,128)(2,1)S(1)} %get-tuple-element.46.res_ref, f32[8,5120]{1,0:T(8,128)S(1)} %add_last.3.back_ref, f32[2,128]{1,0:T(2,128)S(1)} %get-tuple-element.38.refs_1_.refs_5_.refs_0_), custom_call_target="tpu_custom_call" | custom-call | flops 32768000 | bytes 2786304 | tf_op jit(solution)/shard_map/finish/pallas_call | solution.py:143
  96.7 4.3 %collective-permute-done.35.back_ref = f32[8,5120]{1,0:T(8,128)S(1)} collective-permute-done((f32[8,5120]{1,0:T(8,128)S(1)}, f32[8,5120]{1,0:T(8,128)S(1)}, u32[]{:S(2)}, u32[]{:S(2)}) %collective-permute-start.35) | collective-permute-done | bytes 163872 | tf_op jit(solution)/shard_map/ppermute | solution.py:17
  101.0 1.7 %finish.3 = bf16[128,5120]{1,0:T(8,128)(2,1)} custom-call(bf16[144,5120]{1,0:T(8,128)(2,1)S(1)} %collective-permute-done.20.refs_7_.res_ref, f32[8,5120]{1,0:T(8,128)S(1)} %collective-permute-done.35.back_ref), custom_call_target="tpu_custom_call" | custom-call | flops 32768000 | bytes 2949120 | tf_op jit(solution)/shard_map/finish/pallas_call | solution.py:143
  (58 shorter events, 0.8 us)
Async XLA Ops:
  0.6 16.3 %copy-start.5 = (f32[1,128]{1,0:T(1,128)S(1)}, f32[1,128]{1,0:T(1,128)}, u32[]{:S(2)}) copy-start(f32[1,128]{1,0:T(1,128)} %refs_2_.1) | copy-start | bytes 1540
  0.6 16.3 %copy-start.6 = (s32[1,128]{1,0:T(1,128)S(1)}, s32[1,128]{1,0:T(1,128)}, u32[]{:S(2)}) copy-start(s32[1,128]{1,0:T(1,128)} %refs_3_.1) | copy-start | bytes 1540
  0.7 16.3 %copy-start.4 = (f32[1,5120]{1,0:T(1,128)S(1)}, f32[1,5120]{1,0:T(1,128)}, u32[]{:S(2)}) copy-start(f32[1,5120]{1,0:T(1,128)} %refs_1_.1) | copy-start | bytes 61444
  0.7 16.3 %copy-start.1 = (bf16[1,128,5120]{2,1,0:T(8,128)(2,1)S(1)}, bf16[1,128,5120]{2,1,0:T(8,128)(2,1)}, u32[]{:S(2)}) copy-start(bf16[1,128,5120]{2,1,0:T(8,128)(2,1)} %param.9) | copy-start | bytes 3932164
  1.8 1.3 %collective-permute-start = (bf16[8,5120]{1,0:T(8,128)(2,1)S(1)}, bf16[8,5120]{1,0:T(8,128)(2,1)S(1)}, u32[]{:S(2)}, u32[]{:S(2)}) collective-permute-start(bf16[8,5120]{1,0:T(8,128)(2,1)S(1)} %bitcast.28), channel_id=1, source_target_pairs={{0,16},{16,0},{1,17},{17,1},{2,18},{18,2},{3,19},{19,3},{4,20},{20... | collective-permute-start | bytes 245768 | tf_op jit(solution)/shard_map/ppermute | solution.py:22
  2.0 17.7 %copy-start.2 = (bf16[1,128,5120]{2,1,0:T(8,128)(2,1)S(1)}, bf16[1,128,5120]{2,1,0:T(8,128)(2,1)}, u32[]{:S(2)}) copy-start(bf16[1,128,5120]{2,1,0:T(8,128)(2,1)} %param.11) | copy-start | bytes 3932164
  3.2 7.1 %collective-permute-start.3 = (bf16[8,5120]{1,0:T(8,128)(2,1)S(1)}, bf16[8,5120]{1,0:T(8,128)(2,1)S(1)}, u32[]{:S(2)}, u32[]{:S(2)}) collective-permute-start(bf16[8,5120]{1,0:T(8,128)(2,1)S(1)} %broadcast_select_fusion.refs_0_), channel_id=1, source_target_pairs={{0,12},{1,13},{2,14},{3,15},{4,8},{5,9},{6,10},{7,11},{8,4},{9,5},... | collective-permute-start | bytes 245768 | tf_op jit(solution)/shard_map/ppermute | solution.py:50
  7.7 6.6 %collective-permute-start.2 = (bf16[8,5120]{1,0:T(8,128)(2,1)S(1)}, bf16[8,5120]{1,0:T(8,128)(2,1)S(1)}, u32[]{:S(2)}, u32[]{:S(2)}) collective-permute-start(bf16[8,5120]{1,0:T(8,128)(2,1)S(1)} %broadcast_select_fusion.refs_0_), channel_id=1, source_target_pairs={{0,8},{1,9},{2,10},{3,11},{4,12},{5,13},{6,14},{7,15},{8,0},{9,1},... | collective-permute-start | bytes 245768 | tf_op jit(solution)/shard_map/ppermute | solution.py:50
  7.7 6.6 %collective-permute-start.1 = (bf16[8,5120]{1,0:T(8,128)(2,1)S(1)}, bf16[8,5120]{1,0:T(8,128)(2,1)S(1)}, u32[]{:S(2)}, u32[]{:S(2)}) collective-permute-start(bf16[8,5120]{1,0:T(8,128)(2,1)S(1)} %broadcast_select_fusion.refs_0_), channel_id=1, source_target_pairs={{0,4},{1,5},{2,6},{3,7},{4,0},{5,1},{6,2},{7,3},{8,12},{9,13},{10,... | collective-permute-start | bytes 245768 | tf_op jit(solution)/shard_map/ppermute | solution.py:50
  14.4 8.1 %collective-permute-start.7 = (bf16[32,5120]{1,0:T(8,128)(2,1)S(1)}, bf16[32,5120]{1,0:T(8,128)(2,1)S(1)}, u32[]{:S(2)}, u32[]{:S(2)}) collective-permute-start(bf16[32,5120]{1,0:T(8,128)(2,1)S(1)} %join.2.refs_4_), channel_id=1, source_target_pairs={{0,2},{1,3},{2,0},{3,1},{4,6},{5,7},{6,4},{7,5},{8,10},{9,11},{10,... | collective-permute-start | bytes 983048 | tf_op jit(solution)/shard_map/ppermute | solution.py:50
  15.7 8.9 %collective-permute-start.6 = (bf16[32,5120]{1,0:T(8,128)(2,1)S(1)}, bf16[32,5120]{1,0:T(8,128)(2,1)S(1)}, u32[]{:S(2)}, u32[]{:S(2)}) collective-permute-start(bf16[32,5120]{1,0:T(8,128)(2,1)S(1)} %join.2.refs_4_), channel_id=1, source_target_pairs={{0,1},{1,0},{2,3},{3,2},{4,5},{5,4},{6,7},{7,6},{8,9},{9,8},{10,11... | collective-permute-start | bytes 983048 | tf_op jit(solution)/shard_map/ppermute | solution.py:50
  17.8 8.1 %collective-permute-start.4 = (bf16[128,1280]{1,0:T(8,128)(2,1)S(1)}, bf16[128,1280]{1,0:T(8,128)(2,1)S(1)}, u32[]{:S(2)}, u32[]{:S(2)}) collective-permute-start(bf16[128,1280]{1,0:T(8,128)(2,1)S(1)} %get-tuple-element.35), channel_id=1, source_target_pairs={{0,16},{16,0},{1,17},{17,1},{2,18},{18,2},{3,19},{19,3},{4,20},{20... | collective-permute-start | bytes 983048 | tf_op jit(solution)/shard_map/ppermute | solution.py:22
  19.6 7.6 %collective-permute-start.5 = (bf16[128,1280]{1,0:T(8,128)(2,1)S(1)}, bf16[128,1280]{1,0:T(8,128)(2,1)S(1)}, u32[]{:S(2)}, u32[]{:S(2)}) collective-permute-start(bf16[128,1280]{1,0:T(8,128)(2,1)S(1)} %get-tuple-element.36), channel_id=1, source_target_pairs={{0,16},{16,0},{1,17},{17,1},{2,18},{18,2},{3,19},{19,3},{4,20},{20... | collective-permute-start | bytes 983048 | tf_op jit(solution)/shard_map/ppermute | solution.py:22
  19.8 8.7 %collective-permute-start.10 = (bf16[128,1280]{1,0:T(8,128)(2,1)S(1)}, bf16[128,1280]{1,0:T(8,128)(2,1)S(1)}, u32[]{:S(2)}, u32[]{:S(2)}) collective-permute-start(bf16[128,1280]{1,0:T(8,128)(2,1)S(1)} %get-tuple-element.39), channel_id=1, source_target_pairs={{0,16},{16,0},{1,17},{17,1},{2,18},{18,2},{3,19},{19,3},{4,20},{20... | collective-permute-start | bytes 983048 | tf_op jit(solution)/shard_map/ppermute | solution.py:22
  22.5 6.0 %collective-permute-start.11 = (bf16[128,1280]{1,0:T(8,128)(2,1)S(1)}, bf16[128,1280]{1,0:T(8,128)(2,1)S(1)}, u32[]{:S(2)}, u32[]{:S(2)}) collective-permute-start(bf16[128,1280]{1,0:T(8,128)(2,1)S(1)} %get-tuple-element.40), channel_id=1, source_target_pairs={{0,16},{16,0},{1,17},{17,1},{2,18},{18,2},{3,19},{19,3},{4,20},{20... | collective-permute-start | bytes 983048 | tf_op jit(solution)/shard_map/ppermute | solution.py:22
  24.6 39.1 %collective-permute-start.20 = (bf16[144,5120]{1,0:T(8,128)(2,1)S(1)}, bf16[144,5120]{1,0:T(8,128)(2,1)S(1)}, u32[]{:S(2)}, u32[]{:S(2)}) collective-permute-start(bf16[144,5120]{1,0:T(8,128)(2,1)S(1)} %get-tuple-element.34.refs_1_), channel_id=1, source_target_pairs={{0,16},{1,17},{2,18},{3,19},{4,20},{5,21},{6,22},{7,23},{8,24},{9,... | collective-permute-start | bytes 4423688 | tf_op jit(solution)/shard_map/ppermute | solution.py:17
  25.9 4.2 %collective-permute-start.8 = (bf16[16,5120]{1,0:T(8,128)(2,1)S(1)}, bf16[16,5120]{1,0:T(8,128)(2,1)S(1)}, u32[]{:S(2)}, u32[]{:S(2)}) collective-permute-start(bf16[16,5120]{1,0:T(8,128)(2,1)S(1)} %slice.24), channel_id=1, source_target_pairs={{0,1},{1,0},{2,3},{3,2},{4,5},{5,4},{6,7},{7,6},{8,9},{9,8},{10,11... | collective-permute-start | bytes 491528 | tf_op jit(solution)/shard_map/ppermute | solution.py:50
  27.2 4.5 %collective-permute-start.9 = (bf16[16,5120]{1,0:T(8,128)(2,1)S(1)}, bf16[16,5120]{1,0:T(8,128)(2,1)S(1)}, u32[]{:S(2)}, u32[]{:S(2)}) collective-permute-start(bf16[16,5120]{1,0:T(8,128)(2,1)S(1)} %slice.25), channel_id=1, source_target_pairs={{0,2},{1,3},{2,0},{3,1},{4,6},{5,7},{6,4},{7,5},{8,10},{9,11},{10,... | collective-permute-start | bytes 491528 | tf_op jit(solution)/shard_map/ppermute | solution.py:50
  31.7 7.4 %copy-start.3 = (f32[1,5120]{1,0:T(1,128)S(1)}, f32[1,5120]{1,0:T(1,128)}, u32[]{:S(2)}) copy-start(f32[1,5120]{1,0:T(1,128)} %refs_4_.1) | copy-start | bytes 61444
  31.7 34.7 %copy-start = (bf16[1,640,5120]{2,1,0:T(8,128)(2,1)S(1)}, bf16[1,640,5120]{2,1,0:T(8,128)(2,1)}, u32[]{:S(2)}) copy-start(bf16[1,640,5120]{2,1,0:T(8,128)(2,1)} %param.15) | copy-start | bytes 19660804
  33.7 5.3 %collective-permute-start.12 = (bf16[128,2560]{1,0:T(8,128)(2,1)S(1)}, bf16[128,2560]{1,0:T(8,128)(2,1)S(1)}, u32[]{:S(2)}, u32[]{:S(2)}) collective-permute-start(bf16[128,2560]{1,0:T(8,128)(2,1)S(1)} %get-tuple-element.41.refs_3_), channel_id=1, source_target_pairs={{0,16},{1,17},{2,18},{3,19},{4,20},{5,21},{6,22},{7,23},{8,24},{9,... | collective-permute-start | bytes 1966088 | tf_op jit(solution)/shard_map/ppermute | solution.py:27
  35.0 31.3 %slice-start = ((s8[6553600]{0:T(1024)(128)(4,1)}), s8[4194304]{0:T(1024)(128)(4,1)S(1)}, s32[]{:S(2)}) async-start(s8[6553600]{0:T(1024)(128)(4,1)} %bitcast.17), calls=%async_computation | async-start | bytes 8388608
  39.0 27.3 %slice-start.1 = ((s8[6553600]{0:T(1024)(128)(4,1)}), s8[2359296]{0:T(1024)(128)(4,1)S(1)}, s32[]{:S(2)}) async-start(s8[6553600]{0:T(1024)(128)(4,1)} %bitcast.17), calls=%async_computation.1 | async-start | bytes 4718592
  39.7 5.3 %collective-permute-start.15 = (bf16[8,5120]{1,0:T(8,128)(2,1)S(1)}, bf16[8,5120]{1,0:T(8,128)(2,1)S(1)}, u32[]{:S(2)}, u32[]{:S(2)}) collective-permute-start(bf16[8,5120]{1,0:T(8,128)(2,1)S(1)} %get-tuple-element.47.refs_0_), channel_id=1, source_target_pairs={{0,12},{1,13},{2,14},{3,15},{4,8},{5,9},{6,10},{7,11},{8,4},{9,5},... | collective-permute-start | bytes 245768 | tf_op jit(solution)/shard_map/ppermute | solution.py:50
  42.1 7.6 %collective-permute-start.14 = (bf16[8,5120]{1,0:T(8,128)(2,1)S(1)}, bf16[8,5120]{1,0:T(8,128)(2,1)S(1)}, u32[]{:S(2)}, u32[]{:S(2)}) collective-permute-start(bf16[8,5120]{1,0:T(8,128)(2,1)S(1)} %get-tuple-element.47.refs_0_), channel_id=1, source_target_pairs={{0,8},{1,9},{2,10},{3,11},{4,12},{5,13},{6,14},{7,15},{8,0},{9,1},... | collective-permute-start | bytes 245768 | tf_op jit(solution)/shard_map/ppermute | solution.py:50
  42.1 7.6 %collective-permute-start.13 = (bf16[8,5120]{1,0:T(8,128)(2,1)S(1)}, bf16[8,5120]{1,0:T(8,128)(2,1)S(1)}, u32[]{:S(2)}, u32[]{:S(2)}) collective-permute-start(bf16[8,5120]{1,0:T(8,128)(2,1)S(1)} %get-tuple-element.47.refs_0_), channel_id=1, source_target_pairs={{0,4},{1,5},{2,6},{3,7},{4,0},{5,1},{6,2},{7,3},{8,12},{9,13},{10,... | collective-permute-start | bytes 245768 | tf_op jit(solution)/shard_map/ppermute | solution.py:50
  49.8 8.7 %collective-permute-start.17 = (bf16[32,5120]{1,0:T(8,128)(2,1)S(1)}, bf16[32,5120]{1,0:T(8,128)(2,1)S(1)}, u32[]{:S(2)}, u32[]{:S(2)}) collective-permute-start(bf16[32,5120]{1,0:T(8,128)(2,1)S(1)} %join.3.refs_2_), channel_id=1, source_target_pairs={{0,2},{1,3},{2,0},{3,1},{4,6},{5,7},{6,4},{7,5},{8,10},{9,11},{10,... | collective-permute-start | bytes 983048 | tf_op jit(solution)/shard_map/ppermute | solution.py:50
  51.0 8.4 %collective-permute-start.16 = (bf16[32,5120]{1,0:T(8,128)(2,1)S(1)}, bf16[32,5120]{1,0:T(8,128)(2,1)S(1)}, u32[]{:S(2)}, u32[]{:S(2)}) collective-permute-start(bf16[32,5120]{1,0:T(8,128)(2,1)S(1)} %join.3.refs_2_), channel_id=1, source_target_pairs={{0,1},{1,0},{2,3},{3,2},{4,5},{5,4},{6,7},{7,6},{8,9},{9,8},{10,11... | collective-permute-start | bytes 983048 | tf_op jit(solution)/shard_map/ppermute | solution.py:50
  51.2 11.6 %collective-permute-start.21 = (bf16[16,5120]{1,0:T(8,128)(2,1)S(1)}, bf16[16,5120]{1,0:T(8,128)(2,1)S(1)}, u32[]{:S(2)}, u32[]{:S(2)}) collective-permute-start(bf16[16,5120]{1,0:T(8,128)(2,1)S(1)} %get-tuple-element.49), channel_id=1, source_target_pairs={{1,0},{0,1},{3,2},{2,3},{5,4},{4,5},{7,6},{6,7},{9,8},{8,9},{11,10... | collective-permute-start | bytes 491528 | tf_op jit(solution)/shard_map/ppermute | solution.py:50
  52.4 10.9 %collective-permute-start.22 = (bf16[16,5120]{1,0:T(8,128)(2,1)S(1)}, bf16[16,5120]{1,0:T(8,128)(2,1)S(1)}, u32[]{:S(2)}, u32[]{:S(2)}) collective-permute-start(bf16[16,5120]{1,0:T(8,128)(2,1)S(1)} %get-tuple-element.51), channel_id=1, source_target_pairs={{2,0},{3,1},{0,2},{1,3},{6,4},{7,5},{4,6},{5,7},{10,8},{11,9},{8,1... | collective-permute-start | bytes 491528 | tf_op jit(solution)/shard_map/ppermute | solution.py:50
  58.5 7.8 %collective-permute-start.18 = (bf16[16,5120]{1,0:T(8,128)(2,1)S(1)}, bf16[16,5120]{1,0:T(8,128)(2,1)S(1)}, u32[]{:S(2)}, u32[]{:S(2)}) collective-permute-start(bf16[16,5120]{1,0:T(8,128)(2,1)S(1)} %slice.26), channel_id=1, source_target_pairs={{0,1},{1,0},{2,3},{3,2},{4,5},{5,4},{6,7},{7,6},{8,9},{9,8},{10,11... | collective-permute-start | bytes 491528 | tf_op jit(solution)/shard_map/ppermute | solution.py:50
  59.3 7.0 %collective-permute-start.19 = (bf16[16,5120]{1,0:T(8,128)(2,1)S(1)}, bf16[16,5120]{1,0:T(8,128)(2,1)S(1)}, u32[]{:S(2)}, u32[]{:S(2)}) collective-permute-start(bf16[16,5120]{1,0:T(8,128)(2,1)S(1)} %slice.27), channel_id=1, source_target_pairs={{0,2},{1,3},{2,0},{3,1},{4,6},{5,7},{6,4},{7,5},{8,10},{9,11},{10,... | collective-permute-start | bytes 491528 | tf_op jit(solution)/shard_map/ppermute | solution.py:50
  62.9 9.6 %collective-permute-start.24 = (bf16[32,5120]{1,0:T(8,128)(2,1)S(1)}, bf16[32,5120]{1,0:T(8,128)(2,1)S(1)}, u32[]{:S(2)}, u32[]{:S(2)}) collective-permute-start(bf16[32,5120]{1,0:T(8,128)(2,1)S(1)} %add_half.4.refs_8_), channel_id=1, source_target_pairs={{2,0},{3,1},{0,2},{1,3},{6,4},{7,5},{4,6},{5,7},{10,8},{11,9},{8,1... | collective-permute-start | bytes 983048 | tf_op jit(solution)/shard_map/ppermute | solution.py:50
  63.3 9.2 %collective-permute-start.25 = (bf16[32,5120]{1,0:T(8,128)(2,1)S(1)}, bf16[32,5120]{1,0:T(8,128)(2,1)S(1)}, u32[]{:S(2)}, u32[]{:S(2)}) collective-permute-start(bf16[32,5120]{1,0:T(8,128)(2,1)S(1)} %add_half.5.refs_9_), channel_id=1, source_target_pairs={{1,0},{0,1},{3,2},{2,3},{5,4},{4,5},{7,6},{6,7},{9,8},{8,9},{11,10... | collective-permute-start | bytes 983048 | tf_op jit(solution)/shard_map/ppermute | solution.py:50
  68.7 7.3 %collective-permute-start.27 = (bf16[16,5120]{1,0:T(8,128)(2,1)S(1)}, bf16[16,5120]{1,0:T(8,128)(2,1)S(1)}, u32[]{:S(2)}, u32[]{:S(2)}) collective-permute-start(bf16[16,5120]{1,0:T(8,128)(2,1)S(1)} %get-tuple-element.57), channel_id=1, source_target_pairs={{2,0},{3,1},{0,2},{1,3},{6,4},{7,5},{4,6},{5,7},{10,8},{11,9},{8,1... | collective-permute-start | bytes 491528 | tf_op jit(solution)/shard_map/ppermute | solution.py:50
  69.1 7.3 %collective-permute-start.23 = (bf16[16,5120]{1,0:T(8,128)(2,1)S(1)}, bf16[16,5120]{1,0:T(8,128)(2,1)S(1)}, u32[]{:S(2)}, u32[]{:S(2)}) collective-permute-start(bf16[16,5120]{1,0:T(8,128)(2,1)S(1)} %get-tuple-element.54), channel_id=1, source_target_pairs={{1,0},{0,1},{3,2},{2,3},{5,4},{4,5},{7,6},{6,7},{9,8},{8,9},{11,10... | collective-permute-start | bytes 491528 | tf_op jit(solution)/shard_map/ppermute | solution.py:50
  76.1 10.1 %collective-permute-start.28 = (bf16[32,5120]{1,0:T(8,128)(2,1)S(1)}, bf16[32,5120]{1,0:T(8,128)(2,1)S(1)}, u32[]{:S(2)}, u32[]{:S(2)}) collective-permute-start(bf16[32,5120]{1,0:T(8,128)(2,1)S(1)} %add_half.7.refs_5_), channel_id=1, source_target_pairs={{1,0},{0,1},{3,2},{2,3},{5,4},{4,5},{7,6},{6,7},{9,8},{8,9},{11,10... | collective-permute-start | bytes 983048 | tf_op jit(solution)/shard_map/ppermute | solution.py:50
  76.4 9.8 %collective-permute-start.26 = (bf16[32,5120]{1,0:T(8,128)(2,1)S(1)}, bf16[32,5120]{1,0:T(8,128)(2,1)S(1)}, u32[]{:S(2)}, u32[]{:S(2)}) collective-permute-start(bf16[32,5120]{1,0:T(8,128)(2,1)S(1)} %add_half.6.refs_4_), channel_id=1, source_target_pairs={{2,0},{3,1},{0,2},{1,3},{6,4},{7,5},{4,6},{5,7},{10,8},{11,9},{8,1... | collective-permute-start | bytes 983048 | tf_op jit(solution)/shard_map/ppermute | solution.py:50
  76.6 3.6 %collective-permute-start.29 = (bf16[8,5120]{1,0:T(8,128)(2,1)S(1)}, bf16[8,5120]{1,0:T(8,128)(2,1)S(1)}, u32[]{:S(2)}, u32[]{:S(2)}) collective-permute-start(bf16[8,5120]{1,0:T(8,128)(2,1)S(1)} %get-tuple-element.58), channel_id=1, source_target_pairs={{4,0},{5,1},{6,2},{7,3},{0,4},{1,5},{2,6},{3,7},{12,8},{13,9},{14,... | collective-permute-start | bytes 245768 | tf_op jit(solution)/shard_map/ppermute | solution.py:50
  76.6 4.4 %collective-permute-start.30 = (bf16[8,5120]{1,0:T(8,128)(2,1)S(1)}, bf16[8,5120]{1,0:T(8,128)(2,1)S(1)}, u32[]{:S(2)}, u32[]{:S(2)}) collective-permute-start(bf16[8,5120]{1,0:T(8,128)(2,1)S(1)} %get-tuple-element.59), channel_id=1, source_target_pairs={{8,0},{9,1},{10,2},{11,3},{12,4},{13,5},{14,6},{15,7},{0,8},{1,9},... | collective-permute-start | bytes 245768 | tf_op jit(solution)/shard_map/ppermute | solution.py:50
  79.2 5.7 %collective-permute-start.31 = (bf16[8,5120]{1,0:T(8,128)(2,1)S(1)}, bf16[8,5120]{1,0:T(8,128)(2,1)S(1)}, u32[]{:S(2)}, u32[]{:S(2)}) collective-permute-start(bf16[8,5120]{1,0:T(8,128)(2,1)S(1)} %get-tuple-element.60), channel_id=1, source_target_pairs={{12,0},{13,1},{14,2},{15,3},{8,4},{9,5},{10,6},{11,7},{4,8},{5,9},... | collective-permute-start | bytes 245768 | tf_op jit(solution)/shard_map/ppermute | solution.py:50
  84.9 6.4 %collective-permute-start.36 = (f32[8,5120]{1,0:T(8,128)S(1)}, f32[8,5120]{1,0:T(8,128)S(1)}, u32[]{:S(2)}, u32[]{:S(2)}) collective-permute-start(f32[8,5120]{1,0:T(8,128)S(1)} %add_last.2.refs_3_), channel_id=1, source_target_pairs={{0,16},{1,17},{2,18},{3,19},{4,20},{5,21},{6,22},{7,23},{8,24},{9,... | collective-permute-start | bytes 491528 | tf_op jit(solution)/shard_map/ppermute | solution.py:27
  86.3 5.1 %collective-permute-start.32 = (bf16[8,5120]{1,0:T(8,128)(2,1)S(1)}, bf16[8,5120]{1,0:T(8,128)(2,1)S(1)}, u32[]{:S(2)}, u32[]{:S(2)}) collective-permute-start(bf16[8,5120]{1,0:T(8,128)(2,1)S(1)} %get-tuple-element.62), channel_id=1, source_target_pairs={{4,0},{5,1},{6,2},{7,3},{0,4},{1,5},{2,6},{3,7},{12,8},{13,9},{14,... | collective-permute-start | bytes 245768 | tf_op jit(solution)/shard_map/ppermute | solution.py:50
  86.4 5.0 %collective-permute-start.33 = (bf16[8,5120]{1,0:T(8,128)(2,1)S(1)}, bf16[8,5120]{1,0:T(8,128)(2,1)S(1)}, u32[]{:S(2)}, u32[]{:S(2)}) collective-permute-start(bf16[8,5120]{1,0:T(8,128)(2,1)S(1)} %get-tuple-element.63), channel_id=1, source_target_pairs={{8,0},{9,1},{10,2},{11,3},{12,4},{13,5},{14,6},{15,7},{0,8},{1,9},... | collective-permute-start | bytes 245768 | tf_op jit(solution)/shard_map/ppermute | solution.py:50
  87.2 5.6 %collective-permute-start.34 = (bf16[8,5120]{1,0:T(8,128)(2,1)S(1)}, bf16[8,5120]{1,0:T(8,128)(2,1)S(1)}, u32[]{:S(2)}, u32[]{:S(2)}) collective-permute-start(bf16[8,5120]{1,0:T(8,128)(2,1)S(1)} %get-tuple-element.64), channel_id=1, source_target_pairs={{12,0},{13,1},{14,2},{15,3},{8,4},{9,5},{10,6},{11,7},{4,8},{5,9},... | collective-permute-start | bytes 245768 | tf_op jit(solution)/shard_map/ppermute | solution.py:50
  92.8 8.2 %collective-permute-start.35 = (f32[8,5120]{1,0:T(8,128)S(1)}, f32[8,5120]{1,0:T(8,128)S(1)}, u32[]{:S(2)}, u32[]{:S(2)}) collective-permute-start(f32[8,5120]{1,0:T(8,128)S(1)} %add_last.3.back_ref), channel_id=1, source_target_pairs={{0,16},{1,17},{2,18},{3,19},{4,20},{5,21},{6,22},{7,23},{8,24},{9,... | collective-permute-start | bytes 491528 | tf_op jit(solution)/shard_map/ppermute | solution.py:17

commit v4 on v3

--- a/solution.py
+++ b/solution.py
@@ -67,10 +67,10 @@
             listed += [jnp.bfloat16] * 2 if b and c else [jnp.float32]
         return listed
 
-    def gather(self, block):
+    def gather(self, block, first=(), second=lambda own: ()):
         na, nb, nc = self.sizes
         rows = block.shape[0]
-        own = join([block] + [self.shift(block, (s, 0, 0)) for s in range(1, na)])
+        own = join([block] + [self.shift(block, (s, 0, 0)) for s in range(1, na)], first)
         half = rows * (na - na // 2)
         pieces = {(0, 0): [own]}
         for b in range(1, nb):
@@ -79,9 +79,8 @@
             pieces[0, c] = [self.shift(own, (0, 0, c))]
         for b in range(1, nb):
             for c in range(1, nc):
-                first = self.shift(pieces[b, 0][0][:half], (0, 0, c))
-                second = self.shift(pieces[0, c][0][half:], (0, b, 0))
-                pieces[b, c] = [first, second]
+                upper, lower = halves_of(pieces[b, 0][0], pieces[0, c][0], half, second(own))
+                pieces[b, c] = [self.shift(upper, (0, 0, c)), self.shift(lower, (0, b, 0))]
         return sum((pieces[k] for k in self.offsets()), [])
 
     def scatter(self, pieces, rows, after=()):
@@ -104,7 +103,7 @@
         after = yield halves
         blocks = add_blocks(held[0, 0][0], arrived, rows, after)
         more = [self.shift(blocks[s], (s, 0, 0), back=True) for s in range(1, na)]
-        after = yield blocks
+        after = yield blocks, more
         yield add_last(blocks[0], more, after)
 
 
@@ -152,7 +151,7 @@
     )(*args)
 
 
-def join(blocks):
+def join(blocks, after=()):
     if blocks[0].shape[0] % 8:
         return jnp.concatenate(blocks, axis=0)
 
@@ -161,7 +160,23 @@
         refs[-1][...] = rows.astype(jnp.bfloat16)
 
     one = jax.ShapeDtypeStruct((len(blocks) * blocks[0].shape[0], blocks[0].shape[1]), jnp.bfloat16)
-    return local_kernel(kernel, "join", [one], blocks)[0]
+    return local_kernel(kernel, "join", [one], blocks, after)[0]
+
+
+def halves_of(first, second, half, after):
+    if half % 16 or not after:
+        return first[:half], second[half:]
+
+    def kernel(first_ref, second_ref, upper_ref, lower_ref):
+        upper_ref[...] = first_ref[:half]
+        lower_ref[...] = second_ref[half:]
+
+    width = first.shape[1]
+    outs = [
+        jax.ShapeDtypeStruct((half, width), first.dtype),
+        jax.ShapeDtypeStruct((second.shape[0] - half, width), first.dtype),
+    ]
+    return local_kernel(kernel, "halves", outs, [first, second], after)
 
 
 def add_half(piece, more, start, after):
@@ -444,34 +459,68 @@
     )
 
 
-def finish(res, back, gates=None):
+def finish(section, res, back, gates=None):
     tokens, width = res.shape[0] - (EXTRA if gates is None else 0), res.shape[1]
     one = jax.ShapeDtypeStruct((tokens, width), jnp.bfloat16)
     step = next(s for s in (1280, 1024, 512, 256, 128) if width % s == 0)
-
-    def kernel(res_ref, back_ref, *refs):
-        out_ref = refs[-1]
+    parts = [slice(at, at + step) for at in range(0, width, step)]
+
+    def kernel(section, res_ref, back_ref, *refs):
+        out_any, out_ref, sems = refs[-3:]
+        copies = [
+            pltpu.make_async_copy(out_ref.at[:, c], out_any.at[:, c], sems.at[i])
+            for i, c in enumerate(parts)
+        ]
+
+        def compute():
+            if gates is None:
+                extra = res_ref[tokens:, :tokens].astype(jnp.float32)
+                gate, slot = extra[0:1] + extra[1:2] + extra[2:3], extra[3:4]
+            else:
+                gate, slot = refs[0][0:1], refs[0][1:2]
+            gate = jnp.broadcast_to(gate, (CAP, tokens)).T[:, 0:1]
+            slots = lax.broadcasted_iota(jnp.int32, (CAP, tokens), 0).astype(jnp.float32)
+            onehot = jnp.where(slot == slots, 1.0, 0.0).T
+            onehot = jnp.concatenate([onehot] * 3, axis=1).astype(jnp.bfloat16)
+            for copy, columns in zip(copies, parts):
+                back = back_ref[:, columns]
+                high = back.astype(jnp.bfloat16).astype(jnp.float32)
+                middle = (back - high).astype(jnp.bfloat16).astype(jnp.float32)
+                three = jnp.concatenate([high, middle, back - high - middle], axis=0)
+                moved = dot(onehot, three.astype(jnp.bfloat16))
+                here = res_ref[:tokens, columns].astype(jnp.float32)
+                out_ref[:, columns] = (here + gate * moved).astype(jnp.bfloat16)
+                copy.start()
+
         if gates is None:
-            extra = res_ref[tokens:, :tokens].astype(jnp.float32)
-            gate, slot = extra[0:1] + extra[1:2] + extra[2:3], extra[3:4]
+            pl.when(section[0] > 0)(compute)
+
+            @pl.when(section[0] == 0)
+            def _():
+                out_ref[...] = jnp.zeros_like(out_ref)
+                for copy in copies:
+                    copy.start()
         else:
-            gate, slot = refs[0][0:1], refs[0][1:2]
-        gate = jnp.broadcast_to(gate, (CAP, tokens)).T[:, 0:1]
-        slots = lax.broadcasted_iota(jnp.int32, (CAP, tokens), 0).astype(jnp.float32)
-        onehot = jnp.where(slot == slots, 1.0, 0.0).T
-        onehot = jnp.concatenate([onehot] * 3, axis=1).astype(jnp.bfloat16)
-        for at in range(0, width, step):
-            columns = slice(at, at + step)
-            back = back_ref[:, columns]
-            high = back.astype(jnp.bfloat16).astype(jnp.float32)
-            middle = (back - high).astype(jnp.bfloat16).astype(jnp.float32)
-            parts = jnp.concatenate([high, middle, back - high - middle], axis=0)
-            moved = dot(onehot, parts.astype(jnp.bfloat16))
-            here = res_ref[:tokens, columns].astype(jnp.float32)
-            out_ref[:, columns] = (here + gate * moved).astype(jnp.bfloat16)
-
-    args = [res, back] + ([] if gates is None else [gates])
-    return local_kernel(kernel, "finish", [one], args, flops=50 * tokens * width)[0]
+            compute()
+        for copy in copies:
+            copy.wait()
+
+    args = [section.reshape(1), res, back] + ([] if gates is None else [gates])
+    return pl.pallas_call(
+        kernel,
+        out_shape=one,
+        in_specs=[pl.BlockSpec(memory_space=pltpu.SMEM)] + in_vmem(len(args) - 1),
+        out_specs=ANYWHERE,
+        scratch_shapes=[
+            pltpu.VMEM(one.shape, one.dtype),
+            pltpu.SemaphoreType.DMA((len(parts),)),
+        ],
+        compiler_params=compiler_params(),
+        cost_estimate=pl.CostEstimate(
+            flops=50 * tokens * width, bytes_accessed=5 * tokens * width, transcendentals=0
+        ),
+        name="finish",
+    )(*args)
 
 
 def local(
@@ -520,21 +569,27 @@
         extra = extra_rows(gates[0:1], gates[1:2])
         extra = jnp.pad(extra, ((0, 0), (0, width - extra.shape[1])))
         residual_before = passed_along(jnp.concatenate([residual, extra], axis=0), "section", 1)
-    gathered = grid.gather(capacity)
-    grads = grid.scatter(parts, own_rows, [gathered[1]])
+    grads = grid.scatter(parts, own_rows)
     halves = next(grads)
+    sums = []
+
+    def plane_sums(own):
+        if not sums:
+            sums.append(grads.send([own])[0])
+        return [sums[0][0]]
+
+    gathered = grid.gather(capacity, halves, plane_sums)
+    total_grad = grads.send([])
     computed = expert(
-        expert_in[0], expert_out[0], gathered, grid.heights(CAP), grid.types(),
-        [residual_before, *halves],
-    )
-    blocks = grads.send([computed[0]])
-    results = grid.scatter(computed, CAP, [blocks[0]])
-    total_grad = grads.send(next(results))
-    results.send([total_grad])
+        expert_in[0], expert_out[0], gathered, grid.heights(CAP), grid.types(), [total_grad]
+    )
+    results = grid.scatter(computed, CAP)
+    next(results)
+    results.send([residual_before])
     returned = results.send([])
     returned_before = passed_along(returned, "section", 1)
-    output = finish(residual, returned, gates)
-    arriving = finish(residual_before, returned_before)
+    output = finish(section, residual, returned, gates)
+    arriving = finish(section, residual_before, returned_before)
     first = to_decoder(total_grad).reshape(own_rows, 2, half)
     total_grad = jnp.concatenate([first, total_grad.reshape(own_rows, 2, half)], axis=2)
     total_grad = jnp.where(decoder, total_grad, 0.0)

time: 105 us -> 103 us (0.981); the launches traced: 103 us -> 102 us
  waiting for transfers between devices: 51.1 us -> 48.9 us
  starting transfers between devices: 36.4 us -> 38.2 us
    pallas_call x18 -> x17, Pallas kernels: 11.9 us -> 8.5 us  [local_kernel(): pl.pallas_call(body, out_shape=tuple(outs), in_specs=in_specs, out_specs=...]
    ppermute x2, waiting for transfers between devices: 3.21 us -> 0.01 us  [to_decoder(): lax.ppermute(block, 'section', [(i, i + apart) for i in range(apart)])]
    pallas_call x0 -> x2, Pallas kernels: none -> 3.02 us  [finish(): pl.pallas_call(kernel, out_shape=one, in_specs=[pl.BlockSpec(memory_space...]
    ppermute x2, waiting for transfers between devices: 4.29 us -> 6.67 us  [passed_along(): return lax.ppermute(block, axis, route)]
    ppermute x28, starting transfers between devices: 26.6 us -> 28.4 us  [shift(): return lax.ppermute(block, 'expert', route)]
    ppermute x28, waiting for transfers between devices: 42.4 us -> 41 us  [shift(): return lax.ppermute(block, 'expert', route)]
  transfers between devices with their start and end apart: 37 -> 37, of which waited for: 20 -> 17; matrix products, arithmetic and copies ran while one was open for 1% -> 1% of each run, Pallas kernels for 10% -> 8%
where the time goes in v4:
time: 103 us; the launch traced here: 102 us
  waiting for transfers between devices  48.9 us (47%)
  starting transfers between devices  38.2 us (37%)
  Pallas kernels  11.5 us (11%)
  local copies, waits for them, and re-layouts  1.5 us (1%)
    ppermute x28, waiting for transfers between devices, shift(): return lax.ppermute(block, 'expert', route)  41 us
    ppermute x28, starting transfers between devices, shift(): return lax.ppermute(block, 'expert', route)  28.4 us
    pallas_call x17, Pallas kernels, local_kernel(): pl.pallas_call(body, out_shape=tuple(outs), in_specs=in_specs, out_specs=...  8.5 us
    ppermute x2, waiting for transfers between devices, passed_along(): return lax.ppermute(block, axis, route)  6.67 us
    ppermute x5, starting transfers between devices, swapped(): lax.ppermute(block, 'section', [(i, (i + sections // 2) % sections) for i...  4.61 us
    pallas_call x2, Pallas kernels, finish(): pl.pallas_call(kernel, out_shape=one, in_specs=[pl.BlockSpec(memory_space...  3.02 us
    ppermute x2, starting transfers between devices, passed_along(): return lax.ppermute(block, axis, route)  2.58 us
    ppermute x2, starting transfers between devices, to_decoder(): lax.ppermute(block, 'section', [(i, i + apart) for i in range(apart)])  2.57 us
  transfers between devices with their start and end apart: 37, of which 17 were waited for; matrix products, arithmetic and copies ran while one was open for 1% of the time, Pallas kernels for 8%

profile of v4, /device:TPU:1, one launch (start us, length us, event | category | flops | bytes accessed | tf_op | source)
XLA Modules:
  0.0 102.0 jit_solution(18118715192135418457)
XLA Ops:
  0.7 1.1 %slice_bitcast_fusion = (bf16[1,8,2,2560]{3,2,1,0:T(2,128)(2,1)S(1)}, bf16[1,8,2,2560]{3,2,1,0:T(2,128)(2,1)S(1)}) fusion(bf16[1,8,2,5120]{3,2,1,0:T(2,128)(2,1)} %param.10), kind=kLoop, calls=%fused_computation.1 | loop fusion | bytes 327680
  1.8 0.1 collective-permute-start
  2.0 1.2 %collective-permute-done = bf16[8,5120]{1,0:T(8,128)(2,1)S(1)} collective-permute-done((bf16[8,5120]{1,0:T(8,128)(2,1)S(1)}, bf16[8,5120]{1,0:T(8,128)(2,1)S(1)}, u32[]{:S(2)}, u32[]{:S(2)}) %collective-permute-start) | collective-permute-done | bytes 81952 | tf_op jit(solution)/shard_map/ppermute | solution.py:22
  3.2 4.5 %collective-permute-start.3 = (bf16[8,5120]{1,0:T(8,128)(2,1)S(1)}, bf16[8,5120]{1,0:T(8,128)(2,1)S(1)}, u32[]{:S(2)}, u32[]{:S(2)}) collective-permute-start(bf16[8,5120]{1,0:T(8,128)(2,1)S(1)} %broadcast_select_fusion.refs_0_), channel_id=1, source_target_pairs={{0,12},{1,13},{2,14},{3,15},{4,8},{5,9},{6,10},{7,11},{8,4},{9,5},... | collective-permute-start | bytes 245768 | tf_op jit(solution)/shard_map/ppermute | solution.py:50
  7.7 0.4 collective-permute-start.1
  8.1 2.2 %collective-permute-done.3.refs_3_ = bf16[8,5120]{1,0:T(8,128)(2,1)S(1)} collective-permute-done((bf16[8,5120]{1,0:T(8,128)(2,1)S(1)}, bf16[8,5120]{1,0:T(8,128)(2,1)S(1)}, u32[]{:S(2)}, u32[]{:S(2)}) %collective-permute-start.3) | collective-permute-done | bytes 81952 | tf_op jit(solution)/shard_map/ppermute | solution.py:50
  10.3 4.1 %collective-permute-done.2.refs_2_ = bf16[8,5120]{1,0:T(8,128)(2,1)S(1)} collective-permute-done((bf16[8,5120]{1,0:T(8,128)(2,1)S(1)}, bf16[8,5120]{1,0:T(8,128)(2,1)S(1)}, u32[]{:S(2)}, u32[]{:S(2)}) %collective-permute-start.2) | collective-permute-done | bytes 81952 | tf_op jit(solution)/shard_map/ppermute | solution.py:50
  14.4 1.3 %collective-permute-start.7 = (bf16[32,5120]{1,0:T(8,128)(2,1)S(1)}, bf16[32,5120]{1,0:T(8,128)(2,1)S(1)}, u32[]{:S(2)}, u32[]{:S(2)}) collective-permute-start(bf16[32,5120]{1,0:T(8,128)(2,1)S(1)} %join.2.refs_4_), channel_id=1, source_target_pairs={{0,2},{1,3},{2,0},{3,1},{4,6},{5,7},{6,4},{7,5},{8,10},{9,11},{10,... | collective-permute-start | bytes 983048 | tf_op jit(solution)/shard_map/ppermute | solution.py:50
  15.7 1.2 %collective-permute-start.6 = (bf16[32,5120]{1,0:T(8,128)(2,1)S(1)}, bf16[32,5120]{1,0:T(8,128)(2,1)S(1)}, u32[]{:S(2)}, u32[]{:S(2)}) collective-permute-start(bf16[32,5120]{1,0:T(8,128)(2,1)S(1)} %join.2.refs_4_), channel_id=1, source_target_pairs={{0,1},{1,0},{2,3},{3,2},{4,5},{5,4},{6,7},{7,6},{8,9},{9,8},{10,11... | collective-permute-start | bytes 983048 | tf_op jit(solution)/shard_map/ppermute | solution.py:50
  16.9 0.9 queries.1
  17.8 1.8 %collective-permute-start.4 = (bf16[128,1280]{1,0:T(8,128)(2,1)S(1)}, bf16[128,1280]{1,0:T(8,128)(2,1)S(1)}, u32[]{:S(2)}, u32[]{:S(2)}) collective-permute-start(bf16[128,1280]{1,0:T(8,128)(2,1)S(1)} %get-tuple-element.37), channel_id=1, source_target_pairs={{0,16},{16,0},{1,17},{17,1},{2,18},{18,2},{3,19},{19,3},{4,20},{20... | collective-permute-start | bytes 983048 | tf_op jit(solution)/shard_map/ppermute | solution.py:22
  19.6 0.1 collective-permute-start.5
  19.7 0.1 cut.1
  19.8 0.5 collective-permute-start.10
  20.3 2.2 %collective-permute-done.7.refs_6_ = bf16[32,5120]{1,0:T(8,128)(2,1)S(1)} collective-permute-done((bf16[32,5120]{1,0:T(8,128)(2,1)S(1)}, bf16[32,5120]{1,0:T(8,128)(2,1)S(1)}, u32[]{:S(2)}, u32[]{:S(2)}) %collective-permute-start.7) | collective-permute-done | bytes 327712 | tf_op jit(solution)/shard_map/ppermute | solution.py:50
  22.5 2.1 %collective-permute-start.11 = (bf16[128,1280]{1,0:T(8,128)(2,1)S(1)}, bf16[128,1280]{1,0:T(8,128)(2,1)S(1)}, u32[]{:S(2)}, u32[]{:S(2)}) collective-permute-start(bf16[128,1280]{1,0:T(8,128)(2,1)S(1)} %get-tuple-element.42), channel_id=1, source_target_pairs={{0,16},{16,0},{1,17},{17,1},{2,18},{18,2},{3,19},{19,3},{4,20},{20... | collective-permute-start | bytes 983048 | tf_op jit(solution)/shard_map/ppermute | solution.py:22
  24.6 1.3 %collective-permute-start.8 = (bf16[16,5120]{1,0:T(8,128)(2,1)S(1)}, bf16[16,5120]{1,0:T(8,128)(2,1)S(1)}, u32[]{:S(2)}, u32[]{:S(2)}) collective-permute-start(bf16[16,5120]{1,0:T(8,128)(2,1)S(1)} %slice.16), channel_id=1, source_target_pairs={{0,1},{1,0},{2,3},{3,2},{4,5},{5,4},{6,7},{7,6},{8,9},{9,8},{10,11... | collective-permute-start | bytes 491528 | tf_op jit(solution)/shard_map/ppermute | solution.py:50
  25.9 1.3 %collective-permute-start.9 = (bf16[16,5120]{1,0:T(8,128)(2,1)S(1)}, bf16[16,5120]{1,0:T(8,128)(2,1)S(1)}, u32[]{:S(2)}, u32[]{:S(2)}) collective-permute-start(bf16[16,5120]{1,0:T(8,128)(2,1)S(1)} %slice.17), channel_id=1, source_target_pairs={{0,2},{1,3},{2,0},{3,1},{4,6},{5,7},{6,4},{7,5},{8,10},{9,11},{10,... | collective-permute-start | bytes 491528 | tf_op jit(solution)/shard_map/ppermute | solution.py:50
  27.2 2.0 %collective-permute-done.8.refs_7_ = bf16[16,5120]{1,0:T(8,128)(2,1)S(1)} collective-permute-done((bf16[16,5120]{1,0:T(8,128)(2,1)S(1)}, bf16[16,5120]{1,0:T(8,128)(2,1)S(1)}, u32[]{:S(2)}, u32[]{:S(2)}) %collective-permute-start.8) | collective-permute-done | bytes 163872 | tf_op jit(solution)/shard_map/ppermute | solution.py:50
  29.2 1.2 %collective-permute-done.9.refs_8_ = bf16[16,5120]{1,0:T(8,128)(2,1)S(1)} collective-permute-done((bf16[16,5120]{1,0:T(8,128)(2,1)S(1)}, bf16[16,5120]{1,0:T(8,128)(2,1)S(1)}, u32[]{:S(2)}, u32[]{:S(2)}) %collective-permute-start.9) | collective-permute-done | bytes 163872 | tf_op jit(solution)/shard_map/ppermute | solution.py:50
  30.4 2.0 %attend.1 = (bf16[128,2560]{1,0:T(8,128)(2,1)S(1)}, f32[20,128,128]{2,1,0:T(8,128)S(1)}, bf16[128,2560]{1,0:T(8,128)(2,1)S(1)}) custom-call(s32[1]{0:T(128)} %bitcast.refs_0_.section, bf16[128,1280]{1,0:T(8,128)(2,1)S(1)} %collective-permute-done.4.refs_1_, bf16[128,1280]{1,0:T(8,128)(2,1)S(1)} %collective-permute-done.5.refs_2_, ...), custom_call_target="tpu_custom_call" | custom-call | flops 167772160 | bytes 5242884 | tf_op jit(solution)/shard_map/attend/pallas_call | solution.py:142
  32.5 1.3 %collective-permute-start.12 = (bf16[128,2560]{1,0:T(8,128)(2,1)S(1)}, bf16[128,2560]{1,0:T(8,128)(2,1)S(1)}, u32[]{:S(2)}, u32[]{:S(2)}) collective-permute-start(bf16[128,2560]{1,0:T(8,128)(2,1)S(1)} %get-tuple-element.43.refs_3_), channel_id=1, source_target_pairs={{0,16},{1,17},{2,18},{3,19},{4,20},{5,21},{6,22},{7,23},{8,24},{9,... | collective-permute-start | bytes 1966088 | tf_op jit(solution)/shard_map/ppermute | solution.py:27
  33.8 1.3 %collective-permute-start.31 = (bf16[144,5120]{1,0:T(8,128)(2,1)S(1)}, bf16[144,5120]{1,0:T(8,128)(2,1)S(1)}, u32[]{:S(2)}, u32[]{:S(2)}) collective-permute-start(bf16[144,5120]{1,0:T(8,128)(2,1)S(1)} %get-tuple-element.36.refs_1_), channel_id=1, source_target_pairs={{0,16},{1,17},{2,18},{3,19},{4,20},{5,21},{6,22},{7,23},{8,24},{9,... | collective-permute-start | bytes 4423688 | tf_op jit(solution)/shard_map/ppermute | solution.py:17
  35.1 2.0 %gradient.1 = (f32[32,5120]{1,0:T(8,128)S(1)}, f32[32,5120]{1,0:T(8,128)S(1)}, f32[32,5120]{1,0:T(8,128)S(1)}, bf16[16,5120]{1,0:T(8,128)(2,1)S(1)}, bf16[16,5120]{1,0:T(8,128)(2,1)S(1)}) custom-call(s32[1]{0:T(128)} %bitcast.refs_0_.section, bf16[128,2560]{1,0:T(8,128)(2,1)S(1)} %get-tuple-element.44.q_ref, ...), custom_call_target="tpu_custom_call" | custom-call | flops 419430400 | bytes 6881284 | tf_op jit(solution)/shard_map/gradient/pallas_call | solution.py:142
  37.1 2.2 %collective-permute-start.17 = (bf16[16,5120]{1,0:T(8,128)(2,1)S(1)}, bf16[16,5120]{1,0:T(8,128)(2,1)S(1)}, u32[]{:S(2)}, u32[]{:S(2)}) collective-permute-start(bf16[16,5120]{1,0:T(8,128)(2,1)S(1)} %get-tuple-element.53), channel_id=1, source_target_pairs={{2,0},{3,1},{0,2},{1,3},{6,4},{7,5},{4,6},{5,7},{10,8},{11,9},{8,1... | collective-permute-start | bytes 491528 | tf_op jit(solution)/shard_map/ppermute | solution.py:50
  39.3 0.3 collective-permute-start.16
  39.6 0.7 settle.1
  40.2 2.4 %collective-permute-start.15 = (bf16[8,5120]{1,0:T(8,128)(2,1)S(1)}, bf16[8,5120]{1,0:T(8,128)(2,1)S(1)}, u32[]{:S(2)}, u32[]{:S(2)}) collective-permute-start(bf16[8,5120]{1,0:T(8,128)(2,1)S(1)} %get-tuple-element.49.refs_0_), channel_id=1, source_target_pairs={{0,12},{1,13},{2,14},{3,15},{4,8},{5,9},{6,10},{7,11},{8,4},{9,5},... | collective-permute-start | bytes 245768 | tf_op jit(solution)/shard_map/ppermute | solution.py:50
  42.6 1.2 %collective-permute-start.13 = (bf16[8,5120]{1,0:T(8,128)(2,1)S(1)}, bf16[8,5120]{1,0:T(8,128)(2,1)S(1)}, u32[]{:S(2)}, u32[]{:S(2)}) collective-permute-start(bf16[8,5120]{1,0:T(8,128)(2,1)S(1)} %get-tuple-element.49.refs_0_), channel_id=1, source_target_pairs={{0,4},{1,5},{2,6},{3,7},{4,0},{5,1},{6,2},{7,3},{8,12},{9,13},{10,... | collective-permute-start | bytes 245768 | tf_op jit(solution)/shard_map/ppermute | solution.py:50
  43.9 1.3 %collective-permute-start.21 = (bf16[32,5120]{1,0:T(8,128)(2,1)S(1)}, bf16[32,5120]{1,0:T(8,128)(2,1)S(1)}, u32[]{:S(2)}, u32[]{:S(2)}) collective-permute-start(bf16[32,5120]{1,0:T(8,128)(2,1)S(1)} %add_half.5.refs_5_), channel_id=1, source_target_pairs={{1,0},{0,1},{3,2},{2,3},{5,4},{4,5},{7,6},{6,7},{9,8},{8,9},{11,10... | collective-permute-start | bytes 983048 | tf_op jit(solution)/shard_map/ppermute | solution.py:50
  45.2 0.2 collective-permute-done.15.refs_3_
  45.5 4.6 %collective-permute-done.14.refs_2_ = bf16[8,5120]{1,0:T(8,128)(2,1)S(1)} collective-permute-done((bf16[8,5120]{1,0:T(8,128)(2,1)S(1)}, bf16[8,5120]{1,0:T(8,128)(2,1)S(1)}, u32[]{:S(2)}, u32[]{:S(2)}) %collective-permute-start.14) | collective-permute-done | bytes 81952 | tf_op jit(solution)/shard_map/ppermute | solution.py:50
  50.1 0.1 collective-permute-start.19
  50.2 1.3 %collective-permute-start.18 = (bf16[32,5120]{1,0:T(8,128)(2,1)S(1)}, bf16[32,5120]{1,0:T(8,128)(2,1)S(1)}, u32[]{:S(2)}, u32[]{:S(2)}) collective-permute-start(bf16[32,5120]{1,0:T(8,128)(2,1)S(1)} %join.3.refs_3_.refs_2_), channel_id=1, source_target_pairs={{0,1},{1,0},{2,3},{3,2},{4,5},{5,4},{6,7},{7,6},{8,9},{9,8},{10,11... | collective-permute-start | bytes 983048 | tf_op jit(solution)/shard_map/ppermute | solution.py:50
  51.5 0.1 collective-permute-done.20.refs_1_
  51.6 0.1 add_blocks.2
  51.7 0.2 collective-permute-start.24
  52.0 7.9 %collective-permute-done.19.refs_0_.refs_4_ = bf16[32,5120]{1,0:T(8,128)(2,1)S(1)} collective-permute-done((bf16[32,5120]{1,0:T(8,128)(2,1)S(1)}, bf16[32,5120]{1,0:T(8,128)(2,1)S(1)}, u32[]{:S(2)}, u32[]{:S(2)}) %collective-permute-start.19) | collective-permute-done | bytes 327712 | tf_op jit(solution)/shard_map/ppermute | solution.py:50
  59.9 1.3 %collective-permute-start.22 = (bf16[16,5120]{1,0:T(8,128)(2,1)S(1)}, bf16[16,5120]{1,0:T(8,128)(2,1)S(1)}, u32[]{:S(2)}, u32[]{:S(2)}) collective-permute-start(bf16[16,5120]{1,0:T(8,128)(2,1)S(1)} %get-tuple-element.55), channel_id=1, source_target_pairs={{0,1},{1,0},{2,3},{3,2},{4,5},{5,4},{6,7},{7,6},{8,9},{9,8},{10,11... | collective-permute-start | bytes 491528 | tf_op jit(solution)/shard_map/ppermute | solution.py:50
  61.2 0.1 collective-permute-start.23
  61.3 2.2 %collective-permute-start.26 = (bf16[8,5120]{1,0:T(8,128)(2,1)S(1)}, bf16[8,5120]{1,0:T(8,128)(2,1)S(1)}, u32[]{:S(2)}, u32[]{:S(2)}) collective-permute-start(bf16[8,5120]{1,0:T(8,128)(2,1)S(1)} %get-tuple-element.59), channel_id=1, source_target_pairs={{12,0},{13,1},{14,2},{15,3},{8,4},{9,5},{10,6},{11,7},{4,8},{5,9},... | collective-permute-start | bytes 245768 | tf_op jit(solution)/shard_map/ppermute | solution.py:50
  63.4 3.5 %collective-permute-done.25.refs_1_ = bf16[8,5120]{1,0:T(8,128)(2,1)S(1)} collective-permute-done((bf16[8,5120]{1,0:T(8,128)(2,1)S(1)}, bf16[8,5120]{1,0:T(8,128)(2,1)S(1)}, u32[]{:S(2)}, u32[]{:S(2)}) %collective-permute-start.25) | collective-permute-done | bytes 81952 | tf_op jit(solution)/shard_map/ppermute | solution.py:50
  67.0 2.3 %expert.1 = (f32[32,5120]{1,0:T(8,128)S(1)}, f32[32,5120]{1,0:T(8,128)S(1)}, f32[32,5120]{1,0:T(8,128)S(1)}, bf16[16,5120]{1,0:T(8,128)(2,1)S(1)}, bf16[16,5120]{1,0:T(8,128)(2,1)S(1)}) custom-call(bf16[5120,640]{1,0:T(8,128)(2,1)S(1)} %bitcast.19, bf16[640,5120]{1,0:T(8,128)(2,1)S(1)} %bitcast.22, bf16[32,5120]{1,0:T(8,128)(2,1)S(1)} %join.3.refs_3_.refs_2_, ...), custom_call_target="tpu_custom_call" | custom-call | flops 1677721600 | bytes 16711680 | tf_op jit(solution)/shard_map/expert/pallas_call | solution.py:142
  69.4 1.5 %collective-permute-start.29 = (bf16[16,5120]{1,0:T(8,128)(2,1)S(1)}, bf16[16,5120]{1,0:T(8,128)(2,1)S(1)}, u32[]{:S(2)}, u32[]{:S(2)}) collective-permute-start(bf16[16,5120]{1,0:T(8,128)(2,1)S(1)} %get-tuple-element.64), channel_id=1, source_target_pairs={{2,0},{3,1},{0,2},{1,3},{6,4},{7,5},{4,6},{5,7},{10,8},{11,9},{8,1... | collective-permute-start | bytes 491528 | tf_op jit(solution)/shard_map/ppermute | solution.py:50
  70.9 0.1 collective-permute-start.27
  71.0 2.6 %collective-permute-done.29.refs_0_ = bf16[16,5120]{1,0:T(8,128)(2,1)S(1)} collective-permute-done((bf16[16,5120]{1,0:T(8,128)(2,1)S(1)}, bf16[16,5120]{1,0:T(8,128)(2,1)S(1)}, u32[]{:S(2)}, u32[]{:S(2)}) %collective-permute-start.29) | collective-permute-done | bytes 163872 | tf_op jit(solution)/shard_map/ppermute | solution.py:50
  73.7 0.6 collective-permute-start.30
  74.2 0.9 collective-permute-done.27.refs_0_
  75.1 0.3 collective-permute-start.28
  75.4 1.3 %collective-permute-start.36 = (f32[8,5120]{1,0:T(8,128)S(1)}, f32[8,5120]{1,0:T(8,128)S(1)}, u32[]{:S(2)}, u32[]{:S(2)}) collective-permute-start(f32[8,5120]{1,0:T(8,128)S(1)} %add_last.2.refs_7_), channel_id=1, source_target_pairs={{0,16},{1,17},{2,18},{3,19},{4,20},{5,21},{6,22},{7,23},{8,24},{9,... | collective-permute-start | bytes 491528 | tf_op jit(solution)/shard_map/ppermute | solution.py:27
  76.7 4.1 %collective-permute-done.30.refs_2_ = bf16[32,5120]{1,0:T(8,128)(2,1)S(1)} collective-permute-done((bf16[32,5120]{1,0:T(8,128)(2,1)S(1)}, bf16[32,5120]{1,0:T(8,128)(2,1)S(1)}, u32[]{:S(2)}, u32[]{:S(2)}) %collective-permute-start.30) | collective-permute-done | bytes 327712 | tf_op jit(solution)/shard_map/ppermute | solution.py:50
  80.8 2.1 %collective-permute-done.28.refs_1_ = bf16[32,5120]{1,0:T(8,128)(2,1)S(1)} collective-permute-done((bf16[32,5120]{1,0:T(8,128)(2,1)S(1)}, bf16[32,5120]{1,0:T(8,128)(2,1)S(1)}, u32[]{:S(2)}, u32[]{:S(2)}) %collective-permute-start.28) | collective-permute-done | bytes 327712 | tf_op jit(solution)/shard_map/ppermute | solution.py:50
  82.9 0.1 add_blocks.3
  83.0 1.2 %collective-permute-start.32 = (bf16[8,5120]{1,0:T(8,128)(2,1)S(1)}, bf16[8,5120]{1,0:T(8,128)(2,1)S(1)}, u32[]{:S(2)}, u32[]{:S(2)}) collective-permute-start(bf16[8,5120]{1,0:T(8,128)(2,1)S(1)} %get-tuple-element.66), channel_id=1, source_target_pairs={{4,0},{5,1},{6,2},{7,3},{0,4},{1,5},{2,6},{3,7},{12,8},{13,9},{14,... | collective-permute-start | bytes 245768 | tf_op jit(solution)/shard_map/ppermute | solution.py:50
  84.2 0.6 collective-permute-start.33
  84.8 1.8 %collective-permute-start.34 = (bf16[8,5120]{1,0:T(8,128)(2,1)S(1)}, bf16[8,5120]{1,0:T(8,128)(2,1)S(1)}, u32[]{:S(2)}, u32[]{:S(2)}) collective-permute-start(bf16[8,5120]{1,0:T(8,128)(2,1)S(1)} %get-tuple-element.68), channel_id=1, source_target_pairs={{12,0},{13,1},{14,2},{15,3},{8,4},{9,5},{10,6},{11,7},{4,8},{5,9},... | collective-permute-start | bytes 245768 | tf_op jit(solution)/shard_map/ppermute | solution.py:50
  86.6 0.1 copy.13
  86.7 0.1 copy.12
  86.9 3.2 %collective-permute-done.33.refs_1_ = bf16[8,5120]{1,0:T(8,128)(2,1)S(1)} collective-permute-done((bf16[8,5120]{1,0:T(8,128)(2,1)S(1)}, bf16[8,5120]{1,0:T(8,128)(2,1)S(1)}, u32[]{:S(2)}, u32[]{:S(2)}) %collective-permute-start.33) | collective-permute-done | bytes 81952 | tf_op jit(solution)/shard_map/ppermute | solution.py:50
  90.2 1.3 %collective-permute-start.35 = (f32[8,5120]{1,0:T(8,128)S(1)}, f32[8,5120]{1,0:T(8,128)S(1)}, u32[]{:S(2)}, u32[]{:S(2)}) collective-permute-start(f32[8,5120]{1,0:T(8,128)S(1)} %add_last.3.back_ref), channel_id=1, source_target_pairs={{0,16},{1,17},{2,18},{3,19},{4,20},{5,21},{6,22},{7,23},{8,24},{9,... | collective-permute-start | bytes 491528 | tf_op jit(solution)/shard_map/ppermute | solution.py:17
  91.5 0.9 maximum_select_fusion
  92.3 1.5 %finish.2 = bf16[128,5120]{1,0:T(8,128)(2,1)} custom-call(s32[1]{0:T(128)} %bitcast.refs_0_.section, bf16[128,5120]{1,0:T(8,128)(2,1)S(1)} %get-tuple-element.48.res_ref, f32[8,5120]{1,0:T(8,128)S(1)} %add_last.3.back_ref, f32[2,128]{1,0:T(2,128)S(1)} %get-tuple-element.40.refs_1_.refs_5_.refs_0_), custom_call_target="tpu_custom_call" | custom-call | flops 32768000 | bytes 3276800 | tf_op jit(solution)/shard_map/finish/pallas_call | solution.py:509
  93.9 6.7 %collective-permute-done.35.back_ref = f32[8,5120]{1,0:T(8,128)S(1)} collective-permute-done((f32[8,5120]{1,0:T(8,128)S(1)}, f32[8,5120]{1,0:T(8,128)S(1)}, u32[]{:S(2)}, u32[]{:S(2)}) %collective-permute-start.35) | collective-permute-done | bytes 163872 | tf_op jit(solution)/shard_map/ppermute | solution.py:17
  100.5 1.5 %finish.3 = bf16[128,5120]{1,0:T(8,128)(2,1)} custom-call(s32[1]{0:T(128)} %bitcast.refs_0_.section, bf16[144,5120]{1,0:T(8,128)(2,1)S(1)} %collective-permute-done.31.refs_3_.res_ref, f32[8,5120]{1,0:T(8,128)S(1)} %collective-permute-done.35.back_ref), custom_call_target="tpu_custom_call" | custom-call | flops 32768000 | bytes 3276800 | tf_op jit(solution)/shard_map/finish/pallas_call | solution.py:509
  (60 shorter events, 0.6 us)
Async XLA Ops:
  0.6 16.3 %copy-start.4 = (f32[1,128]{1,0:T(1,128)S(1)}, f32[1,128]{1,0:T(1,128)}, u32[]{:S(2)}) copy-start(f32[1,128]{1,0:T(1,128)} %refs_2_.1) | copy-start | bytes 1540
  0.6 16.3 %copy-start.5 = (s32[1,128]{1,0:T(1,128)S(1)}, s32[1,128]{1,0:T(1,128)}, u32[]{:S(2)}) copy-start(s32[1,128]{1,0:T(1,128)} %refs_3_.1) | copy-start | bytes 1540
  0.7 16.3 %copy-start.3 = (f32[1,5120]{1,0:T(1,128)S(1)}, f32[1,5120]{1,0:T(1,128)}, u32[]{:S(2)}) copy-start(f32[1,5120]{1,0:T(1,128)} %refs_1_.1) | copy-start | bytes 61444
  0.7 16.3 %copy-start = (bf16[1,128,5120]{2,1,0:T(8,128)(2,1)S(1)}, bf16[1,128,5120]{2,1,0:T(8,128)(2,1)}, u32[]{:S(2)}) copy-start(bf16[1,128,5120]{2,1,0:T(8,128)(2,1)} %param.9) | copy-start | bytes 3932164
  1.8 1.3 %collective-permute-start = (bf16[8,5120]{1,0:T(8,128)(2,1)S(1)}, bf16[8,5120]{1,0:T(8,128)(2,1)S(1)}, u32[]{:S(2)}, u32[]{:S(2)}) collective-permute-start(bf16[8,5120]{1,0:T(8,128)(2,1)S(1)} %bitcast.30), channel_id=1, source_target_pairs={{0,16},{16,0},{1,17},{17,1},{2,18},{18,2},{3,19},{19,3},{4,20},{20... | collective-permute-start | bytes 245768 | tf_op jit(solution)/shard_map/ppermute | solution.py:22
  2.0 17.7 %copy-start.1 = (bf16[1,128,5120]{2,1,0:T(8,128)(2,1)S(1)}, bf16[1,128,5120]{2,1,0:T(8,128)(2,1)}, u32[]{:S(2)}) copy-start(bf16[1,128,5120]{2,1,0:T(8,128)(2,1)} %param.11) | copy-start | bytes 3932164
  3.2 7.1 %collective-permute-start.3 = (bf16[8,5120]{1,0:T(8,128)(2,1)S(1)}, bf16[8,5120]{1,0:T(8,128)(2,1)S(1)}, u32[]{:S(2)}, u32[]{:S(2)}) collective-permute-start(bf16[8,5120]{1,0:T(8,128)(2,1)S(1)} %broadcast_select_fusion.refs_0_), channel_id=1, source_target_pairs={{0,12},{1,13},{2,14},{3,15},{4,8},{5,9},{6,10},{7,11},{8,4},{9,5},... | collective-permute-start | bytes 245768 | tf_op jit(solution)/shard_map/ppermute | solution.py:50
  7.7 6.6 %collective-permute-start.2 = (bf16[8,5120]{1,0:T(8,128)(2,1)S(1)}, bf16[8,5120]{1,0:T(8,128)(2,1)S(1)}, u32[]{:S(2)}, u32[]{:S(2)}) collective-permute-start(bf16[8,5120]{1,0:T(8,128)(2,1)S(1)} %broadcast_select_fusion.refs_0_), channel_id=1, source_target_pairs={{0,8},{1,9},{2,10},{3,11},{4,12},{5,13},{6,14},{7,15},{8,0},{9,1},... | collective-permute-start | bytes 245768 | tf_op jit(solution)/shard_map/ppermute | solution.py:50
  7.7 6.6 %collective-permute-start.1 = (bf16[8,5120]{1,0:T(8,128)(2,1)S(1)}, bf16[8,5120]{1,0:T(8,128)(2,1)S(1)}, u32[]{:S(2)}, u32[]{:S(2)}) collective-permute-start(bf16[8,5120]{1,0:T(8,128)(2,1)S(1)} %broadcast_select_fusion.refs_0_), channel_id=1, source_target_pairs={{0,4},{1,5},{2,6},{3,7},{4,0},{5,1},{6,2},{7,3},{8,12},{9,13},{10,... | collective-permute-start | bytes 245768 | tf_op jit(solution)/shard_map/ppermute | solution.py:50
  14.4 8.1 %collective-permute-start.7 = (bf16[32,5120]{1,0:T(8,128)(2,1)S(1)}, bf16[32,5120]{1,0:T(8,128)(2,1)S(1)}, u32[]{:S(2)}, u32[]{:S(2)}) collective-permute-start(bf16[32,5120]{1,0:T(8,128)(2,1)S(1)} %join.2.refs_4_), channel_id=1, source_target_pairs={{0,2},{1,3},{2,0},{3,1},{4,6},{5,7},{6,4},{7,5},{8,10},{9,11},{10,... | collective-permute-start | bytes 983048 | tf_op jit(solution)/shard_map/ppermute | solution.py:50
  15.7 8.9 %collective-permute-start.6 = (bf16[32,5120]{1,0:T(8,128)(2,1)S(1)}, bf16[32,5120]{1,0:T(8,128)(2,1)S(1)}, u32[]{:S(2)}, u32[]{:S(2)}) collective-permute-start(bf16[32,5120]{1,0:T(8,128)(2,1)S(1)} %join.2.refs_4_), channel_id=1, source_target_pairs={{0,1},{1,0},{2,3},{3,2},{4,5},{5,4},{6,7},{7,6},{8,9},{9,8},{10,11... | collective-permute-start | bytes 983048 | tf_op jit(solution)/shard_map/ppermute | solution.py:50
  17.8 8.1 %collective-permute-start.4 = (bf16[128,1280]{1,0:T(8,128)(2,1)S(1)}, bf16[128,1280]{1,0:T(8,128)(2,1)S(1)}, u32[]{:S(2)}, u32[]{:S(2)}) collective-permute-start(bf16[128,1280]{1,0:T(8,128)(2,1)S(1)} %get-tuple-element.37), channel_id=1, source_target_pairs={{0,16},{16,0},{1,17},{17,1},{2,18},{18,2},{3,19},{19,3},{4,20},{20... | collective-permute-start | bytes 983048 | tf_op jit(solution)/shard_map/ppermute | solution.py:22
  19.6 7.6 %collective-permute-start.5 = (bf16[128,1280]{1,0:T(8,128)(2,1)S(1)}, bf16[128,1280]{1,0:T(8,128)(2,1)S(1)}, u32[]{:S(2)}, u32[]{:S(2)}) collective-permute-start(bf16[128,1280]{1,0:T(8,128)(2,1)S(1)} %get-tuple-element.38), channel_id=1, source_target_pairs={{0,16},{16,0},{1,17},{17,1},{2,18},{18,2},{3,19},{19,3},{4,20},{20... | collective-permute-start | bytes 983048 | tf_op jit(solution)/shard_map/ppermute | solution.py:22
  19.8 7.4 %collective-permute-start.10 = (bf16[128,1280]{1,0:T(8,128)(2,1)S(1)}, bf16[128,1280]{1,0:T(8,128)(2,1)S(1)}, u32[]{:S(2)}, u32[]{:S(2)}) collective-permute-start(bf16[128,1280]{1,0:T(8,128)(2,1)S(1)} %get-tuple-element.41), channel_id=1, source_target_pairs={{0,16},{16,0},{1,17},{17,1},{2,18},{18,2},{3,19},{19,3},{4,20},{20... | collective-permute-start | bytes 983048 | tf_op jit(solution)/shard_map/ppermute | solution.py:22
  22.5 4.8 %collective-permute-start.11 = (bf16[128,1280]{1,0:T(8,128)(2,1)S(1)}, bf16[128,1280]{1,0:T(8,128)(2,1)S(1)}, u32[]{:S(2)}, u32[]{:S(2)}) collective-permute-start(bf16[128,1280]{1,0:T(8,128)(2,1)S(1)} %get-tuple-element.42), channel_id=1, source_target_pairs={{0,16},{16,0},{1,17},{17,1},{2,18},{18,2},{3,19},{19,3},{4,20},{20... | collective-permute-start | bytes 983048 | tf_op jit(solution)/shard_map/ppermute | solution.py:22
  24.6 42.4 %slice-start.2 = ((s8[6553600]{0:T(1024)(128)(4,1)}), s8[2359296]{0:T(1024)(128)(4,1)S(1)}, s32[]{:S(2)}) async-start(s8[6553600]{0:T(1024)(128)(4,1)} %bitcast.20), calls=%async_computation.2 | async-start | bytes 4718592
  24.6 4.6 %collective-permute-start.8 = (bf16[16,5120]{1,0:T(8,128)(2,1)S(1)}, bf16[16,5120]{1,0:T(8,128)(2,1)S(1)}, u32[]{:S(2)}, u32[]{:S(2)}) collective-permute-start(bf16[16,5120]{1,0:T(8,128)(2,1)S(1)} %slice.16), channel_id=1, source_target_pairs={{0,1},{1,0},{2,3},{3,2},{4,5},{5,4},{6,7},{7,6},{8,9},{9,8},{10,11... | collective-permute-start | bytes 491528 | tf_op jit(solution)/shard_map/ppermute | solution.py:50
  25.9 4.5 %collective-permute-start.9 = (bf16[16,5120]{1,0:T(8,128)(2,1)S(1)}, bf16[16,5120]{1,0:T(8,128)(2,1)S(1)}, u32[]{:S(2)}, u32[]{:S(2)}) collective-permute-start(bf16[16,5120]{1,0:T(8,128)(2,1)S(1)} %slice.17), channel_id=1, source_target_pairs={{0,2},{1,3},{2,0},{3,1},{4,6},{5,7},{6,4},{7,5},{8,10},{9,11},{10,... | collective-permute-start | bytes 491528 | tf_op jit(solution)/shard_map/ppermute | solution.py:50
  32.5 7.1 %collective-permute-start.12 = (bf16[128,2560]{1,0:T(8,128)(2,1)S(1)}, bf16[128,2560]{1,0:T(8,128)(2,1)S(1)}, u32[]{:S(2)}, u32[]{:S(2)}) collective-permute-start(bf16[128,2560]{1,0:T(8,128)(2,1)S(1)} %get-tuple-element.43.refs_3_), channel_id=1, source_target_pairs={{0,16},{1,17},{2,18},{3,19},{4,20},{5,21},{6,22},{7,23},{8,24},{9,... | collective-permute-start | bytes 1966088 | tf_op jit(solution)/shard_map/ppermute | solution.py:27
  33.8 42.9 %collective-permute-start.31 = (bf16[144,5120]{1,0:T(8,128)(2,1)S(1)}, bf16[144,5120]{1,0:T(8,128)(2,1)S(1)}, u32[]{:S(2)}, u32[]{:S(2)}) collective-permute-start(bf16[144,5120]{1,0:T(8,128)(2,1)S(1)} %get-tuple-element.36.refs_1_), channel_id=1, source_target_pairs={{0,16},{1,17},{2,18},{3,19},{4,20},{5,21},{6,22},{7,23},{8,24},{9,... | collective-permute-start | bytes 4423688 | tf_op jit(solution)/shard_map/ppermute | solution.py:17
  35.1 4.5 %copy-start.2 = (f32[1,5120]{1,0:T(1,128)S(1)}, f32[1,5120]{1,0:T(1,128)}, u32[]{:S(2)}) copy-start(f32[1,5120]{1,0:T(1,128)} %refs_4_.1) | copy-start | bytes 61444
  35.1 31.9 %slice-start = ((s8[6553600]{0:T(1024)(128)(4,1)}), s8[4194304]{0:T(1024)(128)(4,1)S(1)}, s32[]{:S(2)}) async-start(s8[6553600]{0:T(1024)(128)(4,1)} %bitcast.17), calls=%async_computation | async-start | bytes 8388608
  37.1 5.5 %collective-permute-start.17 = (bf16[16,5120]{1,0:T(8,128)(2,1)S(1)}, bf16[16,5120]{1,0:T(8,128)(2,1)S(1)}, u32[]{:S(2)}, u32[]{:S(2)}) collective-permute-start(bf16[16,5120]{1,0:T(8,128)(2,1)S(1)} %get-tuple-element.53), channel_id=1, source_target_pairs={{2,0},{3,1},{0,2},{1,3},{6,4},{7,5},{4,6},{5,7},{10,8},{11,9},{8,1... | collective-permute-start | bytes 491528 | tf_op jit(solution)/shard_map/ppermute | solution.py:50
  39.3 4.6 %collective-permute-start.16 = (bf16[16,5120]{1,0:T(8,128)(2,1)S(1)}, bf16[16,5120]{1,0:T(8,128)(2,1)S(1)}, u32[]{:S(2)}, u32[]{:S(2)}) collective-permute-start(bf16[16,5120]{1,0:T(8,128)(2,1)S(1)} %get-tuple-element.51), channel_id=1, source_target_pairs={{1,0},{0,1},{3,2},{2,3},{5,4},{4,5},{7,6},{6,7},{9,8},{8,9},{11,10... | collective-permute-start | bytes 491528 | tf_op jit(solution)/shard_map/ppermute | solution.py:50
  39.5 27.5 %slice-start.1 = ((s8[6553600]{0:T(1024)(128)(4,1)}), s8[2359296]{0:T(1024)(128)(4,1)S(1)}, s32[]{:S(2)}) async-start(s8[6553600]{0:T(1024)(128)(4,1)} %bitcast.17), calls=%async_computation.1 | async-start | bytes 4718592
  39.6 27.5 %slice-start.3 = ((s8[6553600]{0:T(1024)(128)(4,1)}), s8[4194304]{0:T(1024)(128)(4,1)S(1)}, s32[]{:S(2)}) async-start(s8[6553600]{0:T(1024)(128)(4,1)} %bitcast.20), calls=%async_computation.3 | async-start | bytes 8388608
  40.2 5.2 %collective-permute-start.15 = (bf16[8,5120]{1,0:T(8,128)(2,1)S(1)}, bf16[8,5120]{1,0:T(8,128)(2,1)S(1)}, u32[]{:S(2)}, u32[]{:S(2)}) collective-permute-start(bf16[8,5120]{1,0:T(8,128)(2,1)S(1)} %get-tuple-element.49.refs_0_), channel_id=1, source_target_pairs={{0,12},{1,13},{2,14},{3,15},{4,8},{5,9},{6,10},{7,11},{8,4},{9,5},... | collective-permute-start | bytes 245768 | tf_op jit(solution)/shard_map/ppermute | solution.py:50
  42.6 7.5 %collective-permute-start.14 = (bf16[8,5120]{1,0:T(8,128)(2,1)S(1)}, bf16[8,5120]{1,0:T(8,128)(2,1)S(1)}, u32[]{:S(2)}, u32[]{:S(2)}) collective-permute-start(bf16[8,5120]{1,0:T(8,128)(2,1)S(1)} %get-tuple-element.49.refs_0_), channel_id=1, source_target_pairs={{0,8},{1,9},{2,10},{3,11},{4,12},{5,13},{6,14},{7,15},{8,0},{9,1},... | collective-permute-start | bytes 245768 | tf_op jit(solution)/shard_map/ppermute | solution.py:50
  42.6 7.5 %collective-permute-start.13 = (bf16[8,5120]{1,0:T(8,128)(2,1)S(1)}, bf16[8,5120]{1,0:T(8,128)(2,1)S(1)}, u32[]{:S(2)}, u32[]{:S(2)}) collective-permute-start(bf16[8,5120]{1,0:T(8,128)(2,1)S(1)} %get-tuple-element.49.refs_0_), channel_id=1, source_target_pairs={{0,4},{1,5},{2,6},{3,7},{4,0},{5,1},{6,2},{7,3},{8,12},{9,13},{10,... | collective-permute-start | bytes 245768 | tf_op jit(solution)/shard_map/ppermute | solution.py:50
  43.9 7.6 %collective-permute-start.21 = (bf16[32,5120]{1,0:T(8,128)(2,1)S(1)}, bf16[32,5120]{1,0:T(8,128)(2,1)S(1)}, u32[]{:S(2)}, u32[]{:S(2)}) collective-permute-start(bf16[32,5120]{1,0:T(8,128)(2,1)S(1)} %add_half.5.refs_5_), channel_id=1, source_target_pairs={{1,0},{0,1},{3,2},{2,3},{5,4},{4,5},{7,6},{6,7},{9,8},{8,9},{11,10... | collective-permute-start | bytes 983048 | tf_op jit(solution)/shard_map/ppermute | solution.py:50
  45.4 6.2 %collective-permute-start.20 = (bf16[32,5120]{1,0:T(8,128)(2,1)S(1)}, bf16[32,5120]{1,0:T(8,128)(2,1)S(1)}, u32[]{:S(2)}, u32[]{:S(2)}) collective-permute-start(bf16[32,5120]{1,0:T(8,128)(2,1)S(1)} %add_half.4.refs_4_), channel_id=1, source_target_pairs={{2,0},{3,1},{0,2},{1,3},{6,4},{7,5},{4,6},{5,7},{10,8},{11,9},{8,1... | collective-permute-start | bytes 983048 | tf_op jit(solution)/shard_map/ppermute | solution.py:50
  50.1 9.7 %collective-permute-start.19 = (bf16[32,5120]{1,0:T(8,128)(2,1)S(1)}, bf16[32,5120]{1,0:T(8,128)(2,1)S(1)}, u32[]{:S(2)}, u32[]{:S(2)}) collective-permute-start(bf16[32,5120]{1,0:T(8,128)(2,1)S(1)} %join.3.refs_3_.refs_2_), channel_id=1, source_target_pairs={{0,2},{1,3},{2,0},{3,1},{4,6},{5,7},{6,4},{7,5},{8,10},{9,11},{10,... | collective-permute-start | bytes 983048 | tf_op jit(solution)/shard_map/ppermute | solution.py:50
  50.2 9.7 %collective-permute-start.18 = (bf16[32,5120]{1,0:T(8,128)(2,1)S(1)}, bf16[32,5120]{1,0:T(8,128)(2,1)S(1)}, u32[]{:S(2)}, u32[]{:S(2)}) collective-permute-start(bf16[32,5120]{1,0:T(8,128)(2,1)S(1)} %join.3.refs_3_.refs_2_), channel_id=1, source_target_pairs={{0,1},{1,0},{2,3},{3,2},{4,5},{5,4},{6,7},{7,6},{8,9},{9,8},{10,11... | collective-permute-start | bytes 983048 | tf_op jit(solution)/shard_map/ppermute | solution.py:50
  51.7 9.5 %collective-permute-start.24 = (bf16[8,5120]{1,0:T(8,128)(2,1)S(1)}, bf16[8,5120]{1,0:T(8,128)(2,1)S(1)}, u32[]{:S(2)}, u32[]{:S(2)}) collective-permute-start(bf16[8,5120]{1,0:T(8,128)(2,1)S(1)} %get-tuple-element.57), channel_id=1, source_target_pairs={{4,0},{5,1},{6,2},{7,3},{0,4},{1,5},{2,6},{3,7},{12,8},{13,9},{14,... | collective-permute-start | bytes 245768 | tf_op jit(solution)/shard_map/ppermute | solution.py:50
  59.9 7.1 %collective-permute-start.22 = (bf16[16,5120]{1,0:T(8,128)(2,1)S(1)}, bf16[16,5120]{1,0:T(8,128)(2,1)S(1)}, u32[]{:S(2)}, u32[]{:S(2)}) collective-permute-start(bf16[16,5120]{1,0:T(8,128)(2,1)S(1)} %get-tuple-element.55), channel_id=1, source_target_pairs={{0,1},{1,0},{2,3},{3,2},{4,5},{5,4},{6,7},{7,6},{8,9},{9,8},{10,11... | collective-permute-start | bytes 491528 | tf_op jit(solution)/shard_map/ppermute | solution.py:50
  61.2 5.8 %collective-permute-start.23 = (bf16[16,5120]{1,0:T(8,128)(2,1)S(1)}, bf16[16,5120]{1,0:T(8,128)(2,1)S(1)}, u32[]{:S(2)}, u32[]{:S(2)}) collective-permute-start(bf16[16,5120]{1,0:T(8,128)(2,1)S(1)} %get-tuple-element.56), channel_id=1, source_target_pairs={{0,2},{1,3},{2,0},{3,1},{4,6},{5,7},{6,4},{7,5},{8,10},{9,11},{10,... | collective-permute-start | bytes 491528 | tf_op jit(solution)/shard_map/ppermute | solution.py:50
  61.2 5.7 %collective-permute-start.25 = (bf16[8,5120]{1,0:T(8,128)(2,1)S(1)}, bf16[8,5120]{1,0:T(8,128)(2,1)S(1)}, u32[]{:S(2)}, u32[]{:S(2)}) collective-permute-start(bf16[8,5120]{1,0:T(8,128)(2,1)S(1)} %get-tuple-element.58), channel_id=1, source_target_pairs={{8,0},{9,1},{10,2},{11,3},{12,4},{13,5},{14,6},{15,7},{0,8},{1,9},... | collective-permute-start | bytes 245768 | tf_op jit(solution)/shard_map/ppermute | solution.py:50
  61.3 5.7 %collective-permute-start.26 = (bf16[8,5120]{1,0:T(8,128)(2,1)S(1)}, bf16[8,5120]{1,0:T(8,128)(2,1)S(1)}, u32[]{:S(2)}, u32[]{:S(2)}) collective-permute-start(bf16[8,5120]{1,0:T(8,128)(2,1)S(1)} %get-tuple-element.59), channel_id=1, source_target_pairs={{12,0},{13,1},{14,2},{15,3},{8,4},{9,5},{10,6},{11,7},{4,8},{5,9},... | collective-permute-start | bytes 245768 | tf_op jit(solution)/shard_map/ppermute | solution.py:50
  69.4 4.2 %collective-permute-start.29 = (bf16[16,5120]{1,0:T(8,128)(2,1)S(1)}, bf16[16,5120]{1,0:T(8,128)(2,1)S(1)}, u32[]{:S(2)}, u32[]{:S(2)}) collective-permute-start(bf16[16,5120]{1,0:T(8,128)(2,1)S(1)} %get-tuple-element.64), channel_id=1, source_target_pairs={{2,0},{3,1},{0,2},{1,3},{6,4},{7,5},{4,6},{5,7},{10,8},{11,9},{8,1... | collective-permute-start | bytes 491528 | tf_op jit(solution)/shard_map/ppermute | solution.py:50
  70.9 4.2 %collective-permute-start.27 = (bf16[16,5120]{1,0:T(8,128)(2,1)S(1)}, bf16[16,5120]{1,0:T(8,128)(2,1)S(1)}, u32[]{:S(2)}, u32[]{:S(2)}) collective-permute-start(bf16[16,5120]{1,0:T(8,128)(2,1)S(1)} %get-tuple-element.62), channel_id=1, source_target_pairs={{1,0},{0,1},{3,2},{2,3},{5,4},{4,5},{7,6},{6,7},{9,8},{8,9},{11,10... | collective-permute-start | bytes 491528 | tf_op jit(solution)/shard_map/ppermute | solution.py:50
  73.7 7.1 %collective-permute-start.30 = (bf16[32,5120]{1,0:T(8,128)(2,1)S(1)}, bf16[32,5120]{1,0:T(8,128)(2,1)S(1)}, u32[]{:S(2)}, u32[]{:S(2)}) collective-permute-start(bf16[32,5120]{1,0:T(8,128)(2,1)S(1)} %add_half.7), channel_id=1, source_target_pairs={{1,0},{0,1},{3,2},{2,3},{5,4},{4,5},{7,6},{6,7},{9,8},{8,9},{11,10... | collective-permute-start | bytes 983048 | tf_op jit(solution)/shard_map/ppermute | solution.py:50
  75.1 7.7 %collective-permute-start.28 = (bf16[32,5120]{1,0:T(8,128)(2,1)S(1)}, bf16[32,5120]{1,0:T(8,128)(2,1)S(1)}, u32[]{:S(2)}, u32[]{:S(2)}) collective-permute-start(bf16[32,5120]{1,0:T(8,128)(2,1)S(1)} %add_half.6), channel_id=1, source_target_pairs={{2,0},{3,1},{0,2},{1,3},{6,4},{7,5},{4,6},{5,7},{10,8},{11,9},{8,1... | collective-permute-start | bytes 983048 | tf_op jit(solution)/shard_map/ppermute | solution.py:50
  75.4 11.3 %collective-permute-start.36 = (f32[8,5120]{1,0:T(8,128)S(1)}, f32[8,5120]{1,0:T(8,128)S(1)}, u32[]{:S(2)}, u32[]{:S(2)}) collective-permute-start(f32[8,5120]{1,0:T(8,128)S(1)} %add_last.2.refs_7_), channel_id=1, source_target_pairs={{0,16},{1,17},{2,18},{3,19},{4,20},{5,21},{6,22},{7,23},{8,24},{9,... | collective-permute-start | bytes 491528 | tf_op jit(solution)/shard_map/ppermute | solution.py:27
  83.0 3.9 %collective-permute-start.32 = (bf16[8,5120]{1,0:T(8,128)(2,1)S(1)}, bf16[8,5120]{1,0:T(8,128)(2,1)S(1)}, u32[]{:S(2)}, u32[]{:S(2)}) collective-permute-start(bf16[8,5120]{1,0:T(8,128)(2,1)S(1)} %get-tuple-element.66), channel_id=1, source_target_pairs={{4,0},{5,1},{6,2},{7,3},{0,4},{1,5},{2,6},{3,7},{12,8},{13,9},{14,... | collective-permute-start | bytes 245768 | tf_op jit(solution)/shard_map/ppermute | solution.py:50
  84.2 5.9 %collective-permute-start.33 = (bf16[8,5120]{1,0:T(8,128)(2,1)S(1)}, bf16[8,5120]{1,0:T(8,128)(2,1)S(1)}, u32[]{:S(2)}, u32[]{:S(2)}) collective-permute-start(bf16[8,5120]{1,0:T(8,128)(2,1)S(1)} %get-tuple-element.67), channel_id=1, source_target_pairs={{8,0},{9,1},{10,2},{11,3},{12,4},{13,5},{14,6},{15,7},{0,8},{1,9},... | collective-permute-start | bytes 245768 | tf_op jit(solution)/shard_map/ppermute | solution.py:50
  84.8 5.3 %collective-permute-start.34 = (bf16[8,5120]{1,0:T(8,128)(2,1)S(1)}, bf16[8,5120]{1,0:T(8,128)(2,1)S(1)}, u32[]{:S(2)}, u32[]{:S(2)}) collective-permute-start(bf16[8,5120]{1,0:T(8,128)(2,1)S(1)} %get-tuple-element.68), channel_id=1, source_target_pairs={{12,0},{13,1},{14,2},{15,3},{8,4},{9,5},{10,6},{11,7},{4,8},{5,9},... | collective-permute-start | bytes 245768 | tf_op jit(solution)/shard_map/ppermute | solution.py:50
  90.2 10.4 %collective-permute-start.35 = (f32[8,5120]{1,0:T(8,128)S(1)}, f32[8,5120]{1,0:T(8,128)S(1)}, u32[]{:S(2)}, u32[]{:S(2)}) collective-permute-start(f32[8,5120]{1,0:T(8,128)S(1)} %add_last.3.back_ref), channel_id=1, source_target_pairs={{0,16},{1,17},{2,18},{3,19},{4,20},{5,21},{6,22},{7,23},{8,24},{9,... | collective-permute-start | bytes 491528 | tf_op jit(solution)/shard_map/ppermute | solution.py:17

commit v5 on v4

--- a/solution.py
+++ b/solution.py
@@ -267,12 +267,14 @@
 
     quarter = half // 2
 
-    def kernel(x_ref, gain_ref, gate_ref, slot_ref, copy_ref, *refs):
+    def kernel(x_ref, gain_ref, gate_ref, slot_ref, copy_ref, left_ref, right_ref, *refs):
         *q_refs, gates_ref = refs
         gate, slots = gate_ref[...], slot_ref[...].astype(jnp.float32)
-        copy_ref[:tokens] = x_ref[...]
-        copy_ref[tokens:] = jnp.zeros((EXTRA, width), jnp.bfloat16)
-        copy_ref[tokens:, :tokens] = extra_rows(gate, slots)
+        copy_ref[...] = x_ref[...]
+        left_ref[:tokens] = x_ref[:, :half]
+        left_ref[tokens:] = jnp.zeros((EXTRA, half), jnp.bfloat16)
+        left_ref[tokens:, :tokens] = extra_rows(gate, slots)
+        right_ref[...] = x_ref[:, half:]
         gates_ref[0:1] = gate
         gates_ref[1:2] = slots
         x = x_ref[...].astype(jnp.float32)
@@ -284,10 +286,16 @@
 
     part = jax.ShapeDtypeStruct((tokens, quarter), jnp.bfloat16)
     one = jax.ShapeDtypeStruct((tokens, half), jnp.bfloat16)
-    same = jax.ShapeDtypeStruct((tokens + EXTRA, width), x.dtype)
+    same = jax.ShapeDtypeStruct((tokens, width), x.dtype)
+    left = jax.ShapeDtypeStruct((tokens + EXTRA, half), x.dtype)
+    right = jax.ShapeDtypeStruct((tokens, half), x.dtype)
     pair = jax.ShapeDtypeStruct((2, tokens), jnp.float32)
     return local_kernel(
-        kernel, "queries", [same, part, part, one, pair], [x, gain, gate, slots], after
+        kernel,
+        "queries",
+        [same, left, right, part, part, one, pair],
+        [x, gain, gate, slots],
+        after,
     )
 
 
@@ -459,68 +467,110 @@
     )
 
 
-def finish(section, res, back, gates=None):
-    tokens, width = res.shape[0] - (EXTRA if gates is None else 0), res.shape[1]
+def lay_out(section, sections, first, second):
+    rows, width = first.shape
+    half = width // 2
+
+    def kernel(section, first_ref, second_ref, out_ref, after_ref):
+        decodes = jnp.full((rows, 1), section[0]) >= sections // 2
+        after_ref[...] = jnp.zeros_like(after_ref)
+        for at, ref in ((0, first_ref), (half, second_ref)):
+            for side in (0, 1):
+                block = jnp.where(decodes, ref[:, side * half : (side + 1) * half], 0.0)
+                out_ref[:, side, at : at + half] = block
+
+    outs = [
+        jax.ShapeDtypeStruct((rows, 2, width), jnp.float32),
+        jax.ShapeDtypeStruct((8, HD), jnp.float32),
+    ]
+    return local_kernel(kernel, "lay_out", outs, [section.reshape(1), first, second], scalars=1)
+
+
+def blank(section, after, like):
+    def kernel(section, after_any, out_any, after_ref, zero_ref, sem):
+        after_ref[...] = jnp.zeros_like(after_ref)
+
+        @pl.when(section[0] == 0)
+        def _():
+            zero_ref[...] = jnp.zeros_like(zero_ref)
+            copy = pltpu.make_async_copy(zero_ref, out_any, sem)
+            copy.start()
+            copy.wait()
+
+    return pl.pallas_call(
+        kernel,
+        out_shape=(
+            jax.ShapeDtypeStruct(like.shape, like.dtype),
+            jax.ShapeDtypeStruct((8, HD), jnp.float32),
+        ),
+        in_specs=[pl.BlockSpec(memory_space=pltpu.SMEM), ANYWHERE],
+        out_specs=(pl.BlockSpec(memory_space=pltpu.HBM), in_vmem(1)[0]),
+        scratch_shapes=[pltpu.VMEM(like.shape, like.dtype), pltpu.SemaphoreType.DMA],
+        compiler_params=compiler_params(),
+        name="blank",
+    )(section.reshape(1), after)
+
+
+def finish(section, res, back, room=None, gates=None):
+    tokens, part = res[-1].shape
+    width = part * len(res)
     one = jax.ShapeDtypeStruct((tokens, width), jnp.bfloat16)
-    step = next(s for s in (1280, 1024, 512, 256, 128) if width % s == 0)
+    step = next(s for s in (1280, 1024, 512, 256, 128) if part % s == 0)
     parts = [slice(at, at + step) for at in range(0, width, step)]
 
-    def kernel(section, res_ref, back_ref, *refs):
-        out_any, out_ref, sems = refs[-3:]
-        copies = [
-            pltpu.make_async_copy(out_ref.at[:, c], out_any.at[:, c], sems.at[i])
-            for i, c in enumerate(parts)
-        ]
+    def kernel(section, *refs):
+        res_refs, (back_ref, last, out_any, out_ref, sems) = refs[: len(res)], refs[len(res) :]
 
         def compute():
             if gates is None:
-                extra = res_ref[tokens:, :tokens].astype(jnp.float32)
+                extra = res_refs[0][tokens:, :tokens].astype(jnp.float32)
                 gate, slot = extra[0:1] + extra[1:2] + extra[2:3], extra[3:4]
             else:
-                gate, slot = refs[0][0:1], refs[0][1:2]
+                gate, slot = last[0:1], last[1:2]
             gate = jnp.broadcast_to(gate, (CAP, tokens)).T[:, 0:1]
             slots = lax.broadcasted_iota(jnp.int32, (CAP, tokens), 0).astype(jnp.float32)
             onehot = jnp.where(slot == slots, 1.0, 0.0).T
             onehot = jnp.concatenate([onehot] * 3, axis=1).astype(jnp.bfloat16)
-            for copy, columns in zip(copies, parts):
+            copies = []
+            for i, columns in enumerate(parts):
                 back = back_ref[:, columns]
                 high = back.astype(jnp.bfloat16).astype(jnp.float32)
                 middle = (back - high).astype(jnp.bfloat16).astype(jnp.float32)
                 three = jnp.concatenate([high, middle, back - high - middle], axis=0)
                 moved = dot(onehot, three.astype(jnp.bfloat16))
-                here = res_ref[:tokens, columns].astype(jnp.float32)
+                of, at = divmod(columns.start, part)
+                here = res_refs[of][:tokens, at : at + step].astype(jnp.float32)
                 out_ref[:, columns] = (here + gate * moved).astype(jnp.bfloat16)
+                copy = pltpu.make_async_copy(
+                    out_ref.at[:, columns], out_any.at[:, columns], sems.at[i]
+                )
                 copy.start()
+                copies.append(copy)
+            for copy in copies:
+                copy.wait()
 
         if gates is None:
             pl.when(section[0] > 0)(compute)
-
-            @pl.when(section[0] == 0)
-            def _():
-                out_ref[...] = jnp.zeros_like(out_ref)
-                for copy in copies:
-                    copy.start()
         else:
             compute()
-        for copy in copies:
-            copy.wait()
-
-    args = [section.reshape(1), res, back] + ([] if gates is None else [gates])
+
+    last = (room, pl.BlockSpec(memory_space=pltpu.HBM)) if gates is None else (gates, in_vmem(1)[0])
     return pl.pallas_call(
         kernel,
         out_shape=one,
-        in_specs=[pl.BlockSpec(memory_space=pltpu.SMEM)] + in_vmem(len(args) - 1),
-        out_specs=ANYWHERE,
+        in_specs=[pl.BlockSpec(memory_space=pltpu.SMEM), *in_vmem(len(res) + 1), last[1]],
+        out_specs=pl.BlockSpec(memory_space=pltpu.HBM),
         scratch_shapes=[
             pltpu.VMEM(one.shape, one.dtype),
             pltpu.SemaphoreType.DMA((len(parts),)),
         ],
+        input_output_aliases={len(res) + 2: 0} if gates is None else {},
         compiler_params=compiler_params(),
         cost_estimate=pl.CostEstimate(
             flops=50 * tokens * width, bytes_accessed=5 * tokens * width, transcendentals=0
         ),
         name="finish",
-    )(*args)
+    )(section.reshape(1), *res, back, last[0])
 
 
 def local(
@@ -538,7 +588,7 @@
     first = swapped(memory[0, :, :, :half].reshape(own_rows, width))
     second = memory[0, :, :, half:].reshape(own_rows, width)
     pieces = grid.gather(jnp.where(decoder, second, first))
-    current, *first, second, gates = make_queries(
+    current, left, right, *first, second, gates = make_queries(
         layer_in[0], attn_gain, gate_prob, slot_index, [pieces[0]]
     )
     first = [swapped(q) for q in first]
@@ -563,36 +613,34 @@
     residual, capacity = settle(
         section, sections, current, to_decoder(mixed), mixed, norm_gain, gates, [parts[0]]
     )
-    if sections == 2:
-        residual_before = passed_along(current, "section", 1)
-    else:
+    if sections != 2:
         extra = extra_rows(gates[0:1], gates[1:2])
-        extra = jnp.pad(extra, ((0, 0), (0, width - extra.shape[1])))
-        residual_before = passed_along(jnp.concatenate([residual, extra], axis=0), "section", 1)
+        extra = jnp.pad(extra, ((0, 0), (0, half - extra.shape[1])))
+        left, right = jnp.concatenate([residual[:, :half], extra], axis=0), residual[:, half:]
+    residual_before = [passed_along(x, "section", 1) for x in (left, right)]
     grads = grid.scatter(parts, own_rows)
     halves = next(grads)
     sums = []
 
     def plane_sums(own):
         if not sums:
-            sums.append(grads.send([own])[0])
-        return [sums[0][0]]
+            sums.append(grads.send([own]))
+        return [sums[0][0][0]]
 
     gathered = grid.gather(capacity, halves, plane_sums)
-    total_grad = grads.send([])
     computed = expert(
-        expert_in[0], expert_out[0], gathered, grid.heights(CAP), grid.types(), [total_grad]
-    )
-    results = grid.scatter(computed, CAP)
+        expert_in[0], expert_out[0], gathered, grid.heights(CAP), grid.types(), sums[0][1][:2]
+    )
+    total_grad = grads.send([computed[0]])
+    room, made = blank(section, capacity, residual)
+    results = grid.scatter(computed, CAP, [total_grad, made])
     next(results)
-    results.send([residual_before])
-    returned = results.send([])
+    results.send([])
+    total_grad, laid = lay_out(section, sections, to_decoder(total_grad), total_grad)
+    returned = results.send([laid])
     returned_before = passed_along(returned, "section", 1)
-    output = finish(section, residual, returned, gates)
-    arriving = finish(section, residual_before, returned_before)
-    first = to_decoder(total_grad).reshape(own_rows, 2, half)
-    total_grad = jnp.concatenate([first, total_grad.reshape(own_rows, 2, half)], axis=2)
-    total_grad = jnp.where(decoder, total_grad, 0.0)
+    output = finish(section, [residual], returned, gates=gates)
+    arriving = finish(section, residual_before, returned_before, room)
     return (output[None], arriving[None], total_grad[None])
 
 

time: 103 us -> 102 us (level); the launches traced: 102 us -> 102 us
  starting transfers between devices: 38.2 us -> 42.5 us
  waiting for transfers between devices: 48.9 us -> 45 us
    ppermute x28, waiting for transfers between devices: 41 us -> 34.8 us  [shift(): return lax.ppermute(block, 'expert', route)]
    ppermute x28, starting transfers between devices: 28.4 us -> 31.5 us  [shift(): return lax.ppermute(block, 'expert', route)]
    ppermute x2, waiting for transfers between devices: 0.01 us -> 1.29 us  [to_decoder(): lax.ppermute(block, 'section', [(i, i + apart) for i in range(apart)])]
    ppermute x2 -> x3, starting transfers between devices: 2.58 us -> 3.85 us  [passed_along(): return lax.ppermute(block, axis, route)]
    ppermute x2 -> x3, waiting for transfers between devices: 6.67 us -> 7.65 us  [passed_along(): return lax.ppermute(block, axis, route)]
    pallas_call x17 -> x18, Pallas kernels: 8.5 us -> 9.4 us  [local_kernel(): pl.pallas_call(body, out_shape=tuple(outs), in_specs=in_specs, out_specs=...]
  transfers between devices with their start and end apart: 37 -> 38, of which waited for: 17 -> 17; matrix products, arithmetic and copies ran while one was open for 1% -> 0% of each run, Pallas kernels for 8% -> 6%
where the time goes in v5:
time: 102 us
  waiting for transfers between devices  45 us (44%)
  starting transfers between devices  42.5 us (42%)
  Pallas kernels  12.4 us (12%)
  local copies, waits for them, and re-layouts  1.24 us (1%)
    ppermute x28, waiting for transfers between devices, shift(): return lax.ppermute(block, 'expert', route)  34.8 us
    ppermute x28, starting transfers between devices, shift(): return lax.ppermute(block, 'expert', route)  31.5 us
    pallas_call x18, Pallas kernels, local_kernel(): pl.pallas_call(body, out_shape=tuple(outs), in_specs=in_specs, out_specs=...  9.4 us
    ppermute x3, waiting for transfers between devices, passed_along(): return lax.ppermute(block, axis, route)  7.65 us
    ppermute x5, starting transfers between devices, swapped(): lax.ppermute(block, 'section', [(i, (i + sections // 2) % sections) for i...  4.61 us
    ppermute x3, starting transfers between devices, passed_along(): return lax.ppermute(block, axis, route)  3.85 us
    pallas_call x2, Pallas kernels, finish(): pl.pallas_call(kernel, out_shape=one, in_specs=[pl.BlockSpec(memory_space...  3.02 us
    ppermute x2, starting transfers between devices, to_decoder(): lax.ppermute(block, 'section', [(i, i + apart) for i in range(apart)])  2.57 us
  transfers between devices with their start and end apart: 38, of which 17 were waited for; matrix products, arithmetic and copies ran while one was open for 0% of the time, Pallas kernels for 6%

profile of v5, /device:TPU:1, one launch (start us, length us, event | category | flops | bytes accessed | tf_op | source)
XLA Modules:
  0.0 102.1 jit_solution(17843116970796021337)
XLA Ops:
  0.7 1.1 %slice_bitcast_fusion = (bf16[1,8,2,2560]{3,2,1,0:T(2,128)(2,1)S(1)}, bf16[1,8,2,2560]{3,2,1,0:T(2,128)(2,1)S(1)}) fusion(bf16[1,8,2,5120]{3,2,1,0:T(2,128)(2,1)} %param.10), kind=kLoop, calls=%fused_computation | loop fusion | bytes 327680
  1.8 0.1 collective-permute-start
  2.0 1.2 %collective-permute-done = bf16[8,5120]{1,0:T(8,128)(2,1)S(1)} collective-permute-done((bf16[8,5120]{1,0:T(8,128)(2,1)S(1)}, bf16[8,5120]{1,0:T(8,128)(2,1)S(1)}, u32[]{:S(2)}, u32[]{:S(2)}) %collective-permute-start) | collective-permute-done | bytes 81952 | tf_op jit(solution)/shard_map/ppermute | solution.py:22
  3.2 4.5 %collective-permute-start.3 = (bf16[8,5120]{1,0:T(8,128)(2,1)S(1)}, bf16[8,5120]{1,0:T(8,128)(2,1)S(1)}, u32[]{:S(2)}, u32[]{:S(2)}) collective-permute-start(bf16[8,5120]{1,0:T(8,128)(2,1)S(1)} %broadcast_select_fusion.refs_0_), channel_id=1, source_target_pairs={{0,12},{1,13},{2,14},{3,15},{4,8},{5,9},{6,10},{7,11},{8,4},{9,5},... | collective-permute-start | bytes 245768 | tf_op jit(solution)/shard_map/ppermute | solution.py:50
  7.7 0.4 collective-permute-start.1
  8.1 2.2 %collective-permute-done.3.refs_3_ = bf16[8,5120]{1,0:T(8,128)(2,1)S(1)} collective-permute-done((bf16[8,5120]{1,0:T(8,128)(2,1)S(1)}, bf16[8,5120]{1,0:T(8,128)(2,1)S(1)}, u32[]{:S(2)}, u32[]{:S(2)}) %collective-permute-start.3) | collective-permute-done | bytes 81952 | tf_op jit(solution)/shard_map/ppermute | solution.py:50
  10.3 4.1 %collective-permute-done.2.refs_2_ = bf16[8,5120]{1,0:T(8,128)(2,1)S(1)} collective-permute-done((bf16[8,5120]{1,0:T(8,128)(2,1)S(1)}, bf16[8,5120]{1,0:T(8,128)(2,1)S(1)}, u32[]{:S(2)}, u32[]{:S(2)}) %collective-permute-start.2) | collective-permute-done | bytes 81952 | tf_op jit(solution)/shard_map/ppermute | solution.py:50
  14.4 1.3 %collective-permute-start.7 = (bf16[32,5120]{1,0:T(8,128)(2,1)S(1)}, bf16[32,5120]{1,0:T(8,128)(2,1)S(1)}, u32[]{:S(2)}, u32[]{:S(2)}) collective-permute-start(bf16[32,5120]{1,0:T(8,128)(2,1)S(1)} %join.2.refs_4_), channel_id=1, source_target_pairs={{0,2},{1,3},{2,0},{3,1},{4,6},{5,7},{6,4},{7,5},{8,10},{9,11},{10,... | collective-permute-start | bytes 983048 | tf_op jit(solution)/shard_map/ppermute | solution.py:50
  15.7 1.2 %collective-permute-start.6 = (bf16[32,5120]{1,0:T(8,128)(2,1)S(1)}, bf16[32,5120]{1,0:T(8,128)(2,1)S(1)}, u32[]{:S(2)}, u32[]{:S(2)}) collective-permute-start(bf16[32,5120]{1,0:T(8,128)(2,1)S(1)} %join.2.refs_4_), channel_id=1, source_target_pairs={{0,1},{1,0},{2,3},{3,2},{4,5},{5,4},{6,7},{7,6},{8,9},{9,8},{10,11... | collective-permute-start | bytes 983048 | tf_op jit(solution)/shard_map/ppermute | solution.py:50
  16.9 1.0 queries.1
  17.9 1.8 %collective-permute-start.4 = (bf16[128,1280]{1,0:T(8,128)(2,1)S(1)}, bf16[128,1280]{1,0:T(8,128)(2,1)S(1)}, u32[]{:S(2)}, u32[]{:S(2)}) collective-permute-start(bf16[128,1280]{1,0:T(8,128)(2,1)S(1)} %get-tuple-element.43), channel_id=1, source_target_pairs={{0,16},{16,0},{1,17},{17,1},{2,18},{18,2},{3,19},{19,3},{4,20},{20... | collective-permute-start | bytes 983048 | tf_op jit(solution)/shard_map/ppermute | solution.py:22
  19.7 0.1 collective-permute-start.5
  19.8 0.1 cut.1
  19.9 0.5 collective-permute-start.10
  20.4 2.1 %collective-permute-done.7.refs_6_ = bf16[32,5120]{1,0:T(8,128)(2,1)S(1)} collective-permute-done((bf16[32,5120]{1,0:T(8,128)(2,1)S(1)}, bf16[32,5120]{1,0:T(8,128)(2,1)S(1)}, u32[]{:S(2)}, u32[]{:S(2)}) %collective-permute-start.7) | collective-permute-done | bytes 327712 | tf_op jit(solution)/shard_map/ppermute | solution.py:50
  22.5 2.1 %collective-permute-start.11 = (bf16[128,1280]{1,0:T(8,128)(2,1)S(1)}, bf16[128,1280]{1,0:T(8,128)(2,1)S(1)}, u32[]{:S(2)}, u32[]{:S(2)}) collective-permute-start(bf16[128,1280]{1,0:T(8,128)(2,1)S(1)} %get-tuple-element.48), channel_id=1, source_target_pairs={{0,16},{16,0},{1,17},{17,1},{2,18},{18,2},{3,19},{19,3},{4,20},{20... | collective-permute-start | bytes 983048 | tf_op jit(solution)/shard_map/ppermute | solution.py:22
  24.6 1.3 %collective-permute-start.8 = (bf16[16,5120]{1,0:T(8,128)(2,1)S(1)}, bf16[16,5120]{1,0:T(8,128)(2,1)S(1)}, u32[]{:S(2)}, u32[]{:S(2)}) collective-permute-start(bf16[16,5120]{1,0:T(8,128)(2,1)S(1)} %slice.16), channel_id=1, source_target_pairs={{0,1},{1,0},{2,3},{3,2},{4,5},{5,4},{6,7},{7,6},{8,9},{9,8},{10,11... | collective-permute-start | bytes 491528 | tf_op jit(solution)/shard_map/ppermute | solution.py:50
  25.9 1.3 %collective-permute-start.9 = (bf16[16,5120]{1,0:T(8,128)(2,1)S(1)}, bf16[16,5120]{1,0:T(8,128)(2,1)S(1)}, u32[]{:S(2)}, u32[]{:S(2)}) collective-permute-start(bf16[16,5120]{1,0:T(8,128)(2,1)S(1)} %slice.17), channel_id=1, source_target_pairs={{0,2},{1,3},{2,0},{3,1},{4,6},{5,7},{6,4},{7,5},{8,10},{9,11},{10,... | collective-permute-start | bytes 491528 | tf_op jit(solution)/shard_map/ppermute | solution.py:50
  27.2 2.0 %collective-permute-done.8.refs_7_ = bf16[16,5120]{1,0:T(8,128)(2,1)S(1)} collective-permute-done((bf16[16,5120]{1,0:T(8,128)(2,1)S(1)}, bf16[16,5120]{1,0:T(8,128)(2,1)S(1)}, u32[]{:S(2)}, u32[]{:S(2)}) %collective-permute-start.8) | collective-permute-done | bytes 163872 | tf_op jit(solution)/shard_map/ppermute | solution.py:50
  29.2 1.2 %collective-permute-done.9.refs_8_ = bf16[16,5120]{1,0:T(8,128)(2,1)S(1)} collective-permute-done((bf16[16,5120]{1,0:T(8,128)(2,1)S(1)}, bf16[16,5120]{1,0:T(8,128)(2,1)S(1)}, u32[]{:S(2)}, u32[]{:S(2)}) %collective-permute-start.9) | collective-permute-done | bytes 163872 | tf_op jit(solution)/shard_map/ppermute | solution.py:50
  30.4 2.0 %attend.1 = (bf16[128,2560]{1,0:T(8,128)(2,1)S(1)}, f32[20,128,128]{2,1,0:T(8,128)S(1)}, bf16[128,2560]{1,0:T(8,128)(2,1)S(1)}) custom-call(s32[1]{0:T(128)} %bitcast.refs_0_.section, bf16[128,1280]{1,0:T(8,128)(2,1)S(1)} %collective-permute-done.4.refs_1_, bf16[128,1280]{1,0:T(8,128)(2,1)S(1)} %collective-permute-done.5.refs_2_, ...), custom_call_target="tpu_custom_call" | custom-call | flops 167772160 | bytes 5242884 | tf_op jit(solution)/shard_map/attend/pallas_call | solution.py:142
  32.5 1.3 %collective-permute-start.12 = (bf16[128,2560]{1,0:T(8,128)(2,1)S(1)}, bf16[128,2560]{1,0:T(8,128)(2,1)S(1)}, u32[]{:S(2)}, u32[]{:S(2)}) collective-permute-start(bf16[128,2560]{1,0:T(8,128)(2,1)S(1)} %get-tuple-element.49.refs_3_), channel_id=1, source_target_pairs={{0,16},{1,17},{2,18},{3,19},{4,20},{5,21},{6,22},{7,23},{8,24},{9,... | collective-permute-start | bytes 1966088 | tf_op jit(solution)/shard_map/ppermute | solution.py:27
  33.8 2.0 %gradient.1 = (f32[32,5120]{1,0:T(8,128)S(1)}, f32[32,5120]{1,0:T(8,128)S(1)}, f32[32,5120]{1,0:T(8,128)S(1)}, bf16[16,5120]{1,0:T(8,128)(2,1)S(1)}, bf16[16,5120]{1,0:T(8,128)(2,1)S(1)}) custom-call(s32[1]{0:T(128)} %bitcast.refs_0_.section, bf16[128,2560]{1,0:T(8,128)(2,1)S(1)} %get-tuple-element.50.q_ref, ...), custom_call_target="tpu_custom_call" | custom-call | flops 419430400 | bytes 6881284 | tf_op jit(solution)/shard_map/gradient/pallas_call | solution.py:142
  35.8 2.2 %collective-permute-start.17 = (bf16[16,5120]{1,0:T(8,128)(2,1)S(1)}, bf16[16,5120]{1,0:T(8,128)(2,1)S(1)}, u32[]{:S(2)}, u32[]{:S(2)}) collective-permute-start(bf16[16,5120]{1,0:T(8,128)(2,1)S(1)} %get-tuple-element.59), channel_id=1, source_target_pairs={{2,0},{3,1},{0,2},{1,3},{6,4},{7,5},{4,6},{5,7},{10,8},{11,9},{8,1... | collective-permute-start | bytes 491528 | tf_op jit(solution)/shard_map/ppermute | solution.py:50
  38.0 0.3 collective-permute-start.16
  38.3 0.7 settle.1
  38.9 2.4 %collective-permute-start.15 = (bf16[8,5120]{1,0:T(8,128)(2,1)S(1)}, bf16[8,5120]{1,0:T(8,128)(2,1)S(1)}, u32[]{:S(2)}, u32[]{:S(2)}) collective-permute-start(bf16[8,5120]{1,0:T(8,128)(2,1)S(1)} %get-tuple-element.55.refs_0_.after_any), channel_id=1, source_target_pairs={{0,12},{1,13},{2,14},{3,15},{4,8},{5,9},{6,10},{7,11},{8,4},{9,5},... | collective-permute-start | bytes 245768 | tf_op jit(solution)/shard_map/ppermute | solution.py:50
  41.3 1.2 %collective-permute-start.13 = (bf16[8,5120]{1,0:T(8,128)(2,1)S(1)}, bf16[8,5120]{1,0:T(8,128)(2,1)S(1)}, u32[]{:S(2)}, u32[]{:S(2)}) collective-permute-start(bf16[8,5120]{1,0:T(8,128)(2,1)S(1)} %get-tuple-element.55.refs_0_.after_any), channel_id=1, source_target_pairs={{0,4},{1,5},{2,6},{3,7},{4,0},{5,1},{6,2},{7,3},{8,12},{9,13},{10,... | collective-permute-start | bytes 245768 | tf_op jit(solution)/shard_map/ppermute | solution.py:50
  42.6 0.1 add_half.5.refs_5_
  42.6 1.3 %collective-permute-start.21 = (bf16[32,5120]{1,0:T(8,128)(2,1)S(1)}, bf16[32,5120]{1,0:T(8,128)(2,1)S(1)}, u32[]{:S(2)}, u32[]{:S(2)}) collective-permute-start(bf16[32,5120]{1,0:T(8,128)(2,1)S(1)} %add_half.5.refs_5_), channel_id=1, source_target_pairs={{1,0},{0,1},{3,2},{2,3},{5,4},{4,5},{7,6},{6,7},{9,8},{8,9},{11,10... | collective-permute-start | bytes 983048 | tf_op jit(solution)/shard_map/ppermute | solution.py:50
  44.0 0.1 collective-permute-start.20
  44.1 4.7 %collective-permute-done.14.refs_2_ = bf16[8,5120]{1,0:T(8,128)(2,1)S(1)} collective-permute-done((bf16[8,5120]{1,0:T(8,128)(2,1)S(1)}, bf16[8,5120]{1,0:T(8,128)(2,1)S(1)}, u32[]{:S(2)}, u32[]{:S(2)}) %collective-permute-start.14) | collective-permute-done | bytes 81952 | tf_op jit(solution)/shard_map/ppermute | solution.py:50
  48.9 0.6 collective-permute-start.19
  49.4 0.8 collective-permute-start.18
  50.2 0.1 add_blocks.2
  50.4 8.4 %collective-permute-done.19.refs_0_.refs_4_ = bf16[32,5120]{1,0:T(8,128)(2,1)S(1)} collective-permute-done((bf16[32,5120]{1,0:T(8,128)(2,1)S(1)}, bf16[32,5120]{1,0:T(8,128)(2,1)S(1)}, u32[]{:S(2)}, u32[]{:S(2)}) %collective-permute-start.19) | collective-permute-done | bytes 327712 | tf_op jit(solution)/shard_map/ppermute | solution.py:50
  58.7 1.3 %collective-permute-start.22 = (bf16[16,5120]{1,0:T(8,128)(2,1)S(1)}, bf16[16,5120]{1,0:T(8,128)(2,1)S(1)}, u32[]{:S(2)}, u32[]{:S(2)}) collective-permute-start(bf16[16,5120]{1,0:T(8,128)(2,1)S(1)} %get-tuple-element.61), channel_id=1, source_target_pairs={{0,1},{1,0},{2,3},{3,2},{4,5},{5,4},{6,7},{7,6},{8,9},{9,8},{10,11... | collective-permute-start | bytes 491528 | tf_op jit(solution)/shard_map/ppermute | solution.py:50
  60.0 2.1 %collective-permute-start.25 = (bf16[8,5120]{1,0:T(8,128)(2,1)S(1)}, bf16[8,5120]{1,0:T(8,128)(2,1)S(1)}, u32[]{:S(2)}, u32[]{:S(2)}) collective-permute-start(bf16[8,5120]{1,0:T(8,128)(2,1)S(1)} %get-tuple-element.64), channel_id=1, source_target_pairs={{8,0},{9,1},{10,2},{11,3},{12,4},{13,5},{14,6},{15,7},{0,8},{1,9},... | collective-permute-start | bytes 245768 | tf_op jit(solution)/shard_map/ppermute | solution.py:50
  62.2 1.2 %collective-permute-done.24.refs_7_.refs_1_ = bf16[8,5120]{1,0:T(8,128)(2,1)S(1)} collective-permute-done((bf16[8,5120]{1,0:T(8,128)(2,1)S(1)}, bf16[8,5120]{1,0:T(8,128)(2,1)S(1)}, u32[]{:S(2)}, u32[]{:S(2)}) %collective-permute-start.24) | collective-permute-done | bytes 81952 | tf_op jit(solution)/shard_map/ppermute | solution.py:50
  63.3 0.9 collective-permute-done.25.refs_8_.refs_2_
  64.2 0.3 collective-permute-done.23.refs_6_
  64.5 2.3 %expert.1 = (f32[32,5120]{1,0:T(8,128)S(1)}, f32[32,5120]{1,0:T(8,128)S(1)}, f32[32,5120]{1,0:T(8,128)S(1)}, bf16[16,5120]{1,0:T(8,128)(2,1)S(1)}, bf16[16,5120]{1,0:T(8,128)(2,1)S(1)}) custom-call(bf16[5120,640]{1,0:T(8,128)(2,1)S(1)} %bitcast.18, bf16[640,5120]{1,0:T(8,128)(2,1)S(1)} %bitcast.19, bf16[32,5120]{1,0:T(8,128)(2,1)S(1)} %join.3.refs_3_.refs_2_, ...), custom_call_target="tpu_custom_call" | custom-call | flops 1677721600 | bytes 16711680 | tf_op jit(solution)/shard_map/expert/pallas_call | solution.py:142
  66.8 0.6 collective-permute-start.26
  67.4 1.0 collective-permute-start.29
  68.4 1.3 %collective-permute-start.35 = (bf16[144,2560]{1,0:T(8,128)(2,1)S(1)}, bf16[144,2560]{1,0:T(8,128)(2,1)S(1)}, u32[]{:S(2)}, u32[]{:S(2)}) collective-permute-start(bf16[144,2560]{1,0:T(8,128)(2,1)S(1)} %get-tuple-element.77), channel_id=1, source_target_pairs={{0,16},{1,17},{2,18},{3,19},{4,20},{5,21},{6,22},{7,23},{8,24},{9,... | collective-permute-start | bytes 2211848 | tf_op jit(solution)/shard_map/ppermute | solution.py:17
  69.6 2.1 %collective-permute-start.27 = (bf16[8,5120]{1,0:T(8,128)(2,1)S(1)}, bf16[8,5120]{1,0:T(8,128)(2,1)S(1)}, u32[]{:S(2)}, u32[]{:S(2)}) collective-permute-start(bf16[8,5120]{1,0:T(8,128)(2,1)S(1)} %get-tuple-element.68), channel_id=1, source_target_pairs={{12,0},{13,1},{14,2},{15,3},{8,4},{9,5},{10,6},{11,7},{4,8},{5,9},... | collective-permute-start | bytes 245768 | tf_op jit(solution)/shard_map/ppermute | solution.py:50
  71.7 1.3 %collective-permute-start.36 = (bf16[128,2560]{1,0:T(8,128)(2,1)S(1)}, bf16[128,2560]{1,0:T(8,128)(2,1)S(1)}, u32[]{:S(2)}, u32[]{:S(2)}) collective-permute-start(bf16[128,2560]{1,0:T(8,128)(2,1)S(1)} %get-tuple-element.78), channel_id=1, source_target_pairs={{0,16},{1,17},{2,18},{3,19},{4,20},{5,21},{6,22},{7,23},{8,24},{9,... | collective-permute-start | bytes 1966088 | tf_op jit(solution)/shard_map/ppermute | solution.py:17
  73.1 1.9 %collective-permute-done.27.refs_3_ = bf16[8,5120]{1,0:T(8,128)(2,1)S(1)} collective-permute-done((bf16[8,5120]{1,0:T(8,128)(2,1)S(1)}, bf16[8,5120]{1,0:T(8,128)(2,1)S(1)}, u32[]{:S(2)}, u32[]{:S(2)}) %collective-permute-start.27) | collective-permute-done | bytes 81952 | tf_op jit(solution)/shard_map/ppermute | solution.py:50
  75.0 0.6 collective-permute-start.28
  75.7 0.9 collective-permute-start.30
  76.6 1.3 %collective-permute-start.34 = (f32[8,5120]{1,0:T(8,128)S(1)}, f32[8,5120]{1,0:T(8,128)S(1)}, u32[]{:S(2)}, u32[]{:S(2)}) collective-permute-start(f32[8,5120]{1,0:T(8,128)S(1)} %add_last.2.refs_2_.second_ref), channel_id=1, source_target_pairs={{0,16},{1,17},{2,18},{3,19},{4,20},{5,21},{6,22},{7,23},{8,24},{9,... | collective-permute-start | bytes 491528 | tf_op jit(solution)/shard_map/ppermute | solution.py:27
  77.9 3.1 %collective-permute-done.28.refs_1_ = bf16[32,5120]{1,0:T(8,128)(2,1)S(1)} collective-permute-done((bf16[32,5120]{1,0:T(8,128)(2,1)S(1)}, bf16[32,5120]{1,0:T(8,128)(2,1)S(1)}, u32[]{:S(2)}, u32[]{:S(2)}) %collective-permute-start.28) | collective-permute-done | bytes 327712 | tf_op jit(solution)/shard_map/ppermute | solution.py:50
  81.0 0.6 collective-permute-done.30.refs_2_
  81.6 0.1 add_blocks.3
  81.7 0.5 collective-permute-start.31
  82.2 1.5 %collective-permute-start.32 = (bf16[8,5120]{1,0:T(8,128)(2,1)S(1)}, bf16[8,5120]{1,0:T(8,128)(2,1)S(1)}, u32[]{:S(2)}, u32[]{:S(2)}) collective-permute-start(bf16[8,5120]{1,0:T(8,128)(2,1)S(1)} %get-tuple-element.74), channel_id=1, source_target_pairs={{8,0},{9,1},{10,2},{11,3},{12,4},{13,5},{14,6},{15,7},{0,8},{1,9},... | collective-permute-start | bytes 245768 | tf_op jit(solution)/shard_map/ppermute | solution.py:50
  83.7 1.3 %collective-permute-done.34.first_ref = f32[8,5120]{1,0:T(8,128)S(1)} collective-permute-done((f32[8,5120]{1,0:T(8,128)S(1)}, f32[8,5120]{1,0:T(8,128)S(1)}, u32[]{:S(2)}, u32[]{:S(2)}) %collective-permute-start.34) | collective-permute-done | bytes 163872 | tf_op jit(solution)/shard_map/ppermute | solution.py:27
  85.0 2.2 %collective-permute-start.33 = (bf16[8,5120]{1,0:T(8,128)(2,1)S(1)}, bf16[8,5120]{1,0:T(8,128)(2,1)S(1)}, u32[]{:S(2)}, u32[]{:S(2)}) collective-permute-start(bf16[8,5120]{1,0:T(8,128)(2,1)S(1)} %get-tuple-element.75), channel_id=1, source_target_pairs={{12,0},{13,1},{14,2},{15,3},{8,4},{9,5},{10,6},{11,7},{4,8},{5,9},... | collective-permute-start | bytes 245768 | tf_op jit(solution)/shard_map/ppermute | solution.py:50
  87.2 0.8 lay_out.1
  88.0 2.1 %collective-permute-done.33.refs_3_ = bf16[8,5120]{1,0:T(8,128)(2,1)S(1)} collective-permute-done((bf16[8,5120]{1,0:T(8,128)(2,1)S(1)}, bf16[8,5120]{1,0:T(8,128)(2,1)S(1)}, u32[]{:S(2)}, u32[]{:S(2)}) %collective-permute-start.33) | collective-permute-done | bytes 81952 | tf_op jit(solution)/shard_map/ppermute | solution.py:50
  90.1 1.3 %collective-permute-start.37 = (f32[8,5120]{1,0:T(8,128)S(1)}, f32[8,5120]{1,0:T(8,128)S(1)}, u32[]{:S(2)}, u32[]{:S(2)}) collective-permute-start(f32[8,5120]{1,0:T(8,128)S(1)} %add_last.3.refs_1_), channel_id=1, source_target_pairs={{0,16},{1,17},{2,18},{3,19},{4,20},{5,21},{6,22},{7,23},{8,24},{9,... | collective-permute-start | bytes 491528 | tf_op jit(solution)/shard_map/ppermute | solution.py:17
  91.4 1.5 %finish.2 = bf16[128,5120]{1,0:T(8,128)(2,1)} custom-call(s32[1]{0:T(128)} %bitcast.refs_0_.section, bf16[128,5120]{1,0:T(8,128)(2,1)S(1)} %get-tuple-element.54.refs_0_, f32[8,5120]{1,0:T(8,128)S(1)} %add_last.3.refs_1_, f32[2,128]{1,0:T(2,128)S(1)} %get-tuple-element.46.refs_1_.refs_5_.refs_2_), custom_call_target="tpu_custom_call" | custom-call | flops 32768000 | bytes 3276800 | tf_op jit(solution)/shard_map/finish/pallas_call | solution.py:558
  93.0 7.6 %collective-permute-done.37.refs_2_ = f32[8,5120]{1,0:T(8,128)S(1)} collective-permute-done((f32[8,5120]{1,0:T(8,128)S(1)}, f32[8,5120]{1,0:T(8,128)S(1)}, u32[]{:S(2)}, u32[]{:S(2)}) %collective-permute-start.37) | collective-permute-done | bytes 163872 | tf_op jit(solution)/shard_map/ppermute | solution.py:17
  100.6 1.5 %finish.3 = bf16[128,5120]{1,0:T(8,128)(2,1)} custom-call(s32[1]{0:T(128)} %bitcast.refs_0_.section, bf16[144,2560]{1,0:T(8,128)(2,1)S(1)} %collective-permute-done.35.refs_0_, bf16[128,2560]{1,0:T(8,128)(2,1)S(1)} %collective-permute-done.36.refs_1_, f32[8,5120]{1,0:T(8,128)S(1)} %collective-permute-done.37.refs_2_, ...), custom_call_target="tpu_custom_call", output_to_operand_aliasing={{}: (4, {})} | custom-call | flops 32768000 | bytes 3276800 | tf_op jit(solution)/shard_map/finish/pallas_call | solution.py:558
  (58 shorter events, 0.5 us)
Async XLA Ops:
  0.6 16.3 %copy-start.5 = (f32[1,128]{1,0:T(1,128)S(1)}, f32[1,128]{1,0:T(1,128)}, u32[]{:S(2)}) copy-start(f32[1,128]{1,0:T(1,128)} %refs_2_.1) | copy-start | bytes 1540
  0.6 16.3 %copy-start.6 = (s32[1,128]{1,0:T(1,128)S(1)}, s32[1,128]{1,0:T(1,128)}, u32[]{:S(2)}) copy-start(s32[1,128]{1,0:T(1,128)} %refs_3_.1) | copy-start | bytes 1540
  0.7 16.3 %copy-start.4 = (f32[1,5120]{1,0:T(1,128)S(1)}, f32[1,5120]{1,0:T(1,128)}, u32[]{:S(2)}) copy-start(f32[1,5120]{1,0:T(1,128)} %refs_1_.1) | copy-start | bytes 61444
  0.7 16.3 %copy-start.1 = (bf16[1,128,5120]{2,1,0:T(8,128)(2,1)S(1)}, bf16[1,128,5120]{2,1,0:T(8,128)(2,1)}, u32[]{:S(2)}) copy-start(bf16[1,128,5120]{2,1,0:T(8,128)(2,1)} %param.9) | copy-start | bytes 3932164
  1.8 1.3 %collective-permute-start = (bf16[8,5120]{1,0:T(8,128)(2,1)S(1)}, bf16[8,5120]{1,0:T(8,128)(2,1)S(1)}, u32[]{:S(2)}, u32[]{:S(2)}) collective-permute-start(bf16[8,5120]{1,0:T(8,128)(2,1)S(1)} %bitcast.25), channel_id=1, source_target_pairs={{0,16},{16,0},{1,17},{17,1},{2,18},{18,2},{3,19},{19,3},{4,20},{20... | collective-permute-start | bytes 245768 | tf_op jit(solution)/shard_map/ppermute | solution.py:22
  2.0 17.8 %copy-start.2 = (bf16[1,128,5120]{2,1,0:T(8,128)(2,1)S(1)}, bf16[1,128,5120]{2,1,0:T(8,128)(2,1)}, u32[]{:S(2)}) copy-start(bf16[1,128,5120]{2,1,0:T(8,128)(2,1)} %param.11) | copy-start | bytes 3932164
  3.2 7.1 %collective-permute-start.3 = (bf16[8,5120]{1,0:T(8,128)(2,1)S(1)}, bf16[8,5120]{1,0:T(8,128)(2,1)S(1)}, u32[]{:S(2)}, u32[]{:S(2)}) collective-permute-start(bf16[8,5120]{1,0:T(8,128)(2,1)S(1)} %broadcast_select_fusion.refs_0_), channel_id=1, source_target_pairs={{0,12},{1,13},{2,14},{3,15},{4,8},{5,9},{6,10},{7,11},{8,4},{9,5},... | collective-permute-start | bytes 245768 | tf_op jit(solution)/shard_map/ppermute | solution.py:50
  7.7 6.6 %collective-permute-start.2 = (bf16[8,5120]{1,0:T(8,128)(2,1)S(1)}, bf16[8,5120]{1,0:T(8,128)(2,1)S(1)}, u32[]{:S(2)}, u32[]{:S(2)}) collective-permute-start(bf16[8,5120]{1,0:T(8,128)(2,1)S(1)} %broadcast_select_fusion.refs_0_), channel_id=1, source_target_pairs={{0,8},{1,9},{2,10},{3,11},{4,12},{5,13},{6,14},{7,15},{8,0},{9,1},... | collective-permute-start | bytes 245768 | tf_op jit(solution)/shard_map/ppermute | solution.py:50
  7.7 6.6 %collective-permute-start.1 = (bf16[8,5120]{1,0:T(8,128)(2,1)S(1)}, bf16[8,5120]{1,0:T(8,128)(2,1)S(1)}, u32[]{:S(2)}, u32[]{:S(2)}) collective-permute-start(bf16[8,5120]{1,0:T(8,128)(2,1)S(1)} %broadcast_select_fusion.refs_0_), channel_id=1, source_target_pairs={{0,4},{1,5},{2,6},{3,7},{4,0},{5,1},{6,2},{7,3},{8,12},{9,13},{10,... | collective-permute-start | bytes 245768 | tf_op jit(solution)/shard_map/ppermute | solution.py:50
  14.4 8.1 %collective-permute-start.7 = (bf16[32,5120]{1,0:T(8,128)(2,1)S(1)}, bf16[32,5120]{1,0:T(8,128)(2,1)S(1)}, u32[]{:S(2)}, u32[]{:S(2)}) collective-permute-start(bf16[32,5120]{1,0:T(8,128)(2,1)S(1)} %join.2.refs_4_), channel_id=1, source_target_pairs={{0,2},{1,3},{2,0},{3,1},{4,6},{5,7},{6,4},{7,5},{8,10},{9,11},{10,... | collective-permute-start | bytes 983048 | tf_op jit(solution)/shard_map/ppermute | solution.py:50
  15.7 8.9 %collective-permute-start.6 = (bf16[32,5120]{1,0:T(8,128)(2,1)S(1)}, bf16[32,5120]{1,0:T(8,128)(2,1)S(1)}, u32[]{:S(2)}, u32[]{:S(2)}) collective-permute-start(bf16[32,5120]{1,0:T(8,128)(2,1)S(1)} %join.2.refs_4_), channel_id=1, source_target_pairs={{0,1},{1,0},{2,3},{3,2},{4,5},{5,4},{6,7},{7,6},{8,9},{9,8},{10,11... | collective-permute-start | bytes 983048 | tf_op jit(solution)/shard_map/ppermute | solution.py:50
  17.9 8.0 %collective-permute-start.4 = (bf16[128,1280]{1,0:T(8,128)(2,1)S(1)}, bf16[128,1280]{1,0:T(8,128)(2,1)S(1)}, u32[]{:S(2)}, u32[]{:S(2)}) collective-permute-start(bf16[128,1280]{1,0:T(8,128)(2,1)S(1)} %get-tuple-element.43), channel_id=1, source_target_pairs={{0,16},{16,0},{1,17},{17,1},{2,18},{18,2},{3,19},{19,3},{4,20},{20... | collective-permute-start | bytes 983048 | tf_op jit(solution)/shard_map/ppermute | solution.py:22
  19.7 7.5 %collective-permute-start.5 = (bf16[128,1280]{1,0:T(8,128)(2,1)S(1)}, bf16[128,1280]{1,0:T(8,128)(2,1)S(1)}, u32[]{:S(2)}, u32[]{:S(2)}) collective-permute-start(bf16[128,1280]{1,0:T(8,128)(2,1)S(1)} %get-tuple-element.44), channel_id=1, source_target_pairs={{0,16},{16,0},{1,17},{17,1},{2,18},{18,2},{3,19},{19,3},{4,20},{20... | collective-permute-start | bytes 983048 | tf_op jit(solution)/shard_map/ppermute | solution.py:22
  19.9 7.3 %collective-permute-start.10 = (bf16[128,1280]{1,0:T(8,128)(2,1)S(1)}, bf16[128,1280]{1,0:T(8,128)(2,1)S(1)}, u32[]{:S(2)}, u32[]{:S(2)}) collective-permute-start(bf16[128,1280]{1,0:T(8,128)(2,1)S(1)} %get-tuple-element.47), channel_id=1, source_target_pairs={{0,16},{16,0},{1,17},{17,1},{2,18},{18,2},{3,19},{19,3},{4,20},{20... | collective-permute-start | bytes 983048 | tf_op jit(solution)/shard_map/ppermute | solution.py:22
  22.5 4.7 %collective-permute-start.11 = (bf16[128,1280]{1,0:T(8,128)(2,1)S(1)}, bf16[128,1280]{1,0:T(8,128)(2,1)S(1)}, u32[]{:S(2)}, u32[]{:S(2)}) collective-permute-start(bf16[128,1280]{1,0:T(8,128)(2,1)S(1)} %get-tuple-element.48), channel_id=1, source_target_pairs={{0,16},{16,0},{1,17},{17,1},{2,18},{18,2},{3,19},{19,3},{4,20},{20... | collective-permute-start | bytes 983048 | tf_op jit(solution)/shard_map/ppermute | solution.py:22
  24.6 4.6 %collective-permute-start.8 = (bf16[16,5120]{1,0:T(8,128)(2,1)S(1)}, bf16[16,5120]{1,0:T(8,128)(2,1)S(1)}, u32[]{:S(2)}, u32[]{:S(2)}) collective-permute-start(bf16[16,5120]{1,0:T(8,128)(2,1)S(1)} %slice.16), channel_id=1, source_target_pairs={{0,1},{1,0},{2,3},{3,2},{4,5},{5,4},{6,7},{7,6},{8,9},{9,8},{10,11... | collective-permute-start | bytes 491528 | tf_op jit(solution)/shard_map/ppermute | solution.py:50
  25.9 4.5 %collective-permute-start.9 = (bf16[16,5120]{1,0:T(8,128)(2,1)S(1)}, bf16[16,5120]{1,0:T(8,128)(2,1)S(1)}, u32[]{:S(2)}, u32[]{:S(2)}) collective-permute-start(bf16[16,5120]{1,0:T(8,128)(2,1)S(1)} %slice.17), channel_id=1, source_target_pairs={{0,2},{1,3},{2,0},{3,1},{4,6},{5,7},{6,4},{7,5},{8,10},{9,11},{10,... | collective-permute-start | bytes 491528 | tf_op jit(solution)/shard_map/ppermute | solution.py:50
  32.5 5.8 %collective-permute-start.12 = (bf16[128,2560]{1,0:T(8,128)(2,1)S(1)}, bf16[128,2560]{1,0:T(8,128)(2,1)S(1)}, u32[]{:S(2)}, u32[]{:S(2)}) collective-permute-start(bf16[128,2560]{1,0:T(8,128)(2,1)S(1)} %get-tuple-element.49.refs_3_), channel_id=1, source_target_pairs={{0,16},{1,17},{2,18},{3,19},{4,20},{5,21},{6,22},{7,23},{8,24},{9,... | collective-permute-start | bytes 1966088 | tf_op jit(solution)/shard_map/ppermute | solution.py:27
  33.8 4.5 %copy-start.3 = (f32[1,5120]{1,0:T(1,128)S(1)}, f32[1,5120]{1,0:T(1,128)}, u32[]{:S(2)}) copy-start(f32[1,5120]{1,0:T(1,128)} %refs_4_.1) | copy-start | bytes 61444
  33.8 30.7 %slice-start = ((s8[6553600]{0:T(1024)(128)(4,1)}), s8[4194304]{0:T(1024)(128)(4,1)S(1)}, s32[]{:S(2)}) async-start(s8[6553600]{0:T(1024)(128)(4,1)} %bitcast.16), calls=%async_computation | async-start | bytes 8388608
  35.8 6.8 %collective-permute-start.17 = (bf16[16,5120]{1,0:T(8,128)(2,1)S(1)}, bf16[16,5120]{1,0:T(8,128)(2,1)S(1)}, u32[]{:S(2)}, u32[]{:S(2)}) collective-permute-start(bf16[16,5120]{1,0:T(8,128)(2,1)S(1)} %get-tuple-element.59), channel_id=1, source_target_pairs={{2,0},{3,1},{0,2},{1,3},{6,4},{7,5},{4,6},{5,7},{10,8},{11,9},{8,1... | collective-permute-start | bytes 491528 | tf_op jit(solution)/shard_map/ppermute | solution.py:50
  38.0 5.9 %collective-permute-start.16 = (bf16[16,5120]{1,0:T(8,128)(2,1)S(1)}, bf16[16,5120]{1,0:T(8,128)(2,1)S(1)}, u32[]{:S(2)}, u32[]{:S(2)}) collective-permute-start(bf16[16,5120]{1,0:T(8,128)(2,1)S(1)} %get-tuple-element.57), channel_id=1, source_target_pairs={{1,0},{0,1},{3,2},{2,3},{5,4},{4,5},{7,6},{6,7},{9,8},{8,9},{11,10... | collective-permute-start | bytes 491528 | tf_op jit(solution)/shard_map/ppermute | solution.py:50
  38.2 26.2 %slice-start.1 = ((s8[6553600]{0:T(1024)(128)(4,1)}), s8[2359296]{0:T(1024)(128)(4,1)S(1)}, s32[]{:S(2)}) async-start(s8[6553600]{0:T(1024)(128)(4,1)} %bitcast.16), calls=%async_computation.1 | async-start | bytes 4718592
  38.2 26.2 %copy-start = (bf16[1,640,5120]{2,1,0:T(8,128)(2,1)S(1)}, bf16[1,640,5120]{2,1,0:T(8,128)(2,1)}, u32[]{:S(2)}) copy-start(bf16[1,640,5120]{2,1,0:T(8,128)(2,1)} %param.15) | copy-start | bytes 19660804
  38.9 5.2 %collective-permute-start.15 = (bf16[8,5120]{1,0:T(8,128)(2,1)S(1)}, bf16[8,5120]{1,0:T(8,128)(2,1)S(1)}, u32[]{:S(2)}, u32[]{:S(2)}) collective-permute-start(bf16[8,5120]{1,0:T(8,128)(2,1)S(1)} %get-tuple-element.55.refs_0_.after_any), channel_id=1, source_target_pairs={{0,12},{1,13},{2,14},{3,15},{4,8},{5,9},{6,10},{7,11},{8,4},{9,5},... | collective-permute-start | bytes 245768 | tf_op jit(solution)/shard_map/ppermute | solution.py:50
  41.3 7.5 %collective-permute-start.14 = (bf16[8,5120]{1,0:T(8,128)(2,1)S(1)}, bf16[8,5120]{1,0:T(8,128)(2,1)S(1)}, u32[]{:S(2)}, u32[]{:S(2)}) collective-permute-start(bf16[8,5120]{1,0:T(8,128)(2,1)S(1)} %get-tuple-element.55.refs_0_.after_any), channel_id=1, source_target_pairs={{0,8},{1,9},{2,10},{3,11},{4,12},{5,13},{6,14},{7,15},{8,0},{9,1},... | collective-permute-start | bytes 245768 | tf_op jit(solution)/shard_map/ppermute | solution.py:50
  41.3 7.5 %collective-permute-start.13 = (bf16[8,5120]{1,0:T(8,128)(2,1)S(1)}, bf16[8,5120]{1,0:T(8,128)(2,1)S(1)}, u32[]{:S(2)}, u32[]{:S(2)}) collective-permute-start(bf16[8,5120]{1,0:T(8,128)(2,1)S(1)} %get-tuple-element.55.refs_0_.after_any), channel_id=1, source_target_pairs={{0,4},{1,5},{2,6},{3,7},{4,0},{5,1},{6,2},{7,3},{8,12},{9,13},{10,... | collective-permute-start | bytes 245768 | tf_op jit(solution)/shard_map/ppermute | solution.py:50
  42.6 7.6 %collective-permute-start.21 = (bf16[32,5120]{1,0:T(8,128)(2,1)S(1)}, bf16[32,5120]{1,0:T(8,128)(2,1)S(1)}, u32[]{:S(2)}, u32[]{:S(2)}) collective-permute-start(bf16[32,5120]{1,0:T(8,128)(2,1)S(1)} %add_half.5.refs_5_), channel_id=1, source_target_pairs={{1,0},{0,1},{3,2},{2,3},{5,4},{4,5},{7,6},{6,7},{9,8},{8,9},{11,10... | collective-permute-start | bytes 983048 | tf_op jit(solution)/shard_map/ppermute | solution.py:50
  44.0 6.3 %collective-permute-start.20 = (bf16[32,5120]{1,0:T(8,128)(2,1)S(1)}, bf16[32,5120]{1,0:T(8,128)(2,1)S(1)}, u32[]{:S(2)}, u32[]{:S(2)}) collective-permute-start(bf16[32,5120]{1,0:T(8,128)(2,1)S(1)} %add_half.4.refs_4_), channel_id=1, source_target_pairs={{2,0},{3,1},{0,2},{1,3},{6,4},{7,5},{4,6},{5,7},{10,8},{11,9},{8,1... | collective-permute-start | bytes 983048 | tf_op jit(solution)/shard_map/ppermute | solution.py:50
  48.9 9.9 %collective-permute-start.19 = (bf16[32,5120]{1,0:T(8,128)(2,1)S(1)}, bf16[32,5120]{1,0:T(8,128)(2,1)S(1)}, u32[]{:S(2)}, u32[]{:S(2)}) collective-permute-start(bf16[32,5120]{1,0:T(8,128)(2,1)S(1)} %join.3.refs_3_.refs_2_), channel_id=1, source_target_pairs={{0,2},{1,3},{2,0},{3,1},{4,6},{5,7},{6,4},{7,5},{8,10},{9,11},{10,... | collective-permute-start | bytes 983048 | tf_op jit(solution)/shard_map/ppermute | solution.py:50
  49.4 9.3 %collective-permute-start.18 = (bf16[32,5120]{1,0:T(8,128)(2,1)S(1)}, bf16[32,5120]{1,0:T(8,128)(2,1)S(1)}, u32[]{:S(2)}, u32[]{:S(2)}) collective-permute-start(bf16[32,5120]{1,0:T(8,128)(2,1)S(1)} %join.3.refs_3_.refs_2_), channel_id=1, source_target_pairs={{0,1},{1,0},{2,3},{3,2},{4,5},{5,4},{6,7},{7,6},{8,9},{9,8},{10,11... | collective-permute-start | bytes 983048 | tf_op jit(solution)/shard_map/ppermute | solution.py:50
  58.7 5.5 %collective-permute-start.22 = (bf16[16,5120]{1,0:T(8,128)(2,1)S(1)}, bf16[16,5120]{1,0:T(8,128)(2,1)S(1)}, u32[]{:S(2)}, u32[]{:S(2)}) collective-permute-start(bf16[16,5120]{1,0:T(8,128)(2,1)S(1)} %get-tuple-element.61), channel_id=1, source_target_pairs={{0,1},{1,0},{2,3},{3,2},{4,5},{5,4},{6,7},{7,6},{8,9},{9,8},{10,11... | collective-permute-start | bytes 491528 | tf_op jit(solution)/shard_map/ppermute | solution.py:50
  60.0 4.5 %collective-permute-start.23 = (bf16[16,5120]{1,0:T(8,128)(2,1)S(1)}, bf16[16,5120]{1,0:T(8,128)(2,1)S(1)}, u32[]{:S(2)}, u32[]{:S(2)}) collective-permute-start(bf16[16,5120]{1,0:T(8,128)(2,1)S(1)} %get-tuple-element.62), channel_id=1, source_target_pairs={{0,2},{1,3},{2,0},{3,1},{4,6},{5,7},{6,4},{7,5},{8,10},{9,11},{10,... | collective-permute-start | bytes 491528 | tf_op jit(solution)/shard_map/ppermute | solution.py:50
  60.0 3.3 %collective-permute-start.24 = (bf16[8,5120]{1,0:T(8,128)(2,1)S(1)}, bf16[8,5120]{1,0:T(8,128)(2,1)S(1)}, u32[]{:S(2)}, u32[]{:S(2)}) collective-permute-start(bf16[8,5120]{1,0:T(8,128)(2,1)S(1)} %get-tuple-element.63), channel_id=1, source_target_pairs={{4,0},{5,1},{6,2},{7,3},{0,4},{1,5},{2,6},{3,7},{12,8},{13,9},{14,... | collective-permute-start | bytes 245768 | tf_op jit(solution)/shard_map/ppermute | solution.py:50
  60.0 4.2 %collective-permute-start.25 = (bf16[8,5120]{1,0:T(8,128)(2,1)S(1)}, bf16[8,5120]{1,0:T(8,128)(2,1)S(1)}, u32[]{:S(2)}, u32[]{:S(2)}) collective-permute-start(bf16[8,5120]{1,0:T(8,128)(2,1)S(1)} %get-tuple-element.64), channel_id=1, source_target_pairs={{8,0},{9,1},{10,2},{11,3},{12,4},{13,5},{14,6},{15,7},{0,8},{1,9},... | collective-permute-start | bytes 245768 | tf_op jit(solution)/shard_map/ppermute | solution.py:50
  66.8 8.1 %collective-permute-start.26 = (bf16[16,5120]{1,0:T(8,128)(2,1)S(1)}, bf16[16,5120]{1,0:T(8,128)(2,1)S(1)}, u32[]{:S(2)}, u32[]{:S(2)}) collective-permute-start(bf16[16,5120]{1,0:T(8,128)(2,1)S(1)} %get-tuple-element.67), channel_id=1, source_target_pairs={{1,0},{0,1},{3,2},{2,3},{5,4},{4,5},{7,6},{6,7},{9,8},{8,9},{11,10... | collective-permute-start | bytes 491528 | tf_op jit(solution)/shard_map/ppermute | solution.py:50
  67.4 8.2 %collective-permute-start.29 = (bf16[16,5120]{1,0:T(8,128)(2,1)S(1)}, bf16[16,5120]{1,0:T(8,128)(2,1)S(1)}, u32[]{:S(2)}, u32[]{:S(2)}) collective-permute-start(bf16[16,5120]{1,0:T(8,128)(2,1)S(1)} %get-tuple-element.71), channel_id=1, source_target_pairs={{2,0},{3,1},{0,2},{1,3},{6,4},{7,5},{4,6},{5,7},{10,8},{11,9},{8,1... | collective-permute-start | bytes 491528 | tf_op jit(solution)/shard_map/ppermute | solution.py:50
  68.4 24.6 %collective-permute-start.35 = (bf16[144,2560]{1,0:T(8,128)(2,1)S(1)}, bf16[144,2560]{1,0:T(8,128)(2,1)S(1)}, u32[]{:S(2)}, u32[]{:S(2)}) collective-permute-start(bf16[144,2560]{1,0:T(8,128)(2,1)S(1)} %get-tuple-element.77), channel_id=1, source_target_pairs={{0,16},{1,17},{2,18},{3,19},{4,20},{5,21},{6,22},{7,23},{8,24},{9,... | collective-permute-start | bytes 2211848 | tf_op jit(solution)/shard_map/ppermute | solution.py:17
  69.6 5.3 %collective-permute-start.27 = (bf16[8,5120]{1,0:T(8,128)(2,1)S(1)}, bf16[8,5120]{1,0:T(8,128)(2,1)S(1)}, u32[]{:S(2)}, u32[]{:S(2)}) collective-permute-start(bf16[8,5120]{1,0:T(8,128)(2,1)S(1)} %get-tuple-element.68), channel_id=1, source_target_pairs={{12,0},{13,1},{14,2},{15,3},{8,4},{9,5},{10,6},{11,7},{4,8},{5,9},... | collective-permute-start | bytes 245768 | tf_op jit(solution)/shard_map/ppermute | solution.py:50
  71.7 21.2 %collective-permute-start.36 = (bf16[128,2560]{1,0:T(8,128)(2,1)S(1)}, bf16[128,2560]{1,0:T(8,128)(2,1)S(1)}, u32[]{:S(2)}, u32[]{:S(2)}) collective-permute-start(bf16[128,2560]{1,0:T(8,128)(2,1)S(1)} %get-tuple-element.78), channel_id=1, source_target_pairs={{0,16},{1,17},{2,18},{3,19},{4,20},{5,21},{6,22},{7,23},{8,24},{9,... | collective-permute-start | bytes 1966088 | tf_op jit(solution)/shard_map/ppermute | solution.py:17
  75.0 6.0 %collective-permute-start.28 = (bf16[32,5120]{1,0:T(8,128)(2,1)S(1)}, bf16[32,5120]{1,0:T(8,128)(2,1)S(1)}, u32[]{:S(2)}, u32[]{:S(2)}) collective-permute-start(bf16[32,5120]{1,0:T(8,128)(2,1)S(1)} %add_half.6), channel_id=1, source_target_pairs={{2,0},{3,1},{0,2},{1,3},{6,4},{7,5},{4,6},{5,7},{10,8},{11,9},{8,1... | collective-permute-start | bytes 983048 | tf_op jit(solution)/shard_map/ppermute | solution.py:50
  75.7 6.0 %collective-permute-start.30 = (bf16[32,5120]{1,0:T(8,128)(2,1)S(1)}, bf16[32,5120]{1,0:T(8,128)(2,1)S(1)}, u32[]{:S(2)}, u32[]{:S(2)}) collective-permute-start(bf16[32,5120]{1,0:T(8,128)(2,1)S(1)} %add_half.7), channel_id=1, source_target_pairs={{1,0},{0,1},{3,2},{2,3},{5,4},{4,5},{7,6},{6,7},{9,8},{8,9},{11,10... | collective-permute-start | bytes 983048 | tf_op jit(solution)/shard_map/ppermute | solution.py:50
  76.6 8.4 %collective-permute-start.34 = (f32[8,5120]{1,0:T(8,128)S(1)}, f32[8,5120]{1,0:T(8,128)S(1)}, u32[]{:S(2)}, u32[]{:S(2)}) collective-permute-start(f32[8,5120]{1,0:T(8,128)S(1)} %add_last.2.refs_2_.second_ref), channel_id=1, source_target_pairs={{0,16},{1,17},{2,18},{3,19},{4,20},{5,21},{6,22},{7,23},{8,24},{9,... | collective-permute-start | bytes 491528 | tf_op jit(solution)/shard_map/ppermute | solution.py:27
  81.7 6.2 %collective-permute-start.31 = (bf16[8,5120]{1,0:T(8,128)(2,1)S(1)}, bf16[8,5120]{1,0:T(8,128)(2,1)S(1)}, u32[]{:S(2)}, u32[]{:S(2)}) collective-permute-start(bf16[8,5120]{1,0:T(8,128)(2,1)S(1)} %get-tuple-element.73), channel_id=1, source_target_pairs={{4,0},{5,1},{6,2},{7,3},{0,4},{1,5},{2,6},{3,7},{12,8},{13,9},{14,... | collective-permute-start | bytes 245768 | tf_op jit(solution)/shard_map/ppermute | solution.py:50
  82.2 5.7 %collective-permute-start.32 = (bf16[8,5120]{1,0:T(8,128)(2,1)S(1)}, bf16[8,5120]{1,0:T(8,128)(2,1)S(1)}, u32[]{:S(2)}, u32[]{:S(2)}) collective-permute-start(bf16[8,5120]{1,0:T(8,128)(2,1)S(1)} %get-tuple-element.74), channel_id=1, source_target_pairs={{8,0},{9,1},{10,2},{11,3},{12,4},{13,5},{14,6},{15,7},{0,8},{1,9},... | collective-permute-start | bytes 245768 | tf_op jit(solution)/shard_map/ppermute | solution.py:50
  85.0 5.1 %collective-permute-start.33 = (bf16[8,5120]{1,0:T(8,128)(2,1)S(1)}, bf16[8,5120]{1,0:T(8,128)(2,1)S(1)}, u32[]{:S(2)}, u32[]{:S(2)}) collective-permute-start(bf16[8,5120]{1,0:T(8,128)(2,1)S(1)} %get-tuple-element.75), channel_id=1, source_target_pairs={{12,0},{13,1},{14,2},{15,3},{8,4},{9,5},{10,6},{11,7},{4,8},{5,9},... | collective-permute-start | bytes 245768 | tf_op jit(solution)/shard_map/ppermute | solution.py:50
  90.1 10.5 %collective-permute-start.37 = (f32[8,5120]{1,0:T(8,128)S(1)}, f32[8,5120]{1,0:T(8,128)S(1)}, u32[]{:S(2)}, u32[]{:S(2)}) collective-permute-start(f32[8,5120]{1,0:T(8,128)S(1)} %add_last.3.refs_1_), channel_id=1, source_target_pairs={{0,16},{1,17},{2,18},{3,19},{4,20},{5,21},{6,22},{7,23},{8,24},{9,... | collective-permute-start | bytes 491528 | tf_op jit(solution)/shard_map/ppermute | solution.py:17

commit v6 on v5

--- a/solution.py
+++ b/solution.py
@@ -633,9 +633,9 @@
     )
     total_grad = grads.send([computed[0]])
     room, made = blank(section, capacity, residual)
-    results = grid.scatter(computed, CAP, [total_grad, made])
+    results = grid.scatter(computed, CAP)
     next(results)
-    results.send([])
+    results.send([total_grad, made])
     total_grad, laid = lay_out(section, sections, to_decoder(total_grad), total_grad)
     returned = results.send([laid])
     returned_before = passed_along(returned, "section", 1)

time: 102 us -> 103 us (level)
    ppermute x2, waiting for transfers between devices: 1.29 us -> 7.44 us  [to_decoder(): lax.ppermute(block, 'section', [(i, i + apart) for i in range(apart)])]
    ppermute x3, waiting for transfers between devices: 7.65 us -> 3.82 us  [passed_along(): return lax.ppermute(block, axis, route)]
    ppermute x28, waiting for transfers between devices: 34.8 us -> 32.7 us  [shift(): return lax.ppermute(block, 'expert', route)]
  transfers between devices with their start and end apart: 38 -> 38, of which waited for: 17 -> 16; matrix products, arithmetic and copies ran while one was open for 0% -> 0% of each run, Pallas kernels for 6% -> 6%
where the time goes in v6:
time: 103 us
  waiting for transfers between devices  45.2 us (44%)
  starting transfers between devices  42.8 us (42%)
  Pallas kernels  12.4 us (12%)
  local copies, waits for them, and re-layouts  1.24 us (1%)
    ppermute x28, waiting for transfers between devices, shift(): return lax.ppermute(block, 'expert', route)  32.7 us
    ppermute x28, starting transfers between devices, shift(): return lax.ppermute(block, 'expert', route)  31.7 us
    pallas_call x18, Pallas kernels, local_kernel(): pl.pallas_call(body, out_shape=tuple(outs), in_specs=in_specs, out_specs=...  9.39 us
    ppermute x2, waiting for transfers between devices, to_decoder(): lax.ppermute(block, 'section', [(i, i + apart) for i in range(apart)])  7.44 us
    ppermute x5, starting transfers between devices, swapped(): lax.ppermute(block, 'section', [(i, (i + sections // 2) % sections) for i...  4.61 us
    ppermute x3, starting transfers between devices, passed_along(): return lax.ppermute(block, axis, route)  3.86 us
    ppermute x3, waiting for transfers between devices, passed_along(): return lax.ppermute(block, axis, route)  3.82 us
    pallas_call x2, Pallas kernels, finish(): pl.pallas_call(kernel, out_shape=one, in_specs=[pl.BlockSpec(memory_space...  3.03 us
  transfers between devices with their start and end apart: 38, of which 16 were waited for; matrix products, arithmetic and copies ran while one was open for 0% of the time, Pallas kernels for 6%

profile of v6, /device:TPU:1, one launch (start us, length us, event | category | flops | bytes accessed | tf_op | source)
XLA Modules:
  0.0 102.6 jit_solution(13863559144804790156)
XLA Ops:
  0.7 1.1 %slice_bitcast_fusion = (bf16[1,8,2,2560]{3,2,1,0:T(2,128)(2,1)S(1)}, bf16[1,8,2,2560]{3,2,1,0:T(2,128)(2,1)S(1)}) fusion(bf16[1,8,2,5120]{3,2,1,0:T(2,128)(2,1)} %param.10), kind=kLoop, calls=%fused_computation | loop fusion | bytes 327680
  1.8 0.1 collective-permute-start
  2.0 1.2 %collective-permute-done = bf16[8,5120]{1,0:T(8,128)(2,1)S(1)} collective-permute-done((bf16[8,5120]{1,0:T(8,128)(2,1)S(1)}, bf16[8,5120]{1,0:T(8,128)(2,1)S(1)}, u32[]{:S(2)}, u32[]{:S(2)}) %collective-permute-start) | collective-permute-done | bytes 81952 | tf_op jit(solution)/shard_map/ppermute | solution.py:22
  3.2 4.5 %collective-permute-start.3 = (bf16[8,5120]{1,0:T(8,128)(2,1)S(1)}, bf16[8,5120]{1,0:T(8,128)(2,1)S(1)}, u32[]{:S(2)}, u32[]{:S(2)}) collective-permute-start(bf16[8,5120]{1,0:T(8,128)(2,1)S(1)} %broadcast_select_fusion.refs_0_), channel_id=1, source_target_pairs={{0,12},{1,13},{2,14},{3,15},{4,8},{5,9},{6,10},{7,11},{8,4},{9,5},... | collective-permute-start | bytes 245768 | tf_op jit(solution)/shard_map/ppermute | solution.py:50
  7.7 0.4 collective-permute-start.1
  8.1 2.2 %collective-permute-done.3.refs_3_ = bf16[8,5120]{1,0:T(8,128)(2,1)S(1)} collective-permute-done((bf16[8,5120]{1,0:T(8,128)(2,1)S(1)}, bf16[8,5120]{1,0:T(8,128)(2,1)S(1)}, u32[]{:S(2)}, u32[]{:S(2)}) %collective-permute-start.3) | collective-permute-done | bytes 81952 | tf_op jit(solution)/shard_map/ppermute | solution.py:50
  10.3 4.1 %collective-permute-done.2.refs_2_ = bf16[8,5120]{1,0:T(8,128)(2,1)S(1)} collective-permute-done((bf16[8,5120]{1,0:T(8,128)(2,1)S(1)}, bf16[8,5120]{1,0:T(8,128)(2,1)S(1)}, u32[]{:S(2)}, u32[]{:S(2)}) %collective-permute-start.2) | collective-permute-done | bytes 81952 | tf_op jit(solution)/shard_map/ppermute | solution.py:50
  14.4 1.3 %collective-permute-start.7 = (bf16[32,5120]{1,0:T(8,128)(2,1)S(1)}, bf16[32,5120]{1,0:T(8,128)(2,1)S(1)}, u32[]{:S(2)}, u32[]{:S(2)}) collective-permute-start(bf16[32,5120]{1,0:T(8,128)(2,1)S(1)} %join.2.refs_4_), channel_id=1, source_target_pairs={{0,2},{1,3},{2,0},{3,1},{4,6},{5,7},{6,4},{7,5},{8,10},{9,11},{10,... | collective-permute-start | bytes 983048 | tf_op jit(solution)/shard_map/ppermute | solution.py:50
  15.7 1.2 %collective-permute-start.6 = (bf16[32,5120]{1,0:T(8,128)(2,1)S(1)}, bf16[32,5120]{1,0:T(8,128)(2,1)S(1)}, u32[]{:S(2)}, u32[]{:S(2)}) collective-permute-start(bf16[32,5120]{1,0:T(8,128)(2,1)S(1)} %join.2.refs_4_), channel_id=1, source_target_pairs={{0,1},{1,0},{2,3},{3,2},{4,5},{5,4},{6,7},{7,6},{8,9},{9,8},{10,11... | collective-permute-start | bytes 983048 | tf_op jit(solution)/shard_map/ppermute | solution.py:50
  16.9 1.0 queries.1
  17.9 1.8 %collective-permute-start.4 = (bf16[128,1280]{1,0:T(8,128)(2,1)S(1)}, bf16[128,1280]{1,0:T(8,128)(2,1)S(1)}, u32[]{:S(2)}, u32[]{:S(2)}) collective-permute-start(bf16[128,1280]{1,0:T(8,128)(2,1)S(1)} %get-tuple-element.43), channel_id=1, source_target_pairs={{0,16},{16,0},{1,17},{17,1},{2,18},{18,2},{3,19},{19,3},{4,20},{20... | collective-permute-start | bytes 983048 | tf_op jit(solution)/shard_map/ppermute | solution.py:22
  19.7 0.1 collective-permute-start.5
  19.8 0.1 cut.1
  19.9 0.5 collective-permute-start.10
  20.4 2.1 %collective-permute-done.7.refs_6_ = bf16[32,5120]{1,0:T(8,128)(2,1)S(1)} collective-permute-done((bf16[32,5120]{1,0:T(8,128)(2,1)S(1)}, bf16[32,5120]{1,0:T(8,128)(2,1)S(1)}, u32[]{:S(2)}, u32[]{:S(2)}) %collective-permute-start.7) | collective-permute-done | bytes 327712 | tf_op jit(solution)/shard_map/ppermute | solution.py:50
  22.5 2.1 %collective-permute-start.11 = (bf16[128,1280]{1,0:T(8,128)(2,1)S(1)}, bf16[128,1280]{1,0:T(8,128)(2,1)S(1)}, u32[]{:S(2)}, u32[]{:S(2)}) collective-permute-start(bf16[128,1280]{1,0:T(8,128)(2,1)S(1)} %get-tuple-element.48), channel_id=1, source_target_pairs={{0,16},{16,0},{1,17},{17,1},{2,18},{18,2},{3,19},{19,3},{4,20},{20... | collective-permute-start | bytes 983048 | tf_op jit(solution)/shard_map/ppermute | solution.py:22
  24.6 1.3 %collective-permute-start.8 = (bf16[16,5120]{1,0:T(8,128)(2,1)S(1)}, bf16[16,5120]{1,0:T(8,128)(2,1)S(1)}, u32[]{:S(2)}, u32[]{:S(2)}) collective-permute-start(bf16[16,5120]{1,0:T(8,128)(2,1)S(1)} %slice.16), channel_id=1, source_target_pairs={{0,1},{1,0},{2,3},{3,2},{4,5},{5,4},{6,7},{7,6},{8,9},{9,8},{10,11... | collective-permute-start | bytes 491528 | tf_op jit(solution)/shard_map/ppermute | solution.py:50
  25.9 1.3 %collective-permute-start.9 = (bf16[16,5120]{1,0:T(8,128)(2,1)S(1)}, bf16[16,5120]{1,0:T(8,128)(2,1)S(1)}, u32[]{:S(2)}, u32[]{:S(2)}) collective-permute-start(bf16[16,5120]{1,0:T(8,128)(2,1)S(1)} %slice.17), channel_id=1, source_target_pairs={{0,2},{1,3},{2,0},{3,1},{4,6},{5,7},{6,4},{7,5},{8,10},{9,11},{10,... | collective-permute-start | bytes 491528 | tf_op jit(solution)/shard_map/ppermute | solution.py:50
  27.2 2.0 %collective-permute-done.8.refs_7_ = bf16[16,5120]{1,0:T(8,128)(2,1)S(1)} collective-permute-done((bf16[16,5120]{1,0:T(8,128)(2,1)S(1)}, bf16[16,5120]{1,0:T(8,128)(2,1)S(1)}, u32[]{:S(2)}, u32[]{:S(2)}) %collective-permute-start.8) | collective-permute-done | bytes 163872 | tf_op jit(solution)/shard_map/ppermute | solution.py:50
  29.2 1.2 %collective-permute-done.9.refs_8_ = bf16[16,5120]{1,0:T(8,128)(2,1)S(1)} collective-permute-done((bf16[16,5120]{1,0:T(8,128)(2,1)S(1)}, bf16[16,5120]{1,0:T(8,128)(2,1)S(1)}, u32[]{:S(2)}, u32[]{:S(2)}) %collective-permute-start.9) | collective-permute-done | bytes 163872 | tf_op jit(solution)/shard_map/ppermute | solution.py:50
  30.4 2.0 %attend.1 = (bf16[128,2560]{1,0:T(8,128)(2,1)S(1)}, f32[20,128,128]{2,1,0:T(8,128)S(1)}, bf16[128,2560]{1,0:T(8,128)(2,1)S(1)}) custom-call(s32[1]{0:T(128)} %bitcast.refs_0_.section, bf16[128,1280]{1,0:T(8,128)(2,1)S(1)} %collective-permute-done.4.refs_1_, bf16[128,1280]{1,0:T(8,128)(2,1)S(1)} %collective-permute-done.5.refs_2_, ...), custom_call_target="tpu_custom_call" | custom-call | flops 167772160 | bytes 5242884 | tf_op jit(solution)/shard_map/attend/pallas_call | solution.py:142
  32.5 1.3 %collective-permute-start.12 = (bf16[128,2560]{1,0:T(8,128)(2,1)S(1)}, bf16[128,2560]{1,0:T(8,128)(2,1)S(1)}, u32[]{:S(2)}, u32[]{:S(2)}) collective-permute-start(bf16[128,2560]{1,0:T(8,128)(2,1)S(1)} %get-tuple-element.49.refs_3_), channel_id=1, source_target_pairs={{0,16},{1,17},{2,18},{3,19},{4,20},{5,21},{6,22},{7,23},{8,24},{9,... | collective-permute-start | bytes 1966088 | tf_op jit(solution)/shard_map/ppermute | solution.py:27
  33.8 2.0 %gradient.1 = (f32[32,5120]{1,0:T(8,128)S(1)}, f32[32,5120]{1,0:T(8,128)S(1)}, f32[32,5120]{1,0:T(8,128)S(1)}, bf16[16,5120]{1,0:T(8,128)(2,1)S(1)}, bf16[16,5120]{1,0:T(8,128)(2,1)S(1)}) custom-call(s32[1]{0:T(128)} %bitcast.refs_0_.section, bf16[128,2560]{1,0:T(8,128)(2,1)S(1)} %get-tuple-element.50.q_ref, ...), custom_call_target="tpu_custom_call" | custom-call | flops 419430400 | bytes 6881284 | tf_op jit(solution)/shard_map/gradient/pallas_call | solution.py:142
  35.8 2.2 %collective-permute-start.17 = (bf16[16,5120]{1,0:T(8,128)(2,1)S(1)}, bf16[16,5120]{1,0:T(8,128)(2,1)S(1)}, u32[]{:S(2)}, u32[]{:S(2)}) collective-permute-start(bf16[16,5120]{1,0:T(8,128)(2,1)S(1)} %get-tuple-element.59), channel_id=1, source_target_pairs={{2,0},{3,1},{0,2},{1,3},{6,4},{7,5},{4,6},{5,7},{10,8},{11,9},{8,1... | collective-permute-start | bytes 491528 | tf_op jit(solution)/shard_map/ppermute | solution.py:50
  38.0 0.3 collective-permute-start.16
  38.3 0.7 settle.1
  38.9 2.4 %collective-permute-start.15 = (bf16[8,5120]{1,0:T(8,128)(2,1)S(1)}, bf16[8,5120]{1,0:T(8,128)(2,1)S(1)}, u32[]{:S(2)}, u32[]{:S(2)}) collective-permute-start(bf16[8,5120]{1,0:T(8,128)(2,1)S(1)} %get-tuple-element.55.refs_0_.after_any), channel_id=1, source_target_pairs={{0,12},{1,13},{2,14},{3,15},{4,8},{5,9},{6,10},{7,11},{8,4},{9,5},... | collective-permute-start | bytes 245768 | tf_op jit(solution)/shard_map/ppermute | solution.py:50
  41.3 1.2 %collective-permute-start.13 = (bf16[8,5120]{1,0:T(8,128)(2,1)S(1)}, bf16[8,5120]{1,0:T(8,128)(2,1)S(1)}, u32[]{:S(2)}, u32[]{:S(2)}) collective-permute-start(bf16[8,5120]{1,0:T(8,128)(2,1)S(1)} %get-tuple-element.55.refs_0_.after_any), channel_id=1, source_target_pairs={{0,4},{1,5},{2,6},{3,7},{4,0},{5,1},{6,2},{7,3},{8,12},{9,13},{10,... | collective-permute-start | bytes 245768 | tf_op jit(solution)/shard_map/ppermute | solution.py:50
  42.6 0.1 add_half.5.refs_5_
  42.6 1.3 %collective-permute-start.21 = (bf16[32,5120]{1,0:T(8,128)(2,1)S(1)}, bf16[32,5120]{1,0:T(8,128)(2,1)S(1)}, u32[]{:S(2)}, u32[]{:S(2)}) collective-permute-start(bf16[32,5120]{1,0:T(8,128)(2,1)S(1)} %add_half.5.refs_5_), channel_id=1, source_target_pairs={{1,0},{0,1},{3,2},{2,3},{5,4},{4,5},{7,6},{6,7},{9,8},{8,9},{11,10... | collective-permute-start | bytes 983048 | tf_op jit(solution)/shard_map/ppermute | solution.py:50
  44.0 0.1 collective-permute-start.20
  44.1 0.0 collective-permute-done.15.refs_3_
  44.1 4.7 %collective-permute-done.14.refs_2_ = bf16[8,5120]{1,0:T(8,128)(2,1)S(1)} collective-permute-done((bf16[8,5120]{1,0:T(8,128)(2,1)S(1)}, bf16[8,5120]{1,0:T(8,128)(2,1)S(1)}, u32[]{:S(2)}, u32[]{:S(2)}) %collective-permute-start.14) | collective-permute-done | bytes 81952 | tf_op jit(solution)/shard_map/ppermute | solution.py:50
  48.9 0.6 collective-permute-start.19
  49.4 0.8 collective-permute-start.18
  50.2 0.1 add_blocks.2
  50.4 8.4 %collective-permute-done.19.refs_0_.refs_4_ = bf16[32,5120]{1,0:T(8,128)(2,1)S(1)} collective-permute-done((bf16[32,5120]{1,0:T(8,128)(2,1)S(1)}, bf16[32,5120]{1,0:T(8,128)(2,1)S(1)}, u32[]{:S(2)}, u32[]{:S(2)}) %collective-permute-start.19) | collective-permute-done | bytes 327712 | tf_op jit(solution)/shard_map/ppermute | solution.py:50
  58.7 1.3 %collective-permute-start.22 = (bf16[16,5120]{1,0:T(8,128)(2,1)S(1)}, bf16[16,5120]{1,0:T(8,128)(2,1)S(1)}, u32[]{:S(2)}, u32[]{:S(2)}) collective-permute-start(bf16[16,5120]{1,0:T(8,128)(2,1)S(1)} %get-tuple-element.61), channel_id=1, source_target_pairs={{0,1},{1,0},{2,3},{3,2},{4,5},{5,4},{6,7},{7,6},{8,9},{9,8},{10,11... | collective-permute-start | bytes 491528 | tf_op jit(solution)/shard_map/ppermute | solution.py:50
  60.0 2.1 %collective-permute-start.25 = (bf16[8,5120]{1,0:T(8,128)(2,1)S(1)}, bf16[8,5120]{1,0:T(8,128)(2,1)S(1)}, u32[]{:S(2)}, u32[]{:S(2)}) collective-permute-start(bf16[8,5120]{1,0:T(8,128)(2,1)S(1)} %get-tuple-element.64), channel_id=1, source_target_pairs={{8,0},{9,1},{10,2},{11,3},{12,4},{13,5},{14,6},{15,7},{0,8},{1,9},... | collective-permute-start | bytes 245768 | tf_op jit(solution)/shard_map/ppermute | solution.py:50
  62.2 1.2 %collective-permute-done.24.refs_7_.refs_1_ = bf16[8,5120]{1,0:T(8,128)(2,1)S(1)} collective-permute-done((bf16[8,5120]{1,0:T(8,128)(2,1)S(1)}, bf16[8,5120]{1,0:T(8,128)(2,1)S(1)}, u32[]{:S(2)}, u32[]{:S(2)}) %collective-permute-start.24) | collective-permute-done | bytes 81952 | tf_op jit(solution)/shard_map/ppermute | solution.py:50
  63.3 0.9 collective-permute-done.25.refs_8_.refs_2_
  64.2 0.3 collective-permute-done.23.refs_6_
  64.5 2.3 %expert.1 = (f32[32,5120]{1,0:T(8,128)S(1)}, f32[32,5120]{1,0:T(8,128)S(1)}, f32[32,5120]{1,0:T(8,128)S(1)}, bf16[16,5120]{1,0:T(8,128)(2,1)S(1)}, bf16[16,5120]{1,0:T(8,128)(2,1)S(1)}) custom-call(bf16[5120,640]{1,0:T(8,128)(2,1)S(1)} %bitcast.18, bf16[640,5120]{1,0:T(8,128)(2,1)S(1)} %bitcast.19, bf16[32,5120]{1,0:T(8,128)(2,1)S(1)} %join.3.refs_3_.refs_2_, ...), custom_call_target="tpu_custom_call" | custom-call | flops 1677721600 | bytes 16711680 | tf_op jit(solution)/shard_map/expert/pallas_call | solution.py:142
  66.8 1.3 %collective-permute-start.28 = (bf16[16,5120]{1,0:T(8,128)(2,1)S(1)}, bf16[16,5120]{1,0:T(8,128)(2,1)S(1)}, u32[]{:S(2)}, u32[]{:S(2)}) collective-permute-start(bf16[16,5120]{1,0:T(8,128)(2,1)S(1)} %get-tuple-element.69), channel_id=1, source_target_pairs={{2,0},{3,1},{0,2},{1,3},{6,4},{7,5},{4,6},{5,7},{10,8},{11,9},{8,1... | collective-permute-start | bytes 491528 | tf_op jit(solution)/shard_map/ppermute | solution.py:50
  68.1 0.2 collective-permute-start.26
  68.4 1.3 %collective-permute-start.35 = (bf16[144,2560]{1,0:T(8,128)(2,1)S(1)}, bf16[144,2560]{1,0:T(8,128)(2,1)S(1)}, u32[]{:S(2)}, u32[]{:S(2)}) collective-permute-start(bf16[144,2560]{1,0:T(8,128)(2,1)S(1)} %get-tuple-element.77), channel_id=1, source_target_pairs={{0,16},{1,17},{2,18},{3,19},{4,20},{5,21},{6,22},{7,23},{8,24},{9,... | collective-permute-start | bytes 2211848 | tf_op jit(solution)/shard_map/ppermute | solution.py:17
  69.6 1.3 %collective-permute-start.36 = (bf16[128,2560]{1,0:T(8,128)(2,1)S(1)}, bf16[128,2560]{1,0:T(8,128)(2,1)S(1)}, u32[]{:S(2)}, u32[]{:S(2)}) collective-permute-start(bf16[128,2560]{1,0:T(8,128)(2,1)S(1)} %get-tuple-element.78), channel_id=1, source_target_pairs={{0,16},{1,17},{2,18},{3,19},{4,20},{5,21},{6,22},{7,23},{8,24},{9,... | collective-permute-start | bytes 1966088 | tf_op jit(solution)/shard_map/ppermute | solution.py:17
  70.9 0.1 collective-permute-done.28.refs_0_
  71.1 1.2 %collective-permute-start.29 = (bf16[32,5120]{1,0:T(8,128)(2,1)S(1)}, bf16[32,5120]{1,0:T(8,128)(2,1)S(1)}, u32[]{:S(2)}, u32[]{:S(2)}) collective-permute-start(bf16[32,5120]{1,0:T(8,128)(2,1)S(1)} %add_half.7), channel_id=1, source_target_pairs={{1,0},{0,1},{3,2},{2,3},{5,4},{4,5},{7,6},{6,7},{9,8},{8,9},{11,10... | collective-permute-start | bytes 983048 | tf_op jit(solution)/shard_map/ppermute | solution.py:50
  72.3 0.4 collective-permute-start.27
  72.8 2.0 %collective-permute-start.30 = (bf16[8,5120]{1,0:T(8,128)(2,1)S(1)}, bf16[8,5120]{1,0:T(8,128)(2,1)S(1)}, u32[]{:S(2)}, u32[]{:S(2)}) collective-permute-start(bf16[8,5120]{1,0:T(8,128)(2,1)S(1)} %get-tuple-element.70), channel_id=1, source_target_pairs={{12,0},{13,1},{14,2},{15,3},{8,4},{9,5},{10,6},{11,7},{4,8},{5,9},... | collective-permute-start | bytes 245768 | tf_op jit(solution)/shard_map/ppermute | solution.py:50
  74.8 3.2 %collective-permute-done.30.refs_3_ = bf16[8,5120]{1,0:T(8,128)(2,1)S(1)} collective-permute-done((bf16[8,5120]{1,0:T(8,128)(2,1)S(1)}, bf16[8,5120]{1,0:T(8,128)(2,1)S(1)}, u32[]{:S(2)}, u32[]{:S(2)}) %collective-permute-start.30) | collective-permute-done | bytes 81952 | tf_op jit(solution)/shard_map/ppermute | solution.py:50
  78.0 1.3 %collective-permute-start.34 = (f32[8,5120]{1,0:T(8,128)S(1)}, f32[8,5120]{1,0:T(8,128)S(1)}, u32[]{:S(2)}, u32[]{:S(2)}) collective-permute-start(f32[8,5120]{1,0:T(8,128)S(1)} %add_last.2.refs_3_.second_ref), channel_id=1, source_target_pairs={{0,16},{1,17},{2,18},{3,19},{4,20},{5,21},{6,22},{7,23},{8,24},{9,... | collective-permute-start | bytes 491528 | tf_op jit(solution)/shard_map/ppermute | solution.py:27
  79.3 0.1 add_blocks.3
  79.5 0.9 collective-permute-start.31
  80.4 1.4 %collective-permute-start.32 = (bf16[8,5120]{1,0:T(8,128)(2,1)S(1)}, bf16[8,5120]{1,0:T(8,128)(2,1)S(1)}, u32[]{:S(2)}, u32[]{:S(2)}) collective-permute-start(bf16[8,5120]{1,0:T(8,128)(2,1)S(1)} %get-tuple-element.74), channel_id=1, source_target_pairs={{8,0},{9,1},{10,2},{11,3},{12,4},{13,5},{14,6},{15,7},{0,8},{1,9},... | collective-permute-start | bytes 245768 | tf_op jit(solution)/shard_map/ppermute | solution.py:50
  81.8 7.4 %collective-permute-done.34.first_ref = f32[8,5120]{1,0:T(8,128)S(1)} collective-permute-done((f32[8,5120]{1,0:T(8,128)S(1)}, f32[8,5120]{1,0:T(8,128)S(1)}, u32[]{:S(2)}, u32[]{:S(2)}) %collective-permute-start.34) | collective-permute-done | bytes 163872 | tf_op jit(solution)/shard_map/ppermute | solution.py:27
  89.3 1.9 %collective-permute-start.33 = (bf16[8,5120]{1,0:T(8,128)(2,1)S(1)}, bf16[8,5120]{1,0:T(8,128)(2,1)S(1)}, u32[]{:S(2)}, u32[]{:S(2)}) collective-permute-start(bf16[8,5120]{1,0:T(8,128)(2,1)S(1)} %get-tuple-element.75), channel_id=1, source_target_pairs={{12,0},{13,1},{14,2},{15,3},{8,4},{9,5},{10,6},{11,7},{4,8},{5,9},... | collective-permute-start | bytes 245768 | tf_op jit(solution)/shard_map/ppermute | solution.py:50
  91.2 0.8 lay_out.1
  92.0 2.4 %collective-permute-done.33.refs_3_ = bf16[8,5120]{1,0:T(8,128)(2,1)S(1)} collective-permute-done((bf16[8,5120]{1,0:T(8,128)(2,1)S(1)}, bf16[8,5120]{1,0:T(8,128)(2,1)S(1)}, u32[]{:S(2)}, u32[]{:S(2)}) %collective-permute-start.33) | collective-permute-done | bytes 81952 | tf_op jit(solution)/shard_map/ppermute | solution.py:50
  94.4 1.3 %collective-permute-start.37 = (f32[8,5120]{1,0:T(8,128)S(1)}, f32[8,5120]{1,0:T(8,128)S(1)}, u32[]{:S(2)}, u32[]{:S(2)}) collective-permute-start(f32[8,5120]{1,0:T(8,128)S(1)} %add_last.3.refs_1_), channel_id=1, source_target_pairs={{0,16},{1,17},{2,18},{3,19},{4,20},{5,21},{6,22},{7,23},{8,24},{9,... | collective-permute-start | bytes 491528 | tf_op jit(solution)/shard_map/ppermute | solution.py:17
  95.7 1.5 %finish.2 = bf16[128,5120]{1,0:T(8,128)(2,1)} custom-call(s32[1]{0:T(128)} %bitcast.refs_0_.section, bf16[128,5120]{1,0:T(8,128)(2,1)S(1)} %get-tuple-element.54.refs_0_, f32[8,5120]{1,0:T(8,128)S(1)} %add_last.3.refs_1_, f32[2,128]{1,0:T(2,128)S(1)} %get-tuple-element.46.refs_1_.refs_5_.refs_2_), custom_call_target="tpu_custom_call" | custom-call | flops 32768000 | bytes 3276800 | tf_op jit(solution)/shard_map/finish/pallas_call | solution.py:558
  97.3 3.8 %collective-permute-done.37.refs_2_ = f32[8,5120]{1,0:T(8,128)S(1)} collective-permute-done((f32[8,5120]{1,0:T(8,128)S(1)}, f32[8,5120]{1,0:T(8,128)S(1)}, u32[]{:S(2)}, u32[]{:S(2)}) %collective-permute-start.37) | collective-permute-done | bytes 163872 | tf_op jit(solution)/shard_map/ppermute | solution.py:17
  101.1 1.5 %finish.3 = bf16[128,5120]{1,0:T(8,128)(2,1)} custom-call(s32[1]{0:T(128)} %bitcast.refs_0_.section, bf16[144,2560]{1,0:T(8,128)(2,1)S(1)} %collective-permute-done.35.refs_0_, bf16[128,2560]{1,0:T(8,128)(2,1)S(1)} %collective-permute-done.36.refs_1_, f32[8,5120]{1,0:T(8,128)S(1)} %collective-permute-done.37.refs_2_, ...), custom_call_target="tpu_custom_call", output_to_operand_aliasing={{}: (4, {})} | custom-call | flops 32768000 | bytes 3276800 | tf_op jit(solution)/shard_map/finish/pallas_call | solution.py:558
  (58 shorter events, 0.5 us)
Async XLA Ops:
  0.6 16.3 %copy-start.5 = (f32[1,128]{1,0:T(1,128)S(1)}, f32[1,128]{1,0:T(1,128)}, u32[]{:S(2)}) copy-start(f32[1,128]{1,0:T(1,128)} %refs_2_.1) | copy-start | bytes 1540
  0.6 16.3 %copy-start.6 = (s32[1,128]{1,0:T(1,128)S(1)}, s32[1,128]{1,0:T(1,128)}, u32[]{:S(2)}) copy-start(s32[1,128]{1,0:T(1,128)} %refs_3_.1) | copy-start | bytes 1540
  0.7 16.3 %copy-start.4 = (f32[1,5120]{1,0:T(1,128)S(1)}, f32[1,5120]{1,0:T(1,128)}, u32[]{:S(2)}) copy-start(f32[1,5120]{1,0:T(1,128)} %refs_1_.1) | copy-start | bytes 61444
  0.7 16.3 %copy-start.1 = (bf16[1,128,5120]{2,1,0:T(8,128)(2,1)S(1)}, bf16[1,128,5120]{2,1,0:T(8,128)(2,1)}, u32[]{:S(2)}) copy-start(bf16[1,128,5120]{2,1,0:T(8,128)(2,1)} %param.9) | copy-start | bytes 3932164
  1.8 1.3 %collective-permute-start = (bf16[8,5120]{1,0:T(8,128)(2,1)S(1)}, bf16[8,5120]{1,0:T(8,128)(2,1)S(1)}, u32[]{:S(2)}, u32[]{:S(2)}) collective-permute-start(bf16[8,5120]{1,0:T(8,128)(2,1)S(1)} %bitcast.25), channel_id=1, source_target_pairs={{0,16},{16,0},{1,17},{17,1},{2,18},{18,2},{3,19},{19,3},{4,20},{20... | collective-permute-start | bytes 245768 | tf_op jit(solution)/shard_map/ppermute | solution.py:22
  2.0 17.8 %copy-start.2 = (bf16[1,128,5120]{2,1,0:T(8,128)(2,1)S(1)}, bf16[1,128,5120]{2,1,0:T(8,128)(2,1)}, u32[]{:S(2)}) copy-start(bf16[1,128,5120]{2,1,0:T(8,128)(2,1)} %param.11) | copy-start | bytes 3932164
  3.2 7.1 %collective-permute-start.3 = (bf16[8,5120]{1,0:T(8,128)(2,1)S(1)}, bf16[8,5120]{1,0:T(8,128)(2,1)S(1)}, u32[]{:S(2)}, u32[]{:S(2)}) collective-permute-start(bf16[8,5120]{1,0:T(8,128)(2,1)S(1)} %broadcast_select_fusion.refs_0_), channel_id=1, source_target_pairs={{0,12},{1,13},{2,14},{3,15},{4,8},{5,9},{6,10},{7,11},{8,4},{9,5},... | collective-permute-start | bytes 245768 | tf_op jit(solution)/shard_map/ppermute | solution.py:50
  7.7 6.6 %collective-permute-start.2 = (bf16[8,5120]{1,0:T(8,128)(2,1)S(1)}, bf16[8,5120]{1,0:T(8,128)(2,1)S(1)}, u32[]{:S(2)}, u32[]{:S(2)}) collective-permute-start(bf16[8,5120]{1,0:T(8,128)(2,1)S(1)} %broadcast_select_fusion.refs_0_), channel_id=1, source_target_pairs={{0,8},{1,9},{2,10},{3,11},{4,12},{5,13},{6,14},{7,15},{8,0},{9,1},... | collective-permute-start | bytes 245768 | tf_op jit(solution)/shard_map/ppermute | solution.py:50
  7.7 6.6 %collective-permute-start.1 = (bf16[8,5120]{1,0:T(8,128)(2,1)S(1)}, bf16[8,5120]{1,0:T(8,128)(2,1)S(1)}, u32[]{:S(2)}, u32[]{:S(2)}) collective-permute-start(bf16[8,5120]{1,0:T(8,128)(2,1)S(1)} %broadcast_select_fusion.refs_0_), channel_id=1, source_target_pairs={{0,4},{1,5},{2,6},{3,7},{4,0},{5,1},{6,2},{7,3},{8,12},{9,13},{10,... | collective-permute-start | bytes 245768 | tf_op jit(solution)/shard_map/ppermute | solution.py:50
  14.4 8.1 %collective-permute-start.7 = (bf16[32,5120]{1,0:T(8,128)(2,1)S(1)}, bf16[32,5120]{1,0:T(8,128)(2,1)S(1)}, u32[]{:S(2)}, u32[]{:S(2)}) collective-permute-start(bf16[32,5120]{1,0:T(8,128)(2,1)S(1)} %join.2.refs_4_), channel_id=1, source_target_pairs={{0,2},{1,3},{2,0},{3,1},{4,6},{5,7},{6,4},{7,5},{8,10},{9,11},{10,... | collective-permute-start | bytes 983048 | tf_op jit(solution)/shard_map/ppermute | solution.py:50
  15.7 8.9 %collective-permute-start.6 = (bf16[32,5120]{1,0:T(8,128)(2,1)S(1)}, bf16[32,5120]{1,0:T(8,128)(2,1)S(1)}, u32[]{:S(2)}, u32[]{:S(2)}) collective-permute-start(bf16[32,5120]{1,0:T(8,128)(2,1)S(1)} %join.2.refs_4_), channel_id=1, source_target_pairs={{0,1},{1,0},{2,3},{3,2},{4,5},{5,4},{6,7},{7,6},{8,9},{9,8},{10,11... | collective-permute-start | bytes 983048 | tf_op jit(solution)/shard_map/ppermute | solution.py:50
  17.9 8.0 %collective-permute-start.4 = (bf16[128,1280]{1,0:T(8,128)(2,1)S(1)}, bf16[128,1280]{1,0:T(8,128)(2,1)S(1)}, u32[]{:S(2)}, u32[]{:S(2)}) collective-permute-start(bf16[128,1280]{1,0:T(8,128)(2,1)S(1)} %get-tuple-element.43), channel_id=1, source_target_pairs={{0,16},{16,0},{1,17},{17,1},{2,18},{18,2},{3,19},{19,3},{4,20},{20... | collective-permute-start | bytes 983048 | tf_op jit(solution)/shard_map/ppermute | solution.py:22
  19.7 7.5 %collective-permute-start.5 = (bf16[128,1280]{1,0:T(8,128)(2,1)S(1)}, bf16[128,1280]{1,0:T(8,128)(2,1)S(1)}, u32[]{:S(2)}, u32[]{:S(2)}) collective-permute-start(bf16[128,1280]{1,0:T(8,128)(2,1)S(1)} %get-tuple-element.44), channel_id=1, source_target_pairs={{0,16},{16,0},{1,17},{17,1},{2,18},{18,2},{3,19},{19,3},{4,20},{20... | collective-permute-start | bytes 983048 | tf_op jit(solution)/shard_map/ppermute | solution.py:22
  19.9 7.3 %collective-permute-start.10 = (bf16[128,1280]{1,0:T(8,128)(2,1)S(1)}, bf16[128,1280]{1,0:T(8,128)(2,1)S(1)}, u32[]{:S(2)}, u32[]{:S(2)}) collective-permute-start(bf16[128,1280]{1,0:T(8,128)(2,1)S(1)} %get-tuple-element.47), channel_id=1, source_target_pairs={{0,16},{16,0},{1,17},{17,1},{2,18},{18,2},{3,19},{19,3},{4,20},{20... | collective-permute-start | bytes 983048 | tf_op jit(solution)/shard_map/ppermute | solution.py:22
  22.5 4.7 %collective-permute-start.11 = (bf16[128,1280]{1,0:T(8,128)(2,1)S(1)}, bf16[128,1280]{1,0:T(8,128)(2,1)S(1)}, u32[]{:S(2)}, u32[]{:S(2)}) collective-permute-start(bf16[128,1280]{1,0:T(8,128)(2,1)S(1)} %get-tuple-element.48), channel_id=1, source_target_pairs={{0,16},{16,0},{1,17},{17,1},{2,18},{18,2},{3,19},{19,3},{4,20},{20... | collective-permute-start | bytes 983048 | tf_op jit(solution)/shard_map/ppermute | solution.py:22
  24.6 4.6 %collective-permute-start.8 = (bf16[16,5120]{1,0:T(8,128)(2,1)S(1)}, bf16[16,5120]{1,0:T(8,128)(2,1)S(1)}, u32[]{:S(2)}, u32[]{:S(2)}) collective-permute-start(bf16[16,5120]{1,0:T(8,128)(2,1)S(1)} %slice.16), channel_id=1, source_target_pairs={{0,1},{1,0},{2,3},{3,2},{4,5},{5,4},{6,7},{7,6},{8,9},{9,8},{10,11... | collective-permute-start | bytes 491528 | tf_op jit(solution)/shard_map/ppermute | solution.py:50
  25.9 4.5 %collective-permute-start.9 = (bf16[16,5120]{1,0:T(8,128)(2,1)S(1)}, bf16[16,5120]{1,0:T(8,128)(2,1)S(1)}, u32[]{:S(2)}, u32[]{:S(2)}) collective-permute-start(bf16[16,5120]{1,0:T(8,128)(2,1)S(1)} %slice.17), channel_id=1, source_target_pairs={{0,2},{1,3},{2,0},{3,1},{4,6},{5,7},{6,4},{7,5},{8,10},{9,11},{10,... | collective-permute-start | bytes 491528 | tf_op jit(solution)/shard_map/ppermute | solution.py:50
  32.5 5.8 %collective-permute-start.12 = (bf16[128,2560]{1,0:T(8,128)(2,1)S(1)}, bf16[128,2560]{1,0:T(8,128)(2,1)S(1)}, u32[]{:S(2)}, u32[]{:S(2)}) collective-permute-start(bf16[128,2560]{1,0:T(8,128)(2,1)S(1)} %get-tuple-element.49.refs_3_), channel_id=1, source_target_pairs={{0,16},{1,17},{2,18},{3,19},{4,20},{5,21},{6,22},{7,23},{8,24},{9,... | collective-permute-start | bytes 1966088 | tf_op jit(solution)/shard_map/ppermute | solution.py:27
  33.8 4.5 %copy-start.3 = (f32[1,5120]{1,0:T(1,128)S(1)}, f32[1,5120]{1,0:T(1,128)}, u32[]{:S(2)}) copy-start(f32[1,5120]{1,0:T(1,128)} %refs_4_.1) | copy-start | bytes 61444
  33.8 30.7 %slice-start = ((s8[6553600]{0:T(1024)(128)(4,1)}), s8[4194304]{0:T(1024)(128)(4,1)S(1)}, s32[]{:S(2)}) async-start(s8[6553600]{0:T(1024)(128)(4,1)} %bitcast.16), calls=%async_computation | async-start | bytes 8388608
  35.8 6.8 %collective-permute-start.17 = (bf16[16,5120]{1,0:T(8,128)(2,1)S(1)}, bf16[16,5120]{1,0:T(8,128)(2,1)S(1)}, u32[]{:S(2)}, u32[]{:S(2)}) collective-permute-start(bf16[16,5120]{1,0:T(8,128)(2,1)S(1)} %get-tuple-element.59), channel_id=1, source_target_pairs={{2,0},{3,1},{0,2},{1,3},{6,4},{7,5},{4,6},{5,7},{10,8},{11,9},{8,1... | collective-permute-start | bytes 491528 | tf_op jit(solution)/shard_map/ppermute | solution.py:50
  38.0 5.9 %collective-permute-start.16 = (bf16[16,5120]{1,0:T(8,128)(2,1)S(1)}, bf16[16,5120]{1,0:T(8,128)(2,1)S(1)}, u32[]{:S(2)}, u32[]{:S(2)}) collective-permute-start(bf16[16,5120]{1,0:T(8,128)(2,1)S(1)} %get-tuple-element.57), channel_id=1, source_target_pairs={{1,0},{0,1},{3,2},{2,3},{5,4},{4,5},{7,6},{6,7},{9,8},{8,9},{11,10... | collective-permute-start | bytes 491528 | tf_op jit(solution)/shard_map/ppermute | solution.py:50
  38.2 26.2 %slice-start.1 = ((s8[6553600]{0:T(1024)(128)(4,1)}), s8[2359296]{0:T(1024)(128)(4,1)S(1)}, s32[]{:S(2)}) async-start(s8[6553600]{0:T(1024)(128)(4,1)} %bitcast.16), calls=%async_computation.1 | async-start | bytes 4718592
  38.2 26.2 %copy-start = (bf16[1,640,5120]{2,1,0:T(8,128)(2,1)S(1)}, bf16[1,640,5120]{2,1,0:T(8,128)(2,1)}, u32[]{:S(2)}) copy-start(bf16[1,640,5120]{2,1,0:T(8,128)(2,1)} %param.15) | copy-start | bytes 19660804
  38.9 5.2 %collective-permute-start.15 = (bf16[8,5120]{1,0:T(8,128)(2,1)S(1)}, bf16[8,5120]{1,0:T(8,128)(2,1)S(1)}, u32[]{:S(2)}, u32[]{:S(2)}) collective-permute-start(bf16[8,5120]{1,0:T(8,128)(2,1)S(1)} %get-tuple-element.55.refs_0_.after_any), channel_id=1, source_target_pairs={{0,12},{1,13},{2,14},{3,15},{4,8},{5,9},{6,10},{7,11},{8,4},{9,5},... | collective-permute-start | bytes 245768 | tf_op jit(solution)/shard_map/ppermute | solution.py:50
  41.3 7.5 %collective-permute-start.14 = (bf16[8,5120]{1,0:T(8,128)(2,1)S(1)}, bf16[8,5120]{1,0:T(8,128)(2,1)S(1)}, u32[]{:S(2)}, u32[]{:S(2)}) collective-permute-start(bf16[8,5120]{1,0:T(8,128)(2,1)S(1)} %get-tuple-element.55.refs_0_.after_any), channel_id=1, source_target_pairs={{0,8},{1,9},{2,10},{3,11},{4,12},{5,13},{6,14},{7,15},{8,0},{9,1},... | collective-permute-start | bytes 245768 | tf_op jit(solution)/shard_map/ppermute | solution.py:50
  41.3 7.5 %collective-permute-start.13 = (bf16[8,5120]{1,0:T(8,128)(2,1)S(1)}, bf16[8,5120]{1,0:T(8,128)(2,1)S(1)}, u32[]{:S(2)}, u32[]{:S(2)}) collective-permute-start(bf16[8,5120]{1,0:T(8,128)(2,1)S(1)} %get-tuple-element.55.refs_0_.after_any), channel_id=1, source_target_pairs={{0,4},{1,5},{2,6},{3,7},{4,0},{5,1},{6,2},{7,3},{8,12},{9,13},{10,... | collective-permute-start | bytes 245768 | tf_op jit(solution)/shard_map/ppermute | solution.py:50
  42.6 7.6 %collective-permute-start.21 = (bf16[32,5120]{1,0:T(8,128)(2,1)S(1)}, bf16[32,5120]{1,0:T(8,128)(2,1)S(1)}, u32[]{:S(2)}, u32[]{:S(2)}) collective-permute-start(bf16[32,5120]{1,0:T(8,128)(2,1)S(1)} %add_half.5.refs_5_), channel_id=1, source_target_pairs={{1,0},{0,1},{3,2},{2,3},{5,4},{4,5},{7,6},{6,7},{9,8},{8,9},{11,10... | collective-permute-start | bytes 983048 | tf_op jit(solution)/shard_map/ppermute | solution.py:50
  44.0 6.3 %collective-permute-start.20 = (bf16[32,5120]{1,0:T(8,128)(2,1)S(1)}, bf16[32,5120]{1,0:T(8,128)(2,1)S(1)}, u32[]{:S(2)}, u32[]{:S(2)}) collective-permute-start(bf16[32,5120]{1,0:T(8,128)(2,1)S(1)} %add_half.4.refs_4_), channel_id=1, source_target_pairs={{2,0},{3,1},{0,2},{1,3},{6,4},{7,5},{4,6},{5,7},{10,8},{11,9},{8,1... | collective-permute-start | bytes 983048 | tf_op jit(solution)/shard_map/ppermute | solution.py:50
  48.9 9.9 %collective-permute-start.19 = (bf16[32,5120]{1,0:T(8,128)(2,1)S(1)}, bf16[32,5120]{1,0:T(8,128)(2,1)S(1)}, u32[]{:S(2)}, u32[]{:S(2)}) collective-permute-start(bf16[32,5120]{1,0:T(8,128)(2,1)S(1)} %join.3.refs_3_.refs_2_), channel_id=1, source_target_pairs={{0,2},{1,3},{2,0},{3,1},{4,6},{5,7},{6,4},{7,5},{8,10},{9,11},{10,... | collective-permute-start | bytes 983048 | tf_op jit(solution)/shard_map/ppermute | solution.py:50
  49.4 9.3 %collective-permute-start.18 = (bf16[32,5120]{1,0:T(8,128)(2,1)S(1)}, bf16[32,5120]{1,0:T(8,128)(2,1)S(1)}, u32[]{:S(2)}, u32[]{:S(2)}) collective-permute-start(bf16[32,5120]{1,0:T(8,128)(2,1)S(1)} %join.3.refs_3_.refs_2_), channel_id=1, source_target_pairs={{0,1},{1,0},{2,3},{3,2},{4,5},{5,4},{6,7},{7,6},{8,9},{9,8},{10,11... | collective-permute-start | bytes 983048 | tf_op jit(solution)/shard_map/ppermute | solution.py:50
  58.7 5.5 %collective-permute-start.22 = (bf16[16,5120]{1,0:T(8,128)(2,1)S(1)}, bf16[16,5120]{1,0:T(8,128)(2,1)S(1)}, u32[]{:S(2)}, u32[]{:S(2)}) collective-permute-start(bf16[16,5120]{1,0:T(8,128)(2,1)S(1)} %get-tuple-element.61), channel_id=1, source_target_pairs={{0,1},{1,0},{2,3},{3,2},{4,5},{5,4},{6,7},{7,6},{8,9},{9,8},{10,11... | collective-permute-start | bytes 491528 | tf_op jit(solution)/shard_map/ppermute | solution.py:50
  60.0 4.5 %collective-permute-start.23 = (bf16[16,5120]{1,0:T(8,128)(2,1)S(1)}, bf16[16,5120]{1,0:T(8,128)(2,1)S(1)}, u32[]{:S(2)}, u32[]{:S(2)}) collective-permute-start(bf16[16,5120]{1,0:T(8,128)(2,1)S(1)} %get-tuple-element.62), channel_id=1, source_target_pairs={{0,2},{1,3},{2,0},{3,1},{4,6},{5,7},{6,4},{7,5},{8,10},{9,11},{10,... | collective-permute-start | bytes 491528 | tf_op jit(solution)/shard_map/ppermute | solution.py:50
  60.0 3.3 %collective-permute-start.24 = (bf16[8,5120]{1,0:T(8,128)(2,1)S(1)}, bf16[8,5120]{1,0:T(8,128)(2,1)S(1)}, u32[]{:S(2)}, u32[]{:S(2)}) collective-permute-start(bf16[8,5120]{1,0:T(8,128)(2,1)S(1)} %get-tuple-element.63), channel_id=1, source_target_pairs={{4,0},{5,1},{6,2},{7,3},{0,4},{1,5},{2,6},{3,7},{12,8},{13,9},{14,... | collective-permute-start | bytes 245768 | tf_op jit(solution)/shard_map/ppermute | solution.py:50
  60.0 4.2 %collective-permute-start.25 = (bf16[8,5120]{1,0:T(8,128)(2,1)S(1)}, bf16[8,5120]{1,0:T(8,128)(2,1)S(1)}, u32[]{:S(2)}, u32[]{:S(2)}) collective-permute-start(bf16[8,5120]{1,0:T(8,128)(2,1)S(1)} %get-tuple-element.64), channel_id=1, source_target_pairs={{8,0},{9,1},{10,2},{11,3},{12,4},{13,5},{14,6},{15,7},{0,8},{1,9},... | collective-permute-start | bytes 245768 | tf_op jit(solution)/shard_map/ppermute | solution.py:50
  66.8 4.2 %collective-permute-start.28 = (bf16[16,5120]{1,0:T(8,128)(2,1)S(1)}, bf16[16,5120]{1,0:T(8,128)(2,1)S(1)}, u32[]{:S(2)}, u32[]{:S(2)}) collective-permute-start(bf16[16,5120]{1,0:T(8,128)(2,1)S(1)} %get-tuple-element.69), channel_id=1, source_target_pairs={{2,0},{3,1},{0,2},{1,3},{6,4},{7,5},{4,6},{5,7},{10,8},{11,9},{8,1... | collective-permute-start | bytes 491528 | tf_op jit(solution)/shard_map/ppermute | solution.py:50
  68.1 4.2 %collective-permute-start.26 = (bf16[16,5120]{1,0:T(8,128)(2,1)S(1)}, bf16[16,5120]{1,0:T(8,128)(2,1)S(1)}, u32[]{:S(2)}, u32[]{:S(2)}) collective-permute-start(bf16[16,5120]{1,0:T(8,128)(2,1)S(1)} %get-tuple-element.67), channel_id=1, source_target_pairs={{1,0},{0,1},{3,2},{2,3},{5,4},{4,5},{7,6},{6,7},{9,8},{8,9},{11,10... | collective-permute-start | bytes 491528 | tf_op jit(solution)/shard_map/ppermute | solution.py:50
  68.4 28.9 %collective-permute-start.35 = (bf16[144,2560]{1,0:T(8,128)(2,1)S(1)}, bf16[144,2560]{1,0:T(8,128)(2,1)S(1)}, u32[]{:S(2)}, u32[]{:S(2)}) collective-permute-start(bf16[144,2560]{1,0:T(8,128)(2,1)S(1)} %get-tuple-element.77), channel_id=1, source_target_pairs={{0,16},{1,17},{2,18},{3,19},{4,20},{5,21},{6,22},{7,23},{8,24},{9,... | collective-permute-start | bytes 2211848 | tf_op jit(solution)/shard_map/ppermute | solution.py:17
  69.6 27.6 %collective-permute-start.36 = (bf16[128,2560]{1,0:T(8,128)(2,1)S(1)}, bf16[128,2560]{1,0:T(8,128)(2,1)S(1)}, u32[]{:S(2)}, u32[]{:S(2)}) collective-permute-start(bf16[128,2560]{1,0:T(8,128)(2,1)S(1)} %get-tuple-element.78), channel_id=1, source_target_pairs={{0,16},{1,17},{2,18},{3,19},{4,20},{5,21},{6,22},{7,23},{8,24},{9,... | collective-permute-start | bytes 1966088 | tf_op jit(solution)/shard_map/ppermute | solution.py:17
  71.1 8.2 %collective-permute-start.29 = (bf16[32,5120]{1,0:T(8,128)(2,1)S(1)}, bf16[32,5120]{1,0:T(8,128)(2,1)S(1)}, u32[]{:S(2)}, u32[]{:S(2)}) collective-permute-start(bf16[32,5120]{1,0:T(8,128)(2,1)S(1)} %add_half.7), channel_id=1, source_target_pairs={{1,0},{0,1},{3,2},{2,3},{5,4},{4,5},{7,6},{6,7},{9,8},{8,9},{11,10... | collective-permute-start | bytes 983048 | tf_op jit(solution)/shard_map/ppermute | solution.py:50
  72.3 7.0 %collective-permute-start.27 = (bf16[32,5120]{1,0:T(8,128)(2,1)S(1)}, bf16[32,5120]{1,0:T(8,128)(2,1)S(1)}, u32[]{:S(2)}, u32[]{:S(2)}) collective-permute-start(bf16[32,5120]{1,0:T(8,128)(2,1)S(1)} %add_half.6), channel_id=1, source_target_pairs={{2,0},{3,1},{0,2},{1,3},{6,4},{7,5},{4,6},{5,7},{10,8},{11,9},{8,1... | collective-permute-start | bytes 983048 | tf_op jit(solution)/shard_map/ppermute | solution.py:50
  72.8 5.2 %collective-permute-start.30 = (bf16[8,5120]{1,0:T(8,128)(2,1)S(1)}, bf16[8,5120]{1,0:T(8,128)(2,1)S(1)}, u32[]{:S(2)}, u32[]{:S(2)}) collective-permute-start(bf16[8,5120]{1,0:T(8,128)(2,1)S(1)} %get-tuple-element.70), channel_id=1, source_target_pairs={{12,0},{13,1},{14,2},{15,3},{8,4},{9,5},{10,6},{11,7},{4,8},{5,9},... | collective-permute-start | bytes 245768 | tf_op jit(solution)/shard_map/ppermute | solution.py:50
  78.0 11.3 %collective-permute-start.34 = (f32[8,5120]{1,0:T(8,128)S(1)}, f32[8,5120]{1,0:T(8,128)S(1)}, u32[]{:S(2)}, u32[]{:S(2)}) collective-permute-start(f32[8,5120]{1,0:T(8,128)S(1)} %add_last.2.refs_3_.second_ref), channel_id=1, source_target_pairs={{0,16},{1,17},{2,18},{3,19},{4,20},{5,21},{6,22},{7,23},{8,24},{9,... | collective-permute-start | bytes 491528 | tf_op jit(solution)/shard_map/ppermute | solution.py:27
  79.5 12.5 %collective-permute-start.31 = (bf16[8,5120]{1,0:T(8,128)(2,1)S(1)}, bf16[8,5120]{1,0:T(8,128)(2,1)S(1)}, u32[]{:S(2)}, u32[]{:S(2)}) collective-permute-start(bf16[8,5120]{1,0:T(8,128)(2,1)S(1)} %get-tuple-element.73), channel_id=1, source_target_pairs={{4,0},{5,1},{6,2},{7,3},{0,4},{1,5},{2,6},{3,7},{12,8},{13,9},{14,... | collective-permute-start | bytes 245768 | tf_op jit(solution)/shard_map/ppermute | solution.py:50
  80.4 11.6 %collective-permute-start.32 = (bf16[8,5120]{1,0:T(8,128)(2,1)S(1)}, bf16[8,5120]{1,0:T(8,128)(2,1)S(1)}, u32[]{:S(2)}, u32[]{:S(2)}) collective-permute-start(bf16[8,5120]{1,0:T(8,128)(2,1)S(1)} %get-tuple-element.74), channel_id=1, source_target_pairs={{8,0},{9,1},{10,2},{11,3},{12,4},{13,5},{14,6},{15,7},{0,8},{1,9},... | collective-permute-start | bytes 245768 | tf_op jit(solution)/shard_map/ppermute | solution.py:50
  89.3 5.1 %collective-permute-start.33 = (bf16[8,5120]{1,0:T(8,128)(2,1)S(1)}, bf16[8,5120]{1,0:T(8,128)(2,1)S(1)}, u32[]{:S(2)}, u32[]{:S(2)}) collective-permute-start(bf16[8,5120]{1,0:T(8,128)(2,1)S(1)} %get-tuple-element.75), channel_id=1, source_target_pairs={{12,0},{13,1},{14,2},{15,3},{8,4},{9,5},{10,6},{11,7},{4,8},{5,9},... | collective-permute-start | bytes 245768 | tf_op jit(solution)/shard_map/ppermute | solution.py:50
  94.4 6.7 %collective-permute-start.37 = (f32[8,5120]{1,0:T(8,128)S(1)}, f32[8,5120]{1,0:T(8,128)S(1)}, u32[]{:S(2)}, u32[]{:S(2)}) collective-permute-start(f32[8,5120]{1,0:T(8,128)S(1)} %add_last.3.refs_1_), channel_id=1, source_target_pairs={{0,16},{1,17},{2,18},{3,19},{4,20},{5,21},{6,22},{7,23},{8,24},{9,... | collective-permute-start | bytes 491528 | tf_op jit(solution)/shard_map/ppermute | solution.py:17

commit v7 on v6

--- a/solution.py
+++ b/solution.py
@@ -83,7 +83,7 @@
                 pieces[b, c] = [self.shift(upper, (0, 0, c)), self.shift(lower, (0, b, 0))]
         return sum((pieces[k] for k in self.offsets()), [])
 
-    def scatter(self, pieces, rows, after=()):
+    def scatter(self, pieces, rows, after=(), extra=None):
         na, nb, nc = self.sizes
         half = rows * (na - na // 2)
         held, at = {}, 0
@@ -104,7 +104,7 @@
         blocks = add_blocks(held[0, 0][0], arrived, rows, after)
         more = [self.shift(blocks[s], (s, 0, 0), back=True) for s in range(1, na)]
         after = yield blocks, more
-        yield add_last(blocks[0], more, after)
+        yield add_last(blocks[0], more, after, extra)
 
 
 def compiler_params():
@@ -220,15 +220,22 @@
     return local_kernel(kernel, "add_blocks", outs, [piece, *more], after)
 
 
-def add_last(block, more, after):
+def add_last(block, more, after, extra=None):
+    rows, width = block.shape
+    wide = 0 if extra is None else extra.shape[1]
+
     def kernel(block_ref, *refs):
         total = block_ref[...]
-        for ref in refs[:-1]:
+        for ref in refs[: len(more)]:
             total = total + ref[...].astype(jnp.float32)
-        refs[-1][...] = total
-
-    one = jax.ShapeDtypeStruct(block.shape, jnp.float32)
-    return local_kernel(kernel, "add_last", [one], [block, *more], after)[0]
+        refs[-1][:, :width] = total
+        if wide:
+            refs[-1][:, width:] = jnp.zeros((rows, wide), jnp.float32)
+            refs[-1][: extra.shape[0], width:] = refs[len(more)][...]
+
+    one = jax.ShapeDtypeStruct((rows, width + wide), jnp.float32)
+    args = [block, *more] + ([extra] if wide else [])
+    return local_kernel(kernel, "add_last", [one], args, after)[0]
 
 
 def head_loop(heads, some_heads):
@@ -250,33 +257,17 @@
     return [jnp.concatenate([r[:, c] for r in refs], axis=0) for c in columns]
 
 
-EXTRA = 16
-
-
-def extra_rows(gate, slots):
-    high = gate.astype(jnp.bfloat16).astype(jnp.float32)
-    middle = (gate - high).astype(jnp.bfloat16).astype(jnp.float32)
-    none = jnp.zeros((EXTRA - 4, gate.shape[1]), jnp.float32)
-    rows = [high, middle, gate - high - middle, slots, none]
-    return jnp.concatenate(rows, axis=0).astype(jnp.bfloat16)
-
-
 def make_queries(x, gain, gate, slots, after):
     tokens, width = x.shape
     half = width // 2
 
     quarter = half // 2
 
-    def kernel(x_ref, gain_ref, gate_ref, slot_ref, copy_ref, left_ref, right_ref, *refs):
+    def kernel(x_ref, gain_ref, gate_ref, slot_ref, copy_ref, *refs):
         *q_refs, gates_ref = refs
-        gate, slots = gate_ref[...], slot_ref[...].astype(jnp.float32)
         copy_ref[...] = x_ref[...]
-        left_ref[:tokens] = x_ref[:, :half]
-        left_ref[tokens:] = jnp.zeros((EXTRA, half), jnp.bfloat16)
-        left_ref[tokens:, :tokens] = extra_rows(gate, slots)
-        right_ref[...] = x_ref[:, half:]
-        gates_ref[0:1] = gate
-        gates_ref[1:2] = slots
+        gates_ref[0:1] = gate_ref[...]
+        gates_ref[1:2] = slot_ref[...].astype(jnp.float32)
         x = x_ref[...].astype(jnp.float32)
         inverse = lax.rsqrt(jnp.mean(x * x, axis=-1, keepdims=True) + 1e-06)
         for at, ref in zip((0, quarter, half), q_refs):
@@ -287,13 +278,11 @@
     part = jax.ShapeDtypeStruct((tokens, quarter), jnp.bfloat16)
     one = jax.ShapeDtypeStruct((tokens, half), jnp.bfloat16)
     same = jax.ShapeDtypeStruct((tokens, width), x.dtype)
-    left = jax.ShapeDtypeStruct((tokens + EXTRA, half), x.dtype)
-    right = jax.ShapeDtypeStruct((tokens, half), x.dtype)
     pair = jax.ShapeDtypeStruct((2, tokens), jnp.float32)
     return local_kernel(
         kernel,
         "queries",
-        [same, left, right, part, part, one, pair],
+        [same, part, part, one, pair],
         [x, gain, gate, slots],
         after,
     )
@@ -511,22 +500,17 @@
     )(section.reshape(1), after)
 
 
-def finish(section, res, back, room=None, gates=None):
-    tokens, part = res[-1].shape
-    width = part * len(res)
+def finish(section, res, back, room=None):
+    tokens, width = res.shape
     one = jax.ShapeDtypeStruct((tokens, width), jnp.bfloat16)
-    step = next(s for s in (1280, 1024, 512, 256, 128) if part % s == 0)
+    step = next(s for s in (1280, 1024, 512, 256, 128) if width % s == 0)
     parts = [slice(at, at + step) for at in range(0, width, step)]
 
-    def kernel(section, *refs):
-        res_refs, (back_ref, last, out_any, out_ref, sems) = refs[: len(res)], refs[len(res) :]
+    def kernel(section, res_ref, back_ref, *refs):
+        out_any, out_ref, sems = refs[-3:]
 
         def compute():
-            if gates is None:
-                extra = res_refs[0][tokens:, :tokens].astype(jnp.float32)
-                gate, slot = extra[0:1] + extra[1:2] + extra[2:3], extra[3:4]
-            else:
-                gate, slot = last[0:1], last[1:2]
+            gate, slot = back_ref[0:1, width:], back_ref[1:2, width:]
             gate = jnp.broadcast_to(gate, (CAP, tokens)).T[:, 0:1]
             slots = lax.broadcasted_iota(jnp.int32, (CAP, tokens), 0).astype(jnp.float32)
             onehot = jnp.where(slot == slots, 1.0, 0.0).T
@@ -538,8 +522,7 @@
                 middle = (back - high).astype(jnp.bfloat16).astype(jnp.float32)
                 three = jnp.concatenate([high, middle, back - high - middle], axis=0)
                 moved = dot(onehot, three.astype(jnp.bfloat16))
-                of, at = divmod(columns.start, part)
-                here = res_refs[of][:tokens, at : at + step].astype(jnp.float32)
+                here = res_ref[:, columns].astype(jnp.float32)
                 out_ref[:, columns] = (here + gate * moved).astype(jnp.bfloat16)
                 copy = pltpu.make_async_copy(
                     out_ref.at[:, columns], out_any.at[:, columns], sems.at[i]
@@ -549,28 +532,28 @@
             for copy in copies:
                 copy.wait()
 
-        if gates is None:
+        if room is None:
+            compute()
+        else:
             pl.when(section[0] > 0)(compute)
-        else:
-            compute()
-
-    last = (room, pl.BlockSpec(memory_space=pltpu.HBM)) if gates is None else (gates, in_vmem(1)[0])
+
+    aliased = [] if room is None else [pl.BlockSpec(memory_space=pltpu.HBM)]
     return pl.pallas_call(
         kernel,
         out_shape=one,
-        in_specs=[pl.BlockSpec(memory_space=pltpu.SMEM), *in_vmem(len(res) + 1), last[1]],
+        in_specs=[pl.BlockSpec(memory_space=pltpu.SMEM), *in_vmem(2), *aliased],
         out_specs=pl.BlockSpec(memory_space=pltpu.HBM),
         scratch_shapes=[
             pltpu.VMEM(one.shape, one.dtype),
             pltpu.SemaphoreType.DMA((len(parts),)),
         ],
-        input_output_aliases={len(res) + 2: 0} if gates is None else {},
+        input_output_aliases={} if room is None else {3: 0},
         compiler_params=compiler_params(),
         cost_estimate=pl.CostEstimate(
             flops=50 * tokens * width, bytes_accessed=5 * tokens * width, transcendentals=0
         ),
         name="finish",
-    )(section.reshape(1), *res, back, last[0])
+    )(section.reshape(1), res, back, *([] if room is None else [room]))
 
 
 def local(
@@ -588,7 +571,7 @@
     first = swapped(memory[0, :, :, :half].reshape(own_rows, width))
     second = memory[0, :, :, half:].reshape(own_rows, width)
     pieces = grid.gather(jnp.where(decoder, second, first))
-    current, left, right, *first, second, gates = make_queries(
+    current, *first, second, gates = make_queries(
         layer_in[0], attn_gain, gate_prob, slot_index, [pieces[0]]
     )
     first = [swapped(q) for q in first]
@@ -613,11 +596,7 @@
     residual, capacity = settle(
         section, sections, current, to_decoder(mixed), mixed, norm_gain, gates, [parts[0]]
     )
-    if sections != 2:
-        extra = extra_rows(gates[0:1], gates[1:2])
-        extra = jnp.pad(extra, ((0, 0), (0, half - extra.shape[1])))
-        left, right = jnp.concatenate([residual[:, :half], extra], axis=0), residual[:, half:]
-    residual_before = [passed_along(x, "section", 1) for x in (left, right)]
+    residual_before = passed_along(current if sections == 2 else residual, "section", 1)
     grads = grid.scatter(parts, own_rows)
     halves = next(grads)
     sums = []
@@ -629,17 +608,17 @@
 
     gathered = grid.gather(capacity, halves, plane_sums)
     computed = expert(
-        expert_in[0], expert_out[0], gathered, grid.heights(CAP), grid.types(), sums[0][1][:2]
+        expert_in[0], expert_out[0], gathered, grid.heights(CAP), grid.types(), [residual_before, *sums[0][1][:2]]
     )
     total_grad = grads.send([computed[0]])
     room, made = blank(section, capacity, residual)
-    results = grid.scatter(computed, CAP)
+    results = grid.scatter(computed, CAP, [total_grad], gates)
     next(results)
-    results.send([total_grad, made])
+    results.send([made])
     total_grad, laid = lay_out(section, sections, to_decoder(total_grad), total_grad)
     returned = results.send([laid])
     returned_before = passed_along(returned, "section", 1)
-    output = finish(section, [residual], returned, gates=gates)
+    output = finish(section, residual, returned)
     arriving = finish(section, residual_before, returned_before, room)
     return (output[None], arriving[None], total_grad[None])
 

time: 103 us -> 102 us (level)
  starting transfers between devices: 42.8 us -> 41.2 us
    ppermute x2, waiting for transfers between devices: 7.44 us -> 0.01 us  [to_decoder(): lax.ppermute(block, 'section', [(i, i + apart) for i in range(apart)])]
    ppermute x3 -> x2, waiting for transfers between devices: 3.82 us -> 8.55 us  [passed_along(): return lax.ppermute(block, axis, route)]
    ppermute x28, waiting for transfers between devices: 32.7 us -> 36.4 us  [shift(): return lax.ppermute(block, 'expert', route)]
    ppermute x3 -> x2, starting transfers between devices: 3.86 us -> 2.57 us  [passed_along(): return lax.ppermute(block, axis, route)]
  transfers between devices with their start and end apart: 38 -> 37, of which waited for: 16 -> 17; matrix products, arithmetic and copies ran while one was open for 0% -> 0% of each run, Pallas kernels for 6% -> 8%
where the time goes in v7:
time: 102 us
  waiting for transfers between devices  46.1 us (45%)
  starting transfers between devices  41.2 us (40%)
  Pallas kernels  12.3 us (12%)
  local copies, waits for them, and re-layouts  1.24 us (1%)
    ppermute x28, waiting for transfers between devices, shift(): return lax.ppermute(block, 'expert', route)  36.4 us
    ppermute x28, starting transfers between devices, shift(): return lax.ppermute(block, 'expert', route)  31.4 us
    pallas_call x18, Pallas kernels, local_kernel(): pl.pallas_call(body, out_shape=tuple(outs), in_specs=in_specs, out_specs=...  9.26 us
    ppermute x2, waiting for transfers between devices, passed_along(): return lax.ppermute(block, axis, route)  8.55 us
    ppermute x5, starting transfers between devices, swapped(): lax.ppermute(block, 'section', [(i, (i + sections // 2) % sections) for i...  4.61 us
    pallas_call x2, Pallas kernels, finish(): pl.pallas_call(kernel, out_shape=one, in_specs=[pl.BlockSpec(memory_space...  3.03 us
    ppermute x2, starting transfers between devices, passed_along(): return lax.ppermute(block, axis, route)  2.57 us
    ppermute x2, starting transfers between devices, to_decoder(): lax.ppermute(block, 'section', [(i, i + apart) for i in range(apart)])  2.57 us
  transfers between devices with their start and end apart: 37, of which 17 were waited for; matrix products, arithmetic and copies ran while one was open for 0% of the time, Pallas kernels for 8%

profile of v7, /device:TPU:1, one launch (start us, length us, event | category | flops | bytes accessed | tf_op | source)
XLA Modules:
  0.0 101.8 jit_solution(6028498761448332937)
XLA Ops:
  0.7 1.1 %slice_bitcast_fusion = (bf16[1,8,2,2560]{3,2,1,0:T(2,128)(2,1)S(1)}, bf16[1,8,2,2560]{3,2,1,0:T(2,128)(2,1)S(1)}) fusion(bf16[1,8,2,5120]{3,2,1,0:T(2,128)(2,1)} %param.10), kind=kLoop, calls=%fused_computation | loop fusion | bytes 327680
  1.8 0.1 collective-permute-start
  2.0 1.2 %collective-permute-done = bf16[8,5120]{1,0:T(8,128)(2,1)S(1)} collective-permute-done((bf16[8,5120]{1,0:T(8,128)(2,1)S(1)}, bf16[8,5120]{1,0:T(8,128)(2,1)S(1)}, u32[]{:S(2)}, u32[]{:S(2)}) %collective-permute-start) | collective-permute-done | bytes 81952 | tf_op jit(solution)/shard_map/ppermute | solution.py:22
  3.2 4.5 %collective-permute-start.3 = (bf16[8,5120]{1,0:T(8,128)(2,1)S(1)}, bf16[8,5120]{1,0:T(8,128)(2,1)S(1)}, u32[]{:S(2)}, u32[]{:S(2)}) collective-permute-start(bf16[8,5120]{1,0:T(8,128)(2,1)S(1)} %broadcast_select_fusion.refs_0_), channel_id=1, source_target_pairs={{0,12},{1,13},{2,14},{3,15},{4,8},{5,9},{6,10},{7,11},{8,4},{9,5},... | collective-permute-start | bytes 245768 | tf_op jit(solution)/shard_map/ppermute | solution.py:50
  7.7 0.4 collective-permute-start.1
  8.1 2.2 %collective-permute-done.3.refs_3_ = bf16[8,5120]{1,0:T(8,128)(2,1)S(1)} collective-permute-done((bf16[8,5120]{1,0:T(8,128)(2,1)S(1)}, bf16[8,5120]{1,0:T(8,128)(2,1)S(1)}, u32[]{:S(2)}, u32[]{:S(2)}) %collective-permute-start.3) | collective-permute-done | bytes 81952 | tf_op jit(solution)/shard_map/ppermute | solution.py:50
  10.3 4.1 %collective-permute-done.2.refs_2_ = bf16[8,5120]{1,0:T(8,128)(2,1)S(1)} collective-permute-done((bf16[8,5120]{1,0:T(8,128)(2,1)S(1)}, bf16[8,5120]{1,0:T(8,128)(2,1)S(1)}, u32[]{:S(2)}, u32[]{:S(2)}) %collective-permute-start.2) | collective-permute-done | bytes 81952 | tf_op jit(solution)/shard_map/ppermute | solution.py:50
  14.4 1.3 %collective-permute-start.7 = (bf16[32,5120]{1,0:T(8,128)(2,1)S(1)}, bf16[32,5120]{1,0:T(8,128)(2,1)S(1)}, u32[]{:S(2)}, u32[]{:S(2)}) collective-permute-start(bf16[32,5120]{1,0:T(8,128)(2,1)S(1)} %join.2.refs_4_), channel_id=1, source_target_pairs={{0,2},{1,3},{2,0},{3,1},{4,6},{5,7},{6,4},{7,5},{8,10},{9,11},{10,... | collective-permute-start | bytes 983048 | tf_op jit(solution)/shard_map/ppermute | solution.py:50
  15.7 1.2 %collective-permute-start.6 = (bf16[32,5120]{1,0:T(8,128)(2,1)S(1)}, bf16[32,5120]{1,0:T(8,128)(2,1)S(1)}, u32[]{:S(2)}, u32[]{:S(2)}) collective-permute-start(bf16[32,5120]{1,0:T(8,128)(2,1)S(1)} %join.2.refs_4_), channel_id=1, source_target_pairs={{0,1},{1,0},{2,3},{3,2},{4,5},{5,4},{6,7},{7,6},{8,9},{9,8},{10,11... | collective-permute-start | bytes 983048 | tf_op jit(solution)/shard_map/ppermute | solution.py:50
  16.9 0.9 queries.1
  17.8 1.8 %collective-permute-start.4 = (bf16[128,1280]{1,0:T(8,128)(2,1)S(1)}, bf16[128,1280]{1,0:T(8,128)(2,1)S(1)}, u32[]{:S(2)}, u32[]{:S(2)}) collective-permute-start(bf16[128,1280]{1,0:T(8,128)(2,1)S(1)} %get-tuple-element.41), channel_id=1, source_target_pairs={{0,16},{16,0},{1,17},{17,1},{2,18},{18,2},{3,19},{19,3},{4,20},{20... | collective-permute-start | bytes 983048 | tf_op jit(solution)/shard_map/ppermute | solution.py:22
  19.6 0.1 collective-permute-start.5
  19.7 0.1 cut.1
  19.8 0.5 collective-permute-start.10
  20.3 2.2 %collective-permute-done.7.refs_6_ = bf16[32,5120]{1,0:T(8,128)(2,1)S(1)} collective-permute-done((bf16[32,5120]{1,0:T(8,128)(2,1)S(1)}, bf16[32,5120]{1,0:T(8,128)(2,1)S(1)}, u32[]{:S(2)}, u32[]{:S(2)}) %collective-permute-start.7) | collective-permute-done | bytes 327712 | tf_op jit(solution)/shard_map/ppermute | solution.py:50
  22.5 2.1 %collective-permute-start.11 = (bf16[128,1280]{1,0:T(8,128)(2,1)S(1)}, bf16[128,1280]{1,0:T(8,128)(2,1)S(1)}, u32[]{:S(2)}, u32[]{:S(2)}) collective-permute-start(bf16[128,1280]{1,0:T(8,128)(2,1)S(1)} %get-tuple-element.46), channel_id=1, source_target_pairs={{0,16},{16,0},{1,17},{17,1},{2,18},{18,2},{3,19},{19,3},{4,20},{20... | collective-permute-start | bytes 983048 | tf_op jit(solution)/shard_map/ppermute | solution.py:22
  24.6 1.3 %collective-permute-start.8 = (bf16[16,5120]{1,0:T(8,128)(2,1)S(1)}, bf16[16,5120]{1,0:T(8,128)(2,1)S(1)}, u32[]{:S(2)}, u32[]{:S(2)}) collective-permute-start(bf16[16,5120]{1,0:T(8,128)(2,1)S(1)} %slice.16), channel_id=1, source_target_pairs={{0,1},{1,0},{2,3},{3,2},{4,5},{5,4},{6,7},{7,6},{8,9},{9,8},{10,11... | collective-permute-start | bytes 491528 | tf_op jit(solution)/shard_map/ppermute | solution.py:50
  25.9 1.3 %collective-permute-start.9 = (bf16[16,5120]{1,0:T(8,128)(2,1)S(1)}, bf16[16,5120]{1,0:T(8,128)(2,1)S(1)}, u32[]{:S(2)}, u32[]{:S(2)}) collective-permute-start(bf16[16,5120]{1,0:T(8,128)(2,1)S(1)} %slice.17), channel_id=1, source_target_pairs={{0,2},{1,3},{2,0},{3,1},{4,6},{5,7},{6,4},{7,5},{8,10},{9,11},{10,... | collective-permute-start | bytes 491528 | tf_op jit(solution)/shard_map/ppermute | solution.py:50
  27.2 1.3 %collective-permute-start.24 = (bf16[128,5120]{1,0:T(8,128)(2,1)S(1)}, bf16[128,5120]{1,0:T(8,128)(2,1)S(1)}, u32[]{:S(2)}, u32[]{:S(2)}) collective-permute-start(bf16[128,5120]{1,0:T(8,128)(2,1)S(1)} %get-tuple-element.40.refs_1_), channel_id=1, source_target_pairs={{0,16},{1,17},{2,18},{3,19},{4,20},{5,21},{6,22},{7,23},{8,24},{9,... | collective-permute-start | bytes 3932168 | tf_op jit(solution)/shard_map/ppermute | solution.py:17
  28.5 0.7 collective-permute-done.8.refs_7_
  29.2 1.2 %collective-permute-done.9.refs_8_ = bf16[16,5120]{1,0:T(8,128)(2,1)S(1)} collective-permute-done((bf16[16,5120]{1,0:T(8,128)(2,1)S(1)}, bf16[16,5120]{1,0:T(8,128)(2,1)S(1)}, u32[]{:S(2)}, u32[]{:S(2)}) %collective-permute-start.9) | collective-permute-done | bytes 163872 | tf_op jit(solution)/shard_map/ppermute | solution.py:50
  30.4 2.0 %attend.1 = (bf16[128,2560]{1,0:T(8,128)(2,1)S(1)}, f32[20,128,128]{2,1,0:T(8,128)S(1)}, bf16[128,2560]{1,0:T(8,128)(2,1)S(1)}) custom-call(s32[1]{0:T(128)} %bitcast.refs_0_.section, bf16[128,1280]{1,0:T(8,128)(2,1)S(1)} %collective-permute-done.4.refs_1_, bf16[128,1280]{1,0:T(8,128)(2,1)S(1)} %collective-permute-done.5.refs_2_, ...), custom_call_target="tpu_custom_call" | custom-call | flops 167772160 | bytes 5242884 | tf_op jit(solution)/shard_map/attend/pallas_call | solution.py:142
  32.5 1.3 %collective-permute-start.12 = (bf16[128,2560]{1,0:T(8,128)(2,1)S(1)}, bf16[128,2560]{1,0:T(8,128)(2,1)S(1)}, u32[]{:S(2)}, u32[]{:S(2)}) collective-permute-start(bf16[128,2560]{1,0:T(8,128)(2,1)S(1)} %get-tuple-element.47.refs_3_), channel_id=1, source_target_pairs={{0,16},{1,17},{2,18},{3,19},{4,20},{5,21},{6,22},{7,23},{8,24},{9,... | collective-permute-start | bytes 1966088 | tf_op jit(solution)/shard_map/ppermute | solution.py:27
  33.8 0.0 slice-start
  33.8 2.0 %gradient.1 = (f32[32,5120]{1,0:T(8,128)S(1)}, f32[32,5120]{1,0:T(8,128)S(1)}, f32[32,5120]{1,0:T(8,128)S(1)}, bf16[16,5120]{1,0:T(8,128)(2,1)S(1)}, bf16[16,5120]{1,0:T(8,128)(2,1)S(1)}) custom-call(s32[1]{0:T(128)} %bitcast.refs_0_.section, bf16[128,2560]{1,0:T(8,128)(2,1)S(1)} %get-tuple-element.48.q_ref, ...), custom_call_target="tpu_custom_call" | custom-call | flops 419430400 | bytes 6881284 | tf_op jit(solution)/shard_map/gradient/pallas_call | solution.py:142
  35.8 2.2 %collective-permute-start.17 = (bf16[16,5120]{1,0:T(8,128)(2,1)S(1)}, bf16[16,5120]{1,0:T(8,128)(2,1)S(1)}, u32[]{:S(2)}, u32[]{:S(2)}) collective-permute-start(bf16[16,5120]{1,0:T(8,128)(2,1)S(1)} %get-tuple-element.57), channel_id=1, source_target_pairs={{2,0},{3,1},{0,2},{1,3},{6,4},{7,5},{4,6},{5,7},{10,8},{11,9},{8,1... | collective-permute-start | bytes 491528 | tf_op jit(solution)/shard_map/ppermute | solution.py:50
  38.0 0.3 collective-permute-start.16
  38.3 0.6 settle.1
  38.9 2.4 %collective-permute-start.15 = (bf16[8,5120]{1,0:T(8,128)(2,1)S(1)}, bf16[8,5120]{1,0:T(8,128)(2,1)S(1)}, u32[]{:S(2)}, u32[]{:S(2)}) collective-permute-start(bf16[8,5120]{1,0:T(8,128)(2,1)S(1)} %get-tuple-element.53.refs_0_.after_any), channel_id=1, source_target_pairs={{0,12},{1,13},{2,14},{3,15},{4,8},{5,9},{6,10},{7,11},{8,4},{9,5},... | collective-permute-start | bytes 245768 | tf_op jit(solution)/shard_map/ppermute | solution.py:50
  41.3 1.2 %collective-permute-start.13 = (bf16[8,5120]{1,0:T(8,128)(2,1)S(1)}, bf16[8,5120]{1,0:T(8,128)(2,1)S(1)}, u32[]{:S(2)}, u32[]{:S(2)}) collective-permute-start(bf16[8,5120]{1,0:T(8,128)(2,1)S(1)} %get-tuple-element.53.refs_0_.after_any), channel_id=1, source_target_pairs={{0,4},{1,5},{2,6},{3,7},{4,0},{5,1},{6,2},{7,3},{8,12},{9,13},{10,... | collective-permute-start | bytes 245768 | tf_op jit(solution)/shard_map/ppermute | solution.py:50
  42.6 1.3 %collective-permute-start.21 = (bf16[32,5120]{1,0:T(8,128)(2,1)S(1)}, bf16[32,5120]{1,0:T(8,128)(2,1)S(1)}, u32[]{:S(2)}, u32[]{:S(2)}) collective-permute-start(bf16[32,5120]{1,0:T(8,128)(2,1)S(1)} %add_half.5.refs_5_), channel_id=1, source_target_pairs={{1,0},{0,1},{3,2},{2,3},{5,4},{4,5},{7,6},{6,7},{9,8},{8,9},{11,10... | collective-permute-start | bytes 983048 | tf_op jit(solution)/shard_map/ppermute | solution.py:50
  43.9 0.2 collective-permute-done.15.refs_3_
  44.1 0.5 collective-permute-start.20
  44.5 4.2 %collective-permute-done.14.refs_2_ = bf16[8,5120]{1,0:T(8,128)(2,1)S(1)} collective-permute-done((bf16[8,5120]{1,0:T(8,128)(2,1)S(1)}, bf16[8,5120]{1,0:T(8,128)(2,1)S(1)}, u32[]{:S(2)}, u32[]{:S(2)}) %collective-permute-start.14) | collective-permute-done | bytes 81952 | tf_op jit(solution)/shard_map/ppermute | solution.py:50
  48.8 0.6 collective-permute-start.19
  49.4 0.8 collective-permute-start.18
  50.2 0.1 collective-permute-done.20.refs_1_
  50.3 0.1 add_blocks.2
  50.4 8.2 %collective-permute-done.19.refs_0_.refs_4_ = bf16[32,5120]{1,0:T(8,128)(2,1)S(1)} collective-permute-done((bf16[32,5120]{1,0:T(8,128)(2,1)S(1)}, bf16[32,5120]{1,0:T(8,128)(2,1)S(1)}, u32[]{:S(2)}, u32[]{:S(2)}) %collective-permute-start.19) | collective-permute-done | bytes 327712 | tf_op jit(solution)/shard_map/ppermute | solution.py:50
  58.6 1.3 %collective-permute-start.22 = (bf16[16,5120]{1,0:T(8,128)(2,1)S(1)}, bf16[16,5120]{1,0:T(8,128)(2,1)S(1)}, u32[]{:S(2)}, u32[]{:S(2)}) collective-permute-start(bf16[16,5120]{1,0:T(8,128)(2,1)S(1)} %get-tuple-element.59), channel_id=1, source_target_pairs={{0,1},{1,0},{2,3},{3,2},{4,5},{5,4},{6,7},{7,6},{8,9},{9,8},{10,11... | collective-permute-start | bytes 491528 | tf_op jit(solution)/shard_map/ppermute | solution.py:50
  59.9 0.0 collective-permute-start.23
  59.9 2.2 %collective-permute-start.26 = (bf16[8,5120]{1,0:T(8,128)(2,1)S(1)}, bf16[8,5120]{1,0:T(8,128)(2,1)S(1)}, u32[]{:S(2)}, u32[]{:S(2)}) collective-permute-start(bf16[8,5120]{1,0:T(8,128)(2,1)S(1)} %get-tuple-element.62), channel_id=1, source_target_pairs={{8,0},{9,1},{10,2},{11,3},{12,4},{13,5},{14,6},{15,7},{0,8},{1,9},... | collective-permute-start | bytes 245768 | tf_op jit(solution)/shard_map/ppermute | solution.py:50
  62.1 1.1 %collective-permute-done.25.refs_8_.refs_1_ = bf16[8,5120]{1,0:T(8,128)(2,1)S(1)} collective-permute-done((bf16[8,5120]{1,0:T(8,128)(2,1)S(1)}, bf16[8,5120]{1,0:T(8,128)(2,1)S(1)}, u32[]{:S(2)}, u32[]{:S(2)}) %collective-permute-start.25) | collective-permute-done | bytes 81952 | tf_op jit(solution)/shard_map/ppermute | solution.py:50
  63.2 0.9 collective-permute-done.26.refs_9_.refs_2_
  64.2 2.3 %expert.1 = (f32[32,5120]{1,0:T(8,128)S(1)}, f32[32,5120]{1,0:T(8,128)S(1)}, f32[32,5120]{1,0:T(8,128)S(1)}, bf16[16,5120]{1,0:T(8,128)(2,1)S(1)}, bf16[16,5120]{1,0:T(8,128)(2,1)S(1)}) custom-call(bf16[5120,640]{1,0:T(8,128)(2,1)S(1)} %bitcast.18, bf16[640,5120]{1,0:T(8,128)(2,1)S(1)} %bitcast.19, bf16[32,5120]{1,0:T(8,128)(2,1)S(1)} %join.3.refs_3_.refs_2_, ...), custom_call_target="tpu_custom_call" | custom-call | flops 1677721600 | bytes 16711680 | tf_op jit(solution)/shard_map/expert/pallas_call | solution.py:142
  66.5 1.5 %collective-permute-start.30 = (bf16[16,5120]{1,0:T(8,128)(2,1)S(1)}, bf16[16,5120]{1,0:T(8,128)(2,1)S(1)}, u32[]{:S(2)}, u32[]{:S(2)}) collective-permute-start(bf16[16,5120]{1,0:T(8,128)(2,1)S(1)} %get-tuple-element.68), channel_id=1, source_target_pairs={{2,0},{3,1},{0,2},{1,3},{6,4},{7,5},{4,6},{5,7},{10,8},{11,9},{8,1... | collective-permute-start | bytes 491528 | tf_op jit(solution)/shard_map/ppermute | solution.py:50
  68.0 0.3 collective-permute-start.27
  68.2 2.0 %collective-permute-start.28 = (bf16[8,5120]{1,0:T(8,128)(2,1)S(1)}, bf16[8,5120]{1,0:T(8,128)(2,1)S(1)}, u32[]{:S(2)}, u32[]{:S(2)}) collective-permute-start(bf16[8,5120]{1,0:T(8,128)(2,1)S(1)} %get-tuple-element.66), channel_id=1, source_target_pairs={{12,0},{13,1},{14,2},{15,3},{8,4},{9,5},{10,6},{11,7},{4,8},{5,9},... | collective-permute-start | bytes 245768 | tf_op jit(solution)/shard_map/ppermute | solution.py:50
  70.3 3.2 %collective-permute-done.28.refs_3_ = bf16[8,5120]{1,0:T(8,128)(2,1)S(1)} collective-permute-done((bf16[8,5120]{1,0:T(8,128)(2,1)S(1)}, bf16[8,5120]{1,0:T(8,128)(2,1)S(1)}, u32[]{:S(2)}, u32[]{:S(2)}) %collective-permute-start.28) | collective-permute-done | bytes 81952 | tf_op jit(solution)/shard_map/ppermute | solution.py:50
  73.5 1.3 %collective-permute-start.31 = (bf16[32,5120]{1,0:T(8,128)(2,1)S(1)}, bf16[32,5120]{1,0:T(8,128)(2,1)S(1)}, u32[]{:S(2)}, u32[]{:S(2)}) collective-permute-start(bf16[32,5120]{1,0:T(8,128)(2,1)S(1)} %add_half.7), channel_id=1, source_target_pairs={{1,0},{0,1},{3,2},{2,3},{5,4},{4,5},{7,6},{6,7},{9,8},{8,9},{11,10... | collective-permute-start | bytes 983048 | tf_op jit(solution)/shard_map/ppermute | solution.py:50
  74.9 0.1 collective-permute-start.29
  75.0 1.3 %collective-permute-start.35 = (f32[8,5120]{1,0:T(8,128)S(1)}, f32[8,5120]{1,0:T(8,128)S(1)}, u32[]{:S(2)}, u32[]{:S(2)}) collective-permute-start(f32[8,5120]{1,0:T(8,128)S(1)} %add_last.2.refs_2_.second_ref), channel_id=1, source_target_pairs={{0,16},{1,17},{2,18},{3,19},{4,20},{5,21},{6,22},{7,23},{8,24},{9,... | collective-permute-start | bytes 491528 | tf_op jit(solution)/shard_map/ppermute | solution.py:27
  76.3 5.0 %collective-permute-done.31.refs_2_ = bf16[32,5120]{1,0:T(8,128)(2,1)S(1)} collective-permute-done((bf16[32,5120]{1,0:T(8,128)(2,1)S(1)}, bf16[32,5120]{1,0:T(8,128)(2,1)S(1)}, u32[]{:S(2)}, u32[]{:S(2)}) %collective-permute-start.31) | collective-permute-done | bytes 327712 | tf_op jit(solution)/shard_map/ppermute | solution.py:50
  81.3 0.1 add_blocks.3
  81.4 0.7 collective-permute-start.32
  82.2 1.6 %collective-permute-start.33 = (bf16[8,5120]{1,0:T(8,128)(2,1)S(1)}, bf16[8,5120]{1,0:T(8,128)(2,1)S(1)}, u32[]{:S(2)}, u32[]{:S(2)}) collective-permute-start(bf16[8,5120]{1,0:T(8,128)(2,1)S(1)} %get-tuple-element.72), channel_id=1, source_target_pairs={{8,0},{9,1},{10,2},{11,3},{12,4},{13,5},{14,6},{15,7},{0,8},{1,9},... | collective-permute-start | bytes 245768 | tf_op jit(solution)/shard_map/ppermute | solution.py:50
  83.7 1.3 %collective-permute-start.34 = (bf16[8,5120]{1,0:T(8,128)(2,1)S(1)}, bf16[8,5120]{1,0:T(8,128)(2,1)S(1)}, u32[]{:S(2)}, u32[]{:S(2)}) collective-permute-start(bf16[8,5120]{1,0:T(8,128)(2,1)S(1)} %get-tuple-element.73), channel_id=1, source_target_pairs={{12,0},{13,1},{14,2},{15,3},{8,4},{9,5},{10,6},{11,7},{4,8},{5,9},... | collective-permute-start | bytes 245768 | tf_op jit(solution)/shard_map/ppermute | solution.py:50
  85.0 0.8 lay_out.1
  85.8 1.4 %collective-permute-done.33.refs_2_ = bf16[8,5120]{1,0:T(8,128)(2,1)S(1)} collective-permute-done((bf16[8,5120]{1,0:T(8,128)(2,1)S(1)}, bf16[8,5120]{1,0:T(8,128)(2,1)S(1)}, u32[]{:S(2)}, u32[]{:S(2)}) %collective-permute-start.33) | collective-permute-done | bytes 81952 | tf_op jit(solution)/shard_map/ppermute | solution.py:50
  87.2 1.7 %collective-permute-done.34.refs_3_ = bf16[8,5120]{1,0:T(8,128)(2,1)S(1)} collective-permute-done((bf16[8,5120]{1,0:T(8,128)(2,1)S(1)}, bf16[8,5120]{1,0:T(8,128)(2,1)S(1)}, u32[]{:S(2)}, u32[]{:S(2)}) %collective-permute-start.34) | collective-permute-done | bytes 81952 | tf_op jit(solution)/shard_map/ppermute | solution.py:50
  89.0 1.3 %collective-permute-start.36 = (f32[8,5248]{1,0:T(8,128)S(1)}, f32[8,5248]{1,0:T(8,128)S(1)}, u32[]{:S(2)}, u32[]{:S(2)}) collective-permute-start(f32[8,5248]{1,0:T(8,128)S(1)} %add_last.3.back_ref), channel_id=1, source_target_pairs={{0,16},{1,17},{2,18},{3,19},{4,20},{5,21},{6,22},{7,23},{8,24},{9,... | collective-permute-start | bytes 503816 | tf_op jit(solution)/shard_map/ppermute | solution.py:17
  90.3 1.5 %finish.2 = bf16[128,5120]{1,0:T(8,128)(2,1)} custom-call(s32[1]{0:T(128)} %bitcast.refs_0_.section, bf16[128,5120]{1,0:T(8,128)(2,1)S(1)} %get-tuple-element.52.res_ref, f32[8,5248]{1,0:T(8,128)S(1)} %add_last.3.back_ref), custom_call_target="tpu_custom_call" | custom-call | flops 32768000 | bytes 3276800 | tf_op jit(solution)/shard_map/finish/pallas_call | solution.py:541
  91.8 8.5 %collective-permute-done.36.back_ref = f32[8,5248]{1,0:T(8,128)S(1)} collective-permute-done((f32[8,5248]{1,0:T(8,128)S(1)}, f32[8,5248]{1,0:T(8,128)S(1)}, u32[]{:S(2)}, u32[]{:S(2)}) %collective-permute-start.36) | collective-permute-done | bytes 167968 | tf_op jit(solution)/shard_map/ppermute | solution.py:17
  100.3 1.5 %finish.3 = bf16[128,5120]{1,0:T(8,128)(2,1)} custom-call(s32[1]{0:T(128)} %bitcast.refs_0_.section, bf16[128,5120]{1,0:T(8,128)(2,1)S(1)} %collective-permute-done.24.refs_7_.res_ref, f32[8,5248]{1,0:T(8,128)S(1)} %collective-permute-done.36.back_ref, bf16[128,5120]{1,0:T(8,128)(2,1)} %get-tuple-element.75.refs_0_), custom_call_target="tpu_custom_call", output_to_operand_aliasing={{}: (3, {})} | custom-call | flops 32768000 | bytes 3276800 | tf_op jit(solution)/shard_map/finish/pallas_call | solution.py:541
  (56 shorter events, 0.5 us)
Async XLA Ops:
  0.6 16.3 %copy-start.5 = (f32[1,128]{1,0:T(1,128)S(1)}, f32[1,128]{1,0:T(1,128)}, u32[]{:S(2)}) copy-start(f32[1,128]{1,0:T(1,128)} %refs_2_.1) | copy-start | bytes 1540
  0.6 16.3 %copy-start.6 = (s32[1,128]{1,0:T(1,128)S(1)}, s32[1,128]{1,0:T(1,128)}, u32[]{:S(2)}) copy-start(s32[1,128]{1,0:T(1,128)} %refs_3_.1) | copy-start | bytes 1540
  0.7 16.3 %copy-start.4 = (f32[1,5120]{1,0:T(1,128)S(1)}, f32[1,5120]{1,0:T(1,128)}, u32[]{:S(2)}) copy-start(f32[1,5120]{1,0:T(1,128)} %refs_1_.1) | copy-start | bytes 61444
  0.7 16.3 %copy-start.1 = (bf16[1,128,5120]{2,1,0:T(8,128)(2,1)S(1)}, bf16[1,128,5120]{2,1,0:T(8,128)(2,1)}, u32[]{:S(2)}) copy-start(bf16[1,128,5120]{2,1,0:T(8,128)(2,1)} %param.9) | copy-start | bytes 3932164
  1.8 1.3 %collective-permute-start = (bf16[8,5120]{1,0:T(8,128)(2,1)S(1)}, bf16[8,5120]{1,0:T(8,128)(2,1)S(1)}, u32[]{:S(2)}, u32[]{:S(2)}) collective-permute-start(bf16[8,5120]{1,0:T(8,128)(2,1)S(1)} %bitcast.25), channel_id=1, source_target_pairs={{0,16},{16,0},{1,17},{17,1},{2,18},{18,2},{3,19},{19,3},{4,20},{20... | collective-permute-start | bytes 245768 | tf_op jit(solution)/shard_map/ppermute | solution.py:22
  2.0 17.7 %copy-start.2 = (bf16[1,128,5120]{2,1,0:T(8,128)(2,1)S(1)}, bf16[1,128,5120]{2,1,0:T(8,128)(2,1)}, u32[]{:S(2)}) copy-start(bf16[1,128,5120]{2,1,0:T(8,128)(2,1)} %param.11) | copy-start | bytes 3932164
  3.2 7.1 %collective-permute-start.3 = (bf16[8,5120]{1,0:T(8,128)(2,1)S(1)}, bf16[8,5120]{1,0:T(8,128)(2,1)S(1)}, u32[]{:S(2)}, u32[]{:S(2)}) collective-permute-start(bf16[8,5120]{1,0:T(8,128)(2,1)S(1)} %broadcast_select_fusion.refs_0_), channel_id=1, source_target_pairs={{0,12},{1,13},{2,14},{3,15},{4,8},{5,9},{6,10},{7,11},{8,4},{9,5},... | collective-permute-start | bytes 245768 | tf_op jit(solution)/shard_map/ppermute | solution.py:50
  7.7 6.6 %collective-permute-start.2 = (bf16[8,5120]{1,0:T(8,128)(2,1)S(1)}, bf16[8,5120]{1,0:T(8,128)(2,1)S(1)}, u32[]{:S(2)}, u32[]{:S(2)}) collective-permute-start(bf16[8,5120]{1,0:T(8,128)(2,1)S(1)} %broadcast_select_fusion.refs_0_), channel_id=1, source_target_pairs={{0,8},{1,9},{2,10},{3,11},{4,12},{5,13},{6,14},{7,15},{8,0},{9,1},... | collective-permute-start | bytes 245768 | tf_op jit(solution)/shard_map/ppermute | solution.py:50
  7.7 6.6 %collective-permute-start.1 = (bf16[8,5120]{1,0:T(8,128)(2,1)S(1)}, bf16[8,5120]{1,0:T(8,128)(2,1)S(1)}, u32[]{:S(2)}, u32[]{:S(2)}) collective-permute-start(bf16[8,5120]{1,0:T(8,128)(2,1)S(1)} %broadcast_select_fusion.refs_0_), channel_id=1, source_target_pairs={{0,4},{1,5},{2,6},{3,7},{4,0},{5,1},{6,2},{7,3},{8,12},{9,13},{10,... | collective-permute-start | bytes 245768 | tf_op jit(solution)/shard_map/ppermute | solution.py:50
  14.4 8.1 %collective-permute-start.7 = (bf16[32,5120]{1,0:T(8,128)(2,1)S(1)}, bf16[32,5120]{1,0:T(8,128)(2,1)S(1)}, u32[]{:S(2)}, u32[]{:S(2)}) collective-permute-start(bf16[32,5120]{1,0:T(8,128)(2,1)S(1)} %join.2.refs_4_), channel_id=1, source_target_pairs={{0,2},{1,3},{2,0},{3,1},{4,6},{5,7},{6,4},{7,5},{8,10},{9,11},{10,... | collective-permute-start | bytes 983048 | tf_op jit(solution)/shard_map/ppermute | solution.py:50
  15.7 8.9 %collective-permute-start.6 = (bf16[32,5120]{1,0:T(8,128)(2,1)S(1)}, bf16[32,5120]{1,0:T(8,128)(2,1)S(1)}, u32[]{:S(2)}, u32[]{:S(2)}) collective-permute-start(bf16[32,5120]{1,0:T(8,128)(2,1)S(1)} %join.2.refs_4_), channel_id=1, source_target_pairs={{0,1},{1,0},{2,3},{3,2},{4,5},{5,4},{6,7},{7,6},{8,9},{9,8},{10,11... | collective-permute-start | bytes 983048 | tf_op jit(solution)/shard_map/ppermute | solution.py:50
  17.8 8.1 %collective-permute-start.4 = (bf16[128,1280]{1,0:T(8,128)(2,1)S(1)}, bf16[128,1280]{1,0:T(8,128)(2,1)S(1)}, u32[]{:S(2)}, u32[]{:S(2)}) collective-permute-start(bf16[128,1280]{1,0:T(8,128)(2,1)S(1)} %get-tuple-element.41), channel_id=1, source_target_pairs={{0,16},{16,0},{1,17},{17,1},{2,18},{18,2},{3,19},{19,3},{4,20},{20... | collective-permute-start | bytes 983048 | tf_op jit(solution)/shard_map/ppermute | solution.py:22
  19.6 7.6 %collective-permute-start.5 = (bf16[128,1280]{1,0:T(8,128)(2,1)S(1)}, bf16[128,1280]{1,0:T(8,128)(2,1)S(1)}, u32[]{:S(2)}, u32[]{:S(2)}) collective-permute-start(bf16[128,1280]{1,0:T(8,128)(2,1)S(1)} %get-tuple-element.42), channel_id=1, source_target_pairs={{0,16},{16,0},{1,17},{17,1},{2,18},{18,2},{3,19},{19,3},{4,20},{20... | collective-permute-start | bytes 983048 | tf_op jit(solution)/shard_map/ppermute | solution.py:22
  19.8 8.7 %collective-permute-start.10 = (bf16[128,1280]{1,0:T(8,128)(2,1)S(1)}, bf16[128,1280]{1,0:T(8,128)(2,1)S(1)}, u32[]{:S(2)}, u32[]{:S(2)}) collective-permute-start(bf16[128,1280]{1,0:T(8,128)(2,1)S(1)} %get-tuple-element.45), channel_id=1, source_target_pairs={{0,16},{16,0},{1,17},{17,1},{2,18},{18,2},{3,19},{19,3},{4,20},{20... | collective-permute-start | bytes 983048 | tf_op jit(solution)/shard_map/ppermute | solution.py:22
  22.5 6.0 %collective-permute-start.11 = (bf16[128,1280]{1,0:T(8,128)(2,1)S(1)}, bf16[128,1280]{1,0:T(8,128)(2,1)S(1)}, u32[]{:S(2)}, u32[]{:S(2)}) collective-permute-start(bf16[128,1280]{1,0:T(8,128)(2,1)S(1)} %get-tuple-element.46), channel_id=1, source_target_pairs={{0,16},{16,0},{1,17},{17,1},{2,18},{18,2},{3,19},{19,3},{4,20},{20... | collective-permute-start | bytes 983048 | tf_op jit(solution)/shard_map/ppermute | solution.py:22
  24.6 4.6 %collective-permute-start.8 = (bf16[16,5120]{1,0:T(8,128)(2,1)S(1)}, bf16[16,5120]{1,0:T(8,128)(2,1)S(1)}, u32[]{:S(2)}, u32[]{:S(2)}) collective-permute-start(bf16[16,5120]{1,0:T(8,128)(2,1)S(1)} %slice.16), channel_id=1, source_target_pairs={{0,1},{1,0},{2,3},{3,2},{4,5},{5,4},{6,7},{7,6},{8,9},{9,8},{10,11... | collective-permute-start | bytes 491528 | tf_op jit(solution)/shard_map/ppermute | solution.py:50
  25.9 4.5 %collective-permute-start.9 = (bf16[16,5120]{1,0:T(8,128)(2,1)S(1)}, bf16[16,5120]{1,0:T(8,128)(2,1)S(1)}, u32[]{:S(2)}, u32[]{:S(2)}) collective-permute-start(bf16[16,5120]{1,0:T(8,128)(2,1)S(1)} %slice.17), channel_id=1, source_target_pairs={{0,2},{1,3},{2,0},{3,1},{4,6},{5,7},{6,4},{7,5},{8,10},{9,11},{10,... | collective-permute-start | bytes 491528 | tf_op jit(solution)/shard_map/ppermute | solution.py:50
  27.2 34.9 %collective-permute-start.24 = (bf16[128,5120]{1,0:T(8,128)(2,1)S(1)}, bf16[128,5120]{1,0:T(8,128)(2,1)S(1)}, u32[]{:S(2)}, u32[]{:S(2)}) collective-permute-start(bf16[128,5120]{1,0:T(8,128)(2,1)S(1)} %get-tuple-element.40.refs_1_), channel_id=1, source_target_pairs={{0,16},{1,17},{2,18},{3,19},{4,20},{5,21},{6,22},{7,23},{8,24},{9,... | collective-permute-start | bytes 3932168 | tf_op jit(solution)/shard_map/ppermute | solution.py:17
  32.5 5.8 %collective-permute-start.12 = (bf16[128,2560]{1,0:T(8,128)(2,1)S(1)}, bf16[128,2560]{1,0:T(8,128)(2,1)S(1)}, u32[]{:S(2)}, u32[]{:S(2)}) collective-permute-start(bf16[128,2560]{1,0:T(8,128)(2,1)S(1)} %get-tuple-element.47.refs_3_), channel_id=1, source_target_pairs={{0,16},{1,17},{2,18},{3,19},{4,20},{5,21},{6,22},{7,23},{8,24},{9,... | collective-permute-start | bytes 1966088 | tf_op jit(solution)/shard_map/ppermute | solution.py:27
  33.8 4.5 %copy-start.3 = (f32[1,5120]{1,0:T(1,128)S(1)}, f32[1,5120]{1,0:T(1,128)}, u32[]{:S(2)}) copy-start(f32[1,5120]{1,0:T(1,128)} %refs_4_.1) | copy-start | bytes 61444
  33.8 30.4 %slice-start = ((s8[6553600]{0:T(1024)(128)(4,1)}), s8[4194304]{0:T(1024)(128)(4,1)S(1)}, s32[]{:S(2)}) async-start(s8[6553600]{0:T(1024)(128)(4,1)} %bitcast.16), calls=%async_computation | async-start | bytes 8388608
  35.8 5.5 %collective-permute-start.17 = (bf16[16,5120]{1,0:T(8,128)(2,1)S(1)}, bf16[16,5120]{1,0:T(8,128)(2,1)S(1)}, u32[]{:S(2)}, u32[]{:S(2)}) collective-permute-start(bf16[16,5120]{1,0:T(8,128)(2,1)S(1)} %get-tuple-element.57), channel_id=1, source_target_pairs={{2,0},{3,1},{0,2},{1,3},{6,4},{7,5},{4,6},{5,7},{10,8},{11,9},{8,1... | collective-permute-start | bytes 491528 | tf_op jit(solution)/shard_map/ppermute | solution.py:50
  38.0 4.6 %collective-permute-start.16 = (bf16[16,5120]{1,0:T(8,128)(2,1)S(1)}, bf16[16,5120]{1,0:T(8,128)(2,1)S(1)}, u32[]{:S(2)}, u32[]{:S(2)}) collective-permute-start(bf16[16,5120]{1,0:T(8,128)(2,1)S(1)} %get-tuple-element.55), channel_id=1, source_target_pairs={{1,0},{0,1},{3,2},{2,3},{5,4},{4,5},{7,6},{6,7},{9,8},{8,9},{11,10... | collective-permute-start | bytes 491528 | tf_op jit(solution)/shard_map/ppermute | solution.py:50
  38.2 25.9 %slice-start.1 = ((s8[6553600]{0:T(1024)(128)(4,1)}), s8[2359296]{0:T(1024)(128)(4,1)S(1)}, s32[]{:S(2)}) async-start(s8[6553600]{0:T(1024)(128)(4,1)} %bitcast.16), calls=%async_computation.1 | async-start | bytes 4718592
  38.2 25.9 %copy-start = (bf16[1,640,5120]{2,1,0:T(8,128)(2,1)S(1)}, bf16[1,640,5120]{2,1,0:T(8,128)(2,1)}, u32[]{:S(2)}) copy-start(bf16[1,640,5120]{2,1,0:T(8,128)(2,1)} %param.15) | copy-start | bytes 19660804
  38.9 5.2 %collective-permute-start.15 = (bf16[8,5120]{1,0:T(8,128)(2,1)S(1)}, bf16[8,5120]{1,0:T(8,128)(2,1)S(1)}, u32[]{:S(2)}, u32[]{:S(2)}) collective-permute-start(bf16[8,5120]{1,0:T(8,128)(2,1)S(1)} %get-tuple-element.53.refs_0_.after_any), channel_id=1, source_target_pairs={{0,12},{1,13},{2,14},{3,15},{4,8},{5,9},{6,10},{7,11},{8,4},{9,5},... | collective-permute-start | bytes 245768 | tf_op jit(solution)/shard_map/ppermute | solution.py:50
  41.3 7.5 %collective-permute-start.14 = (bf16[8,5120]{1,0:T(8,128)(2,1)S(1)}, bf16[8,5120]{1,0:T(8,128)(2,1)S(1)}, u32[]{:S(2)}, u32[]{:S(2)}) collective-permute-start(bf16[8,5120]{1,0:T(8,128)(2,1)S(1)} %get-tuple-element.53.refs_0_.after_any), channel_id=1, source_target_pairs={{0,8},{1,9},{2,10},{3,11},{4,12},{5,13},{6,14},{7,15},{8,0},{9,1},... | collective-permute-start | bytes 245768 | tf_op jit(solution)/shard_map/ppermute | solution.py:50
  41.3 7.5 %collective-permute-start.13 = (bf16[8,5120]{1,0:T(8,128)(2,1)S(1)}, bf16[8,5120]{1,0:T(8,128)(2,1)S(1)}, u32[]{:S(2)}, u32[]{:S(2)}) collective-permute-start(bf16[8,5120]{1,0:T(8,128)(2,1)S(1)} %get-tuple-element.53.refs_0_.after_any), channel_id=1, source_target_pairs={{0,4},{1,5},{2,6},{3,7},{4,0},{5,1},{6,2},{7,3},{8,12},{9,13},{10,... | collective-permute-start | bytes 245768 | tf_op jit(solution)/shard_map/ppermute | solution.py:50
  42.6 7.6 %collective-permute-start.21 = (bf16[32,5120]{1,0:T(8,128)(2,1)S(1)}, bf16[32,5120]{1,0:T(8,128)(2,1)S(1)}, u32[]{:S(2)}, u32[]{:S(2)}) collective-permute-start(bf16[32,5120]{1,0:T(8,128)(2,1)S(1)} %add_half.5.refs_5_), channel_id=1, source_target_pairs={{1,0},{0,1},{3,2},{2,3},{5,4},{4,5},{7,6},{6,7},{9,8},{8,9},{11,10... | collective-permute-start | bytes 983048 | tf_op jit(solution)/shard_map/ppermute | solution.py:50
  44.1 6.2 %collective-permute-start.20 = (bf16[32,5120]{1,0:T(8,128)(2,1)S(1)}, bf16[32,5120]{1,0:T(8,128)(2,1)S(1)}, u32[]{:S(2)}, u32[]{:S(2)}) collective-permute-start(bf16[32,5120]{1,0:T(8,128)(2,1)S(1)} %add_half.4.refs_4_), channel_id=1, source_target_pairs={{2,0},{3,1},{0,2},{1,3},{6,4},{7,5},{4,6},{5,7},{10,8},{11,9},{8,1... | collective-permute-start | bytes 983048 | tf_op jit(solution)/shard_map/ppermute | solution.py:50
  48.8 9.8 %collective-permute-start.19 = (bf16[32,5120]{1,0:T(8,128)(2,1)S(1)}, bf16[32,5120]{1,0:T(8,128)(2,1)S(1)}, u32[]{:S(2)}, u32[]{:S(2)}) collective-permute-start(bf16[32,5120]{1,0:T(8,128)(2,1)S(1)} %join.3.refs_3_.refs_2_), channel_id=1, source_target_pairs={{0,2},{1,3},{2,0},{3,1},{4,6},{5,7},{6,4},{7,5},{8,10},{9,11},{10,... | collective-permute-start | bytes 983048 | tf_op jit(solution)/shard_map/ppermute | solution.py:50
  49.4 9.2 %collective-permute-start.18 = (bf16[32,5120]{1,0:T(8,128)(2,1)S(1)}, bf16[32,5120]{1,0:T(8,128)(2,1)S(1)}, u32[]{:S(2)}, u32[]{:S(2)}) collective-permute-start(bf16[32,5120]{1,0:T(8,128)(2,1)S(1)} %join.3.refs_3_.refs_2_), channel_id=1, source_target_pairs={{0,1},{1,0},{2,3},{3,2},{4,5},{5,4},{6,7},{7,6},{8,9},{9,8},{10,11... | collective-permute-start | bytes 983048 | tf_op jit(solution)/shard_map/ppermute | solution.py:50
  58.6 5.5 %collective-permute-start.22 = (bf16[16,5120]{1,0:T(8,128)(2,1)S(1)}, bf16[16,5120]{1,0:T(8,128)(2,1)S(1)}, u32[]{:S(2)}, u32[]{:S(2)}) collective-permute-start(bf16[16,5120]{1,0:T(8,128)(2,1)S(1)} %get-tuple-element.59), channel_id=1, source_target_pairs={{0,1},{1,0},{2,3},{3,2},{4,5},{5,4},{6,7},{7,6},{8,9},{9,8},{10,11... | collective-permute-start | bytes 491528 | tf_op jit(solution)/shard_map/ppermute | solution.py:50
  59.9 4.2 %collective-permute-start.23 = (bf16[16,5120]{1,0:T(8,128)(2,1)S(1)}, bf16[16,5120]{1,0:T(8,128)(2,1)S(1)}, u32[]{:S(2)}, u32[]{:S(2)}) collective-permute-start(bf16[16,5120]{1,0:T(8,128)(2,1)S(1)} %get-tuple-element.60), channel_id=1, source_target_pairs={{0,2},{1,3},{2,0},{3,1},{4,6},{5,7},{6,4},{7,5},{8,10},{9,11},{10,... | collective-permute-start | bytes 491528 | tf_op jit(solution)/shard_map/ppermute | solution.py:50
  59.9 3.3 %collective-permute-start.25 = (bf16[8,5120]{1,0:T(8,128)(2,1)S(1)}, bf16[8,5120]{1,0:T(8,128)(2,1)S(1)}, u32[]{:S(2)}, u32[]{:S(2)}) collective-permute-start(bf16[8,5120]{1,0:T(8,128)(2,1)S(1)} %get-tuple-element.61), channel_id=1, source_target_pairs={{4,0},{5,1},{6,2},{7,3},{0,4},{1,5},{2,6},{3,7},{12,8},{13,9},{14,... | collective-permute-start | bytes 245768 | tf_op jit(solution)/shard_map/ppermute | solution.py:50
  59.9 4.2 %collective-permute-start.26 = (bf16[8,5120]{1,0:T(8,128)(2,1)S(1)}, bf16[8,5120]{1,0:T(8,128)(2,1)S(1)}, u32[]{:S(2)}, u32[]{:S(2)}) collective-permute-start(bf16[8,5120]{1,0:T(8,128)(2,1)S(1)} %get-tuple-element.62), channel_id=1, source_target_pairs={{8,0},{9,1},{10,2},{11,3},{12,4},{13,5},{14,6},{15,7},{0,8},{1,9},... | collective-permute-start | bytes 245768 | tf_op jit(solution)/shard_map/ppermute | solution.py:50
  66.5 7.0 %collective-permute-start.30 = (bf16[16,5120]{1,0:T(8,128)(2,1)S(1)}, bf16[16,5120]{1,0:T(8,128)(2,1)S(1)}, u32[]{:S(2)}, u32[]{:S(2)}) collective-permute-start(bf16[16,5120]{1,0:T(8,128)(2,1)S(1)} %get-tuple-element.68), channel_id=1, source_target_pairs={{2,0},{3,1},{0,2},{1,3},{6,4},{7,5},{4,6},{5,7},{10,8},{11,9},{8,1... | collective-permute-start | bytes 491528 | tf_op jit(solution)/shard_map/ppermute | solution.py:50
  68.0 6.8 %collective-permute-start.27 = (bf16[16,5120]{1,0:T(8,128)(2,1)S(1)}, bf16[16,5120]{1,0:T(8,128)(2,1)S(1)}, u32[]{:S(2)}, u32[]{:S(2)}) collective-permute-start(bf16[16,5120]{1,0:T(8,128)(2,1)S(1)} %get-tuple-element.65), channel_id=1, source_target_pairs={{1,0},{0,1},{3,2},{2,3},{5,4},{4,5},{7,6},{6,7},{9,8},{8,9},{11,10... | collective-permute-start | bytes 491528 | tf_op jit(solution)/shard_map/ppermute | solution.py:50
  68.2 5.2 %collective-permute-start.28 = (bf16[8,5120]{1,0:T(8,128)(2,1)S(1)}, bf16[8,5120]{1,0:T(8,128)(2,1)S(1)}, u32[]{:S(2)}, u32[]{:S(2)}) collective-permute-start(bf16[8,5120]{1,0:T(8,128)(2,1)S(1)} %get-tuple-element.66), channel_id=1, source_target_pairs={{12,0},{13,1},{14,2},{15,3},{8,4},{9,5},{10,6},{11,7},{4,8},{5,9},... | collective-permute-start | bytes 245768 | tf_op jit(solution)/shard_map/ppermute | solution.py:50
  73.5 7.7 %collective-permute-start.31 = (bf16[32,5120]{1,0:T(8,128)(2,1)S(1)}, bf16[32,5120]{1,0:T(8,128)(2,1)S(1)}, u32[]{:S(2)}, u32[]{:S(2)}) collective-permute-start(bf16[32,5120]{1,0:T(8,128)(2,1)S(1)} %add_half.7), channel_id=1, source_target_pairs={{1,0},{0,1},{3,2},{2,3},{5,4},{4,5},{7,6},{6,7},{9,8},{8,9},{11,10... | collective-permute-start | bytes 983048 | tf_op jit(solution)/shard_map/ppermute | solution.py:50
  74.9 6.4 %collective-permute-start.29 = (bf16[32,5120]{1,0:T(8,128)(2,1)S(1)}, bf16[32,5120]{1,0:T(8,128)(2,1)S(1)}, u32[]{:S(2)}, u32[]{:S(2)}) collective-permute-start(bf16[32,5120]{1,0:T(8,128)(2,1)S(1)} %add_half.6), channel_id=1, source_target_pairs={{2,0},{3,1},{0,2},{1,3},{6,4},{7,5},{4,6},{5,7},{10,8},{11,9},{8,1... | collective-permute-start | bytes 983048 | tf_op jit(solution)/shard_map/ppermute | solution.py:50
  75.0 10.0 %collective-permute-start.35 = (f32[8,5120]{1,0:T(8,128)S(1)}, f32[8,5120]{1,0:T(8,128)S(1)}, u32[]{:S(2)}, u32[]{:S(2)}) collective-permute-start(f32[8,5120]{1,0:T(8,128)S(1)} %add_last.2.refs_2_.second_ref), channel_id=1, source_target_pairs={{0,16},{1,17},{2,18},{3,19},{4,20},{5,21},{6,22},{7,23},{8,24},{9,... | collective-permute-start | bytes 491528 | tf_op jit(solution)/shard_map/ppermute | solution.py:27
  81.4 4.4 %collective-permute-start.32 = (bf16[8,5120]{1,0:T(8,128)(2,1)S(1)}, bf16[8,5120]{1,0:T(8,128)(2,1)S(1)}, u32[]{:S(2)}, u32[]{:S(2)}) collective-permute-start(bf16[8,5120]{1,0:T(8,128)(2,1)S(1)} %get-tuple-element.71), channel_id=1, source_target_pairs={{4,0},{5,1},{6,2},{7,3},{0,4},{1,5},{2,6},{3,7},{12,8},{13,9},{14,... | collective-permute-start | bytes 245768 | tf_op jit(solution)/shard_map/ppermute | solution.py:50
  82.2 5.1 %collective-permute-start.33 = (bf16[8,5120]{1,0:T(8,128)(2,1)S(1)}, bf16[8,5120]{1,0:T(8,128)(2,1)S(1)}, u32[]{:S(2)}, u32[]{:S(2)}) collective-permute-start(bf16[8,5120]{1,0:T(8,128)(2,1)S(1)} %get-tuple-element.72), channel_id=1, source_target_pairs={{8,0},{9,1},{10,2},{11,3},{12,4},{13,5},{14,6},{15,7},{0,8},{1,9},... | collective-permute-start | bytes 245768 | tf_op jit(solution)/shard_map/ppermute | solution.py:50
  83.7 5.2 %collective-permute-start.34 = (bf16[8,5120]{1,0:T(8,128)(2,1)S(1)}, bf16[8,5120]{1,0:T(8,128)(2,1)S(1)}, u32[]{:S(2)}, u32[]{:S(2)}) collective-permute-start(bf16[8,5120]{1,0:T(8,128)(2,1)S(1)} %get-tuple-element.73), channel_id=1, source_target_pairs={{12,0},{13,1},{14,2},{15,3},{8,4},{9,5},{10,6},{11,7},{4,8},{5,9},... | collective-permute-start | bytes 245768 | tf_op jit(solution)/shard_map/ppermute | solution.py:50
  89.0 11.4 %collective-permute-start.36 = (f32[8,5248]{1,0:T(8,128)S(1)}, f32[8,5248]{1,0:T(8,128)S(1)}, u32[]{:S(2)}, u32[]{:S(2)}) collective-permute-start(f32[8,5248]{1,0:T(8,128)S(1)} %add_last.3.back_ref), channel_id=1, source_target_pairs={{0,16},{1,17},{2,18},{3,19},{4,20},{5,21},{6,22},{7,23},{8,24},{9,... | collective-permute-start | bytes 503816 | tf_op jit(solution)/shard_map/ppermute | solution.py:17

commit v8 on v7

--- a/solution.py
+++ b/solution.py
@@ -460,19 +460,15 @@
     rows, width = first.shape
     half = width // 2
 
-    def kernel(section, first_ref, second_ref, out_ref, after_ref):
+    def kernel(section, first_ref, second_ref, out_ref):
         decodes = jnp.full((rows, 1), section[0]) >= sections // 2
-        after_ref[...] = jnp.zeros_like(after_ref)
         for at, ref in ((0, first_ref), (half, second_ref)):
             for side in (0, 1):
                 block = jnp.where(decodes, ref[:, side * half : (side + 1) * half], 0.0)
                 out_ref[:, side, at : at + half] = block
 
-    outs = [
-        jax.ShapeDtypeStruct((rows, 2, width), jnp.float32),
-        jax.ShapeDtypeStruct((8, HD), jnp.float32),
-    ]
-    return local_kernel(kernel, "lay_out", outs, [section.reshape(1), first, second], scalars=1)
+    one = jax.ShapeDtypeStruct((rows, 2, width), jnp.float32)
+    return local_kernel(kernel, "lay_out", [one], [section.reshape(1), first, second], scalars=1)[0]
 
 
 def blank(section, after, like):
@@ -507,7 +503,8 @@
     parts = [slice(at, at + step) for at in range(0, width, step)]
 
     def kernel(section, res_ref, back_ref, *refs):
-        out_any, out_ref, sems = refs[-3:]
+        out_any, after_ref, out_ref, sems = refs[-4:]
+        after_ref[...] = jnp.zeros_like(after_ref)
 
         def compute():
             gate, slot = back_ref[0:1, width:], back_ref[1:2, width:]
@@ -540,9 +537,9 @@
     aliased = [] if room is None else [pl.BlockSpec(memory_space=pltpu.HBM)]
     return pl.pallas_call(
         kernel,
-        out_shape=one,
+        out_shape=(one, jax.ShapeDtypeStruct((8, HD), jnp.float32)),
         in_specs=[pl.BlockSpec(memory_space=pltpu.SMEM), *in_vmem(2), *aliased],
-        out_specs=pl.BlockSpec(memory_space=pltpu.HBM),
+        out_specs=(pl.BlockSpec(memory_space=pltpu.HBM), in_vmem(1)[0]),
         scratch_shapes=[
             pltpu.VMEM(one.shape, one.dtype),
             pltpu.SemaphoreType.DMA((len(parts),)),
@@ -599,27 +596,29 @@
     residual_before = passed_along(current if sections == 2 else residual, "section", 1)
     grads = grid.scatter(parts, own_rows)
     halves = next(grads)
+    room, made = blank(section, capacity, residual)
     sums = []
 
     def plane_sums(own):
         if not sums:
             sums.append(grads.send([own]))
-        return [sums[0][0][0]]
+        return [sums[0][0][0], made]
 
     gathered = grid.gather(capacity, halves, plane_sums)
+    moved = sums[0][1]
     computed = expert(
-        expert_in[0], expert_out[0], gathered, grid.heights(CAP), grid.types(), [residual_before, *sums[0][1][:2]]
-    )
-    total_grad = grads.send([computed[0]])
-    room, made = blank(section, capacity, residual)
-    results = grid.scatter(computed, CAP, [total_grad], gates)
+        expert_in[0], expert_out[0], gathered, grid.heights(CAP), grid.types(),
+        [residual_before, *moved[:1]],
+    )
+    results = grid.scatter(computed, CAP, moved[1:2], gates)
     next(results)
-    results.send([made])
-    total_grad, laid = lay_out(section, sections, to_decoder(total_grad), total_grad)
-    returned = results.send([laid])
+    results.send(moved[2:])
+    returned = results.send([])
     returned_before = passed_along(returned, "section", 1)
-    output = finish(section, residual, returned)
-    arriving = finish(section, residual_before, returned_before, room)
+    output, done = finish(section, residual, returned)
+    arriving, _ = finish(section, residual_before, returned_before, room)
+    total_grad = grads.send([done])
+    total_grad = lay_out(section, sections, to_decoder(total_grad), total_grad)
     return (output[None], arriving[None], total_grad[None])
 
 

time: 102 us -> 106 us (1.039)
  waiting for transfers between devices: 46.1 us -> 51 us
  starting transfers between devices: 41.2 us -> 39.3 us
    ppermute x2, waiting for transfers between devices: 0.01 us -> 10.6 us  [to_decoder(): lax.ppermute(block, 'section', [(i, i + apart) for i in range(apart)])]
    ppermute x2, waiting for transfers between devices: 8.55 us -> 0.01 us  [passed_along(): return lax.ppermute(block, axis, route)]
    ppermute x28, waiting for transfers between devices: 36.4 us -> 39.2 us  [shift(): return lax.ppermute(block, 'expert', route)]
    ppermute x28, starting transfers between devices: 31.4 us -> 29.5 us  [shift(): return lax.ppermute(block, 'expert', route)]
  transfers between devices with their start and end apart: 37 -> 37, of which waited for: 17 -> 18; matrix products, arithmetic and copies ran while one was open for 0% -> 0% of each run, Pallas kernels for 8% -> 8%
where the time goes in v8:
time: 106 us; the launch traced here: 105 us
  waiting for transfers between devices  51 us (48%)
  starting transfers between devices  39.3 us (37%)
  Pallas kernels  12.8 us (12%)
  local copies, waits for them, and re-layouts  1.24 us (1%)
    ppermute x28, waiting for transfers between devices, shift(): return lax.ppermute(block, 'expert', route)  39.2 us
    ppermute x28, starting transfers between devices, shift(): return lax.ppermute(block, 'expert', route)  29.5 us
    ppermute x2, waiting for transfers between devices, to_decoder(): lax.ppermute(block, 'section', [(i, i + apart) for i in range(apart)])  10.6 us
    pallas_call x18, Pallas kernels, local_kernel(): pl.pallas_call(body, out_shape=tuple(outs), in_specs=in_specs, out_specs=...  9.22 us
    ppermute x5, starting transfers between devices, swapped(): lax.ppermute(block, 'section', [(i, (i + sections // 2) % sections) for i...  4.61 us
    pallas_call x2, Pallas kernels, finish(): pl.pallas_call(kernel, out_shape=(one, jax.ShapeDtypeStruct((8, HD), jnp....  3.61 us
    ppermute x2, starting transfers between devices, to_decoder(): lax.ppermute(block, 'section', [(i, i + apart) for i in range(apart)])  2.58 us
    ppermute x2, starting transfers between devices, passed_along(): return lax.ppermute(block, axis, route)  2.57 us
  transfers between devices with their start and end apart: 37, of which 18 were waited for; matrix products, arithmetic and copies ran while one was open for 0% of the time, Pallas kernels for 8%

profile of v8, /device:TPU:1, one launch (start us, length us, event | category | flops | bytes accessed | tf_op | source)
XLA Modules:
  0.0 105.4 jit_solution(12294467835903525905)
XLA Ops:
  0.7 1.1 %slice_bitcast_fusion = (bf16[1,8,2,2560]{3,2,1,0:T(2,128)(2,1)S(1)}, bf16[1,8,2,2560]{3,2,1,0:T(2,128)(2,1)S(1)}) fusion(bf16[1,8,2,5120]{3,2,1,0:T(2,128)(2,1)} %param.10), kind=kLoop, calls=%fused_computation | loop fusion | bytes 327680
  1.8 0.1 collective-permute-start
  2.0 1.2 %collective-permute-done = bf16[8,5120]{1,0:T(8,128)(2,1)S(1)} collective-permute-done((bf16[8,5120]{1,0:T(8,128)(2,1)S(1)}, bf16[8,5120]{1,0:T(8,128)(2,1)S(1)}, u32[]{:S(2)}, u32[]{:S(2)}) %collective-permute-start) | collective-permute-done | bytes 81952 | tf_op jit(solution)/shard_map/ppermute | solution.py:22
  3.2 4.5 %collective-permute-start.3 = (bf16[8,5120]{1,0:T(8,128)(2,1)S(1)}, bf16[8,5120]{1,0:T(8,128)(2,1)S(1)}, u32[]{:S(2)}, u32[]{:S(2)}) collective-permute-start(bf16[8,5120]{1,0:T(8,128)(2,1)S(1)} %broadcast_select_fusion.refs_0_), channel_id=1, source_target_pairs={{0,12},{1,13},{2,14},{3,15},{4,8},{5,9},{6,10},{7,11},{8,4},{9,5},... | collective-permute-start | bytes 245768 | tf_op jit(solution)/shard_map/ppermute | solution.py:50
  7.7 0.4 collective-permute-start.1
  8.1 2.2 %collective-permute-done.3.refs_3_ = bf16[8,5120]{1,0:T(8,128)(2,1)S(1)} collective-permute-done((bf16[8,5120]{1,0:T(8,128)(2,1)S(1)}, bf16[8,5120]{1,0:T(8,128)(2,1)S(1)}, u32[]{:S(2)}, u32[]{:S(2)}) %collective-permute-start.3) | collective-permute-done | bytes 81952 | tf_op jit(solution)/shard_map/ppermute | solution.py:50
  10.3 4.1 %collective-permute-done.2.refs_2_ = bf16[8,5120]{1,0:T(8,128)(2,1)S(1)} collective-permute-done((bf16[8,5120]{1,0:T(8,128)(2,1)S(1)}, bf16[8,5120]{1,0:T(8,128)(2,1)S(1)}, u32[]{:S(2)}, u32[]{:S(2)}) %collective-permute-start.2) | collective-permute-done | bytes 81952 | tf_op jit(solution)/shard_map/ppermute | solution.py:50
  14.4 1.3 %collective-permute-start.7 = (bf16[32,5120]{1,0:T(8,128)(2,1)S(1)}, bf16[32,5120]{1,0:T(8,128)(2,1)S(1)}, u32[]{:S(2)}, u32[]{:S(2)}) collective-permute-start(bf16[32,5120]{1,0:T(8,128)(2,1)S(1)} %join.2.refs_4_), channel_id=1, source_target_pairs={{0,2},{1,3},{2,0},{3,1},{4,6},{5,7},{6,4},{7,5},{8,10},{9,11},{10,... | collective-permute-start | bytes 983048 | tf_op jit(solution)/shard_map/ppermute | solution.py:50
  15.7 1.2 %collective-permute-start.6 = (bf16[32,5120]{1,0:T(8,128)(2,1)S(1)}, bf16[32,5120]{1,0:T(8,128)(2,1)S(1)}, u32[]{:S(2)}, u32[]{:S(2)}) collective-permute-start(bf16[32,5120]{1,0:T(8,128)(2,1)S(1)} %join.2.refs_4_), channel_id=1, source_target_pairs={{0,1},{1,0},{2,3},{3,2},{4,5},{5,4},{6,7},{7,6},{8,9},{9,8},{10,11... | collective-permute-start | bytes 983048 | tf_op jit(solution)/shard_map/ppermute | solution.py:50
  16.9 0.9 queries.1
  17.8 1.8 %collective-permute-start.4 = (bf16[128,1280]{1,0:T(8,128)(2,1)S(1)}, bf16[128,1280]{1,0:T(8,128)(2,1)S(1)}, u32[]{:S(2)}, u32[]{:S(2)}) collective-permute-start(bf16[128,1280]{1,0:T(8,128)(2,1)S(1)} %get-tuple-element.42), channel_id=1, source_target_pairs={{0,16},{16,0},{1,17},{17,1},{2,18},{18,2},{3,19},{19,3},{4,20},{20... | collective-permute-start | bytes 983048 | tf_op jit(solution)/shard_map/ppermute | solution.py:22
  19.6 0.1 collective-permute-start.5
  19.7 0.1 cut.1
  19.8 0.5 collective-permute-start.10
  20.3 2.2 %collective-permute-done.7.refs_6_ = bf16[32,5120]{1,0:T(8,128)(2,1)S(1)} collective-permute-done((bf16[32,5120]{1,0:T(8,128)(2,1)S(1)}, bf16[32,5120]{1,0:T(8,128)(2,1)S(1)}, u32[]{:S(2)}, u32[]{:S(2)}) %collective-permute-start.7) | collective-permute-done | bytes 327712 | tf_op jit(solution)/shard_map/ppermute | solution.py:50
  22.5 2.1 %collective-permute-start.11 = (bf16[128,1280]{1,0:T(8,128)(2,1)S(1)}, bf16[128,1280]{1,0:T(8,128)(2,1)S(1)}, u32[]{:S(2)}, u32[]{:S(2)}) collective-permute-start(bf16[128,1280]{1,0:T(8,128)(2,1)S(1)} %get-tuple-element.47), channel_id=1, source_target_pairs={{0,16},{16,0},{1,17},{17,1},{2,18},{18,2},{3,19},{19,3},{4,20},{20... | collective-permute-start | bytes 983048 | tf_op jit(solution)/shard_map/ppermute | solution.py:22
  24.6 1.3 %collective-permute-start.8 = (bf16[16,5120]{1,0:T(8,128)(2,1)S(1)}, bf16[16,5120]{1,0:T(8,128)(2,1)S(1)}, u32[]{:S(2)}, u32[]{:S(2)}) collective-permute-start(bf16[16,5120]{1,0:T(8,128)(2,1)S(1)} %slice.16), channel_id=1, source_target_pairs={{0,1},{1,0},{2,3},{3,2},{4,5},{5,4},{6,7},{7,6},{8,9},{9,8},{10,11... | collective-permute-start | bytes 491528 | tf_op jit(solution)/shard_map/ppermute | solution.py:50
  25.9 1.3 %collective-permute-start.9 = (bf16[16,5120]{1,0:T(8,128)(2,1)S(1)}, bf16[16,5120]{1,0:T(8,128)(2,1)S(1)}, u32[]{:S(2)}, u32[]{:S(2)}) collective-permute-start(bf16[16,5120]{1,0:T(8,128)(2,1)S(1)} %slice.17), channel_id=1, source_target_pairs={{0,2},{1,3},{2,0},{3,1},{4,6},{5,7},{6,4},{7,5},{8,10},{9,11},{10,... | collective-permute-start | bytes 491528 | tf_op jit(solution)/shard_map/ppermute | solution.py:50
  27.2 1.3 %collective-permute-start.24 = (bf16[128,5120]{1,0:T(8,128)(2,1)S(1)}, bf16[128,5120]{1,0:T(8,128)(2,1)S(1)}, u32[]{:S(2)}, u32[]{:S(2)}) collective-permute-start(bf16[128,5120]{1,0:T(8,128)(2,1)S(1)} %get-tuple-element.41.refs_1_), channel_id=1, source_target_pairs={{0,16},{1,17},{2,18},{3,19},{4,20},{5,21},{6,22},{7,23},{8,24},{9,... | collective-permute-start | bytes 3932168 | tf_op jit(solution)/shard_map/ppermute | solution.py:17
  28.5 0.7 collective-permute-done.8.refs_7_
  29.2 1.2 %collective-permute-done.9.refs_8_ = bf16[16,5120]{1,0:T(8,128)(2,1)S(1)} collective-permute-done((bf16[16,5120]{1,0:T(8,128)(2,1)S(1)}, bf16[16,5120]{1,0:T(8,128)(2,1)S(1)}, u32[]{:S(2)}, u32[]{:S(2)}) %collective-permute-start.9) | collective-permute-done | bytes 163872 | tf_op jit(solution)/shard_map/ppermute | solution.py:50
  30.4 2.0 %attend.1 = (bf16[128,2560]{1,0:T(8,128)(2,1)S(1)}, f32[20,128,128]{2,1,0:T(8,128)S(1)}, bf16[128,2560]{1,0:T(8,128)(2,1)S(1)}) custom-call(s32[1]{0:T(128)} %bitcast.refs_0_.section, bf16[128,1280]{1,0:T(8,128)(2,1)S(1)} %collective-permute-done.4.refs_1_, bf16[128,1280]{1,0:T(8,128)(2,1)S(1)} %collective-permute-done.5.refs_2_, ...), custom_call_target="tpu_custom_call" | custom-call | flops 167772160 | bytes 5242884 | tf_op jit(solution)/shard_map/attend/pallas_call | solution.py:142
  32.5 1.3 %collective-permute-start.12 = (bf16[128,2560]{1,0:T(8,128)(2,1)S(1)}, bf16[128,2560]{1,0:T(8,128)(2,1)S(1)}, u32[]{:S(2)}, u32[]{:S(2)}) collective-permute-start(bf16[128,2560]{1,0:T(8,128)(2,1)S(1)} %get-tuple-element.48.refs_3_), channel_id=1, source_target_pairs={{0,16},{1,17},{2,18},{3,19},{4,20},{5,21},{6,22},{7,23},{8,24},{9,... | collective-permute-start | bytes 1966088 | tf_op jit(solution)/shard_map/ppermute | solution.py:27
  33.8 2.0 %gradient.1 = (f32[32,5120]{1,0:T(8,128)S(1)}, f32[32,5120]{1,0:T(8,128)S(1)}, f32[32,5120]{1,0:T(8,128)S(1)}, bf16[16,5120]{1,0:T(8,128)(2,1)S(1)}, bf16[16,5120]{1,0:T(8,128)(2,1)S(1)}) custom-call(s32[1]{0:T(128)} %bitcast.refs_0_.section, bf16[128,2560]{1,0:T(8,128)(2,1)S(1)} %get-tuple-element.49.q_ref, ...), custom_call_target="tpu_custom_call" | custom-call | flops 419430400 | bytes 6881284 | tf_op jit(solution)/shard_map/gradient/pallas_call | solution.py:142
  35.8 2.2 %collective-permute-start.17 = (bf16[16,5120]{1,0:T(8,128)(2,1)S(1)}, bf16[16,5120]{1,0:T(8,128)(2,1)S(1)}, u32[]{:S(2)}, u32[]{:S(2)}) collective-permute-start(bf16[16,5120]{1,0:T(8,128)(2,1)S(1)} %get-tuple-element.58), channel_id=1, source_target_pairs={{2,0},{3,1},{0,2},{1,3},{6,4},{7,5},{4,6},{5,7},{10,8},{11,9},{8,1... | collective-permute-start | bytes 491528 | tf_op jit(solution)/shard_map/ppermute | solution.py:50
  38.0 0.3 collective-permute-start.16
  38.3 0.6 settle.1
  38.9 2.4 %collective-permute-start.15 = (bf16[8,5120]{1,0:T(8,128)(2,1)S(1)}, bf16[8,5120]{1,0:T(8,128)(2,1)S(1)}, u32[]{:S(2)}, u32[]{:S(2)}) collective-permute-start(bf16[8,5120]{1,0:T(8,128)(2,1)S(1)} %get-tuple-element.54.refs_0_.after_any), channel_id=1, source_target_pairs={{0,12},{1,13},{2,14},{3,15},{4,8},{5,9},{6,10},{7,11},{8,4},{9,5},... | collective-permute-start | bytes 245768 | tf_op jit(solution)/shard_map/ppermute | solution.py:50
  41.3 1.2 %collective-permute-start.13 = (bf16[8,5120]{1,0:T(8,128)(2,1)S(1)}, bf16[8,5120]{1,0:T(8,128)(2,1)S(1)}, u32[]{:S(2)}, u32[]{:S(2)}) collective-permute-start(bf16[8,5120]{1,0:T(8,128)(2,1)S(1)} %get-tuple-element.54.refs_0_.after_any), channel_id=1, source_target_pairs={{0,4},{1,5},{2,6},{3,7},{4,0},{5,1},{6,2},{7,3},{8,12},{9,13},{10,... | collective-permute-start | bytes 245768 | tf_op jit(solution)/shard_map/ppermute | solution.py:50
  42.6 1.3 %collective-permute-start.21 = (bf16[32,5120]{1,0:T(8,128)(2,1)S(1)}, bf16[32,5120]{1,0:T(8,128)(2,1)S(1)}, u32[]{:S(2)}, u32[]{:S(2)}) collective-permute-start(bf16[32,5120]{1,0:T(8,128)(2,1)S(1)} %add_half.5.refs_5_), channel_id=1, source_target_pairs={{1,0},{0,1},{3,2},{2,3},{5,4},{4,5},{7,6},{6,7},{9,8},{8,9},{11,10... | collective-permute-start | bytes 983048 | tf_op jit(solution)/shard_map/ppermute | solution.py:50
  43.9 0.2 collective-permute-done.15.refs_3_
  44.1 0.5 collective-permute-start.20
  44.5 4.2 %collective-permute-done.14.refs_2_ = bf16[8,5120]{1,0:T(8,128)(2,1)S(1)} collective-permute-done((bf16[8,5120]{1,0:T(8,128)(2,1)S(1)}, bf16[8,5120]{1,0:T(8,128)(2,1)S(1)}, u32[]{:S(2)}, u32[]{:S(2)}) %collective-permute-start.14) | collective-permute-done | bytes 81952 | tf_op jit(solution)/shard_map/ppermute | solution.py:50
  48.8 0.6 collective-permute-start.19
  49.4 0.8 collective-permute-start.18
  50.2 0.1 collective-permute-done.20.refs_1_
  50.3 0.1 add_blocks.2
  50.4 8.2 %collective-permute-done.19.refs_0_.refs_4_ = bf16[32,5120]{1,0:T(8,128)(2,1)S(1)} collective-permute-done((bf16[32,5120]{1,0:T(8,128)(2,1)S(1)}, bf16[32,5120]{1,0:T(8,128)(2,1)S(1)}, u32[]{:S(2)}, u32[]{:S(2)}) %collective-permute-start.19) | collective-permute-done | bytes 327712 | tf_op jit(solution)/shard_map/ppermute | solution.py:50
  58.6 1.3 %collective-permute-start.22 = (bf16[16,5120]{1,0:T(8,128)(2,1)S(1)}, bf16[16,5120]{1,0:T(8,128)(2,1)S(1)}, u32[]{:S(2)}, u32[]{:S(2)}) collective-permute-start(bf16[16,5120]{1,0:T(8,128)(2,1)S(1)} %get-tuple-element.61), channel_id=1, source_target_pairs={{0,1},{1,0},{2,3},{3,2},{4,5},{5,4},{6,7},{7,6},{8,9},{9,8},{10,11... | collective-permute-start | bytes 491528 | tf_op jit(solution)/shard_map/ppermute | solution.py:50
  59.9 0.0 collective-permute-start.23
  59.9 3.3 %collective-permute-done.25.refs_8_.refs_1_ = bf16[8,5120]{1,0:T(8,128)(2,1)S(1)} collective-permute-done((bf16[8,5120]{1,0:T(8,128)(2,1)S(1)}, bf16[8,5120]{1,0:T(8,128)(2,1)S(1)}, u32[]{:S(2)}, u32[]{:S(2)}) %collective-permute-start.25) | collective-permute-done | bytes 81952 | tf_op jit(solution)/shard_map/ppermute | solution.py:50
  63.2 0.8 collective-permute-done.23.refs_6_
  64.1 2.3 %expert.1 = (f32[32,5120]{1,0:T(8,128)S(1)}, f32[32,5120]{1,0:T(8,128)S(1)}, f32[32,5120]{1,0:T(8,128)S(1)}, bf16[16,5120]{1,0:T(8,128)(2,1)S(1)}, bf16[16,5120]{1,0:T(8,128)(2,1)S(1)}) custom-call(bf16[5120,640]{1,0:T(8,128)(2,1)S(1)} %bitcast.18, bf16[640,5120]{1,0:T(8,128)(2,1)S(1)} %bitcast.19, bf16[32,5120]{1,0:T(8,128)(2,1)S(1)} %join.3.refs_3_.refs_2_, ...), custom_call_target="tpu_custom_call" | custom-call | flops 1677721600 | bytes 16711680 | tf_op jit(solution)/shard_map/expert/pallas_call | solution.py:142
  66.4 0.7 collective-permute-start.29
  67.1 0.2 collective-permute-start.26
  67.3 0.8 collective-permute-start.27
  68.2 4.0 %collective-permute-done.27.refs_2_ = bf16[8,5120]{1,0:T(8,128)(2,1)S(1)} collective-permute-done((bf16[8,5120]{1,0:T(8,128)(2,1)S(1)}, bf16[8,5120]{1,0:T(8,128)(2,1)S(1)}, u32[]{:S(2)}, u32[]{:S(2)}) %collective-permute-start.27) | collective-permute-done | bytes 81952 | tf_op jit(solution)/shard_map/ppermute | solution.py:50
  72.2 1.5 %collective-permute-start.30 = (bf16[32,5120]{1,0:T(8,128)(2,1)S(1)}, bf16[32,5120]{1,0:T(8,128)(2,1)S(1)}, u32[]{:S(2)}, u32[]{:S(2)}) collective-permute-start(bf16[32,5120]{1,0:T(8,128)(2,1)S(1)} %add_half.7), channel_id=1, source_target_pairs={{1,0},{0,1},{3,2},{2,3},{5,4},{4,5},{7,6},{6,7},{9,8},{8,9},{11,10... | collective-permute-start | bytes 983048 | tf_op jit(solution)/shard_map/ppermute | solution.py:50
  73.8 0.5 collective-permute-start.28
  74.3 1.6 %collective-permute-start.31 = (bf16[8,5120]{1,0:T(8,128)(2,1)S(1)}, bf16[8,5120]{1,0:T(8,128)(2,1)S(1)}, u32[]{:S(2)}, u32[]{:S(2)}) collective-permute-start(bf16[8,5120]{1,0:T(8,128)(2,1)S(1)} %get-tuple-element.70), channel_id=1, source_target_pairs={{12,0},{13,1},{14,2},{15,3},{8,4},{9,5},{10,6},{11,7},{4,8},{5,9},... | collective-permute-start | bytes 245768 | tf_op jit(solution)/shard_map/ppermute | solution.py:50
  75.9 3.5 %collective-permute-done.31.refs_3_ = bf16[8,5120]{1,0:T(8,128)(2,1)S(1)} collective-permute-done((bf16[8,5120]{1,0:T(8,128)(2,1)S(1)}, bf16[8,5120]{1,0:T(8,128)(2,1)S(1)}, u32[]{:S(2)}, u32[]{:S(2)}) %collective-permute-start.31) | collective-permute-done | bytes 81952 | tf_op jit(solution)/shard_map/ppermute | solution.py:50
  79.4 0.6 collective-permute-done.30.refs_2_
  80.0 0.1 add_blocks.3
  80.1 0.1 collective-permute-start.32
  80.1 2.3 %collective-permute-start.33 = (bf16[8,5120]{1,0:T(8,128)(2,1)S(1)}, bf16[8,5120]{1,0:T(8,128)(2,1)S(1)}, u32[]{:S(2)}, u32[]{:S(2)}) collective-permute-start(bf16[8,5120]{1,0:T(8,128)(2,1)S(1)} %get-tuple-element.73), channel_id=1, source_target_pairs={{8,0},{9,1},{10,2},{11,3},{12,4},{13,5},{14,6},{15,7},{0,8},{1,9},... | collective-permute-start | bytes 245768 | tf_op jit(solution)/shard_map/ppermute | solution.py:50
  82.4 1.3 %collective-permute-start.34 = (bf16[8,5120]{1,0:T(8,128)(2,1)S(1)}, bf16[8,5120]{1,0:T(8,128)(2,1)S(1)}, u32[]{:S(2)}, u32[]{:S(2)}) collective-permute-start(bf16[8,5120]{1,0:T(8,128)(2,1)S(1)} %get-tuple-element.74), channel_id=1, source_target_pairs={{12,0},{13,1},{14,2},{15,3},{8,4},{9,5},{10,6},{11,7},{4,8},{5,9},... | collective-permute-start | bytes 245768 | tf_op jit(solution)/shard_map/ppermute | solution.py:50
  83.7 2.1 %collective-permute-done.33.refs_1_ = bf16[8,5120]{1,0:T(8,128)(2,1)S(1)} collective-permute-done((bf16[8,5120]{1,0:T(8,128)(2,1)S(1)}, bf16[8,5120]{1,0:T(8,128)(2,1)S(1)}, u32[]{:S(2)}, u32[]{:S(2)}) %collective-permute-start.33) | collective-permute-done | bytes 81952 | tf_op jit(solution)/shard_map/ppermute | solution.py:50
  85.8 1.9 %collective-permute-done.34.refs_2_ = bf16[8,5120]{1,0:T(8,128)(2,1)S(1)} collective-permute-done((bf16[8,5120]{1,0:T(8,128)(2,1)S(1)}, bf16[8,5120]{1,0:T(8,128)(2,1)S(1)}, u32[]{:S(2)}, u32[]{:S(2)}) %collective-permute-start.34) | collective-permute-done | bytes 81952 | tf_op jit(solution)/shard_map/ppermute | solution.py:50
  87.7 1.3 %collective-permute-start.35 = (f32[8,5248]{1,0:T(8,128)S(1)}, f32[8,5248]{1,0:T(8,128)S(1)}, u32[]{:S(2)}, u32[]{:S(2)}) collective-permute-start(f32[8,5248]{1,0:T(8,128)S(1)} %add_last.2.back_ref), channel_id=1, source_target_pairs={{0,16},{1,17},{2,18},{3,19},{4,20},{5,21},{6,22},{7,23},{8,24},{9,... | collective-permute-start | bytes 503816 | tf_op jit(solution)/shard_map/ppermute | solution.py:17
  89.0 1.5 %finish.2 = (bf16[128,5120]{1,0:T(8,128)(2,1)}, f32[8,128]{1,0:T(8,128)S(1)}) custom-call(s32[1]{0:T(128)} %bitcast.refs_0_.section, bf16[128,5120]{1,0:T(8,128)(2,1)S(1)} %get-tuple-element.53.res_ref, f32[8,5248]{1,0:T(8,128)S(1)} %add_last.2.back_ref), custom_call_target="tpu_custom_call" | custom-call | flops 32768000 | bytes 3276800 | tf_op jit(solution)/shard_map/finish/pallas_call | solution.py:538
  90.5 1.3 %collective-permute-start.36 = (f32[8,5120]{1,0:T(8,128)S(1)}, f32[8,5120]{1,0:T(8,128)S(1)}, u32[]{:S(2)}, u32[]{:S(2)}) collective-permute-start(f32[8,5120]{1,0:T(8,128)S(1)} %add_last.3.second_ref), channel_id=1, source_target_pairs={{0,16},{1,17},{2,18},{3,19},{4,20},{5,21},{6,22},{7,23},{8,24},{9,... | collective-permute-start | bytes 491528 | tf_op jit(solution)/shard_map/ppermute | solution.py:27
  91.8 10.6 %collective-permute-done.36.first_ref = f32[8,5120]{1,0:T(8,128)S(1)} collective-permute-done((f32[8,5120]{1,0:T(8,128)S(1)}, f32[8,5120]{1,0:T(8,128)S(1)}, u32[]{:S(2)}, u32[]{:S(2)}) %collective-permute-start.36) | collective-permute-done | bytes 163872 | tf_op jit(solution)/shard_map/ppermute | solution.py:27
  102.5 0.8 lay_out.1
  103.3 2.1 %finish.3 = (bf16[128,5120]{1,0:T(8,128)(2,1)}, f32[8,128]{1,0:T(8,128)}) custom-call(s32[1]{0:T(128)} %bitcast.refs_0_.section, bf16[128,5120]{1,0:T(8,128)(2,1)S(1)} %collective-permute-done.24.refs_7_.res_ref, f32[8,5248]{1,0:T(8,128)S(1)} %collective-permute-done.35.back_ref, ...), custom_call_target="tpu_custom_call", output_to_operand_aliasing={{0}: (3, {})} | custom-call | flops 32768000 | bytes 3276800 | tf_op jit(solution)/shard_map/finish/pallas_call | solution.py:538
  (56 shorter events, 0.5 us)
Async XLA Ops:
  0.6 16.3 %copy-start.5 = (f32[1,128]{1,0:T(1,128)S(1)}, f32[1,128]{1,0:T(1,128)}, u32[]{:S(2)}) copy-start(f32[1,128]{1,0:T(1,128)} %refs_2_.1) | copy-start | bytes 1540
  0.6 16.3 %copy-start.6 = (s32[1,128]{1,0:T(1,128)S(1)}, s32[1,128]{1,0:T(1,128)}, u32[]{:S(2)}) copy-start(s32[1,128]{1,0:T(1,128)} %refs_3_.1) | copy-start | bytes 1540
  0.7 16.3 %copy-start.4 = (f32[1,5120]{1,0:T(1,128)S(1)}, f32[1,5120]{1,0:T(1,128)}, u32[]{:S(2)}) copy-start(f32[1,5120]{1,0:T(1,128)} %refs_1_.1) | copy-start | bytes 61444
  0.7 16.3 %copy-start.1 = (bf16[1,128,5120]{2,1,0:T(8,128)(2,1)S(1)}, bf16[1,128,5120]{2,1,0:T(8,128)(2,1)}, u32[]{:S(2)}) copy-start(bf16[1,128,5120]{2,1,0:T(8,128)(2,1)} %param.9) | copy-start | bytes 3932164
  1.8 1.3 %collective-permute-start = (bf16[8,5120]{1,0:T(8,128)(2,1)S(1)}, bf16[8,5120]{1,0:T(8,128)(2,1)S(1)}, u32[]{:S(2)}, u32[]{:S(2)}) collective-permute-start(bf16[8,5120]{1,0:T(8,128)(2,1)S(1)} %bitcast.25), channel_id=1, source_target_pairs={{0,16},{16,0},{1,17},{17,1},{2,18},{18,2},{3,19},{19,3},{4,20},{20... | collective-permute-start | bytes 245768 | tf_op jit(solution)/shard_map/ppermute | solution.py:22
  2.0 17.7 %copy-start.2 = (bf16[1,128,5120]{2,1,0:T(8,128)(2,1)S(1)}, bf16[1,128,5120]{2,1,0:T(8,128)(2,1)}, u32[]{:S(2)}) copy-start(bf16[1,128,5120]{2,1,0:T(8,128)(2,1)} %param.11) | copy-start | bytes 3932164
  3.2 7.1 %collective-permute-start.3 = (bf16[8,5120]{1,0:T(8,128)(2,1)S(1)}, bf16[8,5120]{1,0:T(8,128)(2,1)S(1)}, u32[]{:S(2)}, u32[]{:S(2)}) collective-permute-start(bf16[8,5120]{1,0:T(8,128)(2,1)S(1)} %broadcast_select_fusion.refs_0_), channel_id=1, source_target_pairs={{0,12},{1,13},{2,14},{3,15},{4,8},{5,9},{6,10},{7,11},{8,4},{9,5},... | collective-permute-start | bytes 245768 | tf_op jit(solution)/shard_map/ppermute | solution.py:50
  7.7 6.6 %collective-permute-start.2 = (bf16[8,5120]{1,0:T(8,128)(2,1)S(1)}, bf16[8,5120]{1,0:T(8,128)(2,1)S(1)}, u32[]{:S(2)}, u32[]{:S(2)}) collective-permute-start(bf16[8,5120]{1,0:T(8,128)(2,1)S(1)} %broadcast_select_fusion.refs_0_), channel_id=1, source_target_pairs={{0,8},{1,9},{2,10},{3,11},{4,12},{5,13},{6,14},{7,15},{8,0},{9,1},... | collective-permute-start | bytes 245768 | tf_op jit(solution)/shard_map/ppermute | solution.py:50
  7.7 6.6 %collective-permute-start.1 = (bf16[8,5120]{1,0:T(8,128)(2,1)S(1)}, bf16[8,5120]{1,0:T(8,128)(2,1)S(1)}, u32[]{:S(2)}, u32[]{:S(2)}) collective-permute-start(bf16[8,5120]{1,0:T(8,128)(2,1)S(1)} %broadcast_select_fusion.refs_0_), channel_id=1, source_target_pairs={{0,4},{1,5},{2,6},{3,7},{4,0},{5,1},{6,2},{7,3},{8,12},{9,13},{10,... | collective-permute-start | bytes 245768 | tf_op jit(solution)/shard_map/ppermute | solution.py:50
  14.4 8.1 %collective-permute-start.7 = (bf16[32,5120]{1,0:T(8,128)(2,1)S(1)}, bf16[32,5120]{1,0:T(8,128)(2,1)S(1)}, u32[]{:S(2)}, u32[]{:S(2)}) collective-permute-start(bf16[32,5120]{1,0:T(8,128)(2,1)S(1)} %join.2.refs_4_), channel_id=1, source_target_pairs={{0,2},{1,3},{2,0},{3,1},{4,6},{5,7},{6,4},{7,5},{8,10},{9,11},{10,... | collective-permute-start | bytes 983048 | tf_op jit(solution)/shard_map/ppermute | solution.py:50
  15.7 8.9 %collective-permute-start.6 = (bf16[32,5120]{1,0:T(8,128)(2,1)S(1)}, bf16[32,5120]{1,0:T(8,128)(2,1)S(1)}, u32[]{:S(2)}, u32[]{:S(2)}) collective-permute-start(bf16[32,5120]{1,0:T(8,128)(2,1)S(1)} %join.2.refs_4_), channel_id=1, source_target_pairs={{0,1},{1,0},{2,3},{3,2},{4,5},{5,4},{6,7},{7,6},{8,9},{9,8},{10,11... | collective-permute-start | bytes 983048 | tf_op jit(solution)/shard_map/ppermute | solution.py:50
  17.8 8.1 %collective-permute-start.4 = (bf16[128,1280]{1,0:T(8,128)(2,1)S(1)}, bf16[128,1280]{1,0:T(8,128)(2,1)S(1)}, u32[]{:S(2)}, u32[]{:S(2)}) collective-permute-start(bf16[128,1280]{1,0:T(8,128)(2,1)S(1)} %get-tuple-element.42), channel_id=1, source_target_pairs={{0,16},{16,0},{1,17},{17,1},{2,18},{18,2},{3,19},{19,3},{4,20},{20... | collective-permute-start | bytes 983048 | tf_op jit(solution)/shard_map/ppermute | solution.py:22
  19.6 7.6 %collective-permute-start.5 = (bf16[128,1280]{1,0:T(8,128)(2,1)S(1)}, bf16[128,1280]{1,0:T(8,128)(2,1)S(1)}, u32[]{:S(2)}, u32[]{:S(2)}) collective-permute-start(bf16[128,1280]{1,0:T(8,128)(2,1)S(1)} %get-tuple-element.43), channel_id=1, source_target_pairs={{0,16},{16,0},{1,17},{17,1},{2,18},{18,2},{3,19},{19,3},{4,20},{20... | collective-permute-start | bytes 983048 | tf_op jit(solution)/shard_map/ppermute | solution.py:22
  19.8 8.7 %collective-permute-start.10 = (bf16[128,1280]{1,0:T(8,128)(2,1)S(1)}, bf16[128,1280]{1,0:T(8,128)(2,1)S(1)}, u32[]{:S(2)}, u32[]{:S(2)}) collective-permute-start(bf16[128,1280]{1,0:T(8,128)(2,1)S(1)} %get-tuple-element.46), channel_id=1, source_target_pairs={{0,16},{16,0},{1,17},{17,1},{2,18},{18,2},{3,19},{19,3},{4,20},{20... | collective-permute-start | bytes 983048 | tf_op jit(solution)/shard_map/ppermute | solution.py:22
  22.5 6.0 %collective-permute-start.11 = (bf16[128,1280]{1,0:T(8,128)(2,1)S(1)}, bf16[128,1280]{1,0:T(8,128)(2,1)S(1)}, u32[]{:S(2)}, u32[]{:S(2)}) collective-permute-start(bf16[128,1280]{1,0:T(8,128)(2,1)S(1)} %get-tuple-element.47), channel_id=1, source_target_pairs={{0,16},{16,0},{1,17},{17,1},{2,18},{18,2},{3,19},{19,3},{4,20},{20... | collective-permute-start | bytes 983048 | tf_op jit(solution)/shard_map/ppermute | solution.py:22
  24.6 4.6 %collective-permute-start.8 = (bf16[16,5120]{1,0:T(8,128)(2,1)S(1)}, bf16[16,5120]{1,0:T(8,128)(2,1)S(1)}, u32[]{:S(2)}, u32[]{:S(2)}) collective-permute-start(bf16[16,5120]{1,0:T(8,128)(2,1)S(1)} %slice.16), channel_id=1, source_target_pairs={{0,1},{1,0},{2,3},{3,2},{4,5},{5,4},{6,7},{7,6},{8,9},{9,8},{10,11... | collective-permute-start | bytes 491528 | tf_op jit(solution)/shard_map/ppermute | solution.py:50
  25.9 4.5 %collective-permute-start.9 = (bf16[16,5120]{1,0:T(8,128)(2,1)S(1)}, bf16[16,5120]{1,0:T(8,128)(2,1)S(1)}, u32[]{:S(2)}, u32[]{:S(2)}) collective-permute-start(bf16[16,5120]{1,0:T(8,128)(2,1)S(1)} %slice.17), channel_id=1, source_target_pairs={{0,2},{1,3},{2,0},{3,1},{4,6},{5,7},{6,4},{7,5},{8,10},{9,11},{10,... | collective-permute-start | bytes 491528 | tf_op jit(solution)/shard_map/ppermute | solution.py:50
  27.2 32.7 %collective-permute-start.24 = (bf16[128,5120]{1,0:T(8,128)(2,1)S(1)}, bf16[128,5120]{1,0:T(8,128)(2,1)S(1)}, u32[]{:S(2)}, u32[]{:S(2)}) collective-permute-start(bf16[128,5120]{1,0:T(8,128)(2,1)S(1)} %get-tuple-element.41.refs_1_), channel_id=1, source_target_pairs={{0,16},{1,17},{2,18},{3,19},{4,20},{5,21},{6,22},{7,23},{8,24},{9,... | collective-permute-start | bytes 3932168 | tf_op jit(solution)/shard_map/ppermute | solution.py:17
  32.5 5.8 %collective-permute-start.12 = (bf16[128,2560]{1,0:T(8,128)(2,1)S(1)}, bf16[128,2560]{1,0:T(8,128)(2,1)S(1)}, u32[]{:S(2)}, u32[]{:S(2)}) collective-permute-start(bf16[128,2560]{1,0:T(8,128)(2,1)S(1)} %get-tuple-element.48.refs_3_), channel_id=1, source_target_pairs={{0,16},{1,17},{2,18},{3,19},{4,20},{5,21},{6,22},{7,23},{8,24},{9,... | collective-permute-start | bytes 1966088 | tf_op jit(solution)/shard_map/ppermute | solution.py:27
  33.8 4.5 %copy-start.3 = (f32[1,5120]{1,0:T(1,128)S(1)}, f32[1,5120]{1,0:T(1,128)}, u32[]{:S(2)}) copy-start(f32[1,5120]{1,0:T(1,128)} %refs_4_.1) | copy-start | bytes 61444
  33.8 30.3 %slice-start = ((s8[6553600]{0:T(1024)(128)(4,1)}), s8[4194304]{0:T(1024)(128)(4,1)S(1)}, s32[]{:S(2)}) async-start(s8[6553600]{0:T(1024)(128)(4,1)} %bitcast.16), calls=%async_computation | async-start | bytes 8388608
  35.8 5.5 %collective-permute-start.17 = (bf16[16,5120]{1,0:T(8,128)(2,1)S(1)}, bf16[16,5120]{1,0:T(8,128)(2,1)S(1)}, u32[]{:S(2)}, u32[]{:S(2)}) collective-permute-start(bf16[16,5120]{1,0:T(8,128)(2,1)S(1)} %get-tuple-element.58), channel_id=1, source_target_pairs={{2,0},{3,1},{0,2},{1,3},{6,4},{7,5},{4,6},{5,7},{10,8},{11,9},{8,1... | collective-permute-start | bytes 491528 | tf_op jit(solution)/shard_map/ppermute | solution.py:50
  38.0 4.6 %collective-permute-start.16 = (bf16[16,5120]{1,0:T(8,128)(2,1)S(1)}, bf16[16,5120]{1,0:T(8,128)(2,1)S(1)}, u32[]{:S(2)}, u32[]{:S(2)}) collective-permute-start(bf16[16,5120]{1,0:T(8,128)(2,1)S(1)} %get-tuple-element.56), channel_id=1, source_target_pairs={{1,0},{0,1},{3,2},{2,3},{5,4},{4,5},{7,6},{6,7},{9,8},{8,9},{11,10... | collective-permute-start | bytes 491528 | tf_op jit(solution)/shard_map/ppermute | solution.py:50
  38.2 25.8 %slice-start.1 = ((s8[6553600]{0:T(1024)(128)(4,1)}), s8[2359296]{0:T(1024)(128)(4,1)S(1)}, s32[]{:S(2)}) async-start(s8[6553600]{0:T(1024)(128)(4,1)} %bitcast.16), calls=%async_computation.1 | async-start | bytes 4718592
  38.2 25.8 %copy-start = (bf16[1,640,5120]{2,1,0:T(8,128)(2,1)S(1)}, bf16[1,640,5120]{2,1,0:T(8,128)(2,1)}, u32[]{:S(2)}) copy-start(bf16[1,640,5120]{2,1,0:T(8,128)(2,1)} %param.15) | copy-start | bytes 19660804
  38.9 5.2 %collective-permute-start.15 = (bf16[8,5120]{1,0:T(8,128)(2,1)S(1)}, bf16[8,5120]{1,0:T(8,128)(2,1)S(1)}, u32[]{:S(2)}, u32[]{:S(2)}) collective-permute-start(bf16[8,5120]{1,0:T(8,128)(2,1)S(1)} %get-tuple-element.54.refs_0_.after_any), channel_id=1, source_target_pairs={{0,12},{1,13},{2,14},{3,15},{4,8},{5,9},{6,10},{7,11},{8,4},{9,5},... | collective-permute-start | bytes 245768 | tf_op jit(solution)/shard_map/ppermute | solution.py:50
  41.3 7.5 %collective-permute-start.14 = (bf16[8,5120]{1,0:T(8,128)(2,1)S(1)}, bf16[8,5120]{1,0:T(8,128)(2,1)S(1)}, u32[]{:S(2)}, u32[]{:S(2)}) collective-permute-start(bf16[8,5120]{1,0:T(8,128)(2,1)S(1)} %get-tuple-element.54.refs_0_.after_any), channel_id=1, source_target_pairs={{0,8},{1,9},{2,10},{3,11},{4,12},{5,13},{6,14},{7,15},{8,0},{9,1},... | collective-permute-start | bytes 245768 | tf_op jit(solution)/shard_map/ppermute | solution.py:50
  41.3 7.5 %collective-permute-start.13 = (bf16[8,5120]{1,0:T(8,128)(2,1)S(1)}, bf16[8,5120]{1,0:T(8,128)(2,1)S(1)}, u32[]{:S(2)}, u32[]{:S(2)}) collective-permute-start(bf16[8,5120]{1,0:T(8,128)(2,1)S(1)} %get-tuple-element.54.refs_0_.after_any), channel_id=1, source_target_pairs={{0,4},{1,5},{2,6},{3,7},{4,0},{5,1},{6,2},{7,3},{8,12},{9,13},{10,... | collective-permute-start | bytes 245768 | tf_op jit(solution)/shard_map/ppermute | solution.py:50
  42.6 7.6 %collective-permute-start.21 = (bf16[32,5120]{1,0:T(8,128)(2,1)S(1)}, bf16[32,5120]{1,0:T(8,128)(2,1)S(1)}, u32[]{:S(2)}, u32[]{:S(2)}) collective-permute-start(bf16[32,5120]{1,0:T(8,128)(2,1)S(1)} %add_half.5.refs_5_), channel_id=1, source_target_pairs={{1,0},{0,1},{3,2},{2,3},{5,4},{4,5},{7,6},{6,7},{9,8},{8,9},{11,10... | collective-permute-start | bytes 983048 | tf_op jit(solution)/shard_map/ppermute | solution.py:50
  44.1 6.2 %collective-permute-start.20 = (bf16[32,5120]{1,0:T(8,128)(2,1)S(1)}, bf16[32,5120]{1,0:T(8,128)(2,1)S(1)}, u32[]{:S(2)}, u32[]{:S(2)}) collective-permute-start(bf16[32,5120]{1,0:T(8,128)(2,1)S(1)} %add_half.4.refs_4_), channel_id=1, source_target_pairs={{2,0},{3,1},{0,2},{1,3},{6,4},{7,5},{4,6},{5,7},{10,8},{11,9},{8,1... | collective-permute-start | bytes 983048 | tf_op jit(solution)/shard_map/ppermute | solution.py:50
  48.8 9.8 %collective-permute-start.19 = (bf16[32,5120]{1,0:T(8,128)(2,1)S(1)}, bf16[32,5120]{1,0:T(8,128)(2,1)S(1)}, u32[]{:S(2)}, u32[]{:S(2)}) collective-permute-start(bf16[32,5120]{1,0:T(8,128)(2,1)S(1)} %join.3.refs_3_.refs_2_), channel_id=1, source_target_pairs={{0,2},{1,3},{2,0},{3,1},{4,6},{5,7},{6,4},{7,5},{8,10},{9,11},{10,... | collective-permute-start | bytes 983048 | tf_op jit(solution)/shard_map/ppermute | solution.py:50
  49.4 9.2 %collective-permute-start.18 = (bf16[32,5120]{1,0:T(8,128)(2,1)S(1)}, bf16[32,5120]{1,0:T(8,128)(2,1)S(1)}, u32[]{:S(2)}, u32[]{:S(2)}) collective-permute-start(bf16[32,5120]{1,0:T(8,128)(2,1)S(1)} %join.3.refs_3_.refs_2_), channel_id=1, source_target_pairs={{0,1},{1,0},{2,3},{3,2},{4,5},{5,4},{6,7},{7,6},{8,9},{9,8},{10,11... | collective-permute-start | bytes 983048 | tf_op jit(solution)/shard_map/ppermute | solution.py:50
  58.6 4.6 %collective-permute-start.22 = (bf16[16,5120]{1,0:T(8,128)(2,1)S(1)}, bf16[16,5120]{1,0:T(8,128)(2,1)S(1)}, u32[]{:S(2)}, u32[]{:S(2)}) collective-permute-start(bf16[16,5120]{1,0:T(8,128)(2,1)S(1)} %get-tuple-element.61), channel_id=1, source_target_pairs={{0,1},{1,0},{2,3},{3,2},{4,5},{5,4},{6,7},{7,6},{8,9},{9,8},{10,11... | collective-permute-start | bytes 491528 | tf_op jit(solution)/shard_map/ppermute | solution.py:50
  59.9 4.2 %collective-permute-start.23 = (bf16[16,5120]{1,0:T(8,128)(2,1)S(1)}, bf16[16,5120]{1,0:T(8,128)(2,1)S(1)}, u32[]{:S(2)}, u32[]{:S(2)}) collective-permute-start(bf16[16,5120]{1,0:T(8,128)(2,1)S(1)} %get-tuple-element.62), channel_id=1, source_target_pairs={{0,2},{1,3},{2,0},{3,1},{4,6},{5,7},{6,4},{7,5},{8,10},{9,11},{10,... | collective-permute-start | bytes 491528 | tf_op jit(solution)/shard_map/ppermute | solution.py:50
  59.9 3.3 %collective-permute-start.25 = (bf16[8,5120]{1,0:T(8,128)(2,1)S(1)}, bf16[8,5120]{1,0:T(8,128)(2,1)S(1)}, u32[]{:S(2)}, u32[]{:S(2)}) collective-permute-start(bf16[8,5120]{1,0:T(8,128)(2,1)S(1)} %get-tuple-element.63), channel_id=1, source_target_pairs={{4,0},{5,1},{6,2},{7,3},{0,4},{1,5},{2,6},{3,7},{12,8},{13,9},{14,... | collective-permute-start | bytes 245768 | tf_op jit(solution)/shard_map/ppermute | solution.py:50
  66.4 5.8 %collective-permute-start.29 = (bf16[16,5120]{1,0:T(8,128)(2,1)S(1)}, bf16[16,5120]{1,0:T(8,128)(2,1)S(1)}, u32[]{:S(2)}, u32[]{:S(2)}) collective-permute-start(bf16[16,5120]{1,0:T(8,128)(2,1)S(1)} %get-tuple-element.69), channel_id=1, source_target_pairs={{2,0},{3,1},{0,2},{1,3},{6,4},{7,5},{4,6},{5,7},{10,8},{11,9},{8,1... | collective-permute-start | bytes 491528 | tf_op jit(solution)/shard_map/ppermute | solution.py:50
  67.1 6.6 %collective-permute-start.26 = (bf16[16,5120]{1,0:T(8,128)(2,1)S(1)}, bf16[16,5120]{1,0:T(8,128)(2,1)S(1)}, u32[]{:S(2)}, u32[]{:S(2)}) collective-permute-start(bf16[16,5120]{1,0:T(8,128)(2,1)S(1)} %get-tuple-element.66), channel_id=1, source_target_pairs={{1,0},{0,1},{3,2},{2,3},{5,4},{4,5},{7,6},{6,7},{9,8},{8,9},{11,10... | collective-permute-start | bytes 491528 | tf_op jit(solution)/shard_map/ppermute | solution.py:50
  67.3 4.8 %collective-permute-start.27 = (bf16[8,5120]{1,0:T(8,128)(2,1)S(1)}, bf16[8,5120]{1,0:T(8,128)(2,1)S(1)}, u32[]{:S(2)}, u32[]{:S(2)}) collective-permute-start(bf16[8,5120]{1,0:T(8,128)(2,1)S(1)} %get-tuple-element.67), channel_id=1, source_target_pairs={{8,0},{9,1},{10,2},{11,3},{12,4},{13,5},{14,6},{15,7},{0,8},{1,9},... | collective-permute-start | bytes 245768 | tf_op jit(solution)/shard_map/ppermute | solution.py:50
  72.2 7.7 %collective-permute-start.30 = (bf16[32,5120]{1,0:T(8,128)(2,1)S(1)}, bf16[32,5120]{1,0:T(8,128)(2,1)S(1)}, u32[]{:S(2)}, u32[]{:S(2)}) collective-permute-start(bf16[32,5120]{1,0:T(8,128)(2,1)S(1)} %add_half.7), channel_id=1, source_target_pairs={{1,0},{0,1},{3,2},{2,3},{5,4},{4,5},{7,6},{6,7},{9,8},{8,9},{11,10... | collective-permute-start | bytes 983048 | tf_op jit(solution)/shard_map/ppermute | solution.py:50
  73.8 6.2 %collective-permute-start.28 = (bf16[32,5120]{1,0:T(8,128)(2,1)S(1)}, bf16[32,5120]{1,0:T(8,128)(2,1)S(1)}, u32[]{:S(2)}, u32[]{:S(2)}) collective-permute-start(bf16[32,5120]{1,0:T(8,128)(2,1)S(1)} %add_half.6), channel_id=1, source_target_pairs={{2,0},{3,1},{0,2},{1,3},{6,4},{7,5},{4,6},{5,7},{10,8},{11,9},{8,1... | collective-permute-start | bytes 983048 | tf_op jit(solution)/shard_map/ppermute | solution.py:50
  74.3 5.1 %collective-permute-start.31 = (bf16[8,5120]{1,0:T(8,128)(2,1)S(1)}, bf16[8,5120]{1,0:T(8,128)(2,1)S(1)}, u32[]{:S(2)}, u32[]{:S(2)}) collective-permute-start(bf16[8,5120]{1,0:T(8,128)(2,1)S(1)} %get-tuple-element.70), channel_id=1, source_target_pairs={{12,0},{13,1},{14,2},{15,3},{8,4},{9,5},{10,6},{11,7},{4,8},{5,9},... | collective-permute-start | bytes 245768 | tf_op jit(solution)/shard_map/ppermute | solution.py:50
  80.1 3.7 %collective-permute-start.32 = (bf16[8,5120]{1,0:T(8,128)(2,1)S(1)}, bf16[8,5120]{1,0:T(8,128)(2,1)S(1)}, u32[]{:S(2)}, u32[]{:S(2)}) collective-permute-start(bf16[8,5120]{1,0:T(8,128)(2,1)S(1)} %get-tuple-element.72), channel_id=1, source_target_pairs={{4,0},{5,1},{6,2},{7,3},{0,4},{1,5},{2,6},{3,7},{12,8},{13,9},{14,... | collective-permute-start | bytes 245768 | tf_op jit(solution)/shard_map/ppermute | solution.py:50
  80.1 5.6 %collective-permute-start.33 = (bf16[8,5120]{1,0:T(8,128)(2,1)S(1)}, bf16[8,5120]{1,0:T(8,128)(2,1)S(1)}, u32[]{:S(2)}, u32[]{:S(2)}) collective-permute-start(bf16[8,5120]{1,0:T(8,128)(2,1)S(1)} %get-tuple-element.73), channel_id=1, source_target_pairs={{8,0},{9,1},{10,2},{11,3},{12,4},{13,5},{14,6},{15,7},{0,8},{1,9},... | collective-permute-start | bytes 245768 | tf_op jit(solution)/shard_map/ppermute | solution.py:50
  82.4 5.2 %collective-permute-start.34 = (bf16[8,5120]{1,0:T(8,128)(2,1)S(1)}, bf16[8,5120]{1,0:T(8,128)(2,1)S(1)}, u32[]{:S(2)}, u32[]{:S(2)}) collective-permute-start(bf16[8,5120]{1,0:T(8,128)(2,1)S(1)} %get-tuple-element.74), channel_id=1, source_target_pairs={{12,0},{13,1},{14,2},{15,3},{8,4},{9,5},{10,6},{11,7},{4,8},{5,9},... | collective-permute-start | bytes 245768 | tf_op jit(solution)/shard_map/ppermute | solution.py:50
  87.7 15.6 %collective-permute-start.35 = (f32[8,5248]{1,0:T(8,128)S(1)}, f32[8,5248]{1,0:T(8,128)S(1)}, u32[]{:S(2)}, u32[]{:S(2)}) collective-permute-start(f32[8,5248]{1,0:T(8,128)S(1)} %add_last.2.back_ref), channel_id=1, source_target_pairs={{0,16},{1,17},{2,18},{3,19},{4,20},{5,21},{6,22},{7,23},{8,24},{9,... | collective-permute-start | bytes 503816 | tf_op jit(solution)/shard_map/ppermute | solution.py:17
  90.5 11.9 %collective-permute-start.36 = (f32[8,5120]{1,0:T(8,128)S(1)}, f32[8,5120]{1,0:T(8,128)S(1)}, u32[]{:S(2)}, u32[]{:S(2)}) collective-permute-start(f32[8,5120]{1,0:T(8,128)S(1)} %add_last.3.second_ref), channel_id=1, source_target_pairs={{0,16},{1,17},{2,18},{3,19},{4,20},{5,21},{6,22},{7,23},{8,24},{9,... | collective-permute-start | bytes 491528 | tf_op jit(solution)/shard_map/ppermute | solution.py:27

commit v9 on v7

--- a/solution.py
+++ b/solution.py
@@ -239,7 +239,7 @@
 
 
 def head_loop(heads, some_heads):
-    few = next(u for u in (5, 4, 2, 1) if heads % u == 0)
+    few = next(u for u in (10, 5, 4, 2, 1) if heads % u == 0)
 
     def step(g, carry):
         numbers = [g * few + u for u in range(few)]
@@ -503,7 +503,7 @@
 def finish(section, res, back, room=None):
     tokens, width = res.shape
     one = jax.ShapeDtypeStruct((tokens, width), jnp.bfloat16)
-    step = next(s for s in (1280, 1024, 512, 256, 128) if width % s == 0)
+    step = next(s for s in (640, 512, 256, 128) if width % s == 0)
     parts = [slice(at, at + step) for at in range(0, width, step)]
 
     def kernel(section, res_ref, back_ref, *refs):
@@ -568,9 +568,9 @@
     heights = grid.heights(own_rows)
     narrow = any(n % 16 for n in heights)
 
-    first = swapped(memory[0, :, :, :half].reshape(own_rows, width))
-    second = memory[0, :, :, half:].reshape(own_rows, width)
-    pieces = grid.gather(jnp.where(decoder, second, first))
+    first = swapped(memory[0])[:, :, :half]
+    stash = jnp.where(decoder, memory[0, :, :, half:], first).reshape(own_rows, width)
+    pieces = grid.gather(stash)
     current, *first, second, gates = make_queries(
         layer_in[0], attn_gain, gate_prob, slot_index, [pieces[0]]
     )

time: 102 us -> 101 us (level)
  waiting for transfers between devices: 46.1 us -> 43.2 us
  local copies, waits for them, and re-layouts: 1.24 us -> 3.41 us
  Pallas kernels: 12.3 us -> 11 us
    ppermute x28, waiting for transfers between devices: 36.4 us -> 32.5 us  [shift(): return lax.ppermute(block, 'expert', route)]
    unnamed x21 -> x19, local copies, waits for them, and re-layouts: 1.21 us -> 3.39 us
    pallas_call x18, Pallas kernels: 9.26 us -> 8.04 us  [local_kernel(): pl.pallas_call(body, out_shape=tuple(outs), in_specs=in_specs, out_specs=...]
    ppermute x5, starting transfers between devices: 4.61 us -> 3.48 us  [swapped(): lax.ppermute(block, 'section', [(i, (i + sections // 2) % sections) for i...]
  transfers between devices with their start and end apart: 37 -> 37, of which waited for: 17 -> 17; matrix products, arithmetic and copies ran while one was open for 0% -> 0% of each run, Pallas kernels for 8% -> 7%
where the time goes in v9:
time: 101 us
  waiting for transfers between devices  43.2 us (43%)
  starting transfers between devices  41.1 us (41%)
  Pallas kernels  11 us (11%)
  local copies, waits for them, and re-layouts  3.41 us (3%)
    ppermute x28, waiting for transfers between devices, shift(): return lax.ppermute(block, 'expert', route)  32.5 us
    ppermute x28, starting transfers between devices, shift(): return lax.ppermute(block, 'expert', route)  32.5 us
    ppermute x2, waiting for transfers between devices, passed_along(): return lax.ppermute(block, axis, route)  8.58 us
    pallas_call x18, Pallas kernels, local_kernel(): pl.pallas_call(body, out_shape=tuple(outs), in_specs=in_specs, out_specs=...  8.04 us
    ppermute x5, starting transfers between devices, swapped(): lax.ppermute(block, 'section', [(i, (i + sections // 2) % sections) for i...  3.48 us
    unnamed x19, local copies, waits for them, and re-layouts  3.39 us
    pallas_call x2, Pallas kernels, finish(): pl.pallas_call(kernel, out_shape=one, in_specs=[pl.BlockSpec(memory_space...  2.99 us
    ppermute x2, starting transfers between devices, passed_along(): return lax.ppermute(block, axis, route)  2.57 us
  transfers between devices with their start and end apart: 37, of which 17 were waited for; matrix products, arithmetic and copies ran while one was open for 0% of the time, Pallas kernels for 7%

profile of v9, /device:TPU:1, one launch (start us, length us, event | category | flops | bytes accessed | tf_op | source)
XLA Modules:
  0.0 100.7 jit_solution(12317985203210598000)
XLA Ops:
  0.6 0.1 collective-permute-start
  0.8 1.5 %collective-permute-done = bf16[8,2,5120]{2,1,0:T(2,128)(2,1)S(1)} collective-permute-done((bf16[8,2,5120]{2,1,0:T(2,128)(2,1)}, bf16[8,2,5120]{2,1,0:T(2,128)(2,1)S(1)}, u32[]{:S(2)}, u32[]{:S(2)}) %collective-permute-start) | collective-permute-done | bytes 163872 | tf_op jit(solution)/shard_map/ppermute | solution.py:22
  2.3 1.0 fusion
  3.3 4.5 %collective-permute-start.3 = (bf16[8,5120]{1,0:T(8,128)(2,1)S(1)}, bf16[8,5120]{1,0:T(8,128)(2,1)S(1)}, u32[]{:S(2)}, u32[]{:S(2)}) collective-permute-start(bf16[8,5120]{1,0:T(8,128)(2,1)S(1)} %bitcast.20), channel_id=1, source_target_pairs={{0,12},{1,13},{2,14},{3,15},{4,8},{5,9},{6,10},{7,11},{8,4},{9,5},... | collective-permute-start | bytes 245768 | tf_op jit(solution)/shard_map/ppermute | solution.py:50
  7.8 0.4 collective-permute-start.1
  8.2 2.2 %collective-permute-done.3.refs_3_ = bf16[8,5120]{1,0:T(8,128)(2,1)S(1)} collective-permute-done((bf16[8,5120]{1,0:T(8,128)(2,1)S(1)}, bf16[8,5120]{1,0:T(8,128)(2,1)S(1)}, u32[]{:S(2)}, u32[]{:S(2)}) %collective-permute-start.3) | collective-permute-done | bytes 81952 | tf_op jit(solution)/shard_map/ppermute | solution.py:50
  10.4 4.1 %collective-permute-done.2.refs_2_ = bf16[8,5120]{1,0:T(8,128)(2,1)S(1)} collective-permute-done((bf16[8,5120]{1,0:T(8,128)(2,1)S(1)}, bf16[8,5120]{1,0:T(8,128)(2,1)S(1)}, u32[]{:S(2)}, u32[]{:S(2)}) %collective-permute-start.2) | collective-permute-done | bytes 81952 | tf_op jit(solution)/shard_map/ppermute | solution.py:50
  14.5 1.3 %collective-permute-start.7 = (bf16[32,5120]{1,0:T(8,128)(2,1)S(1)}, bf16[32,5120]{1,0:T(8,128)(2,1)S(1)}, u32[]{:S(2)}, u32[]{:S(2)}) collective-permute-start(bf16[32,5120]{1,0:T(8,128)(2,1)S(1)} %join.2.refs_4_), channel_id=1, source_target_pairs={{0,2},{1,3},{2,0},{3,1},{4,6},{5,7},{6,4},{7,5},{8,10},{9,11},{10,... | collective-permute-start | bytes 983048 | tf_op jit(solution)/shard_map/ppermute | solution.py:50
  15.8 1.2 %collective-permute-start.6 = (bf16[32,5120]{1,0:T(8,128)(2,1)S(1)}, bf16[32,5120]{1,0:T(8,128)(2,1)S(1)}, u32[]{:S(2)}, u32[]{:S(2)}) collective-permute-start(bf16[32,5120]{1,0:T(8,128)(2,1)S(1)} %join.2.refs_4_), channel_id=1, source_target_pairs={{0,1},{1,0},{2,3},{3,2},{4,5},{5,4},{6,7},{7,6},{8,9},{9,8},{10,11... | collective-permute-start | bytes 983048 | tf_op jit(solution)/shard_map/ppermute | solution.py:50
  17.0 1.3 %copy-done.1 = bf16[1,128,5120]{2,1,0:T(8,128)(2,1)S(1)} copy-done((bf16[1,128,5120]{2,1,0:T(8,128)(2,1)S(1)}, bf16[1,128,5120]{2,1,0:T(8,128)(2,1)}, u32[]{:S(2)}) %copy-start.1) | copy-done | bytes 1310744
  18.3 0.7 copy-done.4
  19.0 0.7 copy-done.5
  19.7 0.7 copy-done.6
  20.4 0.9 queries.1
  21.2 1.8 %collective-permute-start.4 = (bf16[128,1280]{1,0:T(8,128)(2,1)S(1)}, bf16[128,1280]{1,0:T(8,128)(2,1)S(1)}, u32[]{:S(2)}, u32[]{:S(2)}) collective-permute-start(bf16[128,1280]{1,0:T(8,128)(2,1)S(1)} %get-tuple-element.41), channel_id=1, source_target_pairs={{0,16},{16,0},{1,17},{17,1},{2,18},{18,2},{3,19},{19,3},{4,20},{20... | collective-permute-start | bytes 983048 | tf_op jit(solution)/shard_map/ppermute | solution.py:22
  23.2 0.5 collective-permute-start.10
  23.7 1.0 collective-permute-start.11
  24.7 1.3 %collective-permute-start.8 = (bf16[16,5120]{1,0:T(8,128)(2,1)S(1)}, bf16[16,5120]{1,0:T(8,128)(2,1)S(1)}, u32[]{:S(2)}, u32[]{:S(2)}) collective-permute-start(bf16[16,5120]{1,0:T(8,128)(2,1)S(1)} %slice.17), channel_id=1, source_target_pairs={{0,1},{1,0},{2,3},{3,2},{4,5},{5,4},{6,7},{7,6},{8,9},{9,8},{10,11... | collective-permute-start | bytes 491528 | tf_op jit(solution)/shard_map/ppermute | solution.py:50
  26.0 1.3 %collective-permute-start.9 = (bf16[16,5120]{1,0:T(8,128)(2,1)S(1)}, bf16[16,5120]{1,0:T(8,128)(2,1)S(1)}, u32[]{:S(2)}, u32[]{:S(2)}) collective-permute-start(bf16[16,5120]{1,0:T(8,128)(2,1)S(1)} %slice.18), channel_id=1, source_target_pairs={{0,2},{1,3},{2,0},{3,1},{4,6},{5,7},{6,4},{7,5},{8,10},{9,11},{10,... | collective-permute-start | bytes 491528 | tf_op jit(solution)/shard_map/ppermute | solution.py:50
  27.3 1.3 %collective-permute-start.24 = (bf16[128,5120]{1,0:T(8,128)(2,1)S(1)}, bf16[128,5120]{1,0:T(8,128)(2,1)S(1)}, u32[]{:S(2)}, u32[]{:S(2)}) collective-permute-start(bf16[128,5120]{1,0:T(8,128)(2,1)S(1)} %get-tuple-element.40.refs_1_), channel_id=1, source_target_pairs={{0,16},{1,17},{2,18},{3,19},{4,20},{5,21},{6,22},{7,23},{8,24},{9,... | collective-permute-start | bytes 3932168 | tf_op jit(solution)/shard_map/ppermute | solution.py:17
  28.6 0.7 collective-permute-done.8.refs_7_
  29.3 1.2 %collective-permute-done.9.refs_8_ = bf16[16,5120]{1,0:T(8,128)(2,1)S(1)} collective-permute-done((bf16[16,5120]{1,0:T(8,128)(2,1)S(1)}, bf16[16,5120]{1,0:T(8,128)(2,1)S(1)}, u32[]{:S(2)}, u32[]{:S(2)}) %collective-permute-start.9) | collective-permute-done | bytes 163872 | tf_op jit(solution)/shard_map/ppermute | solution.py:50
  30.5 1.4 %attend.1 = (bf16[128,2560]{1,0:T(8,128)(2,1)S(1)}, f32[20,128,128]{2,1,0:T(8,128)S(1)}, bf16[128,2560]{1,0:T(8,128)(2,1)S(1)}) custom-call(s32[1]{0:T(128)} %bitcast.refs_0_.section, bf16[128,1280]{1,0:T(8,128)(2,1)S(1)} %collective-permute-done.4.refs_1_, bf16[128,1280]{1,0:T(8,128)(2,1)S(1)} %collective-permute-done.5.refs_2_, ...), custom_call_target="tpu_custom_call" | custom-call | flops 167772160 | bytes 5242884 | tf_op jit(solution)/shard_map/attend/pallas_call | solution.py:142
  31.9 1.3 %collective-permute-start.12 = (bf16[128,2560]{1,0:T(8,128)(2,1)S(1)}, bf16[128,2560]{1,0:T(8,128)(2,1)S(1)}, u32[]{:S(2)}, u32[]{:S(2)}) collective-permute-start(bf16[128,2560]{1,0:T(8,128)(2,1)S(1)} %get-tuple-element.47.refs_3_), channel_id=1, source_target_pairs={{0,16},{1,17},{2,18},{3,19},{4,20},{5,21},{6,22},{7,23},{8,24},{9,... | collective-permute-start | bytes 1966088 | tf_op jit(solution)/shard_map/ppermute | solution.py:27
  33.2 1.4 %gradient.1 = (f32[32,5120]{1,0:T(8,128)S(1)}, f32[32,5120]{1,0:T(8,128)S(1)}, f32[32,5120]{1,0:T(8,128)S(1)}, bf16[16,5120]{1,0:T(8,128)(2,1)S(1)}, bf16[16,5120]{1,0:T(8,128)(2,1)S(1)}) custom-call(s32[1]{0:T(128)} %bitcast.refs_0_.section, bf16[128,2560]{1,0:T(8,128)(2,1)S(1)} %get-tuple-element.48.q_ref, ...), custom_call_target="tpu_custom_call" | custom-call | flops 419430400 | bytes 6881284 | tf_op jit(solution)/shard_map/gradient/pallas_call | solution.py:142
  34.6 2.2 %collective-permute-start.17 = (bf16[16,5120]{1,0:T(8,128)(2,1)S(1)}, bf16[16,5120]{1,0:T(8,128)(2,1)S(1)}, u32[]{:S(2)}, u32[]{:S(2)}) collective-permute-start(bf16[16,5120]{1,0:T(8,128)(2,1)S(1)} %get-tuple-element.57), channel_id=1, source_target_pairs={{2,0},{3,1},{0,2},{1,3},{6,4},{7,5},{4,6},{5,7},{10,8},{11,9},{8,1... | collective-permute-start | bytes 491528 | tf_op jit(solution)/shard_map/ppermute | solution.py:50
  36.8 0.3 collective-permute-start.16
  37.1 0.6 settle.1
  37.7 2.4 %collective-permute-start.15 = (bf16[8,5120]{1,0:T(8,128)(2,1)S(1)}, bf16[8,5120]{1,0:T(8,128)(2,1)S(1)}, u32[]{:S(2)}, u32[]{:S(2)}) collective-permute-start(bf16[8,5120]{1,0:T(8,128)(2,1)S(1)} %get-tuple-element.53.refs_0_.after_any), channel_id=1, source_target_pairs={{0,12},{1,13},{2,14},{3,15},{4,8},{5,9},{6,10},{7,11},{8,4},{9,5},... | collective-permute-start | bytes 245768 | tf_op jit(solution)/shard_map/ppermute | solution.py:50
  40.1 1.2 %collective-permute-start.13 = (bf16[8,5120]{1,0:T(8,128)(2,1)S(1)}, bf16[8,5120]{1,0:T(8,128)(2,1)S(1)}, u32[]{:S(2)}, u32[]{:S(2)}) collective-permute-start(bf16[8,5120]{1,0:T(8,128)(2,1)S(1)} %get-tuple-element.53.refs_0_.after_any), channel_id=1, source_target_pairs={{0,4},{1,5},{2,6},{3,7},{4,0},{5,1},{6,2},{7,3},{8,12},{9,13},{10,... | collective-permute-start | bytes 245768 | tf_op jit(solution)/shard_map/ppermute | solution.py:50
  41.4 1.3 %collective-permute-start.21 = (bf16[32,5120]{1,0:T(8,128)(2,1)S(1)}, bf16[32,5120]{1,0:T(8,128)(2,1)S(1)}, u32[]{:S(2)}, u32[]{:S(2)}) collective-permute-start(bf16[32,5120]{1,0:T(8,128)(2,1)S(1)} %add_half.5.refs_5_), channel_id=1, source_target_pairs={{1,0},{0,1},{3,2},{2,3},{5,4},{4,5},{7,6},{6,7},{9,8},{8,9},{11,10... | collective-permute-start | bytes 983048 | tf_op jit(solution)/shard_map/ppermute | solution.py:50
  42.7 0.2 collective-permute-done.15.refs_3_
  42.9 1.1 %collective-permute-start.20 = (bf16[32,5120]{1,0:T(8,128)(2,1)S(1)}, bf16[32,5120]{1,0:T(8,128)(2,1)S(1)}, u32[]{:S(2)}, u32[]{:S(2)}) collective-permute-start(bf16[32,5120]{1,0:T(8,128)(2,1)S(1)} %add_half.4.refs_4_), channel_id=1, source_target_pairs={{2,0},{3,1},{0,2},{1,3},{6,4},{7,5},{4,6},{5,7},{10,8},{11,9},{8,1... | collective-permute-start | bytes 983048 | tf_op jit(solution)/shard_map/ppermute | solution.py:50
  44.1 3.6 %collective-permute-done.14.refs_2_ = bf16[8,5120]{1,0:T(8,128)(2,1)S(1)} collective-permute-done((bf16[8,5120]{1,0:T(8,128)(2,1)S(1)}, bf16[8,5120]{1,0:T(8,128)(2,1)S(1)}, u32[]{:S(2)}, u32[]{:S(2)}) %collective-permute-start.14) | collective-permute-done | bytes 81952 | tf_op jit(solution)/shard_map/ppermute | solution.py:50
  47.7 1.2 %collective-permute-start.19 = (bf16[32,5120]{1,0:T(8,128)(2,1)S(1)}, bf16[32,5120]{1,0:T(8,128)(2,1)S(1)}, u32[]{:S(2)}, u32[]{:S(2)}) collective-permute-start(bf16[32,5120]{1,0:T(8,128)(2,1)S(1)} %join.3.refs_3_.refs_2_), channel_id=1, source_target_pairs={{0,2},{1,3},{2,0},{3,1},{4,6},{5,7},{6,4},{7,5},{8,10},{9,11},{10,... | collective-permute-start | bytes 983048 | tf_op jit(solution)/shard_map/ppermute | solution.py:50
  48.9 0.2 collective-permute-start.18
  49.1 0.1 add_blocks.2
  49.3 8.2 %collective-permute-done.19.refs_0_.refs_4_ = bf16[32,5120]{1,0:T(8,128)(2,1)S(1)} collective-permute-done((bf16[32,5120]{1,0:T(8,128)(2,1)S(1)}, bf16[32,5120]{1,0:T(8,128)(2,1)S(1)}, u32[]{:S(2)}, u32[]{:S(2)}) %collective-permute-start.19) | collective-permute-done | bytes 327712 | tf_op jit(solution)/shard_map/ppermute | solution.py:50
  57.4 1.3 %collective-permute-start.22 = (bf16[16,5120]{1,0:T(8,128)(2,1)S(1)}, bf16[16,5120]{1,0:T(8,128)(2,1)S(1)}, u32[]{:S(2)}, u32[]{:S(2)}) collective-permute-start(bf16[16,5120]{1,0:T(8,128)(2,1)S(1)} %get-tuple-element.59), channel_id=1, source_target_pairs={{0,1},{1,0},{2,3},{3,2},{4,5},{5,4},{6,7},{7,6},{8,9},{9,8},{10,11... | collective-permute-start | bytes 491528 | tf_op jit(solution)/shard_map/ppermute | solution.py:50
  58.7 0.2 collective-permute-start.23
  58.9 2.4 %collective-permute-start.26 = (bf16[8,5120]{1,0:T(8,128)(2,1)S(1)}, bf16[8,5120]{1,0:T(8,128)(2,1)S(1)}, u32[]{:S(2)}, u32[]{:S(2)}) collective-permute-start(bf16[8,5120]{1,0:T(8,128)(2,1)S(1)} %get-tuple-element.62), channel_id=1, source_target_pairs={{8,0},{9,1},{10,2},{11,3},{12,4},{13,5},{14,6},{15,7},{0,8},{1,9},... | collective-permute-start | bytes 245768 | tf_op jit(solution)/shard_map/ppermute | solution.py:50
  61.3 0.8 collective-permute-done.25.refs_8_.refs_1_
  62.2 1.0 collective-permute-done.26.refs_9_.refs_2_
  63.2 2.3 %expert.1 = (f32[32,5120]{1,0:T(8,128)S(1)}, f32[32,5120]{1,0:T(8,128)S(1)}, f32[32,5120]{1,0:T(8,128)S(1)}, bf16[16,5120]{1,0:T(8,128)(2,1)S(1)}, bf16[16,5120]{1,0:T(8,128)(2,1)S(1)}) custom-call(bf16[5120,640]{1,0:T(8,128)(2,1)S(1)} %bitcast.16, bf16[640,5120]{1,0:T(8,128)(2,1)S(1)} %bitcast.17, bf16[32,5120]{1,0:T(8,128)(2,1)S(1)} %join.3.refs_3_.refs_2_, ...), custom_call_target="tpu_custom_call" | custom-call | flops 1677721600 | bytes 16711680 | tf_op jit(solution)/shard_map/expert/pallas_call | solution.py:142
  65.5 1.4 %collective-permute-start.30 = (bf16[16,5120]{1,0:T(8,128)(2,1)S(1)}, bf16[16,5120]{1,0:T(8,128)(2,1)S(1)}, u32[]{:S(2)}, u32[]{:S(2)}) collective-permute-start(bf16[16,5120]{1,0:T(8,128)(2,1)S(1)} %get-tuple-element.68), channel_id=1, source_target_pairs={{2,0},{3,1},{0,2},{1,3},{6,4},{7,5},{4,6},{5,7},{10,8},{11,9},{8,1... | collective-permute-start | bytes 491528 | tf_op jit(solution)/shard_map/ppermute | solution.py:50
  66.9 0.2 collective-permute-start.27
  67.1 2.0 %collective-permute-start.28 = (bf16[8,5120]{1,0:T(8,128)(2,1)S(1)}, bf16[8,5120]{1,0:T(8,128)(2,1)S(1)}, u32[]{:S(2)}, u32[]{:S(2)}) collective-permute-start(bf16[8,5120]{1,0:T(8,128)(2,1)S(1)} %get-tuple-element.66), channel_id=1, source_target_pairs={{12,0},{13,1},{14,2},{15,3},{8,4},{9,5},{10,6},{11,7},{4,8},{5,9},... | collective-permute-start | bytes 245768 | tf_op jit(solution)/shard_map/ppermute | solution.py:50
  69.1 3.2 %collective-permute-done.28.refs_3_ = bf16[8,5120]{1,0:T(8,128)(2,1)S(1)} collective-permute-done((bf16[8,5120]{1,0:T(8,128)(2,1)S(1)}, bf16[8,5120]{1,0:T(8,128)(2,1)S(1)}, u32[]{:S(2)}, u32[]{:S(2)}) %collective-permute-start.28) | collective-permute-done | bytes 81952 | tf_op jit(solution)/shard_map/ppermute | solution.py:50
  72.4 1.3 %collective-permute-start.31 = (bf16[32,5120]{1,0:T(8,128)(2,1)S(1)}, bf16[32,5120]{1,0:T(8,128)(2,1)S(1)}, u32[]{:S(2)}, u32[]{:S(2)}) collective-permute-start(bf16[32,5120]{1,0:T(8,128)(2,1)S(1)} %add_half.7), channel_id=1, source_target_pairs={{1,0},{0,1},{3,2},{2,3},{5,4},{4,5},{7,6},{6,7},{9,8},{8,9},{11,10... | collective-permute-start | bytes 983048 | tf_op jit(solution)/shard_map/ppermute | solution.py:50
  73.8 0.2 collective-permute-start.29
  74.0 1.3 %collective-permute-start.35 = (f32[8,5120]{1,0:T(8,128)S(1)}, f32[8,5120]{1,0:T(8,128)S(1)}, u32[]{:S(2)}, u32[]{:S(2)}) collective-permute-start(f32[8,5120]{1,0:T(8,128)S(1)} %add_last.2.refs_2_.second_ref), channel_id=1, source_target_pairs={{0,16},{1,17},{2,18},{3,19},{4,20},{5,21},{6,22},{7,23},{8,24},{9,... | collective-permute-start | bytes 491528 | tf_op jit(solution)/shard_map/ppermute | solution.py:27
  75.3 4.8 %collective-permute-done.31.refs_2_ = bf16[32,5120]{1,0:T(8,128)(2,1)S(1)} collective-permute-done((bf16[32,5120]{1,0:T(8,128)(2,1)S(1)}, bf16[32,5120]{1,0:T(8,128)(2,1)S(1)}, u32[]{:S(2)}, u32[]{:S(2)}) %collective-permute-start.31) | collective-permute-done | bytes 327712 | tf_op jit(solution)/shard_map/ppermute | solution.py:50
  80.1 0.1 add_blocks.3
  80.2 0.7 collective-permute-start.32
  80.9 1.6 %collective-permute-start.33 = (bf16[8,5120]{1,0:T(8,128)(2,1)S(1)}, bf16[8,5120]{1,0:T(8,128)(2,1)S(1)}, u32[]{:S(2)}, u32[]{:S(2)}) collective-permute-start(bf16[8,5120]{1,0:T(8,128)(2,1)S(1)} %get-tuple-element.72), channel_id=1, source_target_pairs={{8,0},{9,1},{10,2},{11,3},{12,4},{13,5},{14,6},{15,7},{0,8},{1,9},... | collective-permute-start | bytes 245768 | tf_op jit(solution)/shard_map/ppermute | solution.py:50
  82.6 1.3 %collective-permute-start.34 = (bf16[8,5120]{1,0:T(8,128)(2,1)S(1)}, bf16[8,5120]{1,0:T(8,128)(2,1)S(1)}, u32[]{:S(2)}, u32[]{:S(2)}) collective-permute-start(bf16[8,5120]{1,0:T(8,128)(2,1)S(1)} %get-tuple-element.73), channel_id=1, source_target_pairs={{12,0},{13,1},{14,2},{15,3},{8,4},{9,5},{10,6},{11,7},{4,8},{5,9},... | collective-permute-start | bytes 245768 | tf_op jit(solution)/shard_map/ppermute | solution.py:50
  83.9 0.6 collective-permute-done.35.first_ref
  84.4 0.8 lay_out.1
  85.2 0.8 collective-permute-done.33.refs_2_
  86.0 1.8 %collective-permute-done.34.refs_3_ = bf16[8,5120]{1,0:T(8,128)(2,1)S(1)} collective-permute-done((bf16[8,5120]{1,0:T(8,128)(2,1)S(1)}, bf16[8,5120]{1,0:T(8,128)(2,1)S(1)}, u32[]{:S(2)}, u32[]{:S(2)}) %collective-permute-start.34) | collective-permute-done | bytes 81952 | tf_op jit(solution)/shard_map/ppermute | solution.py:50
  87.8 1.3 %collective-permute-start.36 = (f32[8,5248]{1,0:T(8,128)S(1)}, f32[8,5248]{1,0:T(8,128)S(1)}, u32[]{:S(2)}, u32[]{:S(2)}) collective-permute-start(f32[8,5248]{1,0:T(8,128)S(1)} %add_last.3.back_ref), channel_id=1, source_target_pairs={{0,16},{1,17},{2,18},{3,19},{4,20},{5,21},{6,22},{7,23},{8,24},{9,... | collective-permute-start | bytes 503816 | tf_op jit(solution)/shard_map/ppermute | solution.py:17
  89.1 1.5 %finish.2 = bf16[128,5120]{1,0:T(8,128)(2,1)} custom-call(s32[1]{0:T(128)} %bitcast.refs_0_.section, bf16[128,5120]{1,0:T(8,128)(2,1)S(1)} %get-tuple-element.52.res_ref, f32[8,5248]{1,0:T(8,128)S(1)} %add_last.3.back_ref), custom_call_target="tpu_custom_call" | custom-call | flops 32768000 | bytes 3276800 | tf_op jit(solution)/shard_map/finish/pallas_call | solution.py:541
  90.6 8.6 %collective-permute-done.36.back_ref = f32[8,5248]{1,0:T(8,128)S(1)} collective-permute-done((f32[8,5248]{1,0:T(8,128)S(1)}, f32[8,5248]{1,0:T(8,128)S(1)}, u32[]{:S(2)}, u32[]{:S(2)}) %collective-permute-start.36) | collective-permute-done | bytes 167968 | tf_op jit(solution)/shard_map/ppermute | solution.py:17
  99.2 1.5 %finish.3 = bf16[128,5120]{1,0:T(8,128)(2,1)} custom-call(s32[1]{0:T(128)} %bitcast.refs_0_.section, bf16[128,5120]{1,0:T(8,128)(2,1)S(1)} %collective-permute-done.24.refs_7_.res_ref, f32[8,5248]{1,0:T(8,128)S(1)} %collective-permute-done.36.back_ref, bf16[128,5120]{1,0:T(8,128)(2,1)} %get-tuple-element.75.refs_0_), custom_call_target="tpu_custom_call", output_to_operand_aliasing={{}: (3, {})} | custom-call | flops 32768000 | bytes 3276800 | tf_op jit(solution)/shard_map/finish/pallas_call | solution.py:541
  (54 shorter events, 0.7 us)
Async XLA Ops:
  0.6 1.7 %collective-permute-start = (bf16[8,2,5120]{2,1,0:T(2,128)(2,1)}, bf16[8,2,5120]{2,1,0:T(2,128)(2,1)S(1)}, u32[]{:S(2)}, u32[]{:S(2)}) collective-permute-start(bf16[8,2,5120]{2,1,0:T(2,128)(2,1)} %bitcast.26), channel_id=1, source_target_pairs={{0,16},{16,0},{1,17},{17,1},{2,18},{18,2},{3,19},{19,3},{4,20},{20... | collective-permute-start | bytes 491528 | tf_op jit(solution)/shard_map/ppermute | solution.py:22
  3.3 7.1 %collective-permute-start.3 = (bf16[8,5120]{1,0:T(8,128)(2,1)S(1)}, bf16[8,5120]{1,0:T(8,128)(2,1)S(1)}, u32[]{:S(2)}, u32[]{:S(2)}) collective-permute-start(bf16[8,5120]{1,0:T(8,128)(2,1)S(1)} %bitcast.20), channel_id=1, source_target_pairs={{0,12},{1,13},{2,14},{3,15},{4,8},{5,9},{6,10},{7,11},{8,4},{9,5},... | collective-permute-start | bytes 245768 | tf_op jit(solution)/shard_map/ppermute | solution.py:50
  7.8 6.6 %collective-permute-start.2 = (bf16[8,5120]{1,0:T(8,128)(2,1)S(1)}, bf16[8,5120]{1,0:T(8,128)(2,1)S(1)}, u32[]{:S(2)}, u32[]{:S(2)}) collective-permute-start(bf16[8,5120]{1,0:T(8,128)(2,1)S(1)} %bitcast.21), channel_id=1, source_target_pairs={{0,8},{1,9},{2,10},{3,11},{4,12},{5,13},{6,14},{7,15},{8,0},{9,1},... | collective-permute-start | bytes 245768 | tf_op jit(solution)/shard_map/ppermute | solution.py:50
  7.8 6.6 %collective-permute-start.1 = (bf16[8,5120]{1,0:T(8,128)(2,1)S(1)}, bf16[8,5120]{1,0:T(8,128)(2,1)S(1)}, u32[]{:S(2)}, u32[]{:S(2)}) collective-permute-start(bf16[8,5120]{1,0:T(8,128)(2,1)S(1)} %bitcast.22), channel_id=1, source_target_pairs={{0,4},{1,5},{2,6},{3,7},{4,0},{5,1},{6,2},{7,3},{8,12},{9,13},{10,... | collective-permute-start | bytes 245768 | tf_op jit(solution)/shard_map/ppermute | solution.py:50
  14.5 9.2 %collective-permute-start.7 = (bf16[32,5120]{1,0:T(8,128)(2,1)S(1)}, bf16[32,5120]{1,0:T(8,128)(2,1)S(1)}, u32[]{:S(2)}, u32[]{:S(2)}) collective-permute-start(bf16[32,5120]{1,0:T(8,128)(2,1)S(1)} %join.2.refs_4_), channel_id=1, source_target_pairs={{0,2},{1,3},{2,0},{3,1},{4,6},{5,7},{6,4},{7,5},{8,10},{9,11},{10,... | collective-permute-start | bytes 983048 | tf_op jit(solution)/shard_map/ppermute | solution.py:50
  15.8 8.9 %collective-permute-start.6 = (bf16[32,5120]{1,0:T(8,128)(2,1)S(1)}, bf16[32,5120]{1,0:T(8,128)(2,1)S(1)}, u32[]{:S(2)}, u32[]{:S(2)}) collective-permute-start(bf16[32,5120]{1,0:T(8,128)(2,1)S(1)} %join.2.refs_4_), channel_id=1, source_target_pairs={{0,1},{1,0},{2,3},{3,2},{4,5},{5,4},{6,7},{7,6},{8,9},{9,8},{10,11... | collective-permute-start | bytes 983048 | tf_op jit(solution)/shard_map/ppermute | solution.py:50
  17.0 1.3 %copy-start.1 = (bf16[1,128,5120]{2,1,0:T(8,128)(2,1)S(1)}, bf16[1,128,5120]{2,1,0:T(8,128)(2,1)}, u32[]{:S(2)}) copy-start(bf16[1,128,5120]{2,1,0:T(8,128)(2,1)} %param.9) | copy-start | bytes 3932164
  18.3 0.7 copy-start.4
  19.0 0.7 copy-start.5
  19.7 0.7 copy-start.6
  20.3 2.8 %copy-start.2 = (bf16[1,128,5120]{2,1,0:T(8,128)(2,1)S(1)}, bf16[1,128,5120]{2,1,0:T(8,128)(2,1)}, u32[]{:S(2)}) copy-start(bf16[1,128,5120]{2,1,0:T(8,128)(2,1)} %param.11) | copy-start | bytes 3932164
  21.2 4.8 %collective-permute-start.4 = (bf16[128,1280]{1,0:T(8,128)(2,1)S(1)}, bf16[128,1280]{1,0:T(8,128)(2,1)S(1)}, u32[]{:S(2)}, u32[]{:S(2)}) collective-permute-start(bf16[128,1280]{1,0:T(8,128)(2,1)S(1)} %get-tuple-element.41), channel_id=1, source_target_pairs={{0,16},{16,0},{1,17},{17,1},{2,18},{18,2},{3,19},{19,3},{4,20},{20... | collective-permute-start | bytes 983048 | tf_op jit(solution)/shard_map/ppermute | solution.py:22
  23.0 4.3 %collective-permute-start.5 = (bf16[128,1280]{1,0:T(8,128)(2,1)S(1)}, bf16[128,1280]{1,0:T(8,128)(2,1)S(1)}, u32[]{:S(2)}, u32[]{:S(2)}) collective-permute-start(bf16[128,1280]{1,0:T(8,128)(2,1)S(1)} %get-tuple-element.42), channel_id=1, source_target_pairs={{0,16},{16,0},{1,17},{17,1},{2,18},{18,2},{3,19},{19,3},{4,20},{20... | collective-permute-start | bytes 983048 | tf_op jit(solution)/shard_map/ppermute | solution.py:22
  23.2 5.4 %collective-permute-start.10 = (bf16[128,1280]{1,0:T(8,128)(2,1)S(1)}, bf16[128,1280]{1,0:T(8,128)(2,1)S(1)}, u32[]{:S(2)}, u32[]{:S(2)}) collective-permute-start(bf16[128,1280]{1,0:T(8,128)(2,1)S(1)} %get-tuple-element.45), channel_id=1, source_target_pairs={{0,16},{16,0},{1,17},{17,1},{2,18},{18,2},{3,19},{19,3},{4,20},{20... | collective-permute-start | bytes 983048 | tf_op jit(solution)/shard_map/ppermute | solution.py:22
  23.7 4.9 %collective-permute-start.11 = (bf16[128,1280]{1,0:T(8,128)(2,1)S(1)}, bf16[128,1280]{1,0:T(8,128)(2,1)S(1)}, u32[]{:S(2)}, u32[]{:S(2)}) collective-permute-start(bf16[128,1280]{1,0:T(8,128)(2,1)S(1)} %get-tuple-element.46), channel_id=1, source_target_pairs={{0,16},{16,0},{1,17},{17,1},{2,18},{18,2},{3,19},{19,3},{4,20},{20... | collective-permute-start | bytes 983048 | tf_op jit(solution)/shard_map/ppermute | solution.py:22
  24.7 4.6 %collective-permute-start.8 = (bf16[16,5120]{1,0:T(8,128)(2,1)S(1)}, bf16[16,5120]{1,0:T(8,128)(2,1)S(1)}, u32[]{:S(2)}, u32[]{:S(2)}) collective-permute-start(bf16[16,5120]{1,0:T(8,128)(2,1)S(1)} %slice.17), channel_id=1, source_target_pairs={{0,1},{1,0},{2,3},{3,2},{4,5},{5,4},{6,7},{7,6},{8,9},{9,8},{10,11... | collective-permute-start | bytes 491528 | tf_op jit(solution)/shard_map/ppermute | solution.py:50
  26.0 4.5 %collective-permute-start.9 = (bf16[16,5120]{1,0:T(8,128)(2,1)S(1)}, bf16[16,5120]{1,0:T(8,128)(2,1)S(1)}, u32[]{:S(2)}, u32[]{:S(2)}) collective-permute-start(bf16[16,5120]{1,0:T(8,128)(2,1)S(1)} %slice.18), channel_id=1, source_target_pairs={{0,2},{1,3},{2,0},{3,1},{4,6},{5,7},{6,4},{7,5},{8,10},{9,11},{10,... | collective-permute-start | bytes 491528 | tf_op jit(solution)/shard_map/ppermute | solution.py:50
  27.3 34.0 %collective-permute-start.24 = (bf16[128,5120]{1,0:T(8,128)(2,1)S(1)}, bf16[128,5120]{1,0:T(8,128)(2,1)S(1)}, u32[]{:S(2)}, u32[]{:S(2)}) collective-permute-start(bf16[128,5120]{1,0:T(8,128)(2,1)S(1)} %get-tuple-element.40.refs_1_), channel_id=1, source_target_pairs={{0,16},{1,17},{2,18},{3,19},{4,20},{5,21},{6,22},{7,23},{8,24},{9,... | collective-permute-start | bytes 3932168 | tf_op jit(solution)/shard_map/ppermute | solution.py:17
  31.9 5.2 %collective-permute-start.12 = (bf16[128,2560]{1,0:T(8,128)(2,1)S(1)}, bf16[128,2560]{1,0:T(8,128)(2,1)S(1)}, u32[]{:S(2)}, u32[]{:S(2)}) collective-permute-start(bf16[128,2560]{1,0:T(8,128)(2,1)S(1)} %get-tuple-element.47.refs_3_), channel_id=1, source_target_pairs={{0,16},{1,17},{2,18},{3,19},{4,20},{5,21},{6,22},{7,23},{8,24},{9,... | collective-permute-start | bytes 1966088 | tf_op jit(solution)/shard_map/ppermute | solution.py:27
  33.2 3.9 %copy-start.3 = (f32[1,5120]{1,0:T(1,128)S(1)}, f32[1,5120]{1,0:T(1,128)}, u32[]{:S(2)}) copy-start(f32[1,5120]{1,0:T(1,128)} %refs_4_.1) | copy-start | bytes 61444
  33.2 29.9 %slice-start = ((s8[6553600]{0:T(1024)(128)(4,1)}), s8[4194304]{0:T(1024)(128)(4,1)S(1)}, s32[]{:S(2)}) async-start(s8[6553600]{0:T(1024)(128)(4,1)} %bitcast.14), calls=%async_computation | async-start | bytes 8388608
  34.6 5.5 %collective-permute-start.17 = (bf16[16,5120]{1,0:T(8,128)(2,1)S(1)}, bf16[16,5120]{1,0:T(8,128)(2,1)S(1)}, u32[]{:S(2)}, u32[]{:S(2)}) collective-permute-start(bf16[16,5120]{1,0:T(8,128)(2,1)S(1)} %get-tuple-element.57), channel_id=1, source_target_pairs={{2,0},{3,1},{0,2},{1,3},{6,4},{7,5},{4,6},{5,7},{10,8},{11,9},{8,1... | collective-permute-start | bytes 491528 | tf_op jit(solution)/shard_map/ppermute | solution.py:50
  36.8 4.6 %collective-permute-start.16 = (bf16[16,5120]{1,0:T(8,128)(2,1)S(1)}, bf16[16,5120]{1,0:T(8,128)(2,1)S(1)}, u32[]{:S(2)}, u32[]{:S(2)}) collective-permute-start(bf16[16,5120]{1,0:T(8,128)(2,1)S(1)} %get-tuple-element.55), channel_id=1, source_target_pairs={{1,0},{0,1},{3,2},{2,3},{5,4},{4,5},{7,6},{6,7},{9,8},{8,9},{11,10... | collective-permute-start | bytes 491528 | tf_op jit(solution)/shard_map/ppermute | solution.py:50
  37.1 26.1 %slice-start.1 = ((s8[6553600]{0:T(1024)(128)(4,1)}), s8[2359296]{0:T(1024)(128)(4,1)S(1)}, s32[]{:S(2)}) async-start(s8[6553600]{0:T(1024)(128)(4,1)} %bitcast.14), calls=%async_computation.1 | async-start | bytes 4718592
  37.1 26.1 %copy-start = (bf16[1,640,5120]{2,1,0:T(8,128)(2,1)S(1)}, bf16[1,640,5120]{2,1,0:T(8,128)(2,1)}, u32[]{:S(2)}) copy-start(bf16[1,640,5120]{2,1,0:T(8,128)(2,1)} %param.15) | copy-start | bytes 19660804
  37.7 5.2 %collective-permute-start.15 = (bf16[8,5120]{1,0:T(8,128)(2,1)S(1)}, bf16[8,5120]{1,0:T(8,128)(2,1)S(1)}, u32[]{:S(2)}, u32[]{:S(2)}) collective-permute-start(bf16[8,5120]{1,0:T(8,128)(2,1)S(1)} %get-tuple-element.53.refs_0_.after_any), channel_id=1, source_target_pairs={{0,12},{1,13},{2,14},{3,15},{4,8},{5,9},{6,10},{7,11},{8,4},{9,5},... | collective-permute-start | bytes 245768 | tf_op jit(solution)/shard_map/ppermute | solution.py:50
  40.1 7.5 %collective-permute-start.14 = (bf16[8,5120]{1,0:T(8,128)(2,1)S(1)}, bf16[8,5120]{1,0:T(8,128)(2,1)S(1)}, u32[]{:S(2)}, u32[]{:S(2)}) collective-permute-start(bf16[8,5120]{1,0:T(8,128)(2,1)S(1)} %get-tuple-element.53.refs_0_.after_any), channel_id=1, source_target_pairs={{0,8},{1,9},{2,10},{3,11},{4,12},{5,13},{6,14},{7,15},{8,0},{9,1},... | collective-permute-start | bytes 245768 | tf_op jit(solution)/shard_map/ppermute | solution.py:50
  40.1 7.5 %collective-permute-start.13 = (bf16[8,5120]{1,0:T(8,128)(2,1)S(1)}, bf16[8,5120]{1,0:T(8,128)(2,1)S(1)}, u32[]{:S(2)}, u32[]{:S(2)}) collective-permute-start(bf16[8,5120]{1,0:T(8,128)(2,1)S(1)} %get-tuple-element.53.refs_0_.after_any), channel_id=1, source_target_pairs={{0,4},{1,5},{2,6},{3,7},{4,0},{5,1},{6,2},{7,3},{8,12},{9,13},{10,... | collective-permute-start | bytes 245768 | tf_op jit(solution)/shard_map/ppermute | solution.py:50
  41.4 7.6 %collective-permute-start.21 = (bf16[32,5120]{1,0:T(8,128)(2,1)S(1)}, bf16[32,5120]{1,0:T(8,128)(2,1)S(1)}, u32[]{:S(2)}, u32[]{:S(2)}) collective-permute-start(bf16[32,5120]{1,0:T(8,128)(2,1)S(1)} %add_half.5.refs_5_), channel_id=1, source_target_pairs={{1,0},{0,1},{3,2},{2,3},{5,4},{4,5},{7,6},{6,7},{9,8},{8,9},{11,10... | collective-permute-start | bytes 983048 | tf_op jit(solution)/shard_map/ppermute | solution.py:50
  42.9 6.2 %collective-permute-start.20 = (bf16[32,5120]{1,0:T(8,128)(2,1)S(1)}, bf16[32,5120]{1,0:T(8,128)(2,1)S(1)}, u32[]{:S(2)}, u32[]{:S(2)}) collective-permute-start(bf16[32,5120]{1,0:T(8,128)(2,1)S(1)} %add_half.4.refs_4_), channel_id=1, source_target_pairs={{2,0},{3,1},{0,2},{1,3},{6,4},{7,5},{4,6},{5,7},{10,8},{11,9},{8,1... | collective-permute-start | bytes 983048 | tf_op jit(solution)/shard_map/ppermute | solution.py:50
  47.7 9.8 %collective-permute-start.19 = (bf16[32,5120]{1,0:T(8,128)(2,1)S(1)}, bf16[32,5120]{1,0:T(8,128)(2,1)S(1)}, u32[]{:S(2)}, u32[]{:S(2)}) collective-permute-start(bf16[32,5120]{1,0:T(8,128)(2,1)S(1)} %join.3.refs_3_.refs_2_), channel_id=1, source_target_pairs={{0,2},{1,3},{2,0},{3,1},{4,6},{5,7},{6,4},{7,5},{8,10},{9,11},{10,... | collective-permute-start | bytes 983048 | tf_op jit(solution)/shard_map/ppermute | solution.py:50
  48.9 8.6 %collective-permute-start.18 = (bf16[32,5120]{1,0:T(8,128)(2,1)S(1)}, bf16[32,5120]{1,0:T(8,128)(2,1)S(1)}, u32[]{:S(2)}, u32[]{:S(2)}) collective-permute-start(bf16[32,5120]{1,0:T(8,128)(2,1)S(1)} %join.3.refs_3_.refs_2_), channel_id=1, source_target_pairs={{0,1},{1,0},{2,3},{3,2},{4,5},{5,4},{6,7},{7,6},{8,9},{9,8},{10,11... | collective-permute-start | bytes 983048 | tf_op jit(solution)/shard_map/ppermute | solution.py:50
  57.4 5.7 %collective-permute-start.22 = (bf16[16,5120]{1,0:T(8,128)(2,1)S(1)}, bf16[16,5120]{1,0:T(8,128)(2,1)S(1)}, u32[]{:S(2)}, u32[]{:S(2)}) collective-permute-start(bf16[16,5120]{1,0:T(8,128)(2,1)S(1)} %get-tuple-element.59), channel_id=1, source_target_pairs={{0,1},{1,0},{2,3},{3,2},{4,5},{5,4},{6,7},{7,6},{8,9},{9,8},{10,11... | collective-permute-start | bytes 491528 | tf_op jit(solution)/shard_map/ppermute | solution.py:50
  58.7 4.4 %collective-permute-start.23 = (bf16[16,5120]{1,0:T(8,128)(2,1)S(1)}, bf16[16,5120]{1,0:T(8,128)(2,1)S(1)}, u32[]{:S(2)}, u32[]{:S(2)}) collective-permute-start(bf16[16,5120]{1,0:T(8,128)(2,1)S(1)} %get-tuple-element.60), channel_id=1, source_target_pairs={{0,2},{1,3},{2,0},{3,1},{4,6},{5,7},{6,4},{7,5},{8,10},{9,11},{10,... | collective-permute-start | bytes 491528 | tf_op jit(solution)/shard_map/ppermute | solution.py:50
  58.9 3.3 %collective-permute-start.25 = (bf16[8,5120]{1,0:T(8,128)(2,1)S(1)}, bf16[8,5120]{1,0:T(8,128)(2,1)S(1)}, u32[]{:S(2)}, u32[]{:S(2)}) collective-permute-start(bf16[8,5120]{1,0:T(8,128)(2,1)S(1)} %get-tuple-element.61), channel_id=1, source_target_pairs={{4,0},{5,1},{6,2},{7,3},{0,4},{1,5},{2,6},{3,7},{12,8},{13,9},{14,... | collective-permute-start | bytes 245768 | tf_op jit(solution)/shard_map/ppermute | solution.py:50
  58.9 4.3 %collective-permute-start.26 = (bf16[8,5120]{1,0:T(8,128)(2,1)S(1)}, bf16[8,5120]{1,0:T(8,128)(2,1)S(1)}, u32[]{:S(2)}, u32[]{:S(2)}) collective-permute-start(bf16[8,5120]{1,0:T(8,128)(2,1)S(1)} %get-tuple-element.62), channel_id=1, source_target_pairs={{8,0},{9,1},{10,2},{11,3},{12,4},{13,5},{14,6},{15,7},{0,8},{1,9},... | collective-permute-start | bytes 245768 | tf_op jit(solution)/shard_map/ppermute | solution.py:50
  65.5 6.8 %collective-permute-start.30 = (bf16[16,5120]{1,0:T(8,128)(2,1)S(1)}, bf16[16,5120]{1,0:T(8,128)(2,1)S(1)}, u32[]{:S(2)}, u32[]{:S(2)}) collective-permute-start(bf16[16,5120]{1,0:T(8,128)(2,1)S(1)} %get-tuple-element.68), channel_id=1, source_target_pairs={{2,0},{3,1},{0,2},{1,3},{6,4},{7,5},{4,6},{5,7},{10,8},{11,9},{8,1... | collective-permute-start | bytes 491528 | tf_op jit(solution)/shard_map/ppermute | solution.py:50
  66.9 6.8 %collective-permute-start.27 = (bf16[16,5120]{1,0:T(8,128)(2,1)S(1)}, bf16[16,5120]{1,0:T(8,128)(2,1)S(1)}, u32[]{:S(2)}, u32[]{:S(2)}) collective-permute-start(bf16[16,5120]{1,0:T(8,128)(2,1)S(1)} %get-tuple-element.65), channel_id=1, source_target_pairs={{1,0},{0,1},{3,2},{2,3},{5,4},{4,5},{7,6},{6,7},{9,8},{8,9},{11,10... | collective-permute-start | bytes 491528 | tf_op jit(solution)/shard_map/ppermute | solution.py:50
  67.1 5.2 %collective-permute-start.28 = (bf16[8,5120]{1,0:T(8,128)(2,1)S(1)}, bf16[8,5120]{1,0:T(8,128)(2,1)S(1)}, u32[]{:S(2)}, u32[]{:S(2)}) collective-permute-start(bf16[8,5120]{1,0:T(8,128)(2,1)S(1)} %get-tuple-element.66), channel_id=1, source_target_pairs={{12,0},{13,1},{14,2},{15,3},{8,4},{9,5},{10,6},{11,7},{4,8},{5,9},... | collective-permute-start | bytes 245768 | tf_op jit(solution)/shard_map/ppermute | solution.py:50
  72.4 7.7 %collective-permute-start.31 = (bf16[32,5120]{1,0:T(8,128)(2,1)S(1)}, bf16[32,5120]{1,0:T(8,128)(2,1)S(1)}, u32[]{:S(2)}, u32[]{:S(2)}) collective-permute-start(bf16[32,5120]{1,0:T(8,128)(2,1)S(1)} %add_half.7), channel_id=1, source_target_pairs={{1,0},{0,1},{3,2},{2,3},{5,4},{4,5},{7,6},{6,7},{9,8},{8,9},{11,10... | collective-permute-start | bytes 983048 | tf_op jit(solution)/shard_map/ppermute | solution.py:50
  73.8 6.3 %collective-permute-start.29 = (bf16[32,5120]{1,0:T(8,128)(2,1)S(1)}, bf16[32,5120]{1,0:T(8,128)(2,1)S(1)}, u32[]{:S(2)}, u32[]{:S(2)}) collective-permute-start(bf16[32,5120]{1,0:T(8,128)(2,1)S(1)} %add_half.6), channel_id=1, source_target_pairs={{2,0},{3,1},{0,2},{1,3},{6,4},{7,5},{4,6},{5,7},{10,8},{11,9},{8,1... | collective-permute-start | bytes 983048 | tf_op jit(solution)/shard_map/ppermute | solution.py:50
  74.0 10.4 %collective-permute-start.35 = (f32[8,5120]{1,0:T(8,128)S(1)}, f32[8,5120]{1,0:T(8,128)S(1)}, u32[]{:S(2)}, u32[]{:S(2)}) collective-permute-start(f32[8,5120]{1,0:T(8,128)S(1)} %add_last.2.refs_2_.second_ref), channel_id=1, source_target_pairs={{0,16},{1,17},{2,18},{3,19},{4,20},{5,21},{6,22},{7,23},{8,24},{9,... | collective-permute-start | bytes 491528 | tf_op jit(solution)/shard_map/ppermute | solution.py:27
  80.2 5.0 %collective-permute-start.32 = (bf16[8,5120]{1,0:T(8,128)(2,1)S(1)}, bf16[8,5120]{1,0:T(8,128)(2,1)S(1)}, u32[]{:S(2)}, u32[]{:S(2)}) collective-permute-start(bf16[8,5120]{1,0:T(8,128)(2,1)S(1)} %get-tuple-element.71), channel_id=1, source_target_pairs={{4,0},{5,1},{6,2},{7,3},{0,4},{1,5},{2,6},{3,7},{12,8},{13,9},{14,... | collective-permute-start | bytes 245768 | tf_op jit(solution)/shard_map/ppermute | solution.py:50
  80.9 5.1 %collective-permute-start.33 = (bf16[8,5120]{1,0:T(8,128)(2,1)S(1)}, bf16[8,5120]{1,0:T(8,128)(2,1)S(1)}, u32[]{:S(2)}, u32[]{:S(2)}) collective-permute-start(bf16[8,5120]{1,0:T(8,128)(2,1)S(1)} %get-tuple-element.72), channel_id=1, source_target_pairs={{8,0},{9,1},{10,2},{11,3},{12,4},{13,5},{14,6},{15,7},{0,8},{1,9},... | collective-permute-start | bytes 245768 | tf_op jit(solution)/shard_map/ppermute | solution.py:50
  82.6 5.2 %collective-permute-start.34 = (bf16[8,5120]{1,0:T(8,128)(2,1)S(1)}, bf16[8,5120]{1,0:T(8,128)(2,1)S(1)}, u32[]{:S(2)}, u32[]{:S(2)}) collective-permute-start(bf16[8,5120]{1,0:T(8,128)(2,1)S(1)} %get-tuple-element.73), channel_id=1, source_target_pairs={{12,0},{13,1},{14,2},{15,3},{8,4},{9,5},{10,6},{11,7},{4,8},{5,9},... | collective-permute-start | bytes 245768 | tf_op jit(solution)/shard_map/ppermute | solution.py:50
  87.8 11.4 %collective-permute-start.36 = (f32[8,5248]{1,0:T(8,128)S(1)}, f32[8,5248]{1,0:T(8,128)S(1)}, u32[]{:S(2)}, u32[]{:S(2)}) collective-permute-start(f32[8,5248]{1,0:T(8,128)S(1)} %add_last.3.back_ref), channel_id=1, source_target_pairs={{0,16},{1,17},{2,18},{3,19},{4,20},{5,21},{6,22},{7,23},{8,24},{9,... | collective-permute-start | bytes 503816 | tf_op jit(solution)/shard_map/ppermute | solution.py:17

commit v10 on v7

--- a/solution.py
+++ b/solution.py
@@ -239,7 +239,7 @@
 
 
 def head_loop(heads, some_heads):
-    few = next(u for u in (5, 4, 2, 1) if heads % u == 0)
+    few = next(u for u in (20, 10, 5, 4, 2, 1) if heads % u == 0)
 
     def step(g, carry):
         numbers = [g * few + u for u in range(few)]
@@ -503,7 +503,7 @@
 def finish(section, res, back, room=None):
     tokens, width = res.shape
     one = jax.ShapeDtypeStruct((tokens, width), jnp.bfloat16)
-    step = next(s for s in (1280, 1024, 512, 256, 128) if width % s == 0)
+    step = next(s for s in (640, 512, 256, 128) if width % s == 0)
     parts = [slice(at, at + step) for at in range(0, width, step)]
 
     def kernel(section, res_ref, back_ref, *refs):

time: 102 us -> 100 us (0.980)
  Pallas kernels: 12.3 us -> 10.6 us
  waiting for transfers between devices: 46.1 us -> 45 us
  starting transfers between devices: 41.2 us -> 42.3 us
    ppermute x28, waiting for transfers between devices: 36.4 us -> 34.5 us  [shift(): return lax.ppermute(block, 'expert', route)]
    pallas_call x18, Pallas kernels: 9.26 us -> 7.62 us  [local_kernel(): pl.pallas_call(body, out_shape=tuple(outs), in_specs=in_specs, out_specs=...]
    ppermute x28, starting transfers between devices: 31.4 us -> 32.5 us  [shift(): return lax.ppermute(block, 'expert', route)]
  transfers between devices with their start and end apart: 37 -> 37, of which waited for: 17 -> 19; matrix products, arithmetic and copies ran while one was open for 0% -> 0% of each run, Pallas kernels for 8% -> 7%
where the time goes in v10:
time: 100 us
  waiting for transfers between devices  45 us (45%)
  starting transfers between devices  42.3 us (42%)
  Pallas kernels  10.6 us (11%)
  local copies, waits for them, and re-layouts  1.24 us (1%)
    ppermute x28, waiting for transfers between devices, shift(): return lax.ppermute(block, 'expert', route)  34.5 us
    ppermute x28, starting transfers between devices, shift(): return lax.ppermute(block, 'expert', route)  32.5 us
    ppermute x2, waiting for transfers between devices, passed_along(): return lax.ppermute(block, axis, route)  8.62 us
    pallas_call x18, Pallas kernels, local_kernel(): pl.pallas_call(body, out_shape=tuple(outs), in_specs=in_specs, out_specs=...  7.62 us
    ppermute x5, starting transfers between devices, swapped(): lax.ppermute(block, 'section', [(i, (i + sections // 2) % sections) for i...  4.61 us
    pallas_call x2, Pallas kernels, finish(): pl.pallas_call(kernel, out_shape=one, in_specs=[pl.BlockSpec(memory_space...  2.99 us
    ppermute x2, starting transfers between devices, passed_along(): return lax.ppermute(block, axis, route)  2.57 us
    ppermute x2, starting transfers between devices, to_decoder(): lax.ppermute(block, 'section', [(i, i + apart) for i in range(apart)])  2.57 us
  transfers between devices with their start and end apart: 37, of which 19 were waited for; matrix products, arithmetic and copies ran while one was open for 0% of the time, Pallas kernels for 7%

profile of v10, /device:TPU:1, one launch (start us, length us, event | category | flops | bytes accessed | tf_op | source)
XLA Modules:
  0.0 100.1 jit_solution(6529800437290861129)
XLA Ops:
  0.7 1.1 %slice_bitcast_fusion = (bf16[1,8,2,2560]{3,2,1,0:T(2,128)(2,1)S(1)}, bf16[1,8,2,2560]{3,2,1,0:T(2,128)(2,1)S(1)}) fusion(bf16[1,8,2,5120]{3,2,1,0:T(2,128)(2,1)} %param.10), kind=kLoop, calls=%fused_computation | loop fusion | bytes 327680
  1.8 0.1 collective-permute-start
  2.0 1.2 %collective-permute-done = bf16[8,5120]{1,0:T(8,128)(2,1)S(1)} collective-permute-done((bf16[8,5120]{1,0:T(8,128)(2,1)S(1)}, bf16[8,5120]{1,0:T(8,128)(2,1)S(1)}, u32[]{:S(2)}, u32[]{:S(2)}) %collective-permute-start) | collective-permute-done | bytes 81952 | tf_op jit(solution)/shard_map/ppermute | solution.py:22
  3.2 4.5 %collective-permute-start.3 = (bf16[8,5120]{1,0:T(8,128)(2,1)S(1)}, bf16[8,5120]{1,0:T(8,128)(2,1)S(1)}, u32[]{:S(2)}, u32[]{:S(2)}) collective-permute-start(bf16[8,5120]{1,0:T(8,128)(2,1)S(1)} %broadcast_select_fusion.refs_0_), channel_id=1, source_target_pairs={{0,12},{1,13},{2,14},{3,15},{4,8},{5,9},{6,10},{7,11},{8,4},{9,5},... | collective-permute-start | bytes 245768 | tf_op jit(solution)/shard_map/ppermute | solution.py:50
  7.7 0.4 collective-permute-start.1
  8.1 2.2 %collective-permute-done.3.refs_3_ = bf16[8,5120]{1,0:T(8,128)(2,1)S(1)} collective-permute-done((bf16[8,5120]{1,0:T(8,128)(2,1)S(1)}, bf16[8,5120]{1,0:T(8,128)(2,1)S(1)}, u32[]{:S(2)}, u32[]{:S(2)}) %collective-permute-start.3) | collective-permute-done | bytes 81952 | tf_op jit(solution)/shard_map/ppermute | solution.py:50
  10.3 4.1 %collective-permute-done.2.refs_2_ = bf16[8,5120]{1,0:T(8,128)(2,1)S(1)} collective-permute-done((bf16[8,5120]{1,0:T(8,128)(2,1)S(1)}, bf16[8,5120]{1,0:T(8,128)(2,1)S(1)}, u32[]{:S(2)}, u32[]{:S(2)}) %collective-permute-start.2) | collective-permute-done | bytes 81952 | tf_op jit(solution)/shard_map/ppermute | solution.py:50
  14.4 1.3 %collective-permute-start.7 = (bf16[32,5120]{1,0:T(8,128)(2,1)S(1)}, bf16[32,5120]{1,0:T(8,128)(2,1)S(1)}, u32[]{:S(2)}, u32[]{:S(2)}) collective-permute-start(bf16[32,5120]{1,0:T(8,128)(2,1)S(1)} %join.2.refs_4_), channel_id=1, source_target_pairs={{0,2},{1,3},{2,0},{3,1},{4,6},{5,7},{6,4},{7,5},{8,10},{9,11},{10,... | collective-permute-start | bytes 983048 | tf_op jit(solution)/shard_map/ppermute | solution.py:50
  15.7 1.2 %collective-permute-start.6 = (bf16[32,5120]{1,0:T(8,128)(2,1)S(1)}, bf16[32,5120]{1,0:T(8,128)(2,1)S(1)}, u32[]{:S(2)}, u32[]{:S(2)}) collective-permute-start(bf16[32,5120]{1,0:T(8,128)(2,1)S(1)} %join.2.refs_4_), channel_id=1, source_target_pairs={{0,1},{1,0},{2,3},{3,2},{4,5},{5,4},{6,7},{7,6},{8,9},{9,8},{10,11... | collective-permute-start | bytes 983048 | tf_op jit(solution)/shard_map/ppermute | solution.py:50
  16.9 0.9 queries.1
  17.8 1.8 %collective-permute-start.4 = (bf16[128,1280]{1,0:T(8,128)(2,1)S(1)}, bf16[128,1280]{1,0:T(8,128)(2,1)S(1)}, u32[]{:S(2)}, u32[]{:S(2)}) collective-permute-start(bf16[128,1280]{1,0:T(8,128)(2,1)S(1)} %get-tuple-element.41), channel_id=1, source_target_pairs={{0,16},{16,0},{1,17},{17,1},{2,18},{18,2},{3,19},{19,3},{4,20},{20... | collective-permute-start | bytes 983048 | tf_op jit(solution)/shard_map/ppermute | solution.py:22
  19.6 0.1 collective-permute-start.5
  19.7 0.1 cut.1
  19.8 0.5 collective-permute-start.10
  20.3 2.2 %collective-permute-done.7.refs_6_ = bf16[32,5120]{1,0:T(8,128)(2,1)S(1)} collective-permute-done((bf16[32,5120]{1,0:T(8,128)(2,1)S(1)}, bf16[32,5120]{1,0:T(8,128)(2,1)S(1)}, u32[]{:S(2)}, u32[]{:S(2)}) %collective-permute-start.7) | collective-permute-done | bytes 327712 | tf_op jit(solution)/shard_map/ppermute | solution.py:50
  22.5 2.1 %collective-permute-start.11 = (bf16[128,1280]{1,0:T(8,128)(2,1)S(1)}, bf16[128,1280]{1,0:T(8,128)(2,1)S(1)}, u32[]{:S(2)}, u32[]{:S(2)}) collective-permute-start(bf16[128,1280]{1,0:T(8,128)(2,1)S(1)} %get-tuple-element.46), channel_id=1, source_target_pairs={{0,16},{16,0},{1,17},{17,1},{2,18},{18,2},{3,19},{19,3},{4,20},{20... | collective-permute-start | bytes 983048 | tf_op jit(solution)/shard_map/ppermute | solution.py:22
  24.6 1.3 %collective-permute-start.8 = (bf16[16,5120]{1,0:T(8,128)(2,1)S(1)}, bf16[16,5120]{1,0:T(8,128)(2,1)S(1)}, u32[]{:S(2)}, u32[]{:S(2)}) collective-permute-start(bf16[16,5120]{1,0:T(8,128)(2,1)S(1)} %slice.16), channel_id=1, source_target_pairs={{0,1},{1,0},{2,3},{3,2},{4,5},{5,4},{6,7},{7,6},{8,9},{9,8},{10,11... | collective-permute-start | bytes 491528 | tf_op jit(solution)/shard_map/ppermute | solution.py:50
  25.9 1.3 %collective-permute-start.9 = (bf16[16,5120]{1,0:T(8,128)(2,1)S(1)}, bf16[16,5120]{1,0:T(8,128)(2,1)S(1)}, u32[]{:S(2)}, u32[]{:S(2)}) collective-permute-start(bf16[16,5120]{1,0:T(8,128)(2,1)S(1)} %slice.17), channel_id=1, source_target_pairs={{0,2},{1,3},{2,0},{3,1},{4,6},{5,7},{6,4},{7,5},{8,10},{9,11},{10,... | collective-permute-start | bytes 491528 | tf_op jit(solution)/shard_map/ppermute | solution.py:50
  27.2 1.3 %collective-permute-start.24 = (bf16[128,5120]{1,0:T(8,128)(2,1)S(1)}, bf16[128,5120]{1,0:T(8,128)(2,1)S(1)}, u32[]{:S(2)}, u32[]{:S(2)}) collective-permute-start(bf16[128,5120]{1,0:T(8,128)(2,1)S(1)} %get-tuple-element.40.refs_1_), channel_id=1, source_target_pairs={{0,16},{1,17},{2,18},{3,19},{4,20},{5,21},{6,22},{7,23},{8,24},{9,... | collective-permute-start | bytes 3932168 | tf_op jit(solution)/shard_map/ppermute | solution.py:17
  28.5 0.7 collective-permute-done.8.refs_7_
  29.2 1.2 %collective-permute-done.9.refs_8_ = bf16[16,5120]{1,0:T(8,128)(2,1)S(1)} collective-permute-done((bf16[16,5120]{1,0:T(8,128)(2,1)S(1)}, bf16[16,5120]{1,0:T(8,128)(2,1)S(1)}, u32[]{:S(2)}, u32[]{:S(2)}) %collective-permute-start.9) | collective-permute-done | bytes 163872 | tf_op jit(solution)/shard_map/ppermute | solution.py:50
  30.4 1.0 %attend.1 = (bf16[128,2560]{1,0:T(8,128)(2,1)S(1)}, f32[20,128,128]{2,1,0:T(8,128)S(1)}, bf16[128,2560]{1,0:T(8,128)(2,1)S(1)}) custom-call(s32[1]{0:T(128)} %bitcast.refs_0_.section, bf16[128,1280]{1,0:T(8,128)(2,1)S(1)} %collective-permute-done.4.refs_1_, bf16[128,1280]{1,0:T(8,128)(2,1)S(1)} %collective-permute-done.5.refs_2_, ...), custom_call_target="tpu_custom_call" | custom-call | flops 167772160 | bytes 5242884 | tf_op jit(solution)/shard_map/attend/pallas_call | solution.py:142
  31.5 1.3 %collective-permute-start.12 = (bf16[128,2560]{1,0:T(8,128)(2,1)S(1)}, bf16[128,2560]{1,0:T(8,128)(2,1)S(1)}, u32[]{:S(2)}, u32[]{:S(2)}) collective-permute-start(bf16[128,2560]{1,0:T(8,128)(2,1)S(1)} %get-tuple-element.47.refs_3_), channel_id=1, source_target_pairs={{0,16},{1,17},{2,18},{3,19},{4,20},{5,21},{6,22},{7,23},{8,24},{9,... | collective-permute-start | bytes 1966088 | tf_op jit(solution)/shard_map/ppermute | solution.py:27
  32.8 1.3 %gradient.1 = (f32[32,5120]{1,0:T(8,128)S(1)}, f32[32,5120]{1,0:T(8,128)S(1)}, f32[32,5120]{1,0:T(8,128)S(1)}, bf16[16,5120]{1,0:T(8,128)(2,1)S(1)}, bf16[16,5120]{1,0:T(8,128)(2,1)S(1)}) custom-call(s32[1]{0:T(128)} %bitcast.refs_0_.section, bf16[128,2560]{1,0:T(8,128)(2,1)S(1)} %get-tuple-element.48.q_ref, ...), custom_call_target="tpu_custom_call" | custom-call | flops 419430400 | bytes 6881284 | tf_op jit(solution)/shard_map/gradient/pallas_call | solution.py:142
  34.1 2.2 %collective-permute-start.17 = (bf16[16,5120]{1,0:T(8,128)(2,1)S(1)}, bf16[16,5120]{1,0:T(8,128)(2,1)S(1)}, u32[]{:S(2)}, u32[]{:S(2)}) collective-permute-start(bf16[16,5120]{1,0:T(8,128)(2,1)S(1)} %get-tuple-element.57), channel_id=1, source_target_pairs={{2,0},{3,1},{0,2},{1,3},{6,4},{7,5},{4,6},{5,7},{10,8},{11,9},{8,1... | collective-permute-start | bytes 491528 | tf_op jit(solution)/shard_map/ppermute | solution.py:50
  36.3 0.3 collective-permute-start.16
  36.6 0.6 settle.1
  37.3 2.4 %collective-permute-start.15 = (bf16[8,5120]{1,0:T(8,128)(2,1)S(1)}, bf16[8,5120]{1,0:T(8,128)(2,1)S(1)}, u32[]{:S(2)}, u32[]{:S(2)}) collective-permute-start(bf16[8,5120]{1,0:T(8,128)(2,1)S(1)} %get-tuple-element.53.refs_0_.after_any), channel_id=1, source_target_pairs={{0,12},{1,13},{2,14},{3,15},{4,8},{5,9},{6,10},{7,11},{8,4},{9,5},... | collective-permute-start | bytes 245768 | tf_op jit(solution)/shard_map/ppermute | solution.py:50
  39.7 1.2 %collective-permute-start.13 = (bf16[8,5120]{1,0:T(8,128)(2,1)S(1)}, bf16[8,5120]{1,0:T(8,128)(2,1)S(1)}, u32[]{:S(2)}, u32[]{:S(2)}) collective-permute-start(bf16[8,5120]{1,0:T(8,128)(2,1)S(1)} %get-tuple-element.53.refs_0_.after_any), channel_id=1, source_target_pairs={{0,4},{1,5},{2,6},{3,7},{4,0},{5,1},{6,2},{7,3},{8,12},{9,13},{10,... | collective-permute-start | bytes 245768 | tf_op jit(solution)/shard_map/ppermute | solution.py:50
  41.0 1.2 %collective-permute-start.21 = (bf16[32,5120]{1,0:T(8,128)(2,1)S(1)}, bf16[32,5120]{1,0:T(8,128)(2,1)S(1)}, u32[]{:S(2)}, u32[]{:S(2)}) collective-permute-start(bf16[32,5120]{1,0:T(8,128)(2,1)S(1)} %add_half.5.refs_5_), channel_id=1, source_target_pairs={{1,0},{0,1},{3,2},{2,3},{5,4},{4,5},{7,6},{6,7},{9,8},{8,9},{11,10... | collective-permute-start | bytes 983048 | tf_op jit(solution)/shard_map/ppermute | solution.py:50
  42.2 0.2 collective-permute-done.15.refs_3_
  42.5 1.2 %collective-permute-start.20 = (bf16[32,5120]{1,0:T(8,128)(2,1)S(1)}, bf16[32,5120]{1,0:T(8,128)(2,1)S(1)}, u32[]{:S(2)}, u32[]{:S(2)}) collective-permute-start(bf16[32,5120]{1,0:T(8,128)(2,1)S(1)} %add_half.4.refs_4_), channel_id=1, source_target_pairs={{2,0},{3,1},{0,2},{1,3},{6,4},{7,5},{4,6},{5,7},{10,8},{11,9},{8,1... | collective-permute-start | bytes 983048 | tf_op jit(solution)/shard_map/ppermute | solution.py:50
  43.7 3.5 %collective-permute-done.14.refs_2_ = bf16[8,5120]{1,0:T(8,128)(2,1)S(1)} collective-permute-done((bf16[8,5120]{1,0:T(8,128)(2,1)S(1)}, bf16[8,5120]{1,0:T(8,128)(2,1)S(1)}, u32[]{:S(2)}, u32[]{:S(2)}) %collective-permute-start.14) | collective-permute-done | bytes 81952 | tf_op jit(solution)/shard_map/ppermute | solution.py:50
  47.2 1.2 %collective-permute-start.19 = (bf16[32,5120]{1,0:T(8,128)(2,1)S(1)}, bf16[32,5120]{1,0:T(8,128)(2,1)S(1)}, u32[]{:S(2)}, u32[]{:S(2)}) collective-permute-start(bf16[32,5120]{1,0:T(8,128)(2,1)S(1)} %join.3.refs_3_.refs_2_), channel_id=1, source_target_pairs={{0,2},{1,3},{2,0},{3,1},{4,6},{5,7},{6,4},{7,5},{8,10},{9,11},{10,... | collective-permute-start | bytes 983048 | tf_op jit(solution)/shard_map/ppermute | solution.py:50
  48.4 0.2 collective-permute-start.18
  48.6 0.1 collective-permute-done.20.refs_1_
  48.7 0.1 add_blocks.2
  48.8 8.2 %collective-permute-done.19.refs_0_.refs_4_ = bf16[32,5120]{1,0:T(8,128)(2,1)S(1)} collective-permute-done((bf16[32,5120]{1,0:T(8,128)(2,1)S(1)}, bf16[32,5120]{1,0:T(8,128)(2,1)S(1)}, u32[]{:S(2)}, u32[]{:S(2)}) %collective-permute-start.19) | collective-permute-done | bytes 327712 | tf_op jit(solution)/shard_map/ppermute | solution.py:50
  57.0 1.2 %collective-permute-start.22 = (bf16[16,5120]{1,0:T(8,128)(2,1)S(1)}, bf16[16,5120]{1,0:T(8,128)(2,1)S(1)}, u32[]{:S(2)}, u32[]{:S(2)}) collective-permute-start(bf16[16,5120]{1,0:T(8,128)(2,1)S(1)} %get-tuple-element.59), channel_id=1, source_target_pairs={{0,1},{1,0},{2,3},{3,2},{4,5},{5,4},{6,7},{7,6},{8,9},{9,8},{10,11... | collective-permute-start | bytes 491528 | tf_op jit(solution)/shard_map/ppermute | solution.py:50
  58.2 0.2 collective-permute-start.23
  58.4 2.5 %collective-permute-start.26 = (bf16[8,5120]{1,0:T(8,128)(2,1)S(1)}, bf16[8,5120]{1,0:T(8,128)(2,1)S(1)}, u32[]{:S(2)}, u32[]{:S(2)}) collective-permute-start(bf16[8,5120]{1,0:T(8,128)(2,1)S(1)} %get-tuple-element.62), channel_id=1, source_target_pairs={{8,0},{9,1},{10,2},{11,3},{12,4},{13,5},{14,6},{15,7},{0,8},{1,9},... | collective-permute-start | bytes 245768 | tf_op jit(solution)/shard_map/ppermute | solution.py:50
  60.9 0.8 collective-permute-done.25.refs_8_.refs_1_
  61.7 1.0 %collective-permute-done.26.refs_9_.refs_2_ = bf16[8,5120]{1,0:T(8,128)(2,1)S(1)} collective-permute-done((bf16[8,5120]{1,0:T(8,128)(2,1)S(1)}, bf16[8,5120]{1,0:T(8,128)(2,1)S(1)}, u32[]{:S(2)}, u32[]{:S(2)}) %collective-permute-start.26) | collective-permute-done | bytes 81952 | tf_op jit(solution)/shard_map/ppermute | solution.py:50
  62.7 2.3 %expert.1 = (f32[32,5120]{1,0:T(8,128)S(1)}, f32[32,5120]{1,0:T(8,128)S(1)}, f32[32,5120]{1,0:T(8,128)S(1)}, bf16[16,5120]{1,0:T(8,128)(2,1)S(1)}, bf16[16,5120]{1,0:T(8,128)(2,1)S(1)}) custom-call(bf16[5120,640]{1,0:T(8,128)(2,1)S(1)} %bitcast.18, bf16[640,5120]{1,0:T(8,128)(2,1)S(1)} %bitcast.19, bf16[32,5120]{1,0:T(8,128)(2,1)S(1)} %join.3.refs_3_.refs_2_, ...), custom_call_target="tpu_custom_call" | custom-call | flops 1677721600 | bytes 16711680 | tf_op jit(solution)/shard_map/expert/pallas_call | solution.py:142
  65.1 1.4 %collective-permute-start.30 = (bf16[16,5120]{1,0:T(8,128)(2,1)S(1)}, bf16[16,5120]{1,0:T(8,128)(2,1)S(1)}, u32[]{:S(2)}, u32[]{:S(2)}) collective-permute-start(bf16[16,5120]{1,0:T(8,128)(2,1)S(1)} %get-tuple-element.68), channel_id=1, source_target_pairs={{2,0},{3,1},{0,2},{1,3},{6,4},{7,5},{4,6},{5,7},{10,8},{11,9},{8,1... | collective-permute-start | bytes 491528 | tf_op jit(solution)/shard_map/ppermute | solution.py:50
  66.4 0.2 collective-permute-start.27
  66.6 2.0 %collective-permute-start.28 = (bf16[8,5120]{1,0:T(8,128)(2,1)S(1)}, bf16[8,5120]{1,0:T(8,128)(2,1)S(1)}, u32[]{:S(2)}, u32[]{:S(2)}) collective-permute-start(bf16[8,5120]{1,0:T(8,128)(2,1)S(1)} %get-tuple-element.66), channel_id=1, source_target_pairs={{12,0},{13,1},{14,2},{15,3},{8,4},{9,5},{10,6},{11,7},{4,8},{5,9},... | collective-permute-start | bytes 245768 | tf_op jit(solution)/shard_map/ppermute | solution.py:50
  68.7 3.1 %collective-permute-done.28.refs_3_ = bf16[8,5120]{1,0:T(8,128)(2,1)S(1)} collective-permute-done((bf16[8,5120]{1,0:T(8,128)(2,1)S(1)}, bf16[8,5120]{1,0:T(8,128)(2,1)S(1)}, u32[]{:S(2)}, u32[]{:S(2)}) %collective-permute-start.28) | collective-permute-done | bytes 81952 | tf_op jit(solution)/shard_map/ppermute | solution.py:50
  71.9 1.3 %collective-permute-start.31 = (bf16[32,5120]{1,0:T(8,128)(2,1)S(1)}, bf16[32,5120]{1,0:T(8,128)(2,1)S(1)}, u32[]{:S(2)}, u32[]{:S(2)}) collective-permute-start(bf16[32,5120]{1,0:T(8,128)(2,1)S(1)} %add_half.7), channel_id=1, source_target_pairs={{1,0},{0,1},{3,2},{2,3},{5,4},{4,5},{7,6},{6,7},{9,8},{8,9},{11,10... | collective-permute-start | bytes 983048 | tf_op jit(solution)/shard_map/ppermute | solution.py:50
  73.3 0.2 collective-permute-start.29
  73.6 1.3 %collective-permute-start.35 = (f32[8,5120]{1,0:T(8,128)S(1)}, f32[8,5120]{1,0:T(8,128)S(1)}, u32[]{:S(2)}, u32[]{:S(2)}) collective-permute-start(f32[8,5120]{1,0:T(8,128)S(1)} %add_last.2.refs_2_.second_ref), channel_id=1, source_target_pairs={{0,16},{1,17},{2,18},{3,19},{4,20},{5,21},{6,22},{7,23},{8,24},{9,... | collective-permute-start | bytes 491528 | tf_op jit(solution)/shard_map/ppermute | solution.py:27
  74.9 4.7 %collective-permute-done.31.refs_2_ = bf16[32,5120]{1,0:T(8,128)(2,1)S(1)} collective-permute-done((bf16[32,5120]{1,0:T(8,128)(2,1)S(1)}, bf16[32,5120]{1,0:T(8,128)(2,1)S(1)}, u32[]{:S(2)}, u32[]{:S(2)}) %collective-permute-start.31) | collective-permute-done | bytes 327712 | tf_op jit(solution)/shard_map/ppermute | solution.py:50
  79.6 0.1 add_blocks.3
  79.8 0.6 collective-permute-start.32
  80.3 1.7 %collective-permute-start.33 = (bf16[8,5120]{1,0:T(8,128)(2,1)S(1)}, bf16[8,5120]{1,0:T(8,128)(2,1)S(1)}, u32[]{:S(2)}, u32[]{:S(2)}) collective-permute-start(bf16[8,5120]{1,0:T(8,128)(2,1)S(1)} %get-tuple-element.72), channel_id=1, source_target_pairs={{8,0},{9,1},{10,2},{11,3},{12,4},{13,5},{14,6},{15,7},{0,8},{1,9},... | collective-permute-start | bytes 245768 | tf_op jit(solution)/shard_map/ppermute | solution.py:50
  82.0 1.3 %collective-permute-start.34 = (bf16[8,5120]{1,0:T(8,128)(2,1)S(1)}, bf16[8,5120]{1,0:T(8,128)(2,1)S(1)}, u32[]{:S(2)}, u32[]{:S(2)}) collective-permute-start(bf16[8,5120]{1,0:T(8,128)(2,1)S(1)} %get-tuple-element.73), channel_id=1, source_target_pairs={{12,0},{13,1},{14,2},{15,3},{8,4},{9,5},{10,6},{11,7},{4,8},{5,9},... | collective-permute-start | bytes 245768 | tf_op jit(solution)/shard_map/ppermute | solution.py:50
  83.4 0.6 collective-permute-done.35.first_ref
  84.0 0.8 lay_out.1
  84.8 0.6 collective-permute-done.33.refs_2_
  85.4 1.8 %collective-permute-done.34.refs_3_ = bf16[8,5120]{1,0:T(8,128)(2,1)S(1)} collective-permute-done((bf16[8,5120]{1,0:T(8,128)(2,1)S(1)}, bf16[8,5120]{1,0:T(8,128)(2,1)S(1)}, u32[]{:S(2)}, u32[]{:S(2)}) %collective-permute-start.34) | collective-permute-done | bytes 81952 | tf_op jit(solution)/shard_map/ppermute | solution.py:50
  87.2 1.3 %collective-permute-start.36 = (f32[8,5248]{1,0:T(8,128)S(1)}, f32[8,5248]{1,0:T(8,128)S(1)}, u32[]{:S(2)}, u32[]{:S(2)}) collective-permute-start(f32[8,5248]{1,0:T(8,128)S(1)} %add_last.3.back_ref), channel_id=1, source_target_pairs={{0,16},{1,17},{2,18},{3,19},{4,20},{5,21},{6,22},{7,23},{8,24},{9,... | collective-permute-start | bytes 503816 | tf_op jit(solution)/shard_map/ppermute | solution.py:17
  88.5 1.5 %finish.2 = bf16[128,5120]{1,0:T(8,128)(2,1)} custom-call(s32[1]{0:T(128)} %bitcast.refs_0_.section, bf16[128,5120]{1,0:T(8,128)(2,1)S(1)} %get-tuple-element.52.res_ref, f32[8,5248]{1,0:T(8,128)S(1)} %add_last.3.back_ref), custom_call_target="tpu_custom_call" | custom-call | flops 32768000 | bytes 3276800 | tf_op jit(solution)/shard_map/finish/pallas_call | solution.py:541
  90.0 8.6 %collective-permute-done.36.back_ref = f32[8,5248]{1,0:T(8,128)S(1)} collective-permute-done((f32[8,5248]{1,0:T(8,128)S(1)}, f32[8,5248]{1,0:T(8,128)S(1)}, u32[]{:S(2)}, u32[]{:S(2)}) %collective-permute-start.36) | collective-permute-done | bytes 167968 | tf_op jit(solution)/shard_map/ppermute | solution.py:17
  98.6 1.5 %finish.3 = bf16[128,5120]{1,0:T(8,128)(2,1)} custom-call(s32[1]{0:T(128)} %bitcast.refs_0_.section, bf16[128,5120]{1,0:T(8,128)(2,1)S(1)} %collective-permute-done.24.refs_7_.res_ref, f32[8,5248]{1,0:T(8,128)S(1)} %collective-permute-done.36.back_ref, bf16[128,5120]{1,0:T(8,128)(2,1)} %get-tuple-element.75.refs_0_), custom_call_target="tpu_custom_call", output_to_operand_aliasing={{}: (3, {})} | custom-call | flops 32768000 | bytes 3276800 | tf_op jit(solution)/shard_map/finish/pallas_call | solution.py:541
  (56 shorter events, 0.6 us)
Async XLA Ops:
  0.6 16.3 %copy-start.5 = (f32[1,128]{1,0:T(1,128)S(1)}, f32[1,128]{1,0:T(1,128)}, u32[]{:S(2)}) copy-start(f32[1,128]{1,0:T(1,128)} %refs_2_.1) | copy-start | bytes 1540
  0.6 16.3 %copy-start.6 = (s32[1,128]{1,0:T(1,128)S(1)}, s32[1,128]{1,0:T(1,128)}, u32[]{:S(2)}) copy-start(s32[1,128]{1,0:T(1,128)} %refs_3_.1) | copy-start | bytes 1540
  0.7 16.3 %copy-start.4 = (f32[1,5120]{1,0:T(1,128)S(1)}, f32[1,5120]{1,0:T(1,128)}, u32[]{:S(2)}) copy-start(f32[1,5120]{1,0:T(1,128)} %refs_1_.1) | copy-start | bytes 61444
  0.7 16.3 %copy-start.1 = (bf16[1,128,5120]{2,1,0:T(8,128)(2,1)S(1)}, bf16[1,128,5120]{2,1,0:T(8,128)(2,1)}, u32[]{:S(2)}) copy-start(bf16[1,128,5120]{2,1,0:T(8,128)(2,1)} %param.9) | copy-start | bytes 3932164
  1.8 1.3 %collective-permute-start = (bf16[8,5120]{1,0:T(8,128)(2,1)S(1)}, bf16[8,5120]{1,0:T(8,128)(2,1)S(1)}, u32[]{:S(2)}, u32[]{:S(2)}) collective-permute-start(bf16[8,5120]{1,0:T(8,128)(2,1)S(1)} %bitcast.25), channel_id=1, source_target_pairs={{0,16},{16,0},{1,17},{17,1},{2,18},{18,2},{3,19},{19,3},{4,20},{20... | collective-permute-start | bytes 245768 | tf_op jit(solution)/shard_map/ppermute | solution.py:22
  2.0 17.7 %copy-start.2 = (bf16[1,128,5120]{2,1,0:T(8,128)(2,1)S(1)}, bf16[1,128,5120]{2,1,0:T(8,128)(2,1)}, u32[]{:S(2)}) copy-start(bf16[1,128,5120]{2,1,0:T(8,128)(2,1)} %param.11) | copy-start | bytes 3932164
  3.2 7.1 %collective-permute-start.3 = (bf16[8,5120]{1,0:T(8,128)(2,1)S(1)}, bf16[8,5120]{1,0:T(8,128)(2,1)S(1)}, u32[]{:S(2)}, u32[]{:S(2)}) collective-permute-start(bf16[8,5120]{1,0:T(8,128)(2,1)S(1)} %broadcast_select_fusion.refs_0_), channel_id=1, source_target_pairs={{0,12},{1,13},{2,14},{3,15},{4,8},{5,9},{6,10},{7,11},{8,4},{9,5},... | collective-permute-start | bytes 245768 | tf_op jit(solution)/shard_map/ppermute | solution.py:50
  7.7 6.6 %collective-permute-start.2 = (bf16[8,5120]{1,0:T(8,128)(2,1)S(1)}, bf16[8,5120]{1,0:T(8,128)(2,1)S(1)}, u32[]{:S(2)}, u32[]{:S(2)}) collective-permute-start(bf16[8,5120]{1,0:T(8,128)(2,1)S(1)} %broadcast_select_fusion.refs_0_), channel_id=1, source_target_pairs={{0,8},{1,9},{2,10},{3,11},{4,12},{5,13},{6,14},{7,15},{8,0},{9,1},... | collective-permute-start | bytes 245768 | tf_op jit(solution)/shard_map/ppermute | solution.py:50
  7.7 6.6 %collective-permute-start.1 = (bf16[8,5120]{1,0:T(8,128)(2,1)S(1)}, bf16[8,5120]{1,0:T(8,128)(2,1)S(1)}, u32[]{:S(2)}, u32[]{:S(2)}) collective-permute-start(bf16[8,5120]{1,0:T(8,128)(2,1)S(1)} %broadcast_select_fusion.refs_0_), channel_id=1, source_target_pairs={{0,4},{1,5},{2,6},{3,7},{4,0},{5,1},{6,2},{7,3},{8,12},{9,13},{10,... | collective-permute-start | bytes 245768 | tf_op jit(solution)/shard_map/ppermute | solution.py:50
  14.4 8.1 %collective-permute-start.7 = (bf16[32,5120]{1,0:T(8,128)(2,1)S(1)}, bf16[32,5120]{1,0:T(8,128)(2,1)S(1)}, u32[]{:S(2)}, u32[]{:S(2)}) collective-permute-start(bf16[32,5120]{1,0:T(8,128)(2,1)S(1)} %join.2.refs_4_), channel_id=1, source_target_pairs={{0,2},{1,3},{2,0},{3,1},{4,6},{5,7},{6,4},{7,5},{8,10},{9,11},{10,... | collective-permute-start | bytes 983048 | tf_op jit(solution)/shard_map/ppermute | solution.py:50
  15.7 8.9 %collective-permute-start.6 = (bf16[32,5120]{1,0:T(8,128)(2,1)S(1)}, bf16[32,5120]{1,0:T(8,128)(2,1)S(1)}, u32[]{:S(2)}, u32[]{:S(2)}) collective-permute-start(bf16[32,5120]{1,0:T(8,128)(2,1)S(1)} %join.2.refs_4_), channel_id=1, source_target_pairs={{0,1},{1,0},{2,3},{3,2},{4,5},{5,4},{6,7},{7,6},{8,9},{9,8},{10,11... | collective-permute-start | bytes 983048 | tf_op jit(solution)/shard_map/ppermute | solution.py:50
  17.8 8.1 %collective-permute-start.4 = (bf16[128,1280]{1,0:T(8,128)(2,1)S(1)}, bf16[128,1280]{1,0:T(8,128)(2,1)S(1)}, u32[]{:S(2)}, u32[]{:S(2)}) collective-permute-start(bf16[128,1280]{1,0:T(8,128)(2,1)S(1)} %get-tuple-element.41), channel_id=1, source_target_pairs={{0,16},{16,0},{1,17},{17,1},{2,18},{18,2},{3,19},{19,3},{4,20},{20... | collective-permute-start | bytes 983048 | tf_op jit(solution)/shard_map/ppermute | solution.py:22
  19.6 7.6 %collective-permute-start.5 = (bf16[128,1280]{1,0:T(8,128)(2,1)S(1)}, bf16[128,1280]{1,0:T(8,128)(2,1)S(1)}, u32[]{:S(2)}, u32[]{:S(2)}) collective-permute-start(bf16[128,1280]{1,0:T(8,128)(2,1)S(1)} %get-tuple-element.42), channel_id=1, source_target_pairs={{0,16},{16,0},{1,17},{17,1},{2,18},{18,2},{3,19},{19,3},{4,20},{20... | collective-permute-start | bytes 983048 | tf_op jit(solution)/shard_map/ppermute | solution.py:22
  19.8 8.7 %collective-permute-start.10 = (bf16[128,1280]{1,0:T(8,128)(2,1)S(1)}, bf16[128,1280]{1,0:T(8,128)(2,1)S(1)}, u32[]{:S(2)}, u32[]{:S(2)}) collective-permute-start(bf16[128,1280]{1,0:T(8,128)(2,1)S(1)} %get-tuple-element.45), channel_id=1, source_target_pairs={{0,16},{16,0},{1,17},{17,1},{2,18},{18,2},{3,19},{19,3},{4,20},{20... | collective-permute-start | bytes 983048 | tf_op jit(solution)/shard_map/ppermute | solution.py:22
  22.5 6.0 %collective-permute-start.11 = (bf16[128,1280]{1,0:T(8,128)(2,1)S(1)}, bf16[128,1280]{1,0:T(8,128)(2,1)S(1)}, u32[]{:S(2)}, u32[]{:S(2)}) collective-permute-start(bf16[128,1280]{1,0:T(8,128)(2,1)S(1)} %get-tuple-element.46), channel_id=1, source_target_pairs={{0,16},{16,0},{1,17},{17,1},{2,18},{18,2},{3,19},{19,3},{4,20},{20... | collective-permute-start | bytes 983048 | tf_op jit(solution)/shard_map/ppermute | solution.py:22
  24.6 4.6 %collective-permute-start.8 = (bf16[16,5120]{1,0:T(8,128)(2,1)S(1)}, bf16[16,5120]{1,0:T(8,128)(2,1)S(1)}, u32[]{:S(2)}, u32[]{:S(2)}) collective-permute-start(bf16[16,5120]{1,0:T(8,128)(2,1)S(1)} %slice.16), channel_id=1, source_target_pairs={{0,1},{1,0},{2,3},{3,2},{4,5},{5,4},{6,7},{7,6},{8,9},{9,8},{10,11... | collective-permute-start | bytes 491528 | tf_op jit(solution)/shard_map/ppermute | solution.py:50
  25.9 4.5 %collective-permute-start.9 = (bf16[16,5120]{1,0:T(8,128)(2,1)S(1)}, bf16[16,5120]{1,0:T(8,128)(2,1)S(1)}, u32[]{:S(2)}, u32[]{:S(2)}) collective-permute-start(bf16[16,5120]{1,0:T(8,128)(2,1)S(1)} %slice.17), channel_id=1, source_target_pairs={{0,2},{1,3},{2,0},{3,1},{4,6},{5,7},{6,4},{7,5},{8,10},{9,11},{10,... | collective-permute-start | bytes 491528 | tf_op jit(solution)/shard_map/ppermute | solution.py:50
  27.2 33.7 %collective-permute-start.24 = (bf16[128,5120]{1,0:T(8,128)(2,1)S(1)}, bf16[128,5120]{1,0:T(8,128)(2,1)S(1)}, u32[]{:S(2)}, u32[]{:S(2)}) collective-permute-start(bf16[128,5120]{1,0:T(8,128)(2,1)S(1)} %get-tuple-element.40.refs_1_), channel_id=1, source_target_pairs={{0,16},{1,17},{2,18},{3,19},{4,20},{5,21},{6,22},{7,23},{8,24},{9,... | collective-permute-start | bytes 3932168 | tf_op jit(solution)/shard_map/ppermute | solution.py:17
  31.5 5.1 %collective-permute-start.12 = (bf16[128,2560]{1,0:T(8,128)(2,1)S(1)}, bf16[128,2560]{1,0:T(8,128)(2,1)S(1)}, u32[]{:S(2)}, u32[]{:S(2)}) collective-permute-start(bf16[128,2560]{1,0:T(8,128)(2,1)S(1)} %get-tuple-element.47.refs_3_), channel_id=1, source_target_pairs={{0,16},{1,17},{2,18},{3,19},{4,20},{5,21},{6,22},{7,23},{8,24},{9,... | collective-permute-start | bytes 1966088 | tf_op jit(solution)/shard_map/ppermute | solution.py:27
  32.8 3.9 %copy-start.3 = (f32[1,5120]{1,0:T(1,128)S(1)}, f32[1,5120]{1,0:T(1,128)}, u32[]{:S(2)}) copy-start(f32[1,5120]{1,0:T(1,128)} %refs_4_.1) | copy-start | bytes 61444
  32.8 29.9 %slice-start = ((s8[6553600]{0:T(1024)(128)(4,1)}), s8[4194304]{0:T(1024)(128)(4,1)S(1)}, s32[]{:S(2)}) async-start(s8[6553600]{0:T(1024)(128)(4,1)} %bitcast.16), calls=%async_computation | async-start | bytes 8388608
  34.1 5.5 %collective-permute-start.17 = (bf16[16,5120]{1,0:T(8,128)(2,1)S(1)}, bf16[16,5120]{1,0:T(8,128)(2,1)S(1)}, u32[]{:S(2)}, u32[]{:S(2)}) collective-permute-start(bf16[16,5120]{1,0:T(8,128)(2,1)S(1)} %get-tuple-element.57), channel_id=1, source_target_pairs={{2,0},{3,1},{0,2},{1,3},{6,4},{7,5},{4,6},{5,7},{10,8},{11,9},{8,1... | collective-permute-start | bytes 491528 | tf_op jit(solution)/shard_map/ppermute | solution.py:50
  36.3 4.6 %collective-permute-start.16 = (bf16[16,5120]{1,0:T(8,128)(2,1)S(1)}, bf16[16,5120]{1,0:T(8,128)(2,1)S(1)}, u32[]{:S(2)}, u32[]{:S(2)}) collective-permute-start(bf16[16,5120]{1,0:T(8,128)(2,1)S(1)} %get-tuple-element.55), channel_id=1, source_target_pairs={{1,0},{0,1},{3,2},{2,3},{5,4},{4,5},{7,6},{6,7},{9,8},{8,9},{11,10... | collective-permute-start | bytes 491528 | tf_op jit(solution)/shard_map/ppermute | solution.py:50
  36.6 26.1 %slice-start.1 = ((s8[6553600]{0:T(1024)(128)(4,1)}), s8[2359296]{0:T(1024)(128)(4,1)S(1)}, s32[]{:S(2)}) async-start(s8[6553600]{0:T(1024)(128)(4,1)} %bitcast.16), calls=%async_computation.1 | async-start | bytes 4718592
  36.6 26.1 %copy-start = (bf16[1,640,5120]{2,1,0:T(8,128)(2,1)S(1)}, bf16[1,640,5120]{2,1,0:T(8,128)(2,1)}, u32[]{:S(2)}) copy-start(bf16[1,640,5120]{2,1,0:T(8,128)(2,1)} %param.15) | copy-start | bytes 19660804
  37.3 5.2 %collective-permute-start.15 = (bf16[8,5120]{1,0:T(8,128)(2,1)S(1)}, bf16[8,5120]{1,0:T(8,128)(2,1)S(1)}, u32[]{:S(2)}, u32[]{:S(2)}) collective-permute-start(bf16[8,5120]{1,0:T(8,128)(2,1)S(1)} %get-tuple-element.53.refs_0_.after_any), channel_id=1, source_target_pairs={{0,12},{1,13},{2,14},{3,15},{4,8},{5,9},{6,10},{7,11},{8,4},{9,5},... | collective-permute-start | bytes 245768 | tf_op jit(solution)/shard_map/ppermute | solution.py:50
  39.7 7.5 %collective-permute-start.14 = (bf16[8,5120]{1,0:T(8,128)(2,1)S(1)}, bf16[8,5120]{1,0:T(8,128)(2,1)S(1)}, u32[]{:S(2)}, u32[]{:S(2)}) collective-permute-start(bf16[8,5120]{1,0:T(8,128)(2,1)S(1)} %get-tuple-element.53.refs_0_.after_any), channel_id=1, source_target_pairs={{0,8},{1,9},{2,10},{3,11},{4,12},{5,13},{6,14},{7,15},{8,0},{9,1},... | collective-permute-start | bytes 245768 | tf_op jit(solution)/shard_map/ppermute | solution.py:50
  39.7 7.5 %collective-permute-start.13 = (bf16[8,5120]{1,0:T(8,128)(2,1)S(1)}, bf16[8,5120]{1,0:T(8,128)(2,1)S(1)}, u32[]{:S(2)}, u32[]{:S(2)}) collective-permute-start(bf16[8,5120]{1,0:T(8,128)(2,1)S(1)} %get-tuple-element.53.refs_0_.after_any), channel_id=1, source_target_pairs={{0,4},{1,5},{2,6},{3,7},{4,0},{5,1},{6,2},{7,3},{8,12},{9,13},{10,... | collective-permute-start | bytes 245768 | tf_op jit(solution)/shard_map/ppermute | solution.py:50
  41.0 7.7 %collective-permute-start.21 = (bf16[32,5120]{1,0:T(8,128)(2,1)S(1)}, bf16[32,5120]{1,0:T(8,128)(2,1)S(1)}, u32[]{:S(2)}, u32[]{:S(2)}) collective-permute-start(bf16[32,5120]{1,0:T(8,128)(2,1)S(1)} %add_half.5.refs_5_), channel_id=1, source_target_pairs={{1,0},{0,1},{3,2},{2,3},{5,4},{4,5},{7,6},{6,7},{9,8},{8,9},{11,10... | collective-permute-start | bytes 983048 | tf_op jit(solution)/shard_map/ppermute | solution.py:50
  42.5 6.2 %collective-permute-start.20 = (bf16[32,5120]{1,0:T(8,128)(2,1)S(1)}, bf16[32,5120]{1,0:T(8,128)(2,1)S(1)}, u32[]{:S(2)}, u32[]{:S(2)}) collective-permute-start(bf16[32,5120]{1,0:T(8,128)(2,1)S(1)} %add_half.4.refs_4_), channel_id=1, source_target_pairs={{2,0},{3,1},{0,2},{1,3},{6,4},{7,5},{4,6},{5,7},{10,8},{11,9},{8,1... | collective-permute-start | bytes 983048 | tf_op jit(solution)/shard_map/ppermute | solution.py:50
  47.2 9.8 %collective-permute-start.19 = (bf16[32,5120]{1,0:T(8,128)(2,1)S(1)}, bf16[32,5120]{1,0:T(8,128)(2,1)S(1)}, u32[]{:S(2)}, u32[]{:S(2)}) collective-permute-start(bf16[32,5120]{1,0:T(8,128)(2,1)S(1)} %join.3.refs_3_.refs_2_), channel_id=1, source_target_pairs={{0,2},{1,3},{2,0},{3,1},{4,6},{5,7},{6,4},{7,5},{8,10},{9,11},{10,... | collective-permute-start | bytes 983048 | tf_op jit(solution)/shard_map/ppermute | solution.py:50
  48.4 8.6 %collective-permute-start.18 = (bf16[32,5120]{1,0:T(8,128)(2,1)S(1)}, bf16[32,5120]{1,0:T(8,128)(2,1)S(1)}, u32[]{:S(2)}, u32[]{:S(2)}) collective-permute-start(bf16[32,5120]{1,0:T(8,128)(2,1)S(1)} %join.3.refs_3_.refs_2_), channel_id=1, source_target_pairs={{0,1},{1,0},{2,3},{3,2},{4,5},{5,4},{6,7},{7,6},{8,9},{9,8},{10,11... | collective-permute-start | bytes 983048 | tf_op jit(solution)/shard_map/ppermute | solution.py:50
  57.0 5.7 %collective-permute-start.22 = (bf16[16,5120]{1,0:T(8,128)(2,1)S(1)}, bf16[16,5120]{1,0:T(8,128)(2,1)S(1)}, u32[]{:S(2)}, u32[]{:S(2)}) collective-permute-start(bf16[16,5120]{1,0:T(8,128)(2,1)S(1)} %get-tuple-element.59), channel_id=1, source_target_pairs={{0,1},{1,0},{2,3},{3,2},{4,5},{5,4},{6,7},{7,6},{8,9},{9,8},{10,11... | collective-permute-start | bytes 491528 | tf_op jit(solution)/shard_map/ppermute | solution.py:50
  58.2 4.5 %collective-permute-start.23 = (bf16[16,5120]{1,0:T(8,128)(2,1)S(1)}, bf16[16,5120]{1,0:T(8,128)(2,1)S(1)}, u32[]{:S(2)}, u32[]{:S(2)}) collective-permute-start(bf16[16,5120]{1,0:T(8,128)(2,1)S(1)} %get-tuple-element.60), channel_id=1, source_target_pairs={{0,2},{1,3},{2,0},{3,1},{4,6},{5,7},{6,4},{7,5},{8,10},{9,11},{10,... | collective-permute-start | bytes 491528 | tf_op jit(solution)/shard_map/ppermute | solution.py:50
  58.4 3.3 %collective-permute-start.25 = (bf16[8,5120]{1,0:T(8,128)(2,1)S(1)}, bf16[8,5120]{1,0:T(8,128)(2,1)S(1)}, u32[]{:S(2)}, u32[]{:S(2)}) collective-permute-start(bf16[8,5120]{1,0:T(8,128)(2,1)S(1)} %get-tuple-element.61), channel_id=1, source_target_pairs={{4,0},{5,1},{6,2},{7,3},{0,4},{1,5},{2,6},{3,7},{12,8},{13,9},{14,... | collective-permute-start | bytes 245768 | tf_op jit(solution)/shard_map/ppermute | solution.py:50
  58.4 4.3 %collective-permute-start.26 = (bf16[8,5120]{1,0:T(8,128)(2,1)S(1)}, bf16[8,5120]{1,0:T(8,128)(2,1)S(1)}, u32[]{:S(2)}, u32[]{:S(2)}) collective-permute-start(bf16[8,5120]{1,0:T(8,128)(2,1)S(1)} %get-tuple-element.62), channel_id=1, source_target_pairs={{8,0},{9,1},{10,2},{11,3},{12,4},{13,5},{14,6},{15,7},{0,8},{1,9},... | collective-permute-start | bytes 245768 | tf_op jit(solution)/shard_map/ppermute | solution.py:50
  65.1 6.8 %collective-permute-start.30 = (bf16[16,5120]{1,0:T(8,128)(2,1)S(1)}, bf16[16,5120]{1,0:T(8,128)(2,1)S(1)}, u32[]{:S(2)}, u32[]{:S(2)}) collective-permute-start(bf16[16,5120]{1,0:T(8,128)(2,1)S(1)} %get-tuple-element.68), channel_id=1, source_target_pairs={{2,0},{3,1},{0,2},{1,3},{6,4},{7,5},{4,6},{5,7},{10,8},{11,9},{8,1... | collective-permute-start | bytes 491528 | tf_op jit(solution)/shard_map/ppermute | solution.py:50
  66.4 6.8 %collective-permute-start.27 = (bf16[16,5120]{1,0:T(8,128)(2,1)S(1)}, bf16[16,5120]{1,0:T(8,128)(2,1)S(1)}, u32[]{:S(2)}, u32[]{:S(2)}) collective-permute-start(bf16[16,5120]{1,0:T(8,128)(2,1)S(1)} %get-tuple-element.65), channel_id=1, source_target_pairs={{1,0},{0,1},{3,2},{2,3},{5,4},{4,5},{7,6},{6,7},{9,8},{8,9},{11,10... | collective-permute-start | bytes 491528 | tf_op jit(solution)/shard_map/ppermute | solution.py:50
  66.6 5.2 %collective-permute-start.28 = (bf16[8,5120]{1,0:T(8,128)(2,1)S(1)}, bf16[8,5120]{1,0:T(8,128)(2,1)S(1)}, u32[]{:S(2)}, u32[]{:S(2)}) collective-permute-start(bf16[8,5120]{1,0:T(8,128)(2,1)S(1)} %get-tuple-element.66), channel_id=1, source_target_pairs={{12,0},{13,1},{14,2},{15,3},{8,4},{9,5},{10,6},{11,7},{4,8},{5,9},... | collective-permute-start | bytes 245768 | tf_op jit(solution)/shard_map/ppermute | solution.py:50
  71.9 7.7 %collective-permute-start.31 = (bf16[32,5120]{1,0:T(8,128)(2,1)S(1)}, bf16[32,5120]{1,0:T(8,128)(2,1)S(1)}, u32[]{:S(2)}, u32[]{:S(2)}) collective-permute-start(bf16[32,5120]{1,0:T(8,128)(2,1)S(1)} %add_half.7), channel_id=1, source_target_pairs={{1,0},{0,1},{3,2},{2,3},{5,4},{4,5},{7,6},{6,7},{9,8},{8,9},{11,10... | collective-permute-start | bytes 983048 | tf_op jit(solution)/shard_map/ppermute | solution.py:50
  73.3 6.3 %collective-permute-start.29 = (bf16[32,5120]{1,0:T(8,128)(2,1)S(1)}, bf16[32,5120]{1,0:T(8,128)(2,1)S(1)}, u32[]{:S(2)}, u32[]{:S(2)}) collective-permute-start(bf16[32,5120]{1,0:T(8,128)(2,1)S(1)} %add_half.6), channel_id=1, source_target_pairs={{2,0},{3,1},{0,2},{1,3},{6,4},{7,5},{4,6},{5,7},{10,8},{11,9},{8,1... | collective-permute-start | bytes 983048 | tf_op jit(solution)/shard_map/ppermute | solution.py:50
  73.6 10.4 %collective-permute-start.35 = (f32[8,5120]{1,0:T(8,128)S(1)}, f32[8,5120]{1,0:T(8,128)S(1)}, u32[]{:S(2)}, u32[]{:S(2)}) collective-permute-start(f32[8,5120]{1,0:T(8,128)S(1)} %add_last.2.refs_2_.second_ref), channel_id=1, source_target_pairs={{0,16},{1,17},{2,18},{3,19},{4,20},{5,21},{6,22},{7,23},{8,24},{9,... | collective-permute-start | bytes 491528 | tf_op jit(solution)/shard_map/ppermute | solution.py:27
  79.8 5.0 %collective-permute-start.32 = (bf16[8,5120]{1,0:T(8,128)(2,1)S(1)}, bf16[8,5120]{1,0:T(8,128)(2,1)S(1)}, u32[]{:S(2)}, u32[]{:S(2)}) collective-permute-start(bf16[8,5120]{1,0:T(8,128)(2,1)S(1)} %get-tuple-element.71), channel_id=1, source_target_pairs={{4,0},{5,1},{6,2},{7,3},{0,4},{1,5},{2,6},{3,7},{12,8},{13,9},{14,... | collective-permute-start | bytes 245768 | tf_op jit(solution)/shard_map/ppermute | solution.py:50
  80.3 5.1 %collective-permute-start.33 = (bf16[8,5120]{1,0:T(8,128)(2,1)S(1)}, bf16[8,5120]{1,0:T(8,128)(2,1)S(1)}, u32[]{:S(2)}, u32[]{:S(2)}) collective-permute-start(bf16[8,5120]{1,0:T(8,128)(2,1)S(1)} %get-tuple-element.72), channel_id=1, source_target_pairs={{8,0},{9,1},{10,2},{11,3},{12,4},{13,5},{14,6},{15,7},{0,8},{1,9},... | collective-permute-start | bytes 245768 | tf_op jit(solution)/shard_map/ppermute | solution.py:50
  82.0 5.1 %collective-permute-start.34 = (bf16[8,5120]{1,0:T(8,128)(2,1)S(1)}, bf16[8,5120]{1,0:T(8,128)(2,1)S(1)}, u32[]{:S(2)}, u32[]{:S(2)}) collective-permute-start(bf16[8,5120]{1,0:T(8,128)(2,1)S(1)} %get-tuple-element.73), channel_id=1, source_target_pairs={{12,0},{13,1},{14,2},{15,3},{8,4},{9,5},{10,6},{11,7},{4,8},{5,9},... | collective-permute-start | bytes 245768 | tf_op jit(solution)/shard_map/ppermute | solution.py:50
  87.2 11.4 %collective-permute-start.36 = (f32[8,5248]{1,0:T(8,128)S(1)}, f32[8,5248]{1,0:T(8,128)S(1)}, u32[]{:S(2)}, u32[]{:S(2)}) collective-permute-start(f32[8,5248]{1,0:T(8,128)S(1)} %add_last.3.back_ref), channel_id=1, source_target_pairs={{0,16},{1,17},{2,18},{3,19},{4,20},{5,21},{6,22},{7,23},{8,24},{9,... | collective-permute-start | bytes 503816 | tf_op jit(solution)/shard_map/ppermute | solution.py:17

commit v11 on v10

--- a/solution.py
+++ b/solution.py
@@ -607,12 +607,13 @@
         return [sums[0][0][0]]
 
     gathered = grid.gather(capacity, halves, plane_sums)
+    total_grad = grads.send([])
     computed = expert(
-        expert_in[0], expert_out[0], gathered, grid.heights(CAP), grid.types(), [residual_before, *sums[0][1][:2]]
-    )
-    total_grad = grads.send([computed[0]])
+        expert_in[0], expert_out[0], gathered, grid.heights(CAP), grid.types(),
+        [residual_before, total_grad],
+    )
     room, made = blank(section, capacity, residual)
-    results = grid.scatter(computed, CAP, [total_grad], gates)
+    results = grid.scatter(computed, CAP, [], gates)
     next(results)
     results.send([made])
     total_grad, laid = lay_out(section, sections, to_decoder(total_grad), total_grad)

time: 100 us -> 101 us (1.010)
  waiting for transfers between devices: 45 us -> 47.7 us
  starting transfers between devices: 42.3 us -> 40.3 us
    ppermute x28, waiting for transfers between devices: 34.5 us -> 37.4 us  [shift(): return lax.ppermute(block, 'expert', route)]
    ppermute x28, starting transfers between devices: 32.5 us -> 30.5 us  [shift(): return lax.ppermute(block, 'expert', route)]
  transfers between devices with their start and end apart: 37 -> 37, of which waited for: 19 -> 18; matrix products, arithmetic and copies ran while one was open for 0% -> 0% of each run, Pallas kernels for 7% -> 7%
where the time goes in v11:
time: 101 us
  waiting for transfers between devices  47.7 us (47%)
  starting transfers between devices  40.3 us (40%)
  Pallas kernels  10.6 us (10%)
  local copies, waits for them, and re-layouts  1.24 us (1%)
    ppermute x28, waiting for transfers between devices, shift(): return lax.ppermute(block, 'expert', route)  37.4 us
    ppermute x28, starting transfers between devices, shift(): return lax.ppermute(block, 'expert', route)  30.5 us
    ppermute x2, waiting for transfers between devices, passed_along(): return lax.ppermute(block, axis, route)  9.11 us
    pallas_call x18, Pallas kernels, local_kernel(): pl.pallas_call(body, out_shape=tuple(outs), in_specs=in_specs, out_specs=...  7.63 us
    ppermute x5, starting transfers between devices, swapped(): lax.ppermute(block, 'section', [(i, (i + sections // 2) % sections) for i...  4.61 us
    pallas_call x2, Pallas kernels, finish(): pl.pallas_call(kernel, out_shape=one, in_specs=[pl.BlockSpec(memory_space...  2.99 us
    ppermute x2, starting transfers between devices, passed_along(): return lax.ppermute(block, axis, route)  2.57 us
    ppermute x2, starting transfers between devices, to_decoder(): lax.ppermute(block, 'section', [(i, i + apart) for i in range(apart)])  2.57 us
  transfers between devices with their start and end apart: 37, of which 18 were waited for; matrix products, arithmetic and copies ran while one was open for 0% of the time, Pallas kernels for 7%

profile of v11, /device:TPU:1, one launch (start us, length us, event | category | flops | bytes accessed | tf_op | source)
XLA Modules:
  0.0 100.9 jit_solution(3054292900810298445)
XLA Ops:
  0.7 1.1 %slice_bitcast_fusion = (bf16[1,8,2,2560]{3,2,1,0:T(2,128)(2,1)S(1)}, bf16[1,8,2,2560]{3,2,1,0:T(2,128)(2,1)S(1)}) fusion(bf16[1,8,2,5120]{3,2,1,0:T(2,128)(2,1)} %param.10), kind=kLoop, calls=%fused_computation | loop fusion | bytes 327680
  1.8 0.1 collective-permute-start
  2.0 1.2 %collective-permute-done = bf16[8,5120]{1,0:T(8,128)(2,1)S(1)} collective-permute-done((bf16[8,5120]{1,0:T(8,128)(2,1)S(1)}, bf16[8,5120]{1,0:T(8,128)(2,1)S(1)}, u32[]{:S(2)}, u32[]{:S(2)}) %collective-permute-start) | collective-permute-done | bytes 81952 | tf_op jit(solution)/shard_map/ppermute | solution.py:22
  3.2 4.5 %collective-permute-start.3 = (bf16[8,5120]{1,0:T(8,128)(2,1)S(1)}, bf16[8,5120]{1,0:T(8,128)(2,1)S(1)}, u32[]{:S(2)}, u32[]{:S(2)}) collective-permute-start(bf16[8,5120]{1,0:T(8,128)(2,1)S(1)} %broadcast_select_fusion.refs_0_), channel_id=1, source_target_pairs={{0,12},{1,13},{2,14},{3,15},{4,8},{5,9},{6,10},{7,11},{8,4},{9,5},... | collective-permute-start | bytes 245768 | tf_op jit(solution)/shard_map/ppermute | solution.py:50
  7.7 0.4 collective-permute-start.1
  8.1 2.2 %collective-permute-done.3.refs_3_ = bf16[8,5120]{1,0:T(8,128)(2,1)S(1)} collective-permute-done((bf16[8,5120]{1,0:T(8,128)(2,1)S(1)}, bf16[8,5120]{1,0:T(8,128)(2,1)S(1)}, u32[]{:S(2)}, u32[]{:S(2)}) %collective-permute-start.3) | collective-permute-done | bytes 81952 | tf_op jit(solution)/shard_map/ppermute | solution.py:50
  10.3 4.1 %collective-permute-done.2.refs_2_ = bf16[8,5120]{1,0:T(8,128)(2,1)S(1)} collective-permute-done((bf16[8,5120]{1,0:T(8,128)(2,1)S(1)}, bf16[8,5120]{1,0:T(8,128)(2,1)S(1)}, u32[]{:S(2)}, u32[]{:S(2)}) %collective-permute-start.2) | collective-permute-done | bytes 81952 | tf_op jit(solution)/shard_map/ppermute | solution.py:50
  14.4 1.3 %collective-permute-start.7 = (bf16[32,5120]{1,0:T(8,128)(2,1)S(1)}, bf16[32,5120]{1,0:T(8,128)(2,1)S(1)}, u32[]{:S(2)}, u32[]{:S(2)}) collective-permute-start(bf16[32,5120]{1,0:T(8,128)(2,1)S(1)} %join.2.refs_4_), channel_id=1, source_target_pairs={{0,2},{1,3},{2,0},{3,1},{4,6},{5,7},{6,4},{7,5},{8,10},{9,11},{10,... | collective-permute-start | bytes 983048 | tf_op jit(solution)/shard_map/ppermute | solution.py:50
  15.7 1.2 %collective-permute-start.6 = (bf16[32,5120]{1,0:T(8,128)(2,1)S(1)}, bf16[32,5120]{1,0:T(8,128)(2,1)S(1)}, u32[]{:S(2)}, u32[]{:S(2)}) collective-permute-start(bf16[32,5120]{1,0:T(8,128)(2,1)S(1)} %join.2.refs_4_), channel_id=1, source_target_pairs={{0,1},{1,0},{2,3},{3,2},{4,5},{5,4},{6,7},{7,6},{8,9},{9,8},{10,11... | collective-permute-start | bytes 983048 | tf_op jit(solution)/shard_map/ppermute | solution.py:50
  16.9 0.9 queries.1
  17.8 1.8 %collective-permute-start.4 = (bf16[128,1280]{1,0:T(8,128)(2,1)S(1)}, bf16[128,1280]{1,0:T(8,128)(2,1)S(1)}, u32[]{:S(2)}, u32[]{:S(2)}) collective-permute-start(bf16[128,1280]{1,0:T(8,128)(2,1)S(1)} %get-tuple-element.41), channel_id=1, source_target_pairs={{0,16},{16,0},{1,17},{17,1},{2,18},{18,2},{3,19},{19,3},{4,20},{20... | collective-permute-start | bytes 983048 | tf_op jit(solution)/shard_map/ppermute | solution.py:22
  19.6 0.1 collective-permute-start.5
  19.7 0.1 cut.1
  19.8 0.5 collective-permute-start.10
  20.3 2.2 %collective-permute-done.7.refs_6_ = bf16[32,5120]{1,0:T(8,128)(2,1)S(1)} collective-permute-done((bf16[32,5120]{1,0:T(8,128)(2,1)S(1)}, bf16[32,5120]{1,0:T(8,128)(2,1)S(1)}, u32[]{:S(2)}, u32[]{:S(2)}) %collective-permute-start.7) | collective-permute-done | bytes 327712 | tf_op jit(solution)/shard_map/ppermute | solution.py:50
  22.5 2.1 %collective-permute-start.11 = (bf16[128,1280]{1,0:T(8,128)(2,1)S(1)}, bf16[128,1280]{1,0:T(8,128)(2,1)S(1)}, u32[]{:S(2)}, u32[]{:S(2)}) collective-permute-start(bf16[128,1280]{1,0:T(8,128)(2,1)S(1)} %get-tuple-element.46), channel_id=1, source_target_pairs={{0,16},{16,0},{1,17},{17,1},{2,18},{18,2},{3,19},{19,3},{4,20},{20... | collective-permute-start | bytes 983048 | tf_op jit(solution)/shard_map/ppermute | solution.py:22
  24.6 1.3 %collective-permute-start.8 = (bf16[16,5120]{1,0:T(8,128)(2,1)S(1)}, bf16[16,5120]{1,0:T(8,128)(2,1)S(1)}, u32[]{:S(2)}, u32[]{:S(2)}) collective-permute-start(bf16[16,5120]{1,0:T(8,128)(2,1)S(1)} %slice.16), channel_id=1, source_target_pairs={{0,1},{1,0},{2,3},{3,2},{4,5},{5,4},{6,7},{7,6},{8,9},{9,8},{10,11... | collective-permute-start | bytes 491528 | tf_op jit(solution)/shard_map/ppermute | solution.py:50
  25.9 1.3 %collective-permute-start.9 = (bf16[16,5120]{1,0:T(8,128)(2,1)S(1)}, bf16[16,5120]{1,0:T(8,128)(2,1)S(1)}, u32[]{:S(2)}, u32[]{:S(2)}) collective-permute-start(bf16[16,5120]{1,0:T(8,128)(2,1)S(1)} %slice.17), channel_id=1, source_target_pairs={{0,2},{1,3},{2,0},{3,1},{4,6},{5,7},{6,4},{7,5},{8,10},{9,11},{10,... | collective-permute-start | bytes 491528 | tf_op jit(solution)/shard_map/ppermute | solution.py:50
  27.2 1.3 %collective-permute-start.24 = (bf16[128,5120]{1,0:T(8,128)(2,1)S(1)}, bf16[128,5120]{1,0:T(8,128)(2,1)S(1)}, u32[]{:S(2)}, u32[]{:S(2)}) collective-permute-start(bf16[128,5120]{1,0:T(8,128)(2,1)S(1)} %get-tuple-element.40.refs_1_), channel_id=1, source_target_pairs={{0,16},{1,17},{2,18},{3,19},{4,20},{5,21},{6,22},{7,23},{8,24},{9,... | collective-permute-start | bytes 3932168 | tf_op jit(solution)/shard_map/ppermute | solution.py:17
  28.5 0.7 collective-permute-done.8.refs_7_
  29.2 1.2 %collective-permute-done.9.refs_8_ = bf16[16,5120]{1,0:T(8,128)(2,1)S(1)} collective-permute-done((bf16[16,5120]{1,0:T(8,128)(2,1)S(1)}, bf16[16,5120]{1,0:T(8,128)(2,1)S(1)}, u32[]{:S(2)}, u32[]{:S(2)}) %collective-permute-start.9) | collective-permute-done | bytes 163872 | tf_op jit(solution)/shard_map/ppermute | solution.py:50
  30.4 1.0 %attend.1 = (bf16[128,2560]{1,0:T(8,128)(2,1)S(1)}, f32[20,128,128]{2,1,0:T(8,128)S(1)}, bf16[128,2560]{1,0:T(8,128)(2,1)S(1)}) custom-call(s32[1]{0:T(128)} %bitcast.refs_0_.section, bf16[128,1280]{1,0:T(8,128)(2,1)S(1)} %collective-permute-done.4.refs_1_, bf16[128,1280]{1,0:T(8,128)(2,1)S(1)} %collective-permute-done.5.refs_2_, ...), custom_call_target="tpu_custom_call" | custom-call | flops 167772160 | bytes 5242884 | tf_op jit(solution)/shard_map/attend/pallas_call | solution.py:142
  31.5 1.3 %collective-permute-start.12 = (bf16[128,2560]{1,0:T(8,128)(2,1)S(1)}, bf16[128,2560]{1,0:T(8,128)(2,1)S(1)}, u32[]{:S(2)}, u32[]{:S(2)}) collective-permute-start(bf16[128,2560]{1,0:T(8,128)(2,1)S(1)} %get-tuple-element.47.refs_3_), channel_id=1, source_target_pairs={{0,16},{1,17},{2,18},{3,19},{4,20},{5,21},{6,22},{7,23},{8,24},{9,... | collective-permute-start | bytes 1966088 | tf_op jit(solution)/shard_map/ppermute | solution.py:27
  32.8 1.3 %gradient.1 = (f32[32,5120]{1,0:T(8,128)S(1)}, f32[32,5120]{1,0:T(8,128)S(1)}, f32[32,5120]{1,0:T(8,128)S(1)}, bf16[16,5120]{1,0:T(8,128)(2,1)S(1)}, bf16[16,5120]{1,0:T(8,128)(2,1)S(1)}) custom-call(s32[1]{0:T(128)} %bitcast.refs_0_.section, bf16[128,2560]{1,0:T(8,128)(2,1)S(1)} %get-tuple-element.48.q_ref, ...), custom_call_target="tpu_custom_call" | custom-call | flops 419430400 | bytes 6881284 | tf_op jit(solution)/shard_map/gradient/pallas_call | solution.py:142
  34.1 2.2 %collective-permute-start.17 = (bf16[16,5120]{1,0:T(8,128)(2,1)S(1)}, bf16[16,5120]{1,0:T(8,128)(2,1)S(1)}, u32[]{:S(2)}, u32[]{:S(2)}) collective-permute-start(bf16[16,5120]{1,0:T(8,128)(2,1)S(1)} %get-tuple-element.57), channel_id=1, source_target_pairs={{2,0},{3,1},{0,2},{1,3},{6,4},{7,5},{4,6},{5,7},{10,8},{11,9},{8,1... | collective-permute-start | bytes 491528 | tf_op jit(solution)/shard_map/ppermute | solution.py:50
  36.3 0.3 collective-permute-start.16
  36.6 0.7 settle.1
  37.3 2.4 %collective-permute-start.15 = (bf16[8,5120]{1,0:T(8,128)(2,1)S(1)}, bf16[8,5120]{1,0:T(8,128)(2,1)S(1)}, u32[]{:S(2)}, u32[]{:S(2)}) collective-permute-start(bf16[8,5120]{1,0:T(8,128)(2,1)S(1)} %get-tuple-element.53.refs_0_.after_any), channel_id=1, source_target_pairs={{0,12},{1,13},{2,14},{3,15},{4,8},{5,9},{6,10},{7,11},{8,4},{9,5},... | collective-permute-start | bytes 245768 | tf_op jit(solution)/shard_map/ppermute | solution.py:50
  39.7 1.2 %collective-permute-start.13 = (bf16[8,5120]{1,0:T(8,128)(2,1)S(1)}, bf16[8,5120]{1,0:T(8,128)(2,1)S(1)}, u32[]{:S(2)}, u32[]{:S(2)}) collective-permute-start(bf16[8,5120]{1,0:T(8,128)(2,1)S(1)} %get-tuple-element.53.refs_0_.after_any), channel_id=1, source_target_pairs={{0,4},{1,5},{2,6},{3,7},{4,0},{5,1},{6,2},{7,3},{8,12},{9,13},{10,... | collective-permute-start | bytes 245768 | tf_op jit(solution)/shard_map/ppermute | solution.py:50
  41.0 1.2 %collective-permute-start.21 = (bf16[32,5120]{1,0:T(8,128)(2,1)S(1)}, bf16[32,5120]{1,0:T(8,128)(2,1)S(1)}, u32[]{:S(2)}, u32[]{:S(2)}) collective-permute-start(bf16[32,5120]{1,0:T(8,128)(2,1)S(1)} %add_half.5.refs_5_), channel_id=1, source_target_pairs={{1,0},{0,1},{3,2},{2,3},{5,4},{4,5},{7,6},{6,7},{9,8},{8,9},{11,10... | collective-permute-start | bytes 983048 | tf_op jit(solution)/shard_map/ppermute | solution.py:50
  42.3 0.2 collective-permute-done.15.refs_3_
  42.5 1.2 %collective-permute-start.20 = (bf16[32,5120]{1,0:T(8,128)(2,1)S(1)}, bf16[32,5120]{1,0:T(8,128)(2,1)S(1)}, u32[]{:S(2)}, u32[]{:S(2)}) collective-permute-start(bf16[32,5120]{1,0:T(8,128)(2,1)S(1)} %add_half.4.refs_4_), channel_id=1, source_target_pairs={{2,0},{3,1},{0,2},{1,3},{6,4},{7,5},{4,6},{5,7},{10,8},{11,9},{8,1... | collective-permute-start | bytes 983048 | tf_op jit(solution)/shard_map/ppermute | solution.py:50
  43.7 3.5 %collective-permute-done.14.refs_2_ = bf16[8,5120]{1,0:T(8,128)(2,1)S(1)} collective-permute-done((bf16[8,5120]{1,0:T(8,128)(2,1)S(1)}, bf16[8,5120]{1,0:T(8,128)(2,1)S(1)}, u32[]{:S(2)}, u32[]{:S(2)}) %collective-permute-start.14) | collective-permute-done | bytes 81952 | tf_op jit(solution)/shard_map/ppermute | solution.py:50
  47.2 1.2 %collective-permute-start.19 = (bf16[32,5120]{1,0:T(8,128)(2,1)S(1)}, bf16[32,5120]{1,0:T(8,128)(2,1)S(1)}, u32[]{:S(2)}, u32[]{:S(2)}) collective-permute-start(bf16[32,5120]{1,0:T(8,128)(2,1)S(1)} %join.3.refs_3_.refs_2_), channel_id=1, source_target_pairs={{0,2},{1,3},{2,0},{3,1},{4,6},{5,7},{6,4},{7,5},{8,10},{9,11},{10,... | collective-permute-start | bytes 983048 | tf_op jit(solution)/shard_map/ppermute | solution.py:50
  48.5 0.2 collective-permute-start.18
  48.7 0.1 collective-permute-done.20.refs_1_
  48.7 0.1 add_blocks.2
  48.8 0.2 collective-permute-start.25
  49.0 8.0 %collective-permute-done.19.refs_0_.refs_4_ = bf16[32,5120]{1,0:T(8,128)(2,1)S(1)} collective-permute-done((bf16[32,5120]{1,0:T(8,128)(2,1)S(1)}, bf16[32,5120]{1,0:T(8,128)(2,1)S(1)}, u32[]{:S(2)}, u32[]{:S(2)}) %collective-permute-start.19) | collective-permute-done | bytes 327712 | tf_op jit(solution)/shard_map/ppermute | solution.py:50
  57.0 1.2 %collective-permute-start.22 = (bf16[16,5120]{1,0:T(8,128)(2,1)S(1)}, bf16[16,5120]{1,0:T(8,128)(2,1)S(1)}, u32[]{:S(2)}, u32[]{:S(2)}) collective-permute-start(bf16[16,5120]{1,0:T(8,128)(2,1)S(1)} %get-tuple-element.59), channel_id=1, source_target_pairs={{0,1},{1,0},{2,3},{3,2},{4,5},{5,4},{6,7},{7,6},{8,9},{9,8},{10,11... | collective-permute-start | bytes 491528 | tf_op jit(solution)/shard_map/ppermute | solution.py:50
  58.3 0.2 collective-permute-start.23
  58.4 0.1 collective-permute-start.26
  58.6 2.1 %collective-permute-start.27 = (bf16[8,5120]{1,0:T(8,128)(2,1)S(1)}, bf16[8,5120]{1,0:T(8,128)(2,1)S(1)}, u32[]{:S(2)}, u32[]{:S(2)}) collective-permute-start(bf16[8,5120]{1,0:T(8,128)(2,1)S(1)} %get-tuple-element.63), channel_id=1, source_target_pairs={{12,0},{13,1},{14,2},{15,3},{8,4},{9,5},{10,6},{11,7},{4,8},{5,9},... | collective-permute-start | bytes 245768 | tf_op jit(solution)/shard_map/ppermute | solution.py:50
  60.6 3.6 %collective-permute-done.26.refs_1_ = bf16[8,5120]{1,0:T(8,128)(2,1)S(1)} collective-permute-done((bf16[8,5120]{1,0:T(8,128)(2,1)S(1)}, bf16[8,5120]{1,0:T(8,128)(2,1)S(1)}, u32[]{:S(2)}, u32[]{:S(2)}) %collective-permute-start.26) | collective-permute-done | bytes 81952 | tf_op jit(solution)/shard_map/ppermute | solution.py:50
  64.3 2.3 %expert.1 = (f32[32,5120]{1,0:T(8,128)S(1)}, f32[32,5120]{1,0:T(8,128)S(1)}, f32[32,5120]{1,0:T(8,128)S(1)}, bf16[16,5120]{1,0:T(8,128)(2,1)S(1)}, bf16[16,5120]{1,0:T(8,128)(2,1)S(1)}) custom-call(bf16[5120,640]{1,0:T(8,128)(2,1)S(1)} %bitcast.18, bf16[640,5120]{1,0:T(8,128)(2,1)S(1)} %bitcast.21, bf16[32,5120]{1,0:T(8,128)(2,1)S(1)} %join.3.refs_3_.refs_2_, ...), custom_call_target="tpu_custom_call" | custom-call | flops 1677721600 | bytes 16711680 | tf_op jit(solution)/shard_map/expert/pallas_call | solution.py:142
  66.7 1.4 %collective-permute-start.30 = (bf16[16,5120]{1,0:T(8,128)(2,1)S(1)}, bf16[16,5120]{1,0:T(8,128)(2,1)S(1)}, u32[]{:S(2)}, u32[]{:S(2)}) collective-permute-start(bf16[16,5120]{1,0:T(8,128)(2,1)S(1)} %get-tuple-element.68), channel_id=1, source_target_pairs={{2,0},{3,1},{0,2},{1,3},{6,4},{7,5},{4,6},{5,7},{10,8},{11,9},{8,1... | collective-permute-start | bytes 491528 | tf_op jit(solution)/shard_map/ppermute | solution.py:50
  68.0 0.2 collective-permute-start.28
  68.2 2.6 %collective-permute-done.30.refs_0_ = bf16[16,5120]{1,0:T(8,128)(2,1)S(1)} collective-permute-done((bf16[16,5120]{1,0:T(8,128)(2,1)S(1)}, bf16[16,5120]{1,0:T(8,128)(2,1)S(1)}, u32[]{:S(2)}, u32[]{:S(2)}) %collective-permute-start.30) | collective-permute-done | bytes 163872 | tf_op jit(solution)/shard_map/ppermute | solution.py:50
  70.9 1.5 %collective-permute-start.31 = (bf16[32,5120]{1,0:T(8,128)(2,1)S(1)}, bf16[32,5120]{1,0:T(8,128)(2,1)S(1)}, u32[]{:S(2)}, u32[]{:S(2)}) collective-permute-start(bf16[32,5120]{1,0:T(8,128)(2,1)S(1)} %add_half.7), channel_id=1, source_target_pairs={{1,0},{0,1},{3,2},{2,3},{5,4},{4,5},{7,6},{6,7},{9,8},{8,9},{11,10... | collective-permute-start | bytes 983048 | tf_op jit(solution)/shard_map/ppermute | solution.py:50
  72.5 0.2 collective-permute-start.29
  72.6 1.3 %collective-permute-start.35 = (f32[8,5120]{1,0:T(8,128)S(1)}, f32[8,5120]{1,0:T(8,128)S(1)}, u32[]{:S(2)}, u32[]{:S(2)}) collective-permute-start(f32[8,5120]{1,0:T(8,128)S(1)} %add_last.2.refs_8_.second_ref), channel_id=1, source_target_pairs={{0,16},{1,17},{2,18},{3,19},{4,20},{5,21},{6,22},{7,23},{8,24},{9,... | collective-permute-start | bytes 491528 | tf_op jit(solution)/shard_map/ppermute | solution.py:27
  74.0 4.5 %collective-permute-done.31.refs_2_ = bf16[32,5120]{1,0:T(8,128)(2,1)S(1)} collective-permute-done((bf16[32,5120]{1,0:T(8,128)(2,1)S(1)}, bf16[32,5120]{1,0:T(8,128)(2,1)S(1)}, u32[]{:S(2)}, u32[]{:S(2)}) %collective-permute-start.31) | collective-permute-done | bytes 327712 | tf_op jit(solution)/shard_map/ppermute | solution.py:50
  78.5 1.5 %collective-permute-done.29.refs_1_ = bf16[32,5120]{1,0:T(8,128)(2,1)S(1)} collective-permute-done((bf16[32,5120]{1,0:T(8,128)(2,1)S(1)}, bf16[32,5120]{1,0:T(8,128)(2,1)S(1)}, u32[]{:S(2)}, u32[]{:S(2)}) %collective-permute-start.29) | collective-permute-done | bytes 327712 | tf_op jit(solution)/shard_map/ppermute | solution.py:50
  80.0 0.1 add_blocks.3
  80.1 1.1 %collective-permute-start.32 = (bf16[8,5120]{1,0:T(8,128)(2,1)S(1)}, bf16[8,5120]{1,0:T(8,128)(2,1)S(1)}, u32[]{:S(2)}, u32[]{:S(2)}) collective-permute-start(bf16[8,5120]{1,0:T(8,128)(2,1)S(1)} %get-tuple-element.71), channel_id=1, source_target_pairs={{4,0},{5,1},{6,2},{7,3},{0,4},{1,5},{2,6},{3,7},{12,8},{13,9},{14,... | collective-permute-start | bytes 245768 | tf_op jit(solution)/shard_map/ppermute | solution.py:50
  81.2 1.0 %collective-permute-start.33 = (bf16[8,5120]{1,0:T(8,128)(2,1)S(1)}, bf16[8,5120]{1,0:T(8,128)(2,1)S(1)}, u32[]{:S(2)}, u32[]{:S(2)}) collective-permute-start(bf16[8,5120]{1,0:T(8,128)(2,1)S(1)} %get-tuple-element.72), channel_id=1, source_target_pairs={{8,0},{9,1},{10,2},{11,3},{12,4},{13,5},{14,6},{15,7},{0,8},{1,9},... | collective-permute-start | bytes 245768 | tf_op jit(solution)/shard_map/ppermute | solution.py:50
  82.2 1.5 %collective-permute-start.34 = (bf16[8,5120]{1,0:T(8,128)(2,1)S(1)}, bf16[8,5120]{1,0:T(8,128)(2,1)S(1)}, u32[]{:S(2)}, u32[]{:S(2)}) collective-permute-start(bf16[8,5120]{1,0:T(8,128)(2,1)S(1)} %get-tuple-element.73), channel_id=1, source_target_pairs={{12,0},{13,1},{14,2},{15,3},{8,4},{9,5},{10,6},{11,7},{4,8},{5,9},... | collective-permute-start | bytes 245768 | tf_op jit(solution)/shard_map/ppermute | solution.py:50
  83.8 0.8 lay_out.1
  84.5 1.7 %collective-permute-done.33.refs_2_ = bf16[8,5120]{1,0:T(8,128)(2,1)S(1)} collective-permute-done((bf16[8,5120]{1,0:T(8,128)(2,1)S(1)}, bf16[8,5120]{1,0:T(8,128)(2,1)S(1)}, u32[]{:S(2)}, u32[]{:S(2)}) %collective-permute-start.33) | collective-permute-done | bytes 81952 | tf_op jit(solution)/shard_map/ppermute | solution.py:50
  86.3 1.2 %collective-permute-done.34.refs_3_ = bf16[8,5120]{1,0:T(8,128)(2,1)S(1)} collective-permute-done((bf16[8,5120]{1,0:T(8,128)(2,1)S(1)}, bf16[8,5120]{1,0:T(8,128)(2,1)S(1)}, u32[]{:S(2)}, u32[]{:S(2)}) %collective-permute-start.34) | collective-permute-done | bytes 81952 | tf_op jit(solution)/shard_map/ppermute | solution.py:50
  87.5 1.3 %collective-permute-start.36 = (f32[8,5248]{1,0:T(8,128)S(1)}, f32[8,5248]{1,0:T(8,128)S(1)}, u32[]{:S(2)}, u32[]{:S(2)}) collective-permute-start(f32[8,5248]{1,0:T(8,128)S(1)} %add_last.3.back_ref), channel_id=1, source_target_pairs={{0,16},{1,17},{2,18},{3,19},{4,20},{5,21},{6,22},{7,23},{8,24},{9,... | collective-permute-start | bytes 503816 | tf_op jit(solution)/shard_map/ppermute | solution.py:17
  88.8 1.5 %finish.2 = bf16[128,5120]{1,0:T(8,128)(2,1)} custom-call(s32[1]{0:T(128)} %bitcast.refs_0_.section, bf16[128,5120]{1,0:T(8,128)(2,1)S(1)} %get-tuple-element.52.res_ref, f32[8,5248]{1,0:T(8,128)S(1)} %add_last.3.back_ref), custom_call_target="tpu_custom_call" | custom-call | flops 32768000 | bytes 3276800 | tf_op jit(solution)/shard_map/finish/pallas_call | solution.py:541
  90.3 9.1 %collective-permute-done.36.back_ref = f32[8,5248]{1,0:T(8,128)S(1)} collective-permute-done((f32[8,5248]{1,0:T(8,128)S(1)}, f32[8,5248]{1,0:T(8,128)S(1)}, u32[]{:S(2)}, u32[]{:S(2)}) %collective-permute-start.36) | collective-permute-done | bytes 167968 | tf_op jit(solution)/shard_map/ppermute | solution.py:17
  99.4 1.5 %finish.3 = bf16[128,5120]{1,0:T(8,128)(2,1)} custom-call(s32[1]{0:T(128)} %bitcast.refs_0_.section, bf16[128,5120]{1,0:T(8,128)(2,1)S(1)} %collective-permute-done.24.refs_7_.res_ref, f32[8,5248]{1,0:T(8,128)S(1)} %collective-permute-done.36.back_ref, bf16[128,5120]{1,0:T(8,128)(2,1)} %get-tuple-element.75.refs_0_), custom_call_target="tpu_custom_call", output_to_operand_aliasing={{}: (3, {})} | custom-call | flops 32768000 | bytes 3276800 | tf_op jit(solution)/shard_map/finish/pallas_call | solution.py:541
  (59 shorter events, 0.6 us)
Async XLA Ops:
  0.6 16.3 %copy-start.4 = (f32[1,128]{1,0:T(1,128)S(1)}, f32[1,128]{1,0:T(1,128)}, u32[]{:S(2)}) copy-start(f32[1,128]{1,0:T(1,128)} %refs_2_.1) | copy-start | bytes 1540
  0.6 16.3 %copy-start.5 = (s32[1,128]{1,0:T(1,128)S(1)}, s32[1,128]{1,0:T(1,128)}, u32[]{:S(2)}) copy-start(s32[1,128]{1,0:T(1,128)} %refs_3_.1) | copy-start | bytes 1540
  0.7 16.3 %copy-start.3 = (f32[1,5120]{1,0:T(1,128)S(1)}, f32[1,5120]{1,0:T(1,128)}, u32[]{:S(2)}) copy-start(f32[1,5120]{1,0:T(1,128)} %refs_1_.1) | copy-start | bytes 61444
  0.7 16.3 %copy-start = (bf16[1,128,5120]{2,1,0:T(8,128)(2,1)S(1)}, bf16[1,128,5120]{2,1,0:T(8,128)(2,1)}, u32[]{:S(2)}) copy-start(bf16[1,128,5120]{2,1,0:T(8,128)(2,1)} %param.9) | copy-start | bytes 3932164
  1.8 1.3 %collective-permute-start = (bf16[8,5120]{1,0:T(8,128)(2,1)S(1)}, bf16[8,5120]{1,0:T(8,128)(2,1)S(1)}, u32[]{:S(2)}, u32[]{:S(2)}) collective-permute-start(bf16[8,5120]{1,0:T(8,128)(2,1)S(1)} %bitcast.27), channel_id=1, source_target_pairs={{0,16},{16,0},{1,17},{17,1},{2,18},{18,2},{3,19},{19,3},{4,20},{20... | collective-permute-start | bytes 245768 | tf_op jit(solution)/shard_map/ppermute | solution.py:22
  2.0 17.7 %copy-start.1 = (bf16[1,128,5120]{2,1,0:T(8,128)(2,1)S(1)}, bf16[1,128,5120]{2,1,0:T(8,128)(2,1)}, u32[]{:S(2)}) copy-start(bf16[1,128,5120]{2,1,0:T(8,128)(2,1)} %param.11) | copy-start | bytes 3932164
  3.2 7.1 %collective-permute-start.3 = (bf16[8,5120]{1,0:T(8,128)(2,1)S(1)}, bf16[8,5120]{1,0:T(8,128)(2,1)S(1)}, u32[]{:S(2)}, u32[]{:S(2)}) collective-permute-start(bf16[8,5120]{1,0:T(8,128)(2,1)S(1)} %broadcast_select_fusion.refs_0_), channel_id=1, source_target_pairs={{0,12},{1,13},{2,14},{3,15},{4,8},{5,9},{6,10},{7,11},{8,4},{9,5},... | collective-permute-start | bytes 245768 | tf_op jit(solution)/shard_map/ppermute | solution.py:50
  7.7 6.6 %collective-permute-start.2 = (bf16[8,5120]{1,0:T(8,128)(2,1)S(1)}, bf16[8,5120]{1,0:T(8,128)(2,1)S(1)}, u32[]{:S(2)}, u32[]{:S(2)}) collective-permute-start(bf16[8,5120]{1,0:T(8,128)(2,1)S(1)} %broadcast_select_fusion.refs_0_), channel_id=1, source_target_pairs={{0,8},{1,9},{2,10},{3,11},{4,12},{5,13},{6,14},{7,15},{8,0},{9,1},... | collective-permute-start | bytes 245768 | tf_op jit(solution)/shard_map/ppermute | solution.py:50
  7.7 6.6 %collective-permute-start.1 = (bf16[8,5120]{1,0:T(8,128)(2,1)S(1)}, bf16[8,5120]{1,0:T(8,128)(2,1)S(1)}, u32[]{:S(2)}, u32[]{:S(2)}) collective-permute-start(bf16[8,5120]{1,0:T(8,128)(2,1)S(1)} %broadcast_select_fusion.refs_0_), channel_id=1, source_target_pairs={{0,4},{1,5},{2,6},{3,7},{4,0},{5,1},{6,2},{7,3},{8,12},{9,13},{10,... | collective-permute-start | bytes 245768 | tf_op jit(solution)/shard_map/ppermute | solution.py:50
  14.4 8.1 %collective-permute-start.7 = (bf16[32,5120]{1,0:T(8,128)(2,1)S(1)}, bf16[32,5120]{1,0:T(8,128)(2,1)S(1)}, u32[]{:S(2)}, u32[]{:S(2)}) collective-permute-start(bf16[32,5120]{1,0:T(8,128)(2,1)S(1)} %join.2.refs_4_), channel_id=1, source_target_pairs={{0,2},{1,3},{2,0},{3,1},{4,6},{5,7},{6,4},{7,5},{8,10},{9,11},{10,... | collective-permute-start | bytes 983048 | tf_op jit(solution)/shard_map/ppermute | solution.py:50
  15.7 8.9 %collective-permute-start.6 = (bf16[32,5120]{1,0:T(8,128)(2,1)S(1)}, bf16[32,5120]{1,0:T(8,128)(2,1)S(1)}, u32[]{:S(2)}, u32[]{:S(2)}) collective-permute-start(bf16[32,5120]{1,0:T(8,128)(2,1)S(1)} %join.2.refs_4_), channel_id=1, source_target_pairs={{0,1},{1,0},{2,3},{3,2},{4,5},{5,4},{6,7},{7,6},{8,9},{9,8},{10,11... | collective-permute-start | bytes 983048 | tf_op jit(solution)/shard_map/ppermute | solution.py:50
  17.8 8.1 %collective-permute-start.4 = (bf16[128,1280]{1,0:T(8,128)(2,1)S(1)}, bf16[128,1280]{1,0:T(8,128)(2,1)S(1)}, u32[]{:S(2)}, u32[]{:S(2)}) collective-permute-start(bf16[128,1280]{1,0:T(8,128)(2,1)S(1)} %get-tuple-element.41), channel_id=1, source_target_pairs={{0,16},{16,0},{1,17},{17,1},{2,18},{18,2},{3,19},{19,3},{4,20},{20... | collective-permute-start | bytes 983048 | tf_op jit(solution)/shard_map/ppermute | solution.py:22
  19.6 7.6 %collective-permute-start.5 = (bf16[128,1280]{1,0:T(8,128)(2,1)S(1)}, bf16[128,1280]{1,0:T(8,128)(2,1)S(1)}, u32[]{:S(2)}, u32[]{:S(2)}) collective-permute-start(bf16[128,1280]{1,0:T(8,128)(2,1)S(1)} %get-tuple-element.42), channel_id=1, source_target_pairs={{0,16},{16,0},{1,17},{17,1},{2,18},{18,2},{3,19},{19,3},{4,20},{20... | collective-permute-start | bytes 983048 | tf_op jit(solution)/shard_map/ppermute | solution.py:22
  19.8 8.7 %collective-permute-start.10 = (bf16[128,1280]{1,0:T(8,128)(2,1)S(1)}, bf16[128,1280]{1,0:T(8,128)(2,1)S(1)}, u32[]{:S(2)}, u32[]{:S(2)}) collective-permute-start(bf16[128,1280]{1,0:T(8,128)(2,1)S(1)} %get-tuple-element.45), channel_id=1, source_target_pairs={{0,16},{16,0},{1,17},{17,1},{2,18},{18,2},{3,19},{19,3},{4,20},{20... | collective-permute-start | bytes 983048 | tf_op jit(solution)/shard_map/ppermute | solution.py:22
  22.5 6.0 %collective-permute-start.11 = (bf16[128,1280]{1,0:T(8,128)(2,1)S(1)}, bf16[128,1280]{1,0:T(8,128)(2,1)S(1)}, u32[]{:S(2)}, u32[]{:S(2)}) collective-permute-start(bf16[128,1280]{1,0:T(8,128)(2,1)S(1)} %get-tuple-element.46), channel_id=1, source_target_pairs={{0,16},{16,0},{1,17},{17,1},{2,18},{18,2},{3,19},{19,3},{4,20},{20... | collective-permute-start | bytes 983048 | tf_op jit(solution)/shard_map/ppermute | solution.py:22
  24.6 39.7 %slice-start.2 = ((s8[6553600]{0:T(1024)(128)(4,1)}), s8[2359296]{0:T(1024)(128)(4,1)S(1)}, s32[]{:S(2)}) async-start(s8[6553600]{0:T(1024)(128)(4,1)} %bitcast.19), calls=%async_computation.2 | async-start | bytes 4718592
  24.6 4.6 %collective-permute-start.8 = (bf16[16,5120]{1,0:T(8,128)(2,1)S(1)}, bf16[16,5120]{1,0:T(8,128)(2,1)S(1)}, u32[]{:S(2)}, u32[]{:S(2)}) collective-permute-start(bf16[16,5120]{1,0:T(8,128)(2,1)S(1)} %slice.16), channel_id=1, source_target_pairs={{0,1},{1,0},{2,3},{3,2},{4,5},{5,4},{6,7},{7,6},{8,9},{9,8},{10,11... | collective-permute-start | bytes 491528 | tf_op jit(solution)/shard_map/ppermute | solution.py:50
  25.9 4.5 %collective-permute-start.9 = (bf16[16,5120]{1,0:T(8,128)(2,1)S(1)}, bf16[16,5120]{1,0:T(8,128)(2,1)S(1)}, u32[]{:S(2)}, u32[]{:S(2)}) collective-permute-start(bf16[16,5120]{1,0:T(8,128)(2,1)S(1)} %slice.17), channel_id=1, source_target_pairs={{0,2},{1,3},{2,0},{3,1},{4,6},{5,7},{6,4},{7,5},{8,10},{9,11},{10,... | collective-permute-start | bytes 491528 | tf_op jit(solution)/shard_map/ppermute | solution.py:50
  27.2 37.0 %collective-permute-start.24 = (bf16[128,5120]{1,0:T(8,128)(2,1)S(1)}, bf16[128,5120]{1,0:T(8,128)(2,1)S(1)}, u32[]{:S(2)}, u32[]{:S(2)}) collective-permute-start(bf16[128,5120]{1,0:T(8,128)(2,1)S(1)} %get-tuple-element.40.refs_1_), channel_id=1, source_target_pairs={{0,16},{1,17},{2,18},{3,19},{4,20},{5,21},{6,22},{7,23},{8,24},{9,... | collective-permute-start | bytes 3932168 | tf_op jit(solution)/shard_map/ppermute | solution.py:17
  31.5 5.1 %collective-permute-start.12 = (bf16[128,2560]{1,0:T(8,128)(2,1)S(1)}, bf16[128,2560]{1,0:T(8,128)(2,1)S(1)}, u32[]{:S(2)}, u32[]{:S(2)}) collective-permute-start(bf16[128,2560]{1,0:T(8,128)(2,1)S(1)} %get-tuple-element.47.refs_3_), channel_id=1, source_target_pairs={{0,16},{1,17},{2,18},{3,19},{4,20},{5,21},{6,22},{7,23},{8,24},{9,... | collective-permute-start | bytes 1966088 | tf_op jit(solution)/shard_map/ppermute | solution.py:27
  32.8 3.9 %copy-start.2 = (f32[1,5120]{1,0:T(1,128)S(1)}, f32[1,5120]{1,0:T(1,128)}, u32[]{:S(2)}) copy-start(f32[1,5120]{1,0:T(1,128)} %refs_4_.1) | copy-start | bytes 61444
  32.8 31.5 %slice-start = ((s8[6553600]{0:T(1024)(128)(4,1)}), s8[4194304]{0:T(1024)(128)(4,1)S(1)}, s32[]{:S(2)}) async-start(s8[6553600]{0:T(1024)(128)(4,1)} %bitcast.16), calls=%async_computation | async-start | bytes 8388608
  34.1 5.6 %collective-permute-start.17 = (bf16[16,5120]{1,0:T(8,128)(2,1)S(1)}, bf16[16,5120]{1,0:T(8,128)(2,1)S(1)}, u32[]{:S(2)}, u32[]{:S(2)}) collective-permute-start(bf16[16,5120]{1,0:T(8,128)(2,1)S(1)} %get-tuple-element.57), channel_id=1, source_target_pairs={{2,0},{3,1},{0,2},{1,3},{6,4},{7,5},{4,6},{5,7},{10,8},{11,9},{8,1... | collective-permute-start | bytes 491528 | tf_op jit(solution)/shard_map/ppermute | solution.py:50
  36.3 4.7 %collective-permute-start.16 = (bf16[16,5120]{1,0:T(8,128)(2,1)S(1)}, bf16[16,5120]{1,0:T(8,128)(2,1)S(1)}, u32[]{:S(2)}, u32[]{:S(2)}) collective-permute-start(bf16[16,5120]{1,0:T(8,128)(2,1)S(1)} %get-tuple-element.55), channel_id=1, source_target_pairs={{1,0},{0,1},{3,2},{2,3},{5,4},{4,5},{7,6},{6,7},{9,8},{8,9},{11,10... | collective-permute-start | bytes 491528 | tf_op jit(solution)/shard_map/ppermute | solution.py:50
  36.6 27.7 %slice-start.1 = ((s8[6553600]{0:T(1024)(128)(4,1)}), s8[2359296]{0:T(1024)(128)(4,1)S(1)}, s32[]{:S(2)}) async-start(s8[6553600]{0:T(1024)(128)(4,1)} %bitcast.16), calls=%async_computation.1 | async-start | bytes 4718592
  36.6 27.7 %slice-start.3 = ((s8[6553600]{0:T(1024)(128)(4,1)}), s8[4194304]{0:T(1024)(128)(4,1)S(1)}, s32[]{:S(2)}) async-start(s8[6553600]{0:T(1024)(128)(4,1)} %bitcast.19), calls=%async_computation.3 | async-start | bytes 8388608
  37.3 5.2 %collective-permute-start.15 = (bf16[8,5120]{1,0:T(8,128)(2,1)S(1)}, bf16[8,5120]{1,0:T(8,128)(2,1)S(1)}, u32[]{:S(2)}, u32[]{:S(2)}) collective-permute-start(bf16[8,5120]{1,0:T(8,128)(2,1)S(1)} %get-tuple-element.53.refs_0_.after_any), channel_id=1, source_target_pairs={{0,12},{1,13},{2,14},{3,15},{4,8},{5,9},{6,10},{7,11},{8,4},{9,5},... | collective-permute-start | bytes 245768 | tf_op jit(solution)/shard_map/ppermute | solution.py:50
  39.7 7.5 %collective-permute-start.14 = (bf16[8,5120]{1,0:T(8,128)(2,1)S(1)}, bf16[8,5120]{1,0:T(8,128)(2,1)S(1)}, u32[]{:S(2)}, u32[]{:S(2)}) collective-permute-start(bf16[8,5120]{1,0:T(8,128)(2,1)S(1)} %get-tuple-element.53.refs_0_.after_any), channel_id=1, source_target_pairs={{0,8},{1,9},{2,10},{3,11},{4,12},{5,13},{6,14},{7,15},{8,0},{9,1},... | collective-permute-start | bytes 245768 | tf_op jit(solution)/shard_map/ppermute | solution.py:50
  39.7 7.5 %collective-permute-start.13 = (bf16[8,5120]{1,0:T(8,128)(2,1)S(1)}, bf16[8,5120]{1,0:T(8,128)(2,1)S(1)}, u32[]{:S(2)}, u32[]{:S(2)}) collective-permute-start(bf16[8,5120]{1,0:T(8,128)(2,1)S(1)} %get-tuple-element.53.refs_0_.after_any), channel_id=1, source_target_pairs={{0,4},{1,5},{2,6},{3,7},{4,0},{5,1},{6,2},{7,3},{8,12},{9,13},{10,... | collective-permute-start | bytes 245768 | tf_op jit(solution)/shard_map/ppermute | solution.py:50
  41.0 7.6 %collective-permute-start.21 = (bf16[32,5120]{1,0:T(8,128)(2,1)S(1)}, bf16[32,5120]{1,0:T(8,128)(2,1)S(1)}, u32[]{:S(2)}, u32[]{:S(2)}) collective-permute-start(bf16[32,5120]{1,0:T(8,128)(2,1)S(1)} %add_half.5.refs_5_), channel_id=1, source_target_pairs={{1,0},{0,1},{3,2},{2,3},{5,4},{4,5},{7,6},{6,7},{9,8},{8,9},{11,10... | collective-permute-start | bytes 983048 | tf_op jit(solution)/shard_map/ppermute | solution.py:50
  42.5 6.2 %collective-permute-start.20 = (bf16[32,5120]{1,0:T(8,128)(2,1)S(1)}, bf16[32,5120]{1,0:T(8,128)(2,1)S(1)}, u32[]{:S(2)}, u32[]{:S(2)}) collective-permute-start(bf16[32,5120]{1,0:T(8,128)(2,1)S(1)} %add_half.4.refs_4_), channel_id=1, source_target_pairs={{2,0},{3,1},{0,2},{1,3},{6,4},{7,5},{4,6},{5,7},{10,8},{11,9},{8,1... | collective-permute-start | bytes 983048 | tf_op jit(solution)/shard_map/ppermute | solution.py:50
  47.2 9.8 %collective-permute-start.19 = (bf16[32,5120]{1,0:T(8,128)(2,1)S(1)}, bf16[32,5120]{1,0:T(8,128)(2,1)S(1)}, u32[]{:S(2)}, u32[]{:S(2)}) collective-permute-start(bf16[32,5120]{1,0:T(8,128)(2,1)S(1)} %join.3.refs_3_.refs_2_), channel_id=1, source_target_pairs={{0,2},{1,3},{2,0},{3,1},{4,6},{5,7},{6,4},{7,5},{8,10},{9,11},{10,... | collective-permute-start | bytes 983048 | tf_op jit(solution)/shard_map/ppermute | solution.py:50
  48.5 8.6 %collective-permute-start.18 = (bf16[32,5120]{1,0:T(8,128)(2,1)S(1)}, bf16[32,5120]{1,0:T(8,128)(2,1)S(1)}, u32[]{:S(2)}, u32[]{:S(2)}) collective-permute-start(bf16[32,5120]{1,0:T(8,128)(2,1)S(1)} %join.3.refs_3_.refs_2_), channel_id=1, source_target_pairs={{0,1},{1,0},{2,3},{3,2},{4,5},{5,4},{6,7},{7,6},{8,9},{9,8},{10,11... | collective-permute-start | bytes 983048 | tf_op jit(solution)/shard_map/ppermute | solution.py:50
  48.8 9.7 %collective-permute-start.25 = (bf16[8,5120]{1,0:T(8,128)(2,1)S(1)}, bf16[8,5120]{1,0:T(8,128)(2,1)S(1)}, u32[]{:S(2)}, u32[]{:S(2)}) collective-permute-start(bf16[8,5120]{1,0:T(8,128)(2,1)S(1)} %get-tuple-element.61), channel_id=1, source_target_pairs={{4,0},{5,1},{6,2},{7,3},{0,4},{1,5},{2,6},{3,7},{12,8},{13,9},{14,... | collective-permute-start | bytes 245768 | tf_op jit(solution)/shard_map/ppermute | solution.py:50
  57.0 7.2 %collective-permute-start.22 = (bf16[16,5120]{1,0:T(8,128)(2,1)S(1)}, bf16[16,5120]{1,0:T(8,128)(2,1)S(1)}, u32[]{:S(2)}, u32[]{:S(2)}) collective-permute-start(bf16[16,5120]{1,0:T(8,128)(2,1)S(1)} %get-tuple-element.59), channel_id=1, source_target_pairs={{0,1},{1,0},{2,3},{3,2},{4,5},{5,4},{6,7},{7,6},{8,9},{9,8},{10,11... | collective-permute-start | bytes 491528 | tf_op jit(solution)/shard_map/ppermute | solution.py:50
  58.3 6.0 %collective-permute-start.23 = (bf16[16,5120]{1,0:T(8,128)(2,1)S(1)}, bf16[16,5120]{1,0:T(8,128)(2,1)S(1)}, u32[]{:S(2)}, u32[]{:S(2)}) collective-permute-start(bf16[16,5120]{1,0:T(8,128)(2,1)S(1)} %get-tuple-element.60), channel_id=1, source_target_pairs={{0,2},{1,3},{2,0},{3,1},{4,6},{5,7},{6,4},{7,5},{8,10},{9,11},{10,... | collective-permute-start | bytes 491528 | tf_op jit(solution)/shard_map/ppermute | solution.py:50
  58.4 5.8 %collective-permute-start.26 = (bf16[8,5120]{1,0:T(8,128)(2,1)S(1)}, bf16[8,5120]{1,0:T(8,128)(2,1)S(1)}, u32[]{:S(2)}, u32[]{:S(2)}) collective-permute-start(bf16[8,5120]{1,0:T(8,128)(2,1)S(1)} %get-tuple-element.62), channel_id=1, source_target_pairs={{8,0},{9,1},{10,2},{11,3},{12,4},{13,5},{14,6},{15,7},{0,8},{1,9},... | collective-permute-start | bytes 245768 | tf_op jit(solution)/shard_map/ppermute | solution.py:50
  58.6 5.7 %collective-permute-start.27 = (bf16[8,5120]{1,0:T(8,128)(2,1)S(1)}, bf16[8,5120]{1,0:T(8,128)(2,1)S(1)}, u32[]{:S(2)}, u32[]{:S(2)}) collective-permute-start(bf16[8,5120]{1,0:T(8,128)(2,1)S(1)} %get-tuple-element.63), channel_id=1, source_target_pairs={{12,0},{13,1},{14,2},{15,3},{8,4},{9,5},{10,6},{11,7},{4,8},{5,9},... | collective-permute-start | bytes 245768 | tf_op jit(solution)/shard_map/ppermute | solution.py:50
  66.7 4.2 %collective-permute-start.30 = (bf16[16,5120]{1,0:T(8,128)(2,1)S(1)}, bf16[16,5120]{1,0:T(8,128)(2,1)S(1)}, u32[]{:S(2)}, u32[]{:S(2)}) collective-permute-start(bf16[16,5120]{1,0:T(8,128)(2,1)S(1)} %get-tuple-element.68), channel_id=1, source_target_pairs={{2,0},{3,1},{0,2},{1,3},{6,4},{7,5},{4,6},{5,7},{10,8},{11,9},{8,1... | collective-permute-start | bytes 491528 | tf_op jit(solution)/shard_map/ppermute | solution.py:50
  68.0 4.4 %collective-permute-start.28 = (bf16[16,5120]{1,0:T(8,128)(2,1)S(1)}, bf16[16,5120]{1,0:T(8,128)(2,1)S(1)}, u32[]{:S(2)}, u32[]{:S(2)}) collective-permute-start(bf16[16,5120]{1,0:T(8,128)(2,1)S(1)} %get-tuple-element.66), channel_id=1, source_target_pairs={{1,0},{0,1},{3,2},{2,3},{5,4},{4,5},{7,6},{6,7},{9,8},{8,9},{11,10... | collective-permute-start | bytes 491528 | tf_op jit(solution)/shard_map/ppermute | solution.py:50
  70.9 7.6 %collective-permute-start.31 = (bf16[32,5120]{1,0:T(8,128)(2,1)S(1)}, bf16[32,5120]{1,0:T(8,128)(2,1)S(1)}, u32[]{:S(2)}, u32[]{:S(2)}) collective-permute-start(bf16[32,5120]{1,0:T(8,128)(2,1)S(1)} %add_half.7), channel_id=1, source_target_pairs={{1,0},{0,1},{3,2},{2,3},{5,4},{4,5},{7,6},{6,7},{9,8},{8,9},{11,10... | collective-permute-start | bytes 983048 | tf_op jit(solution)/shard_map/ppermute | solution.py:50
  72.5 7.5 %collective-permute-start.29 = (bf16[32,5120]{1,0:T(8,128)(2,1)S(1)}, bf16[32,5120]{1,0:T(8,128)(2,1)S(1)}, u32[]{:S(2)}, u32[]{:S(2)}) collective-permute-start(bf16[32,5120]{1,0:T(8,128)(2,1)S(1)} %add_half.6), channel_id=1, source_target_pairs={{2,0},{3,1},{0,2},{1,3},{6,4},{7,5},{4,6},{5,7},{10,8},{11,9},{8,1... | collective-permute-start | bytes 983048 | tf_op jit(solution)/shard_map/ppermute | solution.py:50
  72.6 11.1 %collective-permute-start.35 = (f32[8,5120]{1,0:T(8,128)S(1)}, f32[8,5120]{1,0:T(8,128)S(1)}, u32[]{:S(2)}, u32[]{:S(2)}) collective-permute-start(f32[8,5120]{1,0:T(8,128)S(1)} %add_last.2.refs_8_.second_ref), channel_id=1, source_target_pairs={{0,16},{1,17},{2,18},{3,19},{4,20},{5,21},{6,22},{7,23},{8,24},{9,... | collective-permute-start | bytes 491528 | tf_op jit(solution)/shard_map/ppermute | solution.py:27
  80.1 4.4 %collective-permute-start.32 = (bf16[8,5120]{1,0:T(8,128)(2,1)S(1)}, bf16[8,5120]{1,0:T(8,128)(2,1)S(1)}, u32[]{:S(2)}, u32[]{:S(2)}) collective-permute-start(bf16[8,5120]{1,0:T(8,128)(2,1)S(1)} %get-tuple-element.71), channel_id=1, source_target_pairs={{4,0},{5,1},{6,2},{7,3},{0,4},{1,5},{2,6},{3,7},{12,8},{13,9},{14,... | collective-permute-start | bytes 245768 | tf_op jit(solution)/shard_map/ppermute | solution.py:50
  81.2 5.1 %collective-permute-start.33 = (bf16[8,5120]{1,0:T(8,128)(2,1)S(1)}, bf16[8,5120]{1,0:T(8,128)(2,1)S(1)}, u32[]{:S(2)}, u32[]{:S(2)}) collective-permute-start(bf16[8,5120]{1,0:T(8,128)(2,1)S(1)} %get-tuple-element.72), channel_id=1, source_target_pairs={{8,0},{9,1},{10,2},{11,3},{12,4},{13,5},{14,6},{15,7},{0,8},{1,9},... | collective-permute-start | bytes 245768 | tf_op jit(solution)/shard_map/ppermute | solution.py:50
  82.2 5.2 %collective-permute-start.34 = (bf16[8,5120]{1,0:T(8,128)(2,1)S(1)}, bf16[8,5120]{1,0:T(8,128)(2,1)S(1)}, u32[]{:S(2)}, u32[]{:S(2)}) collective-permute-start(bf16[8,5120]{1,0:T(8,128)(2,1)S(1)} %get-tuple-element.73), channel_id=1, source_target_pairs={{12,0},{13,1},{14,2},{15,3},{8,4},{9,5},{10,6},{11,7},{4,8},{5,9},... | collective-permute-start | bytes 245768 | tf_op jit(solution)/shard_map/ppermute | solution.py:50
  87.5 11.9 %collective-permute-start.36 = (f32[8,5248]{1,0:T(8,128)S(1)}, f32[8,5248]{1,0:T(8,128)S(1)}, u32[]{:S(2)}, u32[]{:S(2)}) collective-permute-start(f32[8,5248]{1,0:T(8,128)S(1)} %add_last.3.back_ref), channel_id=1, source_target_pairs={{0,16},{1,17},{2,18},{3,19},{4,20},{5,21},{6,22},{7,23},{8,24},{9,... | collective-permute-start | bytes 503816 | tf_op jit(solution)/shard_map/ppermute | solution.py:17

commit v12 on v10

--- a/solution.py
+++ b/solution.py
@@ -102,7 +102,7 @@
         arrived = [self.shift(piece, by, back=True) for piece, (*_, by) in zip(halves, arrived)]
         after = yield halves
         blocks = add_blocks(held[0, 0][0], arrived, rows, after)
-        more = [self.shift(blocks[s], (s, 0, 0), back=True) for s in range(1, na)]
+        more = [self.shift(blocks[s], (s, 0, 0), back=True) for s in reversed(range(1, na))]
         after = yield blocks, more
         yield add_last(blocks[0], more, after, extra)
 

time: 100 us -> 101 us (1.010)
  waiting for transfers between devices: 45 us -> 47 us
  starting transfers between devices: 42.3 us -> 40.5 us
    ppermute x28, waiting for transfers between devices: 34.5 us -> 37.9 us  [shift(): return lax.ppermute(block, 'expert', route)]
    ppermute x28, starting transfers between devices: 32.5 us -> 30.8 us  [shift(): return lax.ppermute(block, 'expert', route)]
where the time goes in v12:
time: 101 us; the launch traced here: 100 us
  waiting for transfers between devices  47 us (47%)
  starting transfers between devices  40.5 us (40%)
  Pallas kernels  10.6 us (10%)
  local copies, waits for them, and re-layouts  1.24 us (1%)
    ppermute x28, waiting for transfers between devices, shift(): return lax.ppermute(block, 'expert', route)  37.9 us
    ppermute x28, starting transfers between devices, shift(): return lax.ppermute(block, 'expert', route)  30.8 us
    ppermute x2, waiting for transfers between devices, passed_along(): return lax.ppermute(block, axis, route)  7.9 us
    pallas_call x18, Pallas kernels, local_kernel(): pl.pallas_call(body, out_shape=tuple(outs), in_specs=in_specs, out_specs=...  7.58 us
    ppermute x5, starting transfers between devices, swapped(): lax.ppermute(block, 'section', [(i, (i + sections // 2) % sections) for i...  4.61 us
    pallas_call x2, Pallas kernels, finish(): pl.pallas_call(kernel, out_shape=one, in_specs=[pl.BlockSpec(memory_space...  2.99 us
    ppermute x2, starting transfers between devices, passed_along(): return lax.ppermute(block, axis, route)  2.57 us
    ppermute x2, starting transfers between devices, to_decoder(): lax.ppermute(block, 'section', [(i, i + apart) for i in range(apart)])  2.57 us
  transfers between devices with their start and end apart: 37, of which 19 were waited for; matrix products, arithmetic and copies ran while one was open for 0% of the time, Pallas kernels for 7%

profile of v12, /device:TPU:1, one launch (start us, length us, event | category | flops | bytes accessed | tf_op | source)
XLA Modules:
  0.0 100.4 jit_solution(6726392140161190275)
XLA Ops:
  0.7 1.1 %slice_bitcast_fusion = (bf16[1,8,2,2560]{3,2,1,0:T(2,128)(2,1)S(1)}, bf16[1,8,2,2560]{3,2,1,0:T(2,128)(2,1)S(1)}) fusion(bf16[1,8,2,5120]{3,2,1,0:T(2,128)(2,1)} %param.10), kind=kLoop, calls=%fused_computation | loop fusion | bytes 327680
  1.8 0.1 collective-permute-start
  2.0 1.2 %collective-permute-done = bf16[8,5120]{1,0:T(8,128)(2,1)S(1)} collective-permute-done((bf16[8,5120]{1,0:T(8,128)(2,1)S(1)}, bf16[8,5120]{1,0:T(8,128)(2,1)S(1)}, u32[]{:S(2)}, u32[]{:S(2)}) %collective-permute-start) | collective-permute-done | bytes 81952 | tf_op jit(solution)/shard_map/ppermute | solution.py:22
  3.2 4.5 %collective-permute-start.3 = (bf16[8,5120]{1,0:T(8,128)(2,1)S(1)}, bf16[8,5120]{1,0:T(8,128)(2,1)S(1)}, u32[]{:S(2)}, u32[]{:S(2)}) collective-permute-start(bf16[8,5120]{1,0:T(8,128)(2,1)S(1)} %broadcast_select_fusion.refs_0_), channel_id=1, source_target_pairs={{0,12},{1,13},{2,14},{3,15},{4,8},{5,9},{6,10},{7,11},{8,4},{9,5},... | collective-permute-start | bytes 245768 | tf_op jit(solution)/shard_map/ppermute | solution.py:50
  7.7 0.4 collective-permute-start.1
  8.1 2.2 %collective-permute-done.3.refs_3_ = bf16[8,5120]{1,0:T(8,128)(2,1)S(1)} collective-permute-done((bf16[8,5120]{1,0:T(8,128)(2,1)S(1)}, bf16[8,5120]{1,0:T(8,128)(2,1)S(1)}, u32[]{:S(2)}, u32[]{:S(2)}) %collective-permute-start.3) | collective-permute-done | bytes 81952 | tf_op jit(solution)/shard_map/ppermute | solution.py:50
  10.3 4.1 %collective-permute-done.2.refs_2_ = bf16[8,5120]{1,0:T(8,128)(2,1)S(1)} collective-permute-done((bf16[8,5120]{1,0:T(8,128)(2,1)S(1)}, bf16[8,5120]{1,0:T(8,128)(2,1)S(1)}, u32[]{:S(2)}, u32[]{:S(2)}) %collective-permute-start.2) | collective-permute-done | bytes 81952 | tf_op jit(solution)/shard_map/ppermute | solution.py:50
  14.4 1.3 %collective-permute-start.7 = (bf16[32,5120]{1,0:T(8,128)(2,1)S(1)}, bf16[32,5120]{1,0:T(8,128)(2,1)S(1)}, u32[]{:S(2)}, u32[]{:S(2)}) collective-permute-start(bf16[32,5120]{1,0:T(8,128)(2,1)S(1)} %join.2.refs_4_), channel_id=1, source_target_pairs={{0,2},{1,3},{2,0},{3,1},{4,6},{5,7},{6,4},{7,5},{8,10},{9,11},{10,... | collective-permute-start | bytes 983048 | tf_op jit(solution)/shard_map/ppermute | solution.py:50
  15.7 1.2 %collective-permute-start.6 = (bf16[32,5120]{1,0:T(8,128)(2,1)S(1)}, bf16[32,5120]{1,0:T(8,128)(2,1)S(1)}, u32[]{:S(2)}, u32[]{:S(2)}) collective-permute-start(bf16[32,5120]{1,0:T(8,128)(2,1)S(1)} %join.2.refs_4_), channel_id=1, source_target_pairs={{0,1},{1,0},{2,3},{3,2},{4,5},{5,4},{6,7},{7,6},{8,9},{9,8},{10,11... | collective-permute-start | bytes 983048 | tf_op jit(solution)/shard_map/ppermute | solution.py:50
  16.9 0.9 queries.1
  17.8 1.8 %collective-permute-start.4 = (bf16[128,1280]{1,0:T(8,128)(2,1)S(1)}, bf16[128,1280]{1,0:T(8,128)(2,1)S(1)}, u32[]{:S(2)}, u32[]{:S(2)}) collective-permute-start(bf16[128,1280]{1,0:T(8,128)(2,1)S(1)} %get-tuple-element.41), channel_id=1, source_target_pairs={{0,16},{16,0},{1,17},{17,1},{2,18},{18,2},{3,19},{19,3},{4,20},{20... | collective-permute-start | bytes 983048 | tf_op jit(solution)/shard_map/ppermute | solution.py:22
  19.6 0.1 collective-permute-start.5
  19.7 0.1 cut.1
  19.8 0.5 collective-permute-start.10
  20.3 2.2 %collective-permute-done.7.refs_6_ = bf16[32,5120]{1,0:T(8,128)(2,1)S(1)} collective-permute-done((bf16[32,5120]{1,0:T(8,128)(2,1)S(1)}, bf16[32,5120]{1,0:T(8,128)(2,1)S(1)}, u32[]{:S(2)}, u32[]{:S(2)}) %collective-permute-start.7) | collective-permute-done | bytes 327712 | tf_op jit(solution)/shard_map/ppermute | solution.py:50
  22.5 2.1 %collective-permute-start.11 = (bf16[128,1280]{1,0:T(8,128)(2,1)S(1)}, bf16[128,1280]{1,0:T(8,128)(2,1)S(1)}, u32[]{:S(2)}, u32[]{:S(2)}) collective-permute-start(bf16[128,1280]{1,0:T(8,128)(2,1)S(1)} %get-tuple-element.46), channel_id=1, source_target_pairs={{0,16},{16,0},{1,17},{17,1},{2,18},{18,2},{3,19},{19,3},{4,20},{20... | collective-permute-start | bytes 983048 | tf_op jit(solution)/shard_map/ppermute | solution.py:22
  24.6 1.3 %collective-permute-start.8 = (bf16[16,5120]{1,0:T(8,128)(2,1)S(1)}, bf16[16,5120]{1,0:T(8,128)(2,1)S(1)}, u32[]{:S(2)}, u32[]{:S(2)}) collective-permute-start(bf16[16,5120]{1,0:T(8,128)(2,1)S(1)} %slice.16), channel_id=1, source_target_pairs={{0,1},{1,0},{2,3},{3,2},{4,5},{5,4},{6,7},{7,6},{8,9},{9,8},{10,11... | collective-permute-start | bytes 491528 | tf_op jit(solution)/shard_map/ppermute | solution.py:50
  25.9 1.3 %collective-permute-start.9 = (bf16[16,5120]{1,0:T(8,128)(2,1)S(1)}, bf16[16,5120]{1,0:T(8,128)(2,1)S(1)}, u32[]{:S(2)}, u32[]{:S(2)}) collective-permute-start(bf16[16,5120]{1,0:T(8,128)(2,1)S(1)} %slice.17), channel_id=1, source_target_pairs={{0,2},{1,3},{2,0},{3,1},{4,6},{5,7},{6,4},{7,5},{8,10},{9,11},{10,... | collective-permute-start | bytes 491528 | tf_op jit(solution)/shard_map/ppermute | solution.py:50
  27.2 1.3 %collective-permute-start.24 = (bf16[128,5120]{1,0:T(8,128)(2,1)S(1)}, bf16[128,5120]{1,0:T(8,128)(2,1)S(1)}, u32[]{:S(2)}, u32[]{:S(2)}) collective-permute-start(bf16[128,5120]{1,0:T(8,128)(2,1)S(1)} %get-tuple-element.40.refs_1_), channel_id=1, source_target_pairs={{0,16},{1,17},{2,18},{3,19},{4,20},{5,21},{6,22},{7,23},{8,24},{9,... | collective-permute-start | bytes 3932168 | tf_op jit(solution)/shard_map/ppermute | solution.py:17
  28.5 0.7 collective-permute-done.8.refs_7_
  29.2 1.2 %collective-permute-done.9.refs_8_ = bf16[16,5120]{1,0:T(8,128)(2,1)S(1)} collective-permute-done((bf16[16,5120]{1,0:T(8,128)(2,1)S(1)}, bf16[16,5120]{1,0:T(8,128)(2,1)S(1)}, u32[]{:S(2)}, u32[]{:S(2)}) %collective-permute-start.9) | collective-permute-done | bytes 163872 | tf_op jit(solution)/shard_map/ppermute | solution.py:50
  30.4 1.0 %attend.1 = (bf16[128,2560]{1,0:T(8,128)(2,1)S(1)}, f32[20,128,128]{2,1,0:T(8,128)S(1)}, bf16[128,2560]{1,0:T(8,128)(2,1)S(1)}) custom-call(s32[1]{0:T(128)} %bitcast.refs_0_.section, bf16[128,1280]{1,0:T(8,128)(2,1)S(1)} %collective-permute-done.4.refs_1_, bf16[128,1280]{1,0:T(8,128)(2,1)S(1)} %collective-permute-done.5.refs_2_, ...), custom_call_target="tpu_custom_call" | custom-call | flops 167772160 | bytes 5242884 | tf_op jit(solution)/shard_map/attend/pallas_call | solution.py:142
  31.5 1.3 %collective-permute-start.12 = (bf16[128,2560]{1,0:T(8,128)(2,1)S(1)}, bf16[128,2560]{1,0:T(8,128)(2,1)S(1)}, u32[]{:S(2)}, u32[]{:S(2)}) collective-permute-start(bf16[128,2560]{1,0:T(8,128)(2,1)S(1)} %get-tuple-element.47.refs_3_), channel_id=1, source_target_pairs={{0,16},{1,17},{2,18},{3,19},{4,20},{5,21},{6,22},{7,23},{8,24},{9,... | collective-permute-start | bytes 1966088 | tf_op jit(solution)/shard_map/ppermute | solution.py:27
  32.8 0.0 copy-start.3
  32.8 0.0 slice-start
  32.8 1.3 %gradient.1 = (f32[32,5120]{1,0:T(8,128)S(1)}, f32[32,5120]{1,0:T(8,128)S(1)}, f32[32,5120]{1,0:T(8,128)S(1)}, bf16[16,5120]{1,0:T(8,128)(2,1)S(1)}, bf16[16,5120]{1,0:T(8,128)(2,1)S(1)}) custom-call(s32[1]{0:T(128)} %bitcast.refs_0_.section, bf16[128,2560]{1,0:T(8,128)(2,1)S(1)} %get-tuple-element.48.q_ref, ...), custom_call_target="tpu_custom_call" | custom-call | flops 419430400 | bytes 6881284 | tf_op jit(solution)/shard_map/gradient/pallas_call | solution.py:142
  34.1 2.2 %collective-permute-start.17 = (bf16[16,5120]{1,0:T(8,128)(2,1)S(1)}, bf16[16,5120]{1,0:T(8,128)(2,1)S(1)}, u32[]{:S(2)}, u32[]{:S(2)}) collective-permute-start(bf16[16,5120]{1,0:T(8,128)(2,1)S(1)} %get-tuple-element.57), channel_id=1, source_target_pairs={{2,0},{3,1},{0,2},{1,3},{6,4},{7,5},{4,6},{5,7},{10,8},{11,9},{8,1... | collective-permute-start | bytes 491528 | tf_op jit(solution)/shard_map/ppermute | solution.py:50
  36.3 0.3 collective-permute-start.16
  36.6 0.1 collective-permute-done.12.refs_2_
  36.6 0.6 settle.1
  37.3 2.4 %collective-permute-start.15 = (bf16[8,5120]{1,0:T(8,128)(2,1)S(1)}, bf16[8,5120]{1,0:T(8,128)(2,1)S(1)}, u32[]{:S(2)}, u32[]{:S(2)}) collective-permute-start(bf16[8,5120]{1,0:T(8,128)(2,1)S(1)} %get-tuple-element.53.refs_0_.after_any), channel_id=1, source_target_pairs={{0,12},{1,13},{2,14},{3,15},{4,8},{5,9},{6,10},{7,11},{8,4},{9,5},... | collective-permute-start | bytes 245768 | tf_op jit(solution)/shard_map/ppermute | solution.py:50
  39.7 1.2 %collective-permute-start.13 = (bf16[8,5120]{1,0:T(8,128)(2,1)S(1)}, bf16[8,5120]{1,0:T(8,128)(2,1)S(1)}, u32[]{:S(2)}, u32[]{:S(2)}) collective-permute-start(bf16[8,5120]{1,0:T(8,128)(2,1)S(1)} %get-tuple-element.53.refs_0_.after_any), channel_id=1, source_target_pairs={{0,4},{1,5},{2,6},{3,7},{4,0},{5,1},{6,2},{7,3},{8,12},{9,13},{10,... | collective-permute-start | bytes 245768 | tf_op jit(solution)/shard_map/ppermute | solution.py:50
  41.0 1.2 %collective-permute-start.21 = (bf16[32,5120]{1,0:T(8,128)(2,1)S(1)}, bf16[32,5120]{1,0:T(8,128)(2,1)S(1)}, u32[]{:S(2)}, u32[]{:S(2)}) collective-permute-start(bf16[32,5120]{1,0:T(8,128)(2,1)S(1)} %add_half.5.refs_5_), channel_id=1, source_target_pairs={{1,0},{0,1},{3,2},{2,3},{5,4},{4,5},{7,6},{6,7},{9,8},{8,9},{11,10... | collective-permute-start | bytes 983048 | tf_op jit(solution)/shard_map/ppermute | solution.py:50
  42.2 0.2 collective-permute-done.15.refs_3_
  42.5 1.2 %collective-permute-start.20 = (bf16[32,5120]{1,0:T(8,128)(2,1)S(1)}, bf16[32,5120]{1,0:T(8,128)(2,1)S(1)}, u32[]{:S(2)}, u32[]{:S(2)}) collective-permute-start(bf16[32,5120]{1,0:T(8,128)(2,1)S(1)} %add_half.4.refs_4_), channel_id=1, source_target_pairs={{2,0},{3,1},{0,2},{1,3},{6,4},{7,5},{4,6},{5,7},{10,8},{11,9},{8,1... | collective-permute-start | bytes 983048 | tf_op jit(solution)/shard_map/ppermute | solution.py:50
  43.7 3.5 %collective-permute-done.14.refs_2_ = bf16[8,5120]{1,0:T(8,128)(2,1)S(1)} collective-permute-done((bf16[8,5120]{1,0:T(8,128)(2,1)S(1)}, bf16[8,5120]{1,0:T(8,128)(2,1)S(1)}, u32[]{:S(2)}, u32[]{:S(2)}) %collective-permute-start.14) | collective-permute-done | bytes 81952 | tf_op jit(solution)/shard_map/ppermute | solution.py:50
  47.2 1.2 %collective-permute-start.19 = (bf16[32,5120]{1,0:T(8,128)(2,1)S(1)}, bf16[32,5120]{1,0:T(8,128)(2,1)S(1)}, u32[]{:S(2)}, u32[]{:S(2)}) collective-permute-start(bf16[32,5120]{1,0:T(8,128)(2,1)S(1)} %join.3.refs_3_.refs_2_), channel_id=1, source_target_pairs={{0,2},{1,3},{2,0},{3,1},{4,6},{5,7},{6,4},{7,5},{8,10},{9,11},{10,... | collective-permute-start | bytes 983048 | tf_op jit(solution)/shard_map/ppermute | solution.py:50
  48.4 0.2 collective-permute-start.18
  48.6 0.1 collective-permute-done.20.refs_1_
  48.7 0.1 add_blocks.2
  48.8 8.2 %collective-permute-done.19.refs_0_.refs_4_ = bf16[32,5120]{1,0:T(8,128)(2,1)S(1)} collective-permute-done((bf16[32,5120]{1,0:T(8,128)(2,1)S(1)}, bf16[32,5120]{1,0:T(8,128)(2,1)S(1)}, u32[]{:S(2)}, u32[]{:S(2)}) %collective-permute-start.19) | collective-permute-done | bytes 327712 | tf_op jit(solution)/shard_map/ppermute | solution.py:50
  57.0 1.2 %collective-permute-start.22 = (bf16[16,5120]{1,0:T(8,128)(2,1)S(1)}, bf16[16,5120]{1,0:T(8,128)(2,1)S(1)}, u32[]{:S(2)}, u32[]{:S(2)}) collective-permute-start(bf16[16,5120]{1,0:T(8,128)(2,1)S(1)} %get-tuple-element.59), channel_id=1, source_target_pairs={{0,1},{1,0},{2,3},{3,2},{4,5},{5,4},{6,7},{7,6},{8,9},{9,8},{10,11... | collective-permute-start | bytes 491528 | tf_op jit(solution)/shard_map/ppermute | solution.py:50
  58.2 0.2 collective-permute-start.23
  58.4 2.2 %collective-permute-start.25 = (bf16[8,5120]{1,0:T(8,128)(2,1)S(1)}, bf16[8,5120]{1,0:T(8,128)(2,1)S(1)}, u32[]{:S(2)}, u32[]{:S(2)}) collective-permute-start(bf16[8,5120]{1,0:T(8,128)(2,1)S(1)} %get-tuple-element.61), channel_id=1, source_target_pairs={{12,0},{13,1},{14,2},{15,3},{8,4},{9,5},{10,6},{11,7},{4,8},{5,9},... | collective-permute-start | bytes 245768 | tf_op jit(solution)/shard_map/ppermute | solution.py:50
  60.6 2.9 %collective-permute-done.25.refs_8_.refs_1_ = bf16[8,5120]{1,0:T(8,128)(2,1)S(1)} collective-permute-done((bf16[8,5120]{1,0:T(8,128)(2,1)S(1)}, bf16[8,5120]{1,0:T(8,128)(2,1)S(1)}, u32[]{:S(2)}, u32[]{:S(2)}) %collective-permute-start.25) | collective-permute-done | bytes 81952 | tf_op jit(solution)/shard_map/ppermute | solution.py:50
  63.5 2.0 %collective-permute-done.26.refs_9_.refs_2_ = bf16[8,5120]{1,0:T(8,128)(2,1)S(1)} collective-permute-done((bf16[8,5120]{1,0:T(8,128)(2,1)S(1)}, bf16[8,5120]{1,0:T(8,128)(2,1)S(1)}, u32[]{:S(2)}, u32[]{:S(2)}) %collective-permute-start.26) | collective-permute-done | bytes 81952 | tf_op jit(solution)/shard_map/ppermute | solution.py:50
  65.5 2.3 %expert.1 = (f32[32,5120]{1,0:T(8,128)S(1)}, f32[32,5120]{1,0:T(8,128)S(1)}, f32[32,5120]{1,0:T(8,128)S(1)}, bf16[16,5120]{1,0:T(8,128)(2,1)S(1)}, bf16[16,5120]{1,0:T(8,128)(2,1)S(1)}) custom-call(bf16[5120,640]{1,0:T(8,128)(2,1)S(1)} %bitcast.18, bf16[640,5120]{1,0:T(8,128)(2,1)S(1)} %bitcast.19, bf16[32,5120]{1,0:T(8,128)(2,1)S(1)} %join.3.refs_3_.refs_2_, ...), custom_call_target="tpu_custom_call" | custom-call | flops 1677721600 | bytes 16711680 | tf_op jit(solution)/shard_map/expert/pallas_call | solution.py:142
  67.8 2.0 %collective-permute-start.30 = (bf16[16,5120]{1,0:T(8,128)(2,1)S(1)}, bf16[16,5120]{1,0:T(8,128)(2,1)S(1)}, u32[]{:S(2)}, u32[]{:S(2)}) collective-permute-start(bf16[16,5120]{1,0:T(8,128)(2,1)S(1)} %get-tuple-element.68), channel_id=1, source_target_pairs={{2,0},{3,1},{0,2},{1,3},{6,4},{7,5},{4,6},{5,7},{10,8},{11,9},{8,1... | collective-permute-start | bytes 491528 | tf_op jit(solution)/shard_map/ppermute | solution.py:50
  69.8 3.3 %collective-permute-done.28.refs_3_ = bf16[8,5120]{1,0:T(8,128)(2,1)S(1)} collective-permute-done((bf16[8,5120]{1,0:T(8,128)(2,1)S(1)}, bf16[8,5120]{1,0:T(8,128)(2,1)S(1)}, u32[]{:S(2)}, u32[]{:S(2)}) %collective-permute-start.28) | collective-permute-done | bytes 81952 | tf_op jit(solution)/shard_map/ppermute | solution.py:50
  73.2 1.5 %collective-permute-start.31 = (bf16[32,5120]{1,0:T(8,128)(2,1)S(1)}, bf16[32,5120]{1,0:T(8,128)(2,1)S(1)}, u32[]{:S(2)}, u32[]{:S(2)}) collective-permute-start(bf16[32,5120]{1,0:T(8,128)(2,1)S(1)} %add_half.7), channel_id=1, source_target_pairs={{1,0},{0,1},{3,2},{2,3},{5,4},{4,5},{7,6},{6,7},{9,8},{8,9},{11,10... | collective-permute-start | bytes 983048 | tf_op jit(solution)/shard_map/ppermute | solution.py:50
  74.8 0.1 collective-permute-start.29
  75.0 1.3 %collective-permute-start.35 = (f32[8,5120]{1,0:T(8,128)S(1)}, f32[8,5120]{1,0:T(8,128)S(1)}, u32[]{:S(2)}, u32[]{:S(2)}) collective-permute-start(f32[8,5120]{1,0:T(8,128)S(1)} %add_last.2.refs_2_.second_ref), channel_id=1, source_target_pairs={{0,16},{1,17},{2,18},{3,19},{4,20},{5,21},{6,22},{7,23},{8,24},{9,... | collective-permute-start | bytes 491528 | tf_op jit(solution)/shard_map/ppermute | solution.py:27
  76.3 4.7 %collective-permute-done.31.refs_2_ = bf16[32,5120]{1,0:T(8,128)(2,1)S(1)} collective-permute-done((bf16[32,5120]{1,0:T(8,128)(2,1)S(1)}, bf16[32,5120]{1,0:T(8,128)(2,1)S(1)}, u32[]{:S(2)}, u32[]{:S(2)}) %collective-permute-start.31) | collective-permute-done | bytes 327712 | tf_op jit(solution)/shard_map/ppermute | solution.py:50
  81.0 0.1 collective-permute-done.29.refs_1_
  81.1 0.1 add_blocks.3
  81.2 2.3 %collective-permute-start.32 = (bf16[8,5120]{1,0:T(8,128)(2,1)S(1)}, bf16[8,5120]{1,0:T(8,128)(2,1)S(1)}, u32[]{:S(2)}, u32[]{:S(2)}) collective-permute-start(bf16[8,5120]{1,0:T(8,128)(2,1)S(1)} %get-tuple-element.71), channel_id=1, source_target_pairs={{12,0},{13,1},{14,2},{15,3},{8,4},{9,5},{10,6},{11,7},{4,8},{5,9},... | collective-permute-start | bytes 245768 | tf_op jit(solution)/shard_map/ppermute | solution.py:50
  83.5 1.3 %collective-permute-start.34 = (bf16[8,5120]{1,0:T(8,128)(2,1)S(1)}, bf16[8,5120]{1,0:T(8,128)(2,1)S(1)}, u32[]{:S(2)}, u32[]{:S(2)}) collective-permute-start(bf16[8,5120]{1,0:T(8,128)(2,1)S(1)} %get-tuple-element.73), channel_id=1, source_target_pairs={{4,0},{5,1},{6,2},{7,3},{0,4},{1,5},{2,6},{3,7},{12,8},{13,9},{14,... | collective-permute-start | bytes 245768 | tf_op jit(solution)/shard_map/ppermute | solution.py:50
  84.8 0.8 lay_out.1
  85.6 0.8 collective-permute-done.32.refs_1_
  86.4 1.7 %collective-permute-done.33.refs_2_ = bf16[8,5120]{1,0:T(8,128)(2,1)S(1)} collective-permute-done((bf16[8,5120]{1,0:T(8,128)(2,1)S(1)}, bf16[8,5120]{1,0:T(8,128)(2,1)S(1)}, u32[]{:S(2)}, u32[]{:S(2)}) %collective-permute-start.33) | collective-permute-done | bytes 81952 | tf_op jit(solution)/shard_map/ppermute | solution.py:50
  88.2 1.3 %collective-permute-start.36 = (f32[8,5248]{1,0:T(8,128)S(1)}, f32[8,5248]{1,0:T(8,128)S(1)}, u32[]{:S(2)}, u32[]{:S(2)}) collective-permute-start(f32[8,5248]{1,0:T(8,128)S(1)} %add_last.3.back_ref), channel_id=1, source_target_pairs={{0,16},{1,17},{2,18},{3,19},{4,20},{5,21},{6,22},{7,23},{8,24},{9,... | collective-permute-start | bytes 503816 | tf_op jit(solution)/shard_map/ppermute | solution.py:17
  89.5 1.5 %finish.2 = bf16[128,5120]{1,0:T(8,128)(2,1)} custom-call(s32[1]{0:T(128)} %bitcast.refs_0_.section, bf16[128,5120]{1,0:T(8,128)(2,1)S(1)} %get-tuple-element.52.res_ref, f32[8,5248]{1,0:T(8,128)S(1)} %add_last.3.back_ref), custom_call_target="tpu_custom_call" | custom-call | flops 32768000 | bytes 3276800 | tf_op jit(solution)/shard_map/finish/pallas_call | solution.py:541
  91.0 7.9 %collective-permute-done.36.back_ref = f32[8,5248]{1,0:T(8,128)S(1)} collective-permute-done((f32[8,5248]{1,0:T(8,128)S(1)}, f32[8,5248]{1,0:T(8,128)S(1)}, u32[]{:S(2)}, u32[]{:S(2)}) %collective-permute-start.36) | collective-permute-done | bytes 167968 | tf_op jit(solution)/shard_map/ppermute | solution.py:17
  98.9 1.5 %finish.3 = bf16[128,5120]{1,0:T(8,128)(2,1)} custom-call(s32[1]{0:T(128)} %bitcast.refs_0_.section, bf16[128,5120]{1,0:T(8,128)(2,1)S(1)} %collective-permute-done.24.refs_7_.res_ref, f32[8,5248]{1,0:T(8,128)S(1)} %collective-permute-done.36.back_ref, bf16[128,5120]{1,0:T(8,128)(2,1)} %get-tuple-element.75.refs_0_), custom_call_target="tpu_custom_call", output_to_operand_aliasing={{}: (3, {})} | custom-call | flops 32768000 | bytes 3276800 | tf_op jit(solution)/shard_map/finish/pallas_call | solution.py:541
  (56 shorter events, 0.5 us)
Async XLA Ops:
  0.6 16.3 %copy-start.5 = (f32[1,128]{1,0:T(1,128)S(1)}, f32[1,128]{1,0:T(1,128)}, u32[]{:S(2)}) copy-start(f32[1,128]{1,0:T(1,128)} %refs_2_.1) | copy-start | bytes 1540
  0.6 16.3 %copy-start.6 = (s32[1,128]{1,0:T(1,128)S(1)}, s32[1,128]{1,0:T(1,128)}, u32[]{:S(2)}) copy-start(s32[1,128]{1,0:T(1,128)} %refs_3_.1) | copy-start | bytes 1540
  0.7 16.3 %copy-start.4 = (f32[1,5120]{1,0:T(1,128)S(1)}, f32[1,5120]{1,0:T(1,128)}, u32[]{:S(2)}) copy-start(f32[1,5120]{1,0:T(1,128)} %refs_1_.1) | copy-start | bytes 61444
  0.7 16.3 %copy-start.1 = (bf16[1,128,5120]{2,1,0:T(8,128)(2,1)S(1)}, bf16[1,128,5120]{2,1,0:T(8,128)(2,1)}, u32[]{:S(2)}) copy-start(bf16[1,128,5120]{2,1,0:T(8,128)(2,1)} %param.9) | copy-start | bytes 3932164
  1.8 1.3 %collective-permute-start = (bf16[8,5120]{1,0:T(8,128)(2,1)S(1)}, bf16[8,5120]{1,0:T(8,128)(2,1)S(1)}, u32[]{:S(2)}, u32[]{:S(2)}) collective-permute-start(bf16[8,5120]{1,0:T(8,128)(2,1)S(1)} %bitcast.25), channel_id=1, source_target_pairs={{0,16},{16,0},{1,17},{17,1},{2,18},{18,2},{3,19},{19,3},{4,20},{20... | collective-permute-start | bytes 245768 | tf_op jit(solution)/shard_map/ppermute | solution.py:22
  2.0 17.7 %copy-start.2 = (bf16[1,128,5120]{2,1,0:T(8,128)(2,1)S(1)}, bf16[1,128,5120]{2,1,0:T(8,128)(2,1)}, u32[]{:S(2)}) copy-start(bf16[1,128,5120]{2,1,0:T(8,128)(2,1)} %param.11) | copy-start | bytes 3932164
  3.2 7.1 %collective-permute-start.3 = (bf16[8,5120]{1,0:T(8,128)(2,1)S(1)}, bf16[8,5120]{1,0:T(8,128)(2,1)S(1)}, u32[]{:S(2)}, u32[]{:S(2)}) collective-permute-start(bf16[8,5120]{1,0:T(8,128)(2,1)S(1)} %broadcast_select_fusion.refs_0_), channel_id=1, source_target_pairs={{0,12},{1,13},{2,14},{3,15},{4,8},{5,9},{6,10},{7,11},{8,4},{9,5},... | collective-permute-start | bytes 245768 | tf_op jit(solution)/shard_map/ppermute | solution.py:50
  7.7 6.6 %collective-permute-start.2 = (bf16[8,5120]{1,0:T(8,128)(2,1)S(1)}, bf16[8,5120]{1,0:T(8,128)(2,1)S(1)}, u32[]{:S(2)}, u32[]{:S(2)}) collective-permute-start(bf16[8,5120]{1,0:T(8,128)(2,1)S(1)} %broadcast_select_fusion.refs_0_), channel_id=1, source_target_pairs={{0,8},{1,9},{2,10},{3,11},{4,12},{5,13},{6,14},{7,15},{8,0},{9,1},... | collective-permute-start | bytes 245768 | tf_op jit(solution)/shard_map/ppermute | solution.py:50
  7.7 6.6 %collective-permute-start.1 = (bf16[8,5120]{1,0:T(8,128)(2,1)S(1)}, bf16[8,5120]{1,0:T(8,128)(2,1)S(1)}, u32[]{:S(2)}, u32[]{:S(2)}) collective-permute-start(bf16[8,5120]{1,0:T(8,128)(2,1)S(1)} %broadcast_select_fusion.refs_0_), channel_id=1, source_target_pairs={{0,4},{1,5},{2,6},{3,7},{4,0},{5,1},{6,2},{7,3},{8,12},{9,13},{10,... | collective-permute-start | bytes 245768 | tf_op jit(solution)/shard_map/ppermute | solution.py:50
  14.4 8.1 %collective-permute-start.7 = (bf16[32,5120]{1,0:T(8,128)(2,1)S(1)}, bf16[32,5120]{1,0:T(8,128)(2,1)S(1)}, u32[]{:S(2)}, u32[]{:S(2)}) collective-permute-start(bf16[32,5120]{1,0:T(8,128)(2,1)S(1)} %join.2.refs_4_), channel_id=1, source_target_pairs={{0,2},{1,3},{2,0},{3,1},{4,6},{5,7},{6,4},{7,5},{8,10},{9,11},{10,... | collective-permute-start | bytes 983048 | tf_op jit(solution)/shard_map/ppermute | solution.py:50
  15.7 8.9 %collective-permute-start.6 = (bf16[32,5120]{1,0:T(8,128)(2,1)S(1)}, bf16[32,5120]{1,0:T(8,128)(2,1)S(1)}, u32[]{:S(2)}, u32[]{:S(2)}) collective-permute-start(bf16[32,5120]{1,0:T(8,128)(2,1)S(1)} %join.2.refs_4_), channel_id=1, source_target_pairs={{0,1},{1,0},{2,3},{3,2},{4,5},{5,4},{6,7},{7,6},{8,9},{9,8},{10,11... | collective-permute-start | bytes 983048 | tf_op jit(solution)/shard_map/ppermute | solution.py:50
  17.8 8.1 %collective-permute-start.4 = (bf16[128,1280]{1,0:T(8,128)(2,1)S(1)}, bf16[128,1280]{1,0:T(8,128)(2,1)S(1)}, u32[]{:S(2)}, u32[]{:S(2)}) collective-permute-start(bf16[128,1280]{1,0:T(8,128)(2,1)S(1)} %get-tuple-element.41), channel_id=1, source_target_pairs={{0,16},{16,0},{1,17},{17,1},{2,18},{18,2},{3,19},{19,3},{4,20},{20... | collective-permute-start | bytes 983048 | tf_op jit(solution)/shard_map/ppermute | solution.py:22
  19.6 7.6 %collective-permute-start.5 = (bf16[128,1280]{1,0:T(8,128)(2,1)S(1)}, bf16[128,1280]{1,0:T(8,128)(2,1)S(1)}, u32[]{:S(2)}, u32[]{:S(2)}) collective-permute-start(bf16[128,1280]{1,0:T(8,128)(2,1)S(1)} %get-tuple-element.42), channel_id=1, source_target_pairs={{0,16},{16,0},{1,17},{17,1},{2,18},{18,2},{3,19},{19,3},{4,20},{20... | collective-permute-start | bytes 983048 | tf_op jit(solution)/shard_map/ppermute | solution.py:22
  19.8 8.7 %collective-permute-start.10 = (bf16[128,1280]{1,0:T(8,128)(2,1)S(1)}, bf16[128,1280]{1,0:T(8,128)(2,1)S(1)}, u32[]{:S(2)}, u32[]{:S(2)}) collective-permute-start(bf16[128,1280]{1,0:T(8,128)(2,1)S(1)} %get-tuple-element.45), channel_id=1, source_target_pairs={{0,16},{16,0},{1,17},{17,1},{2,18},{18,2},{3,19},{19,3},{4,20},{20... | collective-permute-start | bytes 983048 | tf_op jit(solution)/shard_map/ppermute | solution.py:22
  22.5 6.0 %collective-permute-start.11 = (bf16[128,1280]{1,0:T(8,128)(2,1)S(1)}, bf16[128,1280]{1,0:T(8,128)(2,1)S(1)}, u32[]{:S(2)}, u32[]{:S(2)}) collective-permute-start(bf16[128,1280]{1,0:T(8,128)(2,1)S(1)} %get-tuple-element.46), channel_id=1, source_target_pairs={{0,16},{16,0},{1,17},{17,1},{2,18},{18,2},{3,19},{19,3},{4,20},{20... | collective-permute-start | bytes 983048 | tf_op jit(solution)/shard_map/ppermute | solution.py:22
  24.6 4.6 %collective-permute-start.8 = (bf16[16,5120]{1,0:T(8,128)(2,1)S(1)}, bf16[16,5120]{1,0:T(8,128)(2,1)S(1)}, u32[]{:S(2)}, u32[]{:S(2)}) collective-permute-start(bf16[16,5120]{1,0:T(8,128)(2,1)S(1)} %slice.16), channel_id=1, source_target_pairs={{0,1},{1,0},{2,3},{3,2},{4,5},{5,4},{6,7},{7,6},{8,9},{9,8},{10,11... | collective-permute-start | bytes 491528 | tf_op jit(solution)/shard_map/ppermute | solution.py:50
  25.9 4.5 %collective-permute-start.9 = (bf16[16,5120]{1,0:T(8,128)(2,1)S(1)}, bf16[16,5120]{1,0:T(8,128)(2,1)S(1)}, u32[]{:S(2)}, u32[]{:S(2)}) collective-permute-start(bf16[16,5120]{1,0:T(8,128)(2,1)S(1)} %slice.17), channel_id=1, source_target_pairs={{0,2},{1,3},{2,0},{3,1},{4,6},{5,7},{6,4},{7,5},{8,10},{9,11},{10,... | collective-permute-start | bytes 491528 | tf_op jit(solution)/shard_map/ppermute | solution.py:50
  27.2 33.4 %collective-permute-start.24 = (bf16[128,5120]{1,0:T(8,128)(2,1)S(1)}, bf16[128,5120]{1,0:T(8,128)(2,1)S(1)}, u32[]{:S(2)}, u32[]{:S(2)}) collective-permute-start(bf16[128,5120]{1,0:T(8,128)(2,1)S(1)} %get-tuple-element.40.refs_1_), channel_id=1, source_target_pairs={{0,16},{1,17},{2,18},{3,19},{4,20},{5,21},{6,22},{7,23},{8,24},{9,... | collective-permute-start | bytes 3932168 | tf_op jit(solution)/shard_map/ppermute | solution.py:17
  31.5 5.1 %collective-permute-start.12 = (bf16[128,2560]{1,0:T(8,128)(2,1)S(1)}, bf16[128,2560]{1,0:T(8,128)(2,1)S(1)}, u32[]{:S(2)}, u32[]{:S(2)}) collective-permute-start(bf16[128,2560]{1,0:T(8,128)(2,1)S(1)} %get-tuple-element.47.refs_3_), channel_id=1, source_target_pairs={{0,16},{1,17},{2,18},{3,19},{4,20},{5,21},{6,22},{7,23},{8,24},{9,... | collective-permute-start | bytes 1966088 | tf_op jit(solution)/shard_map/ppermute | solution.py:27
  32.8 3.9 %copy-start.3 = (f32[1,5120]{1,0:T(1,128)S(1)}, f32[1,5120]{1,0:T(1,128)}, u32[]{:S(2)}) copy-start(f32[1,5120]{1,0:T(1,128)} %refs_4_.1) | copy-start | bytes 61444
  32.8 32.7 %slice-start = ((s8[6553600]{0:T(1024)(128)(4,1)}), s8[4194304]{0:T(1024)(128)(4,1)S(1)}, s32[]{:S(2)}) async-start(s8[6553600]{0:T(1024)(128)(4,1)} %bitcast.16), calls=%async_computation | async-start | bytes 8388608
  34.1 5.5 %collective-permute-start.17 = (bf16[16,5120]{1,0:T(8,128)(2,1)S(1)}, bf16[16,5120]{1,0:T(8,128)(2,1)S(1)}, u32[]{:S(2)}, u32[]{:S(2)}) collective-permute-start(bf16[16,5120]{1,0:T(8,128)(2,1)S(1)} %get-tuple-element.57), channel_id=1, source_target_pairs={{2,0},{3,1},{0,2},{1,3},{6,4},{7,5},{4,6},{5,7},{10,8},{11,9},{8,1... | collective-permute-start | bytes 491528 | tf_op jit(solution)/shard_map/ppermute | solution.py:50
  36.3 4.6 %collective-permute-start.16 = (bf16[16,5120]{1,0:T(8,128)(2,1)S(1)}, bf16[16,5120]{1,0:T(8,128)(2,1)S(1)}, u32[]{:S(2)}, u32[]{:S(2)}) collective-permute-start(bf16[16,5120]{1,0:T(8,128)(2,1)S(1)} %get-tuple-element.55), channel_id=1, source_target_pairs={{1,0},{0,1},{3,2},{2,3},{5,4},{4,5},{7,6},{6,7},{9,8},{8,9},{11,10... | collective-permute-start | bytes 491528 | tf_op jit(solution)/shard_map/ppermute | solution.py:50
  36.6 28.9 %slice-start.1 = ((s8[6553600]{0:T(1024)(128)(4,1)}), s8[2359296]{0:T(1024)(128)(4,1)S(1)}, s32[]{:S(2)}) async-start(s8[6553600]{0:T(1024)(128)(4,1)} %bitcast.16), calls=%async_computation.1 | async-start | bytes 4718592
  36.6 28.9 %copy-start = (bf16[1,640,5120]{2,1,0:T(8,128)(2,1)S(1)}, bf16[1,640,5120]{2,1,0:T(8,128)(2,1)}, u32[]{:S(2)}) copy-start(bf16[1,640,5120]{2,1,0:T(8,128)(2,1)} %param.15) | copy-start | bytes 19660804
  37.3 5.2 %collective-permute-start.15 = (bf16[8,5120]{1,0:T(8,128)(2,1)S(1)}, bf16[8,5120]{1,0:T(8,128)(2,1)S(1)}, u32[]{:S(2)}, u32[]{:S(2)}) collective-permute-start(bf16[8,5120]{1,0:T(8,128)(2,1)S(1)} %get-tuple-element.53.refs_0_.after_any), channel_id=1, source_target_pairs={{0,12},{1,13},{2,14},{3,15},{4,8},{5,9},{6,10},{7,11},{8,4},{9,5},... | collective-permute-start | bytes 245768 | tf_op jit(solution)/shard_map/ppermute | solution.py:50
  39.7 7.5 %collective-permute-start.14 = (bf16[8,5120]{1,0:T(8,128)(2,1)S(1)}, bf16[8,5120]{1,0:T(8,128)(2,1)S(1)}, u32[]{:S(2)}, u32[]{:S(2)}) collective-permute-start(bf16[8,5120]{1,0:T(8,128)(2,1)S(1)} %get-tuple-element.53.refs_0_.after_any), channel_id=1, source_target_pairs={{0,8},{1,9},{2,10},{3,11},{4,12},{5,13},{6,14},{7,15},{8,0},{9,1},... | collective-permute-start | bytes 245768 | tf_op jit(solution)/shard_map/ppermute | solution.py:50
  39.7 7.5 %collective-permute-start.13 = (bf16[8,5120]{1,0:T(8,128)(2,1)S(1)}, bf16[8,5120]{1,0:T(8,128)(2,1)S(1)}, u32[]{:S(2)}, u32[]{:S(2)}) collective-permute-start(bf16[8,5120]{1,0:T(8,128)(2,1)S(1)} %get-tuple-element.53.refs_0_.after_any), channel_id=1, source_target_pairs={{0,4},{1,5},{2,6},{3,7},{4,0},{5,1},{6,2},{7,3},{8,12},{9,13},{10,... | collective-permute-start | bytes 245768 | tf_op jit(solution)/shard_map/ppermute | solution.py:50
  41.0 7.7 %collective-permute-start.21 = (bf16[32,5120]{1,0:T(8,128)(2,1)S(1)}, bf16[32,5120]{1,0:T(8,128)(2,1)S(1)}, u32[]{:S(2)}, u32[]{:S(2)}) collective-permute-start(bf16[32,5120]{1,0:T(8,128)(2,1)S(1)} %add_half.5.refs_5_), channel_id=1, source_target_pairs={{1,0},{0,1},{3,2},{2,3},{5,4},{4,5},{7,6},{6,7},{9,8},{8,9},{11,10... | collective-permute-start | bytes 983048 | tf_op jit(solution)/shard_map/ppermute | solution.py:50
  42.5 6.2 %collective-permute-start.20 = (bf16[32,5120]{1,0:T(8,128)(2,1)S(1)}, bf16[32,5120]{1,0:T(8,128)(2,1)S(1)}, u32[]{:S(2)}, u32[]{:S(2)}) collective-permute-start(bf16[32,5120]{1,0:T(8,128)(2,1)S(1)} %add_half.4.refs_4_), channel_id=1, source_target_pairs={{2,0},{3,1},{0,2},{1,3},{6,4},{7,5},{4,6},{5,7},{10,8},{11,9},{8,1... | collective-permute-start | bytes 983048 | tf_op jit(solution)/shard_map/ppermute | solution.py:50
  47.2 9.8 %collective-permute-start.19 = (bf16[32,5120]{1,0:T(8,128)(2,1)S(1)}, bf16[32,5120]{1,0:T(8,128)(2,1)S(1)}, u32[]{:S(2)}, u32[]{:S(2)}) collective-permute-start(bf16[32,5120]{1,0:T(8,128)(2,1)S(1)} %join.3.refs_3_.refs_2_), channel_id=1, source_target_pairs={{0,2},{1,3},{2,0},{3,1},{4,6},{5,7},{6,4},{7,5},{8,10},{9,11},{10,... | collective-permute-start | bytes 983048 | tf_op jit(solution)/shard_map/ppermute | solution.py:50
  48.4 8.6 %collective-permute-start.18 = (bf16[32,5120]{1,0:T(8,128)(2,1)S(1)}, bf16[32,5120]{1,0:T(8,128)(2,1)S(1)}, u32[]{:S(2)}, u32[]{:S(2)}) collective-permute-start(bf16[32,5120]{1,0:T(8,128)(2,1)S(1)} %join.3.refs_3_.refs_2_), channel_id=1, source_target_pairs={{0,1},{1,0},{2,3},{3,2},{4,5},{5,4},{6,7},{7,6},{8,9},{9,8},{10,11... | collective-permute-start | bytes 983048 | tf_op jit(solution)/shard_map/ppermute | solution.py:50
  57.0 8.5 %collective-permute-start.22 = (bf16[16,5120]{1,0:T(8,128)(2,1)S(1)}, bf16[16,5120]{1,0:T(8,128)(2,1)S(1)}, u32[]{:S(2)}, u32[]{:S(2)}) collective-permute-start(bf16[16,5120]{1,0:T(8,128)(2,1)S(1)} %get-tuple-element.59), channel_id=1, source_target_pairs={{0,1},{1,0},{2,3},{3,2},{4,5},{5,4},{6,7},{7,6},{8,9},{9,8},{10,11... | collective-permute-start | bytes 491528 | tf_op jit(solution)/shard_map/ppermute | solution.py:50
  58.2 7.3 %collective-permute-start.23 = (bf16[16,5120]{1,0:T(8,128)(2,1)S(1)}, bf16[16,5120]{1,0:T(8,128)(2,1)S(1)}, u32[]{:S(2)}, u32[]{:S(2)}) collective-permute-start(bf16[16,5120]{1,0:T(8,128)(2,1)S(1)} %get-tuple-element.60), channel_id=1, source_target_pairs={{0,2},{1,3},{2,0},{3,1},{4,6},{5,7},{6,4},{7,5},{8,10},{9,11},{10,... | collective-permute-start | bytes 491528 | tf_op jit(solution)/shard_map/ppermute | solution.py:50
  58.4 5.1 %collective-permute-start.25 = (bf16[8,5120]{1,0:T(8,128)(2,1)S(1)}, bf16[8,5120]{1,0:T(8,128)(2,1)S(1)}, u32[]{:S(2)}, u32[]{:S(2)}) collective-permute-start(bf16[8,5120]{1,0:T(8,128)(2,1)S(1)} %get-tuple-element.61), channel_id=1, source_target_pairs={{12,0},{13,1},{14,2},{15,3},{8,4},{9,5},{10,6},{11,7},{4,8},{5,9},... | collective-permute-start | bytes 245768 | tf_op jit(solution)/shard_map/ppermute | solution.py:50
  60.6 4.9 %collective-permute-start.26 = (bf16[8,5120]{1,0:T(8,128)(2,1)S(1)}, bf16[8,5120]{1,0:T(8,128)(2,1)S(1)}, u32[]{:S(2)}, u32[]{:S(2)}) collective-permute-start(bf16[8,5120]{1,0:T(8,128)(2,1)S(1)} %get-tuple-element.62), channel_id=1, source_target_pairs={{8,0},{9,1},{10,2},{11,3},{12,4},{13,5},{14,6},{15,7},{0,8},{1,9},... | collective-permute-start | bytes 245768 | tf_op jit(solution)/shard_map/ppermute | solution.py:50
  67.8 5.3 %collective-permute-start.30 = (bf16[16,5120]{1,0:T(8,128)(2,1)S(1)}, bf16[16,5120]{1,0:T(8,128)(2,1)S(1)}, u32[]{:S(2)}, u32[]{:S(2)}) collective-permute-start(bf16[16,5120]{1,0:T(8,128)(2,1)S(1)} %get-tuple-element.68), channel_id=1, source_target_pairs={{2,0},{3,1},{0,2},{1,3},{6,4},{7,5},{4,6},{5,7},{10,8},{11,9},{8,1... | collective-permute-start | bytes 491528 | tf_op jit(solution)/shard_map/ppermute | solution.py:50
  69.8 4.9 %collective-permute-start.27 = (bf16[16,5120]{1,0:T(8,128)(2,1)S(1)}, bf16[16,5120]{1,0:T(8,128)(2,1)S(1)}, u32[]{:S(2)}, u32[]{:S(2)}) collective-permute-start(bf16[16,5120]{1,0:T(8,128)(2,1)S(1)} %get-tuple-element.65), channel_id=1, source_target_pairs={{1,0},{0,1},{3,2},{2,3},{5,4},{4,5},{7,6},{6,7},{9,8},{8,9},{11,10... | collective-permute-start | bytes 491528 | tf_op jit(solution)/shard_map/ppermute | solution.py:50
  69.8 3.3 %collective-permute-start.28 = (bf16[8,5120]{1,0:T(8,128)(2,1)S(1)}, bf16[8,5120]{1,0:T(8,128)(2,1)S(1)}, u32[]{:S(2)}, u32[]{:S(2)}) collective-permute-start(bf16[8,5120]{1,0:T(8,128)(2,1)S(1)} %get-tuple-element.66), channel_id=1, source_target_pairs={{4,0},{5,1},{6,2},{7,3},{0,4},{1,5},{2,6},{3,7},{12,8},{13,9},{14,... | collective-permute-start | bytes 245768 | tf_op jit(solution)/shard_map/ppermute | solution.py:50
  73.2 7.7 %collective-permute-start.31 = (bf16[32,5120]{1,0:T(8,128)(2,1)S(1)}, bf16[32,5120]{1,0:T(8,128)(2,1)S(1)}, u32[]{:S(2)}, u32[]{:S(2)}) collective-permute-start(bf16[32,5120]{1,0:T(8,128)(2,1)S(1)} %add_half.7), channel_id=1, source_target_pairs={{1,0},{0,1},{3,2},{2,3},{5,4},{4,5},{7,6},{6,7},{9,8},{8,9},{11,10... | collective-permute-start | bytes 983048 | tf_op jit(solution)/shard_map/ppermute | solution.py:50
  74.8 6.3 %collective-permute-start.29 = (bf16[32,5120]{1,0:T(8,128)(2,1)S(1)}, bf16[32,5120]{1,0:T(8,128)(2,1)S(1)}, u32[]{:S(2)}, u32[]{:S(2)}) collective-permute-start(bf16[32,5120]{1,0:T(8,128)(2,1)S(1)} %add_half.6), channel_id=1, source_target_pairs={{2,0},{3,1},{0,2},{1,3},{6,4},{7,5},{4,6},{5,7},{10,8},{11,9},{8,1... | collective-permute-start | bytes 983048 | tf_op jit(solution)/shard_map/ppermute | solution.py:50
  75.0 9.9 %collective-permute-start.35 = (f32[8,5120]{1,0:T(8,128)S(1)}, f32[8,5120]{1,0:T(8,128)S(1)}, u32[]{:S(2)}, u32[]{:S(2)}) collective-permute-start(f32[8,5120]{1,0:T(8,128)S(1)} %add_last.2.refs_2_.second_ref), channel_id=1, source_target_pairs={{0,16},{1,17},{2,18},{3,19},{4,20},{5,21},{6,22},{7,23},{8,24},{9,... | collective-permute-start | bytes 491528 | tf_op jit(solution)/shard_map/ppermute | solution.py:27
  81.2 5.2 %collective-permute-start.32 = (bf16[8,5120]{1,0:T(8,128)(2,1)S(1)}, bf16[8,5120]{1,0:T(8,128)(2,1)S(1)}, u32[]{:S(2)}, u32[]{:S(2)}) collective-permute-start(bf16[8,5120]{1,0:T(8,128)(2,1)S(1)} %get-tuple-element.71), channel_id=1, source_target_pairs={{12,0},{13,1},{14,2},{15,3},{8,4},{9,5},{10,6},{11,7},{4,8},{5,9},... | collective-permute-start | bytes 245768 | tf_op jit(solution)/shard_map/ppermute | solution.py:50
  83.5 4.6 %collective-permute-start.33 = (bf16[8,5120]{1,0:T(8,128)(2,1)S(1)}, bf16[8,5120]{1,0:T(8,128)(2,1)S(1)}, u32[]{:S(2)}, u32[]{:S(2)}) collective-permute-start(bf16[8,5120]{1,0:T(8,128)(2,1)S(1)} %get-tuple-element.72), channel_id=1, source_target_pairs={{8,0},{9,1},{10,2},{11,3},{12,4},{13,5},{14,6},{15,7},{0,8},{1,9},... | collective-permute-start | bytes 245768 | tf_op jit(solution)/shard_map/ppermute | solution.py:50
  83.5 4.6 %collective-permute-start.34 = (bf16[8,5120]{1,0:T(8,128)(2,1)S(1)}, bf16[8,5120]{1,0:T(8,128)(2,1)S(1)}, u32[]{:S(2)}, u32[]{:S(2)}) collective-permute-start(bf16[8,5120]{1,0:T(8,128)(2,1)S(1)} %get-tuple-element.73), channel_id=1, source_target_pairs={{4,0},{5,1},{6,2},{7,3},{0,4},{1,5},{2,6},{3,7},{12,8},{13,9},{14,... | collective-permute-start | bytes 245768 | tf_op jit(solution)/shard_map/ppermute | solution.py:50
  88.2 10.7 %collective-permute-start.36 = (f32[8,5248]{1,0:T(8,128)S(1)}, f32[8,5248]{1,0:T(8,128)S(1)}, u32[]{:S(2)}, u32[]{:S(2)}) collective-permute-start(f32[8,5248]{1,0:T(8,128)S(1)} %add_last.3.back_ref), channel_id=1, source_target_pairs={{0,16},{1,17},{2,18},{3,19},{4,20},{5,21},{6,22},{7,23},{8,24},{9,... | collective-permute-start | bytes 503816 | tf_op jit(solution)/shard_map/ppermute | solution.py:17

commit v13 on v12

--- a/solution.py
+++ b/solution.py
@@ -102,7 +102,8 @@
         arrived = [self.shift(piece, by, back=True) for piece, (*_, by) in zip(halves, arrived)]
         after = yield halves
         blocks = add_blocks(held[0, 0][0], arrived, rows, after)
-        more = [self.shift(blocks[s], (s, 0, 0), back=True) for s in reversed(range(1, na))]
+        order = range(1, na) if extra is None else reversed(range(1, na))
+        more = [self.shift(blocks[s], (s, 0, 0), back=True) for s in order]
         after = yield blocks, more
         yield add_last(blocks[0], more, after, extra)
 

time: 101 us -> 99.7 us (0.987)
  waiting for transfers between devices: 47 us -> 44.3 us
  starting transfers between devices: 40.5 us -> 42.3 us
    ppermute x28, waiting for transfers between devices: 37.9 us -> 34 us  [shift(): return lax.ppermute(block, 'expert', route)]
    ppermute x28, starting transfers between devices: 30.8 us -> 32.5 us  [shift(): return lax.ppermute(block, 'expert', route)]
where the time goes in v13:
time: 99.7 us; the launch traced here: 99.5 us
  waiting for transfers between devices  44.3 us (44%)
  starting transfers between devices  42.3 us (42%)
  Pallas kernels  10.6 us (11%)
  local copies, waits for them, and re-layouts  1.24 us (1%)
    ppermute x28, waiting for transfers between devices, shift(): return lax.ppermute(block, 'expert', route)  34 us
    ppermute x28, starting transfers between devices, shift(): return lax.ppermute(block, 'expert', route)  32.5 us
    ppermute x2, waiting for transfers between devices, passed_along(): return lax.ppermute(block, axis, route)  8.43 us
    pallas_call x18, Pallas kernels, local_kernel(): pl.pallas_call(body, out_shape=tuple(outs), in_specs=in_specs, out_specs=...  7.62 us
    ppermute x5, starting transfers between devices, swapped(): lax.ppermute(block, 'section', [(i, (i + sections // 2) % sections) for i...  4.61 us
    pallas_call x2, Pallas kernels, finish(): pl.pallas_call(kernel, out_shape=one, in_specs=[pl.BlockSpec(memory_space...  2.99 us
    ppermute x2, starting transfers between devices, passed_along(): return lax.ppermute(block, axis, route)  2.57 us
    ppermute x2, starting transfers between devices, to_decoder(): lax.ppermute(block, 'section', [(i, i + apart) for i in range(apart)])  2.57 us
  transfers between devices with their start and end apart: 37, of which 19 were waited for; matrix products, arithmetic and copies ran while one was open for 0% of the time, Pallas kernels for 7%

profile of v13, /device:TPU:1, one launch (start us, length us, event | category | flops | bytes accessed | tf_op | source)
XLA Modules:
  0.0 99.5 jit_solution(10065098829322154641)
XLA Ops:
  0.7 1.1 %slice_bitcast_fusion = (bf16[1,8,2,2560]{3,2,1,0:T(2,128)(2,1)S(1)}, bf16[1,8,2,2560]{3,2,1,0:T(2,128)(2,1)S(1)}) fusion(bf16[1,8,2,5120]{3,2,1,0:T(2,128)(2,1)} %param.10), kind=kLoop, calls=%fused_computation | loop fusion | bytes 327680
  1.8 0.1 collective-permute-start
  2.0 1.2 %collective-permute-done = bf16[8,5120]{1,0:T(8,128)(2,1)S(1)} collective-permute-done((bf16[8,5120]{1,0:T(8,128)(2,1)S(1)}, bf16[8,5120]{1,0:T(8,128)(2,1)S(1)}, u32[]{:S(2)}, u32[]{:S(2)}) %collective-permute-start) | collective-permute-done | bytes 81952 | tf_op jit(solution)/shard_map/ppermute | solution.py:22
  3.2 4.5 %collective-permute-start.3 = (bf16[8,5120]{1,0:T(8,128)(2,1)S(1)}, bf16[8,5120]{1,0:T(8,128)(2,1)S(1)}, u32[]{:S(2)}, u32[]{:S(2)}) collective-permute-start(bf16[8,5120]{1,0:T(8,128)(2,1)S(1)} %broadcast_select_fusion.refs_0_), channel_id=1, source_target_pairs={{0,12},{1,13},{2,14},{3,15},{4,8},{5,9},{6,10},{7,11},{8,4},{9,5},... | collective-permute-start | bytes 245768 | tf_op jit(solution)/shard_map/ppermute | solution.py:50
  7.7 0.4 collective-permute-start.1
  8.1 2.2 %collective-permute-done.3.refs_3_ = bf16[8,5120]{1,0:T(8,128)(2,1)S(1)} collective-permute-done((bf16[8,5120]{1,0:T(8,128)(2,1)S(1)}, bf16[8,5120]{1,0:T(8,128)(2,1)S(1)}, u32[]{:S(2)}, u32[]{:S(2)}) %collective-permute-start.3) | collective-permute-done | bytes 81952 | tf_op jit(solution)/shard_map/ppermute | solution.py:50
  10.3 4.1 %collective-permute-done.2.refs_2_ = bf16[8,5120]{1,0:T(8,128)(2,1)S(1)} collective-permute-done((bf16[8,5120]{1,0:T(8,128)(2,1)S(1)}, bf16[8,5120]{1,0:T(8,128)(2,1)S(1)}, u32[]{:S(2)}, u32[]{:S(2)}) %collective-permute-start.2) | collective-permute-done | bytes 81952 | tf_op jit(solution)/shard_map/ppermute | solution.py:50
  14.4 1.3 %collective-permute-start.7 = (bf16[32,5120]{1,0:T(8,128)(2,1)S(1)}, bf16[32,5120]{1,0:T(8,128)(2,1)S(1)}, u32[]{:S(2)}, u32[]{:S(2)}) collective-permute-start(bf16[32,5120]{1,0:T(8,128)(2,1)S(1)} %join.2.refs_4_), channel_id=1, source_target_pairs={{0,2},{1,3},{2,0},{3,1},{4,6},{5,7},{6,4},{7,5},{8,10},{9,11},{10,... | collective-permute-start | bytes 983048 | tf_op jit(solution)/shard_map/ppermute | solution.py:50
  15.7 1.2 %collective-permute-start.6 = (bf16[32,5120]{1,0:T(8,128)(2,1)S(1)}, bf16[32,5120]{1,0:T(8,128)(2,1)S(1)}, u32[]{:S(2)}, u32[]{:S(2)}) collective-permute-start(bf16[32,5120]{1,0:T(8,128)(2,1)S(1)} %join.2.refs_4_), channel_id=1, source_target_pairs={{0,1},{1,0},{2,3},{3,2},{4,5},{5,4},{6,7},{7,6},{8,9},{9,8},{10,11... | collective-permute-start | bytes 983048 | tf_op jit(solution)/shard_map/ppermute | solution.py:50
  16.9 0.9 queries.1
  17.8 1.8 %collective-permute-start.4 = (bf16[128,1280]{1,0:T(8,128)(2,1)S(1)}, bf16[128,1280]{1,0:T(8,128)(2,1)S(1)}, u32[]{:S(2)}, u32[]{:S(2)}) collective-permute-start(bf16[128,1280]{1,0:T(8,128)(2,1)S(1)} %get-tuple-element.41), channel_id=1, source_target_pairs={{0,16},{16,0},{1,17},{17,1},{2,18},{18,2},{3,19},{19,3},{4,20},{20... | collective-permute-start | bytes 983048 | tf_op jit(solution)/shard_map/ppermute | solution.py:22
  19.6 0.1 collective-permute-start.5
  19.7 0.1 cut.1
  19.8 0.5 collective-permute-start.10
  20.3 2.2 %collective-permute-done.7.refs_6_ = bf16[32,5120]{1,0:T(8,128)(2,1)S(1)} collective-permute-done((bf16[32,5120]{1,0:T(8,128)(2,1)S(1)}, bf16[32,5120]{1,0:T(8,128)(2,1)S(1)}, u32[]{:S(2)}, u32[]{:S(2)}) %collective-permute-start.7) | collective-permute-done | bytes 327712 | tf_op jit(solution)/shard_map/ppermute | solution.py:50
  22.5 2.1 %collective-permute-start.11 = (bf16[128,1280]{1,0:T(8,128)(2,1)S(1)}, bf16[128,1280]{1,0:T(8,128)(2,1)S(1)}, u32[]{:S(2)}, u32[]{:S(2)}) collective-permute-start(bf16[128,1280]{1,0:T(8,128)(2,1)S(1)} %get-tuple-element.46), channel_id=1, source_target_pairs={{0,16},{16,0},{1,17},{17,1},{2,18},{18,2},{3,19},{19,3},{4,20},{20... | collective-permute-start | bytes 983048 | tf_op jit(solution)/shard_map/ppermute | solution.py:22
  24.6 1.3 %collective-permute-start.8 = (bf16[16,5120]{1,0:T(8,128)(2,1)S(1)}, bf16[16,5120]{1,0:T(8,128)(2,1)S(1)}, u32[]{:S(2)}, u32[]{:S(2)}) collective-permute-start(bf16[16,5120]{1,0:T(8,128)(2,1)S(1)} %slice.16), channel_id=1, source_target_pairs={{0,1},{1,0},{2,3},{3,2},{4,5},{5,4},{6,7},{7,6},{8,9},{9,8},{10,11... | collective-permute-start | bytes 491528 | tf_op jit(solution)/shard_map/ppermute | solution.py:50
  25.9 1.3 %collective-permute-start.9 = (bf16[16,5120]{1,0:T(8,128)(2,1)S(1)}, bf16[16,5120]{1,0:T(8,128)(2,1)S(1)}, u32[]{:S(2)}, u32[]{:S(2)}) collective-permute-start(bf16[16,5120]{1,0:T(8,128)(2,1)S(1)} %slice.17), channel_id=1, source_target_pairs={{0,2},{1,3},{2,0},{3,1},{4,6},{5,7},{6,4},{7,5},{8,10},{9,11},{10,... | collective-permute-start | bytes 491528 | tf_op jit(solution)/shard_map/ppermute | solution.py:50
  27.2 1.3 %collective-permute-start.24 = (bf16[128,5120]{1,0:T(8,128)(2,1)S(1)}, bf16[128,5120]{1,0:T(8,128)(2,1)S(1)}, u32[]{:S(2)}, u32[]{:S(2)}) collective-permute-start(bf16[128,5120]{1,0:T(8,128)(2,1)S(1)} %get-tuple-element.40.refs_1_), channel_id=1, source_target_pairs={{0,16},{1,17},{2,18},{3,19},{4,20},{5,21},{6,22},{7,23},{8,24},{9,... | collective-permute-start | bytes 3932168 | tf_op jit(solution)/shard_map/ppermute | solution.py:17
  28.5 0.7 collective-permute-done.8.refs_7_
  29.2 1.2 %collective-permute-done.9.refs_8_ = bf16[16,5120]{1,0:T(8,128)(2,1)S(1)} collective-permute-done((bf16[16,5120]{1,0:T(8,128)(2,1)S(1)}, bf16[16,5120]{1,0:T(8,128)(2,1)S(1)}, u32[]{:S(2)}, u32[]{:S(2)}) %collective-permute-start.9) | collective-permute-done | bytes 163872 | tf_op jit(solution)/shard_map/ppermute | solution.py:50
  30.4 1.0 %attend.1 = (bf16[128,2560]{1,0:T(8,128)(2,1)S(1)}, f32[20,128,128]{2,1,0:T(8,128)S(1)}, bf16[128,2560]{1,0:T(8,128)(2,1)S(1)}) custom-call(s32[1]{0:T(128)} %bitcast.refs_0_.section, bf16[128,1280]{1,0:T(8,128)(2,1)S(1)} %collective-permute-done.4.refs_1_, bf16[128,1280]{1,0:T(8,128)(2,1)S(1)} %collective-permute-done.5.refs_2_, ...), custom_call_target="tpu_custom_call" | custom-call | flops 167772160 | bytes 5242884 | tf_op jit(solution)/shard_map/attend/pallas_call | solution.py:143
  31.5 1.3 %collective-permute-start.12 = (bf16[128,2560]{1,0:T(8,128)(2,1)S(1)}, bf16[128,2560]{1,0:T(8,128)(2,1)S(1)}, u32[]{:S(2)}, u32[]{:S(2)}) collective-permute-start(bf16[128,2560]{1,0:T(8,128)(2,1)S(1)} %get-tuple-element.47.refs_3_), channel_id=1, source_target_pairs={{0,16},{1,17},{2,18},{3,19},{4,20},{5,21},{6,22},{7,23},{8,24},{9,... | collective-permute-start | bytes 1966088 | tf_op jit(solution)/shard_map/ppermute | solution.py:27
  32.8 1.3 %gradient.1 = (f32[32,5120]{1,0:T(8,128)S(1)}, f32[32,5120]{1,0:T(8,128)S(1)}, f32[32,5120]{1,0:T(8,128)S(1)}, bf16[16,5120]{1,0:T(8,128)(2,1)S(1)}, bf16[16,5120]{1,0:T(8,128)(2,1)S(1)}) custom-call(s32[1]{0:T(128)} %bitcast.refs_0_.section, bf16[128,2560]{1,0:T(8,128)(2,1)S(1)} %get-tuple-element.48.q_ref, ...), custom_call_target="tpu_custom_call" | custom-call | flops 419430400 | bytes 6881284 | tf_op jit(solution)/shard_map/gradient/pallas_call | solution.py:143
  34.1 2.2 %collective-permute-start.17 = (bf16[16,5120]{1,0:T(8,128)(2,1)S(1)}, bf16[16,5120]{1,0:T(8,128)(2,1)S(1)}, u32[]{:S(2)}, u32[]{:S(2)}) collective-permute-start(bf16[16,5120]{1,0:T(8,128)(2,1)S(1)} %get-tuple-element.57), channel_id=1, source_target_pairs={{2,0},{3,1},{0,2},{1,3},{6,4},{7,5},{4,6},{5,7},{10,8},{11,9},{8,1... | collective-permute-start | bytes 491528 | tf_op jit(solution)/shard_map/ppermute | solution.py:50
  36.3 0.3 collective-permute-start.16
  36.6 0.1 collective-permute-done.12.refs_2_
  36.6 0.6 settle.1
  37.3 2.4 %collective-permute-start.15 = (bf16[8,5120]{1,0:T(8,128)(2,1)S(1)}, bf16[8,5120]{1,0:T(8,128)(2,1)S(1)}, u32[]{:S(2)}, u32[]{:S(2)}) collective-permute-start(bf16[8,5120]{1,0:T(8,128)(2,1)S(1)} %get-tuple-element.53.refs_0_.after_any), channel_id=1, source_target_pairs={{0,12},{1,13},{2,14},{3,15},{4,8},{5,9},{6,10},{7,11},{8,4},{9,5},... | collective-permute-start | bytes 245768 | tf_op jit(solution)/shard_map/ppermute | solution.py:50
  39.7 1.2 %collective-permute-start.13 = (bf16[8,5120]{1,0:T(8,128)(2,1)S(1)}, bf16[8,5120]{1,0:T(8,128)(2,1)S(1)}, u32[]{:S(2)}, u32[]{:S(2)}) collective-permute-start(bf16[8,5120]{1,0:T(8,128)(2,1)S(1)} %get-tuple-element.53.refs_0_.after_any), channel_id=1, source_target_pairs={{0,4},{1,5},{2,6},{3,7},{4,0},{5,1},{6,2},{7,3},{8,12},{9,13},{10,... | collective-permute-start | bytes 245768 | tf_op jit(solution)/shard_map/ppermute | solution.py:50
  41.0 1.2 %collective-permute-start.21 = (bf16[32,5120]{1,0:T(8,128)(2,1)S(1)}, bf16[32,5120]{1,0:T(8,128)(2,1)S(1)}, u32[]{:S(2)}, u32[]{:S(2)}) collective-permute-start(bf16[32,5120]{1,0:T(8,128)(2,1)S(1)} %add_half.5.refs_5_), channel_id=1, source_target_pairs={{1,0},{0,1},{3,2},{2,3},{5,4},{4,5},{7,6},{6,7},{9,8},{8,9},{11,10... | collective-permute-start | bytes 983048 | tf_op jit(solution)/shard_map/ppermute | solution.py:50
  42.2 0.2 collective-permute-done.15.refs_3_
  42.5 1.2 %collective-permute-start.20 = (bf16[32,5120]{1,0:T(8,128)(2,1)S(1)}, bf16[32,5120]{1,0:T(8,128)(2,1)S(1)}, u32[]{:S(2)}, u32[]{:S(2)}) collective-permute-start(bf16[32,5120]{1,0:T(8,128)(2,1)S(1)} %add_half.4.refs_4_), channel_id=1, source_target_pairs={{2,0},{3,1},{0,2},{1,3},{6,4},{7,5},{4,6},{5,7},{10,8},{11,9},{8,1... | collective-permute-start | bytes 983048 | tf_op jit(solution)/shard_map/ppermute | solution.py:50
  43.7 3.5 %collective-permute-done.14.refs_2_ = bf16[8,5120]{1,0:T(8,128)(2,1)S(1)} collective-permute-done((bf16[8,5120]{1,0:T(8,128)(2,1)S(1)}, bf16[8,5120]{1,0:T(8,128)(2,1)S(1)}, u32[]{:S(2)}, u32[]{:S(2)}) %collective-permute-start.14) | collective-permute-done | bytes 81952 | tf_op jit(solution)/shard_map/ppermute | solution.py:50
  47.2 1.2 %collective-permute-start.19 = (bf16[32,5120]{1,0:T(8,128)(2,1)S(1)}, bf16[32,5120]{1,0:T(8,128)(2,1)S(1)}, u32[]{:S(2)}, u32[]{:S(2)}) collective-permute-start(bf16[32,5120]{1,0:T(8,128)(2,1)S(1)} %join.3.refs_3_.refs_2_), channel_id=1, source_target_pairs={{0,2},{1,3},{2,0},{3,1},{4,6},{5,7},{6,4},{7,5},{8,10},{9,11},{10,... | collective-permute-start | bytes 983048 | tf_op jit(solution)/shard_map/ppermute | solution.py:50
  48.4 0.2 collective-permute-start.18
  48.6 0.1 collective-permute-done.20.refs_1_
  48.7 0.1 add_blocks.2
  48.8 8.2 %collective-permute-done.19.refs_0_.refs_4_ = bf16[32,5120]{1,0:T(8,128)(2,1)S(1)} collective-permute-done((bf16[32,5120]{1,0:T(8,128)(2,1)S(1)}, bf16[32,5120]{1,0:T(8,128)(2,1)S(1)}, u32[]{:S(2)}, u32[]{:S(2)}) %collective-permute-start.19) | collective-permute-done | bytes 327712 | tf_op jit(solution)/shard_map/ppermute | solution.py:50
  57.0 1.2 %collective-permute-start.22 = (bf16[16,5120]{1,0:T(8,128)(2,1)S(1)}, bf16[16,5120]{1,0:T(8,128)(2,1)S(1)}, u32[]{:S(2)}, u32[]{:S(2)}) collective-permute-start(bf16[16,5120]{1,0:T(8,128)(2,1)S(1)} %get-tuple-element.59), channel_id=1, source_target_pairs={{0,1},{1,0},{2,3},{3,2},{4,5},{5,4},{6,7},{7,6},{8,9},{9,8},{10,11... | collective-permute-start | bytes 491528 | tf_op jit(solution)/shard_map/ppermute | solution.py:50
  58.2 0.2 collective-permute-start.23
  58.4 2.5 %collective-permute-start.26 = (bf16[8,5120]{1,0:T(8,128)(2,1)S(1)}, bf16[8,5120]{1,0:T(8,128)(2,1)S(1)}, u32[]{:S(2)}, u32[]{:S(2)}) collective-permute-start(bf16[8,5120]{1,0:T(8,128)(2,1)S(1)} %get-tuple-element.62), channel_id=1, source_target_pairs={{8,0},{9,1},{10,2},{11,3},{12,4},{13,5},{14,6},{15,7},{0,8},{1,9},... | collective-permute-start | bytes 245768 | tf_op jit(solution)/shard_map/ppermute | solution.py:50
  60.9 0.8 collective-permute-done.25.refs_8_.refs_1_
  61.7 1.0 %collective-permute-done.26.refs_9_.refs_2_ = bf16[8,5120]{1,0:T(8,128)(2,1)S(1)} collective-permute-done((bf16[8,5120]{1,0:T(8,128)(2,1)S(1)}, bf16[8,5120]{1,0:T(8,128)(2,1)S(1)}, u32[]{:S(2)}, u32[]{:S(2)}) %collective-permute-start.26) | collective-permute-done | bytes 81952 | tf_op jit(solution)/shard_map/ppermute | solution.py:50
  62.7 2.3 %expert.1 = (f32[32,5120]{1,0:T(8,128)S(1)}, f32[32,5120]{1,0:T(8,128)S(1)}, f32[32,5120]{1,0:T(8,128)S(1)}, bf16[16,5120]{1,0:T(8,128)(2,1)S(1)}, bf16[16,5120]{1,0:T(8,128)(2,1)S(1)}) custom-call(bf16[5120,640]{1,0:T(8,128)(2,1)S(1)} %bitcast.18, bf16[640,5120]{1,0:T(8,128)(2,1)S(1)} %bitcast.19, bf16[32,5120]{1,0:T(8,128)(2,1)S(1)} %join.3.refs_3_.refs_2_, ...), custom_call_target="tpu_custom_call" | custom-call | flops 1677721600 | bytes 16711680 | tf_op jit(solution)/shard_map/expert/pallas_call | solution.py:143
  65.1 1.4 %collective-permute-start.30 = (bf16[16,5120]{1,0:T(8,128)(2,1)S(1)}, bf16[16,5120]{1,0:T(8,128)(2,1)S(1)}, u32[]{:S(2)}, u32[]{:S(2)}) collective-permute-start(bf16[16,5120]{1,0:T(8,128)(2,1)S(1)} %get-tuple-element.68), channel_id=1, source_target_pairs={{2,0},{3,1},{0,2},{1,3},{6,4},{7,5},{4,6},{5,7},{10,8},{11,9},{8,1... | collective-permute-start | bytes 491528 | tf_op jit(solution)/shard_map/ppermute | solution.py:50
  66.4 0.2 collective-permute-start.27
  66.6 2.0 %collective-permute-start.28 = (bf16[8,5120]{1,0:T(8,128)(2,1)S(1)}, bf16[8,5120]{1,0:T(8,128)(2,1)S(1)}, u32[]{:S(2)}, u32[]{:S(2)}) collective-permute-start(bf16[8,5120]{1,0:T(8,128)(2,1)S(1)} %get-tuple-element.66), channel_id=1, source_target_pairs={{12,0},{13,1},{14,2},{15,3},{8,4},{9,5},{10,6},{11,7},{4,8},{5,9},... | collective-permute-start | bytes 245768 | tf_op jit(solution)/shard_map/ppermute | solution.py:50
  68.7 3.1 %collective-permute-done.28.refs_3_ = bf16[8,5120]{1,0:T(8,128)(2,1)S(1)} collective-permute-done((bf16[8,5120]{1,0:T(8,128)(2,1)S(1)}, bf16[8,5120]{1,0:T(8,128)(2,1)S(1)}, u32[]{:S(2)}, u32[]{:S(2)}) %collective-permute-start.28) | collective-permute-done | bytes 81952 | tf_op jit(solution)/shard_map/ppermute | solution.py:50
  71.9 1.3 %collective-permute-start.31 = (bf16[32,5120]{1,0:T(8,128)(2,1)S(1)}, bf16[32,5120]{1,0:T(8,128)(2,1)S(1)}, u32[]{:S(2)}, u32[]{:S(2)}) collective-permute-start(bf16[32,5120]{1,0:T(8,128)(2,1)S(1)} %add_half.7), channel_id=1, source_target_pairs={{1,0},{0,1},{3,2},{2,3},{5,4},{4,5},{7,6},{6,7},{9,8},{8,9},{11,10... | collective-permute-start | bytes 983048 | tf_op jit(solution)/shard_map/ppermute | solution.py:50
  73.3 0.2 collective-permute-start.29
  73.6 1.3 %collective-permute-start.35 = (f32[8,5120]{1,0:T(8,128)S(1)}, f32[8,5120]{1,0:T(8,128)S(1)}, u32[]{:S(2)}, u32[]{:S(2)}) collective-permute-start(f32[8,5120]{1,0:T(8,128)S(1)} %add_last.2.refs_2_.second_ref), channel_id=1, source_target_pairs={{0,16},{1,17},{2,18},{3,19},{4,20},{5,21},{6,22},{7,23},{8,24},{9,... | collective-permute-start | bytes 491528 | tf_op jit(solution)/shard_map/ppermute | solution.py:27
  74.9 4.7 %collective-permute-done.31.refs_2_ = bf16[32,5120]{1,0:T(8,128)(2,1)S(1)} collective-permute-done((bf16[32,5120]{1,0:T(8,128)(2,1)S(1)}, bf16[32,5120]{1,0:T(8,128)(2,1)S(1)}, u32[]{:S(2)}, u32[]{:S(2)}) %collective-permute-start.31) | collective-permute-done | bytes 327712 | tf_op jit(solution)/shard_map/ppermute | solution.py:50
  79.6 0.1 add_blocks.3
  79.8 2.0 %collective-permute-start.32 = (bf16[8,5120]{1,0:T(8,128)(2,1)S(1)}, bf16[8,5120]{1,0:T(8,128)(2,1)S(1)}, u32[]{:S(2)}, u32[]{:S(2)}) collective-permute-start(bf16[8,5120]{1,0:T(8,128)(2,1)S(1)} %get-tuple-element.71), channel_id=1, source_target_pairs={{12,0},{13,1},{14,2},{15,3},{8,4},{9,5},{10,6},{11,7},{4,8},{5,9},... | collective-permute-start | bytes 245768 | tf_op jit(solution)/shard_map/ppermute | solution.py:50
  81.8 1.6 %collective-permute-start.34 = (bf16[8,5120]{1,0:T(8,128)(2,1)S(1)}, bf16[8,5120]{1,0:T(8,128)(2,1)S(1)}, u32[]{:S(2)}, u32[]{:S(2)}) collective-permute-start(bf16[8,5120]{1,0:T(8,128)(2,1)S(1)} %get-tuple-element.73), channel_id=1, source_target_pairs={{4,0},{5,1},{6,2},{7,3},{0,4},{1,5},{2,6},{3,7},{12,8},{13,9},{14,... | collective-permute-start | bytes 245768 | tf_op jit(solution)/shard_map/ppermute | solution.py:50
  83.4 0.6 collective-permute-done.35.first_ref
  84.0 0.8 lay_out.1
  84.8 0.2 collective-permute-done.32.refs_1_
  85.0 1.7 %collective-permute-done.33.refs_2_ = bf16[8,5120]{1,0:T(8,128)(2,1)S(1)} collective-permute-done((bf16[8,5120]{1,0:T(8,128)(2,1)S(1)}, bf16[8,5120]{1,0:T(8,128)(2,1)S(1)}, u32[]{:S(2)}, u32[]{:S(2)}) %collective-permute-start.33) | collective-permute-done | bytes 81952 | tf_op jit(solution)/shard_map/ppermute | solution.py:50
  86.7 1.3 %collective-permute-start.36 = (f32[8,5248]{1,0:T(8,128)S(1)}, f32[8,5248]{1,0:T(8,128)S(1)}, u32[]{:S(2)}, u32[]{:S(2)}) collective-permute-start(f32[8,5248]{1,0:T(8,128)S(1)} %add_last.3.back_ref), channel_id=1, source_target_pairs={{0,16},{1,17},{2,18},{3,19},{4,20},{5,21},{6,22},{7,23},{8,24},{9,... | collective-permute-start | bytes 503816 | tf_op jit(solution)/shard_map/ppermute | solution.py:17
  88.0 1.5 %finish.2 = bf16[128,5120]{1,0:T(8,128)(2,1)} custom-call(s32[1]{0:T(128)} %bitcast.refs_0_.section, bf16[128,5120]{1,0:T(8,128)(2,1)S(1)} %get-tuple-element.52.res_ref, f32[8,5248]{1,0:T(8,128)S(1)} %add_last.3.back_ref), custom_call_target="tpu_custom_call" | custom-call | flops 32768000 | bytes 3276800 | tf_op jit(solution)/shard_map/finish/pallas_call | solution.py:542
  89.5 8.4 %collective-permute-done.36.back_ref = f32[8,5248]{1,0:T(8,128)S(1)} collective-permute-done((f32[8,5248]{1,0:T(8,128)S(1)}, f32[8,5248]{1,0:T(8,128)S(1)}, u32[]{:S(2)}, u32[]{:S(2)}) %collective-permute-start.36) | collective-permute-done | bytes 167968 | tf_op jit(solution)/shard_map/ppermute | solution.py:17
  98.0 1.5 %finish.3 = bf16[128,5120]{1,0:T(8,128)(2,1)} custom-call(s32[1]{0:T(128)} %bitcast.refs_0_.section, bf16[128,5120]{1,0:T(8,128)(2,1)S(1)} %collective-permute-done.24.refs_7_.res_ref, f32[8,5248]{1,0:T(8,128)S(1)} %collective-permute-done.36.back_ref, bf16[128,5120]{1,0:T(8,128)(2,1)} %get-tuple-element.75.refs_0_), custom_call_target="tpu_custom_call", output_to_operand_aliasing={{}: (3, {})} | custom-call | flops 32768000 | bytes 3276800 | tf_op jit(solution)/shard_map/finish/pallas_call | solution.py:542
  (56 shorter events, 0.5 us)
Async XLA Ops:
  0.6 16.3 %copy-start.5 = (f32[1,128]{1,0:T(1,128)S(1)}, f32[1,128]{1,0:T(1,128)}, u32[]{:S(2)}) copy-start(f32[1,128]{1,0:T(1,128)} %refs_2_.1) | copy-start | bytes 1540
  0.6 16.3 %copy-start.6 = (s32[1,128]{1,0:T(1,128)S(1)}, s32[1,128]{1,0:T(1,128)}, u32[]{:S(2)}) copy-start(s32[1,128]{1,0:T(1,128)} %refs_3_.1) | copy-start | bytes 1540
  0.7 16.3 %copy-start.4 = (f32[1,5120]{1,0:T(1,128)S(1)}, f32[1,5120]{1,0:T(1,128)}, u32[]{:S(2)}) copy-start(f32[1,5120]{1,0:T(1,128)} %refs_1_.1) | copy-start | bytes 61444
  0.7 16.3 %copy-start.1 = (bf16[1,128,5120]{2,1,0:T(8,128)(2,1)S(1)}, bf16[1,128,5120]{2,1,0:T(8,128)(2,1)}, u32[]{:S(2)}) copy-start(bf16[1,128,5120]{2,1,0:T(8,128)(2,1)} %param.9) | copy-start | bytes 3932164
  1.8 1.3 %collective-permute-start = (bf16[8,5120]{1,0:T(8,128)(2,1)S(1)}, bf16[8,5120]{1,0:T(8,128)(2,1)S(1)}, u32[]{:S(2)}, u32[]{:S(2)}) collective-permute-start(bf16[8,5120]{1,0:T(8,128)(2,1)S(1)} %bitcast.25), channel_id=1, source_target_pairs={{0,16},{16,0},{1,17},{17,1},{2,18},{18,2},{3,19},{19,3},{4,20},{20... | collective-permute-start | bytes 245768 | tf_op jit(solution)/shard_map/ppermute | solution.py:22
  2.0 17.7 %copy-start.2 = (bf16[1,128,5120]{2,1,0:T(8,128)(2,1)S(1)}, bf16[1,128,5120]{2,1,0:T(8,128)(2,1)}, u32[]{:S(2)}) copy-start(bf16[1,128,5120]{2,1,0:T(8,128)(2,1)} %param.11) | copy-start | bytes 3932164
  3.2 7.1 %collective-permute-start.3 = (bf16[8,5120]{1,0:T(8,128)(2,1)S(1)}, bf16[8,5120]{1,0:T(8,128)(2,1)S(1)}, u32[]{:S(2)}, u32[]{:S(2)}) collective-permute-start(bf16[8,5120]{1,0:T(8,128)(2,1)S(1)} %broadcast_select_fusion.refs_0_), channel_id=1, source_target_pairs={{0,12},{1,13},{2,14},{3,15},{4,8},{5,9},{6,10},{7,11},{8,4},{9,5},... | collective-permute-start | bytes 245768 | tf_op jit(solution)/shard_map/ppermute | solution.py:50
  7.7 6.6 %collective-permute-start.2 = (bf16[8,5120]{1,0:T(8,128)(2,1)S(1)}, bf16[8,5120]{1,0:T(8,128)(2,1)S(1)}, u32[]{:S(2)}, u32[]{:S(2)}) collective-permute-start(bf16[8,5120]{1,0:T(8,128)(2,1)S(1)} %broadcast_select_fusion.refs_0_), channel_id=1, source_target_pairs={{0,8},{1,9},{2,10},{3,11},{4,12},{5,13},{6,14},{7,15},{8,0},{9,1},... | collective-permute-start | bytes 245768 | tf_op jit(solution)/shard_map/ppermute | solution.py:50
  7.7 6.6 %collective-permute-start.1 = (bf16[8,5120]{1,0:T(8,128)(2,1)S(1)}, bf16[8,5120]{1,0:T(8,128)(2,1)S(1)}, u32[]{:S(2)}, u32[]{:S(2)}) collective-permute-start(bf16[8,5120]{1,0:T(8,128)(2,1)S(1)} %broadcast_select_fusion.refs_0_), channel_id=1, source_target_pairs={{0,4},{1,5},{2,6},{3,7},{4,0},{5,1},{6,2},{7,3},{8,12},{9,13},{10,... | collective-permute-start | bytes 245768 | tf_op jit(solution)/shard_map/ppermute | solution.py:50
  14.4 8.1 %collective-permute-start.7 = (bf16[32,5120]{1,0:T(8,128)(2,1)S(1)}, bf16[32,5120]{1,0:T(8,128)(2,1)S(1)}, u32[]{:S(2)}, u32[]{:S(2)}) collective-permute-start(bf16[32,5120]{1,0:T(8,128)(2,1)S(1)} %join.2.refs_4_), channel_id=1, source_target_pairs={{0,2},{1,3},{2,0},{3,1},{4,6},{5,7},{6,4},{7,5},{8,10},{9,11},{10,... | collective-permute-start | bytes 983048 | tf_op jit(solution)/shard_map/ppermute | solution.py:50
  15.7 8.9 %collective-permute-start.6 = (bf16[32,5120]{1,0:T(8,128)(2,1)S(1)}, bf16[32,5120]{1,0:T(8,128)(2,1)S(1)}, u32[]{:S(2)}, u32[]{:S(2)}) collective-permute-start(bf16[32,5120]{1,0:T(8,128)(2,1)S(1)} %join.2.refs_4_), channel_id=1, source_target_pairs={{0,1},{1,0},{2,3},{3,2},{4,5},{5,4},{6,7},{7,6},{8,9},{9,8},{10,11... | collective-permute-start | bytes 983048 | tf_op jit(solution)/shard_map/ppermute | solution.py:50
  17.8 8.1 %collective-permute-start.4 = (bf16[128,1280]{1,0:T(8,128)(2,1)S(1)}, bf16[128,1280]{1,0:T(8,128)(2,1)S(1)}, u32[]{:S(2)}, u32[]{:S(2)}) collective-permute-start(bf16[128,1280]{1,0:T(8,128)(2,1)S(1)} %get-tuple-element.41), channel_id=1, source_target_pairs={{0,16},{16,0},{1,17},{17,1},{2,18},{18,2},{3,19},{19,3},{4,20},{20... | collective-permute-start | bytes 983048 | tf_op jit(solution)/shard_map/ppermute | solution.py:22
  19.6 7.6 %collective-permute-start.5 = (bf16[128,1280]{1,0:T(8,128)(2,1)S(1)}, bf16[128,1280]{1,0:T(8,128)(2,1)S(1)}, u32[]{:S(2)}, u32[]{:S(2)}) collective-permute-start(bf16[128,1280]{1,0:T(8,128)(2,1)S(1)} %get-tuple-element.42), channel_id=1, source_target_pairs={{0,16},{16,0},{1,17},{17,1},{2,18},{18,2},{3,19},{19,3},{4,20},{20... | collective-permute-start | bytes 983048 | tf_op jit(solution)/shard_map/ppermute | solution.py:22
  19.8 8.7 %collective-permute-start.10 = (bf16[128,1280]{1,0:T(8,128)(2,1)S(1)}, bf16[128,1280]{1,0:T(8,128)(2,1)S(1)}, u32[]{:S(2)}, u32[]{:S(2)}) collective-permute-start(bf16[128,1280]{1,0:T(8,128)(2,1)S(1)} %get-tuple-element.45), channel_id=1, source_target_pairs={{0,16},{16,0},{1,17},{17,1},{2,18},{18,2},{3,19},{19,3},{4,20},{20... | collective-permute-start | bytes 983048 | tf_op jit(solution)/shard_map/ppermute | solution.py:22
  22.5 6.0 %collective-permute-start.11 = (bf16[128,1280]{1,0:T(8,128)(2,1)S(1)}, bf16[128,1280]{1,0:T(8,128)(2,1)S(1)}, u32[]{:S(2)}, u32[]{:S(2)}) collective-permute-start(bf16[128,1280]{1,0:T(8,128)(2,1)S(1)} %get-tuple-element.46), channel_id=1, source_target_pairs={{0,16},{16,0},{1,17},{17,1},{2,18},{18,2},{3,19},{19,3},{4,20},{20... | collective-permute-start | bytes 983048 | tf_op jit(solution)/shard_map/ppermute | solution.py:22
  24.6 4.6 %collective-permute-start.8 = (bf16[16,5120]{1,0:T(8,128)(2,1)S(1)}, bf16[16,5120]{1,0:T(8,128)(2,1)S(1)}, u32[]{:S(2)}, u32[]{:S(2)}) collective-permute-start(bf16[16,5120]{1,0:T(8,128)(2,1)S(1)} %slice.16), channel_id=1, source_target_pairs={{0,1},{1,0},{2,3},{3,2},{4,5},{5,4},{6,7},{7,6},{8,9},{9,8},{10,11... | collective-permute-start | bytes 491528 | tf_op jit(solution)/shard_map/ppermute | solution.py:50
  25.9 4.5 %collective-permute-start.9 = (bf16[16,5120]{1,0:T(8,128)(2,1)S(1)}, bf16[16,5120]{1,0:T(8,128)(2,1)S(1)}, u32[]{:S(2)}, u32[]{:S(2)}) collective-permute-start(bf16[16,5120]{1,0:T(8,128)(2,1)S(1)} %slice.17), channel_id=1, source_target_pairs={{0,2},{1,3},{2,0},{3,1},{4,6},{5,7},{6,4},{7,5},{8,10},{9,11},{10,... | collective-permute-start | bytes 491528 | tf_op jit(solution)/shard_map/ppermute | solution.py:50
  27.2 33.7 %collective-permute-start.24 = (bf16[128,5120]{1,0:T(8,128)(2,1)S(1)}, bf16[128,5120]{1,0:T(8,128)(2,1)S(1)}, u32[]{:S(2)}, u32[]{:S(2)}) collective-permute-start(bf16[128,5120]{1,0:T(8,128)(2,1)S(1)} %get-tuple-element.40.refs_1_), channel_id=1, source_target_pairs={{0,16},{1,17},{2,18},{3,19},{4,20},{5,21},{6,22},{7,23},{8,24},{9,... | collective-permute-start | bytes 3932168 | tf_op jit(solution)/shard_map/ppermute | solution.py:17
  31.5 5.1 %collective-permute-start.12 = (bf16[128,2560]{1,0:T(8,128)(2,1)S(1)}, bf16[128,2560]{1,0:T(8,128)(2,1)S(1)}, u32[]{:S(2)}, u32[]{:S(2)}) collective-permute-start(bf16[128,2560]{1,0:T(8,128)(2,1)S(1)} %get-tuple-element.47.refs_3_), channel_id=1, source_target_pairs={{0,16},{1,17},{2,18},{3,19},{4,20},{5,21},{6,22},{7,23},{8,24},{9,... | collective-permute-start | bytes 1966088 | tf_op jit(solution)/shard_map/ppermute | solution.py:27
  32.8 3.9 %copy-start.3 = (f32[1,5120]{1,0:T(1,128)S(1)}, f32[1,5120]{1,0:T(1,128)}, u32[]{:S(2)}) copy-start(f32[1,5120]{1,0:T(1,128)} %refs_4_.1) | copy-start | bytes 61444
  32.8 29.9 %slice-start = ((s8[6553600]{0:T(1024)(128)(4,1)}), s8[4194304]{0:T(1024)(128)(4,1)S(1)}, s32[]{:S(2)}) async-start(s8[6553600]{0:T(1024)(128)(4,1)} %bitcast.16), calls=%async_computation | async-start | bytes 8388608
  34.1 5.5 %collective-permute-start.17 = (bf16[16,5120]{1,0:T(8,128)(2,1)S(1)}, bf16[16,5120]{1,0:T(8,128)(2,1)S(1)}, u32[]{:S(2)}, u32[]{:S(2)}) collective-permute-start(bf16[16,5120]{1,0:T(8,128)(2,1)S(1)} %get-tuple-element.57), channel_id=1, source_target_pairs={{2,0},{3,1},{0,2},{1,3},{6,4},{7,5},{4,6},{5,7},{10,8},{11,9},{8,1... | collective-permute-start | bytes 491528 | tf_op jit(solution)/shard_map/ppermute | solution.py:50
  36.3 4.6 %collective-permute-start.16 = (bf16[16,5120]{1,0:T(8,128)(2,1)S(1)}, bf16[16,5120]{1,0:T(8,128)(2,1)S(1)}, u32[]{:S(2)}, u32[]{:S(2)}) collective-permute-start(bf16[16,5120]{1,0:T(8,128)(2,1)S(1)} %get-tuple-element.55), channel_id=1, source_target_pairs={{1,0},{0,1},{3,2},{2,3},{5,4},{4,5},{7,6},{6,7},{9,8},{8,9},{11,10... | collective-permute-start | bytes 491528 | tf_op jit(solution)/shard_map/ppermute | solution.py:50
  36.6 26.1 %slice-start.1 = ((s8[6553600]{0:T(1024)(128)(4,1)}), s8[2359296]{0:T(1024)(128)(4,1)S(1)}, s32[]{:S(2)}) async-start(s8[6553600]{0:T(1024)(128)(4,1)} %bitcast.16), calls=%async_computation.1 | async-start | bytes 4718592
  36.6 26.1 %copy-start = (bf16[1,640,5120]{2,1,0:T(8,128)(2,1)S(1)}, bf16[1,640,5120]{2,1,0:T(8,128)(2,1)}, u32[]{:S(2)}) copy-start(bf16[1,640,5120]{2,1,0:T(8,128)(2,1)} %param.15) | copy-start | bytes 19660804
  37.3 5.2 %collective-permute-start.15 = (bf16[8,5120]{1,0:T(8,128)(2,1)S(1)}, bf16[8,5120]{1,0:T(8,128)(2,1)S(1)}, u32[]{:S(2)}, u32[]{:S(2)}) collective-permute-start(bf16[8,5120]{1,0:T(8,128)(2,1)S(1)} %get-tuple-element.53.refs_0_.after_any), channel_id=1, source_target_pairs={{0,12},{1,13},{2,14},{3,15},{4,8},{5,9},{6,10},{7,11},{8,4},{9,5},... | collective-permute-start | bytes 245768 | tf_op jit(solution)/shard_map/ppermute | solution.py:50
  39.7 7.5 %collective-permute-start.14 = (bf16[8,5120]{1,0:T(8,128)(2,1)S(1)}, bf16[8,5120]{1,0:T(8,128)(2,1)S(1)}, u32[]{:S(2)}, u32[]{:S(2)}) collective-permute-start(bf16[8,5120]{1,0:T(8,128)(2,1)S(1)} %get-tuple-element.53.refs_0_.after_any), channel_id=1, source_target_pairs={{0,8},{1,9},{2,10},{3,11},{4,12},{5,13},{6,14},{7,15},{8,0},{9,1},... | collective-permute-start | bytes 245768 | tf_op jit(solution)/shard_map/ppermute | solution.py:50
  39.7 7.5 %collective-permute-start.13 = (bf16[8,5120]{1,0:T(8,128)(2,1)S(1)}, bf16[8,5120]{1,0:T(8,128)(2,1)S(1)}, u32[]{:S(2)}, u32[]{:S(2)}) collective-permute-start(bf16[8,5120]{1,0:T(8,128)(2,1)S(1)} %get-tuple-element.53.refs_0_.after_any), channel_id=1, source_target_pairs={{0,4},{1,5},{2,6},{3,7},{4,0},{5,1},{6,2},{7,3},{8,12},{9,13},{10,... | collective-permute-start | bytes 245768 | tf_op jit(solution)/shard_map/ppermute | solution.py:50
  41.0 7.7 %collective-permute-start.21 = (bf16[32,5120]{1,0:T(8,128)(2,1)S(1)}, bf16[32,5120]{1,0:T(8,128)(2,1)S(1)}, u32[]{:S(2)}, u32[]{:S(2)}) collective-permute-start(bf16[32,5120]{1,0:T(8,128)(2,1)S(1)} %add_half.5.refs_5_), channel_id=1, source_target_pairs={{1,0},{0,1},{3,2},{2,3},{5,4},{4,5},{7,6},{6,7},{9,8},{8,9},{11,10... | collective-permute-start | bytes 983048 | tf_op jit(solution)/shard_map/ppermute | solution.py:50
  42.5 6.2 %collective-permute-start.20 = (bf16[32,5120]{1,0:T(8,128)(2,1)S(1)}, bf16[32,5120]{1,0:T(8,128)(2,1)S(1)}, u32[]{:S(2)}, u32[]{:S(2)}) collective-permute-start(bf16[32,5120]{1,0:T(8,128)(2,1)S(1)} %add_half.4.refs_4_), channel_id=1, source_target_pairs={{2,0},{3,1},{0,2},{1,3},{6,4},{7,5},{4,6},{5,7},{10,8},{11,9},{8,1... | collective-permute-start | bytes 983048 | tf_op jit(solution)/shard_map/ppermute | solution.py:50
  47.2 9.8 %collective-permute-start.19 = (bf16[32,5120]{1,0:T(8,128)(2,1)S(1)}, bf16[32,5120]{1,0:T(8,128)(2,1)S(1)}, u32[]{:S(2)}, u32[]{:S(2)}) collective-permute-start(bf16[32,5120]{1,0:T(8,128)(2,1)S(1)} %join.3.refs_3_.refs_2_), channel_id=1, source_target_pairs={{0,2},{1,3},{2,0},{3,1},{4,6},{5,7},{6,4},{7,5},{8,10},{9,11},{10,... | collective-permute-start | bytes 983048 | tf_op jit(solution)/shard_map/ppermute | solution.py:50
  48.4 8.6 %collective-permute-start.18 = (bf16[32,5120]{1,0:T(8,128)(2,1)S(1)}, bf16[32,5120]{1,0:T(8,128)(2,1)S(1)}, u32[]{:S(2)}, u32[]{:S(2)}) collective-permute-start(bf16[32,5120]{1,0:T(8,128)(2,1)S(1)} %join.3.refs_3_.refs_2_), channel_id=1, source_target_pairs={{0,1},{1,0},{2,3},{3,2},{4,5},{5,4},{6,7},{7,6},{8,9},{9,8},{10,11... | collective-permute-start | bytes 983048 | tf_op jit(solution)/shard_map/ppermute | solution.py:50
  57.0 5.7 %collective-permute-start.22 = (bf16[16,5120]{1,0:T(8,128)(2,1)S(1)}, bf16[16,5120]{1,0:T(8,128)(2,1)S(1)}, u32[]{:S(2)}, u32[]{:S(2)}) collective-permute-start(bf16[16,5120]{1,0:T(8,128)(2,1)S(1)} %get-tuple-element.59), channel_id=1, source_target_pairs={{0,1},{1,0},{2,3},{3,2},{4,5},{5,4},{6,7},{7,6},{8,9},{9,8},{10,11... | collective-permute-start | bytes 491528 | tf_op jit(solution)/shard_map/ppermute | solution.py:50
  58.2 4.5 %collective-permute-start.23 = (bf16[16,5120]{1,0:T(8,128)(2,1)S(1)}, bf16[16,5120]{1,0:T(8,128)(2,1)S(1)}, u32[]{:S(2)}, u32[]{:S(2)}) collective-permute-start(bf16[16,5120]{1,0:T(8,128)(2,1)S(1)} %get-tuple-element.60), channel_id=1, source_target_pairs={{0,2},{1,3},{2,0},{3,1},{4,6},{5,7},{6,4},{7,5},{8,10},{9,11},{10,... | collective-permute-start | bytes 491528 | tf_op jit(solution)/shard_map/ppermute | solution.py:50
  58.4 3.3 %collective-permute-start.25 = (bf16[8,5120]{1,0:T(8,128)(2,1)S(1)}, bf16[8,5120]{1,0:T(8,128)(2,1)S(1)}, u32[]{:S(2)}, u32[]{:S(2)}) collective-permute-start(bf16[8,5120]{1,0:T(8,128)(2,1)S(1)} %get-tuple-element.61), channel_id=1, source_target_pairs={{4,0},{5,1},{6,2},{7,3},{0,4},{1,5},{2,6},{3,7},{12,8},{13,9},{14,... | collective-permute-start | bytes 245768 | tf_op jit(solution)/shard_map/ppermute | solution.py:50
  58.4 4.3 %collective-permute-start.26 = (bf16[8,5120]{1,0:T(8,128)(2,1)S(1)}, bf16[8,5120]{1,0:T(8,128)(2,1)S(1)}, u32[]{:S(2)}, u32[]{:S(2)}) collective-permute-start(bf16[8,5120]{1,0:T(8,128)(2,1)S(1)} %get-tuple-element.62), channel_id=1, source_target_pairs={{8,0},{9,1},{10,2},{11,3},{12,4},{13,5},{14,6},{15,7},{0,8},{1,9},... | collective-permute-start | bytes 245768 | tf_op jit(solution)/shard_map/ppermute | solution.py:50
  65.1 6.8 %collective-permute-start.30 = (bf16[16,5120]{1,0:T(8,128)(2,1)S(1)}, bf16[16,5120]{1,0:T(8,128)(2,1)S(1)}, u32[]{:S(2)}, u32[]{:S(2)}) collective-permute-start(bf16[16,5120]{1,0:T(8,128)(2,1)S(1)} %get-tuple-element.68), channel_id=1, source_target_pairs={{2,0},{3,1},{0,2},{1,3},{6,4},{7,5},{4,6},{5,7},{10,8},{11,9},{8,1... | collective-permute-start | bytes 491528 | tf_op jit(solution)/shard_map/ppermute | solution.py:50
  66.4 6.8 %collective-permute-start.27 = (bf16[16,5120]{1,0:T(8,128)(2,1)S(1)}, bf16[16,5120]{1,0:T(8,128)(2,1)S(1)}, u32[]{:S(2)}, u32[]{:S(2)}) collective-permute-start(bf16[16,5120]{1,0:T(8,128)(2,1)S(1)} %get-tuple-element.65), channel_id=1, source_target_pairs={{1,0},{0,1},{3,2},{2,3},{5,4},{4,5},{7,6},{6,7},{9,8},{8,9},{11,10... | collective-permute-start | bytes 491528 | tf_op jit(solution)/shard_map/ppermute | solution.py:50
  66.6 5.2 %collective-permute-start.28 = (bf16[8,5120]{1,0:T(8,128)(2,1)S(1)}, bf16[8,5120]{1,0:T(8,128)(2,1)S(1)}, u32[]{:S(2)}, u32[]{:S(2)}) collective-permute-start(bf16[8,5120]{1,0:T(8,128)(2,1)S(1)} %get-tuple-element.66), channel_id=1, source_target_pairs={{12,0},{13,1},{14,2},{15,3},{8,4},{9,5},{10,6},{11,7},{4,8},{5,9},... | collective-permute-start | bytes 245768 | tf_op jit(solution)/shard_map/ppermute | solution.py:50
  71.9 7.7 %collective-permute-start.31 = (bf16[32,5120]{1,0:T(8,128)(2,1)S(1)}, bf16[32,5120]{1,0:T(8,128)(2,1)S(1)}, u32[]{:S(2)}, u32[]{:S(2)}) collective-permute-start(bf16[32,5120]{1,0:T(8,128)(2,1)S(1)} %add_half.7), channel_id=1, source_target_pairs={{1,0},{0,1},{3,2},{2,3},{5,4},{4,5},{7,6},{6,7},{9,8},{8,9},{11,10... | collective-permute-start | bytes 983048 | tf_op jit(solution)/shard_map/ppermute | solution.py:50
  73.3 6.3 %collective-permute-start.29 = (bf16[32,5120]{1,0:T(8,128)(2,1)S(1)}, bf16[32,5120]{1,0:T(8,128)(2,1)S(1)}, u32[]{:S(2)}, u32[]{:S(2)}) collective-permute-start(bf16[32,5120]{1,0:T(8,128)(2,1)S(1)} %add_half.6), channel_id=1, source_target_pairs={{2,0},{3,1},{0,2},{1,3},{6,4},{7,5},{4,6},{5,7},{10,8},{11,9},{8,1... | collective-permute-start | bytes 983048 | tf_op jit(solution)/shard_map/ppermute | solution.py:50
  73.6 10.4 %collective-permute-start.35 = (f32[8,5120]{1,0:T(8,128)S(1)}, f32[8,5120]{1,0:T(8,128)S(1)}, u32[]{:S(2)}, u32[]{:S(2)}) collective-permute-start(f32[8,5120]{1,0:T(8,128)S(1)} %add_last.2.refs_2_.second_ref), channel_id=1, source_target_pairs={{0,16},{1,17},{2,18},{3,19},{4,20},{5,21},{6,22},{7,23},{8,24},{9,... | collective-permute-start | bytes 491528 | tf_op jit(solution)/shard_map/ppermute | solution.py:27
  79.8 5.2 %collective-permute-start.32 = (bf16[8,5120]{1,0:T(8,128)(2,1)S(1)}, bf16[8,5120]{1,0:T(8,128)(2,1)S(1)}, u32[]{:S(2)}, u32[]{:S(2)}) collective-permute-start(bf16[8,5120]{1,0:T(8,128)(2,1)S(1)} %get-tuple-element.71), channel_id=1, source_target_pairs={{12,0},{13,1},{14,2},{15,3},{8,4},{9,5},{10,6},{11,7},{4,8},{5,9},... | collective-permute-start | bytes 245768 | tf_op jit(solution)/shard_map/ppermute | solution.py:50
  81.7 4.9 %collective-permute-start.33 = (bf16[8,5120]{1,0:T(8,128)(2,1)S(1)}, bf16[8,5120]{1,0:T(8,128)(2,1)S(1)}, u32[]{:S(2)}, u32[]{:S(2)}) collective-permute-start(bf16[8,5120]{1,0:T(8,128)(2,1)S(1)} %get-tuple-element.72), channel_id=1, source_target_pairs={{8,0},{9,1},{10,2},{11,3},{12,4},{13,5},{14,6},{15,7},{0,8},{1,9},... | collective-permute-start | bytes 245768 | tf_op jit(solution)/shard_map/ppermute | solution.py:50
  81.8 4.9 %collective-permute-start.34 = (bf16[8,5120]{1,0:T(8,128)(2,1)S(1)}, bf16[8,5120]{1,0:T(8,128)(2,1)S(1)}, u32[]{:S(2)}, u32[]{:S(2)}) collective-permute-start(bf16[8,5120]{1,0:T(8,128)(2,1)S(1)} %get-tuple-element.73), channel_id=1, source_target_pairs={{4,0},{5,1},{6,2},{7,3},{0,4},{1,5},{2,6},{3,7},{12,8},{13,9},{14,... | collective-permute-start | bytes 245768 | tf_op jit(solution)/shard_map/ppermute | solution.py:50
  86.7 11.2 %collective-permute-start.36 = (f32[8,5248]{1,0:T(8,128)S(1)}, f32[8,5248]{1,0:T(8,128)S(1)}, u32[]{:S(2)}, u32[]{:S(2)}) collective-permute-start(f32[8,5248]{1,0:T(8,128)S(1)} %add_last.3.back_ref), channel_id=1, source_target_pairs={{0,16},{1,17},{2,18},{3,19},{4,20},{5,21},{6,22},{7,23},{8,24},{9,... | collective-permute-start | bytes 503816 | tf_op jit(solution)/shard_map/ppermute | solution.py:17

commit v14 on v13

--- a/solution.py
+++ b/solution.py
@@ -512,19 +512,19 @@
 
         def compute():
             gate, slot = back_ref[0:1, width:], back_ref[1:2, width:]
-            gate = jnp.broadcast_to(gate, (CAP, tokens)).T[:, 0:1]
             slots = lax.broadcasted_iota(jnp.int32, (CAP, tokens), 0).astype(jnp.float32)
-            onehot = jnp.where(slot == slots, 1.0, 0.0).T
-            onehot = jnp.concatenate([onehot] * 3, axis=1).astype(jnp.bfloat16)
+            match = jnp.where(slot == slots, 1.0, 0.0)
+            gate = jnp.sum(match * gate, axis=1, keepdims=True)
+            onehot = jnp.concatenate([match.T] * 3, axis=1).astype(jnp.bfloat16)
             copies = []
             for i, columns in enumerate(parts):
-                back = back_ref[:, columns]
+                back = back_ref[:, columns] * gate
                 high = back.astype(jnp.bfloat16).astype(jnp.float32)
                 middle = (back - high).astype(jnp.bfloat16).astype(jnp.float32)
                 three = jnp.concatenate([high, middle, back - high - middle], axis=0)
                 moved = dot(onehot, three.astype(jnp.bfloat16))
                 here = res_ref[:, columns].astype(jnp.float32)
-                out_ref[:, columns] = (here + gate * moved).astype(jnp.bfloat16)
+                out_ref[:, columns] = (here + moved).astype(jnp.bfloat16)
                 copy = pltpu.make_async_copy(
                     out_ref.at[:, columns], out_any.at[:, columns], sems.at[i]
                 )

time: 99.7 us -> 99.6 us (level)
  no operation moved by 1% of the time
where the time goes in v14:
time: 99.6 us; the launch traced here: 99.4 us
  waiting for transfers between devices  44.4 us (45%)
  starting transfers between devices  42.3 us (42%)
  Pallas kernels  10.5 us (11%)
  local copies, waits for them, and re-layouts  1.24 us (1%)
    ppermute x28, waiting for transfers between devices, shift(): return lax.ppermute(block, 'expert', route)  34 us
    ppermute x28, starting transfers between devices, shift(): return lax.ppermute(block, 'expert', route)  32.5 us
    ppermute x2, waiting for transfers between devices, passed_along(): return lax.ppermute(block, axis, route)  8.48 us
    pallas_call x18, Pallas kernels, local_kernel(): pl.pallas_call(body, out_shape=tuple(outs), in_specs=in_specs, out_specs=...  7.62 us
    ppermute x5, starting transfers between devices, swapped(): lax.ppermute(block, 'section', [(i, (i + sections // 2) % sections) for i...  4.61 us
    pallas_call x2, Pallas kernels, finish(): pl.pallas_call(kernel, out_shape=one, in_specs=[pl.BlockSpec(memory_space...  2.89 us
    ppermute x2, starting transfers between devices, passed_along(): return lax.ppermute(block, axis, route)  2.57 us
    ppermute x2, starting transfers between devices, to_decoder(): lax.ppermute(block, 'section', [(i, i + apart) for i in range(apart)])  2.57 us
  transfers between devices with their start and end apart: 37, of which 19 were waited for; matrix products, arithmetic and copies ran while one was open for 0% of the time, Pallas kernels for 7%

profile of v14, /device:TPU:1, one launch (start us, length us, event | category | flops | bytes accessed | tf_op | source)
XLA Modules:
  0.0 99.4 jit_solution(6555828199906594477)
XLA Ops:
  0.7 1.1 %slice_bitcast_fusion = (bf16[1,8,2,2560]{3,2,1,0:T(2,128)(2,1)S(1)}, bf16[1,8,2,2560]{3,2,1,0:T(2,128)(2,1)S(1)}) fusion(bf16[1,8,2,5120]{3,2,1,0:T(2,128)(2,1)} %param.10), kind=kLoop, calls=%fused_computation | loop fusion | bytes 327680
  1.8 0.1 collective-permute-start
  2.0 1.2 %collective-permute-done = bf16[8,5120]{1,0:T(8,128)(2,1)S(1)} collective-permute-done((bf16[8,5120]{1,0:T(8,128)(2,1)S(1)}, bf16[8,5120]{1,0:T(8,128)(2,1)S(1)}, u32[]{:S(2)}, u32[]{:S(2)}) %collective-permute-start) | collective-permute-done | bytes 81952 | tf_op jit(solution)/shard_map/ppermute | solution.py:22
  3.2 4.5 %collective-permute-start.3 = (bf16[8,5120]{1,0:T(8,128)(2,1)S(1)}, bf16[8,5120]{1,0:T(8,128)(2,1)S(1)}, u32[]{:S(2)}, u32[]{:S(2)}) collective-permute-start(bf16[8,5120]{1,0:T(8,128)(2,1)S(1)} %broadcast_select_fusion.refs_0_), channel_id=1, source_target_pairs={{0,12},{1,13},{2,14},{3,15},{4,8},{5,9},{6,10},{7,11},{8,4},{9,5},... | collective-permute-start | bytes 245768 | tf_op jit(solution)/shard_map/ppermute | solution.py:50
  7.7 0.4 collective-permute-start.1
  8.1 2.2 %collective-permute-done.3.refs_3_ = bf16[8,5120]{1,0:T(8,128)(2,1)S(1)} collective-permute-done((bf16[8,5120]{1,0:T(8,128)(2,1)S(1)}, bf16[8,5120]{1,0:T(8,128)(2,1)S(1)}, u32[]{:S(2)}, u32[]{:S(2)}) %collective-permute-start.3) | collective-permute-done | bytes 81952 | tf_op jit(solution)/shard_map/ppermute | solution.py:50
  10.3 4.1 %collective-permute-done.2.refs_2_ = bf16[8,5120]{1,0:T(8,128)(2,1)S(1)} collective-permute-done((bf16[8,5120]{1,0:T(8,128)(2,1)S(1)}, bf16[8,5120]{1,0:T(8,128)(2,1)S(1)}, u32[]{:S(2)}, u32[]{:S(2)}) %collective-permute-start.2) | collective-permute-done | bytes 81952 | tf_op jit(solution)/shard_map/ppermute | solution.py:50
  14.4 1.3 %collective-permute-start.7 = (bf16[32,5120]{1,0:T(8,128)(2,1)S(1)}, bf16[32,5120]{1,0:T(8,128)(2,1)S(1)}, u32[]{:S(2)}, u32[]{:S(2)}) collective-permute-start(bf16[32,5120]{1,0:T(8,128)(2,1)S(1)} %join.2.refs_4_), channel_id=1, source_target_pairs={{0,2},{1,3},{2,0},{3,1},{4,6},{5,7},{6,4},{7,5},{8,10},{9,11},{10,... | collective-permute-start | bytes 983048 | tf_op jit(solution)/shard_map/ppermute | solution.py:50
  15.7 1.2 %collective-permute-start.6 = (bf16[32,5120]{1,0:T(8,128)(2,1)S(1)}, bf16[32,5120]{1,0:T(8,128)(2,1)S(1)}, u32[]{:S(2)}, u32[]{:S(2)}) collective-permute-start(bf16[32,5120]{1,0:T(8,128)(2,1)S(1)} %join.2.refs_4_), channel_id=1, source_target_pairs={{0,1},{1,0},{2,3},{3,2},{4,5},{5,4},{6,7},{7,6},{8,9},{9,8},{10,11... | collective-permute-start | bytes 983048 | tf_op jit(solution)/shard_map/ppermute | solution.py:50
  16.9 0.9 queries.1
  17.8 1.8 %collective-permute-start.4 = (bf16[128,1280]{1,0:T(8,128)(2,1)S(1)}, bf16[128,1280]{1,0:T(8,128)(2,1)S(1)}, u32[]{:S(2)}, u32[]{:S(2)}) collective-permute-start(bf16[128,1280]{1,0:T(8,128)(2,1)S(1)} %get-tuple-element.41), channel_id=1, source_target_pairs={{0,16},{16,0},{1,17},{17,1},{2,18},{18,2},{3,19},{19,3},{4,20},{20... | collective-permute-start | bytes 983048 | tf_op jit(solution)/shard_map/ppermute | solution.py:22
  19.6 0.1 collective-permute-start.5
  19.7 0.1 cut.1
  19.8 0.5 collective-permute-start.10
  20.3 2.2 %collective-permute-done.7.refs_6_ = bf16[32,5120]{1,0:T(8,128)(2,1)S(1)} collective-permute-done((bf16[32,5120]{1,0:T(8,128)(2,1)S(1)}, bf16[32,5120]{1,0:T(8,128)(2,1)S(1)}, u32[]{:S(2)}, u32[]{:S(2)}) %collective-permute-start.7) | collective-permute-done | bytes 327712 | tf_op jit(solution)/shard_map/ppermute | solution.py:50
  22.5 2.1 %collective-permute-start.11 = (bf16[128,1280]{1,0:T(8,128)(2,1)S(1)}, bf16[128,1280]{1,0:T(8,128)(2,1)S(1)}, u32[]{:S(2)}, u32[]{:S(2)}) collective-permute-start(bf16[128,1280]{1,0:T(8,128)(2,1)S(1)} %get-tuple-element.46), channel_id=1, source_target_pairs={{0,16},{16,0},{1,17},{17,1},{2,18},{18,2},{3,19},{19,3},{4,20},{20... | collective-permute-start | bytes 983048 | tf_op jit(solution)/shard_map/ppermute | solution.py:22
  24.6 1.3 %collective-permute-start.8 = (bf16[16,5120]{1,0:T(8,128)(2,1)S(1)}, bf16[16,5120]{1,0:T(8,128)(2,1)S(1)}, u32[]{:S(2)}, u32[]{:S(2)}) collective-permute-start(bf16[16,5120]{1,0:T(8,128)(2,1)S(1)} %slice.16), channel_id=1, source_target_pairs={{0,1},{1,0},{2,3},{3,2},{4,5},{5,4},{6,7},{7,6},{8,9},{9,8},{10,11... | collective-permute-start | bytes 491528 | tf_op jit(solution)/shard_map/ppermute | solution.py:50
  25.9 1.3 %collective-permute-start.9 = (bf16[16,5120]{1,0:T(8,128)(2,1)S(1)}, bf16[16,5120]{1,0:T(8,128)(2,1)S(1)}, u32[]{:S(2)}, u32[]{:S(2)}) collective-permute-start(bf16[16,5120]{1,0:T(8,128)(2,1)S(1)} %slice.17), channel_id=1, source_target_pairs={{0,2},{1,3},{2,0},{3,1},{4,6},{5,7},{6,4},{7,5},{8,10},{9,11},{10,... | collective-permute-start | bytes 491528 | tf_op jit(solution)/shard_map/ppermute | solution.py:50
  27.2 1.3 %collective-permute-start.24 = (bf16[128,5120]{1,0:T(8,128)(2,1)S(1)}, bf16[128,5120]{1,0:T(8,128)(2,1)S(1)}, u32[]{:S(2)}, u32[]{:S(2)}) collective-permute-start(bf16[128,5120]{1,0:T(8,128)(2,1)S(1)} %get-tuple-element.40.refs_1_), channel_id=1, source_target_pairs={{0,16},{1,17},{2,18},{3,19},{4,20},{5,21},{6,22},{7,23},{8,24},{9,... | collective-permute-start | bytes 3932168 | tf_op jit(solution)/shard_map/ppermute | solution.py:17
  28.5 0.7 collective-permute-done.8.refs_7_
  29.2 1.2 %collective-permute-done.9.refs_8_ = bf16[16,5120]{1,0:T(8,128)(2,1)S(1)} collective-permute-done((bf16[16,5120]{1,0:T(8,128)(2,1)S(1)}, bf16[16,5120]{1,0:T(8,128)(2,1)S(1)}, u32[]{:S(2)}, u32[]{:S(2)}) %collective-permute-start.9) | collective-permute-done | bytes 163872 | tf_op jit(solution)/shard_map/ppermute | solution.py:50
  30.4 1.0 %attend.1 = (bf16[128,2560]{1,0:T(8,128)(2,1)S(1)}, f32[20,128,128]{2,1,0:T(8,128)S(1)}, bf16[128,2560]{1,0:T(8,128)(2,1)S(1)}) custom-call(s32[1]{0:T(128)} %bitcast.refs_0_.section, bf16[128,1280]{1,0:T(8,128)(2,1)S(1)} %collective-permute-done.4.refs_1_, bf16[128,1280]{1,0:T(8,128)(2,1)S(1)} %collective-permute-done.5.refs_2_, ...), custom_call_target="tpu_custom_call" | custom-call | flops 167772160 | bytes 5242884 | tf_op jit(solution)/shard_map/attend/pallas_call | solution.py:143
  31.5 1.3 %collective-permute-start.12 = (bf16[128,2560]{1,0:T(8,128)(2,1)S(1)}, bf16[128,2560]{1,0:T(8,128)(2,1)S(1)}, u32[]{:S(2)}, u32[]{:S(2)}) collective-permute-start(bf16[128,2560]{1,0:T(8,128)(2,1)S(1)} %get-tuple-element.47.refs_3_), channel_id=1, source_target_pairs={{0,16},{1,17},{2,18},{3,19},{4,20},{5,21},{6,22},{7,23},{8,24},{9,... | collective-permute-start | bytes 1966088 | tf_op jit(solution)/shard_map/ppermute | solution.py:27
  32.8 1.3 %gradient.1 = (f32[32,5120]{1,0:T(8,128)S(1)}, f32[32,5120]{1,0:T(8,128)S(1)}, f32[32,5120]{1,0:T(8,128)S(1)}, bf16[16,5120]{1,0:T(8,128)(2,1)S(1)}, bf16[16,5120]{1,0:T(8,128)(2,1)S(1)}) custom-call(s32[1]{0:T(128)} %bitcast.refs_0_.section, bf16[128,2560]{1,0:T(8,128)(2,1)S(1)} %get-tuple-element.48.q_ref, ...), custom_call_target="tpu_custom_call" | custom-call | flops 419430400 | bytes 6881284 | tf_op jit(solution)/shard_map/gradient/pallas_call | solution.py:143
  34.1 2.2 %collective-permute-start.17 = (bf16[16,5120]{1,0:T(8,128)(2,1)S(1)}, bf16[16,5120]{1,0:T(8,128)(2,1)S(1)}, u32[]{:S(2)}, u32[]{:S(2)}) collective-permute-start(bf16[16,5120]{1,0:T(8,128)(2,1)S(1)} %get-tuple-element.57), channel_id=1, source_target_pairs={{2,0},{3,1},{0,2},{1,3},{6,4},{7,5},{4,6},{5,7},{10,8},{11,9},{8,1... | collective-permute-start | bytes 491528 | tf_op jit(solution)/shard_map/ppermute | solution.py:50
  36.3 0.3 collective-permute-start.16
  36.6 0.1 collective-permute-done.12.refs_2_
  36.6 0.6 settle.1
  37.3 2.4 %collective-permute-start.15 = (bf16[8,5120]{1,0:T(8,128)(2,1)S(1)}, bf16[8,5120]{1,0:T(8,128)(2,1)S(1)}, u32[]{:S(2)}, u32[]{:S(2)}) collective-permute-start(bf16[8,5120]{1,0:T(8,128)(2,1)S(1)} %get-tuple-element.53.refs_0_.after_any), channel_id=1, source_target_pairs={{0,12},{1,13},{2,14},{3,15},{4,8},{5,9},{6,10},{7,11},{8,4},{9,5},... | collective-permute-start | bytes 245768 | tf_op jit(solution)/shard_map/ppermute | solution.py:50
  39.7 1.2 %collective-permute-start.13 = (bf16[8,5120]{1,0:T(8,128)(2,1)S(1)}, bf16[8,5120]{1,0:T(8,128)(2,1)S(1)}, u32[]{:S(2)}, u32[]{:S(2)}) collective-permute-start(bf16[8,5120]{1,0:T(8,128)(2,1)S(1)} %get-tuple-element.53.refs_0_.after_any), channel_id=1, source_target_pairs={{0,4},{1,5},{2,6},{3,7},{4,0},{5,1},{6,2},{7,3},{8,12},{9,13},{10,... | collective-permute-start | bytes 245768 | tf_op jit(solution)/shard_map/ppermute | solution.py:50
  41.0 1.2 %collective-permute-start.21 = (bf16[32,5120]{1,0:T(8,128)(2,1)S(1)}, bf16[32,5120]{1,0:T(8,128)(2,1)S(1)}, u32[]{:S(2)}, u32[]{:S(2)}) collective-permute-start(bf16[32,5120]{1,0:T(8,128)(2,1)S(1)} %add_half.5.refs_5_), channel_id=1, source_target_pairs={{1,0},{0,1},{3,2},{2,3},{5,4},{4,5},{7,6},{6,7},{9,8},{8,9},{11,10... | collective-permute-start | bytes 983048 | tf_op jit(solution)/shard_map/ppermute | solution.py:50
  42.2 0.2 collective-permute-done.15.refs_3_
  42.5 1.2 %collective-permute-start.20 = (bf16[32,5120]{1,0:T(8,128)(2,1)S(1)}, bf16[32,5120]{1,0:T(8,128)(2,1)S(1)}, u32[]{:S(2)}, u32[]{:S(2)}) collective-permute-start(bf16[32,5120]{1,0:T(8,128)(2,1)S(1)} %add_half.4.refs_4_), channel_id=1, source_target_pairs={{2,0},{3,1},{0,2},{1,3},{6,4},{7,5},{4,6},{5,7},{10,8},{11,9},{8,1... | collective-permute-start | bytes 983048 | tf_op jit(solution)/shard_map/ppermute | solution.py:50
  43.7 3.5 %collective-permute-done.14.refs_2_ = bf16[8,5120]{1,0:T(8,128)(2,1)S(1)} collective-permute-done((bf16[8,5120]{1,0:T(8,128)(2,1)S(1)}, bf16[8,5120]{1,0:T(8,128)(2,1)S(1)}, u32[]{:S(2)}, u32[]{:S(2)}) %collective-permute-start.14) | collective-permute-done | bytes 81952 | tf_op jit(solution)/shard_map/ppermute | solution.py:50
  47.2 1.2 %collective-permute-start.19 = (bf16[32,5120]{1,0:T(8,128)(2,1)S(1)}, bf16[32,5120]{1,0:T(8,128)(2,1)S(1)}, u32[]{:S(2)}, u32[]{:S(2)}) collective-permute-start(bf16[32,5120]{1,0:T(8,128)(2,1)S(1)} %join.3.refs_3_.refs_2_), channel_id=1, source_target_pairs={{0,2},{1,3},{2,0},{3,1},{4,6},{5,7},{6,4},{7,5},{8,10},{9,11},{10,... | collective-permute-start | bytes 983048 | tf_op jit(solution)/shard_map/ppermute | solution.py:50
  48.4 0.2 collective-permute-start.18
  48.6 0.1 collective-permute-done.20.refs_1_
  48.7 0.1 add_blocks.2
  48.8 8.2 %collective-permute-done.19.refs_0_.refs_4_ = bf16[32,5120]{1,0:T(8,128)(2,1)S(1)} collective-permute-done((bf16[32,5120]{1,0:T(8,128)(2,1)S(1)}, bf16[32,5120]{1,0:T(8,128)(2,1)S(1)}, u32[]{:S(2)}, u32[]{:S(2)}) %collective-permute-start.19) | collective-permute-done | bytes 327712 | tf_op jit(solution)/shard_map/ppermute | solution.py:50
  57.0 1.2 %collective-permute-start.22 = (bf16[16,5120]{1,0:T(8,128)(2,1)S(1)}, bf16[16,5120]{1,0:T(8,128)(2,1)S(1)}, u32[]{:S(2)}, u32[]{:S(2)}) collective-permute-start(bf16[16,5120]{1,0:T(8,128)(2,1)S(1)} %get-tuple-element.59), channel_id=1, source_target_pairs={{0,1},{1,0},{2,3},{3,2},{4,5},{5,4},{6,7},{7,6},{8,9},{9,8},{10,11... | collective-permute-start | bytes 491528 | tf_op jit(solution)/shard_map/ppermute | solution.py:50
  58.2 0.2 collective-permute-start.23
  58.4 2.5 %collective-permute-start.26 = (bf16[8,5120]{1,0:T(8,128)(2,1)S(1)}, bf16[8,5120]{1,0:T(8,128)(2,1)S(1)}, u32[]{:S(2)}, u32[]{:S(2)}) collective-permute-start(bf16[8,5120]{1,0:T(8,128)(2,1)S(1)} %get-tuple-element.62), channel_id=1, source_target_pairs={{8,0},{9,1},{10,2},{11,3},{12,4},{13,5},{14,6},{15,7},{0,8},{1,9},... | collective-permute-start | bytes 245768 | tf_op jit(solution)/shard_map/ppermute | solution.py:50
  60.9 0.8 collective-permute-done.25.refs_8_.refs_1_
  61.7 1.0 %collective-permute-done.26.refs_9_.refs_2_ = bf16[8,5120]{1,0:T(8,128)(2,1)S(1)} collective-permute-done((bf16[8,5120]{1,0:T(8,128)(2,1)S(1)}, bf16[8,5120]{1,0:T(8,128)(2,1)S(1)}, u32[]{:S(2)}, u32[]{:S(2)}) %collective-permute-start.26) | collective-permute-done | bytes 81952 | tf_op jit(solution)/shard_map/ppermute | solution.py:50
  62.7 2.3 %expert.1 = (f32[32,5120]{1,0:T(8,128)S(1)}, f32[32,5120]{1,0:T(8,128)S(1)}, f32[32,5120]{1,0:T(8,128)S(1)}, bf16[16,5120]{1,0:T(8,128)(2,1)S(1)}, bf16[16,5120]{1,0:T(8,128)(2,1)S(1)}) custom-call(bf16[5120,640]{1,0:T(8,128)(2,1)S(1)} %bitcast.18, bf16[640,5120]{1,0:T(8,128)(2,1)S(1)} %bitcast.19, bf16[32,5120]{1,0:T(8,128)(2,1)S(1)} %join.3.refs_3_.refs_2_, ...), custom_call_target="tpu_custom_call" | custom-call | flops 1677721600 | bytes 16711680 | tf_op jit(solution)/shard_map/expert/pallas_call | solution.py:143
  65.1 1.4 %collective-permute-start.30 = (bf16[16,5120]{1,0:T(8,128)(2,1)S(1)}, bf16[16,5120]{1,0:T(8,128)(2,1)S(1)}, u32[]{:S(2)}, u32[]{:S(2)}) collective-permute-start(bf16[16,5120]{1,0:T(8,128)(2,1)S(1)} %get-tuple-element.68), channel_id=1, source_target_pairs={{2,0},{3,1},{0,2},{1,3},{6,4},{7,5},{4,6},{5,7},{10,8},{11,9},{8,1... | collective-permute-start | bytes 491528 | tf_op jit(solution)/shard_map/ppermute | solution.py:50
  66.4 0.2 collective-permute-start.27
  66.6 2.0 %collective-permute-start.28 = (bf16[8,5120]{1,0:T(8,128)(2,1)S(1)}, bf16[8,5120]{1,0:T(8,128)(2,1)S(1)}, u32[]{:S(2)}, u32[]{:S(2)}) collective-permute-start(bf16[8,5120]{1,0:T(8,128)(2,1)S(1)} %get-tuple-element.66), channel_id=1, source_target_pairs={{12,0},{13,1},{14,2},{15,3},{8,4},{9,5},{10,6},{11,7},{4,8},{5,9},... | collective-permute-start | bytes 245768 | tf_op jit(solution)/shard_map/ppermute | solution.py:50
  68.7 3.1 %collective-permute-done.28.refs_3_ = bf16[8,5120]{1,0:T(8,128)(2,1)S(1)} collective-permute-done((bf16[8,5120]{1,0:T(8,128)(2,1)S(1)}, bf16[8,5120]{1,0:T(8,128)(2,1)S(1)}, u32[]{:S(2)}, u32[]{:S(2)}) %collective-permute-start.28) | collective-permute-done | bytes 81952 | tf_op jit(solution)/shard_map/ppermute | solution.py:50
  71.9 1.3 %collective-permute-start.31 = (bf16[32,5120]{1,0:T(8,128)(2,1)S(1)}, bf16[32,5120]{1,0:T(8,128)(2,1)S(1)}, u32[]{:S(2)}, u32[]{:S(2)}) collective-permute-start(bf16[32,5120]{1,0:T(8,128)(2,1)S(1)} %add_half.7), channel_id=1, source_target_pairs={{1,0},{0,1},{3,2},{2,3},{5,4},{4,5},{7,6},{6,7},{9,8},{8,9},{11,10... | collective-permute-start | bytes 983048 | tf_op jit(solution)/shard_map/ppermute | solution.py:50
  73.3 0.2 collective-permute-start.29
  73.6 1.3 %collective-permute-start.35 = (f32[8,5120]{1,0:T(8,128)S(1)}, f32[8,5120]{1,0:T(8,128)S(1)}, u32[]{:S(2)}, u32[]{:S(2)}) collective-permute-start(f32[8,5120]{1,0:T(8,128)S(1)} %add_last.2.refs_2_.second_ref), channel_id=1, source_target_pairs={{0,16},{1,17},{2,18},{3,19},{4,20},{5,21},{6,22},{7,23},{8,24},{9,... | collective-permute-start | bytes 491528 | tf_op jit(solution)/shard_map/ppermute | solution.py:27
  74.9 4.7 %collective-permute-done.31.refs_2_ = bf16[32,5120]{1,0:T(8,128)(2,1)S(1)} collective-permute-done((bf16[32,5120]{1,0:T(8,128)(2,1)S(1)}, bf16[32,5120]{1,0:T(8,128)(2,1)S(1)}, u32[]{:S(2)}, u32[]{:S(2)}) %collective-permute-start.31) | collective-permute-done | bytes 327712 | tf_op jit(solution)/shard_map/ppermute | solution.py:50
  79.6 0.1 add_blocks.3
  79.8 2.0 %collective-permute-start.32 = (bf16[8,5120]{1,0:T(8,128)(2,1)S(1)}, bf16[8,5120]{1,0:T(8,128)(2,1)S(1)}, u32[]{:S(2)}, u32[]{:S(2)}) collective-permute-start(bf16[8,5120]{1,0:T(8,128)(2,1)S(1)} %get-tuple-element.71), channel_id=1, source_target_pairs={{12,0},{13,1},{14,2},{15,3},{8,4},{9,5},{10,6},{11,7},{4,8},{5,9},... | collective-permute-start | bytes 245768 | tf_op jit(solution)/shard_map/ppermute | solution.py:50
  81.8 1.6 %collective-permute-start.34 = (bf16[8,5120]{1,0:T(8,128)(2,1)S(1)}, bf16[8,5120]{1,0:T(8,128)(2,1)S(1)}, u32[]{:S(2)}, u32[]{:S(2)}) collective-permute-start(bf16[8,5120]{1,0:T(8,128)(2,1)S(1)} %get-tuple-element.73), channel_id=1, source_target_pairs={{4,0},{5,1},{6,2},{7,3},{0,4},{1,5},{2,6},{3,7},{12,8},{13,9},{14,... | collective-permute-start | bytes 245768 | tf_op jit(solution)/shard_map/ppermute | solution.py:50
  83.4 0.6 collective-permute-done.35.first_ref
  84.0 0.8 lay_out.1
  84.8 0.2 collective-permute-done.32.refs_1_
  85.0 1.7 %collective-permute-done.33.refs_2_ = bf16[8,5120]{1,0:T(8,128)(2,1)S(1)} collective-permute-done((bf16[8,5120]{1,0:T(8,128)(2,1)S(1)}, bf16[8,5120]{1,0:T(8,128)(2,1)S(1)}, u32[]{:S(2)}, u32[]{:S(2)}) %collective-permute-start.33) | collective-permute-done | bytes 81952 | tf_op jit(solution)/shard_map/ppermute | solution.py:50
  86.7 1.3 %collective-permute-start.36 = (f32[8,5248]{1,0:T(8,128)S(1)}, f32[8,5248]{1,0:T(8,128)S(1)}, u32[]{:S(2)}, u32[]{:S(2)}) collective-permute-start(f32[8,5248]{1,0:T(8,128)S(1)} %add_last.3.back_ref), channel_id=1, source_target_pairs={{0,16},{1,17},{2,18},{3,19},{4,20},{5,21},{6,22},{7,23},{8,24},{9,... | collective-permute-start | bytes 503816 | tf_op jit(solution)/shard_map/ppermute | solution.py:17
  88.0 1.4 %finish.2 = bf16[128,5120]{1,0:T(8,128)(2,1)} custom-call(s32[1]{0:T(128)} %bitcast.refs_0_.section, bf16[128,5120]{1,0:T(8,128)(2,1)S(1)} %get-tuple-element.52.res_ref, f32[8,5248]{1,0:T(8,128)S(1)} %add_last.3.back_ref), custom_call_target="tpu_custom_call" | custom-call | flops 32768000 | bytes 3276800 | tf_op jit(solution)/shard_map/finish/pallas_call | solution.py:542
  89.5 8.5 %collective-permute-done.36.back_ref = f32[8,5248]{1,0:T(8,128)S(1)} collective-permute-done((f32[8,5248]{1,0:T(8,128)S(1)}, f32[8,5248]{1,0:T(8,128)S(1)}, u32[]{:S(2)}, u32[]{:S(2)}) %collective-permute-start.36) | collective-permute-done | bytes 167968 | tf_op jit(solution)/shard_map/ppermute | solution.py:17
  98.0 1.4 %finish.3 = bf16[128,5120]{1,0:T(8,128)(2,1)} custom-call(s32[1]{0:T(128)} %bitcast.refs_0_.section, bf16[128,5120]{1,0:T(8,128)(2,1)S(1)} %collective-permute-done.24.refs_7_.res_ref, f32[8,5248]{1,0:T(8,128)S(1)} %collective-permute-done.36.back_ref, bf16[128,5120]{1,0:T(8,128)(2,1)} %get-tuple-element.75.refs_0_), custom_call_target="tpu_custom_call", output_to_operand_aliasing={{}: (3, {})} | custom-call | flops 32768000 | bytes 3276800 | tf_op jit(solution)/shard_map/finish/pallas_call | solution.py:542
  (56 shorter events, 0.5 us)
Async XLA Ops:
  0.6 16.3 %copy-start.5 = (f32[1,128]{1,0:T(1,128)S(1)}, f32[1,128]{1,0:T(1,128)}, u32[]{:S(2)}) copy-start(f32[1,128]{1,0:T(1,128)} %refs_2_.1) | copy-start | bytes 1540
  0.6 16.3 %copy-start.6 = (s32[1,128]{1,0:T(1,128)S(1)}, s32[1,128]{1,0:T(1,128)}, u32[]{:S(2)}) copy-start(s32[1,128]{1,0:T(1,128)} %refs_3_.1) | copy-start | bytes 1540
  0.7 16.3 %copy-start.4 = (f32[1,5120]{1,0:T(1,128)S(1)}, f32[1,5120]{1,0:T(1,128)}, u32[]{:S(2)}) copy-start(f32[1,5120]{1,0:T(1,128)} %refs_1_.1) | copy-start | bytes 61444
  0.7 16.3 %copy-start.1 = (bf16[1,128,5120]{2,1,0:T(8,128)(2,1)S(1)}, bf16[1,128,5120]{2,1,0:T(8,128)(2,1)}, u32[]{:S(2)}) copy-start(bf16[1,128,5120]{2,1,0:T(8,128)(2,1)} %param.9) | copy-start | bytes 3932164
  1.8 1.3 %collective-permute-start = (bf16[8,5120]{1,0:T(8,128)(2,1)S(1)}, bf16[8,5120]{1,0:T(8,128)(2,1)S(1)}, u32[]{:S(2)}, u32[]{:S(2)}) collective-permute-start(bf16[8,5120]{1,0:T(8,128)(2,1)S(1)} %bitcast.25), channel_id=1, source_target_pairs={{0,16},{16,0},{1,17},{17,1},{2,18},{18,2},{3,19},{19,3},{4,20},{20... | collective-permute-start | bytes 245768 | tf_op jit(solution)/shard_map/ppermute | solution.py:22
  2.0 17.7 %copy-start.2 = (bf16[1,128,5120]{2,1,0:T(8,128)(2,1)S(1)}, bf16[1,128,5120]{2,1,0:T(8,128)(2,1)}, u32[]{:S(2)}) copy-start(bf16[1,128,5120]{2,1,0:T(8,128)(2,1)} %param.11) | copy-start | bytes 3932164
  3.2 7.1 %collective-permute-start.3 = (bf16[8,5120]{1,0:T(8,128)(2,1)S(1)}, bf16[8,5120]{1,0:T(8,128)(2,1)S(1)}, u32[]{:S(2)}, u32[]{:S(2)}) collective-permute-start(bf16[8,5120]{1,0:T(8,128)(2,1)S(1)} %broadcast_select_fusion.refs_0_), channel_id=1, source_target_pairs={{0,12},{1,13},{2,14},{3,15},{4,8},{5,9},{6,10},{7,11},{8,4},{9,5},... | collective-permute-start | bytes 245768 | tf_op jit(solution)/shard_map/ppermute | solution.py:50
  7.7 6.6 %collective-permute-start.2 = (bf16[8,5120]{1,0:T(8,128)(2,1)S(1)}, bf16[8,5120]{1,0:T(8,128)(2,1)S(1)}, u32[]{:S(2)}, u32[]{:S(2)}) collective-permute-start(bf16[8,5120]{1,0:T(8,128)(2,1)S(1)} %broadcast_select_fusion.refs_0_), channel_id=1, source_target_pairs={{0,8},{1,9},{2,10},{3,11},{4,12},{5,13},{6,14},{7,15},{8,0},{9,1},... | collective-permute-start | bytes 245768 | tf_op jit(solution)/shard_map/ppermute | solution.py:50
  7.7 6.6 %collective-permute-start.1 = (bf16[8,5120]{1,0:T(8,128)(2,1)S(1)}, bf16[8,5120]{1,0:T(8,128)(2,1)S(1)}, u32[]{:S(2)}, u32[]{:S(2)}) collective-permute-start(bf16[8,5120]{1,0:T(8,128)(2,1)S(1)} %broadcast_select_fusion.refs_0_), channel_id=1, source_target_pairs={{0,4},{1,5},{2,6},{3,7},{4,0},{5,1},{6,2},{7,3},{8,12},{9,13},{10,... | collective-permute-start | bytes 245768 | tf_op jit(solution)/shard_map/ppermute | solution.py:50
  14.4 8.1 %collective-permute-start.7 = (bf16[32,5120]{1,0:T(8,128)(2,1)S(1)}, bf16[32,5120]{1,0:T(8,128)(2,1)S(1)}, u32[]{:S(2)}, u32[]{:S(2)}) collective-permute-start(bf16[32,5120]{1,0:T(8,128)(2,1)S(1)} %join.2.refs_4_), channel_id=1, source_target_pairs={{0,2},{1,3},{2,0},{3,1},{4,6},{5,7},{6,4},{7,5},{8,10},{9,11},{10,... | collective-permute-start | bytes 983048 | tf_op jit(solution)/shard_map/ppermute | solution.py:50
  15.7 8.9 %collective-permute-start.6 = (bf16[32,5120]{1,0:T(8,128)(2,1)S(1)}, bf16[32,5120]{1,0:T(8,128)(2,1)S(1)}, u32[]{:S(2)}, u32[]{:S(2)}) collective-permute-start(bf16[32,5120]{1,0:T(8,128)(2,1)S(1)} %join.2.refs_4_), channel_id=1, source_target_pairs={{0,1},{1,0},{2,3},{3,2},{4,5},{5,4},{6,7},{7,6},{8,9},{9,8},{10,11... | collective-permute-start | bytes 983048 | tf_op jit(solution)/shard_map/ppermute | solution.py:50
  17.8 8.1 %collective-permute-start.4 = (bf16[128,1280]{1,0:T(8,128)(2,1)S(1)}, bf16[128,1280]{1,0:T(8,128)(2,1)S(1)}, u32[]{:S(2)}, u32[]{:S(2)}) collective-permute-start(bf16[128,1280]{1,0:T(8,128)(2,1)S(1)} %get-tuple-element.41), channel_id=1, source_target_pairs={{0,16},{16,0},{1,17},{17,1},{2,18},{18,2},{3,19},{19,3},{4,20},{20... | collective-permute-start | bytes 983048 | tf_op jit(solution)/shard_map/ppermute | solution.py:22
  19.6 7.6 %collective-permute-start.5 = (bf16[128,1280]{1,0:T(8,128)(2,1)S(1)}, bf16[128,1280]{1,0:T(8,128)(2,1)S(1)}, u32[]{:S(2)}, u32[]{:S(2)}) collective-permute-start(bf16[128,1280]{1,0:T(8,128)(2,1)S(1)} %get-tuple-element.42), channel_id=1, source_target_pairs={{0,16},{16,0},{1,17},{17,1},{2,18},{18,2},{3,19},{19,3},{4,20},{20... | collective-permute-start | bytes 983048 | tf_op jit(solution)/shard_map/ppermute | solution.py:22
  19.8 8.7 %collective-permute-start.10 = (bf16[128,1280]{1,0:T(8,128)(2,1)S(1)}, bf16[128,1280]{1,0:T(8,128)(2,1)S(1)}, u32[]{:S(2)}, u32[]{:S(2)}) collective-permute-start(bf16[128,1280]{1,0:T(8,128)(2,1)S(1)} %get-tuple-element.45), channel_id=1, source_target_pairs={{0,16},{16,0},{1,17},{17,1},{2,18},{18,2},{3,19},{19,3},{4,20},{20... | collective-permute-start | bytes 983048 | tf_op jit(solution)/shard_map/ppermute | solution.py:22
  22.5 6.0 %collective-permute-start.11 = (bf16[128,1280]{1,0:T(8,128)(2,1)S(1)}, bf16[128,1280]{1,0:T(8,128)(2,1)S(1)}, u32[]{:S(2)}, u32[]{:S(2)}) collective-permute-start(bf16[128,1280]{1,0:T(8,128)(2,1)S(1)} %get-tuple-element.46), channel_id=1, source_target_pairs={{0,16},{16,0},{1,17},{17,1},{2,18},{18,2},{3,19},{19,3},{4,20},{20... | collective-permute-start | bytes 983048 | tf_op jit(solution)/shard_map/ppermute | solution.py:22
  24.6 4.6 %collective-permute-start.8 = (bf16[16,5120]{1,0:T(8,128)(2,1)S(1)}, bf16[16,5120]{1,0:T(8,128)(2,1)S(1)}, u32[]{:S(2)}, u32[]{:S(2)}) collective-permute-start(bf16[16,5120]{1,0:T(8,128)(2,1)S(1)} %slice.16), channel_id=1, source_target_pairs={{0,1},{1,0},{2,3},{3,2},{4,5},{5,4},{6,7},{7,6},{8,9},{9,8},{10,11... | collective-permute-start | bytes 491528 | tf_op jit(solution)/shard_map/ppermute | solution.py:50
  25.9 4.5 %collective-permute-start.9 = (bf16[16,5120]{1,0:T(8,128)(2,1)S(1)}, bf16[16,5120]{1,0:T(8,128)(2,1)S(1)}, u32[]{:S(2)}, u32[]{:S(2)}) collective-permute-start(bf16[16,5120]{1,0:T(8,128)(2,1)S(1)} %slice.17), channel_id=1, source_target_pairs={{0,2},{1,3},{2,0},{3,1},{4,6},{5,7},{6,4},{7,5},{8,10},{9,11},{10,... | collective-permute-start | bytes 491528 | tf_op jit(solution)/shard_map/ppermute | solution.py:50
  27.2 33.7 %collective-permute-start.24 = (bf16[128,5120]{1,0:T(8,128)(2,1)S(1)}, bf16[128,5120]{1,0:T(8,128)(2,1)S(1)}, u32[]{:S(2)}, u32[]{:S(2)}) collective-permute-start(bf16[128,5120]{1,0:T(8,128)(2,1)S(1)} %get-tuple-element.40.refs_1_), channel_id=1, source_target_pairs={{0,16},{1,17},{2,18},{3,19},{4,20},{5,21},{6,22},{7,23},{8,24},{9,... | collective-permute-start | bytes 3932168 | tf_op jit(solution)/shard_map/ppermute | solution.py:17
  31.5 5.1 %collective-permute-start.12 = (bf16[128,2560]{1,0:T(8,128)(2,1)S(1)}, bf16[128,2560]{1,0:T(8,128)(2,1)S(1)}, u32[]{:S(2)}, u32[]{:S(2)}) collective-permute-start(bf16[128,2560]{1,0:T(8,128)(2,1)S(1)} %get-tuple-element.47.refs_3_), channel_id=1, source_target_pairs={{0,16},{1,17},{2,18},{3,19},{4,20},{5,21},{6,22},{7,23},{8,24},{9,... | collective-permute-start | bytes 1966088 | tf_op jit(solution)/shard_map/ppermute | solution.py:27
  32.8 3.9 %copy-start.3 = (f32[1,5120]{1,0:T(1,128)S(1)}, f32[1,5120]{1,0:T(1,128)}, u32[]{:S(2)}) copy-start(f32[1,5120]{1,0:T(1,128)} %refs_4_.1) | copy-start | bytes 61444
  32.8 29.9 %slice-start = ((s8[6553600]{0:T(1024)(128)(4,1)}), s8[4194304]{0:T(1024)(128)(4,1)S(1)}, s32[]{:S(2)}) async-start(s8[6553600]{0:T(1024)(128)(4,1)} %bitcast.16), calls=%async_computation | async-start | bytes 8388608
  34.1 5.5 %collective-permute-start.17 = (bf16[16,5120]{1,0:T(8,128)(2,1)S(1)}, bf16[16,5120]{1,0:T(8,128)(2,1)S(1)}, u32[]{:S(2)}, u32[]{:S(2)}) collective-permute-start(bf16[16,5120]{1,0:T(8,128)(2,1)S(1)} %get-tuple-element.57), channel_id=1, source_target_pairs={{2,0},{3,1},{0,2},{1,3},{6,4},{7,5},{4,6},{5,7},{10,8},{11,9},{8,1... | collective-permute-start | bytes 491528 | tf_op jit(solution)/shard_map/ppermute | solution.py:50
  36.3 4.6 %collective-permute-start.16 = (bf16[16,5120]{1,0:T(8,128)(2,1)S(1)}, bf16[16,5120]{1,0:T(8,128)(2,1)S(1)}, u32[]{:S(2)}, u32[]{:S(2)}) collective-permute-start(bf16[16,5120]{1,0:T(8,128)(2,1)S(1)} %get-tuple-element.55), channel_id=1, source_target_pairs={{1,0},{0,1},{3,2},{2,3},{5,4},{4,5},{7,6},{6,7},{9,8},{8,9},{11,10... | collective-permute-start | bytes 491528 | tf_op jit(solution)/shard_map/ppermute | solution.py:50
  36.6 26.1 %slice-start.1 = ((s8[6553600]{0:T(1024)(128)(4,1)}), s8[2359296]{0:T(1024)(128)(4,1)S(1)}, s32[]{:S(2)}) async-start(s8[6553600]{0:T(1024)(128)(4,1)} %bitcast.16), calls=%async_computation.1 | async-start | bytes 4718592
  36.6 26.1 %copy-start = (bf16[1,640,5120]{2,1,0:T(8,128)(2,1)S(1)}, bf16[1,640,5120]{2,1,0:T(8,128)(2,1)}, u32[]{:S(2)}) copy-start(bf16[1,640,5120]{2,1,0:T(8,128)(2,1)} %param.15) | copy-start | bytes 19660804
  37.3 5.2 %collective-permute-start.15 = (bf16[8,5120]{1,0:T(8,128)(2,1)S(1)}, bf16[8,5120]{1,0:T(8,128)(2,1)S(1)}, u32[]{:S(2)}, u32[]{:S(2)}) collective-permute-start(bf16[8,5120]{1,0:T(8,128)(2,1)S(1)} %get-tuple-element.53.refs_0_.after_any), channel_id=1, source_target_pairs={{0,12},{1,13},{2,14},{3,15},{4,8},{5,9},{6,10},{7,11},{8,4},{9,5},... | collective-permute-start | bytes 245768 | tf_op jit(solution)/shard_map/ppermute | solution.py:50
  39.7 7.5 %collective-permute-start.14 = (bf16[8,5120]{1,0:T(8,128)(2,1)S(1)}, bf16[8,5120]{1,0:T(8,128)(2,1)S(1)}, u32[]{:S(2)}, u32[]{:S(2)}) collective-permute-start(bf16[8,5120]{1,0:T(8,128)(2,1)S(1)} %get-tuple-element.53.refs_0_.after_any), channel_id=1, source_target_pairs={{0,8},{1,9},{2,10},{3,11},{4,12},{5,13},{6,14},{7,15},{8,0},{9,1},... | collective-permute-start | bytes 245768 | tf_op jit(solution)/shard_map/ppermute | solution.py:50
  39.7 7.5 %collective-permute-start.13 = (bf16[8,5120]{1,0:T(8,128)(2,1)S(1)}, bf16[8,5120]{1,0:T(8,128)(2,1)S(1)}, u32[]{:S(2)}, u32[]{:S(2)}) collective-permute-start(bf16[8,5120]{1,0:T(8,128)(2,1)S(1)} %get-tuple-element.53.refs_0_.after_any), channel_id=1, source_target_pairs={{0,4},{1,5},{2,6},{3,7},{4,0},{5,1},{6,2},{7,3},{8,12},{9,13},{10,... | collective-permute-start | bytes 245768 | tf_op jit(solution)/shard_map/ppermute | solution.py:50
  41.0 7.7 %collective-permute-start.21 = (bf16[32,5120]{1,0:T(8,128)(2,1)S(1)}, bf16[32,5120]{1,0:T(8,128)(2,1)S(1)}, u32[]{:S(2)}, u32[]{:S(2)}) collective-permute-start(bf16[32,5120]{1,0:T(8,128)(2,1)S(1)} %add_half.5.refs_5_), channel_id=1, source_target_pairs={{1,0},{0,1},{3,2},{2,3},{5,4},{4,5},{7,6},{6,7},{9,8},{8,9},{11,10... | collective-permute-start | bytes 983048 | tf_op jit(solution)/shard_map/ppermute | solution.py:50
  42.5 6.2 %collective-permute-start.20 = (bf16[32,5120]{1,0:T(8,128)(2,1)S(1)}, bf16[32,5120]{1,0:T(8,128)(2,1)S(1)}, u32[]{:S(2)}, u32[]{:S(2)}) collective-permute-start(bf16[32,5120]{1,0:T(8,128)(2,1)S(1)} %add_half.4.refs_4_), channel_id=1, source_target_pairs={{2,0},{3,1},{0,2},{1,3},{6,4},{7,5},{4,6},{5,7},{10,8},{11,9},{8,1... | collective-permute-start | bytes 983048 | tf_op jit(solution)/shard_map/ppermute | solution.py:50
  47.2 9.8 %collective-permute-start.19 = (bf16[32,5120]{1,0:T(8,128)(2,1)S(1)}, bf16[32,5120]{1,0:T(8,128)(2,1)S(1)}, u32[]{:S(2)}, u32[]{:S(2)}) collective-permute-start(bf16[32,5120]{1,0:T(8,128)(2,1)S(1)} %join.3.refs_3_.refs_2_), channel_id=1, source_target_pairs={{0,2},{1,3},{2,0},{3,1},{4,6},{5,7},{6,4},{7,5},{8,10},{9,11},{10,... | collective-permute-start | bytes 983048 | tf_op jit(solution)/shard_map/ppermute | solution.py:50
  48.4 8.6 %collective-permute-start.18 = (bf16[32,5120]{1,0:T(8,128)(2,1)S(1)}, bf16[32,5120]{1,0:T(8,128)(2,1)S(1)}, u32[]{:S(2)}, u32[]{:S(2)}) collective-permute-start(bf16[32,5120]{1,0:T(8,128)(2,1)S(1)} %join.3.refs_3_.refs_2_), channel_id=1, source_target_pairs={{0,1},{1,0},{2,3},{3,2},{4,5},{5,4},{6,7},{7,6},{8,9},{9,8},{10,11... | collective-permute-start | bytes 983048 | tf_op jit(solution)/shard_map/ppermute | solution.py:50
  57.0 5.7 %collective-permute-start.22 = (bf16[16,5120]{1,0:T(8,128)(2,1)S(1)}, bf16[16,5120]{1,0:T(8,128)(2,1)S(1)}, u32[]{:S(2)}, u32[]{:S(2)}) collective-permute-start(bf16[16,5120]{1,0:T(8,128)(2,1)S(1)} %get-tuple-element.59), channel_id=1, source_target_pairs={{0,1},{1,0},{2,3},{3,2},{4,5},{5,4},{6,7},{7,6},{8,9},{9,8},{10,11... | collective-permute-start | bytes 491528 | tf_op jit(solution)/shard_map/ppermute | solution.py:50
  58.2 4.5 %collective-permute-start.23 = (bf16[16,5120]{1,0:T(8,128)(2,1)S(1)}, bf16[16,5120]{1,0:T(8,128)(2,1)S(1)}, u32[]{:S(2)}, u32[]{:S(2)}) collective-permute-start(bf16[16,5120]{1,0:T(8,128)(2,1)S(1)} %get-tuple-element.60), channel_id=1, source_target_pairs={{0,2},{1,3},{2,0},{3,1},{4,6},{5,7},{6,4},{7,5},{8,10},{9,11},{10,... | collective-permute-start | bytes 491528 | tf_op jit(solution)/shard_map/ppermute | solution.py:50
  58.4 3.3 %collective-permute-start.25 = (bf16[8,5120]{1,0:T(8,128)(2,1)S(1)}, bf16[8,5120]{1,0:T(8,128)(2,1)S(1)}, u32[]{:S(2)}, u32[]{:S(2)}) collective-permute-start(bf16[8,5120]{1,0:T(8,128)(2,1)S(1)} %get-tuple-element.61), channel_id=1, source_target_pairs={{4,0},{5,1},{6,2},{7,3},{0,4},{1,5},{2,6},{3,7},{12,8},{13,9},{14,... | collective-permute-start | bytes 245768 | tf_op jit(solution)/shard_map/ppermute | solution.py:50
  58.4 4.3 %collective-permute-start.26 = (bf16[8,5120]{1,0:T(8,128)(2,1)S(1)}, bf16[8,5120]{1,0:T(8,128)(2,1)S(1)}, u32[]{:S(2)}, u32[]{:S(2)}) collective-permute-start(bf16[8,5120]{1,0:T(8,128)(2,1)S(1)} %get-tuple-element.62), channel_id=1, source_target_pairs={{8,0},{9,1},{10,2},{11,3},{12,4},{13,5},{14,6},{15,7},{0,8},{1,9},... | collective-permute-start | bytes 245768 | tf_op jit(solution)/shard_map/ppermute | solution.py:50
  65.1 6.8 %collective-permute-start.30 = (bf16[16,5120]{1,0:T(8,128)(2,1)S(1)}, bf16[16,5120]{1,0:T(8,128)(2,1)S(1)}, u32[]{:S(2)}, u32[]{:S(2)}) collective-permute-start(bf16[16,5120]{1,0:T(8,128)(2,1)S(1)} %get-tuple-element.68), channel_id=1, source_target_pairs={{2,0},{3,1},{0,2},{1,3},{6,4},{7,5},{4,6},{5,7},{10,8},{11,9},{8,1... | collective-permute-start | bytes 491528 | tf_op jit(solution)/shard_map/ppermute | solution.py:50
  66.4 6.8 %collective-permute-start.27 = (bf16[16,5120]{1,0:T(8,128)(2,1)S(1)}, bf16[16,5120]{1,0:T(8,128)(2,1)S(1)}, u32[]{:S(2)}, u32[]{:S(2)}) collective-permute-start(bf16[16,5120]{1,0:T(8,128)(2,1)S(1)} %get-tuple-element.65), channel_id=1, source_target_pairs={{1,0},{0,1},{3,2},{2,3},{5,4},{4,5},{7,6},{6,7},{9,8},{8,9},{11,10... | collective-permute-start | bytes 491528 | tf_op jit(solution)/shard_map/ppermute | solution.py:50
  66.6 5.2 %collective-permute-start.28 = (bf16[8,5120]{1,0:T(8,128)(2,1)S(1)}, bf16[8,5120]{1,0:T(8,128)(2,1)S(1)}, u32[]{:S(2)}, u32[]{:S(2)}) collective-permute-start(bf16[8,5120]{1,0:T(8,128)(2,1)S(1)} %get-tuple-element.66), channel_id=1, source_target_pairs={{12,0},{13,1},{14,2},{15,3},{8,4},{9,5},{10,6},{11,7},{4,8},{5,9},... | collective-permute-start | bytes 245768 | tf_op jit(solution)/shard_map/ppermute | solution.py:50
  71.9 7.7 %collective-permute-start.31 = (bf16[32,5120]{1,0:T(8,128)(2,1)S(1)}, bf16[32,5120]{1,0:T(8,128)(2,1)S(1)}, u32[]{:S(2)}, u32[]{:S(2)}) collective-permute-start(bf16[32,5120]{1,0:T(8,128)(2,1)S(1)} %add_half.7), channel_id=1, source_target_pairs={{1,0},{0,1},{3,2},{2,3},{5,4},{4,5},{7,6},{6,7},{9,8},{8,9},{11,10... | collective-permute-start | bytes 983048 | tf_op jit(solution)/shard_map/ppermute | solution.py:50
  73.3 6.3 %collective-permute-start.29 = (bf16[32,5120]{1,0:T(8,128)(2,1)S(1)}, bf16[32,5120]{1,0:T(8,128)(2,1)S(1)}, u32[]{:S(2)}, u32[]{:S(2)}) collective-permute-start(bf16[32,5120]{1,0:T(8,128)(2,1)S(1)} %add_half.6), channel_id=1, source_target_pairs={{2,0},{3,1},{0,2},{1,3},{6,4},{7,5},{4,6},{5,7},{10,8},{11,9},{8,1... | collective-permute-start | bytes 983048 | tf_op jit(solution)/shard_map/ppermute | solution.py:50
  73.6 10.4 %collective-permute-start.35 = (f32[8,5120]{1,0:T(8,128)S(1)}, f32[8,5120]{1,0:T(8,128)S(1)}, u32[]{:S(2)}, u32[]{:S(2)}) collective-permute-start(f32[8,5120]{1,0:T(8,128)S(1)} %add_last.2.refs_2_.second_ref), channel_id=1, source_target_pairs={{0,16},{1,17},{2,18},{3,19},{4,20},{5,21},{6,22},{7,23},{8,24},{9,... | collective-permute-start | bytes 491528 | tf_op jit(solution)/shard_map/ppermute | solution.py:27
  79.8 5.2 %collective-permute-start.32 = (bf16[8,5120]{1,0:T(8,128)(2,1)S(1)}, bf16[8,5120]{1,0:T(8,128)(2,1)S(1)}, u32[]{:S(2)}, u32[]{:S(2)}) collective-permute-start(bf16[8,5120]{1,0:T(8,128)(2,1)S(1)} %get-tuple-element.71), channel_id=1, source_target_pairs={{12,0},{13,1},{14,2},{15,3},{8,4},{9,5},{10,6},{11,7},{4,8},{5,9},... | collective-permute-start | bytes 245768 | tf_op jit(solution)/shard_map/ppermute | solution.py:50
  81.7 4.9 %collective-permute-start.33 = (bf16[8,5120]{1,0:T(8,128)(2,1)S(1)}, bf16[8,5120]{1,0:T(8,128)(2,1)S(1)}, u32[]{:S(2)}, u32[]{:S(2)}) collective-permute-start(bf16[8,5120]{1,0:T(8,128)(2,1)S(1)} %get-tuple-element.72), channel_id=1, source_target_pairs={{8,0},{9,1},{10,2},{11,3},{12,4},{13,5},{14,6},{15,7},{0,8},{1,9},... | collective-permute-start | bytes 245768 | tf_op jit(solution)/shard_map/ppermute | solution.py:50
  81.8 4.9 %collective-permute-start.34 = (bf16[8,5120]{1,0:T(8,128)(2,1)S(1)}, bf16[8,5120]{1,0:T(8,128)(2,1)S(1)}, u32[]{:S(2)}, u32[]{:S(2)}) collective-permute-start(bf16[8,5120]{1,0:T(8,128)(2,1)S(1)} %get-tuple-element.73), channel_id=1, source_target_pairs={{4,0},{5,1},{6,2},{7,3},{0,4},{1,5},{2,6},{3,7},{12,8},{13,9},{14,... | collective-permute-start | bytes 245768 | tf_op jit(solution)/shard_map/ppermute | solution.py:50
  86.7 11.2 %collective-permute-start.36 = (f32[8,5248]{1,0:T(8,128)S(1)}, f32[8,5248]{1,0:T(8,128)S(1)}, u32[]{:S(2)}, u32[]{:S(2)}) collective-permute-start(f32[8,5248]{1,0:T(8,128)S(1)} %add_last.3.back_ref), channel_id=1, source_target_pairs={{0,16},{1,17},{2,18},{3,19},{4,20},{5,21},{6,22},{7,23},{8,24},{9,... | collective-permute-start | bytes 503816 | tf_op jit(solution)/shard_map/ppermute | solution.py:17
